TPU v7x, 32 devices: a whole 2x2x4 slice. The times are simulated.
32 devices in a mesh: tok: 4 (over y, core), head: 8 (over z, x).
Axes of the slice: x: 2, y: 2, z: 4, core: 2. Of those that a mesh axis runs over, the one named last changes fastest.
Arguments:
- tokens: bfloat16 [2048, 4096], P('tok', 'head'), may hold values from -32 to 32
- w_query: bfloat16 [4096, 4096], P(None, 'head'), may hold values from -0.09375 to 0.09375
- w_key: bfloat16 [4096, 4096], P(None, 'head'), may hold values from -0.09375 to 0.09375
- w_value: bfloat16 [4096, 4096], P(None, 'head'), may hold values from -0.09375 to 0.09375
- w_out: bfloat16 [4096, 4096], P('head'), may hold values from -0.09375 to 0.09375
- fast_gate: float32 [32, 128, 256], P('head'), may hold values from -0.5 to 0.5
- fast_up: float32 [32, 128, 256], P('head'), may hold values from -0.5 to 0.5
- fast_down: float32 [32, 256, 128], P('head'), may hold values from -0.375 to 0.375
- token_rate: float32 [2048, 32], P('tok', 'head'), may hold values from 0.05 to 1
- head_step: float32 [32], P('head'), may hold values from 0.2 to 1
Outputs:
- mixed: bfloat16 [2048, 4096], P(('tok', 'head'))
All inputs are finite; a program needn't handle non-finite values.
Results may differ from a plain program's by a relative error of at most 0.022.
Values may be sent and summed in bfloat16 or wider, within the bound.
No kernel may reach another device: no remote copies, remote signals or barrier semaphores. Data moves between devices by JAX's collectives and lax.ppermute only.
A program may use at most 64 MiB of HBM per device.

v0:
```python
import jax
import jax.numpy as jnp
from jax import lax
from jax.sharding import PartitionSpec as P

WINDOW = 512


def shifted(value, axis, steps):
    count = lax.axis_size(axis)
    leading, last = (max(0, -steps), min(count, count - steps))
    return lax.ppermute(value, axis, [(source, source + steps) for source in range(leading, last)])


def rms(values):
    return values * lax.rsqrt(jnp.mean(values * values, axis=-1, keepdims=True) + 1e-06)


def batched(form, left, right):
    return jnp.einsum(form, left, right, precision=lax.Precision.HIGHEST)


def fast_apply(inputs, gate, upper, down):
    gate_pre = batched("thd,hdf->thf", inputs, gate)
    up_pre = batched("thd,hdf->thf", inputs, upper)
    return batched("thf,hfd->thd", jax.nn.silu(gate_pre) * up_pre, down)


def shards(
    tokens, w_query, w_key, w_value, w_out, fast_gate, fast_up, fast_down, token_rate, head_step
):
    row_count = tokens.shape[0]
    local_heads = fast_gate.shape[0]
    head_size = fast_gate.shape[1]
    hidden_size = fast_gate.shape[2]
    local_width = local_heads * head_size
    piece = lax.all_gather(tokens, "head", axis=1, tiled=True)
    query_f, key_f, value_f = tuple(
        (
            jnp.dot(piece, weight, preferred_element_type=jnp.float32)
            for weight in (w_query, w_key, w_value)
        )
    )
    shape = (row_count, local_heads, head_size)
    query = query_f.astype(jnp.bfloat16).reshape(shape)
    key = key_f.astype(jnp.bfloat16).reshape(shape)
    value = value_f.astype(jnp.bfloat16).reshape(shape)
    window = WINDOW
    tail = jnp.stack([key, value])
    before = shifted(tail, "tok", 1)
    keys_all = jnp.concatenate([before[0], key], axis=0)
    values_all = jnp.concatenate([before[1], value], axis=0)
    first = lax.axis_index("tok") * row_count
    query_pos = first + jnp.arange(row_count, dtype=jnp.int32)
    key_pos = first - window + jnp.arange(row_count + window, dtype=jnp.int32)
    allowed = (
        (key_pos[None, :] >= 0)
        & (key_pos[None, :] <= query_pos[:, None])
        & (key_pos[None, :] > query_pos[:, None] - window)
    )
    scores = jnp.einsum(
        "qhd,khd->hqk", query, keys_all, preferred_element_type=jnp.float32
    ) * head_size ** (-0.5)
    scores = jnp.where(allowed[None], scores, jnp.float32(-1e30))
    top = jnp.max(scores, axis=-1, keepdims=True)
    expo = jnp.exp(scores - top)
    weights = (expo / jnp.sum(expo, axis=-1, keepdims=True)).astype(jnp.bfloat16)
    attended = jnp.einsum("hqk,khd->qhd", weights, values_all, preferred_element_type=jnp.float32)
    knorm = rms(key.astype(jnp.float32))
    qnorm = rms(query.astype(jnp.float32))
    target = -token_rate[:, :, None] * value.astype(jnp.float32)
    gate_pre = batched("thd,hdf->thf", knorm, fast_gate)
    up_pre = batched("thd,hdf->thf", knorm, fast_up)
    sigma = jax.nn.sigmoid(gate_pre)
    active = gate_pre * sigma
    hidden = active * up_pre
    grad_down_t = batched("thf,thd->hdf", hidden, target)
    back = batched("thd,hfd->thf", target, fast_down)
    grad_up = batched("thd,thf->hdf", knorm, back * active)
    grad_gate = batched(
        "thd,thf->hdf", knorm, back * up_pre * sigma * (1.0 + gate_pre * (1.0 - sigma))
    )
    grads = jnp.stack([grad_gate, grad_up, grad_down_t], axis=1)
    matrices = jnp.stack([fast_gate, fast_up, jnp.transpose(fast_down, (0, 2, 1))], axis=1)
    fan_scale = jnp.array(
        [head_size ** (-0.5), head_size ** (-0.5), hidden_size ** (-0.5)], jnp.float32
    )
    step_scale = head_step[:, None, None, None] * fan_scale[None, :, None, None]
    count = head_size * hidden_size
    summed = lax.psum(grads.astype(jnp.bfloat16), "tok").astype(jnp.float32)
    mean_sq = jnp.sum(summed * summed, axis=(2, 3)) / count
    renewed = matrices - step_scale * summed * lax.rsqrt(mean_sq + 1e-06)[:, :, None, None]
    fast_out = fast_apply(
        qnorm, renewed[:, 0], renewed[:, 1], jnp.transpose(renewed[:, 2], (0, 2, 1))
    )
    combined = (attended + fast_out).astype(jnp.bfloat16).reshape(row_count, local_width)
    return lax.psum_scatter(
        jnp.dot(combined, w_out, preferred_element_type=jnp.float32).astype(jnp.bfloat16),
        "head",
        scatter_dimension=0,
        tiled=True,
    )


def solution(mesh):
    placed = (
        P("tok", "head"),
        P(None, "head"),
        P(None, "head"),
        P(None, "head"),
        P("head", None),
        P("head", None, None),
        P("head", None, None),
        P("head", None, None),
        P("tok", "head"),
        P("head"),
    )
    return jax.shard_map(
        shards, mesh=mesh, in_specs=placed, out_specs=P(("tok", "head"), None), check_vma=False
    )
```

profile of v0, /device:TPU:1, one launch (start us, length us, event | category | flops | bytes accessed | tf_op | source)
XLA Modules:
  0.0 266.2 jit_solution(4419582188890721976)
XLA Ops:
  6.5 0.0 all-gather.2.cloned.1.call-start
  6.5 0.7 all-gather.2.cloned.1.call-update
  7.3 0.0 all-reduce.2.cloned.1.call-start
  7.3 0.7 neg.11
  8.0 1.2 copy.18
  9.3 0.7 broadcast_multiply_fusion
  10.0 1.4 compare_and_fusion
  11.4 0.0 copy-start.2
  11.4 74.7 %all-gather.2.cloned.1.call-done = bf16[512,4096]{1,0:T(8,128)(2,1)} async-done(((bf16[512,512]{1,0:T(8,128)(2,1)}), bf16[512,4096]{1,0:T(8,128)(2,1)}) %all-gather.2.cloned.1.call-update) | async-done | bytes 4194320 | tf_op jit(solution)/shard_map/all_gather | solution.py:37
  86.1 0.0 copy-start.9
  86.1 6.0 %fusion.43 = (f32[512,4]{0,1:T(4,128)S(1)}, bf16[512,512]{0,1:T(8,128)(2,1)S(1)}) fusion(bf16[512,4096]{1,0:T(8,128)(2,1)} %all-gather.2.cloned.1.call-done, bf16[4096,512]{1,0:T(8,128)(2,1)} %param.13), kind=kOutput, calls=%fused_computation.59 | convolution fusion | flops 2148530176 | bytes 8921088 | tf_op jit(solution)/shard_map/dot_general | solution.py:40
  92.1 0.0 copy-start.1
  92.1 0.0 copy-done.2
  92.1 0.0 copy-start.8
  92.2 1.8 fusion.28
  94.0 0.0 copy-done.1
  94.0 1.8 fusion.29
  95.9 0.0 copy-done.9
  95.9 0.0 copy-done.8
  95.9 0.0 copy-start.3
  95.9 2.4 convolution_convert_fusion.2
  98.3 0.0 copy-done.3
  98.3 1.9 fusion.54
  100.2 2.1 fusion.38
  102.2 2.2 fusion.40
  104.4 1.9 fusion.39
  106.4 1.0 copy.13
  107.4 1.0 copy.12
  108.4 1.0 pad_maximum_fusion.1
  109.3 0.0 all-reduce.2.cloned.1.call-update
  109.4 0.0 reduce-scatter.2.cloned.1.call-start
  109.4 0.0 copy-start.4
  109.4 0.0 copy-start.5
  109.4 5.9 %convolution_convert_fusion.1 = bf16[512,512]{0,1:T(8,128)(2,1)S(1)} fusion(bf16[512,4096]{1,0:T(8,128)(2,1)} %all-gather.2.cloned.1.call-done, bf16[4096,512]{1,0:T(8,128)(2,1)} %param.12), kind=kOutput, calls=%fused_computation.48 | convolution fusion | flops 2147745792 | bytes 8912896 | tf_op jit(solution)/shard_map/dot_general | solution.py:40
  115.4 0.0 copy-done.4
  115.4 0.0 copy-done.5
  115.4 1.1 pad_maximum_fusion
  116.4 1.0 copy.14
  117.4 0.3 copy.15
  117.7 0.3 copy.22
  118.0 4.3 %collective-permute-start = (bf16[2,512,4,128]{3,1,2,0:T(8,128)(2,1)}, bf16[2,512,4,128]{3,1,2,0:T(8,128)(2,1)}, u32[]{:S(2)}, u32[]{:S(2)}) collective-permute-start(bf16[2,512,4,128]{3,1,2,0:T(8,128)(2,1)} %pad_maximum_fusion), channel_id=1, source_target_pairs={{0,8},{8,16},{16,24},{1,9},{9,17},{17,25},{2,10},{10,18},{18,26},{... | collective-permute-start | bytes 3145736 | tf_op jit(solution)/shard_map/ppermute | solution.py:12
  122.3 0.4 fusion.44
  122.7 19.5 %all-reduce.2.cloned.1.call-done = bf16[4,3,128,256]{3,2,0,1:T(8,128)(2,1)} async-done(((bf16[4,3,128,256]{3,2,0,1:T(8,128)(2,1)}), bf16[4,3,128,256]{3,2,0,1:T(8,128)(2,1)}) %all-reduce.2.cloned.1.call-update) | async-done | bytes 786448 | tf_op jit(solution)/shard_map/psum | solution.py:90
  142.2 1.4 fusion.26
  143.6 1.5 fusion.25
  145.0 1.8 fusion.31
  146.9 1.8 fusion.32
  148.7 2.6 fusion.6
  151.3 0.0 collective-permute-done
  151.3 1.3 slice_bitcast_fusion.7
  152.6 0.0 copy-start.6
  152.6 1.3 fusion.48
  153.9 0.0 copy-done.6
  153.9 0.0 copy-start.7
  153.9 6.2 %fusion.71 = (f32[4,512]{1,0:T(4,128)S(1)}, f32[4,512,1024]{2,1,0:T(8,128)}) fusion(f32[4,512,1024]{2,1,0:T(8,128)S(1)} %fusion.48, pred[512,1024]{1,0:T(8,128)(4,1)S(1)} %copy-done.6), kind=kOutput, calls=%fused_computation.103 | output fusion | flops 12583935 | bytes 17309696 | tf_op jit(solution)/shard_map/sub | solution.py:66
  160.2 0.0 copy-done.7
  160.2 0.0 copy-start
  160.2 5.2 %fusion.30 = bf16[4,128,512]{2,1,0:T(8,128)(2,1)S(1)} fusion(f32[4,128,512]{2,1,0:T(8,128)S(1)} %fusion.6, f32[4,512,1024]{2,1,0:T(8,128)} %get-tuple-element.10, f32[4,512]{1,0:T(4,128)S(1)} %get-tuple-element.9, bf16[512,4,128]{2,0,1:T(8,128)(2,1)S(1)} %copy-done.7, bf16[512,4,128]{2,0,1:T(8,128)(2,1)S(1)} %get-tuple-element.5), kind=kOutput, calls=%fused_computation.47 | convolution fusion | flops 543686656 | bytes 11018240 | tf_op jit(solution)/shard_map/hqk,khd->qhd/dot_general | solution.py:68
  165.4 0.0 copy-done
  165.4 4.4 %convolution_convert_fusion = bf16[512,4096]{1,0:T(8,128)(2,1)} fusion(bf16[512,512]{0,1:T(8,128)(2,1)S(1)} %bitcast.143, bf16[512,4096]{1,0:T(8,128)(2,1)S(1)} %copy-done), kind=kOutput, calls=%fused_computation.5 | convolution fusion | flops 2149580800 | bytes 8912896 | tf_op jit(solution)/shard_map/dot_general | solution.py:98
  169.8 0.0 reduce-scatter.2.cloned.1.call-update
  169.8 89.9 %reduce-scatter.2.cloned.1.call-done = bf16[64,4096]{1,0:T(8,128)(2,1)} async-done(((bf16[512,4096]{1,0:T(8,128)(2,1)}), bf16[64,4096]{1,0:T(8,128)(2,1)}) %reduce-scatter.2.cloned.1.call-update) | async-done | bytes 524304 | tf_op jit(solution)/shard_map/reduce_scatter | solution.py:97
  (6 shorter events, 0.0 us)
Async XLA Ops:
  6.5 79.6 %all-gather.2.cloned.1.call-start = ((), (), s32[]{:S(2)}) async-start(), calls=%async_computation.1 | async-start | bytes 4718592 | tf_op jit(solution)/shard_map/all_gather | solution.py:37
  7.3 134.9 %all-reduce.2.cloned.1.call-start = ((), (), s32[]{:S(2)}) async-start(), calls=%async_computation.2 | async-start | bytes 1572864 | tf_op jit(solution)/shard_map/psum | solution.py:90
  11.4 80.7 %copy-start.2 = (f32[4,128,256]{2,1,0:T(8,128)S(1)}, f32[4,128,256]{2,1,0:T(8,128)}, u32[]{:S(2)}) copy-start(f32[4,128,256]{2,1,0:T(8,128)} %param.16) | copy-start | bytes 1572868
  86.1 9.8 %copy-start.9 = (bf16[512,4096]{1,0:T(8,128)(2,1)S(1)}, bf16[512,4096]{1,0:T(8,128)(2,1)}, u32[]{:S(2)}) copy-start(bf16[512,4096]{1,0:T(8,128)(2,1)} %all-gather.2.cloned.1.call-done) | copy-start | bytes 12582916
  92.1 1.9 copy-start.1
  92.1 3.7 %copy-start.8 = (bf16[4096,512]{1,0:T(8,128)(2,1)S(1)}, bf16[4096,512]{1,0:T(8,128)(2,1)}, u32[]{:S(2)}) copy-start(bf16[4096,512]{1,0:T(8,128)(2,1)} %param.14) | copy-start | bytes 12582916
  95.9 2.4 copy-start.3
  109.4 150.3 %reduce-scatter.2.cloned.1.call-start = ((), (), s32[]{:S(2)}) async-start(), calls=%async_computation.3 | async-start | bytes 4718592 | tf_op jit(solution)/shard_map/reduce_scatter | solution.py:97
  109.4 5.9 %copy-start.4 = (bf16[1,512,4,128]{3,1,2,0:T(8,128)(2,1)S(1)}, bf16[1,512,4,128]{3,1,2,0:T(8,128)(2,1)}, u32[]{:S(2)}) copy-start(bf16[1,512,4,128]{3,1,2,0:T(8,128)(2,1)} %copy.13) | copy-start | bytes 1572868
  109.4 5.9 %copy-start.5 = (bf16[1,512,4,128]{3,1,2,0:T(8,128)(2,1)S(1)}, bf16[1,512,4,128]{3,1,2,0:T(8,128)(2,1)}, u32[]{:S(2)}) copy-start(bf16[1,512,4,128]{3,1,2,0:T(8,128)(2,1)} %copy.12) | copy-start | bytes 1572868
  118.0 33.3 %collective-permute-start = (bf16[2,512,4,128]{3,1,2,0:T(8,128)(2,1)}, bf16[2,512,4,128]{3,1,2,0:T(8,128)(2,1)}, u32[]{:S(2)}, u32[]{:S(2)}) collective-permute-start(bf16[2,512,4,128]{3,1,2,0:T(8,128)(2,1)} %pad_maximum_fusion), channel_id=1, source_target_pairs={{0,8},{8,16},{16,24},{1,9},{9,17},{17,25},{2,10},{10,18},{18,26},{... | collective-permute-start | bytes 3145736 | tf_op jit(solution)/shard_map/ppermute | solution.py:12
  152.6 1.3 copy-start.6
  153.9 6.2 %copy-start.7 = (bf16[512,4,128]{2,0,1:T(8,128)(2,1)S(1)}, bf16[512,4,128]{2,0,1:T(8,128)(2,1)}, u32[]{:S(2)}) copy-start(bf16[512,4,128]{2,0,1:T(8,128)(2,1)} %copy.14) | copy-start | bytes 1572868
  160.2 5.2 %copy-start = (bf16[512,4096]{1,0:T(8,128)(2,1)S(1)}, bf16[512,4096]{1,0:T(8,128)(2,1)}, u32[]{:S(2)}) copy-start(bf16[512,4096]{1,0:T(8,128)(2,1)} %param.15) | copy-start | bytes 12582916
Sparse Core Ops, SparseCore 0:
  9.4 76.6 all-gather.1
  109.5 32.6 all-reduce.1
  169.9 89.7 reduce-scatter.1
where the time goes:
time: 267 us; the launch traced here: 266 us
  waiting for transfers between devices  185 us (69%)
  matrix products  43.1 us (16%)
  other arithmetic  14.4 us (5%)
  between operations  13.4 us (5%)
  local copies, waits for them, and re-layouts  6.14 us (2%)
  starting transfers between devices  4.38 us (2%)
    reduce_scatter x1, waiting for transfers between devices, shards(): lax.psum_scatter(jnp.dot(combined, w_out, preferred_element_type=jnp.floa...  89.9 us
    all_gather x1, waiting for transfers between devices, shards(): piece = lax.all_gather(tokens, 'head', axis=1, tiled=True)  74.7 us
    psum x1, waiting for transfers between devices, shards(): summed = lax.psum(grads.astype(jnp.bfloat16), 'tok').astype(jnp.float32)  19.5 us
    dot_general x9, matrix products, batched(): return jnp.einsum(form, left, right, precision=lax.Precision.HIGHEST)  18 us
    dot_general x3, matrix products, shards(): jnp.dot(piece, weight, preferred_element_type=jnp.float32)  14.3 us
    sub x1, other arithmetic, shards(): expo = jnp.exp(scores - top)  6.23 us
  transfers between devices with their start and end apart: 4, of which 3 were waited for; matrix products, arithmetic and copies ran while one was open for 8% of the time, Pallas kernels for 0%

commit v1 on v0

v1 whole, which is shorter than its diff:
```python
import functools

import jax
import jax.numpy as jnp
from jax import lax
from jax.experimental import pallas as pl
from jax.experimental.pallas import tpu as pltpu
from jax.sharding import PartitionSpec as P

WINDOW = 512
CHUNKS = 2
F32 = jnp.float32
BF16 = jnp.bfloat16
LOG2E = 1.4426950408889634


def call(body, grid, in_specs, out_specs, out_shape, scratch=(), prefetch=1, vmem=48):
    return pl.pallas_call(
        body,
        grid_spec=pltpu.PrefetchScalarGridSpec(
            num_scalar_prefetch=prefetch,
            grid=grid,
            in_specs=in_specs,
            out_specs=out_specs,
            scratch_shapes=list(scratch),
        ),
        out_shape=out_shape,
        compiler_params=pltpu.CompilerParams(vmem_limit_bytes=vmem * 1024 * 1024),
    )


def fixed(shape):
    return pl.BlockSpec(shape, lambda *_: (0,) * len(shape))


def mm(left, right, dims=((1,), (0,))):
    return lax.dot_general(left, right, (dims, ((), ())), preferred_element_type=F32)


def sigmoid(x):
    return 0.5 * jnp.tanh(0.5 * x) + 0.5


def ring_order(count):
    return list(range(0, count, 2)) + list(range(count - 1, 0, -2))


def ring_send(value, step):
    order = ring_order(lax.axis_size("head"))
    count = len(order)
    return lax.ppermute(
        value, "head", [(order[i], order[(i + step) % count]) for i in range(count)]
    )


def ring_ids(offsets):
    count = lax.axis_size("head")
    me = lax.axis_index("head")
    place = jnp.where(me % 2 == 0, me // 2, count - 1 - me // 2)
    ids = []
    for offset in offsets:
        at = (place + offset) % count
        ids.append(jnp.where(at < count // 2, 2 * at, 2 * (count - 1 - at) + 1))
    return jnp.stack(ids).astype(jnp.int32)


def gather_pieces(own):
    count = lax.axis_size("head")
    half = own.shape[0] // 2
    pieces = [own]
    up, down = own, own
    for _ in range(1, count // 2):
        up, down = ring_send(up, 1), ring_send(down, -1)
        pieces += [up, down]
    return pieces + [ring_send(up[:half], 1), ring_send(down[half:], -1)]


def project(ids, pieces, weights):
    rows, depth = pieces[0].shape
    width = weights[0].shape[1]
    half = rows // 2
    count = len(pieces) - 1
    parts = len(weights)

    def body(ids_ref, *refs):
        piece_refs = refs[: count + 1]
        weight_refs = refs[count + 1 : count + 1 + parts]
        out_ref, acc = refs[-2:]
        step = pl.program_id(0)

        for index in range(count):

            @pl.when(step == index)
            def _(index=index):
                for part in range(parts):
                    weight = weight_refs[part][...]
                    if index < count - 1:
                        term = mm(piece_refs[index][...], weight)
                        if index == 0:
                            acc[part] = term
                        else:
                            acc[part] += term
                    else:
                        for side in range(2):
                            where = slice(side * half, (side + 1) * half)
                            term = mm(piece_refs[index + side][...], weight)
                            out_ref[part, where] = (acc[part, where] + term).astype(BF16)

    return call(
        body,
        (count,),
        [fixed(piece.shape) for piece in pieces]
        + [pl.BlockSpec((depth, width), lambda k, ids_ref: (ids_ref[k], 0))] * parts,
        fixed((parts, rows, width)),
        jax.ShapeDtypeStruct((parts, rows, width), BF16),
        [pltpu.VMEM((parts, rows, width), F32)],
    )(ids, *pieces, *weights)


def head_grads(base, heads, kv, rate, fast_gate, fast_up, fast_down, before):
    rows = kv.shape[1]
    size, hidden_size = fast_gate.shape[1:]
    lanes = rate.shape[1]

    def body(base_ref, k_ref, v_ref, rate_ref, gate_ref, up_ref, down_ref, *rest):
        out_ref = rest[-1]
        head = base_ref[0] + pl.program_id(0)
        lane = lax.broadcasted_iota(jnp.int32, (rows, lanes), 1)
        mine = jnp.sum(jnp.where(lane == head, rate_ref[...], 0.0), axis=1, keepdims=True)
        key = k_ref[0].astype(F32)
        knorm = key * lax.rsqrt(jnp.mean(key * key, axis=-1, keepdims=True) + 1e-06)
        target = -mine * v_ref[0].astype(F32)
        knorm = knorm.astype(BF16)
        gate_pre = mm(knorm, gate_ref[0].astype(BF16))
        up_pre = mm(knorm, up_ref[0].astype(BF16))
        back = mm(target.astype(BF16), down_ref[0].astype(BF16), ((1,), (1,)))
        sigma = sigmoid(gate_pre)
        active = gate_pre * sigma
        first = (back * up_pre * (sigma + active * (1.0 - sigma))).astype(BF16)
        second = (back * active).astype(BF16)
        third = (active * up_pre).astype(BF16)
        terms = (
            mm(knorm, first, ((0,), (0,))),
            mm(knorm, second, ((0,), (0,))),
            mm(target.astype(BF16), third, ((0,), (0,))),
        )
        for index, term in enumerate(terms):
            if before is not None:
                term = term + rest[0][0, index]
            out_ref[0, index] = term

    def spec(shape):
        return pl.BlockSpec((1,) + shape, lambda h, b: (b[0] + h,) + (0,) * len(shape))

    args = [kv, kv, rate, fast_gate, fast_up, fast_down]
    specs = [
        pl.BlockSpec((1, rows, size), lambda h, b: (0, 0, b[0] + h)),
        pl.BlockSpec((1, rows, size), lambda h, b: (1, 0, b[0] + h)),
        fixed(rate.shape),
        spec((size, hidden_size)),
        spec((size, hidden_size)),
        spec((hidden_size, size)),
    ]
    if before is not None:
        args.append(before)
        specs.append(spec((3, size, hidden_size)))
    return call(
        body,
        (heads,),
        specs,
        pl.BlockSpec((1, 3, size, hidden_size), lambda h, b: (h, 0, 0, 0)),
        jax.ShapeDtypeStruct((heads, 3, size, hidden_size), F32),
    )(base, *args)


def renew(base, kept, received, step, fast_gate, fast_up, fast_down):
    heads, _, size, hidden_size = kept.shape

    def body(base_ref, step_ref, kept_ref, gate_ref, up_ref, down_ref, *rest):
        out_ref = rest[-1]
        pace = step_ref[base_ref[0] + pl.program_id(0)]
        for index in range(3):
            grad = kept_ref[0, index]
            for more in rest[:-1]:
                grad = grad + more[0, index].astype(F32)
            if index < 2:
                matrix = (gate_ref, up_ref)[index][0]
                fan = size
            else:
                matrix = down_ref[0].T
                fan = hidden_size
            mean_sq = jnp.sum(grad * grad, keepdims=True) / (size * hidden_size)
            scale = pace * fan ** (-0.5) * lax.rsqrt(mean_sq + 1e-06)
            out_ref[0, index] = (matrix - scale * grad).astype(BF16)

    def spec(shape):
        return pl.BlockSpec((1,) + shape, lambda h, b, s: (b[0] + h,) + (0,) * len(shape))

    own = pl.BlockSpec((1, 3, size, hidden_size), lambda h, b, s: (h, 0, 0, 0))
    return call(
        body,
        (heads,),
        [own, spec((size, hidden_size)), spec((size, hidden_size)), spec((hidden_size, size))]
        + [own] * len(received),
        own,
        jax.ShapeDtypeStruct(kept.shape, BF16),
        prefetch=2,
    )(base, step, kept, fast_gate, fast_up, fast_down, *received)


def attend(place, queries, kvs, halos, size):
    count = len(queries)
    rows = queries[0].shape[1]
    heads = queries[0].shape[2] // size
    factor = size ** (-0.5) * LOG2E

    def body(place_ref, *refs):
        q_refs = refs[:count]
        k_refs, v_refs = refs[count : 3 * count], refs[3 * count : 5 * count]
        out_ref = refs[-1]
        has_halo = place_ref[0] > 0
        row = lax.broadcasted_iota(jnp.int32, (rows, rows), 0)
        col = lax.broadcasted_iota(jnp.int32, (rows, rows), 1)
        for index in range(count):
            query = q_refs[index][0]
            scores = []
            for source in range(index, index + count + 1):
                part = mm(query, k_refs[source][0], ((1,), (1,))) * factor
                if source == index:
                    part = jnp.where((col > row) & has_halo, part, -1e30)
                elif source == index + count:
                    part = jnp.where(col <= row, part, -1e30)
                elif source < count:
                    part = jnp.where(has_halo, part, -1e30)
                scores.append(part)
            top = functools.reduce(
                jnp.maximum, [jnp.max(part, axis=-1, keepdims=True) for part in scores]
            )
            total, result = 0.0, 0.0
            for part, source in zip(scores, range(index, index + count + 1)):
                expo = jnp.exp2(part - top)
                total = total + jnp.sum(expo, axis=-1, keepdims=True)
                result = result + mm(expo.astype(BF16), v_refs[source][0])
            out_ref[index * rows : (index + 1) * rows] = result / total

    def spec(which):
        return pl.BlockSpec((1, rows, size), lambda h, p: (which, 0, h))

    sources = list(halos) + list(kvs)
    return call(
        body,
        (heads,),
        [spec(0)] * count + [spec(0)] * (2 * count) + [spec(1)] * (2 * count),
        pl.BlockSpec((count * rows, size), lambda h, p: (0, h)),
        jax.ShapeDtypeStruct((count * rows, heads * size), F32),
    )(place, *queries, *sources, *sources)


def apply_fast(side, queries, attended, mine, other):
    count = len(queries)
    rows = queries[0].shape[1]
    heads, _, size, hidden_size = mine.shape

    def body(side_ref, *refs):
        q_refs = refs[:count]
        attended_ref, mine_ref, other_ref, out_ref = refs[count:]
        held = side_ref[0] == pl.program_id(0) // heads
        gate, upper, down = (
            jnp.where(held, mine_ref[0, index], other_ref[0, index]) for index in range(3)
        )
        for index in range(count):
            where = slice(index * rows, (index + 1) * rows)
            query = q_refs[index][0].astype(F32)
            qnorm = query * lax.rsqrt(jnp.mean(query * query, axis=-1, keepdims=True) + 1e-06)
            qnorm = qnorm.astype(BF16)
            gate_pre = mm(qnorm, gate)
            hidden = gate_pre * sigmoid(gate_pre) * mm(qnorm, upper)
            out_ref[where] = (
                attended_ref[where] + mm(hidden.astype(BF16), down, ((1,), (1,)))
            ).astype(BF16)

    block = pl.BlockSpec((count * rows, size), lambda h, s: (0, h))
    matrices = pl.BlockSpec((1, 3, size, hidden_size), lambda h, s: (h % heads, 0, 0, 0))
    return call(
        body,
        (2 * heads,),
        [pl.BlockSpec((1, rows, size), lambda h, s: (0, 0, h))] * count
        + [block, matrices, matrices],
        block,
        jax.ShapeDtypeStruct((count * rows, 2 * heads * size), BF16),
    )(side, *queries, attended, mine, other)


def partial_out(ids, combined, w_out, columns):
    total_rows, depth = combined.shape
    rows = total_rows // lax.axis_size("head")
    count = ids.shape[0]
    width = w_out.shape[1]

    def body(ids_ref, combined_ref, w_ref, out_ref):
        left = jnp.concatenate(
            [
                combined_ref[pl.ds(pl.multiple_of(ids_ref[index] * rows, rows), rows)]
                for index in range(count)
            ],
            axis=0,
        )
        result = mm(left, w_ref[...]).astype(BF16)
        for index in range(count):
            out_ref[index] = result[index * rows : (index + 1) * rows]

    return call(
        body,
        (width // columns,),
        [fixed(combined.shape), pl.BlockSpec((depth, columns), lambda c, i: (0, c))],
        pl.BlockSpec((count, rows, columns), lambda c, i: (0, 0, c)),
        jax.ShapeDtypeStruct((count, rows, width), BF16),
    )(ids, combined, w_out)


def ring_reduce(combined, w_out):
    count = lax.axis_size("head")
    steps = count // 2
    half = w_out.shape[1] // 2
    farthest = partial_out(ring_ids([steps]), combined, w_out, half // 2)[0]
    offsets = [sign * step for step in range(steps - 1, 0, -1) for sign in (1, -1)] + [0]
    parts = partial_out(ring_ids(offsets), combined, w_out, half // 4)
    sides = (slice(0, half), slice(half, None))
    coming = {
        (1, 0): ring_send(farthest[:, sides[0]], 1),
        (-1, 1): ring_send(farthest[:, sides[1]], -1),
    }
    for index, offset in enumerate(offsets[:-1]):
        way = 1 if offset > 0 else -1
        for which in range(2):
            term = parts[index][:, sides[which]]
            if (way, which) in coming:
                term = (term.astype(F32) + coming[way, which].astype(F32)).astype(BF16)
            coming[way, which] = ring_send(term, way)
    own = parts[len(offsets) - 1]
    ends = []
    for which in range(2):
        total = own[:, sides[which]].astype(F32)
        for way in (1, -1):
            if (way, which) in coming:
                total = total + coming[way, which].astype(F32)
        ends.append(total.astype(BF16))
    return jnp.concatenate(ends, axis=1)


def swap(value, bit):
    count = lax.axis_size("tok")
    return lax.ppermute(value, "tok", [(index, index ^ bit) for index in range(count)])


def shards(
    tokens, w_query, w_key, w_value, w_out, fast_gate, fast_up, fast_down, token_rate, head_step
):
    row_count = tokens.shape[0]
    local_heads, head_size, _ = fast_gate.shape
    head_count = lax.axis_size("head")
    tok_count = lax.axis_size("tok")
    rows = row_count // CHUNKS
    steps = head_count // 2
    place = lax.axis_index("tok").astype(jnp.int32)
    side = place % 2
    pair = local_heads // 2
    offsets = [0] + [sign * step for step in range(1, steps) for sign in (-1, 1)] + [steps]
    ids = ring_ids(offsets)
    zero = jnp.zeros((1,), jnp.int32)
    far_base = ((1 - side) * pair).reshape(1)
    near_base = (side * pair).reshape(1)

    chunks = [gather_pieces(tokens[c * rows : (c + 1) * rows]) for c in range(CHUNKS)]
    rates = [token_rate[c * rows : (c + 1) * rows] for c in range(CHUNKS)]
    nets = (fast_gate, fast_up, fast_down)
    kvs, halos, queries = [], [], []
    grads = None
    for c in range(CHUNKS):
        kv = project(ids, chunks[c], (w_key, w_value))
        halos.append(
            lax.ppermute(kv, "tok", [(index, index + 1) for index in range(tok_count - 1)])
        )
        kvs.append(kv)
        if c < CHUNKS - 1:
            grads = head_grads(zero, local_heads, kv, rates[c], *nets, grads)
        else:
            far = head_grads(far_base, pair, kv, rates[c], *nets, grads)
            near = head_grads(near_base, pair, kv, rates[c], *nets, grads)
        queries.append(project(ids, chunks[c], (w_query,)))
    near = near + swap(far.astype(BF16), 1).astype(F32)
    received = []
    for bit in range(1, tok_count.bit_length() - 1):
        travel = near
        for more in received:
            travel = travel + more.astype(F32)
        received.append(swap(travel.astype(BF16), 1 << bit))
    attended = attend(place.reshape(1), queries, kvs, halos, head_size)
    mine = renew(near_base, near, received, head_step, *nets)
    other = swap(mine, 1)
    combined = apply_fast(side.reshape(1), queries, attended, mine, other)
    return ring_reduce(combined, w_out)


def solution(mesh):
    placed = (
        P("tok", "head"),
        P(None, "head"),
        P(None, "head"),
        P(None, "head"),
        P("head", None),
        P("head", None, None),
        P("head", None, None),
        P("head", None, None),
        P("tok", "head"),
        P("head"),
    )
    return jax.shard_map(
        shards, mesh=mesh, in_specs=placed, out_specs=P(("tok", "head"), None), check_vma=False
    )
```

time: 267 us -> 181 us (0.68)
  the two profiles are of different devices: /device:TPU:1 before, /device:TPU:0 now
where the time goes in v1:
time: 181 us; the launch traced here: 179 us
  waiting for transfers between devices  56.5 us (31%)
  Pallas kernels  53 us (29%)
  starting transfers between devices  39.2 us (22%)
  local copies, waits for them, and re-layouts  27.2 us (15%)
  other arithmetic  2.82 us (2%)
    ppermute x30, waiting for transfers between devices, ring_send(): lax.ppermute(value, 'head', [(order[i], order[(i + step) % count]) for i...  51 us
    ppermute x30, starting transfers between devices, ring_send(): lax.ppermute(value, 'head', [(order[i], order[(i + step) % count]) for i...  32.9 us
    pallas_call x4, Pallas kernels, project(): call(body, (count,), [fixed(piece.shape) for piece in pieces] + [pl.Block...  29.3 us
    unnamed x92, local copies, waits for them, and re-layouts  22.7 us
    pallas_call x2, Pallas kernels, partial_out(): call(body, (width // columns,), [fixed(combined.shape), pl.BlockSpec((dep...  8.58 us
    ppermute x3, waiting for transfers between devices, swap(): lax.ppermute(value, 'tok', [(index, index ^ bit) for index in range(count)])  5.52 us
    pallas_call x3, Pallas kernels, head_grads(): call(body, (heads,), specs, pl.BlockSpec((1, 3, size, hidden_size), lambd...  4.73 us
    pallas_call x1, Pallas kernels, attend(): call(body, (heads,), [spec(0)] * count + [spec(0)] * (2 * count) + [spec(...  4.62 us
  transfers between devices with their start and end apart: 35, of which 18 were waited for; matrix products, arithmetic and copies ran while one was open for 3% of the time, Pallas kernels for 17%

profile of v1, /device:TPU:0, one launch (start us, length us, event | category | flops | bytes accessed | tf_op | source)
XLA Modules:
  0.0 179.3 jit_solution(16261522348060064953)
XLA Ops:
  0.0 1.1 fusion.2
  1.1 3.1 %collective-permute-start = (bf16[256,512]{1,0:T(8,128)(2,1)S(1)}, bf16[256,512]{1,0:T(8,128)(2,1)S(1)}, u32[]{:S(2)}, u32[]{:S(2)}) collective-permute-start(bf16[256,512]{1,0:T(8,128)(2,1)S(1)} %get-tuple-element.27.refs_0_), channel_id=1, source_target_pairs={{0,2},{2,4},{4,6},{6,7},{7,5},{5,3},{3,1},{1,0},{8,10},{10,12},{12... | collective-permute-start | bytes 786440 | tf_op jit(solution)/shard_map/ppermute | solution.py:51
  4.2 2.0 %collective-permute-start.8 = (bf16[256,512]{1,0:T(8,128)(2,1)S(1)}, bf16[256,512]{1,0:T(8,128)(2,1)S(1)}, u32[]{:S(2)}, u32[]{:S(2)}) collective-permute-start(bf16[256,512]{1,0:T(8,128)(2,1)S(1)} %get-tuple-element.26.refs_0_), channel_id=1, source_target_pairs={{0,2},{2,4},{4,6},{6,7},{7,5},{5,3},{3,1},{1,0},{8,10},{10,12},{12... | collective-permute-start | bytes 786440 | tf_op jit(solution)/shard_map/ppermute | solution.py:51
  6.2 5.0 %collective-permute-done.refs_1_ = bf16[256,512]{1,0:T(8,128)(2,1)S(1)} collective-permute-done((bf16[256,512]{1,0:T(8,128)(2,1)S(1)}, bf16[256,512]{1,0:T(8,128)(2,1)S(1)}, u32[]{:S(2)}, u32[]{:S(2)}) %collective-permute-start) | collective-permute-done | bytes 262176 | tf_op jit(solution)/shard_map/ppermute | solution.py:51
  11.2 2.1 %collective-permute-start.2 = (bf16[256,512]{1,0:T(8,128)(2,1)S(1)}, bf16[256,512]{1,0:T(8,128)(2,1)S(1)}, u32[]{:S(2)}, u32[]{:S(2)}) collective-permute-start(bf16[256,512]{1,0:T(8,128)(2,1)S(1)} %collective-permute-done.refs_1_), channel_id=1, source_target_pairs={{0,2},{2,4},{4,6},{6,7},{7,5},{5,3},{3,1},{1,0},{8,10},{10,12},{12... | collective-permute-start | bytes 786440 | tf_op jit(solution)/shard_map/ppermute | solution.py:51
  13.4 3.4 %collective-permute-done.8.refs_1_ = bf16[256,512]{1,0:T(8,128)(2,1)S(1)} collective-permute-done((bf16[256,512]{1,0:T(8,128)(2,1)S(1)}, bf16[256,512]{1,0:T(8,128)(2,1)S(1)}, u32[]{:S(2)}, u32[]{:S(2)}) %collective-permute-start.8) | collective-permute-done | bytes 262176 | tf_op jit(solution)/shard_map/ppermute | solution.py:51
  16.8 2.1 %collective-permute-start.10 = (bf16[256,512]{1,0:T(8,128)(2,1)S(1)}, bf16[256,512]{1,0:T(8,128)(2,1)S(1)}, u32[]{:S(2)}, u32[]{:S(2)}) collective-permute-start(bf16[256,512]{1,0:T(8,128)(2,1)S(1)} %collective-permute-done.8.refs_1_), channel_id=1, source_target_pairs={{0,2},{2,4},{4,6},{6,7},{7,5},{5,3},{3,1},{1,0},{8,10},{10,12},{12... | collective-permute-start | bytes 786440 | tf_op jit(solution)/shard_map/ppermute | solution.py:51
  20.4 2.0 %collective-permute-done.2.refs_3_ = bf16[256,512]{1,0:T(8,128)(2,1)S(1)} collective-permute-done((bf16[256,512]{1,0:T(8,128)(2,1)S(1)}, bf16[256,512]{1,0:T(8,128)(2,1)S(1)}, u32[]{:S(2)}, u32[]{:S(2)}) %collective-permute-start.2) | collective-permute-done | bytes 262176 | tf_op jit(solution)/shard_map/ppermute | solution.py:51
  22.4 2.1 %collective-permute-start.4 = (bf16[256,512]{1,0:T(8,128)(2,1)S(1)}, bf16[256,512]{1,0:T(8,128)(2,1)S(1)}, u32[]{:S(2)}, u32[]{:S(2)}) collective-permute-start(bf16[256,512]{1,0:T(8,128)(2,1)S(1)} %collective-permute-done.2.refs_3_), channel_id=1, source_target_pairs={{0,2},{2,4},{4,6},{6,7},{7,5},{5,3},{3,1},{1,0},{8,10},{10,12},{12... | collective-permute-start | bytes 786440 | tf_op jit(solution)/shard_map/ppermute | solution.py:51
  25.3 2.7 %collective-permute-done.10.refs_3_ = bf16[256,512]{1,0:T(8,128)(2,1)S(1)} collective-permute-done((bf16[256,512]{1,0:T(8,128)(2,1)S(1)}, bf16[256,512]{1,0:T(8,128)(2,1)S(1)}, u32[]{:S(2)}, u32[]{:S(2)}) %collective-permute-start.10) | collective-permute-done | bytes 262176 | tf_op jit(solution)/shard_map/ppermute | solution.py:51
  28.1 2.1 %collective-permute-start.12 = (bf16[256,512]{1,0:T(8,128)(2,1)S(1)}, bf16[256,512]{1,0:T(8,128)(2,1)S(1)}, u32[]{:S(2)}, u32[]{:S(2)}) collective-permute-start(bf16[256,512]{1,0:T(8,128)(2,1)S(1)} %collective-permute-done.10.refs_3_), channel_id=1, source_target_pairs={{0,2},{2,4},{4,6},{6,7},{7,5},{5,3},{3,1},{1,0},{8,10},{10,12},{12... | collective-permute-start | bytes 786440 | tf_op jit(solution)/shard_map/ppermute | solution.py:51
  31.6 2.0 %collective-permute-done.4.refs_5_ = bf16[256,512]{1,0:T(8,128)(2,1)S(1)} collective-permute-done((bf16[256,512]{1,0:T(8,128)(2,1)S(1)}, bf16[256,512]{1,0:T(8,128)(2,1)S(1)}, u32[]{:S(2)}, u32[]{:S(2)}) %collective-permute-start.4) | collective-permute-done | bytes 262176 | tf_op jit(solution)/shard_map/ppermute | solution.py:51
  34.4 2.1 %collective-permute-start.6 = (bf16[128,512]{1,0:T(8,128)(2,1)}, bf16[128,512]{1,0:T(8,128)(2,1)}, u32[]{:S(2)}, u32[]{:S(2)}) collective-permute-start(bf16[128,512]{1,0:T(8,128)(2,1)} %slice.130), channel_id=1, source_target_pairs={{0,2},{2,4},{4,6},{6,7},{7,5},{5,3},{3,1},{1,0},{8,10},{10,12},{12... | collective-permute-start | bytes 393224 | tf_op jit(solution)/shard_map/ppermute | solution.py:51
  36.6 2.7 %collective-permute-done.12.refs_5_ = bf16[256,512]{1,0:T(8,128)(2,1)S(1)} collective-permute-done((bf16[256,512]{1,0:T(8,128)(2,1)S(1)}, bf16[256,512]{1,0:T(8,128)(2,1)S(1)}, u32[]{:S(2)}, u32[]{:S(2)}) %collective-permute-start.12) | collective-permute-done | bytes 262176 | tf_op jit(solution)/shard_map/ppermute | solution.py:51
  40.0 2.1 %collective-permute-start.14 = (bf16[128,512]{1,0:T(8,128)(2,1)}, bf16[128,512]{1,0:T(8,128)(2,1)}, u32[]{:S(2)}, u32[]{:S(2)}) collective-permute-start(bf16[128,512]{1,0:T(8,128)(2,1)} %slice.132), channel_id=1, source_target_pairs={{0,2},{2,4},{4,6},{6,7},{7,5},{5,3},{3,1},{1,0},{8,10},{10,12},{12... | collective-permute-start | bytes 393224 | tf_op jit(solution)/shard_map/ppermute | solution.py:51
  45.3 0.9 copy-done.34
  47.2 8.0 %shard_map.102.refs_4_.refs_8_.k_ref.v_ref = bf16[2,256,512]{2,1,0:T(8,128)(2,1)S(1)} custom-call(s32[8]{0:T(128)S(1)} %stack.47.ids_ref, bf16[256,512]{1,0:T(8,128)(2,1)S(1)} %get-tuple-element.27.refs_0_, bf16[256,512]{1,0:T(8,128)(2,1)S(1)} %collective-permute-done.refs_1_, bf16[256,512]{1,0:T(8,128)(2,1)S(1)} %collective-permute-done.1.refs_2_, ...), custom_call_target="tpu_custom_call" | custom-call | tf_op jit(solution)/shard_map/pallas_call | solution.py:109
  56.7 2.3 %shard_map.105.rest_0_ = f32[4,3,128,256]{3,2,1,0:T(8,128)S(1)} custom-call(s32[1]{0:T(128)} %constant.117.clone.1.base_ref, bf16[2,256,512]{2,1,0:T(8,128)(2,1)S(1)} %shard_map.102.refs_4_.refs_8_.k_ref.v_ref, bf16[2,256,512]{2,1,0:T(8,128)(2,1)S(1)} %shard_map.102.refs_4_.refs_8_.k_ref.v_ref, f32[256,4]{1,0:T(8,128)S(1)} %copy-done.42, ...), custom_call_target="tpu_custom_call" | custom-call | tf_op jit(solution)/shard_map/pallas_call | solution.py:167
  59.1 8.1 %shard_map.103.refs_5_.refs_9_.k_ref.v_ref = bf16[2,256,512]{2,1,0:T(8,128)(2,1)S(1)} custom-call(s32[8]{0:T(128)S(1)} %stack.47.ids_ref, bf16[256,512]{1,0:T(8,128)(2,1)S(1)} %get-tuple-element.26.refs_0_, bf16[256,512]{1,0:T(8,128)(2,1)S(1)} %copy-done.19, bf16[256,512]{1,0:T(8,128)(2,1)S(1)} %copy-done.24, bf16[256,512]{1,0:T(8,128)(2,1)S(1)} %copy-done.31, ...), custom_call_target="tpu_custom_call" | custom-call | tf_op jit(solution)/shard_map/pallas_call | solution.py:109
  67.2 1.2 shard_map.107
  69.3 1.0 copy-done.3
  70.3 1.0 copy-done.5
  71.3 1.2 shard_map.106
  72.6 1.2 fusion
  73.7 2.0 %collective-permute-start.19 = (bf16[2,3,128,256]{3,2,1,0:T(8,128)(2,1)S(1)}, bf16[2,3,128,256]{3,2,1,0:T(8,128)(2,1)S(1)}, u32[]{:S(2)}, u32[]{:S(2)}) collective-permute-start(bf16[2,3,128,256]{3,2,1,0:T(8,128)(2,1)S(1)} %get-tuple-element.5), channel_id=1, source_target_pairs={{0,16},{8,24},{16,0},{24,8},{1,17},{9,25},{17,1},{25,9},{2,18},{10... | collective-permute-start | bytes 1179656 | tf_op jit(solution)/shard_map/ppermute | solution.py:353
  75.8 2.2 %collective-permute-start.16 = (bf16[2,256,512]{2,1,0:T(8,128)(2,1)S(1)}, bf16[2,256,512]{2,1,0:T(8,128)(2,1)S(1)}, u32[]{:S(2)}, u32[]{:S(2)}) collective-permute-start(bf16[2,256,512]{2,1,0:T(8,128)(2,1)S(1)} %shard_map.102.refs_4_.refs_8_.k_ref.v_ref), channel_id=1, source_target_pairs={{0,8},{8,16},{16,24},{1,9},{9,17},{17,25},{2,10},{10,18},{18,26},{... | collective-permute-start | bytes 1572872 | tf_op jit(solution)/shard_map/ppermute | solution.py:382
  77.9 2.1 %collective-permute-start.17 = (bf16[2,256,512]{2,1,0:T(8,128)(2,1)S(1)}, bf16[2,256,512]{2,1,0:T(8,128)(2,1)S(1)}, u32[]{:S(2)}, u32[]{:S(2)}) collective-permute-start(bf16[2,256,512]{2,1,0:T(8,128)(2,1)S(1)} %shard_map.103.refs_5_.refs_9_.k_ref.v_ref), channel_id=1, source_target_pairs={{0,8},{8,16},{16,24},{1,9},{9,17},{17,25},{2,10},{10,18},{18,26},{... | collective-permute-start | bytes 1572872 | tf_op jit(solution)/shard_map/ppermute | solution.py:382
  80.0 5.5 %collective-permute-done.19.rest_0_ = bf16[2,3,128,256]{3,2,1,0:T(8,128)(2,1)S(1)} collective-permute-done((bf16[2,3,128,256]{3,2,1,0:T(8,128)(2,1)S(1)}, bf16[2,3,128,256]{3,2,1,0:T(8,128)(2,1)S(1)}, u32[]{:S(2)}, u32[]{:S(2)}) %collective-permute-start.19) | collective-permute-done | bytes 393248 | tf_op jit(solution)/shard_map/ppermute | solution.py:353
  85.6 1.7 shard_map.108.refs_3_
  87.4 0.9 copy-done.9
  88.3 0.9 copy-done.14
  89.3 0.9 copy-done.22
  90.2 0.9 copy-done.27
  91.2 0.9 copy-done.29
  92.1 0.9 copy-done.35
  93.1 6.6 %shard_map.100.refs_0_ = bf16[1,256,512]{2,1,0:T(8,128)(2,1)S(1)} custom-call(s32[8]{0:T(128)S(1)} %stack.47.ids_ref, bf16[256,512]{1,0:T(8,128)(2,1)S(1)} %copy-done.7, bf16[256,512]{1,0:T(8,128)(2,1)S(1)} %copy-done.22, bf16[256,512]{1,0:T(8,128)(2,1)S(1)} %copy-done.27, bf16[256,512]{1,0:T(8,128)(2,1)S(1)} %copy-done.29, bf16[256,512]{1,0:T(8,128)(2,1)S(1)} %copy-done.35, ...), custom_call_target="tpu_custom_call" | custom-call | tf_op jit(solution)/shard_map/pallas_call | solution.py:109
  99.7 0.9 copy-done.12
  100.6 0.9 copy-done.17
  101.6 0.9 copy-done.20
  102.5 0.9 copy-done.25
  103.5 0.9 copy-done.32
  104.4 0.9 copy-done.38
  105.4 6.6 %shard_map.101.refs_1_ = bf16[1,256,512]{2,1,0:T(8,128)(2,1)S(1)} custom-call(s32[8]{0:T(128)S(1)} %stack.47.ids_ref, bf16[256,512]{1,0:T(8,128)(2,1)S(1)} %get-tuple-element.26.refs_0_, bf16[256,512]{1,0:T(8,128)(2,1)S(1)} %copy-done.20, bf16[256,512]{1,0:T(8,128)(2,1)S(1)} %copy-done.25, bf16[256,512]{1,0:T(8,128)(2,1)S(1)} %copy-done.32, ...), custom_call_target="tpu_custom_call" | custom-call | tf_op jit(solution)/shard_map/pallas_call | solution.py:109
  112.0 4.6 %shard_map.104.refs_2_ = f32[512,512]{1,0:T(8,128)S(1)} custom-call(s32[1]{0:T(128)} %bitcast.9.place_ref, bf16[1,256,512]{2,1,0:T(8,128)(2,1)S(1)} %shard_map.100.refs_0_, bf16[1,256,512]{2,1,0:T(8,128)(2,1)S(1)} %shard_map.101.refs_1_, bf16[2,256,512]{2,1,0:T(8,128)(2,1)S(1)} %collective-permute-done.16.refs_2_.refs_6_, ...), custom_call_target="tpu_custom_call" | custom-call | tf_op jit(solution)/shard_map/pallas_call | solution.py:250
  116.6 4.0 %shard_map.109.combined_ref = bf16[512,512]{1,0:T(8,128)(2,1)S(1)} custom-call(s32[1]{0:T(128)} %bitcast.7.side_ref, bf16[1,256,512]{2,1,0:T(8,128)(2,1)S(1)} %shard_map.100.refs_0_, bf16[1,256,512]{2,1,0:T(8,128)(2,1)S(1)} %shard_map.101.refs_1_, f32[512,512]{1,0:T(8,128)S(1)} %shard_map.104.refs_2_, bf16[2,3,128,256]{3,2,1,0:T(8,128)(2,1)} %shard_map.108.refs_3_, ...), custom_call_target="tpu_custom_call" | custom-call | tf_op jit(solution)/shard_map/pallas_call | solution.py:284
  120.7 1.6 shard_map.111
  122.3 7.0 %shard_map.110 = bf16[7,64,4096]{2,1,0:T(8,128)(2,1)S(1)} custom-call(s32[7]{0:T(128)S(1)} %stack.45.ids_ref, bf16[512,512]{1,0:T(8,128)(2,1)S(1)} %shard_map.109.combined_ref, bf16[512,4096]{1,0:T(8,128)(2,1)} %w_ref.3), custom_call_target="tpu_custom_call" | custom-call | tf_op jit(solution)/shard_map/pallas_call | solution.py:312
  129.3 1.7 collective-permute-start.31
  131.5 1.7 collective-permute-start.25
  134.0 4.5 %collective-permute-done.31 = bf16[64,2048]{1,0:T(8,128)(2,1)S(1)} collective-permute-done((bf16[64,2048]{1,0:T(8,128)(2,1)S(1)}, bf16[64,2048]{1,0:T(8,128)(2,1)S(1)}, u32[]{:S(2)}, u32[]{:S(2)}) %collective-permute-start.31) | collective-permute-done | bytes 262176 | tf_op jit(solution)/shard_map/ppermute | solution.py:51
  138.5 1.8 collective-permute-start.32
  140.3 2.0 %collective-permute-done.21 = bf16[64,2048]{1,0:T(8,128)(2,1)S(1)} collective-permute-done((bf16[64,2048]{1,0:T(8,128)(2,1)S(1)}, bf16[64,2048]{1,0:T(8,128)(2,1)S(1)}, u32[]{:S(2)}, u32[]{:S(2)}) %collective-permute-start.21) | collective-permute-done | bytes 262176 | tf_op jit(solution)/shard_map/ppermute | solution.py:51
  142.9 1.2 collective-permute-done.25
  144.1 5.3 %collective-permute-done.32 = bf16[64,2048]{1,0:T(8,128)(2,1)S(1)} collective-permute-done((bf16[64,2048]{1,0:T(8,128)(2,1)S(1)}, bf16[64,2048]{1,0:T(8,128)(2,1)S(1)}, u32[]{:S(2)}, u32[]{:S(2)}) %collective-permute-start.32) | collective-permute-done | bytes 262176 | tf_op jit(solution)/shard_map/ppermute | solution.py:51
  149.5 1.7 collective-permute-start.26
  151.2 1.6 collective-permute-start.33
  153.8 5.0 %collective-permute-done.26 = bf16[64,2048]{1,0:T(8,128)(2,1)S(1)} collective-permute-done((bf16[64,2048]{1,0:T(8,128)(2,1)S(1)}, bf16[64,2048]{1,0:T(8,128)(2,1)S(1)}, u32[]{:S(2)}, u32[]{:S(2)}) %collective-permute-start.26) | collective-permute-done | bytes 262176 | tf_op jit(solution)/shard_map/ppermute | solution.py:51
  158.8 4.4 %collective-permute-done.33 = bf16[64,2048]{1,0:T(8,128)(2,1)S(1)} collective-permute-done((bf16[64,2048]{1,0:T(8,128)(2,1)S(1)}, bf16[64,2048]{1,0:T(8,128)(2,1)S(1)}, u32[]{:S(2)}, u32[]{:S(2)}) %collective-permute-start.33) | collective-permute-done | bytes 262176 | tf_op jit(solution)/shard_map/ppermute | solution.py:51
  163.3 1.7 collective-permute-start.27
  165.0 1.0 collective-permute-done.29
  166.7 1.5 collective-permute-start.34
  168.7 3.9 %collective-permute-done.27 = bf16[64,2048]{1,0:T(8,128)(2,1)S(1)} collective-permute-done((bf16[64,2048]{1,0:T(8,128)(2,1)S(1)}, bf16[64,2048]{1,0:T(8,128)(2,1)S(1)}, u32[]{:S(2)}, u32[]{:S(2)}) %collective-permute-start.27) | collective-permute-done | bytes 262176 | tf_op jit(solution)/shard_map/ppermute | solution.py:51
  172.6 2.8 %collective-permute-done.24 = bf16[64,2048]{1,0:T(8,128)(2,1)S(1)} collective-permute-done((bf16[64,2048]{1,0:T(8,128)(2,1)S(1)}, bf16[64,2048]{1,0:T(8,128)(2,1)S(1)}, u32[]{:S(2)}, u32[]{:S(2)}) %collective-permute-start.24) | collective-permute-done | bytes 262176 | tf_op jit(solution)/shard_map/ppermute | solution.py:51
  176.1 2.1 %collective-permute-done.30 = bf16[64,2048]{1,0:T(8,128)(2,1)S(1)} collective-permute-done((bf16[64,2048]{1,0:T(8,128)(2,1)S(1)}, bf16[64,2048]{1,0:T(8,128)(2,1)S(1)}, u32[]{:S(2)}, u32[]{:S(2)}) %collective-permute-start.30) | collective-permute-done | bytes 262176 | tf_op jit(solution)/shard_map/ppermute | solution.py:51
  (132 shorter events, 17.5 us)
Async XLA Ops:
  1.1 54.1 %copy-start.6 = (bf16[256,512]{1,0:T(8,128)(2,1)}, bf16[256,512]{1,0:T(8,128)(2,1)S(1)}, u32[]{:S(2)}) copy-start(bf16[256,512]{1,0:T(8,128)(2,1)S(1)} %get-tuple-element.27.refs_0_) | copy-start | bytes 786436
  1.1 10.1 %collective-permute-start = (bf16[256,512]{1,0:T(8,128)(2,1)S(1)}, bf16[256,512]{1,0:T(8,128)(2,1)S(1)}, u32[]{:S(2)}, u32[]{:S(2)}) collective-permute-start(bf16[256,512]{1,0:T(8,128)(2,1)S(1)} %get-tuple-element.27.refs_0_), channel_id=1, source_target_pairs={{0,2},{2,4},{4,6},{6,7},{7,5},{5,3},{3,1},{1,0},{8,10},{10,12},{12... | collective-permute-start | bytes 786440 | tf_op jit(solution)/shard_map/ppermute | solution.py:51
  4.2 9.2 %collective-permute-start.1 = (bf16[256,512]{1,0:T(8,128)(2,1)S(1)}, bf16[256,512]{1,0:T(8,128)(2,1)S(1)}, u32[]{:S(2)}, u32[]{:S(2)}) collective-permute-start(bf16[256,512]{1,0:T(8,128)(2,1)S(1)} %get-tuple-element.27.refs_0_), channel_id=1, source_target_pairs={{0,1},{2,0},{4,2},{6,4},{7,6},{5,7},{3,5},{1,3},{8,9},{10,8},{12,1... | collective-permute-start | bytes 786440 | tf_op jit(solution)/shard_map/ppermute | solution.py:51
  4.2 12.7 %collective-permute-start.8 = (bf16[256,512]{1,0:T(8,128)(2,1)S(1)}, bf16[256,512]{1,0:T(8,128)(2,1)S(1)}, u32[]{:S(2)}, u32[]{:S(2)}) collective-permute-start(bf16[256,512]{1,0:T(8,128)(2,1)S(1)} %get-tuple-element.26.refs_0_), channel_id=1, source_target_pairs={{0,2},{2,4},{4,6},{6,7},{7,5},{5,3},{3,1},{1,0},{8,10},{10,12},{12... | collective-permute-start | bytes 786440 | tf_op jit(solution)/shard_map/ppermute | solution.py:51
  6.2 13.5 %collective-permute-start.9 = (bf16[256,512]{1,0:T(8,128)(2,1)S(1)}, bf16[256,512]{1,0:T(8,128)(2,1)S(1)}, u32[]{:S(2)}, u32[]{:S(2)}) collective-permute-start(bf16[256,512]{1,0:T(8,128)(2,1)S(1)} %get-tuple-element.26.refs_0_), channel_id=1, source_target_pairs={{0,1},{2,0},{4,2},{6,4},{7,6},{5,7},{3,5},{1,3},{8,9},{10,8},{12,1... | collective-permute-start | bytes 786440 | tf_op jit(solution)/shard_map/ppermute | solution.py:51
  11.2 11.2 %collective-permute-start.2 = (bf16[256,512]{1,0:T(8,128)(2,1)S(1)}, bf16[256,512]{1,0:T(8,128)(2,1)S(1)}, u32[]{:S(2)}, u32[]{:S(2)}) collective-permute-start(bf16[256,512]{1,0:T(8,128)(2,1)S(1)} %collective-permute-done.refs_1_), channel_id=1, source_target_pairs={{0,2},{2,4},{4,6},{6,7},{7,5},{5,3},{3,1},{1,0},{8,10},{10,12},{12... | collective-permute-start | bytes 786440 | tf_op jit(solution)/shard_map/ppermute | solution.py:51
  13.4 11.2 %collective-permute-start.3 = (bf16[256,512]{1,0:T(8,128)(2,1)S(1)}, bf16[256,512]{1,0:T(8,128)(2,1)S(1)}, u32[]{:S(2)}, u32[]{:S(2)}) collective-permute-start(bf16[256,512]{1,0:T(8,128)(2,1)S(1)} %collective-permute-done.1.refs_2_), channel_id=1, source_target_pairs={{0,1},{2,0},{4,2},{6,4},{7,6},{5,7},{3,5},{1,3},{8,9},{10,8},{12,1... | collective-permute-start | bytes 786440 | tf_op jit(solution)/shard_map/ppermute | solution.py:51
  16.8 11.2 %collective-permute-start.10 = (bf16[256,512]{1,0:T(8,128)(2,1)S(1)}, bf16[256,512]{1,0:T(8,128)(2,1)S(1)}, u32[]{:S(2)}, u32[]{:S(2)}) collective-permute-start(bf16[256,512]{1,0:T(8,128)(2,1)S(1)} %collective-permute-done.8.refs_1_), channel_id=1, source_target_pairs={{0,2},{2,4},{4,6},{6,7},{7,5},{5,3},{3,1},{1,0},{8,10},{10,12},{12... | collective-permute-start | bytes 786440 | tf_op jit(solution)/shard_map/ppermute | solution.py:51
  19.7 11.2 %collective-permute-start.11 = (bf16[256,512]{1,0:T(8,128)(2,1)S(1)}, bf16[256,512]{1,0:T(8,128)(2,1)S(1)}, u32[]{:S(2)}, u32[]{:S(2)}) collective-permute-start(bf16[256,512]{1,0:T(8,128)(2,1)S(1)} %collective-permute-done.9.refs_2_), channel_id=1, source_target_pairs={{0,1},{2,0},{4,2},{6,4},{7,6},{5,7},{3,5},{1,3},{8,9},{10,8},{12,1... | collective-permute-start | bytes 786440 | tf_op jit(solution)/shard_map/ppermute | solution.py:51
  22.4 22.2 %copy-start.28 = (bf16[256,512]{1,0:T(8,128)(2,1)}, bf16[256,512]{1,0:T(8,128)(2,1)S(1)}, u32[]{:S(2)}) copy-start(bf16[256,512]{1,0:T(8,128)(2,1)S(1)} %collective-permute-done.2.refs_3_) | copy-start | bytes 786436
  22.4 11.2 %collective-permute-start.4 = (bf16[256,512]{1,0:T(8,128)(2,1)S(1)}, bf16[256,512]{1,0:T(8,128)(2,1)S(1)}, u32[]{:S(2)}, u32[]{:S(2)}) collective-permute-start(bf16[256,512]{1,0:T(8,128)(2,1)S(1)} %collective-permute-done.2.refs_3_), channel_id=1, source_target_pairs={{0,2},{2,4},{4,6},{6,7},{7,5},{5,3},{3,1},{1,0},{8,10},{10,12},{12... | collective-permute-start | bytes 786440 | tf_op jit(solution)/shard_map/ppermute | solution.py:51
  24.6 11.9 %collective-permute-start.5 = (bf16[256,512]{1,0:T(8,128)(2,1)S(1)}, bf16[256,512]{1,0:T(8,128)(2,1)S(1)}, u32[]{:S(2)}, u32[]{:S(2)}) collective-permute-start(bf16[256,512]{1,0:T(8,128)(2,1)S(1)} %collective-permute-done.3.refs_4_), channel_id=1, source_target_pairs={{0,1},{2,0},{4,2},{6,4},{7,6},{5,7},{3,5},{1,3},{8,9},{10,8},{12,1... | collective-permute-start | bytes 786440 | tf_op jit(solution)/shard_map/ppermute | solution.py:51
  28.1 11.2 %collective-permute-start.12 = (bf16[256,512]{1,0:T(8,128)(2,1)S(1)}, bf16[256,512]{1,0:T(8,128)(2,1)S(1)}, u32[]{:S(2)}, u32[]{:S(2)}) collective-permute-start(bf16[256,512]{1,0:T(8,128)(2,1)S(1)} %collective-permute-done.10.refs_3_), channel_id=1, source_target_pairs={{0,2},{2,4},{4,6},{6,7},{7,5},{5,3},{3,1},{1,0},{8,10},{10,12},{12... | collective-permute-start | bytes 786440 | tf_op jit(solution)/shard_map/ppermute | solution.py:51
  30.9 11.2 %collective-permute-start.13 = (bf16[256,512]{1,0:T(8,128)(2,1)S(1)}, bf16[256,512]{1,0:T(8,128)(2,1)S(1)}, u32[]{:S(2)}, u32[]{:S(2)}) collective-permute-start(bf16[256,512]{1,0:T(8,128)(2,1)S(1)} %collective-permute-done.11.refs_4_), channel_id=1, source_target_pairs={{0,1},{2,0},{4,2},{6,4},{7,6},{5,7},{3,5},{1,3},{8,9},{10,8},{12,1... | collective-permute-start | bytes 786440 | tf_op jit(solution)/shard_map/ppermute | solution.py:51
  33.7 21.5 %copy-start.8 = (bf16[256,512]{1,0:T(8,128)(2,1)}, bf16[256,512]{1,0:T(8,128)(2,1)S(1)}, u32[]{:S(2)}) copy-start(bf16[256,512]{1,0:T(8,128)(2,1)S(1)} %collective-permute-done.4.refs_5_) | copy-start | bytes 786436
  34.4 10.2 %collective-permute-start.6 = (bf16[128,512]{1,0:T(8,128)(2,1)}, bf16[128,512]{1,0:T(8,128)(2,1)}, u32[]{:S(2)}, u32[]{:S(2)}) collective-permute-start(bf16[128,512]{1,0:T(8,128)(2,1)} %slice.130), channel_id=1, source_target_pairs={{0,2},{2,4},{4,6},{6,7},{7,5},{5,3},{3,1},{1,0},{8,10},{10,12},{12... | collective-permute-start | bytes 393224 | tf_op jit(solution)/shard_map/ppermute | solution.py:51
  36.5 8.1 %copy-start.13 = (bf16[256,512]{1,0:T(8,128)(2,1)}, bf16[256,512]{1,0:T(8,128)(2,1)S(1)}, u32[]{:S(2)}) copy-start(bf16[256,512]{1,0:T(8,128)(2,1)S(1)} %collective-permute-done.5.refs_6_) | copy-start | bytes 786436
  36.5 8.1 %collective-permute-start.7 = (bf16[128,512]{1,0:T(8,128)(2,1)S(1)}, bf16[128,512]{1,0:T(8,128)(2,1)S(1)}, u32[]{:S(2)}, u32[]{:S(2)}) collective-permute-start(bf16[128,512]{1,0:T(8,128)(2,1)S(1)} %slice.131), channel_id=1, source_target_pairs={{0,1},{2,0},{4,2},{6,4},{7,6},{5,7},{3,5},{1,3},{8,9},{10,8},{12,1... | collective-permute-start | bytes 393224 | tf_op jit(solution)/shard_map/ppermute | solution.py:51
  39.3 5.3 %copy-start.10 = (bf16[256,512]{1,0:T(8,128)(2,1)}, bf16[256,512]{1,0:T(8,128)(2,1)S(1)}, u32[]{:S(2)}) copy-start(bf16[256,512]{1,0:T(8,128)(2,1)S(1)} %collective-permute-done.12.refs_5_) | copy-start | bytes 786436
  40.0 19.1 %collective-permute-start.14 = (bf16[128,512]{1,0:T(8,128)(2,1)}, bf16[128,512]{1,0:T(8,128)(2,1)}, u32[]{:S(2)}, u32[]{:S(2)}) collective-permute-start(bf16[128,512]{1,0:T(8,128)(2,1)} %slice.132), channel_id=1, source_target_pairs={{0,2},{2,4},{4,6},{6,7},{7,5},{5,3},{3,1},{1,0},{8,10},{10,12},{12... | collective-permute-start | bytes 393224 | tf_op jit(solution)/shard_map/ppermute | solution.py:51
  42.1 2.5 %copy-start.15 = (bf16[256,512]{1,0:T(8,128)(2,1)}, bf16[256,512]{1,0:T(8,128)(2,1)S(1)}, u32[]{:S(2)}) copy-start(bf16[256,512]{1,0:T(8,128)(2,1)S(1)} %collective-permute-done.13.refs_6_) | copy-start | bytes 786436
  42.8 16.2 %collective-permute-start.15 = (bf16[128,512]{1,0:T(8,128)(2,1)}, bf16[128,512]{1,0:T(8,128)(2,1)}, u32[]{:S(2)}, u32[]{:S(2)}) collective-permute-start(bf16[128,512]{1,0:T(8,128)(2,1)} %slice.133), channel_id=1, source_target_pairs={{0,1},{2,0},{4,2},{6,4},{7,6},{5,7},{3,5},{1,3},{8,9},{10,8},{12,1... | collective-permute-start | bytes 393224 | tf_op jit(solution)/shard_map/ppermute | solution.py:51
  44.6 12.1 %copy-start.1 = (f32[4,128,256]{2,1,0:T(8,128)S(1)}, f32[4,128,256]{2,1,0:T(8,128)}, u32[]{:S(2)}) copy-start(f32[4,128,256]{2,1,0:T(8,128)} %gate_ref.7) | copy-start | bytes 1572868
  44.6 12.1 %copy-start.2 = (f32[4,128,256]{2,1,0:T(8,128)S(1)}, f32[4,128,256]{2,1,0:T(8,128)}, u32[]{:S(2)}) copy-start(f32[4,128,256]{2,1,0:T(8,128)} %up_ref.7) | copy-start | bytes 1572868
  44.6 12.1 %copy-start.4 = (f32[4,256,128]{2,1,0:T(8,128)S(1)}, f32[4,256,128]{2,1,0:T(8,128)}, u32[]{:S(2)}) copy-start(f32[4,256,128]{2,1,0:T(8,128)} %down_ref.7) | copy-start | bytes 1572868
  45.3 0.9 copy-start.34
  47.2 9.5 %copy-start.42 = (f32[256,4]{1,0:T(8,128)S(1)}, f32[256,4]{1,0:T(8,128)}, u32[]{:S(2)}) copy-start(f32[256,4]{1,0:T(8,128)} %copy.14.rate_ref) | copy-start | bytes 12292
  56.6 2.4 %copy-start.11 = (bf16[256,512]{1,0:T(8,128)(2,1)S(1)}, bf16[256,512]{1,0:T(8,128)(2,1)}, u32[]{:S(2)}) copy-start(bf16[256,512]{1,0:T(8,128)(2,1)} %copy-done.10) | copy-start | bytes 786436
  56.7 2.4 %copy-start.16 = (bf16[256,512]{1,0:T(8,128)(2,1)S(1)}, bf16[256,512]{1,0:T(8,128)(2,1)}, u32[]{:S(2)}) copy-start(bf16[256,512]{1,0:T(8,128)(2,1)} %copy-done.15) | copy-start | bytes 786436
  56.7 2.4 %copy-start.19 = (bf16[256,512]{1,0:T(8,128)(2,1)S(1)}, bf16[256,512]{1,0:T(8,128)(2,1)}, u32[]{:S(2)}) copy-start(bf16[256,512]{1,0:T(8,128)(2,1)} %copy-done.18) | copy-start | bytes 786436
  56.7 2.4 %copy-start.24 = (bf16[256,512]{1,0:T(8,128)(2,1)S(1)}, bf16[256,512]{1,0:T(8,128)(2,1)}, u32[]{:S(2)}) copy-start(bf16[256,512]{1,0:T(8,128)(2,1)} %copy-done.23) | copy-start | bytes 786436
  56.7 2.4 %copy-start.31 = (bf16[256,512]{1,0:T(8,128)(2,1)S(1)}, bf16[256,512]{1,0:T(8,128)(2,1)}, u32[]{:S(2)}) copy-start(bf16[256,512]{1,0:T(8,128)(2,1)} %copy-done.30) | copy-start | bytes 786436
  56.7 2.4 %copy-start.37 = (bf16[256,512]{1,0:T(8,128)(2,1)S(1)}, bf16[256,512]{1,0:T(8,128)(2,1)}, u32[]{:S(2)}) copy-start(bf16[256,512]{1,0:T(8,128)(2,1)} %copy-done.36) | copy-start | bytes 786436
  68.4 17.1 %copy-start.43 = (f32[4]{0:T(128)S(1)}, f32[4]{0:T(128)}, u32[]{:S(2)}) copy-start(f32[4]{0:T(128)} %step_ref.1) | copy-start | bytes 52
  69.2 3.3 %collective-permute-start.18 = (bf16[2,3,128,256]{3,2,1,0:T(8,128)(2,1)}, bf16[2,3,128,256]{3,2,1,0:T(8,128)(2,1)}, u32[]{:S(2)}, u32[]{:S(2)}) collective-permute-start(bf16[2,3,128,256]{3,2,1,0:T(8,128)(2,1)} %convert_element_type.123), channel_id=1, source_target_pairs={{0,8},{8,0},{16,24},{24,16},{1,9},{9,1},{17,25},{25,17},{2,10},{10... | collective-permute-start | bytes 1179656 | tf_op jit(solution)/shard_map/ppermute | solution.py:353
  69.2 1.0 copy-start.3
  70.3 1.0 copy-start.5
  72.5 14.9 %copy-start.7 = (bf16[256,512]{1,0:T(8,128)(2,1)S(1)}, bf16[256,512]{1,0:T(8,128)(2,1)}, u32[]{:S(2)}) copy-start(bf16[256,512]{1,0:T(8,128)(2,1)} %copy-done.6) | copy-start | bytes 786436
  72.5 14.8 %copy-start.41 = (bf16[128,512]{1,0:T(8,128)(2,1)S(1)}, bf16[128,512]{1,0:T(8,128)(2,1)}, u32[]{:S(2)}) copy-start(bf16[128,512]{1,0:T(8,128)(2,1)} %copy-done.39) | copy-start | bytes 393220
  73.7 11.8 %collective-permute-start.19 = (bf16[2,3,128,256]{3,2,1,0:T(8,128)(2,1)S(1)}, bf16[2,3,128,256]{3,2,1,0:T(8,128)(2,1)S(1)}, u32[]{:S(2)}, u32[]{:S(2)}) collective-permute-start(bf16[2,3,128,256]{3,2,1,0:T(8,128)(2,1)S(1)} %get-tuple-element.5), channel_id=1, source_target_pairs={{0,16},{8,24},{16,0},{24,8},{1,17},{9,25},{17,1},{25,9},{2,18},{10... | collective-permute-start | bytes 1179656 | tf_op jit(solution)/shard_map/ppermute | solution.py:353
  75.8 36.2 %collective-permute-start.16 = (bf16[2,256,512]{2,1,0:T(8,128)(2,1)S(1)}, bf16[2,256,512]{2,1,0:T(8,128)(2,1)S(1)}, u32[]{:S(2)}, u32[]{:S(2)}) collective-permute-start(bf16[2,256,512]{2,1,0:T(8,128)(2,1)S(1)} %shard_map.102.refs_4_.refs_8_.k_ref.v_ref), channel_id=1, source_target_pairs={{0,8},{8,16},{16,24},{1,9},{9,17},{17,25},{2,10},{10,18},{18,26},{... | collective-permute-start | bytes 1572872 | tf_op jit(solution)/shard_map/ppermute | solution.py:382
  77.9 34.1 %collective-permute-start.17 = (bf16[2,256,512]{2,1,0:T(8,128)(2,1)S(1)}, bf16[2,256,512]{2,1,0:T(8,128)(2,1)S(1)}, u32[]{:S(2)}, u32[]{:S(2)}) collective-permute-start(bf16[2,256,512]{2,1,0:T(8,128)(2,1)S(1)} %shard_map.103.refs_5_.refs_9_.k_ref.v_ref), channel_id=1, source_target_pairs={{0,8},{8,16},{16,24},{1,9},{9,17},{17,25},{2,10},{10,18},{18,26},{... | collective-permute-start | bytes 1572872 | tf_op jit(solution)/shard_map/ppermute | solution.py:382
  87.3 29.3 %collective-permute-start.20 = (bf16[2,3,128,256]{3,2,1,0:T(8,128)(2,1)}, bf16[2,3,128,256]{3,2,1,0:T(8,128)(2,1)S(1)}, u32[]{:S(2)}, u32[]{:S(2)}) collective-permute-start(bf16[2,3,128,256]{3,2,1,0:T(8,128)(2,1)} %shard_map.108.refs_3_), channel_id=1, source_target_pairs={{0,8},{8,0},{16,24},{24,16},{1,9},{9,1},{17,25},{25,17},{2,10},{10... | collective-permute-start | bytes 1179656 | tf_op jit(solution)/shard_map/ppermute | solution.py:353
  87.4 1.0 copy-start.9
  88.3 0.9 copy-start.14
  89.3 0.9 copy-start.22
  90.2 0.9 copy-start.27
  91.2 0.9 copy-start.29
  99.7 1.0 copy-start.12
  112.0 8.7 %copy-start = (bf16[512,4096]{1,0:T(8,128)(2,1)S(1)}, bf16[512,4096]{1,0:T(8,128)(2,1)}, u32[]{:S(2)}) copy-start(bf16[512,4096]{1,0:T(8,128)(2,1)} %w_ref.3) | copy-start | bytes 12582916
  129.3 9.1 %collective-permute-start.31 = (bf16[64,2048]{1,0:T(8,128)(2,1)S(1)}, bf16[64,2048]{1,0:T(8,128)(2,1)S(1)}, u32[]{:S(2)}, u32[]{:S(2)}) collective-permute-start(bf16[64,2048]{1,0:T(8,128)(2,1)S(1)} %get-tuple-element.21), channel_id=1, source_target_pairs={{0,1},{2,0},{4,2},{6,4},{7,6},{5,7},{3,5},{1,3},{8,9},{10,8},{12,1... | collective-permute-start | bytes 786440 | tf_op jit(solution)/shard_map/ppermute | solution.py:51
  131.5 12.6 %collective-permute-start.25 = (bf16[64,2048]{1,0:T(8,128)(2,1)S(1)}, bf16[64,2048]{1,0:T(8,128)(2,1)S(1)}, u32[]{:S(2)}, u32[]{:S(2)}) collective-permute-start(bf16[64,2048]{1,0:T(8,128)(2,1)S(1)} %slice.148), channel_id=1, source_target_pairs={{0,1},{2,0},{4,2},{6,4},{7,6},{5,7},{3,5},{1,3},{8,9},{10,8},{12,1... | collective-permute-start | bytes 786440 | tf_op jit(solution)/shard_map/ppermute | solution.py:51
  133.1 9.2 %collective-permute-start.21 = (bf16[64,2048]{1,0:T(8,128)(2,1)S(1)}, bf16[64,2048]{1,0:T(8,128)(2,1)S(1)}, u32[]{:S(2)}, u32[]{:S(2)}) collective-permute-start(bf16[64,2048]{1,0:T(8,128)(2,1)S(1)} %get-tuple-element.20), channel_id=1, source_target_pairs={{0,2},{2,4},{4,6},{6,7},{7,5},{5,3},{3,1},{1,0},{8,10},{10,12},{12... | collective-permute-start | bytes 786440 | tf_op jit(solution)/shard_map/ppermute | solution.py:51
  133.6 19.2 %collective-permute-start.28 = (bf16[64,2048]{1,0:T(8,128)(2,1)S(1)}, bf16[64,2048]{1,0:T(8,128)(2,1)S(1)}, u32[]{:S(2)}, u32[]{:S(2)}) collective-permute-start(bf16[64,2048]{1,0:T(8,128)(2,1)S(1)} %slice.152), channel_id=1, source_target_pairs={{0,2},{2,4},{4,6},{6,7},{7,5},{5,3},{3,1},{1,0},{8,10},{10,12},{12... | collective-permute-start | bytes 786440 | tf_op jit(solution)/shard_map/ppermute | solution.py:51
  138.5 10.9 %collective-permute-start.32 = (bf16[64,2048]{1,0:T(8,128)(2,1)S(1)}, bf16[64,2048]{1,0:T(8,128)(2,1)S(1)}, u32[]{:S(2)}, u32[]{:S(2)}) collective-permute-start(bf16[64,2048]{1,0:T(8,128)(2,1)S(1)} %add_convert_fusion.3), channel_id=1, source_target_pairs={{0,1},{2,0},{4,2},{6,4},{7,6},{5,7},{3,5},{1,3},{8,9},{10,8},{12,1... | collective-permute-start | bytes 786440 | tf_op jit(solution)/shard_map/ppermute | solution.py:51
  142.4 10.4 %collective-permute-start.22 = (bf16[64,2048]{1,0:T(8,128)(2,1)S(1)}, bf16[64,2048]{1,0:T(8,128)(2,1)S(1)}, u32[]{:S(2)}, u32[]{:S(2)}) collective-permute-start(bf16[64,2048]{1,0:T(8,128)(2,1)S(1)} %add_convert_fusion.11), channel_id=1, source_target_pairs={{0,2},{2,4},{4,6},{6,7},{7,5},{5,3},{3,1},{1,0},{8,10},{10,12},{12... | collective-permute-start | bytes 786440 | tf_op jit(solution)/shard_map/ppermute | solution.py:51
  149.5 9.3 %collective-permute-start.26 = (bf16[64,2048]{1,0:T(8,128)(2,1)S(1)}, bf16[64,2048]{1,0:T(8,128)(2,1)S(1)}, u32[]{:S(2)}, u32[]{:S(2)}) collective-permute-start(bf16[64,2048]{1,0:T(8,128)(2,1)S(1)} %get-tuple-element.24), channel_id=1, source_target_pairs={{0,1},{2,0},{4,2},{6,4},{7,6},{5,7},{3,5},{1,3},{8,9},{10,8},{12,1... | collective-permute-start | bytes 786440 | tf_op jit(solution)/shard_map/ppermute | solution.py:51
  151.2 12.0 %collective-permute-start.33 = (bf16[64,2048]{1,0:T(8,128)(2,1)S(1)}, bf16[64,2048]{1,0:T(8,128)(2,1)S(1)}, u32[]{:S(2)}, u32[]{:S(2)}) collective-permute-start(bf16[64,2048]{1,0:T(8,128)(2,1)S(1)} %get-tuple-element.25), channel_id=1, source_target_pairs={{0,1},{2,0},{4,2},{6,4},{7,6},{5,7},{3,5},{1,3},{8,9},{10,8},{12,1... | collective-permute-start | bytes 786440 | tf_op jit(solution)/shard_map/ppermute | solution.py:51
  152.9 12.1 %collective-permute-start.23 = (bf16[64,2048]{1,0:T(8,128)(2,1)S(1)}, bf16[64,2048]{1,0:T(8,128)(2,1)S(1)}, u32[]{:S(2)}, u32[]{:S(2)}) collective-permute-start(bf16[64,2048]{1,0:T(8,128)(2,1)S(1)} %get-tuple-element.18), channel_id=1, source_target_pairs={{0,2},{2,4},{4,6},{6,7},{7,5},{5,3},{3,1},{1,0},{8,10},{10,12},{12... | collective-permute-start | bytes 786440 | tf_op jit(solution)/shard_map/ppermute | solution.py:51
  153.4 12.5 %collective-permute-start.29 = (bf16[64,2048]{1,0:T(8,128)(2,1)S(1)}, bf16[64,2048]{1,0:T(8,128)(2,1)S(1)}, u32[]{:S(2)}, u32[]{:S(2)}) collective-permute-start(bf16[64,2048]{1,0:T(8,128)(2,1)S(1)} %get-tuple-element.19), channel_id=1, source_target_pairs={{0,2},{2,4},{4,6},{6,7},{7,5},{5,3},{3,1},{1,0},{8,10},{10,12},{12... | collective-permute-start | bytes 786440 | tf_op jit(solution)/shard_map/ppermute | solution.py:51
  163.3 9.3 %collective-permute-start.27 = (bf16[64,2048]{1,0:T(8,128)(2,1)S(1)}, bf16[64,2048]{1,0:T(8,128)(2,1)S(1)}, u32[]{:S(2)}, u32[]{:S(2)}) collective-permute-start(bf16[64,2048]{1,0:T(8,128)(2,1)S(1)} %get-tuple-element.22), channel_id=1, source_target_pairs={{0,1},{2,0},{4,2},{6,4},{7,6},{5,7},{3,5},{1,3},{8,9},{10,8},{12,1... | collective-permute-start | bytes 786440 | tf_op jit(solution)/shard_map/ppermute | solution.py:51
  166.1 9.3 %collective-permute-start.24 = (bf16[64,2048]{1,0:T(8,128)(2,1)S(1)}, bf16[64,2048]{1,0:T(8,128)(2,1)S(1)}, u32[]{:S(2)}, u32[]{:S(2)}) collective-permute-start(bf16[64,2048]{1,0:T(8,128)(2,1)S(1)} %get-tuple-element.16), channel_id=1, source_target_pairs={{0,2},{2,4},{4,6},{6,7},{7,5},{5,3},{3,1},{1,0},{8,10},{10,12},{12... | collective-permute-start | bytes 786440 | tf_op jit(solution)/shard_map/ppermute | solution.py:51
  166.7 9.5 %collective-permute-start.34 = (bf16[64,2048]{1,0:T(8,128)(2,1)S(1)}, bf16[64,2048]{1,0:T(8,128)(2,1)S(1)}, u32[]{:S(2)}, u32[]{:S(2)}) collective-permute-start(bf16[64,2048]{1,0:T(8,128)(2,1)S(1)} %get-tuple-element.23), channel_id=1, source_target_pairs={{0,1},{2,0},{4,2},{6,4},{7,6},{5,7},{3,5},{1,3},{8,9},{10,8},{12,1... | collective-permute-start | bytes 786440 | tf_op jit(solution)/shard_map/ppermute | solution.py:51
  168.2 10.0 %collective-permute-start.30 = (bf16[64,2048]{1,0:T(8,128)(2,1)S(1)}, bf16[64,2048]{1,0:T(8,128)(2,1)S(1)}, u32[]{:S(2)}, u32[]{:S(2)}) collective-permute-start(bf16[64,2048]{1,0:T(8,128)(2,1)S(1)} %get-tuple-element.17), channel_id=1, source_target_pairs={{0,2},{2,4},{4,6},{6,7},{7,5},{5,3},{3,1},{1,0},{8,10},{10,12},{12... | collective-permute-start | bytes 786440 | tf_op jit(solution)/shard_map/ppermute | solution.py:51
  (16 other events, 13.0 us)

commit v2 on v1

v2 whole, which is shorter than its diff:
```python
import functools

import jax
import jax.numpy as jnp
from jax import lax
from jax.experimental import pallas as pl
from jax.experimental.pallas import tpu as pltpu
from jax.sharding import PartitionSpec as P

WINDOW = 512
CHUNKS = 2
F32 = jnp.float32
BF16 = jnp.bfloat16
LOG2E = 1.4426950408889634


def call(body, grid, in_specs, out_specs, out_shape, scratch=(), prefetch=1, vmem=8, cost=None):
    return pl.pallas_call(
        body,
        grid_spec=pltpu.PrefetchScalarGridSpec(
            num_scalar_prefetch=prefetch,
            grid=grid,
            in_specs=in_specs,
            out_specs=out_specs,
            scratch_shapes=list(scratch),
        ),
        out_shape=out_shape,
        cost_estimate=cost,
        compiler_params=pltpu.CompilerParams(vmem_limit_bytes=vmem * 1024 * 1024),
    )


def cost(flops, moved, exps=0):
    return pl.CostEstimate(flops=int(flops), bytes_accessed=int(moved), transcendentals=int(exps))


WHOLE = pl.BlockSpec(memory_space=pltpu.VMEM)
AFTER = pl.BlockSpec(memory_space=pl.ANY)


def fixed(shape):
    return pl.BlockSpec(shape, lambda *_: (0,) * len(shape))


def mm(left, right, dims=((1,), (0,))):
    return lax.dot_general(left, right, (dims, ((), ())), preferred_element_type=F32)


def sigmoid(x):
    return 0.5 * jnp.tanh(0.5 * x) + 0.5


def ring_order(count):
    return list(range(0, count, 2)) + list(range(count - 1, 0, -2))


def ring_send(value, step):
    order = ring_order(lax.axis_size("head"))
    count = len(order)
    return lax.ppermute(
        value, "head", [(order[i], order[(i + step) % count]) for i in range(count)]
    )


def ring_ids(offsets):
    count = lax.axis_size("head")
    me = lax.axis_index("head")
    place = jnp.where(me % 2 == 0, me // 2, count - 1 - me // 2)
    ids = []
    for offset in offsets:
        at = (place + offset) % count
        ids.append(jnp.where(at < count // 2, 2 * at, 2 * (count - 1 - at) + 1))
    return jnp.stack(ids).astype(jnp.int32)


def load(arrays, after=(), start=0, stop=None, pieces=8):
    stop = arrays[0].shape[0] if stop is None else stop
    size = (stop - start) // pieces
    count = len(arrays)

    def body(*refs):
        out_refs, sems = refs[count + len(after) : -1], refs[-1]
        copies = [
            pltpu.make_async_copy(
                refs[index].at[pl.ds(start + piece * size, size)],
                out_refs[index].at[pl.ds(piece * size, size)],
                sems.at[index, piece],
            )
            for index in range(count)
            for piece in range(pieces)
        ]
        for copy in copies:
            copy.start()
        for copy in copies:
            copy.wait()

    return pl.pallas_call(
        body,
        in_specs=[pl.BlockSpec(memory_space=pltpu.HBM)] * count + [AFTER] * len(after),
        out_specs=[WHOLE] * count,
        out_shape=[
            jax.ShapeDtypeStruct((stop - start,) + array.shape[1:], array.dtype)
            for array in arrays
        ],
        scratch_shapes=[pltpu.SemaphoreType.DMA((count, pieces))],
        cost_estimate=cost(0, sum(2 * (stop - start) * array.shape[1] for array in arrays)),
        compiler_params=pltpu.CompilerParams(vmem_limit_bytes=1024 * 1024),
    )(*[pltpu.with_memory_space_constraint(array, pltpu.HBM) for array in arrays], *after)


def gather_pieces(own, longer):
    count = lax.axis_size("head")
    pieces, offsets = [own], [0]
    held = {1: own, -1: own}
    for step in range(1, count // 2 + 1):
        for way in (1, -1):
            if step < count // 2 or way == longer:
                held[way] = ring_send(held[way], way)
                pieces.append(held[way])
                offsets.append(-way * step)
    return pieces, offsets


def project(gathered, weights):
    pieces, offsets = gathered
    rows, depth = pieces[0].shape
    full, width = weights[0].shape
    count = len(pieces)
    parts = len(weights)

    def body(ids_ref, *refs):
        piece_refs, weight_refs = refs[:count], refs[count : count + parts]
        out_ref, left = refs[count + parts :]
        for index in range(count):
            column = pl.multiple_of(ids_ref[index] * depth, depth)
            left[:, pl.ds(column, depth)] = piece_refs[index][...]
        for part in range(parts):
            out_ref[part] = mm(left[...], weight_refs[part][...]).astype(BF16)

    return call(
        body,
        (),
        [WHOLE] * (count + parts),
        WHOLE,
        jax.ShapeDtypeStruct((parts, rows, width), BF16),
        [pltpu.VMEM((rows, full), BF16)],
        vmem=24,
        cost=cost(2 * rows * full * width * parts, 2 * full * (rows + width * parts)),
    )(ring_ids(offsets), *pieces, *weights)


def head_grads(base, heads, chunk, kv, rate, fast_gate, fast_up, fast_down, before, after=()):
    rows = kv.shape[1]
    size, hidden_size = fast_gate.shape[1:]
    lanes = rate.shape[0]

    def body(base_ref, k_ref, v_ref, rate_ref, gate_ref, up_ref, down_ref, *rest):
        out_ref = rest[-1]
        head = base_ref[0] + pl.program_id(0)
        lane = lax.broadcasted_iota(jnp.int32, (rows, lanes), 1)
        mine = jnp.sum(jnp.where(lane == head, rate_ref[...].T, 0.0), axis=1, keepdims=True)
        key = k_ref[0].astype(F32)
        knorm = key * lax.rsqrt(jnp.mean(key * key, axis=-1, keepdims=True) + 1e-06)
        target = -mine * v_ref[0].astype(F32)
        knorm = knorm.astype(BF16)
        gate_pre = mm(knorm, gate_ref[0].astype(BF16))
        up_pre = mm(knorm, up_ref[0].astype(BF16))
        back = mm(target.astype(BF16), down_ref[0].astype(BF16), ((1,), (1,)))
        sigma = sigmoid(gate_pre)
        active = gate_pre * sigma
        first = (back * up_pre * (sigma + active * (1.0 - sigma))).astype(BF16)
        second = (back * active).astype(BF16)
        third = (active * up_pre).astype(BF16)
        terms = (
            mm(knorm, first, ((0,), (0,))),
            mm(knorm, second, ((0,), (0,))),
            mm(target.astype(BF16), third, ((0,), (0,))),
        )
        for index, term in enumerate(terms):
            if before is not None:
                term = term + rest[0][0, index]
            out_ref[0, index] = term

    def spec(shape):
        return pl.BlockSpec((1,) + shape, lambda h, b: (b[0] + h,) + (0,) * len(shape))

    args = [kv, kv, rate, fast_gate, fast_up, fast_down]
    specs = [
        pl.BlockSpec((1, rows, size), lambda h, b: (0, 0, b[0] + h)),
        pl.BlockSpec((1, rows, size), lambda h, b: (1, 0, b[0] + h)),
        pl.BlockSpec((lanes, rows), lambda h, b: (0, chunk)),
        spec((size, hidden_size)),
        spec((size, hidden_size)),
        spec((hidden_size, size)),
    ]
    if before is not None:
        args.append(before)
        specs.append(spec((3, size, hidden_size)))
    args += after
    specs += [AFTER] * len(after)
    return call(
        body,
        (heads,),
        specs,
        pl.BlockSpec((1, 3, size, hidden_size), lambda h, b: (h, 0, 0, 0)),
        jax.ShapeDtypeStruct((heads, 3, size, hidden_size), F32),
        cost=cost(
            12 * heads * rows * size * hidden_size,
            8 * heads * 3 * size * hidden_size,
            heads * rows * hidden_size,
        ),
    )(base, *args)


def renew(base, kept, received, step, fast_gate, fast_up, fast_down, after):
    heads, _, size, hidden_size = kept.shape

    def body(base_ref, step_ref, kept_ref, gate_ref, up_ref, down_ref, *rest):
        out_ref = rest[-1]
        pace = step_ref[base_ref[0] + pl.program_id(0)]
        for index in range(3):
            grad = kept_ref[0, index]
            for more in rest[: len(received)]:
                grad = grad + more[0, index].astype(F32)
            if index < 2:
                matrix = (gate_ref, up_ref)[index][0]
                fan = size
            else:
                matrix = down_ref[0].T
                fan = hidden_size
            mean_sq = jnp.sum(grad * grad, keepdims=True) / (size * hidden_size)
            scale = pace * fan ** (-0.5) * lax.rsqrt(mean_sq + 1e-06)
            out_ref[0, index] = (matrix - scale * grad).astype(BF16)

    def spec(shape):
        return pl.BlockSpec((1,) + shape, lambda h, b, s: (b[0] + h,) + (0,) * len(shape))

    own = pl.BlockSpec((1, 3, size, hidden_size), lambda h, b, s: (h, 0, 0, 0))
    return call(
        body,
        (heads,),
        [own, spec((size, hidden_size)), spec((size, hidden_size)), spec((hidden_size, size))]
        + [own] * len(received)
        + [AFTER] * len(after),
        own,
        jax.ShapeDtypeStruct(kept.shape, BF16),
        prefetch=2,
        cost=cost(10 * kept.size, 12 * kept.size),
    )(base, step, kept, fast_gate, fast_up, fast_down, *received, *after)


def attend(place, queries, kvs, halos, size):
    count = len(queries)
    rows = queries[0].shape[1]
    heads = queries[0].shape[2] // size
    factor = size ** (-0.5) * LOG2E

    def body(place_ref, *refs):
        q_refs = refs[:count]
        k_refs, v_refs = refs[count : 3 * count], refs[3 * count : 5 * count]
        out_ref = refs[-1]
        has_halo = place_ref[0] > 0
        row = lax.broadcasted_iota(jnp.int32, (rows, rows), 0)
        col = lax.broadcasted_iota(jnp.int32, (rows, rows), 1)
        for index in range(count):
            query = q_refs[index][0]
            scores = []
            for source in range(index, index + count + 1):
                part = mm(query, k_refs[source][0], ((1,), (1,))) * factor
                if source == index:
                    part = jnp.where((col > row) & has_halo, part, -1e30)
                elif source == index + count:
                    part = jnp.where(col <= row, part, -1e30)
                elif source < count:
                    part = jnp.where(has_halo, part, -1e30)
                scores.append(part)
            top = functools.reduce(
                jnp.maximum, [jnp.max(part, axis=-1, keepdims=True) for part in scores]
            )
            total, result = 0.0, 0.0
            for part, source in zip(scores, range(index, index + count + 1)):
                expo = jnp.exp2(part - top)
                total = total + jnp.sum(expo, axis=-1, keepdims=True)
                result = result + mm(expo.astype(BF16), v_refs[source][0])
            out_ref[index * rows : (index + 1) * rows] = result / total

    def spec(which):
        return pl.BlockSpec((1, rows, size), lambda h, p: (which, 0, h))

    sources = list(halos) + list(kvs)
    return call(
        body,
        (heads,),
        [spec(0)] * count + [spec(0)] * (2 * count) + [spec(1)] * (2 * count),
        pl.BlockSpec((count * rows, size), lambda h, p: (0, h)),
        jax.ShapeDtypeStruct((count * rows, heads * size), F32),
        cost=cost(
            4 * heads * size * count * (count + 1) * rows * rows,
            8 * count * rows * heads * size,
            heads * count * (count + 1) * rows * rows,
        ),
    )(place, *queries, *sources, *sources)


def apply_fast(base, queries, attended, nets):
    count = len(queries)
    rows = queries[0].shape[1]
    heads, _, size, hidden_size = nets.shape

    def body(base_ref, *refs):
        q_refs = refs[:count]
        attended_ref, net_ref, out_ref = refs[count:]
        for index in range(count):
            where = slice(index * rows, (index + 1) * rows)
            query = q_refs[index][0].astype(F32)
            qnorm = query * lax.rsqrt(jnp.mean(query * query, axis=-1, keepdims=True) + 1e-06)
            qnorm = qnorm.astype(BF16)
            gate_pre = mm(qnorm, net_ref[0, 0])
            hidden = gate_pre * sigmoid(gate_pre) * mm(qnorm, net_ref[0, 1])
            out_ref[where] = (
                attended_ref[where] + mm(hidden.astype(BF16), net_ref[0, 2], ((1,), (1,)))
            ).astype(BF16)

    return call(
        body,
        (heads,),
        [pl.BlockSpec((1, rows, size), lambda h, b: (0, 0, b[0] + h))] * count
        + [
            pl.BlockSpec((count * rows, size), lambda h, b: (0, b[0] + h)),
            pl.BlockSpec((1, 3, size, hidden_size), lambda h, b: (h, 0, 0, 0)),
        ],
        pl.BlockSpec((count * rows, size), lambda h, b: (0, h)),
        jax.ShapeDtypeStruct((count * rows, heads * size), BF16),
        cost=cost(
            6 * heads * count * rows * size * hidden_size,
            8 * heads * count * rows * size,
            heads * count * rows * hidden_size,
        ),
    )(base, *queries, attended, nets)


def partial_out(ids, side, near, far, w_out, after=()):
    rows = near.shape[0] // lax.axis_size("head")
    depth = near.shape[1]
    count = ids.shape[0]
    width = w_out.shape[1]
    block = width // 8

    def body(ids_ref, side_ref, near_ref, far_ref, w_ref, *refs):
        out_refs = refs[len(after) :]
        lefts = [
            jnp.concatenate(
                [
                    ref[pl.ds(pl.multiple_of(ids_ref[index] * rows, rows), rows)]
                    for index in range(count)
                ],
                axis=0,
            )
            for ref in (near_ref, far_ref)
        ]
        near_row = pl.multiple_of(side_ref[0] * depth, depth)
        far_row = pl.multiple_of((1 - side_ref[0]) * depth, depth)
        for column in range(0, width, block):
            result = mm(lefts[0], w_ref[pl.ds(near_row, depth), column : column + block])
            result += mm(lefts[1], w_ref[pl.ds(far_row, depth), column : column + block])
            result = result.astype(BF16)
            half, at = divmod(column, width // 2)
            for index in range(count):
                out_refs[2 * index + half][:, at : at + block] = result[
                    index * rows : (index + 1) * rows
                ]

    outs = call(
        body,
        (),
        [WHOLE] * 3 + [AFTER] * len(after),
        [WHOLE] * (2 * count),
        [jax.ShapeDtypeStruct((rows, width // 2), BF16)] * (2 * count),
        prefetch=2,
        vmem=16,
        cost=cost(4 * count * rows * depth * width, 2 * width * (2 * depth + count * rows)),
    )(ids, side, near, far, w_out, *after)
    return [tuple(outs[2 * index : 2 * index + 2]) for index in range(count)]


def ring_reduce(side, near, far, w_out):
    count = lax.axis_size("head")
    steps = count // 2
    signed = [sign * step for step in range(steps - 1, 0, -1) for sign in (1, -1)]
    first, second = [steps] + signed[:2], signed[2:] + [0]
    parts = dict(zip(first, partial_out(ring_ids(first), side, near, far, w_out)))
    coming = {
        (1, 0): ring_send(parts[steps][0], 1),
        (-1, 1): ring_send(parts[steps][1], -1),
    }
    after = tuple(coming.values())
    parts |= dict(zip(second, partial_out(ring_ids(second), side, near, far, w_out, after)))
    for offset in signed:
        way = 1 if offset > 0 else -1
        for which in range(2):
            term = parts[offset][which]
            if (way, which) in coming:
                term = (term.astype(F32) + coming[way, which].astype(F32)).astype(BF16)
            coming[way, which] = ring_send(term, way)
    ends = []
    for which in range(2):
        total = parts[0][which].astype(F32)
        for way in (1, -1):
            if (way, which) in coming:
                total = total + coming[way, which].astype(F32)
        ends.append(total.astype(BF16))
    return jnp.concatenate(ends, axis=1)


def swap(value, bit):
    count = lax.axis_size("tok")
    return lax.ppermute(value, "tok", [(index, index ^ bit) for index in range(count)])


def shards(
    tokens, w_query, w_key, w_value, w_out, fast_gate, fast_up, fast_down, token_rate, head_step
):
    row_count = tokens.shape[0]
    local_heads, head_size, _ = fast_gate.shape
    tok_count = lax.axis_size("tok")
    rows = row_count // CHUNKS
    place = lax.axis_index("tok").astype(jnp.int32)
    pair = local_heads // 2
    side = (place % 2).reshape(1)
    near_base, far_base = side * pair, (1 - side) * pair
    zero = jnp.zeros((1,), jnp.int32)

    chunks, after = [], ()
    for c in range(CHUNKS):
        (own,) = load([tokens], after, c * rows, (c + 1) * rows, 1)
        chunks.append(gather_pieces(own, 1 if c % 2 == 0 else -1))
        if c == 0:
            w_key, w_value = load([w_key, w_value])
            after = (*chunks[0][0][1:3], w_key, w_value)
    rate = token_rate.T
    nets = (fast_gate, fast_up, fast_down)
    kvs, halos, queries = [], [], []
    grads = None
    for c in range(CHUNKS):
        kv = project(chunks[c], (w_key, w_value))
        halos.append(
            lax.ppermute(kv, "tok", [(index, index + 1) for index in range(tok_count - 1)])
        )
        kvs.append(kv)
        if c < CHUNKS - 1:
            grads = head_grads(zero, local_heads, c, kv, rate, *nets, grads)
        else:
            far = head_grads(far_base, pair, c, kv, rate, *nets, grads)
            near = head_grads(near_base, pair, c, kv, rate, *nets, grads, halos[:-1])
        queries.append(project(chunks[c], (w_query,)))
    near = near + swap(far.astype(BF16), 1).astype(F32)
    received = []
    for bit in range(1, tok_count.bit_length() - 1):
        travel = near
        for more in received:
            travel = travel + more.astype(F32)
        received.append(swap(travel.astype(BF16), 1 << bit))
    attended = attend(place.reshape(1), queries, kvs, halos, head_size)
    mine = renew(near_base, near, received, head_step, *nets, (attended,))
    other = swap(mine, 1)
    near = apply_fast(near_base, queries, attended, mine)
    far = apply_fast(far_base, queries, attended, other)
    return ring_reduce(side, near, far, w_out)


def solution(mesh):
    placed = (
        P("tok", "head"),
        P(None, "head"),
        P(None, "head"),
        P(None, "head"),
        P("head", None),
        P("head", None, None),
        P("head", None, None),
        P("head", None, None),
        P("tok", "head"),
        P("head"),
    )
    return jax.shard_map(
        shards, mesh=mesh, in_specs=placed, out_specs=P(("tok", "head"), None), check_vma=False
    )
```

time: 181 us -> 136 us (0.75)
  local copies, waits for them, and re-layouts: 27.2 us -> 6.86 us
  Pallas kernels: 53 us -> 37.6 us
  waiting for transfers between devices: 56.5 us -> 50.5 us
    unnamed x92 -> x28, local copies, waits for them, and re-layouts: 22.7 us -> 6.61 us
    pallas_call x7 -> x11, Pallas kernels: 41.9 us -> 26.2 us  [the longest x4 14.2 us: project(): call(body, (), [WHOLE] * (count + parts), WHOLE, jax.ShapeDtypeStruct((pa...]
    ppermute x3, waiting for transfers between devices: 5.52 us -> 0.4 us  [swap(): lax.ppermute(value, 'tok', [(index, index ^ bit) for index in range(count)])]
    slice x9 -> x0, local copies, waits for them, and re-layouts: 3.96 us -> none  [the longest x4 2.11 us: gather_pieces(): return pieces + [ring_send(up[:half], 1), ring_send(down[half:], -1)]]
    ppermute x30 -> x28, starting transfers between devices: 32.9 us -> 30.2 us  [ring_send(): lax.ppermute(value, 'head', [(order[i], order[(i + step) % count]) for i...]
    ppermute x3, starting transfers between devices: 2.04 us -> 4.16 us  [swap(): lax.ppermute(value, 'tok', [(index, index ^ bit) for index in range(count)])]
    ppermute x30 -> x28, waiting for transfers between devices: 51 us -> 50.1 us  [ring_send(): lax.ppermute(value, 'head', [(order[i], order[(i + step) % count]) for i...]
  transfers between devices with their start and end apart: 35 -> 33, of which waited for: 18 -> 17; matrix products, arithmetic and copies ran while one was open for 3% -> 1% of each run, Pallas kernels for 17% -> 23%
where the time goes in v2:
time: 136 us
  waiting for transfers between devices  50.5 us (37%)
  starting transfers between devices  38.3 us (28%)
  Pallas kernels  37.6 us (28%)
  local copies, waits for them, and re-layouts  6.86 us (5%)
  other arithmetic  1.93 us (1%)
    ppermute x28, waiting for transfers between devices, ring_send(): lax.ppermute(value, 'head', [(order[i], order[(i + step) % count]) for i...  50.1 us
    ppermute x28, starting transfers between devices, ring_send(): lax.ppermute(value, 'head', [(order[i], order[(i + step) % count]) for i...  30.2 us
    pallas_call x4, Pallas kernels, project(): call(body, (), [WHOLE] * (count + parts), WHOLE, jax.ShapeDtypeStruct((pa...  14.2 us
    unnamed x28, local copies, waits for them, and re-layouts  6.61 us
    pallas_call x3, Pallas kernels, head_grads(): call(body, (heads,), specs, pl.BlockSpec((1, 3, size, hidden_size), lambd...  5.73 us
    pallas_call x3, Pallas kernels, load(): pl.pallas_call(body, in_specs=[pl.BlockSpec(memory_space=pltpu.HBM)] * co...  5.42 us
    pallas_call x1, Pallas kernels, attend(): call(body, (heads,), [spec(0)] * count + [spec(0)] * (2 * count) + [spec(...  4.6 us
    ppermute x3, starting transfers between devices, swap(): lax.ppermute(value, 'tok', [(index, index ^ bit) for index in range(count)])  4.16 us
  transfers between devices with their start and end apart: 33, of which 17 were waited for; matrix products, arithmetic and copies ran while one was open for 1% of the time, Pallas kernels for 23%

profile of v2, /device:TPU:0, one launch (start us, length us, event | category | flops | bytes accessed | tf_op | source)
XLA Modules:
  0.0 135.7 jit_solution(8191639597153711295)
XLA Ops:
  0.0 1.0 shard_map.100.refs_0_
  1.0 3.0 %collective-permute-start.1 = (bf16[256,512]{1,0:T(8,128)(2,1)S(1)}, bf16[256,512]{1,0:T(8,128)(2,1)S(1)}, u32[]{:S(2)}, u32[]{:S(2)}) collective-permute-start(bf16[256,512]{1,0:T(8,128)(2,1)S(1)} %shard_map.100.refs_0_), channel_id=1, source_target_pairs={{0,1},{2,0},{4,2},{6,4},{7,6},{5,7},{3,5},{1,3},{8,9},{10,8},{12,1... | collective-permute-start | bytes 786440 | tf_op jit(solution)/shard_map/ppermute | solution.py:60
  4.1 3.5 %shard_map.102 = (bf16[4096,512]{1,0:T(8,128)(2,1)S(1)}, bf16[4096,512]{1,0:T(8,128)(2,1)S(1)}) custom-call(bf16[4096,512]{1,0:T(8,128)(2,1)} %refs_0_.4, bf16[4096,512]{1,0:T(8,128)(2,1)} %refs_1_.1), custom_call_target="tpu_custom_call" | custom-call | bytes 8388608 | tf_op jit(solution)/shard_map/pallas_call | solution.py:97
  7.6 2.7 %collective-permute-done.1.refs_2_ = bf16[256,512]{1,0:T(8,128)(2,1)S(1)} collective-permute-done((bf16[256,512]{1,0:T(8,128)(2,1)S(1)}, bf16[256,512]{1,0:T(8,128)(2,1)S(1)}, u32[]{:S(2)}, u32[]{:S(2)}) %collective-permute-start.1) | collective-permute-done | bytes 262176 | tf_op jit(solution)/shard_map/ppermute | solution.py:60
  10.3 1.4 %collective-permute-done.refs_1_ = bf16[256,512]{1,0:T(8,128)(2,1)S(1)} collective-permute-done((bf16[256,512]{1,0:T(8,128)(2,1)S(1)}, bf16[256,512]{1,0:T(8,128)(2,1)S(1)}, u32[]{:S(2)}, u32[]{:S(2)}) %collective-permute-start) | collective-permute-done | bytes 262176 | tf_op jit(solution)/shard_map/ppermute | solution.py:60
  11.7 1.0 shard_map.103.refs_0_
  12.7 1.6 %collective-permute-start.8 = (bf16[256,512]{1,0:T(8,128)(2,1)S(1)}, bf16[256,512]{1,0:T(8,128)(2,1)S(1)}, u32[]{:S(2)}, u32[]{:S(2)}) collective-permute-start(bf16[256,512]{1,0:T(8,128)(2,1)S(1)} %shard_map.103.refs_0_), channel_id=1, source_target_pairs={{0,1},{2,0},{4,2},{6,4},{7,6},{5,7},{3,5},{1,3},{8,9},{10,8},{12,1... | collective-permute-start | bytes 786440 | tf_op jit(solution)/shard_map/ppermute | solution.py:60
  14.3 0.4 collective-permute-start.2
  14.8 0.5 collective-permute-start.7
  15.3 4.3 %collective-permute-done.8.refs_2_ = bf16[256,512]{1,0:T(8,128)(2,1)S(1)} collective-permute-done((bf16[256,512]{1,0:T(8,128)(2,1)S(1)}, bf16[256,512]{1,0:T(8,128)(2,1)S(1)}, u32[]{:S(2)}, u32[]{:S(2)}) %collective-permute-start.8) | collective-permute-done | bytes 262176 | tf_op jit(solution)/shard_map/ppermute | solution.py:60
  19.6 1.6 %collective-permute-start.10 = (bf16[256,512]{1,0:T(8,128)(2,1)S(1)}, bf16[256,512]{1,0:T(8,128)(2,1)S(1)}, u32[]{:S(2)}, u32[]{:S(2)}) collective-permute-start(bf16[256,512]{1,0:T(8,128)(2,1)S(1)} %collective-permute-done.8.refs_2_), channel_id=1, source_target_pairs={{0,1},{2,0},{4,2},{6,4},{7,6},{5,7},{3,5},{1,3},{8,9},{10,8},{12,1... | collective-permute-start | bytes 786440 | tf_op jit(solution)/shard_map/ppermute | solution.py:60
  21.2 1.6 %collective-permute-start.3 = (bf16[256,512]{1,0:T(8,128)(2,1)S(1)}, bf16[256,512]{1,0:T(8,128)(2,1)S(1)}, u32[]{:S(2)}, u32[]{:S(2)}) collective-permute-start(bf16[256,512]{1,0:T(8,128)(2,1)S(1)} %collective-permute-done.1.refs_2_), channel_id=1, source_target_pairs={{0,1},{2,0},{4,2},{6,4},{7,6},{5,7},{3,5},{1,3},{8,9},{10,8},{12,1... | collective-permute-start | bytes 786440 | tf_op jit(solution)/shard_map/ppermute | solution.py:60
  22.8 0.8 collective-permute-done.2.refs_3_
  24.0 5.2 %collective-permute-done.7.refs_1_ = bf16[256,512]{1,0:T(8,128)(2,1)S(1)} collective-permute-done((bf16[256,512]{1,0:T(8,128)(2,1)S(1)}, bf16[256,512]{1,0:T(8,128)(2,1)S(1)}, u32[]{:S(2)}, u32[]{:S(2)}) %collective-permute-start.7) | collective-permute-done | bytes 262176 | tf_op jit(solution)/shard_map/ppermute | solution.py:60
  29.2 0.5 collective-permute-start.9
  29.7 1.6 %collective-permute-start.12 = (bf16[256,512]{1,0:T(8,128)(2,1)S(1)}, bf16[256,512]{1,0:T(8,128)(2,1)S(1)}, u32[]{:S(2)}, u32[]{:S(2)}) collective-permute-start(bf16[256,512]{1,0:T(8,128)(2,1)S(1)} %collective-permute-done.10.refs_4_), channel_id=1, source_target_pairs={{0,1},{2,0},{4,2},{6,4},{7,6},{5,7},{3,5},{1,3},{8,9},{10,8},{12,1... | collective-permute-start | bytes 786440 | tf_op jit(solution)/shard_map/ppermute | solution.py:60
  31.3 3.2 %collective-permute-done.3.refs_4_ = bf16[256,512]{1,0:T(8,128)(2,1)S(1)} collective-permute-done((bf16[256,512]{1,0:T(8,128)(2,1)S(1)}, bf16[256,512]{1,0:T(8,128)(2,1)S(1)}, u32[]{:S(2)}, u32[]{:S(2)}) %collective-permute-start.3) | collective-permute-done | bytes 262176 | tf_op jit(solution)/shard_map/ppermute | solution.py:60
  34.5 1.6 %collective-permute-start.5 = (bf16[256,512]{1,0:T(8,128)(2,1)S(1)}, bf16[256,512]{1,0:T(8,128)(2,1)S(1)}, u32[]{:S(2)}, u32[]{:S(2)}) collective-permute-start(bf16[256,512]{1,0:T(8,128)(2,1)S(1)} %collective-permute-done.3.refs_4_), channel_id=1, source_target_pairs={{0,1},{2,0},{4,2},{6,4},{7,6},{5,7},{3,5},{1,3},{8,9},{10,8},{12,1... | collective-permute-start | bytes 786440 | tf_op jit(solution)/shard_map/ppermute | solution.py:60
  36.1 0.5 collective-permute-start.6
  36.5 3.9 %collective-permute-done.9.refs_3_ = bf16[256,512]{1,0:T(8,128)(2,1)S(1)} collective-permute-done((bf16[256,512]{1,0:T(8,128)(2,1)S(1)}, bf16[256,512]{1,0:T(8,128)(2,1)S(1)}, u32[]{:S(2)}, u32[]{:S(2)}) %collective-permute-start.9) | collective-permute-done | bytes 262176 | tf_op jit(solution)/shard_map/ppermute | solution.py:60
  40.9 1.6 %collective-permute-start.13 = (bf16[256,512]{1,0:T(8,128)(2,1)S(1)}, bf16[256,512]{1,0:T(8,128)(2,1)}, u32[]{:S(2)}, u32[]{:S(2)}) collective-permute-start(bf16[256,512]{1,0:T(8,128)(2,1)S(1)} %collective-permute-done.12.refs_6_), channel_id=1, source_target_pairs={{0,1},{2,0},{4,2},{6,4},{7,6},{5,7},{3,5},{1,3},{8,9},{10,8},{12,1... | collective-permute-start | bytes 786440 | tf_op jit(solution)/shard_map/ppermute | solution.py:60
  42.6 2.6 %collective-permute-done.5.refs_6_ = bf16[256,512]{1,0:T(8,128)(2,1)S(1)} collective-permute-done((bf16[256,512]{1,0:T(8,128)(2,1)S(1)}, bf16[256,512]{1,0:T(8,128)(2,1)S(1)}, u32[]{:S(2)}, u32[]{:S(2)}) %collective-permute-start.5) | collective-permute-done | bytes 262176 | tf_op jit(solution)/shard_map/ppermute | solution.py:60
  45.2 0.9 collective-permute-done.6.refs_7_
  46.2 2.2 %copy-done.1 = bf16[4096,512]{1,0:T(8,128)(2,1)S(1)} copy-done((bf16[4096,512]{1,0:T(8,128)(2,1)S(1)}, bf16[4096,512]{1,0:T(8,128)(2,1)}, u32[]{:S(2)}) %copy-start.1) | copy-done | bytes 4194328
  48.3 2.2 %copy-done.4 = bf16[4096,512]{1,0:T(8,128)(2,1)S(1)} copy-done((bf16[4096,512]{1,0:T(8,128)(2,1)S(1)}, bf16[4096,512]{1,0:T(8,128)(2,1)}, u32[]{:S(2)}) %copy-start.4) | copy-done | bytes 4194328
  50.6 4.3 %shard_map.105.refs_4_.refs_8_.k_ref.v_ref = bf16[2,256,512]{2,1,0:T(8,128)(2,1)S(1)} custom-call(s32[8]{0:T(128)S(1)} %stack.35.ids_ref, bf16[256,512]{1,0:T(8,128)(2,1)S(1)} %shard_map.100.refs_0_, bf16[256,512]{1,0:T(8,128)(2,1)S(1)} %collective-permute-done.refs_1_, bf16[256,512]{1,0:T(8,128)(2,1)S(1)} %collective-permute-done.1.refs_2_, ...), custom_call_target="tpu_custom_call" | custom-call | flops 2147483648 | bytes 10485760 | tf_op jit(solution)/shard_map/pallas_call | solution.py:140
  54.9 1.6 %collective-permute-start.14 = (bf16[2,256,512]{2,1,0:T(8,128)(2,1)S(1)}, bf16[2,256,512]{2,1,0:T(8,128)(2,1)S(1)}, u32[]{:S(2)}, u32[]{:S(2)}) collective-permute-start(bf16[2,256,512]{2,1,0:T(8,128)(2,1)S(1)} %shard_map.105.refs_4_.refs_8_.k_ref.v_ref), channel_id=1, source_target_pairs={{0,8},{8,16},{16,24},{1,9},{9,17},{17,25},{2,10},{10,18},{18,26},{... | collective-permute-start | bytes 1572872 | tf_op jit(solution)/shard_map/ppermute | solution.py:447
  56.5 2.8 %shard_map.108.rest_0_ = f32[4,3,128,256]{3,2,1,0:T(8,128)S(1)} custom-call(s32[1]{0:T(128)} %constant.190.clone.1.base_ref, bf16[2,256,512]{2,1,0:T(8,128)(2,1)S(1)} %shard_map.105.refs_4_.refs_8_.k_ref.v_ref, bf16[2,256,512]{2,1,0:T(8,128)(2,1)S(1)} %shard_map.105.refs_4_.refs_8_.k_ref.v_ref, f32[4,512]{1,0:T(4,128)S(1)} %bitcast.12, ...), custom_call_target="tpu_custom_call" | custom-call | flops 402653184 | bytes 3145728 | tf_op jit(solution)/shard_map/pallas_call | solution.py:201
  59.4 4.1 %shard_map.106.refs_5_.refs_9_.k_ref.v_ref = bf16[2,256,512]{2,1,0:T(8,128)(2,1)S(1)} custom-call(s32[8]{0:T(128)S(1)} %stack.37.ids_ref, bf16[256,512]{1,0:T(8,128)(2,1)S(1)} %shard_map.103.refs_0_, bf16[256,512]{1,0:T(8,128)(2,1)S(1)} %collective-permute-done.7.refs_1_, bf16[256,512]{1,0:T(8,128)(2,1)S(1)} %collective-permute-done.8.refs_2_, ...), custom_call_target="tpu_custom_call" | custom-call | flops 2147483648 | bytes 10485760 | tf_op jit(solution)/shard_map/pallas_call | solution.py:140
  63.5 1.4 %shard_map.110 = f32[2,3,128,256]{3,2,1,0:T(8,128)S(1)} custom-call(s32[1]{0:T(128)S(6)} %mul.59.base_ref, bf16[2,256,512]{2,1,0:T(8,128)(2,1)S(1)} %shard_map.106.refs_5_.refs_9_.k_ref.v_ref, bf16[2,256,512]{2,1,0:T(8,128)(2,1)S(1)} %shard_map.106.refs_5_.refs_9_.k_ref.v_ref, f32[4,512]{1,0:T(4,128)S(1)} %bitcast.13, f32[4,128,256]{2,1,0:T(8,128)S(1)} %copy-done.9, ...), custom_call_target="tpu_custom_call" | custom-call | flops 201326592 | bytes 1572864 | tf_op jit(solution)/shard_map/pallas_call | solution.py:201
  65.0 2.3 %collective-permute-start.16 = (bf16[2,3,128,256]{3,2,1,0:T(8,128)(2,1)S(1)}, bf16[2,3,128,256]{3,2,1,0:T(8,128)(2,1)S(1)}, u32[]{:S(2)}, u32[]{:S(2)}) collective-permute-start(bf16[2,3,128,256]{3,2,1,0:T(8,128)(2,1)S(1)} %convert_element_type.123), channel_id=1, source_target_pairs={{0,8},{8,0},{16,24},{24,16},{1,9},{9,1},{17,25},{25,17},{2,10},{10... | collective-permute-start | bytes 1179656 | tf_op jit(solution)/shard_map/ppermute | solution.py:417
  67.3 2.4 %collective-permute-start.15 = (bf16[2,256,512]{2,1,0:T(8,128)(2,1)S(1)}, bf16[2,256,512]{2,1,0:T(8,128)(2,1)S(1)}, u32[]{:S(2)}, u32[]{:S(2)}) collective-permute-start(bf16[2,256,512]{2,1,0:T(8,128)(2,1)S(1)} %shard_map.106.refs_5_.refs_9_.k_ref.v_ref), channel_id=1, source_target_pairs={{0,8},{8,16},{16,24},{1,9},{9,17},{17,25},{2,10},{10,18},{18,26},{... | collective-permute-start | bytes 1572872 | tf_op jit(solution)/shard_map/ppermute | solution.py:447
  69.7 1.5 %shard_map.109 = f32[2,3,128,256]{3,2,1,0:T(8,128)S(1)} custom-call(s32[1]{0:T(128)S(6)} %mul.50.base_ref, bf16[2,256,512]{2,1,0:T(8,128)(2,1)S(1)} %shard_map.106.refs_5_.refs_9_.k_ref.v_ref, bf16[2,256,512]{2,1,0:T(8,128)(2,1)S(1)} %shard_map.106.refs_5_.refs_9_.k_ref.v_ref, f32[4,512]{1,0:T(4,128)S(1)} %bitcast.14, f32[4,128,256]{2,1,0:T(8,128)S(1)} %copy-done.9, ...), custom_call_target="tpu_custom_call" | custom-call | flops 201326592 | bytes 1572864 | tf_op jit(solution)/shard_map/pallas_call | solution.py:201
  71.4 2.9 %shard_map.101.refs_0_ = bf16[1,256,512]{2,1,0:T(8,128)(2,1)S(1)} custom-call(s32[8]{0:T(128)S(1)} %stack.35.ids_ref, bf16[256,512]{1,0:T(8,128)(2,1)S(1)} %shard_map.100.refs_0_, bf16[256,512]{1,0:T(8,128)(2,1)S(1)} %collective-permute-done.refs_1_, bf16[256,512]{1,0:T(8,128)(2,1)S(1)} %collective-permute-done.1.refs_2_, ...), custom_call_target="tpu_custom_call" | custom-call | flops 1073741824 | bytes 6291456 | tf_op jit(solution)/shard_map/pallas_call | solution.py:140
  74.3 3.0 %shard_map.104.refs_1_ = bf16[1,256,512]{2,1,0:T(8,128)(2,1)S(1)} custom-call(s32[8]{0:T(128)S(1)} %stack.37.ids_ref, bf16[256,512]{1,0:T(8,128)(2,1)S(1)} %shard_map.103.refs_0_, bf16[256,512]{1,0:T(8,128)(2,1)S(1)} %collective-permute-done.7.refs_1_, bf16[256,512]{1,0:T(8,128)(2,1)S(1)} %collective-permute-done.8.refs_2_, ...), custom_call_target="tpu_custom_call" | custom-call | flops 1073741824 | bytes 6291456 | tf_op jit(solution)/shard_map/pallas_call | solution.py:140
  77.4 4.6 %shard_map.107.rest_1_.refs_2_ = f32[512,512]{1,0:T(8,128)S(1)} custom-call(s32[1]{0:T(128)} %bitcast.10.place_ref, bf16[1,256,512]{2,1,0:T(8,128)(2,1)S(1)} %shard_map.101.refs_0_, bf16[1,256,512]{2,1,0:T(8,128)(2,1)S(1)} %shard_map.104.refs_1_, bf16[2,256,512]{2,1,0:T(8,128)(2,1)S(1)} %collective-permute-done.14.refs_2_.refs_6_.rest_1_, ...), custom_call_target="tpu_custom_call" | custom-call | flops 805306368 | bytes 2097152 | tf_op jit(solution)/shard_map/pallas_call | solution.py:291
  82.4 1.0 shard_map.111.refs_3_
  83.4 1.7 %collective-permute-start.18 = (bf16[2,3,128,256]{3,2,1,0:T(8,128)(2,1)S(1)}, bf16[2,3,128,256]{3,2,1,0:T(8,128)(2,1)S(1)}, u32[]{:S(2)}, u32[]{:S(2)}) collective-permute-start(bf16[2,3,128,256]{3,2,1,0:T(8,128)(2,1)S(1)} %shard_map.111.refs_3_), channel_id=1, source_target_pairs={{0,8},{8,0},{16,24},{24,16},{1,9},{9,1},{17,25},{25,17},{2,10},{10... | collective-permute-start | bytes 1179656 | tf_op jit(solution)/shard_map/ppermute | solution.py:417
  85.2 1.4 %shard_map.112.near_ref = bf16[512,256]{1,0:T(8,128)(2,1)S(1)} custom-call(s32[1]{0:T(128)S(6)} %mul.50.base_ref, bf16[1,256,512]{2,1,0:T(8,128)(2,1)S(1)} %shard_map.101.refs_0_, bf16[1,256,512]{2,1,0:T(8,128)(2,1)S(1)} %shard_map.104.refs_1_, f32[512,512]{1,0:T(8,128)S(1)} %shard_map.107.rest_1_.refs_2_, bf16[2,3,128,256]{3,2,1,0:T(8,128)(2,1)S(1)} %shard_map.111.refs_3_), custom_call_target="tpu_custom_call" | custom-call | flops 201326592 | bytes 1048576 | tf_op jit(solution)/shard_map/pallas_call | solution.py:324
  86.7 1.5 %shard_map.113.far_ref = bf16[512,256]{1,0:T(8,128)(2,1)S(1)} custom-call(s32[1]{0:T(128)S(6)} %mul.59.base_ref, bf16[1,256,512]{2,1,0:T(8,128)(2,1)S(1)} %shard_map.101.refs_0_, bf16[1,256,512]{2,1,0:T(8,128)(2,1)S(1)} %shard_map.104.refs_1_, f32[512,512]{1,0:T(8,128)S(1)} %shard_map.107.rest_1_.refs_2_, ...), custom_call_target="tpu_custom_call" | custom-call | flops 201326592 | bytes 1048576 | tf_op jit(solution)/shard_map/pallas_call | solution.py:324
  88.2 1.6 %shard_map.114 = (bf16[64,2048]{1,0:T(8,128)(2,1)S(1)}, bf16[64,2048]{1,0:T(8,128)(2,1)S(1)}, bf16[64,2048]{1,0:T(8,128)(2,1)S(1)}, bf16[64,2048]{1,0:T(8,128)(2...) custom-call(s32[3]{0:T(128)S(1)} %pad_add_fusion.ids_ref, s32[1]{0:T(128)} %bitcast.5.side_ref, ...), custom_call_target="tpu_custom_call" | custom-call | flops 805306368 | bytes 5767168 | tf_op jit(solution)/shard_map/pallas_call | solution.py:373
  89.7 0.5 collective-permute-start.19
  90.3 1.6 %collective-permute-start.20 = (bf16[64,2048]{1,0:T(8,128)(2,1)S(1)}, bf16[64,2048]{1,0:T(8,128)(2,1)S(1)}, u32[]{:S(2)}, u32[]{:S(2)}) collective-permute-start(bf16[64,2048]{1,0:T(8,128)(2,1)S(1)} %get-tuple-element.26), channel_id=1, source_target_pairs={{0,1},{2,0},{4,2},{6,4},{7,6},{5,7},{3,5},{1,3},{8,9},{10,8},{12,1... | collective-permute-start | bytes 786440 | tf_op jit(solution)/shard_map/ppermute | solution.py:60
  91.9 1.6 %collective-permute-start.24 = (bf16[64,2048]{1,0:T(8,128)(2,1)S(1)}, bf16[64,2048]{1,0:T(8,128)(2,1)S(1)}, u32[]{:S(2)}, u32[]{:S(2)}) collective-permute-start(bf16[64,2048]{1,0:T(8,128)(2,1)S(1)} %get-tuple-element.33), channel_id=1, source_target_pairs={{0,1},{2,0},{4,2},{6,4},{7,6},{5,7},{3,5},{1,3},{8,9},{10,8},{12,1... | collective-permute-start | bytes 786440 | tf_op jit(solution)/shard_map/ppermute | solution.py:60
  93.9 5.0 %collective-permute-done.19.refs_0_ = bf16[64,2048]{1,0:T(8,128)(2,1)S(1)} collective-permute-done((bf16[64,2048]{1,0:T(8,128)(2,1)S(1)}, bf16[64,2048]{1,0:T(8,128)(2,1)S(1)}, u32[]{:S(2)}, u32[]{:S(2)}) %collective-permute-start.19) | collective-permute-done | bytes 262176 | tf_op jit(solution)/shard_map/ppermute | solution.py:60
  99.0 0.5 collective-permute-start.21
  99.6 1.6 %collective-permute-start.30 = (bf16[64,2048]{1,0:T(8,128)(2,1)S(1)}, bf16[64,2048]{1,0:T(8,128)(2,1)S(1)}, u32[]{:S(2)}, u32[]{:S(2)}) collective-permute-start(bf16[64,2048]{1,0:T(8,128)(2,1)S(1)} %add_convert_fusion.3), channel_id=1, source_target_pairs={{0,1},{2,0},{4,2},{6,4},{7,6},{5,7},{3,5},{1,3},{8,9},{10,8},{12,1... | collective-permute-start | bytes 786440 | tf_op jit(solution)/shard_map/ppermute | solution.py:60
  101.2 2.2 %copy-done.7 = bf16[512,4096]{1,0:T(8,128)(2,1)S(1)} copy-done((bf16[512,4096]{1,0:T(8,128)(2,1)S(1)}, bf16[512,4096]{1,0:T(8,128)(2,1)}, u32[]{:S(2)}) %copy-start.7) | copy-done | bytes 4194328
  103.4 2.1 %shard_map.115 = (bf16[64,2048]{1,0:T(8,128)(2,1)S(1)}, bf16[64,2048]{1,0:T(8,128)(2,1)S(1)}, bf16[64,2048]{1,0:T(8,128)(2,1)S(1)}, bf16[64,2048]{1,0:T(8,128)(2...) custom-call(s32[5]{0:T(128)S(1)} %stack.31.ids_ref, ...), custom_call_target="tpu_custom_call" | custom-call | flops 1342177280 | bytes 6815744 | tf_op jit(solution)/shard_map/pallas_call | solution.py:373
  105.6 1.6 %collective-permute-start.25 = (bf16[64,2048]{1,0:T(8,128)(2,1)S(1)}, bf16[64,2048]{1,0:T(8,128)(2,1)S(1)}, u32[]{:S(2)}, u32[]{:S(2)}) collective-permute-start(bf16[64,2048]{1,0:T(8,128)(2,1)S(1)} %add_convert_fusion.8), channel_id=1, source_target_pairs={{0,1},{2,0},{4,2},{6,4},{7,6},{5,7},{3,5},{1,3},{8,9},{10,8},{12,1... | collective-permute-start | bytes 786440 | tf_op jit(solution)/shard_map/ppermute | solution.py:60
  107.3 0.5 collective-permute-start.28
  107.8 2.4 %collective-permute-done.21 = bf16[64,2048]{1,0:T(8,128)(2,1)S(1)} collective-permute-done((bf16[64,2048]{1,0:T(8,128)(2,1)S(1)}, bf16[64,2048]{1,0:T(8,128)(2,1)S(1)}, u32[]{:S(2)}, u32[]{:S(2)}) %collective-permute-start.21) | collective-permute-done | bytes 262176 | tf_op jit(solution)/shard_map/ppermute | solution.py:60
  110.2 0.5 collective-permute-start.22
  110.8 4.5 %collective-permute-done.25 = bf16[64,2048]{1,0:T(8,128)(2,1)S(1)} collective-permute-done((bf16[64,2048]{1,0:T(8,128)(2,1)S(1)}, bf16[64,2048]{1,0:T(8,128)(2,1)S(1)}, u32[]{:S(2)}, u32[]{:S(2)}) %collective-permute-start.25) | collective-permute-done | bytes 262176 | tf_op jit(solution)/shard_map/ppermute | solution.py:60
  115.4 1.6 %collective-permute-start.26 = (bf16[64,2048]{1,0:T(8,128)(2,1)S(1)}, bf16[64,2048]{1,0:T(8,128)(2,1)S(1)}, u32[]{:S(2)}, u32[]{:S(2)}) collective-permute-start(bf16[64,2048]{1,0:T(8,128)(2,1)S(1)} %add_convert_fusion.7), channel_id=1, source_target_pairs={{0,1},{2,0},{4,2},{6,4},{7,6},{5,7},{3,5},{1,3},{8,9},{10,8},{12,1... | collective-permute-start | bytes 786440 | tf_op jit(solution)/shard_map/ppermute | solution.py:60
  117.0 0.5 collective-permute-start.29
  117.6 1.6 %collective-permute-start.31 = (bf16[64,2048]{1,0:T(8,128)(2,1)S(1)}, bf16[64,2048]{1,0:T(8,128)(2,1)S(1)}, u32[]{:S(2)}, u32[]{:S(2)}) collective-permute-start(bf16[64,2048]{1,0:T(8,128)(2,1)S(1)} %add_convert_fusion.2), channel_id=1, source_target_pairs={{0,1},{2,0},{4,2},{6,4},{7,6},{5,7},{3,5},{1,3},{8,9},{10,8},{12,1... | collective-permute-start | bytes 786440 | tf_op jit(solution)/shard_map/ppermute | solution.py:60
  119.2 3.0 %collective-permute-done.22 = bf16[64,2048]{1,0:T(8,128)(2,1)S(1)} collective-permute-done((bf16[64,2048]{1,0:T(8,128)(2,1)S(1)}, bf16[64,2048]{1,0:T(8,128)(2,1)S(1)}, u32[]{:S(2)}, u32[]{:S(2)}) %collective-permute-start.22) | collective-permute-done | bytes 262176 | tf_op jit(solution)/shard_map/ppermute | solution.py:60
  122.3 0.5 collective-permute-start.23
  122.8 5.5 %collective-permute-done.31 = bf16[64,2048]{1,0:T(8,128)(2,1)S(1)} collective-permute-done((bf16[64,2048]{1,0:T(8,128)(2,1)S(1)}, bf16[64,2048]{1,0:T(8,128)(2,1)S(1)}, u32[]{:S(2)}, u32[]{:S(2)}) %collective-permute-start.31) | collective-permute-done | bytes 262176 | tf_op jit(solution)/shard_map/ppermute | solution.py:60
  128.3 1.6 %collective-permute-start.32 = (bf16[64,2048]{1,0:T(8,128)(2,1)S(1)}, bf16[64,2048]{1,0:T(8,128)(2,1)S(1)}, u32[]{:S(2)}, u32[]{:S(2)}) collective-permute-start(bf16[64,2048]{1,0:T(8,128)(2,1)S(1)} %add_convert_fusion.1), channel_id=1, source_target_pairs={{0,1},{2,0},{4,2},{6,4},{7,6},{5,7},{3,5},{1,3},{8,9},{10,8},{12,1... | collective-permute-start | bytes 786440 | tf_op jit(solution)/shard_map/ppermute | solution.py:60
  129.9 1.9 %collective-permute-done.23 = bf16[64,2048]{1,0:T(8,128)(2,1)S(1)} collective-permute-done((bf16[64,2048]{1,0:T(8,128)(2,1)S(1)}, bf16[64,2048]{1,0:T(8,128)(2,1)S(1)}, u32[]{:S(2)}, u32[]{:S(2)}) %collective-permute-start.23) | collective-permute-done | bytes 262176 | tf_op jit(solution)/shard_map/ppermute | solution.py:60
  132.0 2.8 %collective-permute-done.32 = bf16[64,2048]{1,0:T(8,128)(2,1)S(1)} collective-permute-done((bf16[64,2048]{1,0:T(8,128)(2,1)S(1)}, bf16[64,2048]{1,0:T(8,128)(2,1)S(1)}, u32[]{:S(2)}, u32[]{:S(2)}) %collective-permute-start.32) | collective-permute-done | bytes 262176 | tf_op jit(solution)/shard_map/ppermute | solution.py:60
  134.8 0.8 pad_maximum_fusion
  (65 shorter events, 3.5 us)
Async XLA Ops:
  1.0 9.4 %collective-permute-start.1 = (bf16[256,512]{1,0:T(8,128)(2,1)S(1)}, bf16[256,512]{1,0:T(8,128)(2,1)S(1)}, u32[]{:S(2)}, u32[]{:S(2)}) collective-permute-start(bf16[256,512]{1,0:T(8,128)(2,1)S(1)} %shard_map.100.refs_0_), channel_id=1, source_target_pairs={{0,1},{2,0},{4,2},{6,4},{7,6},{5,7},{3,5},{1,3},{8,9},{10,8},{12,1... | collective-permute-start | bytes 786440 | tf_op jit(solution)/shard_map/ppermute | solution.py:60
  4.0 7.8 %collective-permute-start = (bf16[256,512]{1,0:T(8,128)(2,1)S(1)}, bf16[256,512]{1,0:T(8,128)(2,1)S(1)}, u32[]{:S(2)}, u32[]{:S(2)}) collective-permute-start(bf16[256,512]{1,0:T(8,128)(2,1)S(1)} %shard_map.100.refs_0_), channel_id=1, source_target_pairs={{0,2},{2,4},{4,6},{6,7},{7,5},{5,3},{3,1},{1,0},{8,10},{10,12},{12... | collective-permute-start | bytes 786440 | tf_op jit(solution)/shard_map/ppermute | solution.py:60
  7.6 5.1 %copy-start = (bf16[4096,512]{1,0:T(8,128)(2,1)}, bf16[4096,512]{1,0:T(8,128)(2,1)S(1)}, u32[]{:S(2)}) copy-start(bf16[4096,512]{1,0:T(8,128)(2,1)S(1)} %get-tuple-element.23.refs_3_.refs_8_) | copy-start | bytes 12582916
  7.6 5.1 %copy-start.3 = (bf16[4096,512]{1,0:T(8,128)(2,1)}, bf16[4096,512]{1,0:T(8,128)(2,1)S(1)}, u32[]{:S(2)}) copy-start(bf16[4096,512]{1,0:T(8,128)(2,1)S(1)} %get-tuple-element.24.refs_4_.refs_9_) | copy-start | bytes 12582916
  12.7 6.9 %collective-permute-start.8 = (bf16[256,512]{1,0:T(8,128)(2,1)S(1)}, bf16[256,512]{1,0:T(8,128)(2,1)S(1)}, u32[]{:S(2)}, u32[]{:S(2)}) collective-permute-start(bf16[256,512]{1,0:T(8,128)(2,1)S(1)} %shard_map.103.refs_0_), channel_id=1, source_target_pairs={{0,1},{2,0},{4,2},{6,4},{7,6},{5,7},{3,5},{1,3},{8,9},{10,8},{12,1... | collective-permute-start | bytes 786440 | tf_op jit(solution)/shard_map/ppermute | solution.py:60
  14.3 9.2 %collective-permute-start.2 = (bf16[256,512]{1,0:T(8,128)(2,1)S(1)}, bf16[256,512]{1,0:T(8,128)(2,1)S(1)}, u32[]{:S(2)}, u32[]{:S(2)}) collective-permute-start(bf16[256,512]{1,0:T(8,128)(2,1)S(1)} %collective-permute-done.refs_1_), channel_id=1, source_target_pairs={{0,2},{2,4},{4,6},{6,7},{7,5},{5,3},{3,1},{1,0},{8,10},{10,12},{12... | collective-permute-start | bytes 786440 | tf_op jit(solution)/shard_map/ppermute | solution.py:60
  14.8 14.4 %collective-permute-start.7 = (bf16[256,512]{1,0:T(8,128)(2,1)S(1)}, bf16[256,512]{1,0:T(8,128)(2,1)S(1)}, u32[]{:S(2)}, u32[]{:S(2)}) collective-permute-start(bf16[256,512]{1,0:T(8,128)(2,1)S(1)} %shard_map.103.refs_0_), channel_id=1, source_target_pairs={{0,2},{2,4},{4,6},{6,7},{7,5},{5,3},{3,1},{1,0},{8,10},{10,12},{12... | collective-permute-start | bytes 786440 | tf_op jit(solution)/shard_map/ppermute | solution.py:60
  19.6 10.1 %collective-permute-start.10 = (bf16[256,512]{1,0:T(8,128)(2,1)S(1)}, bf16[256,512]{1,0:T(8,128)(2,1)S(1)}, u32[]{:S(2)}, u32[]{:S(2)}) collective-permute-start(bf16[256,512]{1,0:T(8,128)(2,1)S(1)} %collective-permute-done.8.refs_2_), channel_id=1, source_target_pairs={{0,1},{2,0},{4,2},{6,4},{7,6},{5,7},{3,5},{1,3},{8,9},{10,8},{12,1... | collective-permute-start | bytes 786440 | tf_op jit(solution)/shard_map/ppermute | solution.py:60
  21.2 13.3 %collective-permute-start.3 = (bf16[256,512]{1,0:T(8,128)(2,1)S(1)}, bf16[256,512]{1,0:T(8,128)(2,1)S(1)}, u32[]{:S(2)}, u32[]{:S(2)}) collective-permute-start(bf16[256,512]{1,0:T(8,128)(2,1)S(1)} %collective-permute-done.1.refs_2_), channel_id=1, source_target_pairs={{0,1},{2,0},{4,2},{6,4},{7,6},{5,7},{3,5},{1,3},{8,9},{10,8},{12,1... | collective-permute-start | bytes 786440 | tf_op jit(solution)/shard_map/ppermute | solution.py:60
  23.6 12.5 %collective-permute-start.4 = (bf16[256,512]{1,0:T(8,128)(2,1)S(1)}, bf16[256,512]{1,0:T(8,128)(2,1)S(1)}, u32[]{:S(2)}, u32[]{:S(2)}) collective-permute-start(bf16[256,512]{1,0:T(8,128)(2,1)S(1)} %collective-permute-done.2.refs_3_), channel_id=1, source_target_pairs={{0,2},{2,4},{4,6},{6,7},{7,5},{5,3},{3,1},{1,0},{8,10},{10,12},{12... | collective-permute-start | bytes 786440 | tf_op jit(solution)/shard_map/ppermute | solution.py:60
  29.2 11.2 %collective-permute-start.9 = (bf16[256,512]{1,0:T(8,128)(2,1)S(1)}, bf16[256,512]{1,0:T(8,128)(2,1)S(1)}, u32[]{:S(2)}, u32[]{:S(2)}) collective-permute-start(bf16[256,512]{1,0:T(8,128)(2,1)S(1)} %collective-permute-done.7.refs_1_), channel_id=1, source_target_pairs={{0,2},{2,4},{4,6},{6,7},{7,5},{5,3},{3,1},{1,0},{8,10},{10,12},{12... | collective-permute-start | bytes 786440 | tf_op jit(solution)/shard_map/ppermute | solution.py:60
  29.7 11.2 %collective-permute-start.12 = (bf16[256,512]{1,0:T(8,128)(2,1)S(1)}, bf16[256,512]{1,0:T(8,128)(2,1)S(1)}, u32[]{:S(2)}, u32[]{:S(2)}) collective-permute-start(bf16[256,512]{1,0:T(8,128)(2,1)S(1)} %collective-permute-done.10.refs_4_), channel_id=1, source_target_pairs={{0,1},{2,0},{4,2},{6,4},{7,6},{5,7},{3,5},{1,3},{8,9},{10,8},{12,1... | collective-permute-start | bytes 786440 | tf_op jit(solution)/shard_map/ppermute | solution.py:60
  34.5 10.7 %collective-permute-start.5 = (bf16[256,512]{1,0:T(8,128)(2,1)S(1)}, bf16[256,512]{1,0:T(8,128)(2,1)S(1)}, u32[]{:S(2)}, u32[]{:S(2)}) collective-permute-start(bf16[256,512]{1,0:T(8,128)(2,1)S(1)} %collective-permute-done.3.refs_4_), channel_id=1, source_target_pairs={{0,1},{2,0},{4,2},{6,4},{7,6},{5,7},{3,5},{1,3},{8,9},{10,8},{12,1... | collective-permute-start | bytes 786440 | tf_op jit(solution)/shard_map/ppermute | solution.py:60
  36.1 10.1 %collective-permute-start.6 = (bf16[256,512]{1,0:T(8,128)(2,1)S(1)}, bf16[256,512]{1,0:T(8,128)(2,1)}, u32[]{:S(2)}, u32[]{:S(2)}) collective-permute-start(bf16[256,512]{1,0:T(8,128)(2,1)S(1)} %collective-permute-done.4.refs_5_), channel_id=1, source_target_pairs={{0,2},{2,4},{4,6},{6,7},{7,5},{5,3},{3,1},{1,0},{8,10},{10,12},{12... | collective-permute-start | bytes 786440 | tf_op jit(solution)/shard_map/ppermute | solution.py:60
  40.4 18.9 %collective-permute-start.11 = (bf16[256,512]{1,0:T(8,128)(2,1)S(1)}, bf16[256,512]{1,0:T(8,128)(2,1)}, u32[]{:S(2)}, u32[]{:S(2)}) collective-permute-start(bf16[256,512]{1,0:T(8,128)(2,1)S(1)} %collective-permute-done.9.refs_3_), channel_id=1, source_target_pairs={{0,2},{2,4},{4,6},{6,7},{7,5},{5,3},{3,1},{1,0},{8,10},{10,12},{12... | collective-permute-start | bytes 786440 | tf_op jit(solution)/shard_map/ppermute | solution.py:60
  40.9 18.5 %collective-permute-start.13 = (bf16[256,512]{1,0:T(8,128)(2,1)S(1)}, bf16[256,512]{1,0:T(8,128)(2,1)}, u32[]{:S(2)}, u32[]{:S(2)}) collective-permute-start(bf16[256,512]{1,0:T(8,128)(2,1)S(1)} %collective-permute-done.12.refs_6_), channel_id=1, source_target_pairs={{0,1},{2,0},{4,2},{6,4},{7,6},{5,7},{3,5},{1,3},{8,9},{10,8},{12,1... | collective-permute-start | bytes 786440 | tf_op jit(solution)/shard_map/ppermute | solution.py:60
  46.2 2.2 %copy-start.1 = (bf16[4096,512]{1,0:T(8,128)(2,1)S(1)}, bf16[4096,512]{1,0:T(8,128)(2,1)}, u32[]{:S(2)}) copy-start(bf16[4096,512]{1,0:T(8,128)(2,1)} %copy-done) | copy-start | bytes 12582916
  48.3 2.2 %copy-start.4 = (bf16[4096,512]{1,0:T(8,128)(2,1)S(1)}, bf16[4096,512]{1,0:T(8,128)(2,1)}, u32[]{:S(2)}) copy-start(bf16[4096,512]{1,0:T(8,128)(2,1)} %copy-done.3) | copy-start | bytes 12582916
  50.5 5.9 %copy-start.9 = (f32[4,128,256]{2,1,0:T(8,128)S(1)}, f32[4,128,256]{2,1,0:T(8,128)}, u32[]{:S(2)}) copy-start(f32[4,128,256]{2,1,0:T(8,128)} %gate_ref.7) | copy-start | bytes 1572868
  50.5 5.9 %copy-start.10 = (f32[4,128,256]{2,1,0:T(8,128)S(1)}, f32[4,128,256]{2,1,0:T(8,128)}, u32[]{:S(2)}) copy-start(f32[4,128,256]{2,1,0:T(8,128)} %up_ref.7) | copy-start | bytes 1572868
  50.5 6.0 %copy-start.11 = (f32[4,256,128]{2,1,0:T(8,128)S(1)}, f32[4,256,128]{2,1,0:T(8,128)}, u32[]{:S(2)}) copy-start(f32[4,256,128]{2,1,0:T(8,128)} %down_ref.7) | copy-start | bytes 1572868
  50.5 6.0 %copy-start.12 = (f32[512,4]{0,1:T(4,128)S(1)}, f32[512,4]{0,1:T(4,128)}, u32[]{:S(2)}) copy-start(f32[512,4]{0,1:T(4,128)} %param.18) | copy-start | bytes 24580
  50.5 8.8 %copy-start.5 = (bf16[4096,512]{1,0:T(8,128)(2,1)S(1)}, bf16[4096,512]{1,0:T(8,128)(2,1)}, u32[]{:S(2)}) copy-start(bf16[4096,512]{1,0:T(8,128)(2,1)} %copy-done.3) | copy-start | bytes 12582916
  54.9 4.5 %copy-start.2 = (bf16[4096,512]{1,0:T(8,128)(2,1)S(1)}, bf16[4096,512]{1,0:T(8,128)(2,1)}, u32[]{:S(2)}) copy-start(bf16[4096,512]{1,0:T(8,128)(2,1)} %copy-done) | copy-start | bytes 12582916
  54.9 14.8 %collective-permute-start.14 = (bf16[2,256,512]{2,1,0:T(8,128)(2,1)S(1)}, bf16[2,256,512]{2,1,0:T(8,128)(2,1)S(1)}, u32[]{:S(2)}, u32[]{:S(2)}) collective-permute-start(bf16[2,256,512]{2,1,0:T(8,128)(2,1)S(1)} %shard_map.105.refs_4_.refs_8_.k_ref.v_ref), channel_id=1, source_target_pairs={{0,8},{8,16},{16,24},{1,9},{9,17},{17,25},{2,10},{10,18},{18,26},{... | collective-permute-start | bytes 1572872 | tf_op jit(solution)/shard_map/ppermute | solution.py:447
  65.0 6.5 %copy-start.8 = (bf16[4096,512]{1,0:T(8,128)(2,1)S(1)}, bf16[4096,512]{1,0:T(8,128)(2,1)}, u32[]{:S(2)}) copy-start(bf16[4096,512]{1,0:T(8,128)(2,1)} %refs_8_.3) | copy-start | bytes 12582916
  65.0 6.2 %collective-permute-start.16 = (bf16[2,3,128,256]{3,2,1,0:T(8,128)(2,1)S(1)}, bf16[2,3,128,256]{3,2,1,0:T(8,128)(2,1)S(1)}, u32[]{:S(2)}, u32[]{:S(2)}) collective-permute-start(bf16[2,3,128,256]{3,2,1,0:T(8,128)(2,1)S(1)} %convert_element_type.123), channel_id=1, source_target_pairs={{0,8},{8,0},{16,24},{24,16},{1,9},{9,1},{17,25},{25,17},{2,10},{10... | collective-permute-start | bytes 1179656 | tf_op jit(solution)/shard_map/ppermute | solution.py:417
  67.3 10.1 %collective-permute-start.15 = (bf16[2,256,512]{2,1,0:T(8,128)(2,1)S(1)}, bf16[2,256,512]{2,1,0:T(8,128)(2,1)S(1)}, u32[]{:S(2)}, u32[]{:S(2)}) collective-permute-start(bf16[2,256,512]{2,1,0:T(8,128)(2,1)S(1)} %shard_map.106.refs_5_.refs_9_.k_ref.v_ref), channel_id=1, source_target_pairs={{0,8},{8,16},{16,24},{1,9},{9,17},{17,25},{2,10},{10,18},{18,26},{... | collective-permute-start | bytes 1572872 | tf_op jit(solution)/shard_map/ppermute | solution.py:447
  71.3 11.1 %collective-permute-start.17 = (bf16[2,3,128,256]{3,2,1,0:T(8,128)(2,1)S(1)}, bf16[2,3,128,256]{3,2,1,0:T(8,128)(2,1)S(1)}, u32[]{:S(2)}, u32[]{:S(2)}) collective-permute-start(bf16[2,3,128,256]{3,2,1,0:T(8,128)(2,1)S(1)} %get-tuple-element.41), channel_id=1, source_target_pairs={{0,16},{8,24},{16,0},{24,8},{1,17},{9,25},{17,1},{25,9},{2,18},{10... | collective-permute-start | bytes 1179656 | tf_op jit(solution)/shard_map/ppermute | solution.py:417
  77.3 5.0 %copy-start.13 = (f32[4]{0:T(128)S(1)}, f32[4]{0:T(128)}, u32[]{:S(2)}) copy-start(f32[4]{0:T(128)} %step_ref.1) | copy-start | bytes 52
  82.4 5.8 %copy-start.6 = (bf16[512,4096]{1,0:T(8,128)(2,1)S(1)}, bf16[512,4096]{1,0:T(8,128)(2,1)}, u32[]{:S(2)}) copy-start(bf16[512,4096]{1,0:T(8,128)(2,1)} %w_ref.3) | copy-start | bytes 12582916
  83.4 3.2 %collective-permute-start.18 = (bf16[2,3,128,256]{3,2,1,0:T(8,128)(2,1)S(1)}, bf16[2,3,128,256]{3,2,1,0:T(8,128)(2,1)S(1)}, u32[]{:S(2)}, u32[]{:S(2)}) collective-permute-start(bf16[2,3,128,256]{3,2,1,0:T(8,128)(2,1)S(1)} %shard_map.111.refs_3_), channel_id=1, source_target_pairs={{0,8},{8,0},{16,24},{24,16},{1,9},{9,1},{17,25},{25,17},{2,10},{10... | collective-permute-start | bytes 1179656 | tf_op jit(solution)/shard_map/ppermute | solution.py:417
  89.7 9.2 %collective-permute-start.19 = (bf16[64,2048]{1,0:T(8,128)(2,1)S(1)}, bf16[64,2048]{1,0:T(8,128)(2,1)S(1)}, u32[]{:S(2)}, u32[]{:S(2)}) collective-permute-start(bf16[64,2048]{1,0:T(8,128)(2,1)S(1)} %get-tuple-element.25), channel_id=1, source_target_pairs={{0,2},{2,4},{4,6},{6,7},{7,5},{5,3},{3,1},{1,0},{8,10},{10,12},{12... | collective-permute-start | bytes 786440 | tf_op jit(solution)/shard_map/ppermute | solution.py:60
  90.3 9.2 %collective-permute-start.20 = (bf16[64,2048]{1,0:T(8,128)(2,1)S(1)}, bf16[64,2048]{1,0:T(8,128)(2,1)S(1)}, u32[]{:S(2)}, u32[]{:S(2)}) collective-permute-start(bf16[64,2048]{1,0:T(8,128)(2,1)S(1)} %get-tuple-element.26), channel_id=1, source_target_pairs={{0,1},{2,0},{4,2},{6,4},{7,6},{5,7},{3,5},{1,3},{8,9},{10,8},{12,1... | collective-permute-start | bytes 786440 | tf_op jit(solution)/shard_map/ppermute | solution.py:60
  91.9 13.6 %collective-permute-start.24 = (bf16[64,2048]{1,0:T(8,128)(2,1)S(1)}, bf16[64,2048]{1,0:T(8,128)(2,1)S(1)}, u32[]{:S(2)}, u32[]{:S(2)}) collective-permute-start(bf16[64,2048]{1,0:T(8,128)(2,1)S(1)} %get-tuple-element.33), channel_id=1, source_target_pairs={{0,1},{2,0},{4,2},{6,4},{7,6},{5,7},{3,5},{1,3},{8,9},{10,8},{12,1... | collective-permute-start | bytes 786440 | tf_op jit(solution)/shard_map/ppermute | solution.py:60
  93.5 13.7 %collective-permute-start.27 = (bf16[64,2048]{1,0:T(8,128)(2,1)S(1)}, bf16[64,2048]{1,0:T(8,128)(2,1)S(1)}, u32[]{:S(2)}, u32[]{:S(2)}) collective-permute-start(bf16[64,2048]{1,0:T(8,128)(2,1)S(1)} %get-tuple-element.37), channel_id=1, source_target_pairs={{0,2},{2,4},{4,6},{6,7},{7,5},{5,3},{3,1},{1,0},{8,10},{10,12},{12... | collective-permute-start | bytes 786440 | tf_op jit(solution)/shard_map/ppermute | solution.py:60
  99.0 11.2 %collective-permute-start.21 = (bf16[64,2048]{1,0:T(8,128)(2,1)S(1)}, bf16[64,2048]{1,0:T(8,128)(2,1)S(1)}, u32[]{:S(2)}, u32[]{:S(2)}) collective-permute-start(bf16[64,2048]{1,0:T(8,128)(2,1)S(1)} %add_convert_fusion.11), channel_id=1, source_target_pairs={{0,2},{2,4},{4,6},{6,7},{7,5},{5,3},{3,1},{1,0},{8,10},{10,12},{12... | collective-permute-start | bytes 786440 | tf_op jit(solution)/shard_map/ppermute | solution.py:60
  99.6 18.0 %collective-permute-start.30 = (bf16[64,2048]{1,0:T(8,128)(2,1)S(1)}, bf16[64,2048]{1,0:T(8,128)(2,1)S(1)}, u32[]{:S(2)}, u32[]{:S(2)}) collective-permute-start(bf16[64,2048]{1,0:T(8,128)(2,1)S(1)} %add_convert_fusion.3), channel_id=1, source_target_pairs={{0,1},{2,0},{4,2},{6,4},{7,6},{5,7},{3,5},{1,3},{8,9},{10,8},{12,1... | collective-permute-start | bytes 786440 | tf_op jit(solution)/shard_map/ppermute | solution.py:60
  101.2 2.2 %copy-start.7 = (bf16[512,4096]{1,0:T(8,128)(2,1)S(1)}, bf16[512,4096]{1,0:T(8,128)(2,1)}, u32[]{:S(2)}) copy-start(bf16[512,4096]{1,0:T(8,128)(2,1)} %w_ref.3) | copy-start | bytes 12582916
  105.6 9.7 %collective-permute-start.25 = (bf16[64,2048]{1,0:T(8,128)(2,1)S(1)}, bf16[64,2048]{1,0:T(8,128)(2,1)S(1)}, u32[]{:S(2)}, u32[]{:S(2)}) collective-permute-start(bf16[64,2048]{1,0:T(8,128)(2,1)S(1)} %add_convert_fusion.8), channel_id=1, source_target_pairs={{0,1},{2,0},{4,2},{6,4},{7,6},{5,7},{3,5},{1,3},{8,9},{10,8},{12,1... | collective-permute-start | bytes 786440 | tf_op jit(solution)/shard_map/ppermute | solution.py:60
  107.3 9.7 %collective-permute-start.28 = (bf16[64,2048]{1,0:T(8,128)(2,1)S(1)}, bf16[64,2048]{1,0:T(8,128)(2,1)S(1)}, u32[]{:S(2)}, u32[]{:S(2)}) collective-permute-start(bf16[64,2048]{1,0:T(8,128)(2,1)S(1)} %add_convert_fusion.5), channel_id=1, source_target_pairs={{0,2},{2,4},{4,6},{6,7},{7,5},{5,3},{3,1},{1,0},{8,10},{10,12},{12... | collective-permute-start | bytes 786440 | tf_op jit(solution)/shard_map/ppermute | solution.py:60
  110.2 12.0 %collective-permute-start.22 = (bf16[64,2048]{1,0:T(8,128)(2,1)S(1)}, bf16[64,2048]{1,0:T(8,128)(2,1)S(1)}, u32[]{:S(2)}, u32[]{:S(2)}) collective-permute-start(bf16[64,2048]{1,0:T(8,128)(2,1)S(1)} %add_convert_fusion.10), channel_id=1, source_target_pairs={{0,2},{2,4},{4,6},{6,7},{7,5},{5,3},{3,1},{1,0},{8,10},{10,12},{12... | collective-permute-start | bytes 786440 | tf_op jit(solution)/shard_map/ppermute | solution.py:60
  115.4 14.6 %collective-permute-start.26 = (bf16[64,2048]{1,0:T(8,128)(2,1)S(1)}, bf16[64,2048]{1,0:T(8,128)(2,1)S(1)}, u32[]{:S(2)}, u32[]{:S(2)}) collective-permute-start(bf16[64,2048]{1,0:T(8,128)(2,1)S(1)} %add_convert_fusion.7), channel_id=1, source_target_pairs={{0,1},{2,0},{4,2},{6,4},{7,6},{5,7},{3,5},{1,3},{8,9},{10,8},{12,1... | collective-permute-start | bytes 786440 | tf_op jit(solution)/shard_map/ppermute | solution.py:60
  117.0 14.9 %collective-permute-start.29 = (bf16[64,2048]{1,0:T(8,128)(2,1)S(1)}, bf16[64,2048]{1,0:T(8,128)(2,1)S(1)}, u32[]{:S(2)}, u32[]{:S(2)}) collective-permute-start(bf16[64,2048]{1,0:T(8,128)(2,1)S(1)} %add_convert_fusion.4), channel_id=1, source_target_pairs={{0,2},{2,4},{4,6},{6,7},{7,5},{5,3},{3,1},{1,0},{8,10},{10,12},{12... | collective-permute-start | bytes 786440 | tf_op jit(solution)/shard_map/ppermute | solution.py:60
  117.6 10.6 %collective-permute-start.31 = (bf16[64,2048]{1,0:T(8,128)(2,1)S(1)}, bf16[64,2048]{1,0:T(8,128)(2,1)S(1)}, u32[]{:S(2)}, u32[]{:S(2)}) collective-permute-start(bf16[64,2048]{1,0:T(8,128)(2,1)S(1)} %add_convert_fusion.2), channel_id=1, source_target_pairs={{0,1},{2,0},{4,2},{6,4},{7,6},{5,7},{3,5},{1,3},{8,9},{10,8},{12,1... | collective-permute-start | bytes 786440 | tf_op jit(solution)/shard_map/ppermute | solution.py:60
  122.3 9.6 %collective-permute-start.23 = (bf16[64,2048]{1,0:T(8,128)(2,1)S(1)}, bf16[64,2048]{1,0:T(8,128)(2,1)S(1)}, u32[]{:S(2)}, u32[]{:S(2)}) collective-permute-start(bf16[64,2048]{1,0:T(8,128)(2,1)S(1)} %add_convert_fusion.9), channel_id=1, source_target_pairs={{0,2},{2,4},{4,6},{6,7},{7,5},{5,3},{3,1},{1,0},{8,10},{10,12},{12... | collective-permute-start | bytes 786440 | tf_op jit(solution)/shard_map/ppermute | solution.py:60
  128.3 6.4 %collective-permute-start.32 = (bf16[64,2048]{1,0:T(8,128)(2,1)S(1)}, bf16[64,2048]{1,0:T(8,128)(2,1)S(1)}, u32[]{:S(2)}, u32[]{:S(2)}) collective-permute-start(bf16[64,2048]{1,0:T(8,128)(2,1)S(1)} %add_convert_fusion.1), channel_id=1, source_target_pairs={{0,1},{2,0},{4,2},{6,4},{7,6},{5,7},{3,5},{1,3},{8,9},{10,8},{12,1... | collective-permute-start | bytes 786440 | tf_op jit(solution)/shard_map/ppermute | solution.py:60

commit v3 on v2

v3 whole, which is shorter than its diff:
```python
import functools

import jax
import jax.numpy as jnp
from jax import lax
from jax.experimental import pallas as pl
from jax.experimental.pallas import tpu as pltpu
from jax.sharding import PartitionSpec as P

WINDOW = 512
CHUNKS = 2
F32 = jnp.float32
BF16 = jnp.bfloat16
LOG2E = 1.4426950408889634


def call(body, grid, in_specs, out_specs, out_shape, scratch=(), prefetch=1, vmem=8, cost=None):
    return pl.pallas_call(
        body,
        grid_spec=pltpu.PrefetchScalarGridSpec(
            num_scalar_prefetch=prefetch,
            grid=grid,
            in_specs=in_specs,
            out_specs=out_specs,
            scratch_shapes=list(scratch),
        ),
        out_shape=out_shape,
        cost_estimate=cost,
        compiler_params=pltpu.CompilerParams(vmem_limit_bytes=vmem * 1024 * 1024),
    )


def cost(flops, moved, exps=0):
    return pl.CostEstimate(flops=int(flops), bytes_accessed=int(moved), transcendentals=int(exps))


WHOLE = pl.BlockSpec(memory_space=pltpu.VMEM)
AFTER = pl.BlockSpec(memory_space=pl.ANY)


def fixed(shape):
    return pl.BlockSpec(shape, lambda *_: (0,) * len(shape))


def mm(left, right, dims=((1,), (0,))):
    return lax.dot_general(left, right, (dims, ((), ())), preferred_element_type=F32)


def sigmoid(x):
    return 0.5 * jnp.tanh(0.5 * x) + 0.5


def ring_order(count):
    return list(range(0, count, 2)) + list(range(count - 1, 0, -2))


def ring_send(value, step):
    order = ring_order(lax.axis_size("head"))
    count = len(order)
    return lax.ppermute(
        value, "head", [(order[i], order[(i + step) % count]) for i in range(count)]
    )


def ring_ids(offsets):
    count = lax.axis_size("head")
    me = lax.axis_index("head")
    place = jnp.where(me % 2 == 0, me // 2, count - 1 - me // 2)
    ids = []
    for offset in offsets:
        at = (place + offset) % count
        ids.append(jnp.where(at < count // 2, 2 * at, 2 * (count - 1 - at) + 1))
    return jnp.stack(ids).astype(jnp.int32)


def load(arrays, blocks, order):
    count = len(arrays)
    sizes = [array.shape[0] // blocks for array in arrays]

    def body(order_ref, *refs):
        out_refs, sems = refs[count:-1], refs[-1]
        copies = [
            pltpu.make_async_copy(
                refs[index].at[pl.ds(pl.multiple_of(order_ref[block] * size, size), size)],
                out_refs[index].at[pl.ds(block * size, size)],
                sems.at[index, block],
            )
            for index, size in enumerate(sizes)
            for block in range(blocks)
        ]
        for copy in copies:
            copy.start()
        for copy in copies:
            copy.wait()

    return call(
        body,
        (),
        [pl.BlockSpec(memory_space=pltpu.HBM)] * count,
        [WHOLE] * count,
        [jax.ShapeDtypeStruct(array.shape, array.dtype) for array in arrays],
        [pltpu.SemaphoreType.DMA((count, blocks))],
        vmem=1,
        cost=cost(0, sum(4 * array.size for array in arrays)),
    )(order, *[pltpu.with_memory_space_constraint(array, pltpu.HBM) for array in arrays])


def split_rows(tokens):
    rows, width = tokens.shape[0] // CHUNKS, tokens.shape[1]

    def body(in_ref, *refs):
        out_refs, sems = refs[:-1], refs[-1]
        copies = [
            pltpu.make_async_copy(in_ref.at[pl.ds(c * rows, rows)], out_refs[c], sems.at[c])
            for c in range(CHUNKS)
        ]
        for copy in copies:
            copy.start()
        for copy in copies:
            copy.wait()

    return pl.pallas_call(
        body,
        in_specs=[pl.BlockSpec(memory_space=pltpu.HBM)],
        out_specs=[WHOLE] * CHUNKS,
        out_shape=[jax.ShapeDtypeStruct((rows, width), tokens.dtype)] * CHUNKS,
        scratch_shapes=[pltpu.SemaphoreType.DMA((CHUNKS,))],
        cost_estimate=cost(0, 4 * rows * width),
        compiler_params=pltpu.CompilerParams(vmem_limit_bytes=1024 * 1024),
    )(pltpu.with_memory_space_constraint(tokens, pltpu.HBM))


def ring_offsets():
    steps = lax.axis_size("head") // 2
    return [0] + [way * step for step in range(1, steps) for way in (-1, 1)] + [steps]


def gather_pieces(own, longer):
    steps = lax.axis_size("head") // 2
    pieces = [own]
    held = {1: own, -1: own}
    for step in range(1, steps + 1):
        for way in (1, -1):
            if step < steps or way == longer:
                held[way] = ring_send(held[way], way)
                pieces.append(held[way])
    return pieces


def accumulate(chunks, first, last, weights, before=None, lead=0):
    rows, depth = chunks[0][0].shape
    width = weights[0].shape[1]
    parts, span = len(weights), last - first
    total = rows * len(chunks)
    final = last == len(chunks[0])
    dtype = BF16 if final else F32
    pieces = [chunk[index] for chunk in chunks for index in range(first, last)]

    def body(*refs):
        piece_refs = refs[: len(pieces)]
        weight_refs = refs[len(pieces) : len(pieces) + parts]
        out_ref, left = refs[-2:]
        for index, ref in enumerate(piece_refs):
            chunk, piece = divmod(index, span)
            left[chunk * rows : (chunk + 1) * rows, piece * depth : (piece + 1) * depth] = ref[...]
        for part in range(parts):
            term = mm(left[...], weight_refs[part][first * depth : last * depth])
            if before is not None:
                term = term + refs[-3][lead + part]
            out_ref[part] = term.astype(dtype)

    aliased = before is not None and not final
    args = [*pieces, *weights] + ([] if before is None else [before])
    return pl.pallas_call(
        body,
        in_specs=[WHOLE] * len(args),
        out_specs=WHOLE,
        out_shape=jax.ShapeDtypeStruct((parts, total, width), dtype),
        scratch_shapes=[pltpu.VMEM((total, span * depth), BF16)],
        input_output_aliases={len(args) - 1: 0} if aliased else {},
        cost_estimate=cost(
            2 * total * span * depth * width * parts,
            2 * span * depth * (total + width * parts) + 8 * total * width * parts,
        ),
        compiler_params=pltpu.CompilerParams(vmem_limit_bytes=12 * 1024 * 1024),
    )(*args)


def head_grads(base, heads, kv, rate, fast_gate, fast_up, fast_down, before=None):
    rows = kv.shape[1]
    size, hidden_size = fast_gate.shape[1:]
    lanes = rate.shape[0]

    def body(base_ref, k_ref, v_ref, rate_ref, gate_ref, up_ref, down_ref, *rest):
        head = base_ref[0] + pl.program_id(0)
        lane = lax.broadcasted_iota(jnp.int32, (rows, lanes), 1)
        mine = jnp.sum(jnp.where(lane == head, rate_ref[...].T, 0.0), axis=1, keepdims=True)
        key = k_ref[0].astype(F32)
        knorm = key * lax.rsqrt(jnp.mean(key * key, axis=-1, keepdims=True) + 1e-06)
        target = (-mine * v_ref[0].astype(F32)).astype(BF16)
        knorm = knorm.astype(BF16)
        gate_pre = mm(knorm, gate_ref[0].astype(BF16))
        up_pre = mm(knorm, up_ref[0].astype(BF16))
        back = mm(target, down_ref[0].astype(BF16), ((1,), (1,)))
        sigma = sigmoid(gate_pre)
        active = gate_pre * sigma
        first = (back * up_pre * (sigma + active * (1.0 - sigma))).astype(BF16)
        second = (back * active).astype(BF16)
        third = (active * up_pre).astype(BF16)
        terms = (
            mm(knorm, first, ((0,), (0,))),
            mm(knorm, second, ((0,), (0,))),
            mm(target, third, ((0,), (0,))),
        )
        for index, term in enumerate(terms):
            if before is not None:
                term = term + rest[0][0, index]
                rest[-1][0, index] = term.astype(BF16)
                rest[-2][0, index] = term
            else:
                rest[-1][0, index] = term

    def spec(shape):
        return pl.BlockSpec((1,) + shape, lambda h, b: (b[0] + h,) + (0,) * len(shape))

    own = pl.BlockSpec((1, 3, size, hidden_size), lambda h, b: (h, 0, 0, 0))
    args = [kv, kv, rate, fast_gate, fast_up, fast_down]
    specs = [
        pl.BlockSpec((1, rows, size), lambda h, b: (0, 0, b[0] + h)),
        pl.BlockSpec((1, rows, size), lambda h, b: (1, 0, b[0] + h)),
        fixed(rate.shape),
        spec((size, hidden_size)),
        spec((size, hidden_size)),
        spec((hidden_size, size)),
    ]
    kinds = [F32]
    if before is not None:
        args.append(before)
        specs.append(own)
        kinds.append(BF16)
    return call(
        body,
        (heads,),
        specs,
        [own] * len(kinds),
        [jax.ShapeDtypeStruct((heads, 3, size, hidden_size), kind) for kind in kinds],
        cost=cost(
            12 * heads * rows * size * hidden_size,
            8 * heads * 3 * size * hidden_size,
            heads * rows * hidden_size,
        ),
    )(base, *args)


def renew(base, kept, received, step, fast_gate, fast_up, fast_down, after):
    heads, _, size, hidden_size = kept.shape

    def body(base_ref, step_ref, kept_ref, gate_ref, up_ref, down_ref, *rest):
        out_ref = rest[-1]
        pace = step_ref[base_ref[0] + pl.program_id(0)]
        for index in range(3):
            grad = kept_ref[0, index]
            for more in rest[: len(received)]:
                grad = grad + more[0, index].astype(F32)
            if index < 2:
                matrix = (gate_ref, up_ref)[index][0]
                fan = size
            else:
                matrix = down_ref[0].T
                fan = hidden_size
            mean_sq = jnp.sum(grad * grad, keepdims=True) / (size * hidden_size)
            scale = pace * fan ** (-0.5) * lax.rsqrt(mean_sq + 1e-06)
            out_ref[0, index] = (matrix - scale * grad).astype(BF16)

    def spec(shape):
        return pl.BlockSpec((1,) + shape, lambda h, b, s: (b[0] + h,) + (0,) * len(shape))

    own = pl.BlockSpec((1, 3, size, hidden_size), lambda h, b, s: (h, 0, 0, 0))
    return call(
        body,
        (heads,),
        [own, spec((size, hidden_size)), spec((size, hidden_size)), spec((hidden_size, size))]
        + [own] * len(received)
        + [AFTER] * len(after),
        own,
        jax.ShapeDtypeStruct(kept.shape, BF16),
        prefetch=2,
        cost=cost(10 * kept.size, 12 * kept.size),
    )(base, step, kept, fast_gate, fast_up, fast_down, *received, *after)


def attend(place, query, kv, beside, behind, size):
    total = query.shape[1]
    heads = query.shape[2] // size
    rows = total // 2
    factor = size ** (-0.5) * LOG2E

    def body(place_ref, q_ref, k_ref, v_ref, k_beside, v_beside, k_behind, v_behind, out_ref):
        has_halo = place_ref[0] > 0
        odd = place_ref[0] % 2 == 1
        keys = (jnp.where(odd, k_beside[0], k_behind[0]), k_ref[0])
        values = (jnp.where(odd, v_beside[0], v_behind[0]), v_ref[0])
        row = lax.broadcasted_iota(jnp.int32, (rows, rows), 0)
        col = lax.broadcasted_iota(jnp.int32, (rows, rows), 1)

        def block(pair, index):
            side, at = divmod(index, 2)
            return pair[side][at * rows : (at + 1) * rows]

        for index in range(2):
            query_block = q_ref[0, index * rows : (index + 1) * rows]
            scores = []
            for source in range(index, index + 3):
                part = mm(query_block, block(keys, source), ((1,), (1,))) * factor
                if source == index:
                    part = jnp.where((col > row) & has_halo, part, -1e30)
                elif source == index + 2:
                    part = jnp.where(col <= row, part, -1e30)
                elif source < 2:
                    part = jnp.where(has_halo, part, -1e30)
                scores.append(part)
            top = functools.reduce(
                jnp.maximum, [jnp.max(part, axis=-1, keepdims=True) for part in scores]
            )
            sums, result = 0.0, 0.0
            for part, source in zip(scores, range(index, index + 3)):
                expo = jnp.exp2(part - top)
                sums = sums + jnp.sum(expo, axis=-1, keepdims=True)
                result = result + mm(expo.astype(BF16), block(values, source))
            out_ref[index * rows : (index + 1) * rows] = result / sums

    def spec(which):
        return pl.BlockSpec((1, total, size), lambda h, p: (which, 0, h))

    return call(
        body,
        (heads,),
        [spec(0)] + [spec(0), spec(1)] * 3,
        pl.BlockSpec((total, size), lambda h, p: (0, h)),
        jax.ShapeDtypeStruct((total, heads * size), F32),
        cost=cost(
            24 * heads * size * rows * rows,
            8 * total * heads * size,
            6 * heads * rows * rows,
        ),
    )(place, query, kv, kv, beside, beside, behind, behind)


def apply_fast(base, query, attended, nets):
    rows = query.shape[1]
    heads, _, size, hidden_size = nets.shape

    def body(base_ref, q_ref, attended_ref, net_ref, out_ref):
        query = q_ref[0].astype(F32)
        qnorm = query * lax.rsqrt(jnp.mean(query * query, axis=-1, keepdims=True) + 1e-06)
        qnorm = qnorm.astype(BF16)
        gate_pre = mm(qnorm, net_ref[0, 0])
        hidden = gate_pre * sigmoid(gate_pre) * mm(qnorm, net_ref[0, 1])
        fast = mm(hidden.astype(BF16), net_ref[0, 2], ((1,), (1,)))
        out_ref[...] = (attended_ref[...] + fast).astype(BF16)

    return call(
        body,
        (heads,),
        [
            pl.BlockSpec((1, rows, size), lambda h, b: (0, 0, b[0] + h)),
            pl.BlockSpec((rows, size), lambda h, b: (0, b[0] + h)),
            pl.BlockSpec((1, 3, size, hidden_size), lambda h, b: (h, 0, 0, 0)),
        ],
        pl.BlockSpec((rows, size), lambda h, b: (0, h)),
        jax.ShapeDtypeStruct((rows, heads * size), BF16),
        cost=cost(
            6 * heads * rows * size * hidden_size,
            8 * heads * rows * size,
            heads * rows * hidden_size,
        ),
    )(base, query, attended, nets)


def partial_out(ids, side, near, far, w_out, after=()):
    rows = near.shape[0] // lax.axis_size("head")
    depth = near.shape[1]
    count = ids.shape[0]
    width = w_out.shape[1]
    block = width // 8

    def body(ids_ref, side_ref, near_ref, far_ref, w_ref, *refs):
        out_refs = refs[len(after) :]
        lefts = [
            jnp.concatenate(
                [
                    ref[pl.ds(pl.multiple_of(ids_ref[index] * rows, rows), rows)]
                    for index in range(count)
                ],
                axis=0,
            )
            for ref in (near_ref, far_ref)
        ]
        near_row = pl.multiple_of(side_ref[0] * depth, depth)
        far_row = pl.multiple_of((1 - side_ref[0]) * depth, depth)
        for column in range(0, width, block):
            result = mm(lefts[0], w_ref[pl.ds(near_row, depth), column : column + block])
            result += mm(lefts[1], w_ref[pl.ds(far_row, depth), column : column + block])
            result = result.astype(BF16)
            half, at = divmod(column, width // 2)
            for index in range(count):
                out_refs[2 * index + half][:, at : at + block] = result[
                    index * rows : (index + 1) * rows
                ]

    outs = call(
        body,
        (),
        [WHOLE] * 3 + [AFTER] * len(after),
        [WHOLE] * (2 * count),
        [jax.ShapeDtypeStruct((rows, width // 2), BF16)] * (2 * count),
        prefetch=2,
        vmem=16,
        cost=cost(4 * count * rows * depth * width, 2 * width * (2 * depth + count * rows)),
    )(ids, side, near, far, w_out, *after)
    return [tuple(outs[2 * index : 2 * index + 2]) for index in range(count)]


def ring_reduce(side, near, far, w_out):
    count = lax.axis_size("head")
    steps = count // 2
    signed = [sign * step for step in range(steps - 1, 0, -1) for sign in (1, -1)]
    first, second = [steps] + signed[:2], signed[2:] + [0]
    parts = dict(zip(first, partial_out(ring_ids(first), side, near, far, w_out)))
    coming = {}
    ordered = ()
    for which in range(2 * steps - 1):
        step, lane = steps - (which + 1) // 2, which % 2
        if which == 2:
            after = tuple(coming.values())
            later = partial_out(ring_ids(second), side, near, far, w_out, after[:2])
            parts |= dict(zip(second, later))
        terms = []
        for way in (1, -1):
            half = lane if way == 1 else 1 - lane
            term = parts[steps if step == steps else way * step][half]
            if (way, half) in coming:
                term = (term.astype(F32) + coming[way, half].astype(F32)).astype(BF16)
            terms.append(term)
        ordered = lax.optimization_barrier((*terms, *ordered))[:2]
        for way, term in zip((1, -1), ordered):
            coming[way, lane if way == 1 else 1 - lane] = ring_send(term, way)
    ends = []
    for which in range(2):
        total = parts[0][which].astype(F32)
        for way in (1, -1):
            if (way, which) in coming:
                total = total + coming[way, which].astype(F32)
        ends.append(total.astype(BF16))
    return jnp.concatenate(ends, axis=1)


def swap(value, bit):
    count = lax.axis_size("tok")
    return lax.ppermute(value, "tok", [(index, index ^ bit) for index in range(count)])


def shards(
    tokens, w_query, w_key, w_value, w_out, fast_gate, fast_up, fast_down, token_rate, head_step
):
    local_heads, head_size, _ = fast_gate.shape
    tok_count = lax.axis_size("tok")
    place = lax.axis_index("tok").astype(jnp.int32)
    pair = local_heads // 2
    side = (place % 2).reshape(1)
    near_base, far_base = side * pair, (1 - side) * pair
    nets = (fast_gate, fast_up, fast_down)

    own = split_rows(tokens)
    chunks = [gather_pieces(own[c], 1 if c % 2 == 0 else -1) for c in range(CHUNKS)]
    offsets = ring_offsets()
    rate = token_rate.T
    order, rate_beside = lax.optimization_barrier((ring_ids(offsets), swap(rate, 1)))
    weights = load([w_key, w_value, w_query], len(offsets), order)
    sums, done = None, 0
    for step in range(1, len(offsets) // 2):
        sums = accumulate(chunks, done, 2 * step + 1, weights, sums)
        done = 2 * step + 1
    kv = accumulate(chunks, done, len(offsets), weights[:2], sums)
    query = accumulate(chunks, done, len(offsets), weights[2:], sums, 2)

    beside = swap(kv, 1)
    behind = lax.ppermute(kv, "tok", [(index, index + 1) for index in range(1, tok_count - 1, 2)])
    (grads,) = head_grads(near_base, pair, kv, rate, *nets)
    grads, travel = head_grads(near_base, pair, beside, rate_beside, *nets, grads)
    received = []
    for bit in range(1, tok_count.bit_length() - 1):
        if received:
            travel = grads
            for more in received:
                travel = travel + more.astype(F32)
            travel = travel.astype(BF16)
        received.append(swap(travel, 1 << bit))
    attended = attend(place.reshape(1), query, kv, beside, behind, head_size)
    mine = renew(near_base, grads, received, head_step, *nets, (attended,))
    other = swap(mine, 1)
    near = apply_fast(near_base, query, attended, mine)
    far = apply_fast(far_base, query, attended, other)
    return ring_reduce(side, near, far, w_out)


def solution(mesh):
    placed = (
        P("tok", "head"),
        P(None, "head"),
        P(None, "head"),
        P(None, "head"),
        P("head", None),
        P("head", None, None),
        P("head", None, None),
        P("head", None, None),
        P("tok", "head"),
        P("head"),
    )
    return jax.shard_map(
        shards, mesh=mesh, in_specs=placed, out_specs=P(("tok", "head"), None), check_vma=False
    )
```

time: 136 us -> 127 us (0.934)
  waiting for transfers between devices: 50.5 us -> 39.3 us
  local copies, waits for them, and re-layouts: 6.86 us -> 12.7 us
  starting transfers between devices: 38.3 us -> 35.8 us
  Pallas kernels: 37.6 us -> 35.8 us
    ppermute x28, waiting for transfers between devices: 50.1 us -> 35.6 us  [ring_send(): lax.ppermute(value, 'head', [(order[i], order[(i + step) % count]) for i...]
    unnamed x28 -> x54, local copies, waits for them, and re-layouts: 6.61 us -> 12.5 us
    ppermute x3 -> x4, waiting for transfers between devices: 0.4 us -> 3.69 us  [swap(): lax.ppermute(value, 'tok', [(index, index ^ bit) for index in range(count)])]
    ppermute x2 -> x1, starting transfers between devices: 3.98 us -> 1.65 us  [shards(): lax.ppermute(kv, 'tok', [(index, index + 1) for index in range(1, tok_cou...]
    pallas_call x11 -> x10, Pallas kernels: 30 us -> 28.6 us  [the longest x5 10.7 us: accumulate(): pl.pallas_call(body, in_specs=[WHOLE] * len(args), out_specs=WHOLE, out_s...]
    ppermute x3 -> x4, starting transfers between devices: 4.16 us -> 3.12 us  [swap(): lax.ppermute(value, 'tok', [(index, index ^ bit) for index in range(count)])]
where the time goes in v3:
time: 127 us; the launch traced here: 126 us
  waiting for transfers between devices  39.3 us (31%)
  Pallas kernels  35.8 us (28%)
  starting transfers between devices  35.8 us (28%)
  local copies, waits for them, and re-layouts  12.7 us (10%)
  other arithmetic  1.75 us (1%)
    ppermute x28, waiting for transfers between devices, ring_send(): lax.ppermute(value, 'head', [(order[i], order[(i + step) % count]) for i...  35.6 us
    ppermute x28, starting transfers between devices, ring_send(): lax.ppermute(value, 'head', [(order[i], order[(i + step) % count]) for i...  31.1 us
    unnamed x54, local copies, waits for them, and re-layouts  12.5 us
    pallas_call x5, Pallas kernels, accumulate(): pl.pallas_call(body, in_specs=[WHOLE] * len(args), out_specs=WHOLE, out_s...  10.7 us
    pallas_call x2, Pallas kernels, head_grads(): call(body, (heads,), specs, [own] * len(kinds), [jax.ShapeDtypeStruct((he...  5.79 us
    pallas_call x1, Pallas kernels, attend(): call(body, (heads,), [spec(0)] + [spec(0), spec(1)] * 3, pl.BlockSpec((to...  5.73 us
    pallas_call x1, Pallas kernels, load(): call(body, (), [pl.BlockSpec(memory_space=pltpu.HBM)] * count, [WHOLE] *...  5.32 us
    ppermute x4, waiting for transfers between devices, swap(): lax.ppermute(value, 'tok', [(index, index ^ bit) for index in range(count)])  3.69 us
  transfers between devices with their start and end apart: 33, of which 17 were waited for; matrix products, arithmetic and copies ran while one was open for 1% of the time, Pallas kernels for 23%

profile of v3, /device:TPU:0, one launch (start us, length us, event | category | flops | bytes accessed | tf_op | source)
XLA Modules:
  0.0 126.0 jit_solution(12009068685258308059)
XLA Ops:
  0.0 1.0 shard_map.100
  1.1 3.1 %collective-permute-start = (bf16[256,512]{1,0:T(8,128)(2,1)S(1)}, bf16[256,512]{1,0:T(8,128)(2,1)S(1)}, u32[]{:S(2)}, u32[]{:S(2)}) collective-permute-start(bf16[256,512]{1,0:T(8,128)(2,1)S(1)} %get-tuple-element.44.refs_0_), channel_id=1, source_target_pairs={{0,2},{2,4},{4,6},{6,7},{7,5},{5,3},{3,1},{1,0},{8,10},{10,12},{12... | collective-permute-start | bytes 786440 | tf_op jit(solution)/shard_map/ppermute | solution.py:60
  4.1 1.9 %collective-permute-start.9 = (bf16[256,512]{1,0:T(8,128)(2,1)S(1)}, bf16[256,512]{1,0:T(8,128)(2,1)S(1)}, u32[]{:S(2)}, u32[]{:S(2)}) collective-permute-start(bf16[256,512]{1,0:T(8,128)(2,1)S(1)} %get-tuple-element.44.refs_0_), channel_id=1, source_target_pairs={{0,1},{2,0},{4,2},{6,4},{7,6},{5,7},{3,5},{1,3},{8,9},{10,8},{12,1... | collective-permute-start | bytes 786440 | tf_op jit(solution)/shard_map/ppermute | solution.py:60
  6.2 0.7 copy-done.15
  6.9 4.3 %collective-permute-done.refs_1_ = bf16[256,512]{1,0:T(8,128)(2,1)S(1)} collective-permute-done((bf16[256,512]{1,0:T(8,128)(2,1)S(1)}, bf16[256,512]{1,0:T(8,128)(2,1)S(1)}, u32[]{:S(2)}, u32[]{:S(2)}) %collective-permute-start) | collective-permute-done | bytes 262176 | tf_op jit(solution)/shard_map/ppermute | solution.py:60
  11.2 2.1 %collective-permute-start.1 = (bf16[256,512]{1,0:T(8,128)(2,1)S(1)}, bf16[256,512]{1,0:T(8,128)(2,1)}, u32[]{:S(2)}, u32[]{:S(2)}) collective-permute-start(bf16[256,512]{1,0:T(8,128)(2,1)S(1)} %collective-permute-done.refs_1_), channel_id=1, source_target_pairs={{0,2},{2,4},{4,6},{6,7},{7,5},{5,3},{3,1},{1,0},{8,10},{10,12},{12... | collective-permute-start | bytes 786440 | tf_op jit(solution)/shard_map/ppermute | solution.py:60
  13.3 0.7 copy-done.17
  14.0 0.7 copy-done.19
  14.7 4.2 %collective-permute-done.9.refs_2_ = bf16[256,512]{1,0:T(8,128)(2,1)S(1)} collective-permute-done((bf16[256,512]{1,0:T(8,128)(2,1)S(1)}, bf16[256,512]{1,0:T(8,128)(2,1)S(1)}, u32[]{:S(2)}, u32[]{:S(2)}) %collective-permute-start.9) | collective-permute-done | bytes 262176 | tf_op jit(solution)/shard_map/ppermute | solution.py:60
  19.0 2.0 %collective-permute-start.13 = (bf16[256,512]{1,0:T(8,128)(2,1)S(1)}, bf16[256,512]{1,0:T(8,128)(2,1)}, u32[]{:S(2)}, u32[]{:S(2)}) collective-permute-start(bf16[256,512]{1,0:T(8,128)(2,1)S(1)} %collective-permute-done.12.refs_4_), channel_id=1, source_target_pairs={{0,2},{2,4},{4,6},{6,7},{7,5},{5,3},{3,1},{1,0},{8,10},{10,12},{12... | collective-permute-start | bytes 786440 | tf_op jit(solution)/shard_map/ppermute | solution.py:60
  21.0 1.5 %collective-permute-done.1.refs_0_ = bf16[256,512]{1,0:T(8,128)(2,1)} collective-permute-done((bf16[256,512]{1,0:T(8,128)(2,1)S(1)}, bf16[256,512]{1,0:T(8,128)(2,1)}, u32[]{:S(2)}, u32[]{:S(2)}) %collective-permute-start.1) | collective-permute-done | bytes 262176 | tf_op jit(solution)/shard_map/ppermute | solution.py:60
  22.5 2.1 %collective-permute-start.2 = (bf16[256,512]{1,0:T(8,128)(2,1)}, bf16[256,512]{1,0:T(8,128)(2,1)}, u32[]{:S(2)}, u32[]{:S(2)}) collective-permute-start(bf16[256,512]{1,0:T(8,128)(2,1)} %collective-permute-done.1.refs_0_), channel_id=1, source_target_pairs={{0,2},{2,4},{4,6},{6,7},{7,5},{5,3},{3,1},{1,0},{8,10},{10,12},{12... | collective-permute-start | bytes 786440 | tf_op jit(solution)/shard_map/ppermute | solution.py:60
  25.0 1.1 collective-permute-done.8.rate_ref
  26.1 5.3 %shard_map.101 = (bf16[4096,512]{1,0:T(8,128)(2,1)S(1)}, bf16[4096,512]{1,0:T(8,128)(2,1)S(1)}, bf16[4096,512]{1,0:T(8,128)(2,1)S(1)}) custom-call(s32[8]{0:T(128)S(1)} %stack.50.order_ref, bf16[4096,512]{1,0:T(8,128)(2,1)} %refs_0_.1, bf16[4096,512]{1,0:T(8,128)(2,1)} %refs_1_.1, bf16[4096,512]{1,0:T(8,128)(2,1)} %refs_2_.1), custom_call_target="tpu_custom_call" | custom-call | bytes 25165824 | tf_op jit(solution)/shard_map/pallas_call | solution.py:96
  31.5 2.0 %collective-permute-start.11 = (bf16[256,512]{1,0:T(8,128)(2,1)}, bf16[256,512]{1,0:T(8,128)(2,1)S(1)}, u32[]{:S(2)}, u32[]{:S(2)}) collective-permute-start(bf16[256,512]{1,0:T(8,128)(2,1)} %collective-permute-done.10.refs_1_), channel_id=1, source_target_pairs={{0,1},{2,0},{4,2},{6,4},{7,6},{5,7},{3,5},{1,3},{8,9},{10,8},{12,1... | collective-permute-start | bytes 786440 | tf_op jit(solution)/shard_map/ppermute | solution.py:60
  33.6 0.9 copy-done.22
  34.6 0.9 copy-done.24
  35.5 2.6 %shard_map.102.refs_7_ = f32[3,512,512]{2,1,0:T(8,128)S(1)} custom-call(bf16[256,512]{1,0:T(8,128)(2,1)S(1)} %get-tuple-element.44.refs_0_, bf16[256,512]{1,0:T(8,128)(2,1)S(1)} %copy-done.18, bf16[256,512]{1,0:T(8,128)(2,1)S(1)} %copy-done.22, bf16[256,512]{1,0:T(8,128)(2,1)S(1)} %copy-done.16, bf16[256,512]{1,0:T(8,128)(2,1)S(1)} %copy-done.24, ...), custom_call_target="tpu_custom_call" | custom-call | flops 2415919104 | bytes 12582912 | tf_op jit(solution)/shard_map/pallas_call | solution.py:174
  38.1 2.0 %collective-permute-start.3 = (bf16[256,512]{1,0:T(8,128)(2,1)}, bf16[256,512]{1,0:T(8,128)(2,1)S(1)}, u32[]{:S(2)}, u32[]{:S(2)}) collective-permute-start(bf16[256,512]{1,0:T(8,128)(2,1)} %collective-permute-done.2.refs_0_), channel_id=1, source_target_pairs={{0,2},{2,4},{4,6},{6,7},{7,5},{5,3},{3,1},{1,0},{8,10},{10,12},{12... | collective-permute-start | bytes 786440 | tf_op jit(solution)/shard_map/ppermute | solution.py:60
  40.2 3.0 %shard_map.103.refs_7_ = f32[3,512,512]{2,1,0:T(8,128)S(1)} custom-call(bf16[256,512]{1,0:T(8,128)(2,1)} %collective-permute-done.1.refs_0_, bf16[256,512]{1,0:T(8,128)(2,1)} %collective-permute-done.10.refs_1_, bf16[256,512]{1,0:T(8,128)(2,1)} %collective-permute-done.13.refs_2_, ...), custom_call_target="tpu_custom_call", output_to_operand_aliasing={{}: (7, {})} | custom-call | flops 1610612736 | bytes 10485760 | tf_op jit(solution)/shard_map/pallas_call | solution.py:174
  43.3 2.9 %shard_map.104.refs_3_.refs_4_ = f32[3,512,512]{2,1,0:T(8,128)S(1)} custom-call(bf16[256,512]{1,0:T(8,128)(2,1)} %collective-permute-done.2.refs_0_, bf16[256,512]{1,0:T(8,128)(2,1)S(1)} %collective-permute-done.11.refs_1_, bf16[256,512]{1,0:T(8,128)(2,1)S(1)} %collective-permute-done.14.refs_2_, ...), custom_call_target="tpu_custom_call", output_to_operand_aliasing={{}: (7, {})} | custom-call | flops 1610612736 | bytes 10485760 | tf_op jit(solution)/shard_map/pallas_call | solution.py:174
  46.2 1.2 collective-permute-done.3.refs_0_
  47.4 0.5 collective-permute-done.7.refs_1_
  47.9 1.7 %shard_map.106.k_ref.v_ref = bf16[2,512,512]{2,1,0:T(8,128)(2,1)} custom-call(bf16[256,512]{1,0:T(8,128)(2,1)S(1)} %collective-permute-done.3.refs_0_, bf16[256,512]{1,0:T(8,128)(2,1)S(1)} %collective-permute-done.7.refs_1_, bf16[4096,512]{1,0:T(8,128)(2,1)S(1)} %get-tuple-element.48.refs_6_.refs_4_.refs_2_, ...), custom_call_target="tpu_custom_call" | custom-call | flops 536870912 | bytes 5767168 | tf_op jit(solution)/shard_map/pallas_call | solution.py:174
  49.6 1.6 %collective-permute-start.16 = (bf16[2,512,512]{2,1,0:T(8,128)(2,1)}, bf16[2,512,512]{2,1,0:T(8,128)(2,1)}, u32[]{:S(2)}, u32[]{:S(2)}) collective-permute-start(bf16[2,512,512]{2,1,0:T(8,128)(2,1)} %shard_map.106.k_ref.v_ref), channel_id=1, source_target_pairs={{8,16},{9,17},{10,18},{11,19},{12,20},{13,21},{14,22},{15,23}} | collective-permute-start | bytes 3145736 | tf_op jit(solution)/shard_map/ppermute | solution.py:488
  51.3 1.0 copy-done.4
  52.3 1.0 copy-done.7
  53.4 1.0 copy-done.10
  54.4 3.0 %shard_map.108.rest_0_ = f32[2,3,128,256]{3,2,1,0:T(8,128)S(1)} custom-call(s32[1]{0:T(128)S(6)} %mul.80.base_ref, bf16[2,512,512]{2,1,0:T(8,128)(2,1)} %shard_map.106.k_ref.v_ref, bf16[2,512,512]{2,1,0:T(8,128)(2,1)} %shard_map.106.k_ref.v_ref, f32[4,512]{1,0:T(4,128)S(1)} %bitcast.12, f32[4,128,256]{2,1,0:T(8,128)S(1)} %copy-done.4, ...), custom_call_target="tpu_custom_call" | custom-call | flops 402653184 | bytes 1572864 | tf_op jit(solution)/shard_map/pallas_call | solution.py:241
  57.4 1.0 copy-done.5
  58.4 1.0 copy-done.8
  59.5 1.0 copy-done.11
  60.5 2.8 %shard_map.109 = (f32[2,3,128,256]{3,2,1,0:T(8,128)S(1)}, bf16[2,3,128,256]{3,2,1,0:T(8,128)(2,1)S(1)}) custom-call(s32[1]{0:T(128)S(6)} %mul.80.base_ref, bf16[2,512,512]{2,1,0:T(8,128)(2,1)} %collective-permute-done.15.k_beside.v_beside.k_ref.v_ref, bf16[2,512,512]{2,1,0:T(8,128)(2,1)} %collective-permute-done.15.k_beside.v_beside.k_ref.v_ref, ...), custom_call_target="tpu_custom_call" | custom-call | flops 402653184 | bytes 1572864 | tf_op jit(solution)/shard_map/pallas_call | solution.py:241
  63.4 1.2 collective-permute-start.17
  65.1 5.7 %shard_map.107.rest_1_.attended_ref = f32[512,512]{1,0:T(8,128)S(1)} custom-call(s32[1]{0:T(128)} %bitcast.10.place_ref, bf16[1,512,512]{2,1,0:T(8,128)(2,1)S(1)} %shard_map.105.q_ref, bf16[2,512,512]{2,1,0:T(8,128)(2,1)} %shard_map.106.k_ref.v_ref, bf16[2,512,512]{2,1,0:T(8,128)(2,1)} %shard_map.106.k_ref.v_ref, ...), custom_call_target="tpu_custom_call" | custom-call | flops 805306368 | bytes 2097152 | tf_op jit(solution)/shard_map/pallas_call | solution.py:335
  70.8 2.6 %collective-permute-done.17.rest_0_ = bf16[2,3,128,256]{3,2,1,0:T(8,128)(2,1)S(1)} collective-permute-done((bf16[2,3,128,256]{3,2,1,0:T(8,128)(2,1)S(1)}, bf16[2,3,128,256]{3,2,1,0:T(8,128)(2,1)S(1)}, u32[]{:S(2)}, u32[]{:S(2)}) %collective-permute-start.17) | collective-permute-done | bytes 393248 | tf_op jit(solution)/shard_map/ppermute | solution.py:460
  73.5 1.0 shard_map.110.net_ref
  74.5 1.9 %collective-permute-start.18 = (bf16[2,3,128,256]{3,2,1,0:T(8,128)(2,1)S(1)}, bf16[2,3,128,256]{3,2,1,0:T(8,128)(2,1)S(1)}, u32[]{:S(2)}, u32[]{:S(2)}) collective-permute-start(bf16[2,3,128,256]{3,2,1,0:T(8,128)(2,1)S(1)} %shard_map.110.net_ref), channel_id=1, source_target_pairs={{0,8},{8,0},{16,24},{24,16},{1,9},{9,1},{17,25},{25,17},{2,10},{10... | collective-permute-start | bytes 1179656 | tf_op jit(solution)/shard_map/ppermute | solution.py:460
  76.5 1.3 %shard_map.111.near_ref = bf16[512,256]{1,0:T(8,128)(2,1)S(1)} custom-call(s32[1]{0:T(128)S(6)} %mul.80.base_ref, bf16[1,512,512]{2,1,0:T(8,128)(2,1)S(1)} %shard_map.105.q_ref, f32[512,512]{1,0:T(8,128)S(1)} %shard_map.107.rest_1_.attended_ref, bf16[2,3,128,256]{3,2,1,0:T(8,128)(2,1)S(1)} %shard_map.110.net_ref), custom_call_target="tpu_custom_call" | custom-call | flops 201326592 | bytes 1048576 | tf_op jit(solution)/shard_map/pallas_call | solution.py:362
  77.8 1.3 %shard_map.112.far_ref = bf16[512,256]{1,0:T(8,128)(2,1)S(1)} custom-call(s32[1]{0:T(128)S(6)} %mul.87.base_ref, bf16[1,512,512]{2,1,0:T(8,128)(2,1)S(1)} %shard_map.105.q_ref, f32[512,512]{1,0:T(8,128)S(1)} %shard_map.107.rest_1_.attended_ref, bf16[2,3,128,256]{3,2,1,0:T(8,128)(2,1)S(1)} %collective-permute-done.18.net_ref), custom_call_target="tpu_custom_call" | custom-call | flops 201326592 | bytes 1048576 | tf_op jit(solution)/shard_map/pallas_call | solution.py:362
  79.1 1.6 %shard_map.113 = (bf16[64,2048]{1,0:T(8,128)(2,1)S(1)}, bf16[64,2048]{1,0:T(8,128)(2,1)S(1)}, bf16[64,2048]{1,0:T(8,128)(2,1)S(1)}, bf16[64,2048]{1,0:T(8,128)(2...) custom-call(s32[3]{0:T(128)S(1)} %pad_add_fusion.ids_ref, s32[1]{0:T(128)} %bitcast.5.side_ref, ...), custom_call_target="tpu_custom_call" | custom-call | flops 805306368 | bytes 5767168 | tf_op jit(solution)/shard_map/pallas_call | solution.py:411
  80.6 1.1 collective-permute-start.20
  81.9 1.0 collective-permute-start.19
  82.8 1.1 collective-permute-start.24
  83.9 1.0 collective-permute-start.23
  84.8 5.0 %collective-permute-done.20.refs_1_ = bf16[64,2048]{1,0:T(8,128)(2,1)S(1)} collective-permute-done((bf16[64,2048]{1,0:T(8,128)(2,1)S(1)}, bf16[64,2048]{1,0:T(8,128)(2,1)S(1)}, u32[]{:S(2)}, u32[]{:S(2)}) %collective-permute-start.20) | collective-permute-done | bytes 262176 | tf_op jit(solution)/shard_map/ppermute | solution.py:60
  89.9 1.1 collective-permute-done.19.refs_0_
  91.1 1.6 %collective-permute-start.22 = (bf16[64,2048]{1,0:T(8,128)(2,1)S(1)}, bf16[64,2048]{1,0:T(8,128)(2,1)S(1)}, u32[]{:S(2)}, u32[]{:S(2)}) collective-permute-start(bf16[64,2048]{1,0:T(8,128)(2,1)S(1)} %add_convert_fusion.10), channel_id=1, source_target_pairs={{0,1},{2,0},{4,2},{6,4},{7,6},{5,7},{3,5},{1,3},{8,9},{10,8},{12,1... | collective-permute-start | bytes 786440 | tf_op jit(solution)/shard_map/ppermute | solution.py:60
  93.2 2.2 %copy-done.3 = bf16[512,4096]{1,0:T(8,128)(2,1)S(1)} copy-done((bf16[512,4096]{1,0:T(8,128)(2,1)S(1)}, bf16[512,4096]{1,0:T(8,128)(2,1)}, u32[]{:S(2)}) %copy-start.3) | copy-done | bytes 4194328
  95.4 2.1 %shard_map.114 = (bf16[64,2048]{1,0:T(8,128)(2,1)S(1)}, bf16[64,2048]{1,0:T(8,128)(2,1)S(1)}, bf16[64,2048]{1,0:T(8,128)(2,1)S(1)}, bf16[64,2048]{1,0:T(8,128)(2...) custom-call(s32[5]{0:T(128)S(1)} %stack.46.ids_ref, ...), custom_call_target="tpu_custom_call" | custom-call | flops 1342177280 | bytes 6815744 | tf_op jit(solution)/shard_map/pallas_call | solution.py:411
  97.6 1.6 %collective-permute-start.28 = (bf16[64,2048]{1,0:T(8,128)(2,1)S(1)}, bf16[64,2048]{1,0:T(8,128)(2,1)S(1)}, u32[]{:S(2)}, u32[]{:S(2)}) collective-permute-start(bf16[64,2048]{1,0:T(8,128)(2,1)S(1)} %add_convert_fusion.6), channel_id=1, source_target_pairs={{0,1},{2,0},{4,2},{6,4},{7,6},{5,7},{3,5},{1,3},{8,9},{10,8},{12,1... | collective-permute-start | bytes 786440 | tf_op jit(solution)/shard_map/ppermute | solution.py:60
  99.7 1.4 %collective-permute-done.22 = bf16[64,2048]{1,0:T(8,128)(2,1)S(1)} collective-permute-done((bf16[64,2048]{1,0:T(8,128)(2,1)S(1)}, bf16[64,2048]{1,0:T(8,128)(2,1)S(1)}, u32[]{:S(2)}, u32[]{:S(2)}) %collective-permute-start.22) | collective-permute-done | bytes 262176 | tf_op jit(solution)/shard_map/ppermute | solution.py:60
  101.1 1.1 collective-permute-done.21
  102.3 1.6 %collective-permute-start.26 = (bf16[64,2048]{1,0:T(8,128)(2,1)S(1)}, bf16[64,2048]{1,0:T(8,128)(2,1)S(1)}, u32[]{:S(2)}, u32[]{:S(2)}) collective-permute-start(bf16[64,2048]{1,0:T(8,128)(2,1)S(1)} %add_convert_fusion.8), channel_id=1, source_target_pairs={{0,1},{2,0},{4,2},{6,4},{7,6},{5,7},{3,5},{1,3},{8,9},{10,8},{12,1... | collective-permute-start | bytes 786440 | tf_op jit(solution)/shard_map/ppermute | solution.py:60
  104.4 2.5 %collective-permute-done.28 = bf16[64,2048]{1,0:T(8,128)(2,1)S(1)} collective-permute-done((bf16[64,2048]{1,0:T(8,128)(2,1)S(1)}, bf16[64,2048]{1,0:T(8,128)(2,1)S(1)}, u32[]{:S(2)}, u32[]{:S(2)}) %collective-permute-start.28) | collective-permute-done | bytes 262176 | tf_op jit(solution)/shard_map/ppermute | solution.py:60
  107.0 1.5 %collective-permute-done.27 = bf16[64,2048]{1,0:T(8,128)(2,1)S(1)} collective-permute-done((bf16[64,2048]{1,0:T(8,128)(2,1)S(1)}, bf16[64,2048]{1,0:T(8,128)(2,1)S(1)}, u32[]{:S(2)}, u32[]{:S(2)}) %collective-permute-start.27) | collective-permute-done | bytes 262176 | tf_op jit(solution)/shard_map/ppermute | solution.py:60
  108.6 1.6 %collective-permute-start.30 = (bf16[64,2048]{1,0:T(8,128)(2,1)S(1)}, bf16[64,2048]{1,0:T(8,128)(2,1)S(1)}, u32[]{:S(2)}, u32[]{:S(2)}) collective-permute-start(bf16[64,2048]{1,0:T(8,128)(2,1)S(1)} %add_convert_fusion.2), channel_id=1, source_target_pairs={{0,1},{2,0},{4,2},{6,4},{7,6},{5,7},{3,5},{1,3},{8,9},{10,8},{12,1... | collective-permute-start | bytes 786440 | tf_op jit(solution)/shard_map/ppermute | solution.py:60
  110.2 2.3 %collective-permute-done.26 = bf16[64,2048]{1,0:T(8,128)(2,1)S(1)} collective-permute-done((bf16[64,2048]{1,0:T(8,128)(2,1)S(1)}, bf16[64,2048]{1,0:T(8,128)(2,1)S(1)}, u32[]{:S(2)}, u32[]{:S(2)}) %collective-permute-start.26) | collective-permute-done | bytes 262176 | tf_op jit(solution)/shard_map/ppermute | solution.py:60
  112.7 1.4 %collective-permute-start.29 = (bf16[64,2048]{1,0:T(8,128)(2,1)S(1)}, bf16[64,2048]{1,0:T(8,128)(2,1)S(1)}, u32[]{:S(2)}, u32[]{:S(2)}) collective-permute-start(bf16[64,2048]{1,0:T(8,128)(2,1)S(1)} %add_convert_fusion.5), channel_id=1, source_target_pairs={{0,2},{2,4},{4,6},{6,7},{7,5},{5,3},{3,1},{1,0},{8,10},{10,12},{12... | collective-permute-start | bytes 786440 | tf_op jit(solution)/shard_map/ppermute | solution.py:60
  114.1 1.6 %collective-permute-start.31 = (bf16[64,2048]{1,0:T(8,128)(2,1)S(1)}, bf16[64,2048]{1,0:T(8,128)(2,1)S(1)}, u32[]{:S(2)}, u32[]{:S(2)}) collective-permute-start(bf16[64,2048]{1,0:T(8,128)(2,1)S(1)} %add_convert_fusion.3), channel_id=1, source_target_pairs={{0,2},{2,4},{4,6},{6,7},{7,5},{5,3},{3,1},{1,0},{8,10},{10,12},{12... | collective-permute-start | bytes 786440 | tf_op jit(solution)/shard_map/ppermute | solution.py:60
  116.1 1.8 %collective-permute-done.30 = bf16[64,2048]{1,0:T(8,128)(2,1)S(1)} collective-permute-done((bf16[64,2048]{1,0:T(8,128)(2,1)S(1)}, bf16[64,2048]{1,0:T(8,128)(2,1)S(1)}, u32[]{:S(2)}, u32[]{:S(2)}) %collective-permute-start.30) | collective-permute-done | bytes 262176 | tf_op jit(solution)/shard_map/ppermute | solution.py:60
  118.0 4.0 %collective-permute-done.29 = bf16[64,2048]{1,0:T(8,128)(2,1)S(1)} collective-permute-done((bf16[64,2048]{1,0:T(8,128)(2,1)S(1)}, bf16[64,2048]{1,0:T(8,128)(2,1)S(1)}, u32[]{:S(2)}, u32[]{:S(2)}) %collective-permute-start.29) | collective-permute-done | bytes 262176 | tf_op jit(solution)/shard_map/ppermute | solution.py:60
  122.1 3.0 %collective-permute-done.31 = bf16[64,2048]{1,0:T(8,128)(2,1)S(1)} collective-permute-done((bf16[64,2048]{1,0:T(8,128)(2,1)S(1)}, bf16[64,2048]{1,0:T(8,128)(2,1)S(1)}, u32[]{:S(2)}, u32[]{:S(2)}) %collective-permute-start.31) | collective-permute-done | bytes 262176 | tf_op jit(solution)/shard_map/ppermute | solution.py:60
  125.2 0.8 pad_maximum_fusion
  (87 shorter events, 3.9 us)
Async XLA Ops:
  1.1 10.1 %collective-permute-start = (bf16[256,512]{1,0:T(8,128)(2,1)S(1)}, bf16[256,512]{1,0:T(8,128)(2,1)S(1)}, u32[]{:S(2)}, u32[]{:S(2)}) collective-permute-start(bf16[256,512]{1,0:T(8,128)(2,1)S(1)} %get-tuple-element.44.refs_0_), channel_id=1, source_target_pairs={{0,2},{2,4},{4,6},{6,7},{7,5},{5,3},{3,1},{1,0},{8,10},{10,12},{12... | collective-permute-start | bytes 786440 | tf_op jit(solution)/shard_map/ppermute | solution.py:60
  4.1 9.9 %collective-permute-start.4 = (bf16[256,512]{1,0:T(8,128)(2,1)S(1)}, bf16[256,512]{1,0:T(8,128)(2,1)S(1)}, u32[]{:S(2)}, u32[]{:S(2)}) collective-permute-start(bf16[256,512]{1,0:T(8,128)(2,1)S(1)} %get-tuple-element.45.refs_3_), channel_id=1, source_target_pairs={{0,1},{2,0},{4,2},{6,4},{7,6},{5,7},{3,5},{1,3},{8,9},{10,8},{12,1... | collective-permute-start | bytes 786440 | tf_op jit(solution)/shard_map/ppermute | solution.py:60
  4.1 14.8 %collective-permute-start.9 = (bf16[256,512]{1,0:T(8,128)(2,1)S(1)}, bf16[256,512]{1,0:T(8,128)(2,1)S(1)}, u32[]{:S(2)}, u32[]{:S(2)}) collective-permute-start(bf16[256,512]{1,0:T(8,128)(2,1)S(1)} %get-tuple-element.44.refs_0_), channel_id=1, source_target_pairs={{0,1},{2,0},{4,2},{6,4},{7,6},{5,7},{3,5},{1,3},{8,9},{10,8},{12,1... | collective-permute-start | bytes 786440 | tf_op jit(solution)/shard_map/ppermute | solution.py:60
  6.1 12.9 %collective-permute-start.12 = (bf16[256,512]{1,0:T(8,128)(2,1)S(1)}, bf16[256,512]{1,0:T(8,128)(2,1)S(1)}, u32[]{:S(2)}, u32[]{:S(2)}) collective-permute-start(bf16[256,512]{1,0:T(8,128)(2,1)S(1)} %get-tuple-element.45.refs_3_), channel_id=1, source_target_pairs={{0,2},{2,4},{4,6},{6,7},{7,5},{5,3},{3,1},{1,0},{8,10},{10,12},{12... | collective-permute-start | bytes 786440 | tf_op jit(solution)/shard_map/ppermute | solution.py:60
  6.2 0.7 copy-start.15
  11.2 11.3 %collective-permute-start.1 = (bf16[256,512]{1,0:T(8,128)(2,1)S(1)}, bf16[256,512]{1,0:T(8,128)(2,1)}, u32[]{:S(2)}, u32[]{:S(2)}) collective-permute-start(bf16[256,512]{1,0:T(8,128)(2,1)S(1)} %collective-permute-done.refs_1_), channel_id=1, source_target_pairs={{0,2},{2,4},{4,6},{6,7},{7,5},{5,3},{3,1},{1,0},{8,10},{10,12},{12... | collective-permute-start | bytes 786440 | tf_op jit(solution)/shard_map/ppermute | solution.py:60
  13.3 0.7 copy-start.17
  14.0 10.7 %collective-permute-start.5 = (bf16[256,512]{1,0:T(8,128)(2,1)S(1)}, bf16[256,512]{1,0:T(8,128)(2,1)}, u32[]{:S(2)}, u32[]{:S(2)}) collective-permute-start(bf16[256,512]{1,0:T(8,128)(2,1)S(1)} %collective-permute-done.4.refs_5_), channel_id=1, source_target_pairs={{0,1},{2,0},{4,2},{6,4},{7,6},{5,7},{3,5},{1,3},{8,9},{10,8},{12,1... | collective-permute-start | bytes 786440 | tf_op jit(solution)/shard_map/ppermute | solution.py:60
  14.0 0.7 copy-start.19
  19.0 12.4 %copy-start.21 = (bf16[256,512]{1,0:T(8,128)(2,1)}, bf16[256,512]{1,0:T(8,128)(2,1)S(1)}, u32[]{:S(2)}) copy-start(bf16[256,512]{1,0:T(8,128)(2,1)S(1)} %collective-permute-done.9.refs_2_) | copy-start | bytes 786436
  19.0 12.5 %collective-permute-start.10 = (bf16[256,512]{1,0:T(8,128)(2,1)S(1)}, bf16[256,512]{1,0:T(8,128)(2,1)}, u32[]{:S(2)}, u32[]{:S(2)}) collective-permute-start(bf16[256,512]{1,0:T(8,128)(2,1)S(1)} %collective-permute-done.9.refs_2_), channel_id=1, source_target_pairs={{0,1},{2,0},{4,2},{6,4},{7,6},{5,7},{3,5},{1,3},{8,9},{10,8},{12,1... | collective-permute-start | bytes 786440 | tf_op jit(solution)/shard_map/ppermute | solution.py:60
  19.0 12.4 %copy-start.23 = (bf16[256,512]{1,0:T(8,128)(2,1)}, bf16[256,512]{1,0:T(8,128)(2,1)S(1)}, u32[]{:S(2)}) copy-start(bf16[256,512]{1,0:T(8,128)(2,1)S(1)} %collective-permute-done.12.refs_4_) | copy-start | bytes 786436
  19.0 14.5 %collective-permute-start.13 = (bf16[256,512]{1,0:T(8,128)(2,1)S(1)}, bf16[256,512]{1,0:T(8,128)(2,1)}, u32[]{:S(2)}, u32[]{:S(2)}) collective-permute-start(bf16[256,512]{1,0:T(8,128)(2,1)S(1)} %collective-permute-done.12.refs_4_), channel_id=1, source_target_pairs={{0,2},{2,4},{4,6},{6,7},{7,5},{5,3},{3,1},{1,0},{8,10},{10,12},{12... | collective-permute-start | bytes 786440 | tf_op jit(solution)/shard_map/ppermute | solution.py:60
  22.5 15.6 %collective-permute-start.2 = (bf16[256,512]{1,0:T(8,128)(2,1)}, bf16[256,512]{1,0:T(8,128)(2,1)}, u32[]{:S(2)}, u32[]{:S(2)}) collective-permute-start(bf16[256,512]{1,0:T(8,128)(2,1)} %collective-permute-done.1.refs_0_), channel_id=1, source_target_pairs={{0,2},{2,4},{4,6},{6,7},{7,5},{5,3},{3,1},{1,0},{8,10},{10,12},{12... | collective-permute-start | bytes 786440 | tf_op jit(solution)/shard_map/ppermute | solution.py:60
  24.7 15.4 %collective-permute-start.6 = (bf16[256,512]{1,0:T(8,128)(2,1)}, bf16[256,512]{1,0:T(8,128)(2,1)}, u32[]{:S(2)}, u32[]{:S(2)}) collective-permute-start(bf16[256,512]{1,0:T(8,128)(2,1)} %collective-permute-done.5.refs_3_), channel_id=1, source_target_pairs={{0,1},{2,0},{4,2},{6,4},{7,6},{5,7},{3,5},{1,3},{8,9},{10,8},{12,1... | collective-permute-start | bytes 786440 | tf_op jit(solution)/shard_map/ppermute | solution.py:60
  24.7 1.4 %collective-permute-start.8 = (f32[4,512]{1,0:T(4,128)}, f32[4,512]{1,0:T(4,128)S(1)}, u32[]{:S(2)}, u32[]{:S(2)}) collective-permute-start(f32[4,512]{1,0:T(4,128)} %bitcast.11), channel_id=1, source_target_pairs={{0,8},{8,0},{16,24},{24,16},{1,9},{9,1},{17,25},{25,17},{2,10},{10... | collective-permute-start | bytes 24584 | tf_op jit(solution)/shard_map/ppermute | solution.py:460
  25.0 8.7 %copy-start.16 = (bf16[256,512]{1,0:T(8,128)(2,1)S(1)}, bf16[256,512]{1,0:T(8,128)(2,1)}, u32[]{:S(2)}) copy-start(bf16[256,512]{1,0:T(8,128)(2,1)} %copy-done.15) | copy-start | bytes 786436
  25.0 8.7 %copy-start.18 = (bf16[256,512]{1,0:T(8,128)(2,1)S(1)}, bf16[256,512]{1,0:T(8,128)(2,1)}, u32[]{:S(2)}) copy-start(bf16[256,512]{1,0:T(8,128)(2,1)} %copy-done.17) | copy-start | bytes 786436
  25.0 8.7 %copy-start.20 = (bf16[256,512]{1,0:T(8,128)(2,1)S(1)}, bf16[256,512]{1,0:T(8,128)(2,1)}, u32[]{:S(2)}) copy-start(bf16[256,512]{1,0:T(8,128)(2,1)} %copy-done.19) | copy-start | bytes 786436
  31.4 11.8 %copy-start = (bf16[4096,512]{1,0:T(8,128)(2,1)}, bf16[4096,512]{1,0:T(8,128)(2,1)S(1)}, u32[]{:S(2)}) copy-start(bf16[4096,512]{1,0:T(8,128)(2,1)S(1)} %get-tuple-element.47.refs_8_.refs_6_.refs_2_) | copy-start | bytes 12582916
  31.5 11.8 %collective-permute-start.11 = (bf16[256,512]{1,0:T(8,128)(2,1)}, bf16[256,512]{1,0:T(8,128)(2,1)S(1)}, u32[]{:S(2)}, u32[]{:S(2)}) collective-permute-start(bf16[256,512]{1,0:T(8,128)(2,1)} %collective-permute-done.10.refs_1_), channel_id=1, source_target_pairs={{0,1},{2,0},{4,2},{6,4},{7,6},{5,7},{3,5},{1,3},{8,9},{10,8},{12,1... | collective-permute-start | bytes 786440 | tf_op jit(solution)/shard_map/ppermute | solution.py:60
  33.5 9.8 %collective-permute-start.14 = (bf16[256,512]{1,0:T(8,128)(2,1)}, bf16[256,512]{1,0:T(8,128)(2,1)S(1)}, u32[]{:S(2)}, u32[]{:S(2)}) collective-permute-start(bf16[256,512]{1,0:T(8,128)(2,1)} %collective-permute-done.13.refs_2_), channel_id=1, source_target_pairs={{0,2},{2,4},{4,6},{6,7},{7,5},{5,3},{3,1},{1,0},{8,10},{10,12},{12... | collective-permute-start | bytes 786440 | tf_op jit(solution)/shard_map/ppermute | solution.py:60
  33.6 1.0 copy-start.22
  34.6 0.9 copy-start.24
  38.1 9.2 %collective-permute-start.3 = (bf16[256,512]{1,0:T(8,128)(2,1)}, bf16[256,512]{1,0:T(8,128)(2,1)S(1)}, u32[]{:S(2)}, u32[]{:S(2)}) collective-permute-start(bf16[256,512]{1,0:T(8,128)(2,1)} %collective-permute-done.2.refs_0_), channel_id=1, source_target_pairs={{0,2},{2,4},{4,6},{6,7},{7,5},{5,3},{3,1},{1,0},{8,10},{10,12},{12... | collective-permute-start | bytes 786440 | tf_op jit(solution)/shard_map/ppermute | solution.py:60
  40.1 7.7 %collective-permute-start.7 = (bf16[256,512]{1,0:T(8,128)(2,1)}, bf16[256,512]{1,0:T(8,128)(2,1)S(1)}, u32[]{:S(2)}, u32[]{:S(2)}) collective-permute-start(bf16[256,512]{1,0:T(8,128)(2,1)} %collective-permute-done.6.refs_3_), channel_id=1, source_target_pairs={{0,1},{2,0},{4,2},{6,4},{7,6},{5,7},{3,5},{1,3},{8,9},{10,8},{12,1... | collective-permute-start | bytes 786440 | tf_op jit(solution)/shard_map/ppermute | solution.py:60
  46.2 5.1 %copy-start.25 = (f32[512,4]{0,1:T(4,128)S(1)}, f32[512,4]{0,1:T(4,128)}, u32[]{:S(2)}) copy-start(f32[512,4]{0,1:T(4,128)} %param.18) | copy-start | bytes 24580
  47.9 1.7 %copy-start.13 = (bf16[256,512]{1,0:T(8,128)(2,1)}, bf16[256,512]{1,0:T(8,128)(2,1)S(1)}, u32[]{:S(2)}) copy-start(bf16[256,512]{1,0:T(8,128)(2,1)S(1)} %collective-permute-done.7.refs_1_) | copy-start | bytes 786436
  49.6 7.8 %collective-permute-start.15 = (bf16[2,512,512]{2,1,0:T(8,128)(2,1)}, bf16[2,512,512]{2,1,0:T(8,128)(2,1)}, u32[]{:S(2)}, u32[]{:S(2)}) collective-permute-start(bf16[2,512,512]{2,1,0:T(8,128)(2,1)} %shard_map.106.k_ref.v_ref), channel_id=1, source_target_pairs={{0,8},{8,0},{16,24},{24,16},{1,9},{9,1},{17,25},{25,17},{2,10},{10... | collective-permute-start | bytes 3145736 | tf_op jit(solution)/shard_map/ppermute | solution.py:460
  49.6 15.5 %collective-permute-start.16 = (bf16[2,512,512]{2,1,0:T(8,128)(2,1)}, bf16[2,512,512]{2,1,0:T(8,128)(2,1)}, u32[]{:S(2)}, u32[]{:S(2)}) collective-permute-start(bf16[2,512,512]{2,1,0:T(8,128)(2,1)} %shard_map.106.k_ref.v_ref), channel_id=1, source_target_pairs={{8,16},{9,17},{10,18},{11,19},{12,20},{13,21},{14,22},{15,23}} | collective-permute-start | bytes 3145736 | tf_op jit(solution)/shard_map/ppermute | solution.py:488
  51.3 1.0 copy-start.4
  52.3 1.0 copy-start.7
  53.4 1.0 copy-start.10
  54.4 10.2 %copy-start.1 = (bf16[4096,512]{1,0:T(8,128)(2,1)S(1)}, bf16[4096,512]{1,0:T(8,128)(2,1)}, u32[]{:S(2)}) copy-start(bf16[4096,512]{1,0:T(8,128)(2,1)} %copy-done) | copy-start | bytes 12582916
  54.4 10.2 %copy-start.14 = (bf16[256,512]{1,0:T(8,128)(2,1)S(1)}, bf16[256,512]{1,0:T(8,128)(2,1)}, u32[]{:S(2)}) copy-start(bf16[256,512]{1,0:T(8,128)(2,1)} %copy-done.13) | copy-start | bytes 786436
  57.4 1.0 copy-start.5
  58.4 1.0 copy-start.8
  59.5 1.0 copy-start.11
  63.4 10.1 %collective-permute-start.17 = (bf16[2,3,128,256]{3,2,1,0:T(8,128)(2,1)S(1)}, bf16[2,3,128,256]{3,2,1,0:T(8,128)(2,1)S(1)}, u32[]{:S(2)}, u32[]{:S(2)}) collective-permute-start(bf16[2,3,128,256]{3,2,1,0:T(8,128)(2,1)S(1)} %get-tuple-element.52), channel_id=1, source_target_pairs={{0,16},{8,24},{16,0},{24,8},{1,17},{9,25},{17,1},{25,9},{2,18},{10... | collective-permute-start | bytes 1179656 | tf_op jit(solution)/shard_map/ppermute | solution.py:460
  65.0 8.4 %copy-start.6 = (f32[4,128,256]{2,1,0:T(8,128)S(1)}, f32[4,128,256]{2,1,0:T(8,128)}, u32[]{:S(2)}) copy-start(f32[4,128,256]{2,1,0:T(8,128)} %gate_ref.5) | copy-start | bytes 1572868
  65.1 8.4 %copy-start.9 = (f32[4,128,256]{2,1,0:T(8,128)S(1)}, f32[4,128,256]{2,1,0:T(8,128)}, u32[]{:S(2)}) copy-start(f32[4,128,256]{2,1,0:T(8,128)} %up_ref.5) | copy-start | bytes 1572868
  65.1 8.4 %copy-start.12 = (f32[4,256,128]{2,1,0:T(8,128)S(1)}, f32[4,256,128]{2,1,0:T(8,128)}, u32[]{:S(2)}) copy-start(f32[4,256,128]{2,1,0:T(8,128)} %down_ref.5) | copy-start | bytes 1572868
  65.1 8.4 %copy-start.26 = (f32[4]{0:T(128)S(1)}, f32[4]{0:T(128)}, u32[]{:S(2)}) copy-start(f32[4]{0:T(128)} %step_ref.1) | copy-start | bytes 52
  73.4 5.6 %copy-start.2 = (bf16[512,4096]{1,0:T(8,128)(2,1)S(1)}, bf16[512,4096]{1,0:T(8,128)(2,1)}, u32[]{:S(2)}) copy-start(bf16[512,4096]{1,0:T(8,128)(2,1)} %w_ref.3) | copy-start | bytes 12582916
  74.5 3.2 %collective-permute-start.18 = (bf16[2,3,128,256]{3,2,1,0:T(8,128)(2,1)S(1)}, bf16[2,3,128,256]{3,2,1,0:T(8,128)(2,1)S(1)}, u32[]{:S(2)}, u32[]{:S(2)}) collective-permute-start(bf16[2,3,128,256]{3,2,1,0:T(8,128)(2,1)S(1)} %shard_map.110.net_ref), channel_id=1, source_target_pairs={{0,8},{8,0},{16,24},{24,16},{1,9},{9,1},{17,25},{25,17},{2,10},{10... | collective-permute-start | bytes 1179656 | tf_op jit(solution)/shard_map/ppermute | solution.py:460
  80.6 9.2 %collective-permute-start.20 = (bf16[64,2048]{1,0:T(8,128)(2,1)S(1)}, bf16[64,2048]{1,0:T(8,128)(2,1)S(1)}, u32[]{:S(2)}, u32[]{:S(2)}) collective-permute-start(bf16[64,2048]{1,0:T(8,128)(2,1)S(1)} %get-tuple-element.56), channel_id=1, source_target_pairs={{0,1},{2,0},{4,2},{6,4},{7,6},{5,7},{3,5},{1,3},{8,9},{10,8},{12,1... | collective-permute-start | bytes 786440 | tf_op jit(solution)/shard_map/ppermute | solution.py:60
  81.9 9.2 %collective-permute-start.19 = (bf16[64,2048]{1,0:T(8,128)(2,1)S(1)}, bf16[64,2048]{1,0:T(8,128)(2,1)S(1)}, u32[]{:S(2)}, u32[]{:S(2)}) collective-permute-start(bf16[64,2048]{1,0:T(8,128)(2,1)S(1)} %get-tuple-element.55), channel_id=1, source_target_pairs={{0,2},{2,4},{4,6},{6,7},{7,5},{5,3},{3,1},{1,0},{8,10},{10,12},{12... | collective-permute-start | bytes 786440 | tf_op jit(solution)/shard_map/ppermute | solution.py:60
  82.8 14.6 %collective-permute-start.24 = (bf16[64,2048]{1,0:T(8,128)(2,1)S(1)}, bf16[64,2048]{1,0:T(8,128)(2,1)S(1)}, u32[]{:S(2)}, u32[]{:S(2)}) collective-permute-start(bf16[64,2048]{1,0:T(8,128)(2,1)S(1)} %get-tuple-element.65), channel_id=1, source_target_pairs={{0,1},{2,0},{4,2},{6,4},{7,6},{5,7},{3,5},{1,3},{8,9},{10,8},{12,1... | collective-permute-start | bytes 786440 | tf_op jit(solution)/shard_map/ppermute | solution.py:60
  83.9 13.7 %collective-permute-start.23 = (bf16[64,2048]{1,0:T(8,128)(2,1)S(1)}, bf16[64,2048]{1,0:T(8,128)(2,1)S(1)}, u32[]{:S(2)}, u32[]{:S(2)}) collective-permute-start(bf16[64,2048]{1,0:T(8,128)(2,1)S(1)} %get-tuple-element.64), channel_id=1, source_target_pairs={{0,2},{2,4},{4,6},{6,7},{7,5},{5,3},{3,1},{1,0},{8,10},{10,12},{12... | collective-permute-start | bytes 786440 | tf_op jit(solution)/shard_map/ppermute | solution.py:60
  91.1 10.0 %collective-permute-start.22 = (bf16[64,2048]{1,0:T(8,128)(2,1)S(1)}, bf16[64,2048]{1,0:T(8,128)(2,1)S(1)}, u32[]{:S(2)}, u32[]{:S(2)}) collective-permute-start(bf16[64,2048]{1,0:T(8,128)(2,1)S(1)} %add_convert_fusion.10), channel_id=1, source_target_pairs={{0,1},{2,0},{4,2},{6,4},{7,6},{5,7},{3,5},{1,3},{8,9},{10,8},{12,1... | collective-permute-start | bytes 786440 | tf_op jit(solution)/shard_map/ppermute | solution.py:60
  92.7 9.5 %collective-permute-start.21 = (bf16[64,2048]{1,0:T(8,128)(2,1)S(1)}, bf16[64,2048]{1,0:T(8,128)(2,1)S(1)}, u32[]{:S(2)}, u32[]{:S(2)}) collective-permute-start(bf16[64,2048]{1,0:T(8,128)(2,1)S(1)} %add_convert_fusion.11), channel_id=1, source_target_pairs={{0,2},{2,4},{4,6},{6,7},{7,5},{5,3},{3,1},{1,0},{8,10},{10,12},{12... | collective-permute-start | bytes 786440 | tf_op jit(solution)/shard_map/ppermute | solution.py:60
  93.2 2.2 %copy-start.3 = (bf16[512,4096]{1,0:T(8,128)(2,1)S(1)}, bf16[512,4096]{1,0:T(8,128)(2,1)}, u32[]{:S(2)}) copy-start(bf16[512,4096]{1,0:T(8,128)(2,1)} %w_ref.3) | copy-start | bytes 12582916
  97.6 9.3 %collective-permute-start.28 = (bf16[64,2048]{1,0:T(8,128)(2,1)S(1)}, bf16[64,2048]{1,0:T(8,128)(2,1)S(1)}, u32[]{:S(2)}, u32[]{:S(2)}) collective-permute-start(bf16[64,2048]{1,0:T(8,128)(2,1)S(1)} %add_convert_fusion.6), channel_id=1, source_target_pairs={{0,1},{2,0},{4,2},{6,4},{7,6},{5,7},{3,5},{1,3},{8,9},{10,8},{12,1... | collective-permute-start | bytes 786440 | tf_op jit(solution)/shard_map/ppermute | solution.py:60
  99.3 9.2 %collective-permute-start.27 = (bf16[64,2048]{1,0:T(8,128)(2,1)S(1)}, bf16[64,2048]{1,0:T(8,128)(2,1)S(1)}, u32[]{:S(2)}, u32[]{:S(2)}) collective-permute-start(bf16[64,2048]{1,0:T(8,128)(2,1)S(1)} %add_convert_fusion.7), channel_id=1, source_target_pairs={{0,2},{2,4},{4,6},{6,7},{7,5},{5,3},{3,1},{1,0},{8,10},{10,12},{12... | collective-permute-start | bytes 786440 | tf_op jit(solution)/shard_map/ppermute | solution.py:60
  102.3 10.2 %collective-permute-start.26 = (bf16[64,2048]{1,0:T(8,128)(2,1)S(1)}, bf16[64,2048]{1,0:T(8,128)(2,1)S(1)}, u32[]{:S(2)}, u32[]{:S(2)}) collective-permute-start(bf16[64,2048]{1,0:T(8,128)(2,1)S(1)} %add_convert_fusion.8), channel_id=1, source_target_pairs={{0,1},{2,0},{4,2},{6,4},{7,6},{5,7},{3,5},{1,3},{8,9},{10,8},{12,1... | collective-permute-start | bytes 786440 | tf_op jit(solution)/shard_map/ppermute | solution.py:60
  104.0 8.7 %collective-permute-start.25 = (bf16[64,2048]{1,0:T(8,128)(2,1)S(1)}, bf16[64,2048]{1,0:T(8,128)(2,1)S(1)}, u32[]{:S(2)}, u32[]{:S(2)}) collective-permute-start(bf16[64,2048]{1,0:T(8,128)(2,1)S(1)} %add_convert_fusion.9), channel_id=1, source_target_pairs={{0,2},{2,4},{4,6},{6,7},{7,5},{5,3},{3,1},{1,0},{8,10},{10,12},{12... | collective-permute-start | bytes 786440 | tf_op jit(solution)/shard_map/ppermute | solution.py:60
  108.6 9.4 %collective-permute-start.30 = (bf16[64,2048]{1,0:T(8,128)(2,1)S(1)}, bf16[64,2048]{1,0:T(8,128)(2,1)S(1)}, u32[]{:S(2)}, u32[]{:S(2)}) collective-permute-start(bf16[64,2048]{1,0:T(8,128)(2,1)S(1)} %add_convert_fusion.2), channel_id=1, source_target_pairs={{0,1},{2,0},{4,2},{6,4},{7,6},{5,7},{3,5},{1,3},{8,9},{10,8},{12,1... | collective-permute-start | bytes 786440 | tf_op jit(solution)/shard_map/ppermute | solution.py:60
  112.7 9.3 %collective-permute-start.29 = (bf16[64,2048]{1,0:T(8,128)(2,1)S(1)}, bf16[64,2048]{1,0:T(8,128)(2,1)S(1)}, u32[]{:S(2)}, u32[]{:S(2)}) collective-permute-start(bf16[64,2048]{1,0:T(8,128)(2,1)S(1)} %add_convert_fusion.5), channel_id=1, source_target_pairs={{0,2},{2,4},{4,6},{6,7},{7,5},{5,3},{3,1},{1,0},{8,10},{10,12},{12... | collective-permute-start | bytes 786440 | tf_op jit(solution)/shard_map/ppermute | solution.py:60
  114.1 11.0 %collective-permute-start.31 = (bf16[64,2048]{1,0:T(8,128)(2,1)S(1)}, bf16[64,2048]{1,0:T(8,128)(2,1)S(1)}, u32[]{:S(2)}, u32[]{:S(2)}) collective-permute-start(bf16[64,2048]{1,0:T(8,128)(2,1)S(1)} %add_convert_fusion.3), channel_id=1, source_target_pairs={{0,2},{2,4},{4,6},{6,7},{7,5},{5,3},{3,1},{1,0},{8,10},{10,12},{12... | collective-permute-start | bytes 786440 | tf_op jit(solution)/shard_map/ppermute | solution.py:60
  115.7 9.4 %collective-permute-start.32 = (bf16[64,2048]{1,0:T(8,128)(2,1)S(1)}, bf16[64,2048]{1,0:T(8,128)(2,1)S(1)}, u32[]{:S(2)}, u32[]{:S(2)}) collective-permute-start(bf16[64,2048]{1,0:T(8,128)(2,1)S(1)} %add_convert_fusion.4), channel_id=1, source_target_pairs={{0,1},{2,0},{4,2},{6,4},{7,6},{5,7},{3,5},{1,3},{8,9},{10,8},{12,1... | collective-permute-start | bytes 786440 | tf_op jit(solution)/shard_map/ppermute | solution.py:60

commit v4 on v0

v4 whole, which is shorter than its diff:
```python
import functools

import jax
import jax.numpy as jnp
import numpy as np
from jax import lax
from jax.experimental import pallas as pl
from jax.experimental.pallas import tpu as pltpu
from jax.sharding import PartitionSpec as P

WINDOW = 512
CHUNKS = 2
F32 = jnp.float32
BF16 = jnp.bfloat16
LOG2E = 1.4426950408889634


def call(body, in_specs, out_specs, out_shape, scratch=(), vmem=8, cost=None, aliases=None):
    return pl.pallas_call(
        body,
        in_specs=in_specs,
        out_specs=out_specs,
        out_shape=out_shape,
        scratch_shapes=list(scratch),
        input_output_aliases=aliases or {},
        cost_estimate=cost,
        compiler_params=pltpu.CompilerParams(vmem_limit_bytes=vmem * 1024 * 1024),
    )


def cost(flops, moved, exps=0):
    return pl.CostEstimate(flops=int(flops), bytes_accessed=int(moved), transcendentals=int(exps))


WHOLE = pl.BlockSpec(memory_space=pltpu.VMEM)
AFTER = pl.BlockSpec(memory_space=pl.ANY)
NUMBERS = pl.BlockSpec(memory_space=pltpu.SMEM)
IN_HBM = pl.BlockSpec(memory_space=pltpu.HBM)
PLACE, NEAR, FAR, RING = range(4)


def mm(left, right, dims=((1,), (0,))):
    return lax.dot_general(left, right, (dims, ((), ())), preferred_element_type=F32)


def sigmoid(x):
    return 0.5 * jnp.tanh(0.5 * x) + 0.5


def ring_order(count):
    return list(range(0, count, 2)) + list(range(count - 1, 0, -2))


def ring_send(value, step):
    order = ring_order(lax.axis_size("head"))
    count = len(order)
    return lax.ppermute(
        value, "head", [(order[i], order[(i + step) % count]) for i in range(count)]
    )


def ring_offsets():
    steps = lax.axis_size("head") // 2
    return [0] + [way * step for step in range(1, steps) for way in (-1, 1)] + [steps]


def own_numbers(pair):
    order = ring_order(lax.axis_size("head"))
    count = len(order)
    rows = []
    for place in range(lax.axis_size("tok")):
        for head in range(count):
            ring = [order[(order.index(head) + offset) % count] for offset in ring_offsets()]
            rows.append([place, place % 2 * pair, (1 - place % 2) * pair] + ring)
    table = jnp.array(np.array(rows, np.int32))
    return lax.dynamic_index_in_dim(table, lax.axis_index(("tok", "head")), 0, keepdims=False)


def hbm(array):
    return pltpu.with_memory_space_constraint(array, pltpu.HBM)


def run_copies(copies):
    for copy in copies:
        copy.start()
    for copy in copies:
        copy.wait()


def load(numbers, arrays):
    count = len(arrays)
    blocks = len(ring_offsets())
    size = arrays[0].shape[0] // blocks

    def body(numbers_ref, *refs):
        out_refs, sems = refs[count:-1], refs[-1]
        run_copies(
            [
                pltpu.make_async_copy(
                    refs[index].at[
                        pl.ds(pl.multiple_of(numbers_ref[RING + block] * size, size), size)
                    ],
                    out_refs[index].at[pl.ds(block * size, size)],
                    sems.at[index, block],
                )
                for block in range(blocks)
                for index in range(count)
            ]
        )

    return call(
        body,
        [NUMBERS] + [IN_HBM] * count,
        [WHOLE] * count,
        [jax.ShapeDtypeStruct(array.shape, array.dtype) for array in arrays],
        [pltpu.SemaphoreType.DMA((count, blocks))],
        vmem=1,
        cost=cost(0, sum(4 * array.size for array in arrays)),
    )(numbers, *[hbm(array) for array in arrays])


def split_rows(numbers, tokens):
    rows, width = tokens.shape[0] // CHUNKS, tokens.shape[1]

    def body(numbers_ref, in_ref, *refs):
        out_refs, sems = refs[:-1], refs[-1]
        run_copies(
            [
                pltpu.make_async_copy(in_ref.at[pl.ds(c * rows, rows)], out_refs[c], sems.at[c])
                for c in range(CHUNKS)
            ]
        )

    return call(
        body,
        [NUMBERS, IN_HBM],
        [WHOLE] * CHUNKS,
        [jax.ShapeDtypeStruct((rows, width), tokens.dtype)] * CHUNKS,
        [pltpu.SemaphoreType.DMA((CHUNKS,))],
        vmem=1,
        cost=cost(0, 4 * tokens.size),
    )(numbers, hbm(tokens))


def gather_step(held, ways, after):
    moved = {}
    for way in ways:
        value = held[way]
        if after is not None:
            value, _ = lax.optimization_barrier((value, after))
        moved[way] = ring_send(value, way)
    return moved


def accumulate(chunks, first, last, weights, before=None, lead=0):
    rows, depth = chunks[0][0].shape
    width = weights[0].shape[1]
    parts, span = len(weights), last - first
    total = rows * len(chunks)
    final = last == lax.axis_size("head")
    dtype = BF16 if final else F32
    pieces = [chunk[index] for chunk in chunks for index in range(first, last)]

    def body(*refs):
        piece_refs = refs[: len(pieces)]
        weight_refs = refs[len(pieces) : len(pieces) + parts]
        out_ref, left = refs[-2:]
        for index, ref in enumerate(piece_refs):
            chunk, piece = divmod(index, span)
            left[chunk * rows : (chunk + 1) * rows, piece * depth : (piece + 1) * depth] = ref[...]
        for part in range(parts):
            term = mm(left[...], weight_refs[part][first * depth : last * depth])
            if before is not None:
                term = term + refs[-3][lead + part]
            out_ref[part] = term.astype(dtype)

    aliased = before is not None and not final
    args = [*pieces, *weights] + ([] if before is None else [before])
    return call(
        body,
        [WHOLE] * len(args),
        WHOLE,
        jax.ShapeDtypeStruct((parts, total, width), dtype),
        [pltpu.VMEM((total, span * depth), BF16)],
        vmem=12,
        cost=cost(
            2 * total * span * depth * width * parts,
            2 * span * depth * (total + width * parts) + 8 * total * width * parts,
        ),
        aliases={len(args) - 1: 0} if aliased else None,
    )(*args)


def lanes(head, size):
    return pl.ds(pl.multiple_of(head * size, size), size)


def normed(values):
    values = values.astype(F32)
    scale = lax.rsqrt(jnp.mean(values * values, axis=-1, keepdims=True) + 1e-06)
    return (values * scale).astype(BF16)


def head_grads(numbers, kv, rate, fast_gate, fast_up, fast_down, before=None):
    rows = kv.shape[1]
    size, hidden_size = fast_gate.shape[1:]
    count = rate.shape[0]
    heads = count // 2

    def body(numbers_ref, kv_ref, rate_ref, gate_ref, up_ref, down_ref, *rest):
        rates = rate_ref[...].T
        lane = lax.broadcasted_iota(jnp.int32, (rows, count), 1)
        for index in range(heads):
            head = numbers_ref[NEAR] + index
            mine = jnp.sum(jnp.where(lane == head, rates, 0.0), axis=1, keepdims=True)
            knorm = normed(kv_ref[0, :, lanes(head, size)])
            target = (-mine * kv_ref[1, :, lanes(head, size)].astype(F32)).astype(BF16)
            gate_pre = mm(knorm, gate_ref[head].astype(BF16))
            up_pre = mm(knorm, up_ref[head].astype(BF16))
            back = mm(target, down_ref[head].astype(BF16), ((1,), (1,)))
            sigma = sigmoid(gate_pre)
            active = gate_pre * sigma
            first = back * up_pre * (sigma + active * (1.0 - sigma))
            both = jnp.concatenate([first.astype(BF16), (back * active).astype(BF16)], axis=1)
            third = (active * up_pre).astype(BF16)
            pair = mm(knorm, both, ((0,), (0,)))
            terms = (pair[:, :hidden_size], pair[:, hidden_size:], mm(target, third, ((0,), (0,))))
            for part, term in enumerate(terms):
                if before is not None:
                    term = term + rest[0][index, part]
                    rest[-1][index, part] = term.astype(BF16)
                    rest[-2][index, part] = term
                else:
                    rest[-1][index, part] = term

    args = [kv, rate, fast_gate, fast_up, fast_down] + ([] if before is None else [before])
    kinds = [F32] if before is None else [F32, BF16]
    return call(
        body,
        [NUMBERS] + [WHOLE] * len(args),
        [WHOLE] * len(kinds),
        [jax.ShapeDtypeStruct((heads, 3, size, hidden_size), kind) for kind in kinds],
        cost=cost(
            12 * heads * rows * size * hidden_size,
            8 * heads * 3 * size * hidden_size,
            heads * rows * hidden_size,
        ),
    )(numbers, *args)


def renew(numbers, kept, received, step, fast_gate, fast_up, fast_down, after):
    heads, _, size, hidden_size = kept.shape

    def body(numbers_ref, step_ref, kept_ref, gate_ref, up_ref, down_ref, *rest):
        out_ref = rest[-1]
        for index in range(heads):
            head = numbers_ref[NEAR] + index
            for part in range(3):
                grad = kept_ref[index, part]
                for more in rest[: len(received)]:
                    grad = grad + more[index, part].astype(F32)
                if part < 2:
                    matrix = (gate_ref, up_ref)[part][head]
                    fan = size
                else:
                    matrix = down_ref[head].T
                    fan = hidden_size
                mean_sq = jnp.sum(grad * grad, keepdims=True) / (size * hidden_size)
                scale = step_ref[head] * fan ** (-0.5) * lax.rsqrt(mean_sq + 1e-06)
                out_ref[index, part] = (matrix - scale * grad).astype(BF16)

    return call(
        body,
        [NUMBERS, NUMBERS] + [WHOLE] * (4 + len(received)) + [AFTER] * len(after),
        WHOLE,
        jax.ShapeDtypeStruct(kept.shape, BF16),
        cost=cost(10 * kept.size, 12 * kept.size),
    )(numbers, step, kept, fast_gate, fast_up, fast_down, *received, *after)


def attend(numbers, query, kv, beside, behind, size):
    total = query.shape[1]
    heads = query.shape[2] // size
    rows = total // 2
    factor = size ** (-0.5) * LOG2E

    def body(numbers_ref, q_ref, kv_ref, beside_ref, behind_ref, out_ref):
        has_halo = numbers_ref[PLACE] > 0
        odd = numbers_ref[PLACE] % 2 == 1
        row = lax.broadcasted_iota(jnp.int32, (rows, rows), 0)
        col = lax.broadcasted_iota(jnp.int32, (rows, rows), 1)

        def block(which, source, lane):
            side, at = divmod(source, 2)
            where = slice(at * rows, (at + 1) * rows)
            if side == 1:
                return kv_ref[which, where, lane]
            return jnp.where(odd, beside_ref[which, where, lane], behind_ref[which, where, lane])

        for head in range(heads):
            lane = slice(head * size, (head + 1) * size)
            for index in range(2):
                where = slice(index * rows, (index + 1) * rows)
                query_block = q_ref[0, where, lane]
                scores = []
                for source in range(index, index + 3):
                    part = mm(query_block, block(0, source, lane), ((1,), (1,))) * factor
                    if source == index:
                        part = jnp.where((col > row) & has_halo, part, -1e30)
                    elif source == index + 2:
                        part = jnp.where(col <= row, part, -1e30)
                    elif source < 2:
                        part = jnp.where(has_halo, part, -1e30)
                    scores.append(part)
                top = functools.reduce(
                    jnp.maximum, [jnp.max(part, axis=-1, keepdims=True) for part in scores]
                )
                sums, result = 0.0, 0.0
                for part, source in zip(scores, range(index, index + 3)):
                    expo = jnp.exp2(part - top)
                    sums = sums + jnp.sum(expo, axis=-1, keepdims=True)
                    result = result + mm(expo.astype(BF16), block(1, source, lane))
                out_ref[where, lane] = result / sums

    return call(
        body,
        [NUMBERS] + [WHOLE] * 4,
        WHOLE,
        jax.ShapeDtypeStruct((total, heads * size), F32),
        cost=cost(
            24 * heads * size * rows * rows,
            8 * total * heads * size,
            6 * heads * rows * rows,
        ),
    )(numbers, query, kv, beside, behind)


def fast_apply(query, gate, upper, down):
    qnorm = normed(query)
    gate_pre = mm(qnorm, gate)
    hidden = gate_pre * sigmoid(gate_pre) * mm(qnorm, upper)
    return mm(hidden.astype(BF16), down, ((1,), (1,)))


def combine_near(numbers, query, attended, nets):
    rows = query.shape[1]
    heads, _, size, hidden_size = nets.shape

    def body(numbers_ref, q_ref, attended_ref, net_ref, out_ref):
        for index in range(heads):
            lane = lanes(numbers_ref[NEAR] + index, size)
            fast = fast_apply(q_ref[0, :, lane], *(net_ref[index, part] for part in range(3)))
            where = slice(index * size, (index + 1) * size)
            out_ref[:, where] = (attended_ref[:, lane] + fast).astype(BF16)

    return call(
        body,
        [NUMBERS] + [WHOLE] * 3,
        WHOLE,
        jax.ShapeDtypeStruct((rows, heads * size), BF16),
        cost=cost(
            6 * heads * rows * size * hidden_size,
            8 * heads * rows * size,
            heads * rows * hidden_size,
        ),
    )(numbers, query, attended, nets)


def partial_out(numbers, offsets, query, attended, nets, near, w_out, after=()):
    known = ring_offsets()
    rows = near.shape[0] // len(known)
    heads, _, size, hidden_size = nets.shape
    depth = heads * size
    count = len(offsets)
    width = w_out.shape[1]
    block = width // 8

    def body(numbers_ref, q_ref, attended_ref, net_ref, near_ref, w_ref, *refs):
        out_refs, far_ref = refs[len(after) : -1], refs[-1]
        starts = [
            pl.multiple_of(numbers_ref[RING + known.index(offset)] * rows, rows)
            for offset in offsets
        ]

        def take(ref, lane):
            return jnp.concatenate([ref[pl.ds(start, rows), lane] for start in starts], axis=0)

        for index in range(heads):
            lane = lanes(numbers_ref[FAR] + index, size)
            fast = fast_apply(
                take(q_ref.at[0], lane), *(net_ref[index, part] for part in range(3))
            )
            where = slice(index * size, (index + 1) * size)
            far_ref[:, where] = (take(attended_ref, lane) + fast).astype(BF16)
        left = take(near_ref, slice(None))
        near_rows = pl.ds(pl.multiple_of(numbers_ref[NEAR] * size, size), depth)
        far_rows = pl.ds(pl.multiple_of(numbers_ref[FAR] * size, size), depth)
        for column in range(0, width, block):
            result = mm(left, w_ref[near_rows, column : column + block])
            result += mm(far_ref[...], w_ref[far_rows, column : column + block])
            result = result.astype(BF16)
            half, at = divmod(column, width // 2)
            for index in range(count):
                out_refs[2 * index + half][:, at : at + block] = result[
                    index * rows : (index + 1) * rows
                ]

    outs = call(
        body,
        [NUMBERS] + [WHOLE] * 5 + [AFTER] * len(after),
        [WHOLE] * (2 * count),
        [jax.ShapeDtypeStruct((rows, width // 2), BF16)] * (2 * count),
        [pltpu.VMEM((count * rows, depth), BF16)],
        vmem=8,
        cost=cost(4 * count * rows * depth * width, 2 * width * (2 * depth + count * rows)),
    )(numbers, query, attended, nets, near, w_out, *after)
    return {offset: tuple(outs[2 * at : 2 * at + 2]) for at, offset in enumerate(offsets)}


def ring_reduce(numbers, query, attended, nets, near, w_out):
    steps = lax.axis_size("head") // 2
    signed = [sign * step for step in range(steps - 1, 0, -1) for sign in (1, -1)]
    shared = (query, attended, nets, near, w_out)
    parts = partial_out(numbers, [steps] + signed[:2], *shared)
    coming = {}
    ordered = ()
    for which in range(2 * steps - 1):
        step, half = steps - (which + 1) // 2, which % 2
        if which == 2:
            parts |= partial_out(numbers, signed[2:] + [0], *shared, tuple(coming.values())[:2])
        terms = []
        for way in (1, -1):
            side = half if way == 1 else 1 - half
            term = parts[steps if step == steps else way * step][side]
            if (way, side) in coming:
                term = (term.astype(F32) + coming[way, side].astype(F32)).astype(BF16)
            terms.append(term)
        ordered = lax.optimization_barrier((*terms, *ordered))[:2]
        for way, term in zip((1, -1), ordered):
            coming[way, half if way == 1 else 1 - half] = ring_send(term, way)
    sides = {1: 1 - half, -1: half}
    totals = add_pair(
        [parts[0][sides[way]] for way in (1, -1)], [coming.pop((way, sides[way])) for way in (1, -1)]
    )
    totals = {sides[way]: total for way, total in zip((1, -1), totals)}
    ends = [totals[side] for side in range(2)]
    for (_, side), more in coming.items():
        ends[side] = ends[side] + more.astype(F32)
    return jnp.concatenate([end.astype(BF16) for end in ends], axis=1)


def add_pair(own, came):
    def body(*refs):
        for index in range(2):
            refs[4 + index][...] = refs[index][...].astype(F32) + refs[2 + index][...].astype(F32)

    return call(
        body,
        [WHOLE] * 4,
        [WHOLE] * 2,
        [jax.ShapeDtypeStruct(value.shape, F32) for value in own],
        cost=cost(0, 64 * own[0].size),
    )(*own, *came)


def swap(value, bit):
    count = lax.axis_size("tok")
    return lax.ppermute(value, "tok", [(index, index ^ bit) for index in range(count)])


def shards(
    tokens, w_query, w_key, w_value, w_out, fast_gate, fast_up, fast_down, token_rate, head_step
):
    local_heads, head_size, _ = fast_gate.shape
    tok_count = lax.axis_size("tok")
    steps = lax.axis_size("head") // 2
    nets = (fast_gate, fast_up, fast_down)
    numbers = own_numbers(local_heads // 2)
    rate = token_rate.T
    rate_beside = swap(rate, 1)

    own = split_rows(numbers, tokens)
    weights = load(numbers, [w_key, w_value, w_query])
    chunks = [[piece] for piece in own]
    held = [{1: piece, -1: piece} for piece in own]
    sums, done = None, 0
    for step in range(1, steps + 1):
        after = (None, None, weights[0], (sums, rate_beside))[step] if step < 4 else sums
        for c in range(CHUNKS):
            last = (1,) if c % 2 == 0 else (-1,)
            held[c] = gather_step(held[c], (1, -1) if step < steps else last, after)
            chunks[c] += held[c].values()
        if step > 1:
            sums = accumulate([chunk[: 2 * step - 1] for chunk in chunks], done, 2 * step - 1, weights, sums)
            done = 2 * step - 1
    kv = accumulate(chunks, done, 2 * steps, weights[:2], sums)
    query = accumulate(chunks, done, 2 * steps, weights[2:], sums, 2)

    beside = swap(kv, 1)
    behind = lax.ppermute(kv, "tok", [(index, index + 1) for index in range(1, tok_count - 1, 2)])
    (grads,) = head_grads(numbers, kv, rate, *nets)
    grads, travel = head_grads(numbers, beside, rate_beside, *nets, grads)
    received = []
    for bit in range(1, tok_count.bit_length() - 1):
        if received:
            travel = grads
            for more in received:
                travel = travel + more.astype(F32)
            travel = travel.astype(BF16)
        received.append(swap(travel, 1 << bit))
    attended = attend(numbers, query, kv, beside, behind, head_size)
    mine = renew(numbers, grads, received, head_step, *nets, (attended,))
    near = combine_near(numbers, query, attended, mine)
    return ring_reduce(numbers, query, attended, swap(mine, 1), near, w_out)


def solution(mesh):
    placed = (
        P("tok", "head"),
        P(None, "head"),
        P(None, "head"),
        P(None, "head"),
        P("head", None),
        P("head", None, None),
        P("head", None, None),
        P("head", None, None),
        P("tok", "head"),
        P("head"),
    )
    return jax.shard_map(
        shards, mesh=mesh, in_specs=placed, out_specs=P(("tok", "head"), None), check_vma=False
    )
```

time: 267 us -> 120 us (0.45)
  waiting for transfers between devices: 185 us -> 58.1 us
  matrix products: 43.1 us -> 0 us
  Pallas kernels: 0 us -> 29.2 us
  starting transfers between devices: 4.38 us -> 29.1 us
  between operations: 13.4 us -> 0.28 us
  other arithmetic: 14.4 us -> 1.58 us
  local copies, waits for them, and re-layouts: 6.14 us -> 0.73 us
    reduce_scatter x1 -> x0, waiting for transfers between devices: 89.9 us -> none  [shards(): lax.psum_scatter(jnp.dot(combined, w_out, preferred_element_type=jnp.floa...]
    all_gather x1 -> x0, waiting for transfers between devices: 74.7 us -> none  [shards(): piece = lax.all_gather(tokens, 'head', axis=1, tiled=True)]
    ppermute x1 -> x33, waiting for transfers between devices: 0.01 us -> 58.1 us  [the longest x28 46.3 us: ring_send(): lax.ppermute(value, 'head', [(order[i], order[(i + step) % count]) for i...]
    dot_general x15 -> x0, matrix products: 43.1 us -> none  [the longest x9 18 us: batched(): return jnp.einsum(form, left, right, precision=lax.Precision.HIGHEST)]
    pallas_call x0 -> x15, Pallas kernels: none -> 29.2 us  [the longest x5 7.42 us: accumulate(): call(body, [WHOLE] * len(args), WHOLE, jax.ShapeDtypeStruct((parts, total...]
    ppermute x1 -> x33, starting transfers between devices: 4.3 us -> 29.1 us  [the longest x28 21.7 us: ring_send(): lax.ppermute(value, 'head', [(order[i], order[(i + step) % count]) for i...]
    psum x1 -> x0, waiting for transfers between devices: 19.5 us -> none  [shards(): summed = lax.psum(grads.astype(jnp.bfloat16), 'tok').astype(jnp.float32)]
    sub x2 -> x0, other arithmetic: 7.69 us -> none  [the longest x1 6.23 us: shards(): expo = jnp.exp(scores - top)]
  transfers between devices with their start and end apart: 4 -> 33, of which waited for: 3 -> 25; matrix products, arithmetic and copies ran while one was open for 8% -> 1% of each run, Pallas kernels for 0% -> 20%
where the time goes in v4:
time: 120 us; the launch traced here: 119 us
  waiting for transfers between devices  58.1 us (48%)
  Pallas kernels  29.2 us (24%)
  starting transfers between devices  29.1 us (24%)
  other arithmetic  1.58 us (1%)
    ppermute x28, waiting for transfers between devices, ring_send(): lax.ppermute(value, 'head', [(order[i], order[(i + step) % count]) for i...  46.3 us
    ppermute x28, starting transfers between devices, ring_send(): lax.ppermute(value, 'head', [(order[i], order[(i + step) % count]) for i...  21.7 us
    ppermute x1, waiting for transfers between devices, shards(): lax.ppermute(kv, 'tok', [(index, index + 1) for index in range(1, tok_cou...  11.1 us
    pallas_call x5, Pallas kernels, accumulate(): call(body, [WHOLE] * len(args), WHOLE, jax.ShapeDtypeStruct((parts, total...  7.42 us
    pallas_call x1, Pallas kernels, load(): call(body, [NUMBERS] + [IN_HBM] * count, [WHOLE] * count, [jax.ShapeDtype...  5.32 us
    pallas_call x2, Pallas kernels, partial_out(): call(body, [NUMBERS] + [WHOLE] * 5 + [AFTER] * len(after), [WHOLE] * (2 *...  4.68 us
    ppermute x4, starting transfers between devices, swap(): lax.ppermute(value, 'tok', [(index, index ^ bit) for index in range(count)])  4.15 us
    pallas_call x2, Pallas kernels, head_grads(): call(body, [NUMBERS] + [WHOLE] * len(args), [WHOLE] * len(kinds), [jax.Sh...  3.96 us
  transfers between devices with their start and end apart: 33, of which 25 were waited for; matrix products, arithmetic and copies ran while one was open for 1% of the time, Pallas kernels for 20%

profile of v4, /device:TPU:1, one launch (start us, length us, event | category | flops | bytes accessed | tf_op | source)
XLA Modules:
  0.0 119.0 jit_solution(9355361267760637252)
XLA Ops:
  0.0 0.7 dynamic-slice_bitcast_fusion.numbers_ref
  0.7 1.6 %shard_map.109 = (bf16[256,512]{1,0:T(8,128)(2,1)S(1)}, bf16[256,512]{1,0:T(8,128)(2,1)S(1)}) custom-call(s32[11]{0:T(128)S(1)} %dynamic-slice_bitcast_fusion.numbers_ref, bf16[512,512]{1,0:T(8,128)(2,1)} %in_ref.1), custom_call_target="tpu_custom_call" | custom-call | bytes 1048576 | tf_op jit(solution)/shard_map/pallas_call | solution.py:134
  2.3 2.1 %collective-permute-start.4 = (bf16[256,512]{1,0:T(8,128)(2,1)S(1)}, bf16[256,512]{1,0:T(8,128)(2,1)S(1)}, u32[]{:S(2)}, u32[]{:S(2)}) collective-permute-start(bf16[256,512]{1,0:T(8,128)(2,1)S(1)} %get-tuple-element.57.refs_3_), channel_id=1, source_target_pairs={{0,1},{2,0},{4,2},{6,4},{7,6},{5,7},{3,5},{1,3},{8,9},{10,8},{12,1... | collective-permute-start | bytes 786440 | tf_op jit(solution)/shard_map/ppermute | solution.py:57
  4.5 1.3 %collective-permute-start.2 = (bf16[256,512]{1,0:T(8,128)(2,1)S(1)}, bf16[256,512]{1,0:T(8,128)(2,1)S(1)}, u32[]{:S(2)}, u32[]{:S(2)}) collective-permute-start(bf16[256,512]{1,0:T(8,128)(2,1)S(1)} %get-tuple-element.54.refs_0_), channel_id=1, source_target_pairs={{0,1},{2,0},{4,2},{6,4},{7,6},{5,7},{3,5},{1,3},{8,9},{10,8},{12,1... | collective-permute-start | bytes 786440 | tf_op jit(solution)/shard_map/ppermute | solution.py:57
  6.0 5.3 %shard_map.110 = (bf16[4096,512]{1,0:T(8,128)(2,1)S(1)}, bf16[4096,512]{1,0:T(8,128)(2,1)S(1)}, bf16[4096,512]{1,0:T(8,128)(2,1)S(1)}) custom-call(s32[11]{0:T(128)S(1)} %dynamic-slice_bitcast_fusion.numbers_ref, bf16[4096,512]{1,0:T(8,128)(2,1)} %refs_0_.1, bf16[4096,512]{1,0:T(8,128)(2,1)} %refs_1_.1, bf16[4096,512]{1,0:T(8,128)(2,1)} %refs_2_.1), custom_call_target="tpu_custom_call" | custom-call | bytes 25165824 | tf_op jit(solution)/shard_map/pallas_call | solution.py:111
  11.4 1.4 %collective-permute-start.9 = (bf16[256,512]{1,0:T(8,128)(2,1)S(1)}, bf16[256,512]{1,0:T(8,128)(2,1)S(1)}, u32[]{:S(2)}, u32[]{:S(2)}) collective-permute-start(bf16[256,512]{1,0:T(8,128)(2,1)S(1)} %collective-permute-done.4.refs_5_), channel_id=1, source_target_pairs={{0,1},{2,0},{4,2},{6,4},{7,6},{5,7},{3,5},{1,3},{8,9},{10,8},{12,1... | collective-permute-start | bytes 786440 | tf_op jit(solution)/shard_map/ppermute | solution.py:57
  12.9 2.1 %collective-permute-start.5 = (f32[4,512]{1,0:T(4,128)S(1)}, f32[4,512]{1,0:T(4,128)S(1)}, u32[]{:S(2)}, u32[]{:S(2)}) collective-permute-start(f32[4,512]{1,0:T(4,128)S(1)} %bitcast.3), channel_id=1, source_target_pairs={{0,8},{8,0},{16,24},{24,16},{1,9},{9,1},{17,25},{25,17},{2,10},{10... | collective-permute-start | bytes 24584 | tf_op jit(solution)/shard_map/ppermute | solution.py:468
  15.0 1.2 collective-permute-done.2.refs_2_
  16.1 1.1 collective-permute-start.7
  17.2 0.4 collective-permute-start.8
  17.6 2.6 %shard_map.111.refs_7_ = f32[3,512,512]{2,1,0:T(8,128)S(1)} custom-call(bf16[256,512]{1,0:T(8,128)(2,1)S(1)} %get-tuple-element.54.refs_0_, bf16[256,512]{1,0:T(8,128)(2,1)S(1)} %collective-permute-done.refs_1_, bf16[256,512]{1,0:T(8,128)(2,1)S(1)} %collective-permute-done.2.refs_2_, bf16[256,512]{1,0:T(8,128)(2,1)S(1)} %get-tuple-element.57.refs_3_, ...), custom_call_target="tpu_custom_call" | custom-call | flops 2415919104 | bytes 12582912 | tf_op jit(solution)/shard_map/pallas_call | solution.py:179
  20.2 1.5 %collective-permute-done.9.refs_3_ = bf16[256,512]{1,0:T(8,128)(2,1)S(1)} collective-permute-done((bf16[256,512]{1,0:T(8,128)(2,1)S(1)}, bf16[256,512]{1,0:T(8,128)(2,1)S(1)}, u32[]{:S(2)}, u32[]{:S(2)}) %collective-permute-start.9) | collective-permute-done | bytes 262176 | tf_op jit(solution)/shard_map/ppermute | solution.py:57
  21.7 1.1 collective-permute-start.11
  22.8 0.4 collective-permute-start.6
  23.2 4.1 %collective-permute-done.7.refs_1_ = bf16[256,512]{1,0:T(8,128)(2,1)S(1)} collective-permute-done((bf16[256,512]{1,0:T(8,128)(2,1)S(1)}, bf16[256,512]{1,0:T(8,128)(2,1)S(1)}, u32[]{:S(2)}, u32[]{:S(2)}) %collective-permute-start.7) | collective-permute-done | bytes 262176 | tf_op jit(solution)/shard_map/ppermute | solution.py:57
  27.3 0.7 collective-permute-done.8.refs_2_
  28.1 1.3 %collective-permute-start.13 = (bf16[256,512]{1,0:T(8,128)(2,1)S(1)}, bf16[256,512]{1,0:T(8,128)(2,1)S(1)}, u32[]{:S(2)}, u32[]{:S(2)}) collective-permute-start(bf16[256,512]{1,0:T(8,128)(2,1)S(1)} %collective-permute-done.7.refs_1_), channel_id=1, source_target_pairs={{0,1},{2,0},{4,2},{6,4},{7,6},{5,7},{3,5},{1,3},{8,9},{10,8},{12,1... | collective-permute-start | bytes 786440 | tf_op jit(solution)/shard_map/ppermute | solution.py:57
  29.6 1.8 %shard_map.112.refs_7_ = f32[3,512,512]{2,1,0:T(8,128)S(1)} custom-call(bf16[256,512]{1,0:T(8,128)(2,1)S(1)} %collective-permute-done.1.refs_0_, bf16[256,512]{1,0:T(8,128)(2,1)S(1)} %collective-permute-done.7.refs_1_, bf16[256,512]{1,0:T(8,128)(2,1)S(1)} %collective-permute-done.8.refs_2_, ...), custom_call_target="tpu_custom_call", output_to_operand_aliasing={{}: (7, {})} | custom-call | flops 1610612736 | bytes 10485760 | tf_op jit(solution)/shard_map/pallas_call | solution.py:179
  31.4 1.6 %collective-permute-done.11.refs_3_ = bf16[256,512]{1,0:T(8,128)(2,1)S(1)} collective-permute-done((bf16[256,512]{1,0:T(8,128)(2,1)S(1)}, bf16[256,512]{1,0:T(8,128)(2,1)S(1)}, u32[]{:S(2)}, u32[]{:S(2)}) %collective-permute-start.11) | collective-permute-done | bytes 262176 | tf_op jit(solution)/shard_map/ppermute | solution.py:57
  33.0 0.7 collective-permute-done.6.refs_0_
  33.7 1.3 %collective-permute-start.12 = (bf16[256,512]{1,0:T(8,128)(2,1)S(1)}, bf16[256,512]{1,0:T(8,128)(2,1)S(1)}, u32[]{:S(2)}, u32[]{:S(2)}) collective-permute-start(bf16[256,512]{1,0:T(8,128)(2,1)S(1)} %collective-permute-done.11.refs_3_), channel_id=1, source_target_pairs={{0,1},{2,0},{4,2},{6,4},{7,6},{5,7},{3,5},{1,3},{8,9},{10,8},{12,1... | collective-permute-start | bytes 786440 | tf_op jit(solution)/shard_map/ppermute | solution.py:57
  35.0 0.2 collective-permute-start.10
  35.2 3.4 %collective-permute-done.13.refs_1_ = bf16[256,512]{1,0:T(8,128)(2,1)S(1)} collective-permute-done((bf16[256,512]{1,0:T(8,128)(2,1)S(1)}, bf16[256,512]{1,0:T(8,128)(2,1)S(1)}, u32[]{:S(2)}, u32[]{:S(2)}) %collective-permute-start.13) | collective-permute-done | bytes 262176 | tf_op jit(solution)/shard_map/ppermute | solution.py:57
  38.6 0.7 collective-permute-done.14.refs_2_
  39.3 1.8 %shard_map.113.refs_3_.refs_4_ = f32[3,512,512]{2,1,0:T(8,128)S(1)} custom-call(bf16[256,512]{1,0:T(8,128)(2,1)S(1)} %collective-permute-done.6.refs_0_, bf16[256,512]{1,0:T(8,128)(2,1)S(1)} %collective-permute-done.13.refs_1_, bf16[256,512]{1,0:T(8,128)(2,1)S(1)} %collective-permute-done.14.refs_2_, ...), custom_call_target="tpu_custom_call", output_to_operand_aliasing={{}: (7, {})} | custom-call | flops 1610612736 | bytes 10485760 | tf_op jit(solution)/shard_map/pallas_call | solution.py:179
  41.2 3.0 %collective-permute-done.12.refs_1_ = bf16[256,512]{1,0:T(8,128)(2,1)S(1)} collective-permute-done((bf16[256,512]{1,0:T(8,128)(2,1)S(1)}, bf16[256,512]{1,0:T(8,128)(2,1)S(1)}, u32[]{:S(2)}, u32[]{:S(2)}) %collective-permute-start.12) | collective-permute-done | bytes 262176 | tf_op jit(solution)/shard_map/ppermute | solution.py:57
  44.2 0.7 collective-permute-done.10.refs_0_
  44.9 0.7 shard_map.115.kv_ref
  45.7 1.9 %collective-permute-start.15 = (bf16[2,512,512]{2,1,0:T(8,128)(2,1)S(1)}, bf16[2,512,512]{2,1,0:T(8,128)(2,1)S(1)}, u32[]{:S(2)}, u32[]{:S(2)}) collective-permute-start(bf16[2,512,512]{2,1,0:T(8,128)(2,1)S(1)} %shard_map.115.kv_ref), channel_id=1, source_target_pairs={{0,8},{8,0},{16,24},{24,16},{1,9},{9,1},{17,25},{25,17},{2,10},{10... | collective-permute-start | bytes 3145736 | tf_op jit(solution)/shard_map/ppermute | solution.py:468
  47.6 3.3 %collective-permute-start.16 = (bf16[2,512,512]{2,1,0:T(8,128)(2,1)S(1)}, bf16[2,512,512]{2,1,0:T(8,128)(2,1)S(1)}, u32[]{:S(2)}, u32[]{:S(2)}) collective-permute-start(bf16[2,512,512]{2,1,0:T(8,128)(2,1)S(1)} %shard_map.115.kv_ref), channel_id=1, source_target_pairs={{8,16},{9,17},{10,18},{11,19},{12,20},{13,21},{14,22},{15,23}} | collective-permute-start | bytes 3145736 | tf_op jit(solution)/shard_map/ppermute | solution.py:500
  50.9 2.0 %shard_map.117.rest_0_ = f32[2,3,128,256]{3,2,1,0:T(8,128)S(1)} custom-call(s32[11]{0:T(128)S(1)} %dynamic-slice_bitcast_fusion.numbers_ref, bf16[2,512,512]{2,1,0:T(8,128)(2,1)S(1)} %shard_map.115.kv_ref, f32[4,512]{1,0:T(4,128)S(1)} %bitcast.4, f32[4,128,256]{2,1,0:T(8,128)S(1)} %copy-done.1, f32[4,128,256]{2,1,0:T(8,128)S(1)} %copy-done.2, ...), custom_call_target="tpu_custom_call" | custom-call | flops 402653184 | bytes 1572864 | tf_op jit(solution)/shard_map/pallas_call | solution.py:238
  52.9 2.0 %shard_map.118 = (f32[2,3,128,256]{3,2,1,0:T(8,128)S(1)}, bf16[2,3,128,256]{3,2,1,0:T(8,128)(2,1)S(1)}) custom-call(s32[11]{0:T(128)S(1)} %dynamic-slice_bitcast_fusion.numbers_ref, bf16[2,512,512]{2,1,0:T(8,128)(2,1)S(1)} %collective-permute-done.15.beside_ref.kv_ref, f32[4,512]{1,0:T(4,128)S(1)} %collective-permute-done.5.rate_ref, ...), custom_call_target="tpu_custom_call" | custom-call | flops 402653184 | bytes 1572864 | tf_op jit(solution)/shard_map/pallas_call | solution.py:238
  55.0 0.4 shard_map.114.q_ref
  55.4 11.1 %collective-permute-done.16.behind_ref = bf16[2,512,512]{2,1,0:T(8,128)(2,1)S(1)} collective-permute-done((bf16[2,512,512]{2,1,0:T(8,128)(2,1)S(1)}, bf16[2,512,512]{2,1,0:T(8,128)(2,1)S(1)}, u32[]{:S(2)}, u32[]{:S(2)}) %collective-permute-start.16) | collective-permute-done | bytes 1048608 | tf_op jit(solution)/shard_map/ppermute | solution.py:500
  66.6 3.9 %shard_map.116.rest_1_.attended_ref = f32[512,512]{1,0:T(8,128)S(1)} custom-call(s32[11]{0:T(128)S(1)} %dynamic-slice_bitcast_fusion.numbers_ref, bf16[1,512,512]{2,1,0:T(8,128)(2,1)S(1)} %shard_map.114.q_ref, bf16[2,512,512]{2,1,0:T(8,128)(2,1)S(1)} %shard_map.115.kv_ref, bf16[2,512,512]{2,1,0:T(8,128)(2,1)S(1)} %collective-permute-done.15.beside_ref.kv_ref, ...), custom_call_target="tpu_custom_call" | custom-call | flops 805306368 | bytes 2097152 | tf_op jit(solution)/shard_map/pallas_call | solution.py:325
  70.5 0.3 collective-permute-done.17.rest_0_
  70.8 0.9 shard_map.119.net_ref
  71.7 1.3 %shard_map.120.near_ref = bf16[512,256]{1,0:T(8,128)(2,1)S(1)} custom-call(s32[11]{0:T(128)S(1)} %dynamic-slice_bitcast_fusion.numbers_ref, bf16[1,512,512]{2,1,0:T(8,128)(2,1)S(1)} %shard_map.114.q_ref, f32[512,512]{1,0:T(8,128)S(1)} %shard_map.116.rest_1_.attended_ref, bf16[2,3,128,256]{3,2,1,0:T(8,128)(2,1)S(1)} %shard_map.119.net_ref), custom_call_target="tpu_custom_call" | custom-call | flops 201326592 | bytes 1048576 | tf_op jit(solution)/shard_map/pallas_call | solution.py:356
  73.0 0.4 collective-permute-done.18.net_ref
  73.4 2.0 %shard_map.121 = (bf16[64,2048]{1,0:T(8,128)(2,1)S(1)}, bf16[64,2048]{1,0:T(8,128)(2,1)S(1)}, bf16[64,2048]{1,0:T(8,128)(2,1)S(1)}, bf16[64,2048]{1,0:T(8,128)(2...) custom-call(s32[11]{0:T(128)S(1)} %dynamic-slice_bitcast_fusion.numbers_ref, ...), custom_call_target="tpu_custom_call" | custom-call | flops 805306368 | bytes 5767168 | tf_op jit(solution)/shard_map/pallas_call | solution.py:408
  75.5 1.3 %collective-permute-start.20 = (bf16[64,2048]{1,0:T(8,128)(2,1)S(1)}, bf16[64,2048]{1,0:T(8,128)(2,1)S(1)}, u32[]{:S(2)}, u32[]{:S(2)}) collective-permute-start(bf16[64,2048]{1,0:T(8,128)(2,1)S(1)} %get-tuple-element.74), channel_id=1, source_target_pairs={{0,1},{2,0},{4,2},{6,4},{7,6},{5,7},{3,5},{1,3},{8,9},{10,8},{12,1... | collective-permute-start | bytes 786440 | tf_op jit(solution)/shard_map/ppermute | solution.py:57
  77.0 1.3 %collective-permute-start.22 = (bf16[64,2048]{1,0:T(8,128)(2,1)S(1)}, bf16[64,2048]{1,0:T(8,128)(2,1)S(1)}, u32[]{:S(2)}, u32[]{:S(2)}) collective-permute-start(bf16[64,2048]{1,0:T(8,128)(2,1)S(1)} %get-tuple-element.83), channel_id=1, source_target_pairs={{0,1},{2,0},{4,2},{6,4},{7,6},{5,7},{3,5},{1,3},{8,9},{10,8},{12,1... | collective-permute-start | bytes 786440 | tf_op jit(solution)/shard_map/ppermute | solution.py:57
  78.3 0.2 collective-permute-start.21
  78.5 4.8 %collective-permute-done.20.refs_1_ = bf16[64,2048]{1,0:T(8,128)(2,1)S(1)} collective-permute-done((bf16[64,2048]{1,0:T(8,128)(2,1)S(1)}, bf16[64,2048]{1,0:T(8,128)(2,1)S(1)}, u32[]{:S(2)}, u32[]{:S(2)}) %collective-permute-start.20) | collective-permute-done | bytes 262176 | tf_op jit(solution)/shard_map/ppermute | solution.py:57
  83.4 0.9 collective-permute-done.19.refs_0_
  84.4 1.3 %collective-permute-start.26 = (bf16[64,2048]{1,0:T(8,128)(2,1)S(1)}, bf16[64,2048]{1,0:T(8,128)(2,1)S(1)}, u32[]{:S(2)}, u32[]{:S(2)}) collective-permute-start(bf16[64,2048]{1,0:T(8,128)(2,1)S(1)} %add_convert_fusion.8), channel_id=1, source_target_pairs={{0,1},{2,0},{4,2},{6,4},{7,6},{5,7},{3,5},{1,3},{8,9},{10,8},{12,1... | collective-permute-start | bytes 786440 | tf_op jit(solution)/shard_map/ppermute | solution.py:57
  85.9 2.6 %shard_map.122 = (bf16[64,2048]{1,0:T(8,128)(2,1)S(1)}, bf16[64,2048]{1,0:T(8,128)(2,1)S(1)}, bf16[64,2048]{1,0:T(8,128)(2,1)S(1)}, bf16[64,2048]{1,0:T(8,128)(2...) custom-call(s32[11]{0:T(128)S(1)} %dynamic-slice_bitcast_fusion.numb, ...), custom_call_target="tpu_custom_call" | custom-call | flops 1342177280 | bytes 6815744 | tf_op jit(solution)/shard_map/pallas_call | solution.py:408
  88.5 0.4 collective-permute-done.22
  89.0 0.9 collective-permute-done.21
  90.0 1.3 %collective-permute-start.24 = (bf16[64,2048]{1,0:T(8,128)(2,1)S(1)}, bf16[64,2048]{1,0:T(8,128)(2,1)S(1)}, u32[]{:S(2)}, u32[]{:S(2)}) collective-permute-start(bf16[64,2048]{1,0:T(8,128)(2,1)S(1)} %add_convert_fusion.10), channel_id=1, source_target_pairs={{0,1},{2,0},{4,2},{6,4},{7,6},{5,7},{3,5},{1,3},{8,9},{10,8},{12,1... | collective-permute-start | bytes 786440 | tf_op jit(solution)/shard_map/ppermute | solution.py:57
  91.5 3.1 %collective-permute-done.26 = bf16[64,2048]{1,0:T(8,128)(2,1)S(1)} collective-permute-done((bf16[64,2048]{1,0:T(8,128)(2,1)S(1)}, bf16[64,2048]{1,0:T(8,128)(2,1)S(1)}, u32[]{:S(2)}, u32[]{:S(2)}) %collective-permute-start.26) | collective-permute-done | bytes 262176 | tf_op jit(solution)/shard_map/ppermute | solution.py:57
  94.6 0.9 collective-permute-done.25
  95.6 1.3 %collective-permute-start.30 = (bf16[64,2048]{1,0:T(8,128)(2,1)S(1)}, bf16[64,2048]{1,0:T(8,128)(2,1)S(1)}, u32[]{:S(2)}, u32[]{:S(2)}) collective-permute-start(bf16[64,2048]{1,0:T(8,128)(2,1)S(1)} %add_convert_fusion.4), channel_id=1, source_target_pairs={{0,1},{2,0},{4,2},{6,4},{7,6},{5,7},{3,5},{1,3},{8,9},{10,8},{12,1... | collective-permute-start | bytes 786440 | tf_op jit(solution)/shard_map/ppermute | solution.py:57
  97.1 3.1 %collective-permute-done.24 = bf16[64,2048]{1,0:T(8,128)(2,1)S(1)} collective-permute-done((bf16[64,2048]{1,0:T(8,128)(2,1)S(1)}, bf16[64,2048]{1,0:T(8,128)(2,1)S(1)}, u32[]{:S(2)}, u32[]{:S(2)}) %collective-permute-start.24) | collective-permute-done | bytes 262176 | tf_op jit(solution)/shard_map/ppermute | solution.py:57
  100.2 0.9 collective-permute-done.23
  101.2 0.2 collective-permute-start.27
  101.4 1.3 %collective-permute-start.28 = (bf16[64,2048]{1,0:T(8,128)(2,1)S(1)}, bf16[64,2048]{1,0:T(8,128)(2,1)S(1)}, u32[]{:S(2)}, u32[]{:S(2)}) collective-permute-start(bf16[64,2048]{1,0:T(8,128)(2,1)S(1)} %add_convert_fusion.6), channel_id=1, source_target_pairs={{0,1},{2,0},{4,2},{6,4},{7,6},{5,7},{3,5},{1,3},{8,9},{10,8},{12,1... | collective-permute-start | bytes 786440 | tf_op jit(solution)/shard_map/ppermute | solution.py:57
  102.7 3.1 %collective-permute-done.30 = bf16[64,2048]{1,0:T(8,128)(2,1)S(1)} collective-permute-done((bf16[64,2048]{1,0:T(8,128)(2,1)S(1)}, bf16[64,2048]{1,0:T(8,128)(2,1)S(1)}, u32[]{:S(2)}, u32[]{:S(2)}) %collective-permute-start.30) | collective-permute-done | bytes 262176 | tf_op jit(solution)/shard_map/ppermute | solution.py:57
  105.9 0.9 collective-permute-done.29
  106.8 0.2 collective-permute-start.31
  107.1 1.3 %collective-permute-start.32 = (bf16[64,2048]{1,0:T(8,128)(2,1)S(1)}, bf16[64,2048]{1,0:T(8,128)(2,1)S(1)}, u32[]{:S(2)}, u32[]{:S(2)}) collective-permute-start(bf16[64,2048]{1,0:T(8,128)(2,1)S(1)} %add_convert_fusion.2), channel_id=1, source_target_pairs={{0,1},{2,0},{4,2},{6,4},{7,6},{5,7},{3,5},{1,3},{8,9},{10,8},{12,1... | collective-permute-start | bytes 786440 | tf_op jit(solution)/shard_map/ppermute | solution.py:57
  108.4 4.0 %collective-permute-done.27.refs_2_ = bf16[64,2048]{1,0:T(8,128)(2,1)S(1)} collective-permute-done((bf16[64,2048]{1,0:T(8,128)(2,1)S(1)}, bf16[64,2048]{1,0:T(8,128)(2,1)S(1)}, u32[]{:S(2)}, u32[]{:S(2)}) %collective-permute-start.27) | collective-permute-done | bytes 262176 | tf_op jit(solution)/shard_map/ppermute | solution.py:57
  112.5 5.5 %collective-permute-done.31 = bf16[64,2048]{1,0:T(8,128)(2,1)S(1)} collective-permute-done((bf16[64,2048]{1,0:T(8,128)(2,1)S(1)}, bf16[64,2048]{1,0:T(8,128)(2,1)S(1)}, u32[]{:S(2)}, u32[]{:S(2)}) %collective-permute-start.31) | collective-permute-done | bytes 262176 | tf_op jit(solution)/shard_map/ppermute | solution.py:57
  118.1 0.8 pad_maximum_fusion
  (43 shorter events, 2.4 us)
Async XLA Ops:
  2.3 9.1 %collective-permute-start.4 = (bf16[256,512]{1,0:T(8,128)(2,1)S(1)}, bf16[256,512]{1,0:T(8,128)(2,1)S(1)}, u32[]{:S(2)}, u32[]{:S(2)}) collective-permute-start(bf16[256,512]{1,0:T(8,128)(2,1)S(1)} %get-tuple-element.57.refs_3_), channel_id=1, source_target_pairs={{0,1},{2,0},{4,2},{6,4},{7,6},{5,7},{3,5},{1,3},{8,9},{10,8},{12,1... | collective-permute-start | bytes 786440 | tf_op jit(solution)/shard_map/ppermute | solution.py:57
  4.4 8.5 %copy-start.4 = (f32[512,4]{0,1:T(4,128)S(1)}, f32[512,4]{0,1:T(4,128)}, u32[]{:S(2)}) copy-start(f32[512,4]{0,1:T(4,128)} %param.19) | copy-start | bytes 24580
  4.4 8.3 %collective-permute-start = (bf16[256,512]{1,0:T(8,128)(2,1)S(1)}, bf16[256,512]{1,0:T(8,128)(2,1)S(1)}, u32[]{:S(2)}, u32[]{:S(2)}) collective-permute-start(bf16[256,512]{1,0:T(8,128)(2,1)S(1)} %get-tuple-element.54.refs_0_), channel_id=1, source_target_pairs={{0,2},{2,4},{4,6},{6,7},{7,5},{5,3},{3,1},{1,0},{8,10},{10,12},{12... | collective-permute-start | bytes 786440 | tf_op jit(solution)/shard_map/ppermute | solution.py:57
  4.5 11.6 %collective-permute-start.2 = (bf16[256,512]{1,0:T(8,128)(2,1)S(1)}, bf16[256,512]{1,0:T(8,128)(2,1)S(1)}, u32[]{:S(2)}, u32[]{:S(2)}) collective-permute-start(bf16[256,512]{1,0:T(8,128)(2,1)S(1)} %get-tuple-element.54.refs_0_), channel_id=1, source_target_pairs={{0,1},{2,0},{4,2},{6,4},{7,6},{5,7},{3,5},{1,3},{8,9},{10,8},{12,1... | collective-permute-start | bytes 786440 | tf_op jit(solution)/shard_map/ppermute | solution.py:57
  5.8 11.3 %collective-permute-start.3 = (bf16[256,512]{1,0:T(8,128)(2,1)S(1)}, bf16[256,512]{1,0:T(8,128)(2,1)S(1)}, u32[]{:S(2)}, u32[]{:S(2)}) collective-permute-start(bf16[256,512]{1,0:T(8,128)(2,1)S(1)} %get-tuple-element.57.refs_3_), channel_id=1, source_target_pairs={{0,2},{2,4},{4,6},{6,7},{7,5},{5,3},{3,1},{1,0},{8,10},{10,12},{12... | collective-permute-start | bytes 786440 | tf_op jit(solution)/shard_map/ppermute | solution.py:57
  11.4 10.4 %collective-permute-start.9 = (bf16[256,512]{1,0:T(8,128)(2,1)S(1)}, bf16[256,512]{1,0:T(8,128)(2,1)S(1)}, u32[]{:S(2)}, u32[]{:S(2)}) collective-permute-start(bf16[256,512]{1,0:T(8,128)(2,1)S(1)} %collective-permute-done.4.refs_5_), channel_id=1, source_target_pairs={{0,1},{2,0},{4,2},{6,4},{7,6},{5,7},{3,5},{1,3},{8,9},{10,8},{12,1... | collective-permute-start | bytes 786440 | tf_op jit(solution)/shard_map/ppermute | solution.py:57
  12.7 10.1 %collective-permute-start.1 = (bf16[256,512]{1,0:T(8,128)(2,1)S(1)}, bf16[256,512]{1,0:T(8,128)(2,1)S(1)}, u32[]{:S(2)}, u32[]{:S(2)}) collective-permute-start(bf16[256,512]{1,0:T(8,128)(2,1)S(1)} %collective-permute-done.refs_1_), channel_id=1, source_target_pairs={{0,2},{2,4},{4,6},{6,7},{7,5},{5,3},{3,1},{1,0},{8,10},{10,12},{12... | collective-permute-start | bytes 786440 | tf_op jit(solution)/shard_map/ppermute | solution.py:57
  12.9 7.3 %collective-permute-start.5 = (f32[4,512]{1,0:T(4,128)S(1)}, f32[4,512]{1,0:T(4,128)S(1)}, u32[]{:S(2)}, u32[]{:S(2)}) collective-permute-start(f32[4,512]{1,0:T(4,128)S(1)} %bitcast.3), channel_id=1, source_target_pairs={{0,8},{8,0},{16,24},{24,16},{1,9},{9,1},{17,25},{25,17},{2,10},{10... | collective-permute-start | bytes 24584 | tf_op jit(solution)/shard_map/ppermute | solution.py:468
  16.1 11.2 %collective-permute-start.7 = (bf16[256,512]{1,0:T(8,128)(2,1)S(1)}, bf16[256,512]{1,0:T(8,128)(2,1)S(1)}, u32[]{:S(2)}, u32[]{:S(2)}) collective-permute-start(bf16[256,512]{1,0:T(8,128)(2,1)S(1)} %collective-permute-done.2.refs_2_), channel_id=1, source_target_pairs={{0,1},{2,0},{4,2},{6,4},{7,6},{5,7},{3,5},{1,3},{8,9},{10,8},{12,1... | collective-permute-start | bytes 786440 | tf_op jit(solution)/shard_map/ppermute | solution.py:57
  17.2 10.9 %collective-permute-start.8 = (bf16[256,512]{1,0:T(8,128)(2,1)S(1)}, bf16[256,512]{1,0:T(8,128)(2,1)S(1)}, u32[]{:S(2)}, u32[]{:S(2)}) collective-permute-start(bf16[256,512]{1,0:T(8,128)(2,1)S(1)} %collective-permute-done.3.refs_4_), channel_id=1, source_target_pairs={{0,2},{2,4},{4,6},{6,7},{7,5},{5,3},{3,1},{1,0},{8,10},{10,12},{12... | collective-permute-start | bytes 786440 | tf_op jit(solution)/shard_map/ppermute | solution.py:57
  21.7 11.2 %collective-permute-start.11 = (bf16[256,512]{1,0:T(8,128)(2,1)S(1)}, bf16[256,512]{1,0:T(8,128)(2,1)S(1)}, u32[]{:S(2)}, u32[]{:S(2)}) collective-permute-start(bf16[256,512]{1,0:T(8,128)(2,1)S(1)} %collective-permute-done.9.refs_3_), channel_id=1, source_target_pairs={{0,1},{2,0},{4,2},{6,4},{7,6},{5,7},{3,5},{1,3},{8,9},{10,8},{12,1... | collective-permute-start | bytes 786440 | tf_op jit(solution)/shard_map/ppermute | solution.py:57
  22.8 10.9 %collective-permute-start.6 = (bf16[256,512]{1,0:T(8,128)(2,1)S(1)}, bf16[256,512]{1,0:T(8,128)(2,1)S(1)}, u32[]{:S(2)}, u32[]{:S(2)}) collective-permute-start(bf16[256,512]{1,0:T(8,128)(2,1)S(1)} %collective-permute-done.1.refs_0_), channel_id=1, source_target_pairs={{0,2},{2,4},{4,6},{6,7},{7,5},{5,3},{3,1},{1,0},{8,10},{10,12},{12... | collective-permute-start | bytes 786440 | tf_op jit(solution)/shard_map/ppermute | solution.py:57
  28.1 10.5 %collective-permute-start.13 = (bf16[256,512]{1,0:T(8,128)(2,1)S(1)}, bf16[256,512]{1,0:T(8,128)(2,1)S(1)}, u32[]{:S(2)}, u32[]{:S(2)}) collective-permute-start(bf16[256,512]{1,0:T(8,128)(2,1)S(1)} %collective-permute-done.7.refs_1_), channel_id=1, source_target_pairs={{0,1},{2,0},{4,2},{6,4},{7,6},{5,7},{3,5},{1,3},{8,9},{10,8},{12,1... | collective-permute-start | bytes 786440 | tf_op jit(solution)/shard_map/ppermute | solution.py:57
  29.4 9.9 %collective-permute-start.14 = (bf16[256,512]{1,0:T(8,128)(2,1)S(1)}, bf16[256,512]{1,0:T(8,128)(2,1)S(1)}, u32[]{:S(2)}, u32[]{:S(2)}) collective-permute-start(bf16[256,512]{1,0:T(8,128)(2,1)S(1)} %collective-permute-done.8.refs_2_), channel_id=1, source_target_pairs={{0,2},{2,4},{4,6},{6,7},{7,5},{5,3},{3,1},{1,0},{8,10},{10,12},{12... | collective-permute-start | bytes 786440 | tf_op jit(solution)/shard_map/ppermute | solution.py:57
  33.7 10.5 %collective-permute-start.12 = (bf16[256,512]{1,0:T(8,128)(2,1)S(1)}, bf16[256,512]{1,0:T(8,128)(2,1)S(1)}, u32[]{:S(2)}, u32[]{:S(2)}) collective-permute-start(bf16[256,512]{1,0:T(8,128)(2,1)S(1)} %collective-permute-done.11.refs_3_), channel_id=1, source_target_pairs={{0,1},{2,0},{4,2},{6,4},{7,6},{5,7},{3,5},{1,3},{8,9},{10,8},{12,1... | collective-permute-start | bytes 786440 | tf_op jit(solution)/shard_map/ppermute | solution.py:57
  35.0 9.9 %collective-permute-start.10 = (bf16[256,512]{1,0:T(8,128)(2,1)S(1)}, bf16[256,512]{1,0:T(8,128)(2,1)S(1)}, u32[]{:S(2)}, u32[]{:S(2)}) collective-permute-start(bf16[256,512]{1,0:T(8,128)(2,1)S(1)} %collective-permute-done.6.refs_0_), channel_id=1, source_target_pairs={{0,2},{2,4},{4,6},{6,7},{7,5},{5,3},{3,1},{1,0},{8,10},{10,12},{12... | collective-permute-start | bytes 786440 | tf_op jit(solution)/shard_map/ppermute | solution.py:57
  41.2 9.7 %copy-start.1 = (f32[4,128,256]{2,1,0:T(8,128)S(1)}, f32[4,128,256]{2,1,0:T(8,128)}, u32[]{:S(2)}) copy-start(f32[4,128,256]{2,1,0:T(8,128)} %gate_ref.5) | copy-start | bytes 1572868
  41.2 9.7 %copy-start.2 = (f32[4,128,256]{2,1,0:T(8,128)S(1)}, f32[4,128,256]{2,1,0:T(8,128)}, u32[]{:S(2)}) copy-start(f32[4,128,256]{2,1,0:T(8,128)} %up_ref.5) | copy-start | bytes 1572868
  41.2 9.7 %copy-start.3 = (f32[4,256,128]{2,1,0:T(8,128)S(1)}, f32[4,256,128]{2,1,0:T(8,128)}, u32[]{:S(2)}) copy-start(f32[4,256,128]{2,1,0:T(8,128)} %down_ref.5) | copy-start | bytes 1572868
  45.7 7.2 %collective-permute-start.15 = (bf16[2,512,512]{2,1,0:T(8,128)(2,1)S(1)}, bf16[2,512,512]{2,1,0:T(8,128)(2,1)S(1)}, u32[]{:S(2)}, u32[]{:S(2)}) collective-permute-start(bf16[2,512,512]{2,1,0:T(8,128)(2,1)S(1)} %shard_map.115.kv_ref), channel_id=1, source_target_pairs={{0,8},{8,0},{16,24},{24,16},{1,9},{9,1},{17,25},{25,17},{2,10},{10... | collective-permute-start | bytes 3145736 | tf_op jit(solution)/shard_map/ppermute | solution.py:468
  47.6 19.0 %collective-permute-start.16 = (bf16[2,512,512]{2,1,0:T(8,128)(2,1)S(1)}, bf16[2,512,512]{2,1,0:T(8,128)(2,1)S(1)}, u32[]{:S(2)}, u32[]{:S(2)}) collective-permute-start(bf16[2,512,512]{2,1,0:T(8,128)(2,1)S(1)} %shard_map.115.kv_ref), channel_id=1, source_target_pairs={{8,16},{9,17},{10,18},{11,19},{12,20},{13,21},{14,22},{15,23}} | collective-permute-start | bytes 3145736 | tf_op jit(solution)/shard_map/ppermute | solution.py:500
  54.9 15.9 %collective-permute-start.17 = (bf16[2,3,128,256]{3,2,1,0:T(8,128)(2,1)S(1)}, bf16[2,3,128,256]{3,2,1,0:T(8,128)(2,1)S(1)}, u32[]{:S(2)}, u32[]{:S(2)}) collective-permute-start(bf16[2,3,128,256]{3,2,1,0:T(8,128)(2,1)S(1)} %get-tuple-element.70), channel_id=1, source_target_pairs={{0,16},{8,24},{16,0},{24,8},{1,17},{9,25},{17,1},{25,9},{2,18},{10... | collective-permute-start | bytes 1179656 | tf_op jit(solution)/shard_map/ppermute | solution.py:468
  55.4 15.4 %copy-start.5 = (f32[4]{0:T(128)S(1)}, f32[4]{0:T(128)}, u32[]{:S(2)}) copy-start(f32[4]{0:T(128)} %step_ref.1) | copy-start | bytes 52
  70.5 3.0 %copy-start = (bf16[512,4096]{1,0:T(8,128)(2,1)S(1)}, bf16[512,4096]{1,0:T(8,128)(2,1)}, u32[]{:S(2)}) copy-start(bf16[512,4096]{1,0:T(8,128)(2,1)} %w_ref.3) | copy-start | bytes 12582916
  71.7 1.8 %collective-permute-start.18 = (bf16[2,3,128,256]{3,2,1,0:T(8,128)(2,1)S(1)}, bf16[2,3,128,256]{3,2,1,0:T(8,128)(2,1)S(1)}, u32[]{:S(2)}, u32[]{:S(2)}) collective-permute-start(bf16[2,3,128,256]{3,2,1,0:T(8,128)(2,1)S(1)} %shard_map.119.net_ref), channel_id=1, source_target_pairs={{0,8},{8,0},{16,24},{24,16},{1,9},{9,1},{17,25},{25,17},{2,10},{10... | collective-permute-start | bytes 1179656 | tf_op jit(solution)/shard_map/ppermute | solution.py:468
  75.5 7.8 %collective-permute-start.20 = (bf16[64,2048]{1,0:T(8,128)(2,1)S(1)}, bf16[64,2048]{1,0:T(8,128)(2,1)S(1)}, u32[]{:S(2)}, u32[]{:S(2)}) collective-permute-start(bf16[64,2048]{1,0:T(8,128)(2,1)S(1)} %get-tuple-element.74), channel_id=1, source_target_pairs={{0,1},{2,0},{4,2},{6,4},{7,6},{5,7},{3,5},{1,3},{8,9},{10,8},{12,1... | collective-permute-start | bytes 786440 | tf_op jit(solution)/shard_map/ppermute | solution.py:57
  76.8 7.5 %collective-permute-start.19 = (bf16[64,2048]{1,0:T(8,128)(2,1)S(1)}, bf16[64,2048]{1,0:T(8,128)(2,1)S(1)}, u32[]{:S(2)}, u32[]{:S(2)}) collective-permute-start(bf16[64,2048]{1,0:T(8,128)(2,1)S(1)} %get-tuple-element.73), channel_id=1, source_target_pairs={{0,2},{2,4},{4,6},{6,7},{7,5},{5,3},{3,1},{1,0},{8,10},{10,12},{12... | collective-permute-start | bytes 786440 | tf_op jit(solution)/shard_map/ppermute | solution.py:57
  77.0 11.9 %collective-permute-start.22 = (bf16[64,2048]{1,0:T(8,128)(2,1)S(1)}, bf16[64,2048]{1,0:T(8,128)(2,1)S(1)}, u32[]{:S(2)}, u32[]{:S(2)}) collective-permute-start(bf16[64,2048]{1,0:T(8,128)(2,1)S(1)} %get-tuple-element.83), channel_id=1, source_target_pairs={{0,1},{2,0},{4,2},{6,4},{7,6},{5,7},{3,5},{1,3},{8,9},{10,8},{12,1... | collective-permute-start | bytes 786440 | tf_op jit(solution)/shard_map/ppermute | solution.py:57
  78.3 11.6 %collective-permute-start.21 = (bf16[64,2048]{1,0:T(8,128)(2,1)S(1)}, bf16[64,2048]{1,0:T(8,128)(2,1)S(1)}, u32[]{:S(2)}, u32[]{:S(2)}) collective-permute-start(bf16[64,2048]{1,0:T(8,128)(2,1)S(1)} %get-tuple-element.81), channel_id=1, source_target_pairs={{0,2},{2,4},{4,6},{6,7},{7,5},{5,3},{3,1},{1,0},{8,10},{10,12},{12... | collective-permute-start | bytes 786440 | tf_op jit(solution)/shard_map/ppermute | solution.py:57
  84.4 10.2 %collective-permute-start.26 = (bf16[64,2048]{1,0:T(8,128)(2,1)S(1)}, bf16[64,2048]{1,0:T(8,128)(2,1)S(1)}, u32[]{:S(2)}, u32[]{:S(2)}) collective-permute-start(bf16[64,2048]{1,0:T(8,128)(2,1)S(1)} %add_convert_fusion.8), channel_id=1, source_target_pairs={{0,1},{2,0},{4,2},{6,4},{7,6},{5,7},{3,5},{1,3},{8,9},{10,8},{12,1... | collective-permute-start | bytes 786440 | tf_op jit(solution)/shard_map/ppermute | solution.py:57
  85.7 9.8 %collective-permute-start.25 = (bf16[64,2048]{1,0:T(8,128)(2,1)S(1)}, bf16[64,2048]{1,0:T(8,128)(2,1)S(1)}, u32[]{:S(2)}, u32[]{:S(2)}) collective-permute-start(bf16[64,2048]{1,0:T(8,128)(2,1)S(1)} %add_convert_fusion.9), channel_id=1, source_target_pairs={{0,2},{2,4},{4,6},{6,7},{7,5},{5,3},{3,1},{1,0},{8,10},{10,12},{12... | collective-permute-start | bytes 786440 | tf_op jit(solution)/shard_map/ppermute | solution.py:57
  90.0 10.2 %collective-permute-start.24 = (bf16[64,2048]{1,0:T(8,128)(2,1)S(1)}, bf16[64,2048]{1,0:T(8,128)(2,1)S(1)}, u32[]{:S(2)}, u32[]{:S(2)}) collective-permute-start(bf16[64,2048]{1,0:T(8,128)(2,1)S(1)} %add_convert_fusion.10), channel_id=1, source_target_pairs={{0,1},{2,0},{4,2},{6,4},{7,6},{5,7},{3,5},{1,3},{8,9},{10,8},{12,1... | collective-permute-start | bytes 786440 | tf_op jit(solution)/shard_map/ppermute | solution.py:57
  91.3 9.8 %collective-permute-start.23 = (bf16[64,2048]{1,0:T(8,128)(2,1)S(1)}, bf16[64,2048]{1,0:T(8,128)(2,1)S(1)}, u32[]{:S(2)}, u32[]{:S(2)}) collective-permute-start(bf16[64,2048]{1,0:T(8,128)(2,1)S(1)} %add_convert_fusion.11), channel_id=1, source_target_pairs={{0,2},{2,4},{4,6},{6,7},{7,5},{5,3},{3,1},{1,0},{8,10},{10,12},{12... | collective-permute-start | bytes 786440 | tf_op jit(solution)/shard_map/ppermute | solution.py:57
  95.6 10.2 %collective-permute-start.30 = (bf16[64,2048]{1,0:T(8,128)(2,1)S(1)}, bf16[64,2048]{1,0:T(8,128)(2,1)S(1)}, u32[]{:S(2)}, u32[]{:S(2)}) collective-permute-start(bf16[64,2048]{1,0:T(8,128)(2,1)S(1)} %add_convert_fusion.4), channel_id=1, source_target_pairs={{0,1},{2,0},{4,2},{6,4},{7,6},{5,7},{3,5},{1,3},{8,9},{10,8},{12,1... | collective-permute-start | bytes 786440 | tf_op jit(solution)/shard_map/ppermute | solution.py:57
  97.0 9.8 %collective-permute-start.29 = (bf16[64,2048]{1,0:T(8,128)(2,1)S(1)}, bf16[64,2048]{1,0:T(8,128)(2,1)S(1)}, u32[]{:S(2)}, u32[]{:S(2)}) collective-permute-start(bf16[64,2048]{1,0:T(8,128)(2,1)S(1)} %add_convert_fusion.5), channel_id=1, source_target_pairs={{0,2},{2,4},{4,6},{6,7},{7,5},{5,3},{3,1},{1,0},{8,10},{10,12},{12... | collective-permute-start | bytes 786440 | tf_op jit(solution)/shard_map/ppermute | solution.py:57
  101.2 11.2 %collective-permute-start.27 = (bf16[64,2048]{1,0:T(8,128)(2,1)S(1)}, bf16[64,2048]{1,0:T(8,128)(2,1)S(1)}, u32[]{:S(2)}, u32[]{:S(2)}) collective-permute-start(bf16[64,2048]{1,0:T(8,128)(2,1)S(1)} %add_convert_fusion.7), channel_id=1, source_target_pairs={{0,2},{2,4},{4,6},{6,7},{7,5},{5,3},{3,1},{1,0},{8,10},{10,12},{12... | collective-permute-start | bytes 786440 | tf_op jit(solution)/shard_map/ppermute | solution.py:57
  101.4 10.9 %collective-permute-start.28 = (bf16[64,2048]{1,0:T(8,128)(2,1)S(1)}, bf16[64,2048]{1,0:T(8,128)(2,1)S(1)}, u32[]{:S(2)}, u32[]{:S(2)}) collective-permute-start(bf16[64,2048]{1,0:T(8,128)(2,1)S(1)} %add_convert_fusion.6), channel_id=1, source_target_pairs={{0,1},{2,0},{4,2},{6,4},{7,6},{5,7},{3,5},{1,3},{8,9},{10,8},{12,1... | collective-permute-start | bytes 786440 | tf_op jit(solution)/shard_map/ppermute | solution.py:57
  106.8 11.2 %collective-permute-start.31 = (bf16[64,2048]{1,0:T(8,128)(2,1)S(1)}, bf16[64,2048]{1,0:T(8,128)(2,1)S(1)}, u32[]{:S(2)}, u32[]{:S(2)}) collective-permute-start(bf16[64,2048]{1,0:T(8,128)(2,1)S(1)} %add_convert_fusion.3), channel_id=1, source_target_pairs={{0,2},{2,4},{4,6},{6,7},{7,5},{5,3},{3,1},{1,0},{8,10},{10,12},{12... | collective-permute-start | bytes 786440 | tf_op jit(solution)/shard_map/ppermute | solution.py:57
  107.1 11.0 %collective-permute-start.32 = (bf16[64,2048]{1,0:T(8,128)(2,1)S(1)}, bf16[64,2048]{1,0:T(8,128)(2,1)S(1)}, u32[]{:S(2)}, u32[]{:S(2)}) collective-permute-start(bf16[64,2048]{1,0:T(8,128)(2,1)S(1)} %add_convert_fusion.2), channel_id=1, source_target_pairs={{0,1},{2,0},{4,2},{6,4},{7,6},{5,7},{3,5},{1,3},{8,9},{10,8},{12,1... | collective-permute-start | bytes 786440 | tf_op jit(solution)/shard_map/ppermute | solution.py:57

commit v5 on v4

v5 whole, which is shorter than its diff:
```python
import functools

import jax
import jax.numpy as jnp
from jax import lax
from jax.experimental import pallas as pl
from jax.experimental.pallas import tpu as pltpu
from jax.sharding import PartitionSpec as P

WINDOW = 512
CHUNKS = 2
F32 = jnp.float32
BF16 = jnp.bfloat16
LOG2E = 1.4426950408889634


def call(body, in_specs, out_specs, out_shape, scratch=(), vmem=8, cost=None, aliases=None):
    return pl.pallas_call(
        body,
        in_specs=in_specs,
        out_specs=out_specs,
        out_shape=out_shape,
        scratch_shapes=list(scratch),
        input_output_aliases=aliases or {},
        cost_estimate=cost,
        compiler_params=pltpu.CompilerParams(vmem_limit_bytes=vmem * 1024 * 1024),
    )


def cost(flops, moved, exps=0):
    return pl.CostEstimate(flops=int(flops), bytes_accessed=int(moved), transcendentals=int(exps))


WHOLE = pl.BlockSpec(memory_space=pltpu.VMEM)
AFTER = pl.BlockSpec(memory_space=pl.ANY)
SCALARS = pl.BlockSpec(memory_space=pltpu.SMEM)
IN_HBM = pl.BlockSpec(memory_space=pltpu.HBM)


def mm(left, right, dims=((1,), (0,))):
    return lax.dot_general(left, right, (dims, ((), ())), preferred_element_type=F32)


def sigmoid(x):
    return 0.5 * jnp.tanh(0.5 * x) + 0.5


def ring_order(count):
    return list(range(0, count, 2)) + list(range(count - 1, 0, -2))


def ring_send(value, step):
    order = ring_order(lax.axis_size("head"))
    count = len(order)
    return lax.ppermute(
        value, "head", [(order[i], order[(i + step) % count]) for i in range(count)]
    )


def ring_offsets():
    steps = lax.axis_size("head") // 2
    return [0] + [way * step for step in range(1, steps) for way in (-1, 1)] + [steps]


def ring_index(offset):
    count = lax.axis_size("head")
    me = lax.axis_index("head")
    at = lax.rem(jnp.where(me % 2 == 0, me // 2, count - 1 - me // 2) + offset + count, count)
    return jnp.where(at < count // 2, 2 * at, 2 * (count - 1 - at) + 1)


def first_head(heads, other=False):
    side = lax.axis_index("tok") % 2
    return (1 - side if other else side) * heads


def hbm(array):
    return pltpu.with_memory_space_constraint(array, pltpu.HBM)


def run_copies(copies):
    for copy in copies:
        copy.start()
    for copy in copies:
        copy.wait()


def load(arrays):
    count = len(arrays)
    blocks = len(ring_offsets())
    size = arrays[0].shape[0] // blocks

    def body(*refs):
        out_refs, sems = refs[count:-1], refs[-1]
        starts = [pl.multiple_of(ring_index(offset) * size, size) for offset in ring_offsets()]
        run_copies(
            [
                pltpu.make_async_copy(
                    refs[index].at[pl.ds(starts[block], size)],
                    out_refs[index].at[pl.ds(block * size, size)],
                    sems.at[index, block],
                )
                for block in range(blocks)
                for index in range(count)
            ]
        )

    return call(
        body,
        [IN_HBM] * count,
        [WHOLE] * count,
        [jax.ShapeDtypeStruct(array.shape, array.dtype) for array in arrays],
        [pltpu.SemaphoreType.DMA((count, blocks))],
        vmem=1,
        cost=cost(0, sum(4 * array.size for array in arrays)),
    )(*[hbm(array) for array in arrays])


def split_rows(tokens):
    rows, width = tokens.shape[0] // CHUNKS, tokens.shape[1]

    def body(in_ref, *refs):
        out_refs, sems = refs[:-1], refs[-1]
        run_copies(
            [
                pltpu.make_async_copy(in_ref.at[pl.ds(c * rows, rows)], out_refs[c], sems.at[c])
                for c in range(CHUNKS)
            ]
        )

    return call(
        body,
        [IN_HBM],
        [WHOLE] * CHUNKS,
        [jax.ShapeDtypeStruct((rows, width), tokens.dtype)] * CHUNKS,
        [pltpu.SemaphoreType.DMA((CHUNKS,))],
        vmem=1,
        cost=cost(0, 4 * tokens.size),
    )(hbm(tokens))


def gather_step(held, ways, after):
    moved = {}
    for way in ways:
        value = held[way]
        if after is not None:
            value, _ = lax.optimization_barrier((value, after))
        moved[way] = ring_send(value, way)
    return moved


def accumulate(chunks, first, last, weights, before=None, lead=0, shared=False):
    rows, depth = chunks[0][0].shape
    width = weights[0].shape[1]
    parts, span = len(weights), last - first
    total = rows * len(chunks)
    final = last == lax.axis_size("head")
    dtype = BF16 if final else F32
    pieces = [chunk[index] for chunk in chunks for index in range(first, last)]

    def body(*refs):
        piece_refs = refs[: len(pieces)]
        weight_refs = refs[len(pieces) : len(pieces) + parts]
        out_ref, left = refs[-2 - shared], refs[-1]
        for index, ref in enumerate(piece_refs):
            chunk, piece = divmod(index, span)
            left[chunk * rows : (chunk + 1) * rows, piece * depth : (piece + 1) * depth] = ref[...]
        for part in range(parts):
            term = mm(left[...], weight_refs[part][first * depth : last * depth])
            if before is not None:
                term = term + refs[len(args) - 1][lead + part]
            out_ref[part] = term.astype(dtype)
            if shared:
                refs[-2][part] = out_ref[part, :, lanes(1 - lax.axis_index("tok") % 2, width // 2)]

    aliased = before is not None and not final
    args = [*pieces, *weights] + ([] if before is None else [before])
    return call(
        body,
        [WHOLE] * len(args),
        [WHOLE] * (1 + shared),
        [jax.ShapeDtypeStruct((parts, total, size), dtype) for size in (width, width // 2)[: 1 + shared]],
        [pltpu.VMEM((total, span * depth), BF16)],
        vmem=12,
        cost=cost(
            2 * total * span * depth * width * parts,
            2 * span * depth * (total + width * parts) + 8 * total * width * parts,
        ),
        aliases={len(args) - 1: 0} if aliased else None,
    )(*args)


def lanes(head, size):
    return pl.ds(pl.multiple_of(head * size, size), size)


def normed(values):
    values = values.astype(F32)
    scale = lax.rsqrt(jnp.mean(values * values, axis=-1, keepdims=True) + 1e-06)
    return (values * scale).astype(BF16)


def head_grads(kv, rate, fast_gate, fast_up, fast_down, before=None):
    rows = kv.shape[1]
    size, hidden_size = fast_gate.shape[1:]
    count = rate.shape[0]
    heads = count // 2
    whole = kv.shape[2] == count * size

    def body(kv_ref, rate_ref, gate_ref, up_ref, down_ref, *rest):
        rates = rate_ref[...].T
        column = lax.broadcasted_iota(jnp.int32, (rows, count), 1)
        for index in range(heads):
            head = first_head(heads) + index
            mine = jnp.sum(jnp.where(column == head, rates, 0.0), axis=1, keepdims=True)
            lane = lanes(head if whole else index, size)
            knorm = normed(kv_ref[0, :, lane])
            target = (-mine * kv_ref[1, :, lane].astype(F32)).astype(BF16)
            gate_pre = mm(knorm, gate_ref[head].astype(BF16))
            up_pre = mm(knorm, up_ref[head].astype(BF16))
            back = mm(target, down_ref[head].astype(BF16), ((1,), (1,)))
            sigma = sigmoid(gate_pre)
            active = gate_pre * sigma
            first = back * up_pre * (sigma + active * (1.0 - sigma))
            both = jnp.concatenate([first.astype(BF16), (back * active).astype(BF16)], axis=1)
            third = (active * up_pre).astype(BF16)
            pair = mm(knorm, both, ((0,), (0,)))
            terms = (pair[:, :hidden_size], pair[:, hidden_size:], mm(target, third, ((0,), (0,))))
            for part, term in enumerate(terms):
                if before is not None:
                    term = term + rest[0][index, part]
                    rest[-1][index, part] = term.astype(BF16)
                    rest[-2][index, part] = term
                else:
                    rest[-1][index, part] = term

    args = [kv, rate, fast_gate, fast_up, fast_down] + ([] if before is None else [before])
    kinds = [F32] if before is None else [F32, BF16]
    return call(
        body,
        [WHOLE] * len(args),
        [WHOLE] * len(kinds),
        [jax.ShapeDtypeStruct((heads, 3, size, hidden_size), kind) for kind in kinds],
        cost=cost(
            12 * heads * rows * size * hidden_size,
            8 * heads * 3 * size * hidden_size,
            heads * rows * hidden_size,
        ),
    )(*args)


def renew(kept, received, step, fast_gate, fast_up, fast_down, after):
    heads, _, size, hidden_size = kept.shape

    def body(step_ref, kept_ref, gate_ref, up_ref, down_ref, *rest):
        out_ref = rest[-1]
        for index in range(heads):
            head = first_head(heads) + index
            for part in range(3):
                grad = kept_ref[index, part]
                for more in rest[: len(received)]:
                    grad = grad + more[index, part].astype(F32)
                if part < 2:
                    matrix = (gate_ref, up_ref)[part][head]
                    fan = size
                else:
                    matrix = down_ref[head].T
                    fan = hidden_size
                mean_sq = jnp.sum(grad * grad, keepdims=True) / (size * hidden_size)
                scale = step_ref[head] * fan ** (-0.5) * lax.rsqrt(mean_sq + 1e-06)
                out_ref[index, part] = (matrix - scale * grad).astype(BF16)

    return call(
        body,
        [SCALARS] + [WHOLE] * (4 + len(received)) + [AFTER] * len(after),
        WHOLE,
        jax.ShapeDtypeStruct(kept.shape, BF16),
        cost=cost(10 * kept.size, 12 * kept.size),
    )(step, kept, fast_gate, fast_up, fast_down, *received, *after)


def attend_blocks(query, blocks, earlier=None):
    factor = query.shape[-1] ** (-0.5) * LOG2E
    scores = []
    for key, _, allowed in blocks:
        part = mm(query, key, ((1,), (1,))) * factor
        scores.append(part if allowed is None else jnp.where(allowed, part, -1e30))
    tops = [jnp.max(part, axis=-1, keepdims=True) for part in scores]
    result, total = 0.0, 0.0
    if earlier is not None:
        tops.append(earlier[1])
    top = functools.reduce(jnp.maximum, tops)
    if earlier is not None:
        shrink = jnp.exp2(earlier[1] - top)
        result, total = earlier[0] * shrink, earlier[2] * shrink
    for part, (_, value, _) in zip(scores, blocks):
        weight = jnp.exp2(part - top)
        total = total + jnp.sum(weight, axis=-1, keepdims=True)
        result = result + mm(weight.astype(BF16), value)
    return result, top, total


def halves(rows):
    return [slice(index * rows // 2, (index + 1) * rows // 2) for index in range(2)]


def earlier_blocks(ref, index, lane):
    rows = ref.shape[1]
    row = lax.broadcasted_iota(jnp.int32, (rows // 2, rows // 2), 0)
    col = lax.broadcasted_iota(jnp.int32, (rows // 2, rows // 2), 1)
    blocks = [(ref[0, halves(rows)[index], lane], ref[1, halves(rows)[index], lane], col > row)]
    if index == 0:
        blocks.append((ref[0, halves(rows)[1], lane], ref[1, halves(rows)[1], lane], None))
    return blocks


def attend_own(query, kv, size):
    rows = query.shape[1]
    heads = query.shape[2] // size
    row = (rows // 2, rows // 2)

    def body(q_ref, kv_ref, out_ref, stats_ref):
        causal = lax.broadcasted_iota(jnp.int32, row, 1) <= lax.broadcasted_iota(jnp.int32, row, 0)
        for index, where in enumerate(halves(rows)):
            stats = []
            for head in range(heads):
                lane = slice(head * size, (head + 1) * size)
                blocks = [
                    (kv_ref[0, keys, lane], kv_ref[1, keys, lane], causal if at == index else None)
                    for at, keys in enumerate(halves(rows)[: index + 1])
                ]
                result, top, total = attend_blocks(q_ref[0, where, lane], blocks)
                out_ref[where, lane] = result
                stats += [top, total]
            stats_ref[where] = jnp.concatenate(stats, axis=1)

    return call(
        body,
        [WHOLE] * 2,
        [WHOLE] * 2,
        [
            jax.ShapeDtypeStruct((rows, heads * size), F32),
            jax.ShapeDtypeStruct((rows, 2 * heads), F32),
        ],
        cost=cost(3 * heads * size * rows * rows, 8 * rows * heads * size, heads * rows * rows),
    )(query, kv)


def attend_behind(summed, stats, query, behind, size):
    rows = query.shape[1]
    heads = query.shape[2] // size

    def body(sum_ref, stats_ref, q_ref, behind_ref, out_ref):
        needed = lax.axis_index("tok") > 0

        @pl.when(needed)
        def _():
            for index, where in enumerate(halves(rows)):
                for head in range(heads):
                    lane = slice(head * size, (head + 1) * size)
                    top, total = (stats_ref[where, 2 * head + at : 2 * head + at + 1] for at in (0, 1))
                    result, _, total = attend_blocks(
                        q_ref[0, where, lane],
                        earlier_blocks(behind_ref, index, lane),
                        (sum_ref[where, lane], top, total),
                    )
                    out_ref[where, lane] = result / total

        @pl.when(jnp.logical_not(needed))
        def _():
            for head in range(heads):
                lane = slice(head * size, (head + 1) * size)
                out_ref[:, lane] = sum_ref[:, lane] / stats_ref[:, 2 * head + 1 : 2 * head + 2]

    return call(
        body,
        [WHOLE] * 4,
        WHOLE,
        jax.ShapeDtypeStruct(summed.shape, F32),
        cost=cost(3 * heads * size * rows * rows, 8 * rows * heads * size, heads * rows * rows),
    )(summed, stats, query, behind)


def fast_apply(query, gate, upper, down):
    qnorm = normed(query)
    gate_pre = mm(qnorm, gate)
    hidden = gate_pre * sigmoid(gate_pre) * mm(qnorm, upper)
    return mm(hidden.astype(BF16), down, ((1,), (1,)))


def combine_near(query, attended, nets):
    rows = query.shape[1]
    heads, _, size, hidden_size = nets.shape

    def body(q_ref, attended_ref, net_ref, out_ref):
        for index in range(heads):
            lane = lanes(first_head(heads) + index, size)
            fast = fast_apply(q_ref[0, :, lane], *(net_ref[index, part] for part in range(3)))
            where = slice(index * size, (index + 1) * size)
            out_ref[:, where] = (attended_ref[:, lane] + fast).astype(BF16)

    return call(
        body,
        [WHOLE] * 3,
        WHOLE,
        jax.ShapeDtypeStruct((rows, heads * size), BF16),
        cost=cost(
            6 * heads * rows * size * hidden_size,
            8 * heads * rows * size,
            heads * rows * hidden_size,
        ),
    )(query, attended, nets)


def partial_out(offsets, query, attended, nets, near, w_out, after=()):
    rows = near.shape[0] // lax.axis_size("head")
    heads, _, size, hidden_size = nets.shape
    depth = heads * size
    count = len(offsets)
    width = w_out.shape[1]
    block = width // 8

    def body(q_ref, attended_ref, net_ref, near_ref, w_ref, *refs):
        out_refs, far_ref = refs[len(after) : -1], refs[-1]
        starts = [pl.multiple_of(ring_index(offset) * rows, rows) for offset in offsets]

        def take(ref, lane):
            return jnp.concatenate([ref[pl.ds(start, rows), lane] for start in starts], axis=0)

        for index in range(heads):
            lane = lanes(first_head(heads, True) + index, size)
            fast = fast_apply(
                take(q_ref.at[0], lane), *(net_ref[index, part] for part in range(3))
            )
            where = slice(index * size, (index + 1) * size)
            far_ref[:, where] = (take(attended_ref, lane) + fast).astype(BF16)
        left = take(near_ref, slice(None))
        near_rows = pl.ds(pl.multiple_of(first_head(heads) * size, depth), depth)
        far_rows = pl.ds(pl.multiple_of(first_head(heads, True) * size, depth), depth)
        for column in range(0, width, block):
            result = mm(left, w_ref[near_rows, column : column + block])
            result += mm(far_ref[...], w_ref[far_rows, column : column + block])
            result = result.astype(BF16)
            half, at = divmod(column, width // 2)
            for index in range(count):
                out_refs[2 * index + half][:, at : at + block] = result[
                    index * rows : (index + 1) * rows
                ]

    outs = call(
        body,
        [WHOLE] * 5 + [AFTER] * len(after),
        [WHOLE] * (2 * count),
        [jax.ShapeDtypeStruct((rows, width // 2), BF16)] * (2 * count),
        [pltpu.VMEM((count * rows, depth), BF16)],
        vmem=8,
        cost=cost(4 * count * rows * depth * width, 2 * width * (2 * depth + count * rows)),
    )(query, attended, nets, near, w_out, *after)
    return {offset: tuple(outs[2 * at : 2 * at + 2]) for at, offset in enumerate(offsets)}


def ring_reduce(query, attended, nets, near, w_out):
    steps = lax.axis_size("head") // 2
    signed = [sign * step for step in range(steps - 1, 0, -1) for sign in (1, -1)]
    shared = (query, attended, nets, near, w_out)
    parts = partial_out([steps], *shared) | partial_out(signed[:2], *shared)
    coming = {}
    ordered = ()
    for which in range(2 * steps - 1):
        step, half = steps - (which + 1) // 2, which % 2
        if which == 2:
            parts |= partial_out(signed[2:] + [0], *shared, tuple(coming.values())[:2])
        terms = []
        for way in (1, -1):
            side = half if way == 1 else 1 - half
            term = parts[steps if step == steps else way * step][side]
            if (way, side) in coming:
                term = (term.astype(F32) + coming[way, side].astype(F32)).astype(BF16)
            terms.append(term)
        ordered = lax.optimization_barrier((*terms, *ordered))[:2]
        for way, term in zip((1, -1), ordered):
            coming[way, half if way == 1 else 1 - half] = ring_send(term, way)
    sides = {1: 1 - half, -1: half}
    totals = add_pair(
        [parts[0][sides[way]] for way in (1, -1)], [coming.pop((way, sides[way])) for way in (1, -1)]
    )
    totals = {sides[way]: total for way, total in zip((1, -1), totals)}
    ends = [totals[side] for side in range(2)]
    for (_, side), more in coming.items():
        ends[side] = ends[side] + more.astype(F32)
    return jnp.concatenate([end.astype(BF16) for end in ends], axis=1)


def add_pair(own, came):
    def body(*refs):
        for index in range(2):
            refs[4 + index][...] = refs[index][...].astype(F32) + refs[2 + index][...].astype(F32)

    return call(
        body,
        [WHOLE] * 4,
        [WHOLE] * 2,
        [jax.ShapeDtypeStruct(value.shape, F32) for value in own],
        cost=cost(0, 64 * own[0].size),
    )(*own, *came)


def swap(value, bit):
    count = lax.axis_size("tok")
    return lax.ppermute(value, "tok", [(index, index ^ bit) for index in range(count)])


def shards(
    tokens, w_query, w_key, w_value, w_out, fast_gate, fast_up, fast_down, token_rate, head_step
):
    local_heads, head_size, _ = fast_gate.shape
    tok_count = lax.axis_size("tok")
    steps = lax.axis_size("head") // 2
    nets = (fast_gate, fast_up, fast_down)
    rate = token_rate.T
    rate_beside = swap(rate, 1)

    own = split_rows(tokens)
    weights = load([w_key, w_value, w_query])
    chunks = [[piece] for piece in own]
    held = [{1: piece, -1: piece} for piece in own]
    sums, done = None, 0
    for step in range(1, steps + 1):
        after = (None, None, weights[0], (sums, rate_beside))[step] if step < 4 else sums
        for c in range(CHUNKS):
            last = (1,) if c % 2 == 0 else (-1,)
            held[c] = gather_step(held[c], (1, -1) if step < steps else last, after)
            chunks[c] += held[c].values()
        if step > 1:
            known = [chunk[: 2 * step - 1] for chunk in chunks]
            (sums,) = accumulate(known, done, 2 * step - 1, weights, sums)
            done = 2 * step - 1
    kv, far = accumulate(chunks, done, 2 * steps, weights[:2], sums, shared=True)
    (query,) = accumulate(chunks, done, 2 * steps, weights[2:], sums, 2)

    behind = lax.ppermute(kv, "tok", [(index, index + 1) for index in range(tok_count - 1)])
    beside = swap(far, 1)
    (grads,) = head_grads(kv, rate, *nets)
    grads, travel = head_grads(beside, rate_beside, *nets, grads)
    received = []
    for bit in range(1, tok_count.bit_length() - 1):
        if received:
            travel = grads
            for more in received:
                travel = travel + more.astype(F32)
            travel = travel.astype(BF16)
        received.append(swap(travel, 1 << bit))
    summed, stats = attend_own(query, kv, head_size)
    attended = attend_behind(summed, stats, query, behind, head_size)
    mine = renew(grads, received, head_step, *nets, (attended,))
    near = combine_near(query, attended, mine)
    return ring_reduce(query, attended, swap(mine, 1), near, w_out)


def solution(mesh):
    placed = (
        P("tok", "head"),
        P(None, "head"),
        P(None, "head"),
        P(None, "head"),
        P("head", None),
        P("head", None, None),
        P("head", None, None),
        P("head", None, None),
        P("tok", "head"),
        P("head"),
    )
    return jax.shard_map(
        shards, mesh=mesh, in_specs=placed, out_specs=P(("tok", "head"), None), check_vma=False
    )
```

time: 120 us -> 119 us (level)
  waiting for transfers between devices: 58.1 us -> 56 us
    ppermute x1, waiting for transfers between devices: 11.1 us -> 8.89 us  [shards(): lax.ppermute(kv, 'tok', [(index, index + 1) for index in range(tok_count...]
    ppermute x1, starting transfers between devices: 3.29 us -> 4.9 us  [shards(): lax.ppermute(kv, 'tok', [(index, index + 1) for index in range(tok_count...]
    pallas_call x14 -> x16, Pallas kernels: 29.1 us -> 29.2 us  [the longest x5 7.61 us: accumulate(): call(body, [WHOLE] * len(args), [WHOLE] * (1 + shared), [jax.ShapeDtypeSt...]
  transfers between devices with their start and end apart: 33 -> 33, of which waited for: 25 -> 25; matrix products, arithmetic and copies ran while one was open for 1% -> 1% of each run, Pallas kernels for 20% -> 22%
where the time goes in v5:
time: 119 us; the launch traced here: 117 us
  waiting for transfers between devices  56 us (47%)
  starting transfers between devices  30.2 us (25%)
  Pallas kernels  29.3 us (25%)
  other arithmetic  1.6 us (1%)
    ppermute x28, waiting for transfers between devices, ring_send(): lax.ppermute(value, 'head', [(order[i], order[(i + step) % count]) for i...  45.7 us
    ppermute x28, starting transfers between devices, ring_send(): lax.ppermute(value, 'head', [(order[i], order[(i + step) % count]) for i...  21.7 us
    ppermute x1, waiting for transfers between devices, shards(): lax.ppermute(kv, 'tok', [(index, index + 1) for index in range(tok_count...  8.89 us
    pallas_call x5, Pallas kernels, accumulate(): call(body, [WHOLE] * len(args), [WHOLE] * (1 + shared), [jax.ShapeDtypeSt...  7.61 us
    ppermute x1, starting transfers between devices, shards(): lax.ppermute(kv, 'tok', [(index, index + 1) for index in range(tok_count...  4.9 us
    pallas_call x1, Pallas kernels, load(): call(body, [IN_HBM] * count, [WHOLE] * count, [jax.ShapeDtypeStruct(array...  4.78 us
    pallas_call x1, Pallas kernels, attend_behind(): call(body, [WHOLE] * 4, WHOLE, jax.ShapeDtypeStruct(summed.shape, F32), c...  4.63 us
    pallas_call x3, Pallas kernels, partial_out(): call(body, [WHOLE] * 5 + [AFTER] * len(after), [WHOLE] * (2 * count), [ja...  4.58 us
  transfers between devices with their start and end apart: 33, of which 25 were waited for; matrix products, arithmetic and copies ran while one was open for 1% of the time, Pallas kernels for 22%

profile of v5, /device:TPU:1, one launch (start us, length us, event | category | flops | bytes accessed | tf_op | source)
XLA Modules:
  0.0 117.5 jit_solution(1002432482257248046)
XLA Ops:
  0.0 1.0 shard_map.100
  1.1 2.1 %collective-permute-start.4 = (bf16[256,512]{1,0:T(8,128)(2,1)S(1)}, bf16[256,512]{1,0:T(8,128)(2,1)S(1)}, u32[]{:S(2)}, u32[]{:S(2)}) collective-permute-start(bf16[256,512]{1,0:T(8,128)(2,1)S(1)} %get-tuple-element.59.refs_3_), channel_id=1, source_target_pairs={{0,1},{2,0},{4,2},{6,4},{7,6},{5,7},{3,5},{1,3},{8,9},{10,8},{12,1... | collective-permute-start | bytes 786440 | tf_op jit(solution)/shard_map/ppermute | solution.py:55
  3.3 1.3 %collective-permute-start.2 = (bf16[256,512]{1,0:T(8,128)(2,1)S(1)}, bf16[256,512]{1,0:T(8,128)(2,1)S(1)}, u32[]{:S(2)}, u32[]{:S(2)}) collective-permute-start(bf16[256,512]{1,0:T(8,128)(2,1)S(1)} %get-tuple-element.56.refs_0_), channel_id=1, source_target_pairs={{0,1},{2,0},{4,2},{6,4},{7,6},{5,7},{3,5},{1,3},{8,9},{10,8},{12,1... | collective-permute-start | bytes 786440 | tf_op jit(solution)/shard_map/ppermute | solution.py:55
  4.8 4.8 %shard_map.101 = (bf16[4096,512]{1,0:T(8,128)(2,1)S(1)}, bf16[4096,512]{1,0:T(8,128)(2,1)S(1)}, bf16[4096,512]{1,0:T(8,128)(2,1)S(1)}) custom-call(bf16[4096,512]{1,0:T(8,128)(2,1)} %refs_0_.1, bf16[4096,512]{1,0:T(8,128)(2,1)} %refs_1_.1, bf16[4096,512]{1,0:T(8,128)(2,1)} %refs_2_.1), custom_call_target="tpu_custom_call" | custom-call | bytes 25165824 | tf_op jit(solution)/shard_map/pallas_call | solution.py:108
  9.6 1.4 %collective-permute-start.9 = (bf16[256,512]{1,0:T(8,128)(2,1)S(1)}, bf16[256,512]{1,0:T(8,128)(2,1)S(1)}, u32[]{:S(2)}, u32[]{:S(2)}) collective-permute-start(bf16[256,512]{1,0:T(8,128)(2,1)S(1)} %collective-permute-done.4.refs_5_), channel_id=1, source_target_pairs={{0,1},{2,0},{4,2},{6,4},{7,6},{5,7},{3,5},{1,3},{8,9},{10,8},{12,1... | collective-permute-start | bytes 786440 | tf_op jit(solution)/shard_map/ppermute | solution.py:55
  11.1 2.4 %collective-permute-start.5 = (f32[4,512]{1,0:T(4,128)S(1)}, f32[4,512]{1,0:T(4,128)S(1)}, u32[]{:S(2)}, u32[]{:S(2)}) collective-permute-start(f32[4,512]{1,0:T(4,128)S(1)} %bitcast.1), channel_id=1, source_target_pairs={{0,8},{8,0},{16,24},{24,16},{1,9},{9,1},{17,25},{25,17},{2,10},{10... | collective-permute-start | bytes 24584 | tf_op jit(solution)/shard_map/ppermute | solution.py:510
  13.5 1.4 %collective-permute-done.2.refs_2_ = bf16[256,512]{1,0:T(8,128)(2,1)S(1)} collective-permute-done((bf16[256,512]{1,0:T(8,128)(2,1)S(1)}, bf16[256,512]{1,0:T(8,128)(2,1)S(1)}, u32[]{:S(2)}, u32[]{:S(2)}) %collective-permute-start.2) | collective-permute-done | bytes 262176 | tf_op jit(solution)/shard_map/ppermute | solution.py:55
  14.9 1.1 collective-permute-start.7
  15.9 0.4 collective-permute-start.8
  16.4 2.6 %shard_map.102.refs_7_ = f32[3,512,512]{2,1,0:T(8,128)S(1)} custom-call(bf16[256,512]{1,0:T(8,128)(2,1)S(1)} %get-tuple-element.56.refs_0_, bf16[256,512]{1,0:T(8,128)(2,1)S(1)} %collective-permute-done.refs_1_, bf16[256,512]{1,0:T(8,128)(2,1)S(1)} %collective-permute-done.2.refs_2_, bf16[256,512]{1,0:T(8,128)(2,1)S(1)} %get-tuple-element.59.refs_3_, ...), custom_call_target="tpu_custom_call" | custom-call | flops 2415919104 | bytes 12582912 | tf_op jit(solution)/shard_map/pallas_call | solution.py:178
  19.0 1.5 %collective-permute-done.9.refs_3_ = bf16[256,512]{1,0:T(8,128)(2,1)S(1)} collective-permute-done((bf16[256,512]{1,0:T(8,128)(2,1)S(1)}, bf16[256,512]{1,0:T(8,128)(2,1)S(1)}, u32[]{:S(2)}, u32[]{:S(2)}) %collective-permute-start.9) | collective-permute-done | bytes 262176 | tf_op jit(solution)/shard_map/ppermute | solution.py:55
  20.5 1.1 collective-permute-start.11
  21.6 0.4 collective-permute-start.6
  22.0 4.1 %collective-permute-done.7.refs_1_ = bf16[256,512]{1,0:T(8,128)(2,1)S(1)} collective-permute-done((bf16[256,512]{1,0:T(8,128)(2,1)S(1)}, bf16[256,512]{1,0:T(8,128)(2,1)S(1)}, u32[]{:S(2)}, u32[]{:S(2)}) %collective-permute-start.7) | collective-permute-done | bytes 262176 | tf_op jit(solution)/shard_map/ppermute | solution.py:55
  26.1 0.7 collective-permute-done.8.refs_2_
  26.9 1.3 %collective-permute-start.13 = (bf16[256,512]{1,0:T(8,128)(2,1)S(1)}, bf16[256,512]{1,0:T(8,128)(2,1)S(1)}, u32[]{:S(2)}, u32[]{:S(2)}) collective-permute-start(bf16[256,512]{1,0:T(8,128)(2,1)S(1)} %collective-permute-done.7.refs_1_), channel_id=1, source_target_pairs={{0,1},{2,0},{4,2},{6,4},{7,6},{5,7},{3,5},{1,3},{8,9},{10,8},{12,1... | collective-permute-start | bytes 786440 | tf_op jit(solution)/shard_map/ppermute | solution.py:55
  28.2 0.2 collective-permute-start.14
  28.3 1.8 %shard_map.103.refs_7_ = f32[3,512,512]{2,1,0:T(8,128)S(1)} custom-call(bf16[256,512]{1,0:T(8,128)(2,1)S(1)} %collective-permute-done.1.refs_0_, bf16[256,512]{1,0:T(8,128)(2,1)S(1)} %collective-permute-done.7.refs_1_, bf16[256,512]{1,0:T(8,128)(2,1)S(1)} %collective-permute-done.8.refs_2_, ...), custom_call_target="tpu_custom_call", output_to_operand_aliasing={{}: (7, {})} | custom-call | flops 1610612736 | bytes 10485760 | tf_op jit(solution)/shard_map/pallas_call | solution.py:178
  30.2 1.6 %collective-permute-done.11.refs_3_ = bf16[256,512]{1,0:T(8,128)(2,1)S(1)} collective-permute-done((bf16[256,512]{1,0:T(8,128)(2,1)S(1)}, bf16[256,512]{1,0:T(8,128)(2,1)S(1)}, u32[]{:S(2)}, u32[]{:S(2)}) %collective-permute-start.11) | collective-permute-done | bytes 262176 | tf_op jit(solution)/shard_map/ppermute | solution.py:55
  31.7 0.7 collective-permute-done.6.refs_0_
  32.5 1.3 %collective-permute-start.12 = (bf16[256,512]{1,0:T(8,128)(2,1)S(1)}, bf16[256,512]{1,0:T(8,128)(2,1)S(1)}, u32[]{:S(2)}, u32[]{:S(2)}) collective-permute-start(bf16[256,512]{1,0:T(8,128)(2,1)S(1)} %collective-permute-done.11.refs_3_), channel_id=1, source_target_pairs={{0,1},{2,0},{4,2},{6,4},{7,6},{5,7},{3,5},{1,3},{8,9},{10,8},{12,1... | collective-permute-start | bytes 786440 | tf_op jit(solution)/shard_map/ppermute | solution.py:55
  33.9 3.4 %collective-permute-done.13.refs_1_ = bf16[256,512]{1,0:T(8,128)(2,1)S(1)} collective-permute-done((bf16[256,512]{1,0:T(8,128)(2,1)S(1)}, bf16[256,512]{1,0:T(8,128)(2,1)S(1)}, u32[]{:S(2)}, u32[]{:S(2)}) %collective-permute-start.13) | collective-permute-done | bytes 262176 | tf_op jit(solution)/shard_map/ppermute | solution.py:55
  37.4 0.7 collective-permute-done.14.refs_2_
  38.1 1.8 %shard_map.104.refs_3_.refs_4_ = f32[3,512,512]{2,1,0:T(8,128)S(1)} custom-call(bf16[256,512]{1,0:T(8,128)(2,1)S(1)} %collective-permute-done.6.refs_0_, bf16[256,512]{1,0:T(8,128)(2,1)S(1)} %collective-permute-done.13.refs_1_, bf16[256,512]{1,0:T(8,128)(2,1)S(1)} %collective-permute-done.14.refs_2_, ...), custom_call_target="tpu_custom_call", output_to_operand_aliasing={{}: (7, {})} | custom-call | flops 1610612736 | bytes 10485760 | tf_op jit(solution)/shard_map/pallas_call | solution.py:178
  40.0 3.0 %collective-permute-done.12.refs_1_ = bf16[256,512]{1,0:T(8,128)(2,1)S(1)} collective-permute-done((bf16[256,512]{1,0:T(8,128)(2,1)S(1)}, bf16[256,512]{1,0:T(8,128)(2,1)S(1)}, u32[]{:S(2)}, u32[]{:S(2)}) %collective-permute-start.12) | collective-permute-done | bytes 262176 | tf_op jit(solution)/shard_map/ppermute | solution.py:55
  43.0 0.7 collective-permute-done.10.refs_0_
  43.7 0.9 shard_map.106
  44.6 4.9 %collective-permute-start.15 = (bf16[2,512,512]{2,1,0:T(8,128)(2,1)S(1)}, bf16[2,512,512]{2,1,0:T(8,128)(2,1)S(1)}, u32[]{:S(2)}, u32[]{:S(2)}) collective-permute-start(bf16[2,512,512]{2,1,0:T(8,128)(2,1)S(1)} %get-tuple-element.71.kv_ref), channel_id=1, source_target_pairs={{0,8},{8,16},{16,24},{1,9},{9,17},{17,25},{2,10},{10,18},{18,26},{... | collective-permute-start | bytes 3145736 | tf_op jit(solution)/shard_map/ppermute | solution.py:541
  49.6 1.4 %shard_map.109.rest_0_ = f32[2,3,128,256]{3,2,1,0:T(8,128)S(1)} custom-call(bf16[2,512,512]{2,1,0:T(8,128)(2,1)S(1)} %get-tuple-element.71.kv_ref, f32[4,512]{1,0:T(4,128)S(1)} %bitcast.2, f32[4,128,256]{2,1,0:T(8,128)S(1)} %copy-done.1, f32[4,128,256]{2,1,0:T(8,128)S(1)} %copy-done.2, f32[4,256,128]{2,1,0:T(8,128)S(1)} %copy-done.3), custom_call_target="tpu_custom_call" | custom-call | flops 402653184 | bytes 1572864 | tf_op jit(solution)/shard_map/pallas_call | solution.py:239
  51.1 0.4 collective-permute-done.16.kv_ref
  51.5 1.4 %shard_map.110 = (f32[2,3,128,256]{3,2,1,0:T(8,128)S(1)}, bf16[2,3,128,256]{3,2,1,0:T(8,128)(2,1)S(1)}) custom-call(bf16[2,512,256]{2,1,0:T(8,128)(2,1)S(1)} %collective-permute-done.16.kv_ref, f32[4,512]{1,0:T(4,128)S(1)} %collective-permute-done.5.rate_ref, f32[4,128,256]{2,1,0:T(8,128)S(1)} %copy-done.1, f32[4,128,256]{2,1,0:T(8,128)S(1)} %copy-done.2, ...), custom_call_target="tpu_custom_call" | custom-call | flops 402653184 | bytes 1572864 | tf_op jit(solution)/shard_map/pallas_call | solution.py:239
  52.9 1.1 collective-permute-start.17
  54.0 0.4 shard_map.105.q_ref
  54.5 2.1 %shard_map.107 = (f32[512,512]{1,0:T(8,128)S(1)}, f32[512,8]{1,0:T(8,128)S(1)}) custom-call(bf16[1,512,512]{2,1,0:T(8,128)(2,1)S(1)} %shard_map.105.q_ref, bf16[2,512,512]{2,1,0:T(8,128)(2,1)S(1)} %get-tuple-element.71.kv_ref), custom_call_target="tpu_custom_call" | custom-call | flops 402653184 | bytes 2097152 | tf_op jit(solution)/shard_map/pallas_call | solution.py:337
  56.6 8.9 %collective-permute-done.15.behind_ref = bf16[2,512,512]{2,1,0:T(8,128)(2,1)S(1)} collective-permute-done((bf16[2,512,512]{2,1,0:T(8,128)(2,1)S(1)}, bf16[2,512,512]{2,1,0:T(8,128)(2,1)S(1)}, u32[]{:S(2)}, u32[]{:S(2)}) %collective-permute-start.15) | collective-permute-done | bytes 1048608 | tf_op jit(solution)/shard_map/ppermute | solution.py:541
  65.4 4.6 %shard_map.108.rest_1_.attended_ref = f32[512,512]{1,0:T(8,128)S(1)} custom-call(f32[512,512]{1,0:T(8,128)S(1)} %get-tuple-element.72.sum_ref, f32[512,8]{1,0:T(8,128)S(1)} %get-tuple-element.73.stats_ref, bf16[1,512,512]{2,1,0:T(8,128)(2,1)S(1)} %shard_map.105.q_ref, bf16[2,512,512]{2,1,0:T(8,128)(2,1)S(1)} %collective-permute-done.15.behind_ref), custom_call_target="tpu_custom_call" | custom-call | flops 402653184 | bytes 2097152 | tf_op jit(solution)/shard_map/pallas_call | solution.py:375
  70.1 0.8 shard_map.111.net_ref
  71.0 0.8 shard_map.112.near_ref
  71.8 0.9 collective-permute-done.18.net_ref
  72.8 1.2 %shard_map.113 = (bf16[64,2048]{1,0:T(8,128)(2,1)S(1)}, bf16[64,2048]{1,0:T(8,128)(2,1)S(1)}) custom-call(bf16[1,512,512]{2,1,0:T(8,128)(2,1)S(1)} %shard_map.105.q_ref, f32[512,512]{1,0:T(8,128)S(1)} %shard_map.108.rest_1_.attended_ref, bf16[2,3,128,256]{3,2,1,0:T(8,128)(2,1)S(1)} %collective-permute-done.18.net_ref, ...), custom_call_target="tpu_custom_call" | custom-call | flops 268435456 | bytes 4718592 | tf_op jit(solution)/shard_map/pallas_call | solution.py:450
  74.0 1.4 %collective-permute-start.20 = (bf16[64,2048]{1,0:T(8,128)(2,1)S(1)}, bf16[64,2048]{1,0:T(8,128)(2,1)S(1)}, u32[]{:S(2)}, u32[]{:S(2)}) collective-permute-start(bf16[64,2048]{1,0:T(8,128)(2,1)S(1)} %get-tuple-element.78), channel_id=1, source_target_pairs={{0,1},{2,0},{4,2},{6,4},{7,6},{5,7},{3,5},{1,3},{8,9},{10,8},{12,1... | collective-permute-start | bytes 786440 | tf_op jit(solution)/shard_map/ppermute | solution.py:55
  75.5 1.2 %shard_map.115 = (bf16[64,2048]{1,0:T(8,128)(2,1)S(1)}, bf16[64,2048]{1,0:T(8,128)(2,1)S(1)}, bf16[64,2048]{1,0:T(8,128)(2,1)S(1)}, bf16[64,2048]{1,0:T(8,128)(2,1)S(1)}) custom-call(bf16[1,512,512]{2,1,0:T(8,128)(2,1)S(1)} %shard_map.105.q_ref, f32[512,512]{1,0:T(8,128)S(1)} %shard_map.108.rest_1_.attended_ref, ...), custom_call_target="tpu_custom_call" | custom-call | flops 536870912 | bytes 5242880 | tf_op jit(solution)/shard_map/pallas_call | solution.py:450
  76.8 1.4 %collective-permute-start.22 = (bf16[64,2048]{1,0:T(8,128)(2,1)S(1)}, bf16[64,2048]{1,0:T(8,128)(2,1)S(1)}, u32[]{:S(2)}, u32[]{:S(2)}) collective-permute-start(bf16[64,2048]{1,0:T(8,128)(2,1)S(1)} %get-tuple-element.87), channel_id=1, source_target_pairs={{0,1},{2,0},{4,2},{6,4},{7,6},{5,7},{3,5},{1,3},{8,9},{10,8},{12,1... | collective-permute-start | bytes 786440 | tf_op jit(solution)/shard_map/ppermute | solution.py:55
  78.3 3.5 %collective-permute-done.20.refs_1_ = bf16[64,2048]{1,0:T(8,128)(2,1)S(1)} collective-permute-done((bf16[64,2048]{1,0:T(8,128)(2,1)S(1)}, bf16[64,2048]{1,0:T(8,128)(2,1)S(1)}, u32[]{:S(2)}, u32[]{:S(2)}) %collective-permute-start.20) | collective-permute-done | bytes 262176 | tf_op jit(solution)/shard_map/ppermute | solution.py:55
  81.9 0.9 collective-permute-done.19.refs_0_
  82.9 1.3 %collective-permute-start.26 = (bf16[64,2048]{1,0:T(8,128)(2,1)S(1)}, bf16[64,2048]{1,0:T(8,128)(2,1)S(1)}, u32[]{:S(2)}, u32[]{:S(2)}) collective-permute-start(bf16[64,2048]{1,0:T(8,128)(2,1)S(1)} %add_convert_fusion.8), channel_id=1, source_target_pairs={{0,1},{2,0},{4,2},{6,4},{7,6},{5,7},{3,5},{1,3},{8,9},{10,8},{12,1... | collective-permute-start | bytes 786440 | tf_op jit(solution)/shard_map/ppermute | solution.py:55
  84.4 2.1 %shard_map.114 = (bf16[64,2048]{1,0:T(8,128)(2,1)S(1)}, bf16[64,2048]{1,0:T(8,128)(2,1)S(1)}, bf16[64,2048]{1,0:T(8,128)(2,1)S(1)}, bf16[64,2048]{1,0:T(8,128)(2...) custom-call(bf16[1,512,512]{2,1,0:T(8,128)(2,1)S(1)} %shard_map.105., ...), custom_call_target="tpu_custom_call" | custom-call | flops 1342177280 | bytes 6815744 | tf_op jit(solution)/shard_map/pallas_call | solution.py:450
  86.5 0.9 collective-permute-done.22
  87.5 0.9 collective-permute-done.21
  88.5 1.3 %collective-permute-start.24 = (bf16[64,2048]{1,0:T(8,128)(2,1)S(1)}, bf16[64,2048]{1,0:T(8,128)(2,1)S(1)}, u32[]{:S(2)}, u32[]{:S(2)}) collective-permute-start(bf16[64,2048]{1,0:T(8,128)(2,1)S(1)} %add_convert_fusion.10), channel_id=1, source_target_pairs={{0,1},{2,0},{4,2},{6,4},{7,6},{5,7},{3,5},{1,3},{8,9},{10,8},{12,1... | collective-permute-start | bytes 786440 | tf_op jit(solution)/shard_map/ppermute | solution.py:55
  90.0 3.0 %collective-permute-done.26 = bf16[64,2048]{1,0:T(8,128)(2,1)S(1)} collective-permute-done((bf16[64,2048]{1,0:T(8,128)(2,1)S(1)}, bf16[64,2048]{1,0:T(8,128)(2,1)S(1)}, u32[]{:S(2)}, u32[]{:S(2)}) %collective-permute-start.26) | collective-permute-done | bytes 262176 | tf_op jit(solution)/shard_map/ppermute | solution.py:55
  93.1 0.9 collective-permute-done.25
  94.1 1.3 %collective-permute-start.30 = (bf16[64,2048]{1,0:T(8,128)(2,1)S(1)}, bf16[64,2048]{1,0:T(8,128)(2,1)S(1)}, u32[]{:S(2)}, u32[]{:S(2)}) collective-permute-start(bf16[64,2048]{1,0:T(8,128)(2,1)S(1)} %add_convert_fusion.4), channel_id=1, source_target_pairs={{0,1},{2,0},{4,2},{6,4},{7,6},{5,7},{3,5},{1,3},{8,9},{10,8},{12,1... | collective-permute-start | bytes 786440 | tf_op jit(solution)/shard_map/ppermute | solution.py:55
  95.6 3.0 %collective-permute-done.24 = bf16[64,2048]{1,0:T(8,128)(2,1)S(1)} collective-permute-done((bf16[64,2048]{1,0:T(8,128)(2,1)S(1)}, bf16[64,2048]{1,0:T(8,128)(2,1)S(1)}, u32[]{:S(2)}, u32[]{:S(2)}) %collective-permute-start.24) | collective-permute-done | bytes 262176 | tf_op jit(solution)/shard_map/ppermute | solution.py:55
  98.7 0.9 collective-permute-done.23
  99.7 0.2 collective-permute-start.27
  99.9 1.3 %collective-permute-start.28 = (bf16[64,2048]{1,0:T(8,128)(2,1)S(1)}, bf16[64,2048]{1,0:T(8,128)(2,1)S(1)}, u32[]{:S(2)}, u32[]{:S(2)}) collective-permute-start(bf16[64,2048]{1,0:T(8,128)(2,1)S(1)} %add_convert_fusion.6), channel_id=1, source_target_pairs={{0,1},{2,0},{4,2},{6,4},{7,6},{5,7},{3,5},{1,3},{8,9},{10,8},{12,1... | collective-permute-start | bytes 786440 | tf_op jit(solution)/shard_map/ppermute | solution.py:55
  101.2 3.1 %collective-permute-done.30 = bf16[64,2048]{1,0:T(8,128)(2,1)S(1)} collective-permute-done((bf16[64,2048]{1,0:T(8,128)(2,1)S(1)}, bf16[64,2048]{1,0:T(8,128)(2,1)S(1)}, u32[]{:S(2)}, u32[]{:S(2)}) %collective-permute-start.30) | collective-permute-done | bytes 262176 | tf_op jit(solution)/shard_map/ppermute | solution.py:55
  104.4 0.9 collective-permute-done.29
  105.3 0.2 collective-permute-start.31
  105.6 1.3 %collective-permute-start.32 = (bf16[64,2048]{1,0:T(8,128)(2,1)S(1)}, bf16[64,2048]{1,0:T(8,128)(2,1)S(1)}, u32[]{:S(2)}, u32[]{:S(2)}) collective-permute-start(bf16[64,2048]{1,0:T(8,128)(2,1)S(1)} %add_convert_fusion.2), channel_id=1, source_target_pairs={{0,1},{2,0},{4,2},{6,4},{7,6},{5,7},{3,5},{1,3},{8,9},{10,8},{12,1... | collective-permute-start | bytes 786440 | tf_op jit(solution)/shard_map/ppermute | solution.py:55
  106.9 4.0 %collective-permute-done.27.refs_2_ = bf16[64,2048]{1,0:T(8,128)(2,1)S(1)} collective-permute-done((bf16[64,2048]{1,0:T(8,128)(2,1)S(1)}, bf16[64,2048]{1,0:T(8,128)(2,1)S(1)}, u32[]{:S(2)}, u32[]{:S(2)}) %collective-permute-start.27) | collective-permute-done | bytes 262176 | tf_op jit(solution)/shard_map/ppermute | solution.py:55
  111.0 5.5 %collective-permute-done.31 = bf16[64,2048]{1,0:T(8,128)(2,1)S(1)} collective-permute-done((bf16[64,2048]{1,0:T(8,128)(2,1)S(1)}, bf16[64,2048]{1,0:T(8,128)(2,1)S(1)}, u32[]{:S(2)}, u32[]{:S(2)}) %collective-permute-start.31) | collective-permute-done | bytes 262176 | tf_op jit(solution)/shard_map/ppermute | solution.py:55
  116.6 0.8 pad_maximum_fusion
  (44 shorter events, 2.6 us)
Async XLA Ops:
  1.1 8.5 %collective-permute-start.4 = (bf16[256,512]{1,0:T(8,128)(2,1)S(1)}, bf16[256,512]{1,0:T(8,128)(2,1)S(1)}, u32[]{:S(2)}, u32[]{:S(2)}) collective-permute-start(bf16[256,512]{1,0:T(8,128)(2,1)S(1)} %get-tuple-element.59.refs_3_), channel_id=1, source_target_pairs={{0,1},{2,0},{4,2},{6,4},{7,6},{5,7},{3,5},{1,3},{8,9},{10,8},{12,1... | collective-permute-start | bytes 786440 | tf_op jit(solution)/shard_map/ppermute | solution.py:55
  3.1 8.0 %copy-start.4 = (f32[512,4]{0,1:T(4,128)S(1)}, f32[512,4]{0,1:T(4,128)}, u32[]{:S(2)}) copy-start(f32[512,4]{0,1:T(4,128)} %param.18) | copy-start | bytes 24580
  3.1 7.8 %collective-permute-start = (bf16[256,512]{1,0:T(8,128)(2,1)S(1)}, bf16[256,512]{1,0:T(8,128)(2,1)S(1)}, u32[]{:S(2)}, u32[]{:S(2)}) collective-permute-start(bf16[256,512]{1,0:T(8,128)(2,1)S(1)} %get-tuple-element.56.refs_0_), channel_id=1, source_target_pairs={{0,2},{2,4},{4,6},{6,7},{7,5},{5,3},{3,1},{1,0},{8,10},{10,12},{12... | collective-permute-start | bytes 786440 | tf_op jit(solution)/shard_map/ppermute | solution.py:55
  3.3 11.6 %collective-permute-start.2 = (bf16[256,512]{1,0:T(8,128)(2,1)S(1)}, bf16[256,512]{1,0:T(8,128)(2,1)S(1)}, u32[]{:S(2)}, u32[]{:S(2)}) collective-permute-start(bf16[256,512]{1,0:T(8,128)(2,1)S(1)} %get-tuple-element.56.refs_0_), channel_id=1, source_target_pairs={{0,1},{2,0},{4,2},{6,4},{7,6},{5,7},{3,5},{1,3},{8,9},{10,8},{12,1... | collective-permute-start | bytes 786440 | tf_op jit(solution)/shard_map/ppermute | solution.py:55
  4.6 11.3 %collective-permute-start.3 = (bf16[256,512]{1,0:T(8,128)(2,1)S(1)}, bf16[256,512]{1,0:T(8,128)(2,1)S(1)}, u32[]{:S(2)}, u32[]{:S(2)}) collective-permute-start(bf16[256,512]{1,0:T(8,128)(2,1)S(1)} %get-tuple-element.59.refs_3_), channel_id=1, source_target_pairs={{0,2},{2,4},{4,6},{6,7},{7,5},{5,3},{3,1},{1,0},{8,10},{10,12},{12... | collective-permute-start | bytes 786440 | tf_op jit(solution)/shard_map/ppermute | solution.py:55
  9.6 10.9 %collective-permute-start.9 = (bf16[256,512]{1,0:T(8,128)(2,1)S(1)}, bf16[256,512]{1,0:T(8,128)(2,1)S(1)}, u32[]{:S(2)}, u32[]{:S(2)}) collective-permute-start(bf16[256,512]{1,0:T(8,128)(2,1)S(1)} %collective-permute-done.4.refs_5_), channel_id=1, source_target_pairs={{0,1},{2,0},{4,2},{6,4},{7,6},{5,7},{3,5},{1,3},{8,9},{10,8},{12,1... | collective-permute-start | bytes 786440 | tf_op jit(solution)/shard_map/ppermute | solution.py:55
  10.9 10.6 %collective-permute-start.1 = (bf16[256,512]{1,0:T(8,128)(2,1)S(1)}, bf16[256,512]{1,0:T(8,128)(2,1)S(1)}, u32[]{:S(2)}, u32[]{:S(2)}) collective-permute-start(bf16[256,512]{1,0:T(8,128)(2,1)S(1)} %collective-permute-done.refs_1_), channel_id=1, source_target_pairs={{0,2},{2,4},{4,6},{6,7},{7,5},{5,3},{3,1},{1,0},{8,10},{10,12},{12... | collective-permute-start | bytes 786440 | tf_op jit(solution)/shard_map/ppermute | solution.py:55
  11.1 7.9 %collective-permute-start.5 = (f32[4,512]{1,0:T(4,128)S(1)}, f32[4,512]{1,0:T(4,128)S(1)}, u32[]{:S(2)}, u32[]{:S(2)}) collective-permute-start(f32[4,512]{1,0:T(4,128)S(1)} %bitcast.1), channel_id=1, source_target_pairs={{0,8},{8,0},{16,24},{24,16},{1,9},{9,1},{17,25},{25,17},{2,10},{10... | collective-permute-start | bytes 24584 | tf_op jit(solution)/shard_map/ppermute | solution.py:510
  14.9 11.2 %collective-permute-start.7 = (bf16[256,512]{1,0:T(8,128)(2,1)S(1)}, bf16[256,512]{1,0:T(8,128)(2,1)S(1)}, u32[]{:S(2)}, u32[]{:S(2)}) collective-permute-start(bf16[256,512]{1,0:T(8,128)(2,1)S(1)} %collective-permute-done.2.refs_2_), channel_id=1, source_target_pairs={{0,1},{2,0},{4,2},{6,4},{7,6},{5,7},{3,5},{1,3},{8,9},{10,8},{12,1... | collective-permute-start | bytes 786440 | tf_op jit(solution)/shard_map/ppermute | solution.py:55
  15.9 10.9 %collective-permute-start.8 = (bf16[256,512]{1,0:T(8,128)(2,1)S(1)}, bf16[256,512]{1,0:T(8,128)(2,1)S(1)}, u32[]{:S(2)}, u32[]{:S(2)}) collective-permute-start(bf16[256,512]{1,0:T(8,128)(2,1)S(1)} %collective-permute-done.3.refs_4_), channel_id=1, source_target_pairs={{0,2},{2,4},{4,6},{6,7},{7,5},{5,3},{3,1},{1,0},{8,10},{10,12},{12... | collective-permute-start | bytes 786440 | tf_op jit(solution)/shard_map/ppermute | solution.py:55
  20.5 11.2 %collective-permute-start.11 = (bf16[256,512]{1,0:T(8,128)(2,1)S(1)}, bf16[256,512]{1,0:T(8,128)(2,1)S(1)}, u32[]{:S(2)}, u32[]{:S(2)}) collective-permute-start(bf16[256,512]{1,0:T(8,128)(2,1)S(1)} %collective-permute-done.9.refs_3_), channel_id=1, source_target_pairs={{0,1},{2,0},{4,2},{6,4},{7,6},{5,7},{3,5},{1,3},{8,9},{10,8},{12,1... | collective-permute-start | bytes 786440 | tf_op jit(solution)/shard_map/ppermute | solution.py:55
  21.6 10.9 %collective-permute-start.6 = (bf16[256,512]{1,0:T(8,128)(2,1)S(1)}, bf16[256,512]{1,0:T(8,128)(2,1)S(1)}, u32[]{:S(2)}, u32[]{:S(2)}) collective-permute-start(bf16[256,512]{1,0:T(8,128)(2,1)S(1)} %collective-permute-done.1.refs_0_), channel_id=1, source_target_pairs={{0,2},{2,4},{4,6},{6,7},{7,5},{5,3},{3,1},{1,0},{8,10},{10,12},{12... | collective-permute-start | bytes 786440 | tf_op jit(solution)/shard_map/ppermute | solution.py:55
  26.9 10.5 %collective-permute-start.13 = (bf16[256,512]{1,0:T(8,128)(2,1)S(1)}, bf16[256,512]{1,0:T(8,128)(2,1)S(1)}, u32[]{:S(2)}, u32[]{:S(2)}) collective-permute-start(bf16[256,512]{1,0:T(8,128)(2,1)S(1)} %collective-permute-done.7.refs_1_), channel_id=1, source_target_pairs={{0,1},{2,0},{4,2},{6,4},{7,6},{5,7},{3,5},{1,3},{8,9},{10,8},{12,1... | collective-permute-start | bytes 786440 | tf_op jit(solution)/shard_map/ppermute | solution.py:55
  28.2 9.9 %collective-permute-start.14 = (bf16[256,512]{1,0:T(8,128)(2,1)S(1)}, bf16[256,512]{1,0:T(8,128)(2,1)S(1)}, u32[]{:S(2)}, u32[]{:S(2)}) collective-permute-start(bf16[256,512]{1,0:T(8,128)(2,1)S(1)} %collective-permute-done.8.refs_2_), channel_id=1, source_target_pairs={{0,2},{2,4},{4,6},{6,7},{7,5},{5,3},{3,1},{1,0},{8,10},{10,12},{12... | collective-permute-start | bytes 786440 | tf_op jit(solution)/shard_map/ppermute | solution.py:55
  32.5 10.5 %collective-permute-start.12 = (bf16[256,512]{1,0:T(8,128)(2,1)S(1)}, bf16[256,512]{1,0:T(8,128)(2,1)S(1)}, u32[]{:S(2)}, u32[]{:S(2)}) collective-permute-start(bf16[256,512]{1,0:T(8,128)(2,1)S(1)} %collective-permute-done.11.refs_3_), channel_id=1, source_target_pairs={{0,1},{2,0},{4,2},{6,4},{7,6},{5,7},{3,5},{1,3},{8,9},{10,8},{12,1... | collective-permute-start | bytes 786440 | tf_op jit(solution)/shard_map/ppermute | solution.py:55
  33.8 9.9 %collective-permute-start.10 = (bf16[256,512]{1,0:T(8,128)(2,1)S(1)}, bf16[256,512]{1,0:T(8,128)(2,1)S(1)}, u32[]{:S(2)}, u32[]{:S(2)}) collective-permute-start(bf16[256,512]{1,0:T(8,128)(2,1)S(1)} %collective-permute-done.6.refs_0_), channel_id=1, source_target_pairs={{0,2},{2,4},{4,6},{6,7},{7,5},{5,3},{3,1},{1,0},{8,10},{10,12},{12... | collective-permute-start | bytes 786440 | tf_op jit(solution)/shard_map/ppermute | solution.py:55
  39.9 9.6 %copy-start.1 = (f32[4,128,256]{2,1,0:T(8,128)S(1)}, f32[4,128,256]{2,1,0:T(8,128)}, u32[]{:S(2)}) copy-start(f32[4,128,256]{2,1,0:T(8,128)} %gate_ref.5) | copy-start | bytes 1572868
  40.0 9.6 %copy-start.2 = (f32[4,128,256]{2,1,0:T(8,128)S(1)}, f32[4,128,256]{2,1,0:T(8,128)}, u32[]{:S(2)}) copy-start(f32[4,128,256]{2,1,0:T(8,128)} %up_ref.5) | copy-start | bytes 1572868
  40.0 9.6 %copy-start.3 = (f32[4,256,128]{2,1,0:T(8,128)S(1)}, f32[4,256,128]{2,1,0:T(8,128)}, u32[]{:S(2)}) copy-start(f32[4,256,128]{2,1,0:T(8,128)} %down_ref.5) | copy-start | bytes 1572868
  44.6 20.8 %collective-permute-start.15 = (bf16[2,512,512]{2,1,0:T(8,128)(2,1)S(1)}, bf16[2,512,512]{2,1,0:T(8,128)(2,1)S(1)}, u32[]{:S(2)}, u32[]{:S(2)}) collective-permute-start(bf16[2,512,512]{2,1,0:T(8,128)(2,1)S(1)} %get-tuple-element.71.kv_ref), channel_id=1, source_target_pairs={{0,8},{8,16},{16,24},{1,9},{9,17},{17,25},{2,10},{10,18},{18,26},{... | collective-permute-start | bytes 3145736 | tf_op jit(solution)/shard_map/ppermute | solution.py:541
  49.5 2.0 %collective-permute-start.16 = (bf16[2,512,256]{2,1,0:T(8,128)(2,1)S(1)}, bf16[2,512,256]{2,1,0:T(8,128)(2,1)S(1)}, u32[]{:S(2)}, u32[]{:S(2)}) collective-permute-start(bf16[2,512,256]{2,1,0:T(8,128)(2,1)S(1)} %get-tuple-element.74), channel_id=1, source_target_pairs={{0,8},{8,0},{16,24},{24,16},{1,9},{9,1},{17,25},{25,17},{2,10},{10... | collective-permute-start | bytes 1572872 | tf_op jit(solution)/shard_map/ppermute | solution.py:510
  52.9 17.2 %collective-permute-start.17 = (bf16[2,3,128,256]{3,2,1,0:T(8,128)(2,1)S(1)}, bf16[2,3,128,256]{3,2,1,0:T(8,128)(2,1)S(1)}, u32[]{:S(2)}, u32[]{:S(2)}) collective-permute-start(bf16[2,3,128,256]{3,2,1,0:T(8,128)(2,1)S(1)} %get-tuple-element.76), channel_id=1, source_target_pairs={{0,16},{8,24},{16,0},{24,8},{1,17},{9,25},{17,1},{25,9},{2,18},{10... | collective-permute-start | bytes 1179656 | tf_op jit(solution)/shard_map/ppermute | solution.py:510
  54.5 15.7 %copy-start.5 = (f32[4]{0:T(128)S(1)}, f32[4]{0:T(128)}, u32[]{:S(2)}) copy-start(f32[4]{0:T(128)} %step_ref.1) | copy-start | bytes 52
  70.1 2.7 %copy-start = (bf16[512,4096]{1,0:T(8,128)(2,1)S(1)}, bf16[512,4096]{1,0:T(8,128)(2,1)}, u32[]{:S(2)}) copy-start(bf16[512,4096]{1,0:T(8,128)(2,1)} %w_ref.5) | copy-start | bytes 12582916
  71.0 1.8 %collective-permute-start.18 = (bf16[2,3,128,256]{3,2,1,0:T(8,128)(2,1)S(1)}, bf16[2,3,128,256]{3,2,1,0:T(8,128)(2,1)S(1)}, u32[]{:S(2)}, u32[]{:S(2)}) collective-permute-start(bf16[2,3,128,256]{3,2,1,0:T(8,128)(2,1)S(1)} %shard_map.111.net_ref), channel_id=1, source_target_pairs={{0,8},{8,0},{16,24},{24,16},{1,9},{9,1},{17,25},{25,17},{2,10},{10... | collective-permute-start | bytes 1179656 | tf_op jit(solution)/shard_map/ppermute | solution.py:510
  74.0 7.8 %collective-permute-start.20 = (bf16[64,2048]{1,0:T(8,128)(2,1)S(1)}, bf16[64,2048]{1,0:T(8,128)(2,1)S(1)}, u32[]{:S(2)}, u32[]{:S(2)}) collective-permute-start(bf16[64,2048]{1,0:T(8,128)(2,1)S(1)} %get-tuple-element.78), channel_id=1, source_target_pairs={{0,1},{2,0},{4,2},{6,4},{7,6},{5,7},{3,5},{1,3},{8,9},{10,8},{12,1... | collective-permute-start | bytes 786440 | tf_op jit(solution)/shard_map/ppermute | solution.py:55
  75.3 7.4 %collective-permute-start.19 = (bf16[64,2048]{1,0:T(8,128)(2,1)S(1)}, bf16[64,2048]{1,0:T(8,128)(2,1)S(1)}, u32[]{:S(2)}, u32[]{:S(2)}) collective-permute-start(bf16[64,2048]{1,0:T(8,128)(2,1)S(1)} %get-tuple-element.77), channel_id=1, source_target_pairs={{0,2},{2,4},{4,6},{6,7},{7,5},{5,3},{3,1},{1,0},{8,10},{10,12},{12... | collective-permute-start | bytes 786440 | tf_op jit(solution)/shard_map/ppermute | solution.py:55
  76.8 10.7 %collective-permute-start.22 = (bf16[64,2048]{1,0:T(8,128)(2,1)S(1)}, bf16[64,2048]{1,0:T(8,128)(2,1)S(1)}, u32[]{:S(2)}, u32[]{:S(2)}) collective-permute-start(bf16[64,2048]{1,0:T(8,128)(2,1)S(1)} %get-tuple-element.87), channel_id=1, source_target_pairs={{0,1},{2,0},{4,2},{6,4},{7,6},{5,7},{3,5},{1,3},{8,9},{10,8},{12,1... | collective-permute-start | bytes 786440 | tf_op jit(solution)/shard_map/ppermute | solution.py:55
  78.1 10.3 %collective-permute-start.21 = (bf16[64,2048]{1,0:T(8,128)(2,1)S(1)}, bf16[64,2048]{1,0:T(8,128)(2,1)S(1)}, u32[]{:S(2)}, u32[]{:S(2)}) collective-permute-start(bf16[64,2048]{1,0:T(8,128)(2,1)S(1)} %get-tuple-element.85), channel_id=1, source_target_pairs={{0,2},{2,4},{4,6},{6,7},{7,5},{5,3},{3,1},{1,0},{8,10},{10,12},{12... | collective-permute-start | bytes 786440 | tf_op jit(solution)/shard_map/ppermute | solution.py:55
  82.9 10.2 %collective-permute-start.26 = (bf16[64,2048]{1,0:T(8,128)(2,1)S(1)}, bf16[64,2048]{1,0:T(8,128)(2,1)S(1)}, u32[]{:S(2)}, u32[]{:S(2)}) collective-permute-start(bf16[64,2048]{1,0:T(8,128)(2,1)S(1)} %add_convert_fusion.8), channel_id=1, source_target_pairs={{0,1},{2,0},{4,2},{6,4},{7,6},{5,7},{3,5},{1,3},{8,9},{10,8},{12,1... | collective-permute-start | bytes 786440 | tf_op jit(solution)/shard_map/ppermute | solution.py:55
  84.2 9.8 %collective-permute-start.25 = (bf16[64,2048]{1,0:T(8,128)(2,1)S(1)}, bf16[64,2048]{1,0:T(8,128)(2,1)S(1)}, u32[]{:S(2)}, u32[]{:S(2)}) collective-permute-start(bf16[64,2048]{1,0:T(8,128)(2,1)S(1)} %add_convert_fusion.9), channel_id=1, source_target_pairs={{0,2},{2,4},{4,6},{6,7},{7,5},{5,3},{3,1},{1,0},{8,10},{10,12},{12... | collective-permute-start | bytes 786440 | tf_op jit(solution)/shard_map/ppermute | solution.py:55
  88.5 10.2 %collective-permute-start.24 = (bf16[64,2048]{1,0:T(8,128)(2,1)S(1)}, bf16[64,2048]{1,0:T(8,128)(2,1)S(1)}, u32[]{:S(2)}, u32[]{:S(2)}) collective-permute-start(bf16[64,2048]{1,0:T(8,128)(2,1)S(1)} %add_convert_fusion.10), channel_id=1, source_target_pairs={{0,1},{2,0},{4,2},{6,4},{7,6},{5,7},{3,5},{1,3},{8,9},{10,8},{12,1... | collective-permute-start | bytes 786440 | tf_op jit(solution)/shard_map/ppermute | solution.py:55
  89.8 9.8 %collective-permute-start.23 = (bf16[64,2048]{1,0:T(8,128)(2,1)S(1)}, bf16[64,2048]{1,0:T(8,128)(2,1)S(1)}, u32[]{:S(2)}, u32[]{:S(2)}) collective-permute-start(bf16[64,2048]{1,0:T(8,128)(2,1)S(1)} %add_convert_fusion.11), channel_id=1, source_target_pairs={{0,2},{2,4},{4,6},{6,7},{7,5},{5,3},{3,1},{1,0},{8,10},{10,12},{12... | collective-permute-start | bytes 786440 | tf_op jit(solution)/shard_map/ppermute | solution.py:55
  94.1 10.2 %collective-permute-start.30 = (bf16[64,2048]{1,0:T(8,128)(2,1)S(1)}, bf16[64,2048]{1,0:T(8,128)(2,1)S(1)}, u32[]{:S(2)}, u32[]{:S(2)}) collective-permute-start(bf16[64,2048]{1,0:T(8,128)(2,1)S(1)} %add_convert_fusion.4), channel_id=1, source_target_pairs={{0,1},{2,0},{4,2},{6,4},{7,6},{5,7},{3,5},{1,3},{8,9},{10,8},{12,1... | collective-permute-start | bytes 786440 | tf_op jit(solution)/shard_map/ppermute | solution.py:55
  95.4 9.8 %collective-permute-start.29 = (bf16[64,2048]{1,0:T(8,128)(2,1)S(1)}, bf16[64,2048]{1,0:T(8,128)(2,1)S(1)}, u32[]{:S(2)}, u32[]{:S(2)}) collective-permute-start(bf16[64,2048]{1,0:T(8,128)(2,1)S(1)} %add_convert_fusion.5), channel_id=1, source_target_pairs={{0,2},{2,4},{4,6},{6,7},{7,5},{5,3},{3,1},{1,0},{8,10},{10,12},{12... | collective-permute-start | bytes 786440 | tf_op jit(solution)/shard_map/ppermute | solution.py:55
  99.7 11.2 %collective-permute-start.27 = (bf16[64,2048]{1,0:T(8,128)(2,1)S(1)}, bf16[64,2048]{1,0:T(8,128)(2,1)S(1)}, u32[]{:S(2)}, u32[]{:S(2)}) collective-permute-start(bf16[64,2048]{1,0:T(8,128)(2,1)S(1)} %add_convert_fusion.7), channel_id=1, source_target_pairs={{0,2},{2,4},{4,6},{6,7},{7,5},{5,3},{3,1},{1,0},{8,10},{10,12},{12... | collective-permute-start | bytes 786440 | tf_op jit(solution)/shard_map/ppermute | solution.py:55
  99.9 11.0 %collective-permute-start.28 = (bf16[64,2048]{1,0:T(8,128)(2,1)S(1)}, bf16[64,2048]{1,0:T(8,128)(2,1)S(1)}, u32[]{:S(2)}, u32[]{:S(2)}) collective-permute-start(bf16[64,2048]{1,0:T(8,128)(2,1)S(1)} %add_convert_fusion.6), channel_id=1, source_target_pairs={{0,1},{2,0},{4,2},{6,4},{7,6},{5,7},{3,5},{1,3},{8,9},{10,8},{12,1... | collective-permute-start | bytes 786440 | tf_op jit(solution)/shard_map/ppermute | solution.py:55
  105.3 11.2 %collective-permute-start.31 = (bf16[64,2048]{1,0:T(8,128)(2,1)S(1)}, bf16[64,2048]{1,0:T(8,128)(2,1)S(1)}, u32[]{:S(2)}, u32[]{:S(2)}) collective-permute-start(bf16[64,2048]{1,0:T(8,128)(2,1)S(1)} %add_convert_fusion.3), channel_id=1, source_target_pairs={{0,2},{2,4},{4,6},{6,7},{7,5},{5,3},{3,1},{1,0},{8,10},{10,12},{12... | collective-permute-start | bytes 786440 | tf_op jit(solution)/shard_map/ppermute | solution.py:55
  105.6 11.0 %collective-permute-start.32 = (bf16[64,2048]{1,0:T(8,128)(2,1)S(1)}, bf16[64,2048]{1,0:T(8,128)(2,1)S(1)}, u32[]{:S(2)}, u32[]{:S(2)}) collective-permute-start(bf16[64,2048]{1,0:T(8,128)(2,1)S(1)} %add_convert_fusion.2), channel_id=1, source_target_pairs={{0,1},{2,0},{4,2},{6,4},{7,6},{5,7},{3,5},{1,3},{8,9},{10,8},{12,1... | collective-permute-start | bytes 786440 | tf_op jit(solution)/shard_map/ppermute | solution.py:55

commit v6 on v5

--- a/solution.py
+++ b/solution.py
@@ -161,7 +161,7 @@
     def body(*refs):
         piece_refs = refs[: len(pieces)]
         weight_refs = refs[len(pieces) : len(pieces) + parts]
-        out_ref, left = refs[-2 - shared], refs[-1]
+        out_ref, left = refs[-2 - 2 * shared], refs[-1]
         for index, ref in enumerate(piece_refs):
             chunk, piece = divmod(index, span)
             left[chunk * rows : (chunk + 1) * rows, piece * depth : (piece + 1) * depth] = ref[...]
@@ -171,15 +171,20 @@
                 term = term + refs[len(args) - 1][lead + part]
             out_ref[part] = term.astype(dtype)
             if shared:
-                refs[-2][part] = out_ref[part, :, lanes(1 - lax.axis_index("tok") % 2, width // 2)]
+                side = lax.axis_index("tok") % 2
+                refs[-3][part] = out_ref[part, :, lanes(1 - side, width // 2)]
+                refs[-2][part] = out_ref[part, :, lanes(side, width // 2)]
 
     aliased = before is not None and not final
     args = [*pieces, *weights] + ([] if before is None else [before])
     return call(
         body,
         [WHOLE] * len(args),
-        [WHOLE] * (1 + shared),
-        [jax.ShapeDtypeStruct((parts, total, size), dtype) for size in (width, width // 2)[: 1 + shared]],
+        [WHOLE] * (1 + 2 * shared),
+        [
+            jax.ShapeDtypeStruct((parts, total, size), dtype)
+            for size in (width, width // 2, width // 2)[: 1 + 2 * shared]
+        ],
         [pltpu.VMEM((total, span * depth), BF16)],
         vmem=12,
         cost=cost(
@@ -279,20 +284,15 @@
     )(step, kept, fast_gate, fast_up, fast_down, *received, *after)
 
 
-def attend_blocks(query, blocks, earlier=None):
+def attend_blocks(query, blocks):
     factor = query.shape[-1] ** (-0.5) * LOG2E
     scores = []
     for key, _, allowed in blocks:
         part = mm(query, key, ((1,), (1,))) * factor
         scores.append(part if allowed is None else jnp.where(allowed, part, -1e30))
     tops = [jnp.max(part, axis=-1, keepdims=True) for part in scores]
+    top = functools.reduce(jnp.maximum, tops)
     result, total = 0.0, 0.0
-    if earlier is not None:
-        tops.append(earlier[1])
-    top = functools.reduce(jnp.maximum, tops)
-    if earlier is not None:
-        shrink = jnp.exp2(earlier[1] - top)
-        result, total = earlier[0] * shrink, earlier[2] * shrink
     for part, (_, value, _) in zip(scores, blocks):
         weight = jnp.exp2(part - top)
         total = total + jnp.sum(weight, axis=-1, keepdims=True)
@@ -314,36 +314,54 @@
     return blocks
 
 
-def attend_own(query, kv, size):
+def attend_chip(query, kv, beside_near, beside_far, size):
     rows = query.shape[1]
     heads = query.shape[2] // size
     row = (rows // 2, rows // 2)
 
-    def body(q_ref, kv_ref, out_ref, stats_ref):
+    def body(q_ref, kv_ref, near_ref, far_ref, out_ref, stats_ref):
+        place = lax.axis_index("tok")
+        odd = place % 2 == 1
         causal = lax.broadcasted_iota(jnp.int32, row, 1) <= lax.broadcasted_iota(jnp.int32, row, 0)
-        for index, where in enumerate(halves(rows)):
-            stats = []
-            for head in range(heads):
-                lane = slice(head * size, (head + 1) * size)
-                blocks = [
-                    (kv_ref[0, keys, lane], kv_ref[1, keys, lane], causal if at == index else None)
-                    for at, keys in enumerate(halves(rows)[: index + 1])
-                ]
-                result, top, total = attend_blocks(q_ref[0, where, lane], blocks)
-                out_ref[where, lane] = result
-                stats += [top, total]
-            stats_ref[where] = jnp.concatenate(stats, axis=1)
-
-    return call(
-        body,
-        [WHOLE] * 2,
+
+        def one(index, where, head, earlier):
+            lane = slice(head * size, (head + 1) * size)
+            blocks = [
+                (kv_ref[0, keys, lane], kv_ref[1, keys, lane], causal if at == index else None)
+                for at, keys in enumerate(halves(rows)[: index + 1])
+            ]
+            if earlier is not None:
+                half, at = divmod(head, heads // 2)
+                ref = (far_ref, near_ref)[half]
+                blocks += earlier_blocks(ref, index, slice(at * size, (at + 1) * size))
+            return lane, attend_blocks(q_ref[0, where, lane], blocks)
+
+        @pl.when(odd)
+        def _():
+            for index, where in enumerate(halves(rows)):
+                for head in range(heads):
+                    lane, (result, _, total) = one(index, where, head, True)
+                    out_ref[where, lane] = result / total
+
+        @pl.when(jnp.logical_not(odd))
+        def _():
+            for index, where in enumerate(halves(rows)):
+                for head in range(heads):
+                    lane, (result, top, total) = one(index, where, head, None)
+                    out_ref[where, lane] = result / jnp.where(place == 0, total, 1.0)
+                    stats_ref[0, where, lane] = jnp.broadcast_to(top, result.shape)
+                    stats_ref[1, where, lane] = jnp.broadcast_to(total, result.shape)
+
+    return call(
+        body,
+        [WHOLE] * 4,
         [WHOLE] * 2,
         [
             jax.ShapeDtypeStruct((rows, heads * size), F32),
-            jax.ShapeDtypeStruct((rows, 2 * heads), F32),
+            jax.ShapeDtypeStruct((2, rows, heads * size), F32),
         ],
         cost=cost(3 * heads * size * rows * rows, 8 * rows * heads * size, heads * rows * rows),
-    )(query, kv)
+    )(query, kv, beside_near, beside_far)
 
 
 def attend_behind(summed, stats, query, behind, size):
@@ -351,26 +369,21 @@
     heads = query.shape[2] // size
 
     def body(sum_ref, stats_ref, q_ref, behind_ref, out_ref):
-        needed = lax.axis_index("tok") > 0
-
-        @pl.when(needed)
+        place = lax.axis_index("tok")
+
+        @pl.when((place > 0) & (place % 2 == 0))
         def _():
             for index, where in enumerate(halves(rows)):
                 for head in range(heads):
                     lane = slice(head * size, (head + 1) * size)
-                    top, total = (stats_ref[where, 2 * head + at : 2 * head + at + 1] for at in (0, 1))
-                    result, _, total = attend_blocks(
-                        q_ref[0, where, lane],
-                        earlier_blocks(behind_ref, index, lane),
-                        (sum_ref[where, lane], top, total),
+                    result, top, total = attend_blocks(
+                        q_ref[0, where, lane], earlier_blocks(behind_ref, index, lane)
                     )
-                    out_ref[where, lane] = result / total
-
-        @pl.when(jnp.logical_not(needed))
-        def _():
-            for head in range(heads):
-                lane = slice(head * size, (head + 1) * size)
-                out_ref[:, lane] = sum_ref[:, lane] / stats_ref[:, 2 * head + 1 : 2 * head + 2]
+                    before = stats_ref[0, where, lane]
+                    both = jnp.maximum(before, top)
+                    old, new = jnp.exp2(before - both), jnp.exp2(top - both)
+                    total = stats_ref[1, where, lane] * old + total * new
+                    out_ref[where, lane] = (sum_ref[where, lane] * old + result * new) / total
 
     return call(
         body,
@@ -378,6 +391,7 @@
         WHOLE,
         jax.ShapeDtypeStruct(summed.shape, F32),
         cost=cost(3 * heads * size * rows * rows, 8 * rows * heads * size, heads * rows * rows),
+        aliases={0: 0},
     )(summed, stats, query, behind)
 
 
@@ -535,11 +549,12 @@
             known = [chunk[: 2 * step - 1] for chunk in chunks]
             (sums,) = accumulate(known, done, 2 * step - 1, weights, sums)
             done = 2 * step - 1
-    kv, far = accumulate(chunks, done, 2 * steps, weights[:2], sums, shared=True)
+    kv, far, near = accumulate(chunks, done, 2 * steps, weights[:2], sums, shared=True)
     (query,) = accumulate(chunks, done, 2 * steps, weights[2:], sums, 2)
 
-    behind = lax.ppermute(kv, "tok", [(index, index + 1) for index in range(tok_count - 1)])
+    behind = lax.ppermute(kv, "tok", [(index, index + 1) for index in range(1, tok_count - 1, 2)])
     beside = swap(far, 1)
+    beside_far = lax.ppermute(near, "tok", [(index, index + 1) for index in range(0, tok_count, 2)])
     (grads,) = head_grads(kv, rate, *nets)
     grads, travel = head_grads(beside, rate_beside, *nets, grads)
     received = []
@@ -550,7 +565,7 @@
                 travel = travel + more.astype(F32)
             travel = travel.astype(BF16)
         received.append(swap(travel, 1 << bit))
-    summed, stats = attend_own(query, kv, head_size)
+    summed, stats = attend_chip(query, kv, beside, beside_far, head_size)
     attended = attend_behind(summed, stats, query, behind, head_size)
     mine = renew(grads, received, head_step, *nets, (attended,))
     near = combine_near(query, attended, mine)

time: 119 us -> 118 us (level)
  Pallas kernels: 29.3 us -> 26.1 us
  waiting for transfers between devices: 56 us -> 58.4 us
    pallas_call x1, Pallas kernels: 4.63 us -> 0.01 us  [attend_behind(): call(body, [WHOLE] * 4, WHOLE, jax.ShapeDtypeStruct(summed.shape, F32), c...]
    ppermute x4, waiting for transfers between devices: 1.34 us -> 5.13 us  [swap(): lax.ppermute(value, 'tok', [(index, index ^ bit) for index in range(count)])]
    pallas_call x6, Pallas kernels: 9.7 us -> 11.1 us  [the longest x5 7.65 us: accumulate(): call(body, [WHOLE] * len(args), [WHOLE] * (1 + 2 * shared), [jax.ShapeDty...]
    ppermute x1 -> x2, waiting for transfers between devices: 8.89 us -> 7.54 us  [the longest x1 7.54 us: shards(): lax.ppermute(kv, 'tok', [(index, index + 1) for index in range(1, tok_cou...]
    ppermute x1 -> x2, starting transfers between devices: 4.9 us -> 6.24 us  [the longest x1 4.95 us: shards(): lax.ppermute(kv, 'tok', [(index, index + 1) for index in range(1, tok_cou...]
  transfers between devices with their start and end apart: 33 -> 34, of which waited for: 25 -> 25; matrix products, arithmetic and copies ran while one was open for 1% -> 1% of each run, Pallas kernels for 22% -> 19%
where the time goes in v6:
time: 118 us; the launch traced here: 117 us
  waiting for transfers between devices  58.4 us (49%)
  starting transfers between devices  30.5 us (26%)
  Pallas kernels  26.1 us (22%)
  other arithmetic  1.61 us (1%)
    ppermute x28, waiting for transfers between devices, ring_send(): lax.ppermute(value, 'head', [(order[i], order[(i + step) % count]) for i...  45.7 us
    ppermute x28, starting transfers between devices, ring_send(): lax.ppermute(value, 'head', [(order[i], order[(i + step) % count]) for i...  21.7 us
    pallas_call x5, Pallas kernels, accumulate(): call(body, [WHOLE] * len(args), [WHOLE] * (1 + 2 * shared), [jax.ShapeDty...  7.65 us
    ppermute x1, waiting for transfers between devices, shards(): lax.ppermute(kv, 'tok', [(index, index + 1) for index in range(1, tok_cou...  7.54 us
    ppermute x4, waiting for transfers between devices, swap(): lax.ppermute(value, 'tok', [(index, index ^ bit) for index in range(count)])  5.13 us
    ppermute x1, starting transfers between devices, shards(): lax.ppermute(kv, 'tok', [(index, index + 1) for index in range(1, tok_cou...  4.95 us
    pallas_call x1, Pallas kernels, load(): call(body, [IN_HBM] * count, [WHOLE] * count, [jax.ShapeDtypeStruct(array...  4.78 us
    pallas_call x3, Pallas kernels, partial_out(): call(body, [WHOLE] * 5 + [AFTER] * len(after), [WHOLE] * (2 * count), [ja...  4.58 us
  transfers between devices with their start and end apart: 34, of which 25 were waited for; matrix products, arithmetic and copies ran while one was open for 1% of the time, Pallas kernels for 19%

profile of v6, /device:TPU:1, one launch (start us, length us, event | category | flops | bytes accessed | tf_op | source)
XLA Modules:
  0.0 117.0 jit_solution(5442243372511639281)
XLA Ops:
  0.0 1.0 shard_map.100
  1.1 2.1 %collective-permute-start.4 = (bf16[256,512]{1,0:T(8,128)(2,1)S(1)}, bf16[256,512]{1,0:T(8,128)(2,1)S(1)}, u32[]{:S(2)}, u32[]{:S(2)}) collective-permute-start(bf16[256,512]{1,0:T(8,128)(2,1)S(1)} %get-tuple-element.60.refs_3_), channel_id=1, source_target_pairs={{0,1},{2,0},{4,2},{6,4},{7,6},{5,7},{3,5},{1,3},{8,9},{10,8},{12,1... | collective-permute-start | bytes 786440 | tf_op jit(solution)/shard_map/ppermute | solution.py:55
  3.3 1.3 %collective-permute-start.2 = (bf16[256,512]{1,0:T(8,128)(2,1)S(1)}, bf16[256,512]{1,0:T(8,128)(2,1)S(1)}, u32[]{:S(2)}, u32[]{:S(2)}) collective-permute-start(bf16[256,512]{1,0:T(8,128)(2,1)S(1)} %get-tuple-element.57.refs_0_), channel_id=1, source_target_pairs={{0,1},{2,0},{4,2},{6,4},{7,6},{5,7},{3,5},{1,3},{8,9},{10,8},{12,1... | collective-permute-start | bytes 786440 | tf_op jit(solution)/shard_map/ppermute | solution.py:55
  4.8 4.8 %shard_map.101 = (bf16[4096,512]{1,0:T(8,128)(2,1)S(1)}, bf16[4096,512]{1,0:T(8,128)(2,1)S(1)}, bf16[4096,512]{1,0:T(8,128)(2,1)S(1)}) custom-call(bf16[4096,512]{1,0:T(8,128)(2,1)} %refs_0_.1, bf16[4096,512]{1,0:T(8,128)(2,1)} %refs_1_.1, bf16[4096,512]{1,0:T(8,128)(2,1)} %refs_2_.1), custom_call_target="tpu_custom_call" | custom-call | bytes 25165824 | tf_op jit(solution)/shard_map/pallas_call | solution.py:108
  9.6 1.4 %collective-permute-start.9 = (bf16[256,512]{1,0:T(8,128)(2,1)S(1)}, bf16[256,512]{1,0:T(8,128)(2,1)S(1)}, u32[]{:S(2)}, u32[]{:S(2)}) collective-permute-start(bf16[256,512]{1,0:T(8,128)(2,1)S(1)} %collective-permute-done.4.refs_5_), channel_id=1, source_target_pairs={{0,1},{2,0},{4,2},{6,4},{7,6},{5,7},{3,5},{1,3},{8,9},{10,8},{12,1... | collective-permute-start | bytes 786440 | tf_op jit(solution)/shard_map/ppermute | solution.py:55
  11.1 2.4 %collective-permute-start.5 = (f32[4,512]{1,0:T(4,128)S(1)}, f32[4,512]{1,0:T(4,128)S(1)}, u32[]{:S(2)}, u32[]{:S(2)}) collective-permute-start(f32[4,512]{1,0:T(4,128)S(1)} %bitcast.1), channel_id=1, source_target_pairs={{0,8},{8,0},{16,24},{24,16},{1,9},{9,1},{17,25},{25,17},{2,10},{10... | collective-permute-start | bytes 24584 | tf_op jit(solution)/shard_map/ppermute | solution.py:524
  13.5 1.4 %collective-permute-done.2.refs_2_ = bf16[256,512]{1,0:T(8,128)(2,1)S(1)} collective-permute-done((bf16[256,512]{1,0:T(8,128)(2,1)S(1)}, bf16[256,512]{1,0:T(8,128)(2,1)S(1)}, u32[]{:S(2)}, u32[]{:S(2)}) %collective-permute-start.2) | collective-permute-done | bytes 262176 | tf_op jit(solution)/shard_map/ppermute | solution.py:55
  14.9 1.1 collective-permute-start.7
  15.9 0.4 collective-permute-start.8
  16.4 2.6 %shard_map.102.refs_7_ = f32[3,512,512]{2,1,0:T(8,128)S(1)} custom-call(bf16[256,512]{1,0:T(8,128)(2,1)S(1)} %get-tuple-element.57.refs_0_, bf16[256,512]{1,0:T(8,128)(2,1)S(1)} %collective-permute-done.refs_1_, bf16[256,512]{1,0:T(8,128)(2,1)S(1)} %collective-permute-done.2.refs_2_, bf16[256,512]{1,0:T(8,128)(2,1)S(1)} %get-tuple-element.60.refs_3_, ...), custom_call_target="tpu_custom_call" | custom-call | flops 2415919104 | bytes 12582912 | tf_op jit(solution)/shard_map/pallas_call | solution.py:180
  19.0 1.5 %collective-permute-done.9.refs_3_ = bf16[256,512]{1,0:T(8,128)(2,1)S(1)} collective-permute-done((bf16[256,512]{1,0:T(8,128)(2,1)S(1)}, bf16[256,512]{1,0:T(8,128)(2,1)S(1)}, u32[]{:S(2)}, u32[]{:S(2)}) %collective-permute-start.9) | collective-permute-done | bytes 262176 | tf_op jit(solution)/shard_map/ppermute | solution.py:55
  20.5 1.1 collective-permute-start.11
  21.6 0.4 collective-permute-start.6
  22.0 4.1 %collective-permute-done.7.refs_1_ = bf16[256,512]{1,0:T(8,128)(2,1)S(1)} collective-permute-done((bf16[256,512]{1,0:T(8,128)(2,1)S(1)}, bf16[256,512]{1,0:T(8,128)(2,1)S(1)}, u32[]{:S(2)}, u32[]{:S(2)}) %collective-permute-start.7) | collective-permute-done | bytes 262176 | tf_op jit(solution)/shard_map/ppermute | solution.py:55
  26.1 0.7 collective-permute-done.8.refs_2_
  26.9 1.3 %collective-permute-start.13 = (bf16[256,512]{1,0:T(8,128)(2,1)S(1)}, bf16[256,512]{1,0:T(8,128)(2,1)S(1)}, u32[]{:S(2)}, u32[]{:S(2)}) collective-permute-start(bf16[256,512]{1,0:T(8,128)(2,1)S(1)} %collective-permute-done.7.refs_1_), channel_id=1, source_target_pairs={{0,1},{2,0},{4,2},{6,4},{7,6},{5,7},{3,5},{1,3},{8,9},{10,8},{12,1... | collective-permute-start | bytes 786440 | tf_op jit(solution)/shard_map/ppermute | solution.py:55
  28.3 1.8 %shard_map.103.refs_7_ = f32[3,512,512]{2,1,0:T(8,128)S(1)} custom-call(bf16[256,512]{1,0:T(8,128)(2,1)S(1)} %collective-permute-done.1.refs_0_, bf16[256,512]{1,0:T(8,128)(2,1)S(1)} %collective-permute-done.7.refs_1_, bf16[256,512]{1,0:T(8,128)(2,1)S(1)} %collective-permute-done.8.refs_2_, ...), custom_call_target="tpu_custom_call", output_to_operand_aliasing={{}: (7, {})} | custom-call | flops 1610612736 | bytes 10485760 | tf_op jit(solution)/shard_map/pallas_call | solution.py:180
  30.2 1.6 %collective-permute-done.11.refs_3_ = bf16[256,512]{1,0:T(8,128)(2,1)S(1)} collective-permute-done((bf16[256,512]{1,0:T(8,128)(2,1)S(1)}, bf16[256,512]{1,0:T(8,128)(2,1)S(1)}, u32[]{:S(2)}, u32[]{:S(2)}) %collective-permute-start.11) | collective-permute-done | bytes 262176 | tf_op jit(solution)/shard_map/ppermute | solution.py:55
  31.7 0.7 collective-permute-done.6.refs_0_
  32.5 1.3 %collective-permute-start.12 = (bf16[256,512]{1,0:T(8,128)(2,1)S(1)}, bf16[256,512]{1,0:T(8,128)(2,1)S(1)}, u32[]{:S(2)}, u32[]{:S(2)}) collective-permute-start(bf16[256,512]{1,0:T(8,128)(2,1)S(1)} %collective-permute-done.11.refs_3_), channel_id=1, source_target_pairs={{0,1},{2,0},{4,2},{6,4},{7,6},{5,7},{3,5},{1,3},{8,9},{10,8},{12,1... | collective-permute-start | bytes 786440 | tf_op jit(solution)/shard_map/ppermute | solution.py:55
  33.9 3.4 %collective-permute-done.13.refs_1_ = bf16[256,512]{1,0:T(8,128)(2,1)S(1)} collective-permute-done((bf16[256,512]{1,0:T(8,128)(2,1)S(1)}, bf16[256,512]{1,0:T(8,128)(2,1)S(1)}, u32[]{:S(2)}, u32[]{:S(2)}) %collective-permute-start.13) | collective-permute-done | bytes 262176 | tf_op jit(solution)/shard_map/ppermute | solution.py:55
  37.4 0.7 collective-permute-done.14.refs_2_
  38.1 1.8 %shard_map.104.refs_3_.refs_4_ = f32[3,512,512]{2,1,0:T(8,128)S(1)} custom-call(bf16[256,512]{1,0:T(8,128)(2,1)S(1)} %collective-permute-done.6.refs_0_, bf16[256,512]{1,0:T(8,128)(2,1)S(1)} %collective-permute-done.13.refs_1_, bf16[256,512]{1,0:T(8,128)(2,1)S(1)} %collective-permute-done.14.refs_2_, ...), custom_call_target="tpu_custom_call", output_to_operand_aliasing={{}: (7, {})} | custom-call | flops 1610612736 | bytes 10485760 | tf_op jit(solution)/shard_map/pallas_call | solution.py:180
  40.0 3.0 %collective-permute-done.12.refs_1_ = bf16[256,512]{1,0:T(8,128)(2,1)S(1)} collective-permute-done((bf16[256,512]{1,0:T(8,128)(2,1)S(1)}, bf16[256,512]{1,0:T(8,128)(2,1)S(1)}, u32[]{:S(2)}, u32[]{:S(2)}) %collective-permute-start.12) | collective-permute-done | bytes 262176 | tf_op jit(solution)/shard_map/ppermute | solution.py:55
  43.0 0.7 collective-permute-done.10.refs_0_
  43.7 0.9 shard_map.106
  44.6 5.0 %collective-permute-start.17 = (bf16[2,512,512]{2,1,0:T(8,128)(2,1)S(1)}, bf16[2,512,512]{2,1,0:T(8,128)(2,1)S(1)}, u32[]{:S(2)}, u32[]{:S(2)}) collective-permute-start(bf16[2,512,512]{2,1,0:T(8,128)(2,1)S(1)} %get-tuple-element.72.kv_ref), channel_id=1, source_target_pairs={{8,16},{9,17},{10,18},{11,19},{12,20},{13,21},{14,22},{15,23}} | collective-permute-start | bytes 3145736 | tf_op jit(solution)/shard_map/ppermute | solution.py:555
  49.7 1.3 %collective-permute-start.16 = (bf16[2,512,256]{2,1,0:T(8,128)(2,1)S(1)}, bf16[2,512,256]{2,1,0:T(8,128)(2,1)S(1)}, u32[]{:S(2)}, u32[]{:S(2)}) collective-permute-start(bf16[2,512,256]{2,1,0:T(8,128)(2,1)S(1)} %get-tuple-element.74), channel_id=1, source_target_pairs={{0,8},{16,24},{1,9},{17,25},{2,10},{18,26},{3,11},{19,27},{4,12},{... | collective-permute-start | bytes 1572872 | tf_op jit(solution)/shard_map/ppermute | solution.py:557
  51.0 1.4 %shard_map.109.rest_0_ = f32[2,3,128,256]{3,2,1,0:T(8,128)S(1)} custom-call(bf16[2,512,512]{2,1,0:T(8,128)(2,1)S(1)} %get-tuple-element.72.kv_ref, f32[4,512]{1,0:T(4,128)S(1)} %bitcast.2, f32[4,128,256]{2,1,0:T(8,128)S(1)} %copy-done.1, f32[4,128,256]{2,1,0:T(8,128)S(1)} %copy-done.2, f32[4,256,128]{2,1,0:T(8,128)S(1)} %copy-done.3), custom_call_target="tpu_custom_call" | custom-call | flops 402653184 | bytes 1572864 | tf_op jit(solution)/shard_map/pallas_call | solution.py:244
  52.5 1.4 %shard_map.110 = (f32[2,3,128,256]{3,2,1,0:T(8,128)S(1)}, bf16[2,3,128,256]{3,2,1,0:T(8,128)(2,1)S(1)}) custom-call(bf16[2,512,256]{2,1,0:T(8,128)(2,1)S(1)} %collective-permute-done.15.near_ref.kv_ref, f32[4,512]{1,0:T(4,128)S(1)} %collective-permute-done.5.rate_ref, f32[4,128,256]{2,1,0:T(8,128)S(1)} %copy-done.1, f32[4,128,256]{2,1,0:T(8,128)S(1)} %copy-done.2, ...), custom_call_target="tpu_custom_call" | custom-call | flops 402653184 | bytes 1572864 | tf_op jit(solution)/shard_map/pallas_call | solution.py:244
  54.0 0.4 shard_map.105.q_ref
  54.4 3.5 %shard_map.107 = (f32[512,512]{1,0:T(8,128)S(1)}, f32[2,512,512]{2,1,0:T(8,128)S(1)}) custom-call(bf16[1,512,512]{2,1,0:T(8,128)(2,1)S(1)} %shard_map.105.q_ref, bf16[2,512,512]{2,1,0:T(8,128)(2,1)S(1)} %get-tuple-element.72.kv_ref, bf16[2,512,256]{2,1,0:T(8,128)(2,1)S(1)} %collective-permute-done.15.near_ref.kv_ref, ...), custom_call_target="tpu_custom_call" | custom-call | flops 402653184 | bytes 2097152 | tf_op jit(solution)/shard_map/pallas_call | solution.py:355
  57.9 7.5 %collective-permute-done.17.behind_ref = bf16[2,512,512]{2,1,0:T(8,128)(2,1)S(1)} collective-permute-done((bf16[2,512,512]{2,1,0:T(8,128)(2,1)S(1)}, bf16[2,512,512]{2,1,0:T(8,128)(2,1)S(1)}, u32[]{:S(2)}, u32[]{:S(2)}) %collective-permute-start.17) | collective-permute-done | bytes 1048608 | tf_op jit(solution)/shard_map/ppermute | solution.py:555
  65.5 4.2 %collective-permute-done.18.rest_0_ = bf16[2,3,128,256]{3,2,1,0:T(8,128)(2,1)S(1)} collective-permute-done((bf16[2,3,128,256]{3,2,1,0:T(8,128)(2,1)S(1)}, bf16[2,3,128,256]{3,2,1,0:T(8,128)(2,1)S(1)}, u32[]{:S(2)}, u32[]{:S(2)}) %collective-permute-start.18) | collective-permute-done | bytes 393248 | tf_op jit(solution)/shard_map/ppermute | solution.py:524
  69.7 0.8 shard_map.111.net_ref
  70.6 0.8 shard_map.112.near_ref
  71.4 0.9 collective-permute-done.19.net_ref
  72.3 1.2 %shard_map.113 = (bf16[64,2048]{1,0:T(8,128)(2,1)S(1)}, bf16[64,2048]{1,0:T(8,128)(2,1)S(1)}) custom-call(bf16[1,512,512]{2,1,0:T(8,128)(2,1)S(1)} %shard_map.105.q_ref, f32[512,512]{1,0:T(8,128)S(1)} %shard_map.108.rest_1_.attended_ref, bf16[2,3,128,256]{3,2,1,0:T(8,128)(2,1)S(1)} %collective-permute-done.19.net_ref, ...), custom_call_target="tpu_custom_call" | custom-call | flops 268435456 | bytes 4718592 | tf_op jit(solution)/shard_map/pallas_call | solution.py:464
  73.6 1.3 %collective-permute-start.21 = (bf16[64,2048]{1,0:T(8,128)(2,1)S(1)}, bf16[64,2048]{1,0:T(8,128)(2,1)S(1)}, u32[]{:S(2)}, u32[]{:S(2)}) collective-permute-start(bf16[64,2048]{1,0:T(8,128)(2,1)S(1)} %get-tuple-element.80), channel_id=1, source_target_pairs={{0,1},{2,0},{4,2},{6,4},{7,6},{5,7},{3,5},{1,3},{8,9},{10,8},{12,1... | collective-permute-start | bytes 786440 | tf_op jit(solution)/shard_map/ppermute | solution.py:55
  74.9 0.2 collective-permute-start.20
  75.1 1.2 %shard_map.115 = (bf16[64,2048]{1,0:T(8,128)(2,1)S(1)}, bf16[64,2048]{1,0:T(8,128)(2,1)S(1)}, bf16[64,2048]{1,0:T(8,128)(2,1)S(1)}, bf16[64,2048]{1,0:T(8,128)(2,1)S(1)}) custom-call(bf16[1,512,512]{2,1,0:T(8,128)(2,1)S(1)} %shard_map.105.q_ref, f32[512,512]{1,0:T(8,128)S(1)} %shard_map.108.rest_1_.attended_ref, ...), custom_call_target="tpu_custom_call" | custom-call | flops 536870912 | bytes 5242880 | tf_op jit(solution)/shard_map/pallas_call | solution.py:464
  76.3 1.3 %collective-permute-start.23 = (bf16[64,2048]{1,0:T(8,128)(2,1)S(1)}, bf16[64,2048]{1,0:T(8,128)(2,1)S(1)}, u32[]{:S(2)}, u32[]{:S(2)}) collective-permute-start(bf16[64,2048]{1,0:T(8,128)(2,1)S(1)} %get-tuple-element.89), channel_id=1, source_target_pairs={{0,1},{2,0},{4,2},{6,4},{7,6},{5,7},{3,5},{1,3},{8,9},{10,8},{12,1... | collective-permute-start | bytes 786440 | tf_op jit(solution)/shard_map/ppermute | solution.py:55
  77.7 0.2 collective-permute-start.22
  77.9 3.5 %collective-permute-done.21.refs_1_ = bf16[64,2048]{1,0:T(8,128)(2,1)S(1)} collective-permute-done((bf16[64,2048]{1,0:T(8,128)(2,1)S(1)}, bf16[64,2048]{1,0:T(8,128)(2,1)S(1)}, u32[]{:S(2)}, u32[]{:S(2)}) %collective-permute-start.21) | collective-permute-done | bytes 262176 | tf_op jit(solution)/shard_map/ppermute | solution.py:55
  81.5 0.9 collective-permute-done.20.refs_0_
  82.4 1.3 %collective-permute-start.27 = (bf16[64,2048]{1,0:T(8,128)(2,1)S(1)}, bf16[64,2048]{1,0:T(8,128)(2,1)S(1)}, u32[]{:S(2)}, u32[]{:S(2)}) collective-permute-start(bf16[64,2048]{1,0:T(8,128)(2,1)S(1)} %add_convert_fusion.8), channel_id=1, source_target_pairs={{0,1},{2,0},{4,2},{6,4},{7,6},{5,7},{3,5},{1,3},{8,9},{10,8},{12,1... | collective-permute-start | bytes 786440 | tf_op jit(solution)/shard_map/ppermute | solution.py:55
  83.9 2.1 %shard_map.114 = (bf16[64,2048]{1,0:T(8,128)(2,1)S(1)}, bf16[64,2048]{1,0:T(8,128)(2,1)S(1)}, bf16[64,2048]{1,0:T(8,128)(2,1)S(1)}, bf16[64,2048]{1,0:T(8,128)(2...) custom-call(bf16[1,512,512]{2,1,0:T(8,128)(2,1)S(1)} %shard_map.105., ...), custom_call_target="tpu_custom_call" | custom-call | flops 1342177280 | bytes 6815744 | tf_op jit(solution)/shard_map/pallas_call | solution.py:464
  86.1 0.9 collective-permute-done.23
  87.1 0.9 collective-permute-done.22
  88.0 1.3 %collective-permute-start.25 = (bf16[64,2048]{1,0:T(8,128)(2,1)S(1)}, bf16[64,2048]{1,0:T(8,128)(2,1)S(1)}, u32[]{:S(2)}, u32[]{:S(2)}) collective-permute-start(bf16[64,2048]{1,0:T(8,128)(2,1)S(1)} %add_convert_fusion.10), channel_id=1, source_target_pairs={{0,1},{2,0},{4,2},{6,4},{7,6},{5,7},{3,5},{1,3},{8,9},{10,8},{12,1... | collective-permute-start | bytes 786440 | tf_op jit(solution)/shard_map/ppermute | solution.py:55
  89.6 3.1 %collective-permute-done.27 = bf16[64,2048]{1,0:T(8,128)(2,1)S(1)} collective-permute-done((bf16[64,2048]{1,0:T(8,128)(2,1)S(1)}, bf16[64,2048]{1,0:T(8,128)(2,1)S(1)}, u32[]{:S(2)}, u32[]{:S(2)}) %collective-permute-start.27) | collective-permute-done | bytes 262176 | tf_op jit(solution)/shard_map/ppermute | solution.py:55
  92.7 0.9 collective-permute-done.26
  93.7 1.3 %collective-permute-start.31 = (bf16[64,2048]{1,0:T(8,128)(2,1)S(1)}, bf16[64,2048]{1,0:T(8,128)(2,1)S(1)}, u32[]{:S(2)}, u32[]{:S(2)}) collective-permute-start(bf16[64,2048]{1,0:T(8,128)(2,1)S(1)} %add_convert_fusion.4), channel_id=1, source_target_pairs={{0,1},{2,0},{4,2},{6,4},{7,6},{5,7},{3,5},{1,3},{8,9},{10,8},{12,1... | collective-permute-start | bytes 786440 | tf_op jit(solution)/shard_map/ppermute | solution.py:55
  95.2 3.1 %collective-permute-done.25 = bf16[64,2048]{1,0:T(8,128)(2,1)S(1)} collective-permute-done((bf16[64,2048]{1,0:T(8,128)(2,1)S(1)}, bf16[64,2048]{1,0:T(8,128)(2,1)S(1)}, u32[]{:S(2)}, u32[]{:S(2)}) %collective-permute-start.25) | collective-permute-done | bytes 262176 | tf_op jit(solution)/shard_map/ppermute | solution.py:55
  98.3 0.9 collective-permute-done.24
  99.3 0.2 collective-permute-start.28
  99.5 1.3 %collective-permute-start.29 = (bf16[64,2048]{1,0:T(8,128)(2,1)S(1)}, bf16[64,2048]{1,0:T(8,128)(2,1)S(1)}, u32[]{:S(2)}, u32[]{:S(2)}) collective-permute-start(bf16[64,2048]{1,0:T(8,128)(2,1)S(1)} %add_convert_fusion.6), channel_id=1, source_target_pairs={{0,1},{2,0},{4,2},{6,4},{7,6},{5,7},{3,5},{1,3},{8,9},{10,8},{12,1... | collective-permute-start | bytes 786440 | tf_op jit(solution)/shard_map/ppermute | solution.py:55
  100.8 3.1 %collective-permute-done.31 = bf16[64,2048]{1,0:T(8,128)(2,1)S(1)} collective-permute-done((bf16[64,2048]{1,0:T(8,128)(2,1)S(1)}, bf16[64,2048]{1,0:T(8,128)(2,1)S(1)}, u32[]{:S(2)}, u32[]{:S(2)}) %collective-permute-start.31) | collective-permute-done | bytes 262176 | tf_op jit(solution)/shard_map/ppermute | solution.py:55
  103.9 0.9 collective-permute-done.30
  104.9 0.2 collective-permute-start.32
  105.1 1.3 %collective-permute-start.33 = (bf16[64,2048]{1,0:T(8,128)(2,1)S(1)}, bf16[64,2048]{1,0:T(8,128)(2,1)S(1)}, u32[]{:S(2)}, u32[]{:S(2)}) collective-permute-start(bf16[64,2048]{1,0:T(8,128)(2,1)S(1)} %add_convert_fusion.2), channel_id=1, source_target_pairs={{0,1},{2,0},{4,2},{6,4},{7,6},{5,7},{3,5},{1,3},{8,9},{10,8},{12,1... | collective-permute-start | bytes 786440 | tf_op jit(solution)/shard_map/ppermute | solution.py:55
  106.4 4.0 %collective-permute-done.28.refs_2_ = bf16[64,2048]{1,0:T(8,128)(2,1)S(1)} collective-permute-done((bf16[64,2048]{1,0:T(8,128)(2,1)S(1)}, bf16[64,2048]{1,0:T(8,128)(2,1)S(1)}, u32[]{:S(2)}, u32[]{:S(2)}) %collective-permute-start.28) | collective-permute-done | bytes 262176 | tf_op jit(solution)/shard_map/ppermute | solution.py:55
  110.6 5.5 %collective-permute-done.32 = bf16[64,2048]{1,0:T(8,128)(2,1)S(1)} collective-permute-done((bf16[64,2048]{1,0:T(8,128)(2,1)S(1)}, bf16[64,2048]{1,0:T(8,128)(2,1)S(1)}, u32[]{:S(2)}, u32[]{:S(2)}) %collective-permute-start.32) | collective-permute-done | bytes 262176 | tf_op jit(solution)/shard_map/ppermute | solution.py:55
  116.2 0.8 pad_maximum_fusion
  (46 shorter events, 2.5 us)
Async XLA Ops:
  1.1 8.5 %collective-permute-start.4 = (bf16[256,512]{1,0:T(8,128)(2,1)S(1)}, bf16[256,512]{1,0:T(8,128)(2,1)S(1)}, u32[]{:S(2)}, u32[]{:S(2)}) collective-permute-start(bf16[256,512]{1,0:T(8,128)(2,1)S(1)} %get-tuple-element.60.refs_3_), channel_id=1, source_target_pairs={{0,1},{2,0},{4,2},{6,4},{7,6},{5,7},{3,5},{1,3},{8,9},{10,8},{12,1... | collective-permute-start | bytes 786440 | tf_op jit(solution)/shard_map/ppermute | solution.py:55
  3.1 8.0 %copy-start.4 = (f32[512,4]{0,1:T(4,128)S(1)}, f32[512,4]{0,1:T(4,128)}, u32[]{:S(2)}) copy-start(f32[512,4]{0,1:T(4,128)} %param.18) | copy-start | bytes 24580
  3.1 7.8 %collective-permute-start = (bf16[256,512]{1,0:T(8,128)(2,1)S(1)}, bf16[256,512]{1,0:T(8,128)(2,1)S(1)}, u32[]{:S(2)}, u32[]{:S(2)}) collective-permute-start(bf16[256,512]{1,0:T(8,128)(2,1)S(1)} %get-tuple-element.57.refs_0_), channel_id=1, source_target_pairs={{0,2},{2,4},{4,6},{6,7},{7,5},{5,3},{3,1},{1,0},{8,10},{10,12},{12... | collective-permute-start | bytes 786440 | tf_op jit(solution)/shard_map/ppermute | solution.py:55
  3.3 11.6 %collective-permute-start.2 = (bf16[256,512]{1,0:T(8,128)(2,1)S(1)}, bf16[256,512]{1,0:T(8,128)(2,1)S(1)}, u32[]{:S(2)}, u32[]{:S(2)}) collective-permute-start(bf16[256,512]{1,0:T(8,128)(2,1)S(1)} %get-tuple-element.57.refs_0_), channel_id=1, source_target_pairs={{0,1},{2,0},{4,2},{6,4},{7,6},{5,7},{3,5},{1,3},{8,9},{10,8},{12,1... | collective-permute-start | bytes 786440 | tf_op jit(solution)/shard_map/ppermute | solution.py:55
  4.6 11.3 %collective-permute-start.3 = (bf16[256,512]{1,0:T(8,128)(2,1)S(1)}, bf16[256,512]{1,0:T(8,128)(2,1)S(1)}, u32[]{:S(2)}, u32[]{:S(2)}) collective-permute-start(bf16[256,512]{1,0:T(8,128)(2,1)S(1)} %get-tuple-element.60.refs_3_), channel_id=1, source_target_pairs={{0,2},{2,4},{4,6},{6,7},{7,5},{5,3},{3,1},{1,0},{8,10},{10,12},{12... | collective-permute-start | bytes 786440 | tf_op jit(solution)/shard_map/ppermute | solution.py:55
  9.6 10.9 %collective-permute-start.9 = (bf16[256,512]{1,0:T(8,128)(2,1)S(1)}, bf16[256,512]{1,0:T(8,128)(2,1)S(1)}, u32[]{:S(2)}, u32[]{:S(2)}) collective-permute-start(bf16[256,512]{1,0:T(8,128)(2,1)S(1)} %collective-permute-done.4.refs_5_), channel_id=1, source_target_pairs={{0,1},{2,0},{4,2},{6,4},{7,6},{5,7},{3,5},{1,3},{8,9},{10,8},{12,1... | collective-permute-start | bytes 786440 | tf_op jit(solution)/shard_map/ppermute | solution.py:55
  10.9 10.6 %collective-permute-start.1 = (bf16[256,512]{1,0:T(8,128)(2,1)S(1)}, bf16[256,512]{1,0:T(8,128)(2,1)S(1)}, u32[]{:S(2)}, u32[]{:S(2)}) collective-permute-start(bf16[256,512]{1,0:T(8,128)(2,1)S(1)} %collective-permute-done.refs_1_), channel_id=1, source_target_pairs={{0,2},{2,4},{4,6},{6,7},{7,5},{5,3},{3,1},{1,0},{8,10},{10,12},{12... | collective-permute-start | bytes 786440 | tf_op jit(solution)/shard_map/ppermute | solution.py:55
  11.1 7.9 %collective-permute-start.5 = (f32[4,512]{1,0:T(4,128)S(1)}, f32[4,512]{1,0:T(4,128)S(1)}, u32[]{:S(2)}, u32[]{:S(2)}) collective-permute-start(f32[4,512]{1,0:T(4,128)S(1)} %bitcast.1), channel_id=1, source_target_pairs={{0,8},{8,0},{16,24},{24,16},{1,9},{9,1},{17,25},{25,17},{2,10},{10... | collective-permute-start | bytes 24584 | tf_op jit(solution)/shard_map/ppermute | solution.py:524
  14.9 11.2 %collective-permute-start.7 = (bf16[256,512]{1,0:T(8,128)(2,1)S(1)}, bf16[256,512]{1,0:T(8,128)(2,1)S(1)}, u32[]{:S(2)}, u32[]{:S(2)}) collective-permute-start(bf16[256,512]{1,0:T(8,128)(2,1)S(1)} %collective-permute-done.2.refs_2_), channel_id=1, source_target_pairs={{0,1},{2,0},{4,2},{6,4},{7,6},{5,7},{3,5},{1,3},{8,9},{10,8},{12,1... | collective-permute-start | bytes 786440 | tf_op jit(solution)/shard_map/ppermute | solution.py:55
  15.9 10.9 %collective-permute-start.8 = (bf16[256,512]{1,0:T(8,128)(2,1)S(1)}, bf16[256,512]{1,0:T(8,128)(2,1)S(1)}, u32[]{:S(2)}, u32[]{:S(2)}) collective-permute-start(bf16[256,512]{1,0:T(8,128)(2,1)S(1)} %collective-permute-done.3.refs_4_), channel_id=1, source_target_pairs={{0,2},{2,4},{4,6},{6,7},{7,5},{5,3},{3,1},{1,0},{8,10},{10,12},{12... | collective-permute-start | bytes 786440 | tf_op jit(solution)/shard_map/ppermute | solution.py:55
  20.5 11.2 %collective-permute-start.11 = (bf16[256,512]{1,0:T(8,128)(2,1)S(1)}, bf16[256,512]{1,0:T(8,128)(2,1)S(1)}, u32[]{:S(2)}, u32[]{:S(2)}) collective-permute-start(bf16[256,512]{1,0:T(8,128)(2,1)S(1)} %collective-permute-done.9.refs_3_), channel_id=1, source_target_pairs={{0,1},{2,0},{4,2},{6,4},{7,6},{5,7},{3,5},{1,3},{8,9},{10,8},{12,1... | collective-permute-start | bytes 786440 | tf_op jit(solution)/shard_map/ppermute | solution.py:55
  21.6 10.9 %collective-permute-start.6 = (bf16[256,512]{1,0:T(8,128)(2,1)S(1)}, bf16[256,512]{1,0:T(8,128)(2,1)S(1)}, u32[]{:S(2)}, u32[]{:S(2)}) collective-permute-start(bf16[256,512]{1,0:T(8,128)(2,1)S(1)} %collective-permute-done.1.refs_0_), channel_id=1, source_target_pairs={{0,2},{2,4},{4,6},{6,7},{7,5},{5,3},{3,1},{1,0},{8,10},{10,12},{12... | collective-permute-start | bytes 786440 | tf_op jit(solution)/shard_map/ppermute | solution.py:55
  26.9 10.5 %collective-permute-start.13 = (bf16[256,512]{1,0:T(8,128)(2,1)S(1)}, bf16[256,512]{1,0:T(8,128)(2,1)S(1)}, u32[]{:S(2)}, u32[]{:S(2)}) collective-permute-start(bf16[256,512]{1,0:T(8,128)(2,1)S(1)} %collective-permute-done.7.refs_1_), channel_id=1, source_target_pairs={{0,1},{2,0},{4,2},{6,4},{7,6},{5,7},{3,5},{1,3},{8,9},{10,8},{12,1... | collective-permute-start | bytes 786440 | tf_op jit(solution)/shard_map/ppermute | solution.py:55
  28.2 9.9 %collective-permute-start.14 = (bf16[256,512]{1,0:T(8,128)(2,1)S(1)}, bf16[256,512]{1,0:T(8,128)(2,1)S(1)}, u32[]{:S(2)}, u32[]{:S(2)}) collective-permute-start(bf16[256,512]{1,0:T(8,128)(2,1)S(1)} %collective-permute-done.8.refs_2_), channel_id=1, source_target_pairs={{0,2},{2,4},{4,6},{6,7},{7,5},{5,3},{3,1},{1,0},{8,10},{10,12},{12... | collective-permute-start | bytes 786440 | tf_op jit(solution)/shard_map/ppermute | solution.py:55
  32.5 10.5 %collective-permute-start.12 = (bf16[256,512]{1,0:T(8,128)(2,1)S(1)}, bf16[256,512]{1,0:T(8,128)(2,1)S(1)}, u32[]{:S(2)}, u32[]{:S(2)}) collective-permute-start(bf16[256,512]{1,0:T(8,128)(2,1)S(1)} %collective-permute-done.11.refs_3_), channel_id=1, source_target_pairs={{0,1},{2,0},{4,2},{6,4},{7,6},{5,7},{3,5},{1,3},{8,9},{10,8},{12,1... | collective-permute-start | bytes 786440 | tf_op jit(solution)/shard_map/ppermute | solution.py:55
  33.8 9.9 %collective-permute-start.10 = (bf16[256,512]{1,0:T(8,128)(2,1)S(1)}, bf16[256,512]{1,0:T(8,128)(2,1)S(1)}, u32[]{:S(2)}, u32[]{:S(2)}) collective-permute-start(bf16[256,512]{1,0:T(8,128)(2,1)S(1)} %collective-permute-done.6.refs_0_), channel_id=1, source_target_pairs={{0,2},{2,4},{4,6},{6,7},{7,5},{5,3},{3,1},{1,0},{8,10},{10,12},{12... | collective-permute-start | bytes 786440 | tf_op jit(solution)/shard_map/ppermute | solution.py:55
  39.9 11.0 %copy-start.1 = (f32[4,128,256]{2,1,0:T(8,128)S(1)}, f32[4,128,256]{2,1,0:T(8,128)}, u32[]{:S(2)}) copy-start(f32[4,128,256]{2,1,0:T(8,128)} %gate_ref.5) | copy-start | bytes 1572868
  40.0 11.0 %copy-start.2 = (f32[4,128,256]{2,1,0:T(8,128)S(1)}, f32[4,128,256]{2,1,0:T(8,128)}, u32[]{:S(2)}) copy-start(f32[4,128,256]{2,1,0:T(8,128)} %up_ref.5) | copy-start | bytes 1572868
  40.0 11.0 %copy-start.3 = (f32[4,256,128]{2,1,0:T(8,128)S(1)}, f32[4,256,128]{2,1,0:T(8,128)}, u32[]{:S(2)}) copy-start(f32[4,256,128]{2,1,0:T(8,128)} %down_ref.5) | copy-start | bytes 1572868
  44.6 20.8 %collective-permute-start.17 = (bf16[2,512,512]{2,1,0:T(8,128)(2,1)S(1)}, bf16[2,512,512]{2,1,0:T(8,128)(2,1)S(1)}, u32[]{:S(2)}, u32[]{:S(2)}) collective-permute-start(bf16[2,512,512]{2,1,0:T(8,128)(2,1)S(1)} %get-tuple-element.72.kv_ref), channel_id=1, source_target_pairs={{8,16},{9,17},{10,18},{11,19},{12,20},{13,21},{14,22},{15,23}} | collective-permute-start | bytes 3145736 | tf_op jit(solution)/shard_map/ppermute | solution.py:555
  49.6 2.9 %collective-permute-start.15 = (bf16[2,512,256]{2,1,0:T(8,128)(2,1)S(1)}, bf16[2,512,256]{2,1,0:T(8,128)(2,1)S(1)}, u32[]{:S(2)}, u32[]{:S(2)}) collective-permute-start(bf16[2,512,256]{2,1,0:T(8,128)(2,1)S(1)} %get-tuple-element.73), channel_id=1, source_target_pairs={{0,8},{8,0},{16,24},{24,16},{1,9},{9,1},{17,25},{25,17},{2,10},{10... | collective-permute-start | bytes 1572872 | tf_op jit(solution)/shard_map/ppermute | solution.py:524
  49.7 4.7 %collective-permute-start.16 = (bf16[2,512,256]{2,1,0:T(8,128)(2,1)S(1)}, bf16[2,512,256]{2,1,0:T(8,128)(2,1)S(1)}, u32[]{:S(2)}, u32[]{:S(2)}) collective-permute-start(bf16[2,512,256]{2,1,0:T(8,128)(2,1)S(1)} %get-tuple-element.74), channel_id=1, source_target_pairs={{0,8},{16,24},{1,9},{17,25},{2,10},{18,26},{3,11},{19,27},{4,12},{... | collective-permute-start | bytes 1572872 | tf_op jit(solution)/shard_map/ppermute | solution.py:557
  53.9 15.8 %collective-permute-start.18 = (bf16[2,3,128,256]{3,2,1,0:T(8,128)(2,1)S(1)}, bf16[2,3,128,256]{3,2,1,0:T(8,128)(2,1)S(1)}, u32[]{:S(2)}, u32[]{:S(2)}) collective-permute-start(bf16[2,3,128,256]{3,2,1,0:T(8,128)(2,1)S(1)} %get-tuple-element.78), channel_id=1, source_target_pairs={{0,16},{8,24},{16,0},{24,8},{1,17},{9,25},{17,1},{25,9},{2,18},{10... | collective-permute-start | bytes 1179656 | tf_op jit(solution)/shard_map/ppermute | solution.py:524
  54.4 15.3 %copy-start.5 = (f32[4]{0:T(128)S(1)}, f32[4]{0:T(128)}, u32[]{:S(2)}) copy-start(f32[4]{0:T(128)} %step_ref.1) | copy-start | bytes 52
  65.5 6.9 %copy-start = (bf16[512,4096]{1,0:T(8,128)(2,1)S(1)}, bf16[512,4096]{1,0:T(8,128)(2,1)}, u32[]{:S(2)}) copy-start(bf16[512,4096]{1,0:T(8,128)(2,1)} %w_ref.5) | copy-start | bytes 12582916
  70.5 1.8 %collective-permute-start.19 = (bf16[2,3,128,256]{3,2,1,0:T(8,128)(2,1)S(1)}, bf16[2,3,128,256]{3,2,1,0:T(8,128)(2,1)S(1)}, u32[]{:S(2)}, u32[]{:S(2)}) collective-permute-start(bf16[2,3,128,256]{3,2,1,0:T(8,128)(2,1)S(1)} %shard_map.111.net_ref), channel_id=1, source_target_pairs={{0,8},{8,0},{16,24},{24,16},{1,9},{9,1},{17,25},{25,17},{2,10},{10... | collective-permute-start | bytes 1179656 | tf_op jit(solution)/shard_map/ppermute | solution.py:524
  73.6 7.8 %collective-permute-start.21 = (bf16[64,2048]{1,0:T(8,128)(2,1)S(1)}, bf16[64,2048]{1,0:T(8,128)(2,1)S(1)}, u32[]{:S(2)}, u32[]{:S(2)}) collective-permute-start(bf16[64,2048]{1,0:T(8,128)(2,1)S(1)} %get-tuple-element.80), channel_id=1, source_target_pairs={{0,1},{2,0},{4,2},{6,4},{7,6},{5,7},{3,5},{1,3},{8,9},{10,8},{12,1... | collective-permute-start | bytes 786440 | tf_op jit(solution)/shard_map/ppermute | solution.py:55
  74.9 7.4 %collective-permute-start.20 = (bf16[64,2048]{1,0:T(8,128)(2,1)S(1)}, bf16[64,2048]{1,0:T(8,128)(2,1)S(1)}, u32[]{:S(2)}, u32[]{:S(2)}) collective-permute-start(bf16[64,2048]{1,0:T(8,128)(2,1)S(1)} %get-tuple-element.79), channel_id=1, source_target_pairs={{0,2},{2,4},{4,6},{6,7},{7,5},{5,3},{3,1},{1,0},{8,10},{10,12},{12... | collective-permute-start | bytes 786440 | tf_op jit(solution)/shard_map/ppermute | solution.py:55
  76.3 10.7 %collective-permute-start.23 = (bf16[64,2048]{1,0:T(8,128)(2,1)S(1)}, bf16[64,2048]{1,0:T(8,128)(2,1)S(1)}, u32[]{:S(2)}, u32[]{:S(2)}) collective-permute-start(bf16[64,2048]{1,0:T(8,128)(2,1)S(1)} %get-tuple-element.89), channel_id=1, source_target_pairs={{0,1},{2,0},{4,2},{6,4},{7,6},{5,7},{3,5},{1,3},{8,9},{10,8},{12,1... | collective-permute-start | bytes 786440 | tf_op jit(solution)/shard_map/ppermute | solution.py:55
  77.7 10.3 %collective-permute-start.22 = (bf16[64,2048]{1,0:T(8,128)(2,1)S(1)}, bf16[64,2048]{1,0:T(8,128)(2,1)S(1)}, u32[]{:S(2)}, u32[]{:S(2)}) collective-permute-start(bf16[64,2048]{1,0:T(8,128)(2,1)S(1)} %get-tuple-element.87), channel_id=1, source_target_pairs={{0,2},{2,4},{4,6},{6,7},{7,5},{5,3},{3,1},{1,0},{8,10},{10,12},{12... | collective-permute-start | bytes 786440 | tf_op jit(solution)/shard_map/ppermute | solution.py:55
  82.4 10.2 %collective-permute-start.27 = (bf16[64,2048]{1,0:T(8,128)(2,1)S(1)}, bf16[64,2048]{1,0:T(8,128)(2,1)S(1)}, u32[]{:S(2)}, u32[]{:S(2)}) collective-permute-start(bf16[64,2048]{1,0:T(8,128)(2,1)S(1)} %add_convert_fusion.8), channel_id=1, source_target_pairs={{0,1},{2,0},{4,2},{6,4},{7,6},{5,7},{3,5},{1,3},{8,9},{10,8},{12,1... | collective-permute-start | bytes 786440 | tf_op jit(solution)/shard_map/ppermute | solution.py:55
  83.8 9.8 %collective-permute-start.26 = (bf16[64,2048]{1,0:T(8,128)(2,1)S(1)}, bf16[64,2048]{1,0:T(8,128)(2,1)S(1)}, u32[]{:S(2)}, u32[]{:S(2)}) collective-permute-start(bf16[64,2048]{1,0:T(8,128)(2,1)S(1)} %add_convert_fusion.9), channel_id=1, source_target_pairs={{0,2},{2,4},{4,6},{6,7},{7,5},{5,3},{3,1},{1,0},{8,10},{10,12},{12... | collective-permute-start | bytes 786440 | tf_op jit(solution)/shard_map/ppermute | solution.py:55
  88.0 10.2 %collective-permute-start.25 = (bf16[64,2048]{1,0:T(8,128)(2,1)S(1)}, bf16[64,2048]{1,0:T(8,128)(2,1)S(1)}, u32[]{:S(2)}, u32[]{:S(2)}) collective-permute-start(bf16[64,2048]{1,0:T(8,128)(2,1)S(1)} %add_convert_fusion.10), channel_id=1, source_target_pairs={{0,1},{2,0},{4,2},{6,4},{7,6},{5,7},{3,5},{1,3},{8,9},{10,8},{12,1... | collective-permute-start | bytes 786440 | tf_op jit(solution)/shard_map/ppermute | solution.py:55
  89.4 9.8 %collective-permute-start.24 = (bf16[64,2048]{1,0:T(8,128)(2,1)S(1)}, bf16[64,2048]{1,0:T(8,128)(2,1)S(1)}, u32[]{:S(2)}, u32[]{:S(2)}) collective-permute-start(bf16[64,2048]{1,0:T(8,128)(2,1)S(1)} %add_convert_fusion.11), channel_id=1, source_target_pairs={{0,2},{2,4},{4,6},{6,7},{7,5},{5,3},{3,1},{1,0},{8,10},{10,12},{12... | collective-permute-start | bytes 786440 | tf_op jit(solution)/shard_map/ppermute | solution.py:55
  93.7 10.2 %collective-permute-start.31 = (bf16[64,2048]{1,0:T(8,128)(2,1)S(1)}, bf16[64,2048]{1,0:T(8,128)(2,1)S(1)}, u32[]{:S(2)}, u32[]{:S(2)}) collective-permute-start(bf16[64,2048]{1,0:T(8,128)(2,1)S(1)} %add_convert_fusion.4), channel_id=1, source_target_pairs={{0,1},{2,0},{4,2},{6,4},{7,6},{5,7},{3,5},{1,3},{8,9},{10,8},{12,1... | collective-permute-start | bytes 786440 | tf_op jit(solution)/shard_map/ppermute | solution.py:55
  95.0 9.8 %collective-permute-start.30 = (bf16[64,2048]{1,0:T(8,128)(2,1)S(1)}, bf16[64,2048]{1,0:T(8,128)(2,1)S(1)}, u32[]{:S(2)}, u32[]{:S(2)}) collective-permute-start(bf16[64,2048]{1,0:T(8,128)(2,1)S(1)} %add_convert_fusion.5), channel_id=1, source_target_pairs={{0,2},{2,4},{4,6},{6,7},{7,5},{5,3},{3,1},{1,0},{8,10},{10,12},{12... | collective-permute-start | bytes 786440 | tf_op jit(solution)/shard_map/ppermute | solution.py:55
  99.3 11.2 %collective-permute-start.28 = (bf16[64,2048]{1,0:T(8,128)(2,1)S(1)}, bf16[64,2048]{1,0:T(8,128)(2,1)S(1)}, u32[]{:S(2)}, u32[]{:S(2)}) collective-permute-start(bf16[64,2048]{1,0:T(8,128)(2,1)S(1)} %add_convert_fusion.7), channel_id=1, source_target_pairs={{0,2},{2,4},{4,6},{6,7},{7,5},{5,3},{3,1},{1,0},{8,10},{10,12},{12... | collective-permute-start | bytes 786440 | tf_op jit(solution)/shard_map/ppermute | solution.py:55
  99.5 10.9 %collective-permute-start.29 = (bf16[64,2048]{1,0:T(8,128)(2,1)S(1)}, bf16[64,2048]{1,0:T(8,128)(2,1)S(1)}, u32[]{:S(2)}, u32[]{:S(2)}) collective-permute-start(bf16[64,2048]{1,0:T(8,128)(2,1)S(1)} %add_convert_fusion.6), channel_id=1, source_target_pairs={{0,1},{2,0},{4,2},{6,4},{7,6},{5,7},{3,5},{1,3},{8,9},{10,8},{12,1... | collective-permute-start | bytes 786440 | tf_op jit(solution)/shard_map/ppermute | solution.py:55
  104.9 11.2 %collective-permute-start.32 = (bf16[64,2048]{1,0:T(8,128)(2,1)S(1)}, bf16[64,2048]{1,0:T(8,128)(2,1)S(1)}, u32[]{:S(2)}, u32[]{:S(2)}) collective-permute-start(bf16[64,2048]{1,0:T(8,128)(2,1)S(1)} %add_convert_fusion.3), channel_id=1, source_target_pairs={{0,2},{2,4},{4,6},{6,7},{7,5},{5,3},{3,1},{1,0},{8,10},{10,12},{12... | collective-permute-start | bytes 786440 | tf_op jit(solution)/shard_map/ppermute | solution.py:55
  105.1 11.0 %collective-permute-start.33 = (bf16[64,2048]{1,0:T(8,128)(2,1)S(1)}, bf16[64,2048]{1,0:T(8,128)(2,1)S(1)}, u32[]{:S(2)}, u32[]{:S(2)}) collective-permute-start(bf16[64,2048]{1,0:T(8,128)(2,1)S(1)} %add_convert_fusion.2), channel_id=1, source_target_pairs={{0,1},{2,0},{4,2},{6,4},{7,6},{5,7},{3,5},{1,3},{8,9},{10,8},{12,1... | collective-permute-start | bytes 786440 | tf_op jit(solution)/shard_map/ppermute | solution.py:55

commit v7 on v6

--- a/solution.py
+++ b/solution.py
@@ -314,70 +314,53 @@
     return blocks
 
 
-def attend_chip(query, kv, beside_near, beside_far, size):
+def attend_own(query, kv, size):
     rows = query.shape[1]
     heads = query.shape[2] // size
     row = (rows // 2, rows // 2)
 
-    def body(q_ref, kv_ref, near_ref, far_ref, out_ref, stats_ref):
-        place = lax.axis_index("tok")
-        odd = place % 2 == 1
+    def body(q_ref, kv_ref, out_ref, stats_ref):
+        alone = lax.axis_index("tok") == 0
         causal = lax.broadcasted_iota(jnp.int32, row, 1) <= lax.broadcasted_iota(jnp.int32, row, 0)
-
-        def one(index, where, head, earlier):
-            lane = slice(head * size, (head + 1) * size)
-            blocks = [
-                (kv_ref[0, keys, lane], kv_ref[1, keys, lane], causal if at == index else None)
-                for at, keys in enumerate(halves(rows)[: index + 1])
-            ]
-            if earlier is not None:
-                half, at = divmod(head, heads // 2)
-                ref = (far_ref, near_ref)[half]
-                blocks += earlier_blocks(ref, index, slice(at * size, (at + 1) * size))
-            return lane, attend_blocks(q_ref[0, where, lane], blocks)
-
-        @pl.when(odd)
-        def _():
-            for index, where in enumerate(halves(rows)):
-                for head in range(heads):
-                    lane, (result, _, total) = one(index, where, head, True)
-                    out_ref[where, lane] = result / total
-
-        @pl.when(jnp.logical_not(odd))
-        def _():
-            for index, where in enumerate(halves(rows)):
-                for head in range(heads):
-                    lane, (result, top, total) = one(index, where, head, None)
-                    out_ref[where, lane] = result / jnp.where(place == 0, total, 1.0)
-                    stats_ref[0, where, lane] = jnp.broadcast_to(top, result.shape)
-                    stats_ref[1, where, lane] = jnp.broadcast_to(total, result.shape)
-
-    return call(
-        body,
-        [WHOLE] * 4,
+        for index, where in enumerate(halves(rows)):
+            for head in range(heads):
+                lane = slice(head * size, (head + 1) * size)
+                blocks = [
+                    (kv_ref[0, keys, lane], kv_ref[1, keys, lane], causal if at == index else None)
+                    for at, keys in enumerate(halves(rows)[: index + 1])
+                ]
+                result, top, total = attend_blocks(q_ref[0, where, lane], blocks)
+                out_ref[where, lane] = result / jnp.where(alone, total, 1.0)
+                stats_ref[0, where, lane] = jnp.broadcast_to(top, result.shape)
+                stats_ref[1, where, lane] = jnp.broadcast_to(total, result.shape)
+
+    return call(
+        body,
+        [WHOLE] * 2,
         [WHOLE] * 2,
         [
             jax.ShapeDtypeStruct((rows, heads * size), F32),
             jax.ShapeDtypeStruct((2, rows, heads * size), F32),
         ],
         cost=cost(3 * heads * size * rows * rows, 8 * rows * heads * size, heads * rows * rows),
-    )(query, kv, beside_near, beside_far)
-
-
-def attend_behind(summed, stats, query, behind, size):
+    )(query, kv)
+
+
+def attend_earlier(summed, stats, query, sources, other, size, after=()):
     rows = query.shape[1]
-    heads = query.shape[2] // size
-
-    def body(sum_ref, stats_ref, q_ref, behind_ref, out_ref):
+    heads = sources[0].shape[2] // size
+
+    def body(sum_ref, stats_ref, q_ref, *refs):
+        out_ref = refs[-1]
         place = lax.axis_index("tok")
 
-        @pl.when((place > 0) & (place % 2 == 0))
-        def _():
+        def add(ref):
             for index, where in enumerate(halves(rows)):
-                for head in range(heads):
-                    lane = slice(head * size, (head + 1) * size)
+                for at in range(heads):
+                    lane = lanes(first_head(heads, other) + at, size)
                     result, top, total = attend_blocks(
-                        q_ref[0, where, lane], earlier_blocks(behind_ref, index, lane)
+                        q_ref[0, where, lane],
+                        earlier_blocks(ref, index, slice(at * size, (at + 1) * size)),
                     )
                     before = stats_ref[0, where, lane]
                     both = jnp.maximum(before, top)
@@ -385,14 +368,20 @@
                     total = stats_ref[1, where, lane] * old + total * new
                     out_ref[where, lane] = (sum_ref[where, lane] * old + result * new) / total
 
-    return call(
-        body,
-        [WHOLE] * 4,
+        if len(sources) == 1:
+            pl.when(place > 0)(lambda: add(refs[0]))
+        else:
+            pl.when((place > 0) & (place % 2 == 0))(lambda: add(refs[0]))
+            pl.when(place % 2 == 1)(lambda: add(refs[1]))
+
+    return call(
+        body,
+        [WHOLE] * (3 + len(sources)) + [AFTER] * len(after),
         WHOLE,
         jax.ShapeDtypeStruct(summed.shape, F32),
         cost=cost(3 * heads * size * rows * rows, 8 * rows * heads * size, heads * rows * rows),
         aliases={0: 0},
-    )(summed, stats, query, behind)
+    )(summed, stats, query, *sources, *after)
 
 
 def fast_apply(query, gate, upper, down):
@@ -540,7 +529,7 @@
     held = [{1: piece, -1: piece} for piece in own]
     sums, done = None, 0
     for step in range(1, steps + 1):
-        after = (None, None, weights[0], (sums, rate_beside))[step] if step < 4 else sums
+        after = {2: weights[0], 3: (sums, rate_beside)}.get(step)
         for c in range(CHUNKS):
             last = (1,) if c % 2 == 0 else (-1,)
             held[c] = gather_step(held[c], (1, -1) if step < steps else last, after)
@@ -552,9 +541,8 @@
     kv, far, near = accumulate(chunks, done, 2 * steps, weights[:2], sums, shared=True)
     (query,) = accumulate(chunks, done, 2 * steps, weights[2:], sums, 2)
 
-    behind = lax.ppermute(kv, "tok", [(index, index + 1) for index in range(1, tok_count - 1, 2)])
+    behind = lax.ppermute(far, "tok", [(index, index + 1) for index in range(1, tok_count - 1, 2)])
     beside = swap(far, 1)
-    beside_far = lax.ppermute(near, "tok", [(index, index + 1) for index in range(0, tok_count, 2)])
     (grads,) = head_grads(kv, rate, *nets)
     grads, travel = head_grads(beside, rate_beside, *nets, grads)
     received = []
@@ -565,10 +553,13 @@
                 travel = travel + more.astype(F32)
             travel = travel.astype(BF16)
         received.append(swap(travel, 1 << bit))
-    summed, stats = attend_chip(query, kv, beside, beside_far, head_size)
-    attended = attend_behind(summed, stats, query, behind, head_size)
+    attended, stats = attend_own(query, kv, head_size)
+    near, _ = lax.optimization_barrier((near, attended))
+    behind_far = lax.ppermute(near, "tok", [(index, index + 1) for index in range(tok_count - 1)])
+    attended = attend_earlier(attended, stats, query, (behind, beside), False, head_size)
     mine = renew(grads, received, head_step, *nets, (attended,))
     near = combine_near(query, attended, mine)
+    attended = attend_earlier(attended, stats, query, (behind_far,), True, head_size, (near,))
     return ring_reduce(query, attended, swap(mine, 1), near, w_out)
 
 

time: 118 us -> 114 us (0.966)
  waiting for transfers between devices: 58.4 us -> 53.2 us
    ppermute x2, waiting for transfers between devices: 7.54 us -> 5.1 us  [the longest x1 3.89 us: shards(): lax.ppermute(near, 'tok', [(index, index + 1) for index in range(tok_coun...]
    ppermute x28, waiting for transfers between devices: 45.7 us -> 43.5 us  [ring_send(): lax.ppermute(value, 'head', [(order[i], order[(i + step) % count]) for i...]
    ppermute x4, starting transfers between devices: 2.58 us -> 4.43 us  [swap(): lax.ppermute(value, 'tok', [(index, index ^ bit) for index in range(count)])]
    ppermute x2, starting transfers between devices: 6.24 us -> 4.99 us  [the longest x1 3.07 us: shards(): lax.ppermute(far, 'tok', [(index, index + 1) for index in range(1, tok_co...]
    pallas_call x2 -> x3, Pallas kernels: 3.49 us -> 4.51 us  [the longest x2 2.43 us: attend_earlier(): call(body, [WHOLE] * (3 + len(sources)) + [AFTER] * len(after), WHOLE, ja...]
  transfers between devices with their start and end apart: 34 -> 34, of which waited for: 25 -> 23; matrix products, arithmetic and copies ran while one was open for 1% -> 1% of each run, Pallas kernels for 19% -> 21%
where the time goes in v7:
time: 114 us; the launch traced here: 113 us
  waiting for transfers between devices  53.2 us (47%)
  starting transfers between devices  31.2 us (27%)
  Pallas kernels  27.1 us (24%)
  other arithmetic  1.6 us (1%)
    ppermute x28, waiting for transfers between devices, ring_send(): lax.ppermute(value, 'head', [(order[i], order[(i + step) % count]) for i...  43.5 us
    ppermute x28, starting transfers between devices, ring_send(): lax.ppermute(value, 'head', [(order[i], order[(i + step) % count]) for i...  21.7 us
    pallas_call x5, Pallas kernels, accumulate(): call(body, [WHOLE] * len(args), [WHOLE] * (1 + 2 * shared), [jax.ShapeDty...  7.64 us
    pallas_call x1, Pallas kernels, load(): call(body, [IN_HBM] * count, [WHOLE] * count, [jax.ShapeDtypeStruct(array...  4.78 us
    ppermute x4, waiting for transfers between devices, swap(): lax.ppermute(value, 'tok', [(index, index ^ bit) for index in range(count)])  4.61 us
    pallas_call x3, Pallas kernels, partial_out(): call(body, [WHOLE] * 5 + [AFTER] * len(after), [WHOLE] * (2 * count), [ja...  4.55 us
    ppermute x4, starting transfers between devices, swap(): lax.ppermute(value, 'tok', [(index, index ^ bit) for index in range(count)])  4.43 us
    ppermute x1, waiting for transfers between devices, shards(): lax.ppermute(near, 'tok', [(index, index + 1) for index in range(tok_coun...  3.89 us
  transfers between devices with their start and end apart: 34, of which 23 were waited for; matrix products, arithmetic and copies ran while one was open for 1% of the time, Pallas kernels for 21%

profile of v7, /device:TPU:1, one launch (start us, length us, event | category | flops | bytes accessed | tf_op | source)
XLA Modules:
  0.0 113.4 jit_solution(2385529412102340944)
XLA Ops:
  0.0 1.0 shard_map.100
  1.1 2.1 %collective-permute-start.4 = (bf16[256,512]{1,0:T(8,128)(2,1)S(1)}, bf16[256,512]{1,0:T(8,128)(2,1)S(1)}, u32[]{:S(2)}, u32[]{:S(2)}) collective-permute-start(bf16[256,512]{1,0:T(8,128)(2,1)S(1)} %get-tuple-element.59.refs_3_), channel_id=1, source_target_pairs={{0,1},{2,0},{4,2},{6,4},{7,6},{5,7},{3,5},{1,3},{8,9},{10,8},{12,1... | collective-permute-start | bytes 786440 | tf_op jit(solution)/shard_map/ppermute | solution.py:55
  3.3 1.4 %collective-permute-start.3 = (bf16[256,512]{1,0:T(8,128)(2,1)S(1)}, bf16[256,512]{1,0:T(8,128)(2,1)S(1)}, u32[]{:S(2)}, u32[]{:S(2)}) collective-permute-start(bf16[256,512]{1,0:T(8,128)(2,1)S(1)} %get-tuple-element.59.refs_3_), channel_id=1, source_target_pairs={{0,2},{2,4},{4,6},{6,7},{7,5},{5,3},{3,1},{1,0},{8,10},{10,12},{12... | collective-permute-start | bytes 786440 | tf_op jit(solution)/shard_map/ppermute | solution.py:55
  4.8 4.8 %shard_map.101 = (bf16[4096,512]{1,0:T(8,128)(2,1)S(1)}, bf16[4096,512]{1,0:T(8,128)(2,1)S(1)}, bf16[4096,512]{1,0:T(8,128)(2,1)S(1)}) custom-call(bf16[4096,512]{1,0:T(8,128)(2,1)} %refs_0_.1, bf16[4096,512]{1,0:T(8,128)(2,1)} %refs_1_.1, bf16[4096,512]{1,0:T(8,128)(2,1)} %refs_2_.1), custom_call_target="tpu_custom_call" | custom-call | bytes 25165824 | tf_op jit(solution)/shard_map/pallas_call | solution.py:108
  9.6 1.4 %collective-permute-start.8 = (bf16[256,512]{1,0:T(8,128)(2,1)S(1)}, bf16[256,512]{1,0:T(8,128)(2,1)S(1)}, u32[]{:S(2)}, u32[]{:S(2)}) collective-permute-start(bf16[256,512]{1,0:T(8,128)(2,1)S(1)} %collective-permute-done.4.refs_5_), channel_id=1, source_target_pairs={{0,1},{2,0},{4,2},{6,4},{7,6},{5,7},{3,5},{1,3},{8,9},{10,8},{12,1... | collective-permute-start | bytes 786440 | tf_op jit(solution)/shard_map/ppermute | solution.py:55
  11.1 2.4 %collective-permute-start.5 = (f32[4,512]{1,0:T(4,128)S(1)}, f32[4,512]{1,0:T(4,128)S(1)}, u32[]{:S(2)}, u32[]{:S(2)}) collective-permute-start(f32[4,512]{1,0:T(4,128)S(1)} %bitcast.1), channel_id=1, source_target_pairs={{0,8},{8,0},{16,24},{24,16},{1,9},{9,1},{17,25},{25,17},{2,10},{10... | collective-permute-start | bytes 24584 | tf_op jit(solution)/shard_map/ppermute | solution.py:513
  13.5 2.2 %collective-permute-done.3.refs_4_ = bf16[256,512]{1,0:T(8,128)(2,1)S(1)} collective-permute-done((bf16[256,512]{1,0:T(8,128)(2,1)S(1)}, bf16[256,512]{1,0:T(8,128)(2,1)S(1)}, u32[]{:S(2)}, u32[]{:S(2)}) %collective-permute-start.3) | collective-permute-done | bytes 262176 | tf_op jit(solution)/shard_map/ppermute | solution.py:55
  15.6 0.5 collective-permute-start.13
  16.1 1.0 collective-permute-start.11
  17.1 2.6 %shard_map.102.refs_7_ = f32[3,512,512]{2,1,0:T(8,128)S(1)} custom-call(bf16[256,512]{1,0:T(8,128)(2,1)S(1)} %get-tuple-element.56.refs_0_, bf16[256,512]{1,0:T(8,128)(2,1)S(1)} %collective-permute-done.refs_1_, bf16[256,512]{1,0:T(8,128)(2,1)S(1)} %collective-permute-done.2.refs_2_, bf16[256,512]{1,0:T(8,128)(2,1)S(1)} %get-tuple-element.59.refs_3_, ...), custom_call_target="tpu_custom_call" | custom-call | flops 2415919104 | bytes 12582912 | tf_op jit(solution)/shard_map/pallas_call | solution.py:180
  19.7 0.8 collective-permute-done.8.refs_3_
  20.5 0.7 collective-permute-done.1.refs_0_
  21.2 1.3 %collective-permute-start.9 = (bf16[256,512]{1,0:T(8,128)(2,1)S(1)}, bf16[256,512]{1,0:T(8,128)(2,1)S(1)}, u32[]{:S(2)}, u32[]{:S(2)}) collective-permute-start(bf16[256,512]{1,0:T(8,128)(2,1)S(1)} %collective-permute-done.8.refs_3_), channel_id=1, source_target_pairs={{0,1},{2,0},{4,2},{6,4},{7,6},{5,7},{3,5},{1,3},{8,9},{10,8},{12,1... | collective-permute-start | bytes 786440 | tf_op jit(solution)/shard_map/ppermute | solution.py:55
  22.7 4.2 %collective-permute-done.13.refs_2_ = bf16[256,512]{1,0:T(8,128)(2,1)S(1)} collective-permute-done((bf16[256,512]{1,0:T(8,128)(2,1)S(1)}, bf16[256,512]{1,0:T(8,128)(2,1)S(1)}, u32[]{:S(2)}, u32[]{:S(2)}) %collective-permute-start.13) | collective-permute-done | bytes 262176 | tf_op jit(solution)/shard_map/ppermute | solution.py:55
  26.9 0.5 collective-permute-start.14
  27.3 1.0 collective-permute-start.12
  28.3 3.3 %collective-permute-done.9.refs_3_ = bf16[256,512]{1,0:T(8,128)(2,1)S(1)} collective-permute-done((bf16[256,512]{1,0:T(8,128)(2,1)S(1)}, bf16[256,512]{1,0:T(8,128)(2,1)S(1)}, u32[]{:S(2)}, u32[]{:S(2)}) %collective-permute-start.9) | collective-permute-done | bytes 262176 | tf_op jit(solution)/shard_map/ppermute | solution.py:55
  31.6 1.1 collective-permute-start.10
  32.7 0.3 collective-permute-start.7
  33.1 1.8 %shard_map.103.refs_7_ = f32[3,512,512]{2,1,0:T(8,128)S(1)} custom-call(bf16[256,512]{1,0:T(8,128)(2,1)S(1)} %collective-permute-done.1.refs_0_, bf16[256,512]{1,0:T(8,128)(2,1)S(1)} %collective-permute-done.11.refs_1_, bf16[256,512]{1,0:T(8,128)(2,1)S(1)} %collective-permute-done.13.refs_2_, ...), custom_call_target="tpu_custom_call", output_to_operand_aliasing={{}: (7, {})} | custom-call | flops 1610612736 | bytes 10485760 | tf_op jit(solution)/shard_map/pallas_call | solution.py:180
  34.9 3.2 %collective-permute-done.14.refs_2_ = bf16[256,512]{1,0:T(8,128)(2,1)S(1)} collective-permute-done((bf16[256,512]{1,0:T(8,128)(2,1)S(1)}, bf16[256,512]{1,0:T(8,128)(2,1)S(1)}, u32[]{:S(2)}, u32[]{:S(2)}) %collective-permute-start.14) | collective-permute-done | bytes 262176 | tf_op jit(solution)/shard_map/ppermute | solution.py:55
  38.1 1.8 %shard_map.104.refs_3_.refs_4_ = f32[3,512,512]{2,1,0:T(8,128)S(1)} custom-call(bf16[256,512]{1,0:T(8,128)(2,1)S(1)} %collective-permute-done.6.refs_0_, bf16[256,512]{1,0:T(8,128)(2,1)S(1)} %collective-permute-done.12.refs_1_, bf16[256,512]{1,0:T(8,128)(2,1)S(1)} %collective-permute-done.14.refs_2_, ...), custom_call_target="tpu_custom_call", output_to_operand_aliasing={{}: (7, {})} | custom-call | flops 1610612736 | bytes 10485760 | tf_op jit(solution)/shard_map/pallas_call | solution.py:180
  40.0 2.8 %collective-permute-done.10.refs_1_ = bf16[256,512]{1,0:T(8,128)(2,1)S(1)} collective-permute-done((bf16[256,512]{1,0:T(8,128)(2,1)S(1)}, bf16[256,512]{1,0:T(8,128)(2,1)S(1)}, u32[]{:S(2)}, u32[]{:S(2)}) %collective-permute-start.10) | collective-permute-done | bytes 262176 | tf_op jit(solution)/shard_map/ppermute | solution.py:55
  42.8 0.9 collective-permute-done.7.refs_0_
  43.7 0.9 shard_map.106
  44.6 1.9 %collective-permute-start.16 = (bf16[2,512,256]{2,1,0:T(8,128)(2,1)S(1)}, bf16[2,512,256]{2,1,0:T(8,128)(2,1)S(1)}, u32[]{:S(2)}, u32[]{:S(2)}) collective-permute-start(bf16[2,512,256]{2,1,0:T(8,128)(2,1)S(1)} %get-tuple-element.72), channel_id=1, source_target_pairs={{0,8},{8,0},{16,24},{24,16},{1,9},{9,1},{17,25},{25,17},{2,10},{10... | collective-permute-start | bytes 1572872 | tf_op jit(solution)/shard_map/ppermute | solution.py:513
  46.6 3.1 %collective-permute-start.15 = (bf16[2,512,256]{2,1,0:T(8,128)(2,1)S(1)}, bf16[2,512,256]{2,1,0:T(8,128)(2,1)S(1)}, u32[]{:S(2)}, u32[]{:S(2)}) collective-permute-start(bf16[2,512,256]{2,1,0:T(8,128)(2,1)S(1)} %get-tuple-element.72), channel_id=1, source_target_pairs={{8,16},{9,17},{10,18},{11,19},{12,20},{13,21},{14,22},{15,23}} | collective-permute-start | bytes 1572872 | tf_op jit(solution)/shard_map/ppermute | solution.py:544
  49.7 1.4 %shard_map.109.rest_0_ = f32[2,3,128,256]{3,2,1,0:T(8,128)S(1)} custom-call(bf16[2,512,512]{2,1,0:T(8,128)(2,1)S(1)} %get-tuple-element.69.kv_ref, f32[4,512]{1,0:T(4,128)S(1)} %bitcast.2, f32[4,128,256]{2,1,0:T(8,128)S(1)} %copy-done.1, f32[4,128,256]{2,1,0:T(8,128)S(1)} %copy-done.2, f32[4,256,128]{2,1,0:T(8,128)S(1)} %copy-done.3), custom_call_target="tpu_custom_call" | custom-call | flops 402653184 | bytes 1572864 | tf_op jit(solution)/shard_map/pallas_call | solution.py:244
  51.1 1.4 %shard_map.110 = (f32[2,3,128,256]{3,2,1,0:T(8,128)S(1)}, bf16[2,3,128,256]{3,2,1,0:T(8,128)(2,1)S(1)}) custom-call(bf16[2,512,256]{2,1,0:T(8,128)(2,1)S(1)} %collective-permute-done.16.refs_1_.kv_ref, f32[4,512]{1,0:T(4,128)S(1)} %collective-permute-done.5.rate_ref, f32[4,128,256]{2,1,0:T(8,128)S(1)} %copy-done.1, f32[4,128,256]{2,1,0:T(8,128)S(1)} %copy-done.2, ...), custom_call_target="tpu_custom_call" | custom-call | flops 402653184 | bytes 1572864 | tf_op jit(solution)/shard_map/pallas_call | solution.py:244
  52.6 0.4 shard_map.105.q_ref
  53.1 2.1 %shard_map.107 = (f32[512,512]{1,0:T(8,128)S(1)}, f32[2,512,512]{2,1,0:T(8,128)S(1)}) custom-call(bf16[1,512,512]{2,1,0:T(8,128)(2,1)S(1)} %shard_map.105.q_ref, bf16[2,512,512]{2,1,0:T(8,128)(2,1)S(1)} %get-tuple-element.69.kv_ref), custom_call_target="tpu_custom_call" | custom-call | flops 402653184 | bytes 2097152 | tf_op jit(solution)/shard_map/pallas_call | solution.py:337
  55.2 1.9 %collective-permute-start.17 = (bf16[2,512,256]{2,1,0:T(8,128)(2,1)S(1)}, bf16[2,512,256]{2,1,0:T(8,128)(2,1)S(1)}, u32[]{:S(2)}, u32[]{:S(2)}) collective-permute-start(bf16[2,512,256]{2,1,0:T(8,128)(2,1)S(1)} %get-tuple-element.74), channel_id=1, source_target_pairs={{0,8},{8,16},{16,24},{1,9},{9,17},{17,25},{2,10},{10,18},{18,26},{... | collective-permute-start | bytes 1572872 | tf_op jit(solution)/shard_map/ppermute | solution.py:558
  57.1 1.2 %collective-permute-done.15.refs_0_ = bf16[2,512,256]{2,1,0:T(8,128)(2,1)S(1)} collective-permute-done((bf16[2,512,256]{2,1,0:T(8,128)(2,1)S(1)}, bf16[2,512,256]{2,1,0:T(8,128)(2,1)S(1)}, u32[]{:S(2)}, u32[]{:S(2)}) %collective-permute-start.15) | collective-permute-done | bytes 524320 | tf_op jit(solution)/shard_map/ppermute | solution.py:544
  58.3 1.2 %shard_map.108.rest_1_.attended_ref.sum_ref = f32[512,512]{1,0:T(8,128)S(1)} custom-call(f32[512,512]{1,0:T(8,128)S(1)} %get-tuple-element.70.sum_ref, f32[2,512,512]{2,1,0:T(8,128)S(1)} %get-tuple-element.71.stats_ref, bf16[1,512,512]{2,1,0:T(8,128)(2,1)S(1)} %shard_map.105.q_ref, ...), custom_call_target="tpu_custom_call", output_to_operand_aliasing={{}: (0, {})} | custom-call | flops 201326592 | bytes 1048576 | tf_op jit(solution)/shard_map/pallas_call | solution.py:377
  59.6 4.6 %collective-permute-done.18.rest_0_ = bf16[2,3,128,256]{3,2,1,0:T(8,128)(2,1)S(1)} collective-permute-done((bf16[2,3,128,256]{3,2,1,0:T(8,128)(2,1)S(1)}, bf16[2,3,128,256]{3,2,1,0:T(8,128)(2,1)S(1)}, u32[]{:S(2)}, u32[]{:S(2)}) %collective-permute-start.18) | collective-permute-done | bytes 393248 | tf_op jit(solution)/shard_map/ppermute | solution.py:513
  64.2 0.8 shard_map.111.net_ref
  65.1 0.8 shard_map.112.refs_1_.near_ref
  65.9 3.9 %collective-permute-done.17.refs_0_ = bf16[2,512,256]{2,1,0:T(8,128)(2,1)S(1)} collective-permute-done((bf16[2,512,256]{2,1,0:T(8,128)(2,1)S(1)}, bf16[2,512,256]{2,1,0:T(8,128)(2,1)S(1)}, u32[]{:S(2)}, u32[]{:S(2)}) %collective-permute-start.17) | collective-permute-done | bytes 524320 | tf_op jit(solution)/shard_map/ppermute | solution.py:558
  69.8 1.2 %shard_map.113.attended_ref = f32[512,512]{1,0:T(8,128)S(1)} custom-call(f32[512,512]{1,0:T(8,128)S(1)} %shard_map.108.rest_1_.attended_ref.sum_ref, f32[2,512,512]{2,1,0:T(8,128)S(1)} %get-tuple-element.71.stats_ref, bf16[1,512,512]{2,1,0:T(8,128)(2,1)S(1)} %shard_map.105.q_ref, ...), custom_call_target="tpu_custom_call", output_to_operand_aliasing={{}: (0, {})} | custom-call | flops 201326592 | bytes 1048576 | tf_op jit(solution)/shard_map/pallas_call | solution.py:377
  71.0 1.2 %shard_map.114 = (bf16[64,2048]{1,0:T(8,128)(2,1)S(1)}, bf16[64,2048]{1,0:T(8,128)(2,1)S(1)}) custom-call(bf16[1,512,512]{2,1,0:T(8,128)(2,1)S(1)} %shard_map.105.q_ref, f32[512,512]{1,0:T(8,128)S(1)} %shard_map.113.attended_ref, bf16[2,3,128,256]{3,2,1,0:T(8,128)(2,1)S(1)} %collective-permute-done.19.net_ref, ...), custom_call_target="tpu_custom_call" | custom-call | flops 268435456 | bytes 4718592 | tf_op jit(solution)/shard_map/pallas_call | solution.py:453
  72.2 1.3 %collective-permute-start.21 = (bf16[64,2048]{1,0:T(8,128)(2,1)S(1)}, bf16[64,2048]{1,0:T(8,128)(2,1)S(1)}, u32[]{:S(2)}, u32[]{:S(2)}) collective-permute-start(bf16[64,2048]{1,0:T(8,128)(2,1)S(1)} %get-tuple-element.78), channel_id=1, source_target_pairs={{0,1},{2,0},{4,2},{6,4},{7,6},{5,7},{3,5},{1,3},{8,9},{10,8},{12,1... | collective-permute-start | bytes 786440 | tf_op jit(solution)/shard_map/ppermute | solution.py:55
  73.7 1.2 %shard_map.116 = (bf16[64,2048]{1,0:T(8,128)(2,1)S(1)}, bf16[64,2048]{1,0:T(8,128)(2,1)S(1)}, bf16[64,2048]{1,0:T(8,128)(2,1)S(1)}, bf16[64,2048]{1,0:T(8,128)(2,1)S(1)}) custom-call(bf16[1,512,512]{2,1,0:T(8,128)(2,1)S(1)} %shard_map.105.q_ref, f32[512,512]{1,0:T(8,128)S(1)} %shard_map.113.attended_ref, ...), custom_call_target="tpu_custom_call" | custom-call | flops 536870912 | bytes 5242880 | tf_op jit(solution)/shard_map/pallas_call | solution.py:453
  75.0 1.3 %collective-permute-start.23 = (bf16[64,2048]{1,0:T(8,128)(2,1)S(1)}, bf16[64,2048]{1,0:T(8,128)(2,1)S(1)}, u32[]{:S(2)}, u32[]{:S(2)}) collective-permute-start(bf16[64,2048]{1,0:T(8,128)(2,1)S(1)} %get-tuple-element.87), channel_id=1, source_target_pairs={{0,1},{2,0},{4,2},{6,4},{7,6},{5,7},{3,5},{1,3},{8,9},{10,8},{12,1... | collective-permute-start | bytes 786440 | tf_op jit(solution)/shard_map/ppermute | solution.py:55
  76.5 4.1 %collective-permute-done.21.refs_1_ = bf16[64,2048]{1,0:T(8,128)(2,1)S(1)} collective-permute-done((bf16[64,2048]{1,0:T(8,128)(2,1)S(1)}, bf16[64,2048]{1,0:T(8,128)(2,1)S(1)}, u32[]{:S(2)}, u32[]{:S(2)}) %collective-permute-start.21) | collective-permute-done | bytes 262176 | tf_op jit(solution)/shard_map/ppermute | solution.py:55
  80.7 1.2 %collective-permute-done.20.refs_0_ = bf16[64,2048]{1,0:T(8,128)(2,1)S(1)} collective-permute-done((bf16[64,2048]{1,0:T(8,128)(2,1)S(1)}, bf16[64,2048]{1,0:T(8,128)(2,1)S(1)}, u32[]{:S(2)}, u32[]{:S(2)}) %collective-permute-start.20) | collective-permute-done | bytes 262176 | tf_op jit(solution)/shard_map/ppermute | solution.py:55
  82.0 1.3 %collective-permute-start.27 = (bf16[64,2048]{1,0:T(8,128)(2,1)S(1)}, bf16[64,2048]{1,0:T(8,128)(2,1)S(1)}, u32[]{:S(2)}, u32[]{:S(2)}) collective-permute-start(bf16[64,2048]{1,0:T(8,128)(2,1)S(1)} %add_convert_fusion.8), channel_id=1, source_target_pairs={{0,1},{2,0},{4,2},{6,4},{7,6},{5,7},{3,5},{1,3},{8,9},{10,8},{12,1... | collective-permute-start | bytes 786440 | tf_op jit(solution)/shard_map/ppermute | solution.py:55
  83.5 2.1 %shard_map.115 = (bf16[64,2048]{1,0:T(8,128)(2,1)S(1)}, bf16[64,2048]{1,0:T(8,128)(2,1)S(1)}, bf16[64,2048]{1,0:T(8,128)(2,1)S(1)}, bf16[64,2048]{1,0:T(8,128)(2...) custom-call(bf16[1,512,512]{2,1,0:T(8,128)(2,1)S(1)} %shard_map.105., ...), custom_call_target="tpu_custom_call" | custom-call | flops 1342177280 | bytes 6815744 | tf_op jit(solution)/shard_map/pallas_call | solution.py:453
  85.6 0.6 collective-permute-done.23
  86.3 1.2 %collective-permute-done.22 = bf16[64,2048]{1,0:T(8,128)(2,1)S(1)} collective-permute-done((bf16[64,2048]{1,0:T(8,128)(2,1)S(1)}, bf16[64,2048]{1,0:T(8,128)(2,1)S(1)}, u32[]{:S(2)}, u32[]{:S(2)}) %collective-permute-start.22) | collective-permute-done | bytes 262176 | tf_op jit(solution)/shard_map/ppermute | solution.py:55
  87.6 1.3 %collective-permute-start.25 = (bf16[64,2048]{1,0:T(8,128)(2,1)S(1)}, bf16[64,2048]{1,0:T(8,128)(2,1)S(1)}, u32[]{:S(2)}, u32[]{:S(2)}) collective-permute-start(bf16[64,2048]{1,0:T(8,128)(2,1)S(1)} %add_convert_fusion.10), channel_id=1, source_target_pairs={{0,1},{2,0},{4,2},{6,4},{7,6},{5,7},{3,5},{1,3},{8,9},{10,8},{12,1... | collective-permute-start | bytes 786440 | tf_op jit(solution)/shard_map/ppermute | solution.py:55
  89.1 2.7 %collective-permute-done.27 = bf16[64,2048]{1,0:T(8,128)(2,1)S(1)} collective-permute-done((bf16[64,2048]{1,0:T(8,128)(2,1)S(1)}, bf16[64,2048]{1,0:T(8,128)(2,1)S(1)}, u32[]{:S(2)}, u32[]{:S(2)}) %collective-permute-start.27) | collective-permute-done | bytes 262176 | tf_op jit(solution)/shard_map/ppermute | solution.py:55
  91.9 1.2 %collective-permute-done.26 = bf16[64,2048]{1,0:T(8,128)(2,1)S(1)} collective-permute-done((bf16[64,2048]{1,0:T(8,128)(2,1)S(1)}, bf16[64,2048]{1,0:T(8,128)(2,1)S(1)}, u32[]{:S(2)}, u32[]{:S(2)}) %collective-permute-start.26) | collective-permute-done | bytes 262176 | tf_op jit(solution)/shard_map/ppermute | solution.py:55
  93.2 1.3 %collective-permute-start.31 = (bf16[64,2048]{1,0:T(8,128)(2,1)S(1)}, bf16[64,2048]{1,0:T(8,128)(2,1)S(1)}, u32[]{:S(2)}, u32[]{:S(2)}) collective-permute-start(bf16[64,2048]{1,0:T(8,128)(2,1)S(1)} %add_convert_fusion.4), channel_id=1, source_target_pairs={{0,1},{2,0},{4,2},{6,4},{7,6},{5,7},{3,5},{1,3},{8,9},{10,8},{12,1... | collective-permute-start | bytes 786440 | tf_op jit(solution)/shard_map/ppermute | solution.py:55
  94.7 2.4 %collective-permute-done.25 = bf16[64,2048]{1,0:T(8,128)(2,1)S(1)} collective-permute-done((bf16[64,2048]{1,0:T(8,128)(2,1)S(1)}, bf16[64,2048]{1,0:T(8,128)(2,1)S(1)}, u32[]{:S(2)}, u32[]{:S(2)}) %collective-permute-start.25) | collective-permute-done | bytes 262176 | tf_op jit(solution)/shard_map/ppermute | solution.py:55
  97.2 1.5 %collective-permute-done.24 = bf16[64,2048]{1,0:T(8,128)(2,1)S(1)} collective-permute-done((bf16[64,2048]{1,0:T(8,128)(2,1)S(1)}, bf16[64,2048]{1,0:T(8,128)(2,1)S(1)}, u32[]{:S(2)}, u32[]{:S(2)}) %collective-permute-start.24) | collective-permute-done | bytes 262176 | tf_op jit(solution)/shard_map/ppermute | solution.py:55
  98.8 0.2 collective-permute-start.28
  99.0 1.3 %collective-permute-start.29 = (bf16[64,2048]{1,0:T(8,128)(2,1)S(1)}, bf16[64,2048]{1,0:T(8,128)(2,1)S(1)}, u32[]{:S(2)}, u32[]{:S(2)}) collective-permute-start(bf16[64,2048]{1,0:T(8,128)(2,1)S(1)} %add_convert_fusion.6), channel_id=1, source_target_pairs={{0,1},{2,0},{4,2},{6,4},{7,6},{5,7},{3,5},{1,3},{8,9},{10,8},{12,1... | collective-permute-start | bytes 786440 | tf_op jit(solution)/shard_map/ppermute | solution.py:55
  100.3 2.3 %collective-permute-done.31 = bf16[64,2048]{1,0:T(8,128)(2,1)S(1)} collective-permute-done((bf16[64,2048]{1,0:T(8,128)(2,1)S(1)}, bf16[64,2048]{1,0:T(8,128)(2,1)S(1)}, u32[]{:S(2)}, u32[]{:S(2)}) %collective-permute-start.31) | collective-permute-done | bytes 262176 | tf_op jit(solution)/shard_map/ppermute | solution.py:55
  102.7 1.7 %collective-permute-done.30 = bf16[64,2048]{1,0:T(8,128)(2,1)S(1)} collective-permute-done((bf16[64,2048]{1,0:T(8,128)(2,1)S(1)}, bf16[64,2048]{1,0:T(8,128)(2,1)S(1)}, u32[]{:S(2)}, u32[]{:S(2)}) %collective-permute-start.30) | collective-permute-done | bytes 262176 | tf_op jit(solution)/shard_map/ppermute | solution.py:55
  104.4 0.2 collective-permute-start.32
  104.7 1.3 %collective-permute-start.33 = (bf16[64,2048]{1,0:T(8,128)(2,1)S(1)}, bf16[64,2048]{1,0:T(8,128)(2,1)S(1)}, u32[]{:S(2)}, u32[]{:S(2)}) collective-permute-start(bf16[64,2048]{1,0:T(8,128)(2,1)S(1)} %add_convert_fusion.2), channel_id=1, source_target_pairs={{0,1},{2,0},{4,2},{6,4},{7,6},{5,7},{3,5},{1,3},{8,9},{10,8},{12,1... | collective-permute-start | bytes 786440 | tf_op jit(solution)/shard_map/ppermute | solution.py:55
  106.0 4.0 %collective-permute-done.28.refs_2_ = bf16[64,2048]{1,0:T(8,128)(2,1)S(1)} collective-permute-done((bf16[64,2048]{1,0:T(8,128)(2,1)S(1)}, bf16[64,2048]{1,0:T(8,128)(2,1)S(1)}, u32[]{:S(2)}, u32[]{:S(2)}) %collective-permute-start.28) | collective-permute-done | bytes 262176 | tf_op jit(solution)/shard_map/ppermute | solution.py:55
  110.0 2.4 %collective-permute-done.32 = bf16[64,2048]{1,0:T(8,128)(2,1)S(1)} collective-permute-done((bf16[64,2048]{1,0:T(8,128)(2,1)S(1)}, bf16[64,2048]{1,0:T(8,128)(2,1)S(1)}, u32[]{:S(2)}, u32[]{:S(2)}) %collective-permute-start.32) | collective-permute-done | bytes 262176 | tf_op jit(solution)/shard_map/ppermute | solution.py:55
  112.6 0.8 pad_maximum_fusion
  (47 shorter events, 2.5 us)
Async XLA Ops:
  1.1 8.5 %collective-permute-start.4 = (bf16[256,512]{1,0:T(8,128)(2,1)S(1)}, bf16[256,512]{1,0:T(8,128)(2,1)S(1)}, u32[]{:S(2)}, u32[]{:S(2)}) collective-permute-start(bf16[256,512]{1,0:T(8,128)(2,1)S(1)} %get-tuple-element.59.refs_3_), channel_id=1, source_target_pairs={{0,1},{2,0},{4,2},{6,4},{7,6},{5,7},{3,5},{1,3},{8,9},{10,8},{12,1... | collective-permute-start | bytes 786440 | tf_op jit(solution)/shard_map/ppermute | solution.py:55
  3.1 8.0 %copy-start.4 = (f32[512,4]{0,1:T(4,128)S(1)}, f32[512,4]{0,1:T(4,128)}, u32[]{:S(2)}) copy-start(f32[512,4]{0,1:T(4,128)} %param.18) | copy-start | bytes 24580
  3.1 7.8 %collective-permute-start = (bf16[256,512]{1,0:T(8,128)(2,1)S(1)}, bf16[256,512]{1,0:T(8,128)(2,1)S(1)}, u32[]{:S(2)}, u32[]{:S(2)}) collective-permute-start(bf16[256,512]{1,0:T(8,128)(2,1)S(1)} %get-tuple-element.56.refs_0_), channel_id=1, source_target_pairs={{0,2},{2,4},{4,6},{6,7},{7,5},{5,3},{3,1},{1,0},{8,10},{10,12},{12... | collective-permute-start | bytes 786440 | tf_op jit(solution)/shard_map/ppermute | solution.py:55
  3.3 12.3 %collective-permute-start.3 = (bf16[256,512]{1,0:T(8,128)(2,1)S(1)}, bf16[256,512]{1,0:T(8,128)(2,1)S(1)}, u32[]{:S(2)}, u32[]{:S(2)}) collective-permute-start(bf16[256,512]{1,0:T(8,128)(2,1)S(1)} %get-tuple-element.59.refs_3_), channel_id=1, source_target_pairs={{0,2},{2,4},{4,6},{6,7},{7,5},{5,3},{3,1},{1,0},{8,10},{10,12},{12... | collective-permute-start | bytes 786440 | tf_op jit(solution)/shard_map/ppermute | solution.py:55
  4.7 11.4 %collective-permute-start.2 = (bf16[256,512]{1,0:T(8,128)(2,1)S(1)}, bf16[256,512]{1,0:T(8,128)(2,1)S(1)}, u32[]{:S(2)}, u32[]{:S(2)}) collective-permute-start(bf16[256,512]{1,0:T(8,128)(2,1)S(1)} %get-tuple-element.56.refs_0_), channel_id=1, source_target_pairs={{0,1},{2,0},{4,2},{6,4},{7,6},{5,7},{3,5},{1,3},{8,9},{10,8},{12,1... | collective-permute-start | bytes 786440 | tf_op jit(solution)/shard_map/ppermute | solution.py:55
  9.6 10.9 %collective-permute-start.8 = (bf16[256,512]{1,0:T(8,128)(2,1)S(1)}, bf16[256,512]{1,0:T(8,128)(2,1)S(1)}, u32[]{:S(2)}, u32[]{:S(2)}) collective-permute-start(bf16[256,512]{1,0:T(8,128)(2,1)S(1)} %collective-permute-done.4.refs_5_), channel_id=1, source_target_pairs={{0,1},{2,0},{4,2},{6,4},{7,6},{5,7},{3,5},{1,3},{8,9},{10,8},{12,1... | collective-permute-start | bytes 786440 | tf_op jit(solution)/shard_map/ppermute | solution.py:55
  10.9 10.3 %collective-permute-start.1 = (bf16[256,512]{1,0:T(8,128)(2,1)S(1)}, bf16[256,512]{1,0:T(8,128)(2,1)S(1)}, u32[]{:S(2)}, u32[]{:S(2)}) collective-permute-start(bf16[256,512]{1,0:T(8,128)(2,1)S(1)} %collective-permute-done.refs_1_), channel_id=1, source_target_pairs={{0,2},{2,4},{4,6},{6,7},{7,5},{5,3},{3,1},{1,0},{8,10},{10,12},{12... | collective-permute-start | bytes 786440 | tf_op jit(solution)/shard_map/ppermute | solution.py:55
  11.1 8.6 %collective-permute-start.5 = (f32[4,512]{1,0:T(4,128)S(1)}, f32[4,512]{1,0:T(4,128)S(1)}, u32[]{:S(2)}, u32[]{:S(2)}) collective-permute-start(f32[4,512]{1,0:T(4,128)S(1)} %bitcast.1), channel_id=1, source_target_pairs={{0,8},{8,0},{16,24},{24,16},{1,9},{9,1},{17,25},{25,17},{2,10},{10... | collective-permute-start | bytes 24584 | tf_op jit(solution)/shard_map/ppermute | solution.py:513
  15.6 11.2 %collective-permute-start.13 = (bf16[256,512]{1,0:T(8,128)(2,1)S(1)}, bf16[256,512]{1,0:T(8,128)(2,1)S(1)}, u32[]{:S(2)}, u32[]{:S(2)}) collective-permute-start(bf16[256,512]{1,0:T(8,128)(2,1)S(1)} %collective-permute-done.3.refs_4_), channel_id=1, source_target_pairs={{0,2},{2,4},{4,6},{6,7},{7,5},{5,3},{3,1},{1,0},{8,10},{10,12},{12... | collective-permute-start | bytes 786440 | tf_op jit(solution)/shard_map/ppermute | solution.py:55
  16.1 10.8 %collective-permute-start.11 = (bf16[256,512]{1,0:T(8,128)(2,1)S(1)}, bf16[256,512]{1,0:T(8,128)(2,1)S(1)}, u32[]{:S(2)}, u32[]{:S(2)}) collective-permute-start(bf16[256,512]{1,0:T(8,128)(2,1)S(1)} %collective-permute-done.2.refs_2_), channel_id=1, source_target_pairs={{0,1},{2,0},{4,2},{6,4},{7,6},{5,7},{3,5},{1,3},{8,9},{10,8},{12,1... | collective-permute-start | bytes 786440 | tf_op jit(solution)/shard_map/ppermute | solution.py:55
  21.2 10.3 %collective-permute-start.9 = (bf16[256,512]{1,0:T(8,128)(2,1)S(1)}, bf16[256,512]{1,0:T(8,128)(2,1)S(1)}, u32[]{:S(2)}, u32[]{:S(2)}) collective-permute-start(bf16[256,512]{1,0:T(8,128)(2,1)S(1)} %collective-permute-done.8.refs_3_), channel_id=1, source_target_pairs={{0,1},{2,0},{4,2},{6,4},{7,6},{5,7},{3,5},{1,3},{8,9},{10,8},{12,1... | collective-permute-start | bytes 786440 | tf_op jit(solution)/shard_map/ppermute | solution.py:55
  22.5 10.2 %collective-permute-start.6 = (bf16[256,512]{1,0:T(8,128)(2,1)S(1)}, bf16[256,512]{1,0:T(8,128)(2,1)S(1)}, u32[]{:S(2)}, u32[]{:S(2)}) collective-permute-start(bf16[256,512]{1,0:T(8,128)(2,1)S(1)} %collective-permute-done.1.refs_0_), channel_id=1, source_target_pairs={{0,2},{2,4},{4,6},{6,7},{7,5},{5,3},{3,1},{1,0},{8,10},{10,12},{12... | collective-permute-start | bytes 786440 | tf_op jit(solution)/shard_map/ppermute | solution.py:55
  26.9 11.2 %collective-permute-start.14 = (bf16[256,512]{1,0:T(8,128)(2,1)S(1)}, bf16[256,512]{1,0:T(8,128)(2,1)S(1)}, u32[]{:S(2)}, u32[]{:S(2)}) collective-permute-start(bf16[256,512]{1,0:T(8,128)(2,1)S(1)} %collective-permute-done.13.refs_2_), channel_id=1, source_target_pairs={{0,2},{2,4},{4,6},{6,7},{7,5},{5,3},{3,1},{1,0},{8,10},{10,12},{12... | collective-permute-start | bytes 786440 | tf_op jit(solution)/shard_map/ppermute | solution.py:55
  27.3 10.8 %collective-permute-start.12 = (bf16[256,512]{1,0:T(8,128)(2,1)S(1)}, bf16[256,512]{1,0:T(8,128)(2,1)S(1)}, u32[]{:S(2)}, u32[]{:S(2)}) collective-permute-start(bf16[256,512]{1,0:T(8,128)(2,1)S(1)} %collective-permute-done.11.refs_1_), channel_id=1, source_target_pairs={{0,1},{2,0},{4,2},{6,4},{7,6},{5,7},{3,5},{1,3},{8,9},{10,8},{12,1... | collective-permute-start | bytes 786440 | tf_op jit(solution)/shard_map/ppermute | solution.py:55
  31.6 11.2 %collective-permute-start.10 = (bf16[256,512]{1,0:T(8,128)(2,1)S(1)}, bf16[256,512]{1,0:T(8,128)(2,1)S(1)}, u32[]{:S(2)}, u32[]{:S(2)}) collective-permute-start(bf16[256,512]{1,0:T(8,128)(2,1)S(1)} %collective-permute-done.9.refs_3_), channel_id=1, source_target_pairs={{0,1},{2,0},{4,2},{6,4},{7,6},{5,7},{3,5},{1,3},{8,9},{10,8},{12,1... | collective-permute-start | bytes 786440 | tf_op jit(solution)/shard_map/ppermute | solution.py:55
  32.7 11.0 %collective-permute-start.7 = (bf16[256,512]{1,0:T(8,128)(2,1)S(1)}, bf16[256,512]{1,0:T(8,128)(2,1)S(1)}, u32[]{:S(2)}, u32[]{:S(2)}) collective-permute-start(bf16[256,512]{1,0:T(8,128)(2,1)S(1)} %collective-permute-done.6.refs_0_), channel_id=1, source_target_pairs={{0,2},{2,4},{4,6},{6,7},{7,5},{5,3},{3,1},{1,0},{8,10},{10,12},{12... | collective-permute-start | bytes 786440 | tf_op jit(solution)/shard_map/ppermute | solution.py:55
  39.9 9.7 %copy-start.1 = (f32[4,128,256]{2,1,0:T(8,128)S(1)}, f32[4,128,256]{2,1,0:T(8,128)}, u32[]{:S(2)}) copy-start(f32[4,128,256]{2,1,0:T(8,128)} %gate_ref.5) | copy-start | bytes 1572868
  40.0 9.7 %copy-start.2 = (f32[4,128,256]{2,1,0:T(8,128)S(1)}, f32[4,128,256]{2,1,0:T(8,128)}, u32[]{:S(2)}) copy-start(f32[4,128,256]{2,1,0:T(8,128)} %up_ref.5) | copy-start | bytes 1572868
  40.0 9.7 %copy-start.3 = (f32[4,256,128]{2,1,0:T(8,128)S(1)}, f32[4,256,128]{2,1,0:T(8,128)}, u32[]{:S(2)}) copy-start(f32[4,256,128]{2,1,0:T(8,128)} %down_ref.5) | copy-start | bytes 1572868
  44.6 6.5 %collective-permute-start.16 = (bf16[2,512,256]{2,1,0:T(8,128)(2,1)S(1)}, bf16[2,512,256]{2,1,0:T(8,128)(2,1)S(1)}, u32[]{:S(2)}, u32[]{:S(2)}) collective-permute-start(bf16[2,512,256]{2,1,0:T(8,128)(2,1)S(1)} %get-tuple-element.72), channel_id=1, source_target_pairs={{0,8},{8,0},{16,24},{24,16},{1,9},{9,1},{17,25},{25,17},{2,10},{10... | collective-permute-start | bytes 1572872 | tf_op jit(solution)/shard_map/ppermute | solution.py:513
  46.6 11.8 %collective-permute-start.15 = (bf16[2,512,256]{2,1,0:T(8,128)(2,1)S(1)}, bf16[2,512,256]{2,1,0:T(8,128)(2,1)S(1)}, u32[]{:S(2)}, u32[]{:S(2)}) collective-permute-start(bf16[2,512,256]{2,1,0:T(8,128)(2,1)S(1)} %get-tuple-element.72), channel_id=1, source_target_pairs={{8,16},{9,17},{10,18},{11,19},{12,20},{13,21},{14,22},{15,23}} | collective-permute-start | bytes 1572872 | tf_op jit(solution)/shard_map/ppermute | solution.py:544
  52.6 11.6 %collective-permute-start.18 = (bf16[2,3,128,256]{3,2,1,0:T(8,128)(2,1)S(1)}, bf16[2,3,128,256]{3,2,1,0:T(8,128)(2,1)S(1)}, u32[]{:S(2)}, u32[]{:S(2)}) collective-permute-start(bf16[2,3,128,256]{3,2,1,0:T(8,128)(2,1)S(1)} %get-tuple-element.76), channel_id=1, source_target_pairs={{0,16},{8,24},{16,0},{24,8},{1,17},{9,25},{17,1},{25,9},{2,18},{10... | collective-permute-start | bytes 1179656 | tf_op jit(solution)/shard_map/ppermute | solution.py:513
  53.1 11.1 %copy-start.5 = (f32[4]{0:T(128)S(1)}, f32[4]{0:T(128)}, u32[]{:S(2)}) copy-start(f32[4]{0:T(128)} %step_ref.1) | copy-start | bytes 52
  55.2 14.6 %collective-permute-start.17 = (bf16[2,512,256]{2,1,0:T(8,128)(2,1)S(1)}, bf16[2,512,256]{2,1,0:T(8,128)(2,1)S(1)}, u32[]{:S(2)}, u32[]{:S(2)}) collective-permute-start(bf16[2,512,256]{2,1,0:T(8,128)(2,1)S(1)} %get-tuple-element.74), channel_id=1, source_target_pairs={{0,8},{8,16},{16,24},{1,9},{9,17},{17,25},{2,10},{10,18},{18,26},{... | collective-permute-start | bytes 1572872 | tf_op jit(solution)/shard_map/ppermute | solution.py:558
  65.0 6.0 %copy-start = (bf16[512,4096]{1,0:T(8,128)(2,1)S(1)}, bf16[512,4096]{1,0:T(8,128)(2,1)}, u32[]{:S(2)}) copy-start(bf16[512,4096]{1,0:T(8,128)(2,1)} %w_ref.5) | copy-start | bytes 12582916
  65.0 6.0 %collective-permute-start.19 = (bf16[2,3,128,256]{3,2,1,0:T(8,128)(2,1)S(1)}, bf16[2,3,128,256]{3,2,1,0:T(8,128)(2,1)S(1)}, u32[]{:S(2)}, u32[]{:S(2)}) collective-permute-start(bf16[2,3,128,256]{3,2,1,0:T(8,128)(2,1)S(1)} %shard_map.111.net_ref), channel_id=1, source_target_pairs={{0,8},{8,0},{16,24},{24,16},{1,9},{9,1},{17,25},{25,17},{2,10},{10... | collective-permute-start | bytes 1179656 | tf_op jit(solution)/shard_map/ppermute | solution.py:513
  72.2 8.4 %collective-permute-start.21 = (bf16[64,2048]{1,0:T(8,128)(2,1)S(1)}, bf16[64,2048]{1,0:T(8,128)(2,1)S(1)}, u32[]{:S(2)}, u32[]{:S(2)}) collective-permute-start(bf16[64,2048]{1,0:T(8,128)(2,1)S(1)} %get-tuple-element.78), channel_id=1, source_target_pairs={{0,1},{2,0},{4,2},{6,4},{7,6},{5,7},{3,5},{1,3},{8,9},{10,8},{12,1... | collective-permute-start | bytes 786440 | tf_op jit(solution)/shard_map/ppermute | solution.py:55
  73.6 8.3 %collective-permute-start.20 = (bf16[64,2048]{1,0:T(8,128)(2,1)S(1)}, bf16[64,2048]{1,0:T(8,128)(2,1)S(1)}, u32[]{:S(2)}, u32[]{:S(2)}) collective-permute-start(bf16[64,2048]{1,0:T(8,128)(2,1)S(1)} %get-tuple-element.77), channel_id=1, source_target_pairs={{0,2},{2,4},{4,6},{6,7},{7,5},{5,3},{3,1},{1,0},{8,10},{10,12},{12... | collective-permute-start | bytes 786440 | tf_op jit(solution)/shard_map/ppermute | solution.py:55
  75.0 11.2 %collective-permute-start.23 = (bf16[64,2048]{1,0:T(8,128)(2,1)S(1)}, bf16[64,2048]{1,0:T(8,128)(2,1)S(1)}, u32[]{:S(2)}, u32[]{:S(2)}) collective-permute-start(bf16[64,2048]{1,0:T(8,128)(2,1)S(1)} %get-tuple-element.87), channel_id=1, source_target_pairs={{0,1},{2,0},{4,2},{6,4},{7,6},{5,7},{3,5},{1,3},{8,9},{10,8},{12,1... | collective-permute-start | bytes 786440 | tf_op jit(solution)/shard_map/ppermute | solution.py:55
  76.3 11.2 %collective-permute-start.22 = (bf16[64,2048]{1,0:T(8,128)(2,1)S(1)}, bf16[64,2048]{1,0:T(8,128)(2,1)S(1)}, u32[]{:S(2)}, u32[]{:S(2)}) collective-permute-start(bf16[64,2048]{1,0:T(8,128)(2,1)S(1)} %get-tuple-element.85), channel_id=1, source_target_pairs={{0,2},{2,4},{4,6},{6,7},{7,5},{5,3},{3,1},{1,0},{8,10},{10,12},{12... | collective-permute-start | bytes 786440 | tf_op jit(solution)/shard_map/ppermute | solution.py:55
  82.0 9.9 %collective-permute-start.27 = (bf16[64,2048]{1,0:T(8,128)(2,1)S(1)}, bf16[64,2048]{1,0:T(8,128)(2,1)S(1)}, u32[]{:S(2)}, u32[]{:S(2)}) collective-permute-start(bf16[64,2048]{1,0:T(8,128)(2,1)S(1)} %add_convert_fusion.8), channel_id=1, source_target_pairs={{0,1},{2,0},{4,2},{6,4},{7,6},{5,7},{3,5},{1,3},{8,9},{10,8},{12,1... | collective-permute-start | bytes 786440 | tf_op jit(solution)/shard_map/ppermute | solution.py:55
  83.3 9.8 %collective-permute-start.26 = (bf16[64,2048]{1,0:T(8,128)(2,1)S(1)}, bf16[64,2048]{1,0:T(8,128)(2,1)S(1)}, u32[]{:S(2)}, u32[]{:S(2)}) collective-permute-start(bf16[64,2048]{1,0:T(8,128)(2,1)S(1)} %add_convert_fusion.9), channel_id=1, source_target_pairs={{0,2},{2,4},{4,6},{6,7},{7,5},{5,3},{3,1},{1,0},{8,10},{10,12},{12... | collective-permute-start | bytes 786440 | tf_op jit(solution)/shard_map/ppermute | solution.py:55
  87.6 9.6 %collective-permute-start.25 = (bf16[64,2048]{1,0:T(8,128)(2,1)S(1)}, bf16[64,2048]{1,0:T(8,128)(2,1)S(1)}, u32[]{:S(2)}, u32[]{:S(2)}) collective-permute-start(bf16[64,2048]{1,0:T(8,128)(2,1)S(1)} %add_convert_fusion.10), channel_id=1, source_target_pairs={{0,1},{2,0},{4,2},{6,4},{7,6},{5,7},{3,5},{1,3},{8,9},{10,8},{12,1... | collective-permute-start | bytes 786440 | tf_op jit(solution)/shard_map/ppermute | solution.py:55
  88.9 9.8 %collective-permute-start.24 = (bf16[64,2048]{1,0:T(8,128)(2,1)S(1)}, bf16[64,2048]{1,0:T(8,128)(2,1)S(1)}, u32[]{:S(2)}, u32[]{:S(2)}) collective-permute-start(bf16[64,2048]{1,0:T(8,128)(2,1)S(1)} %add_convert_fusion.11), channel_id=1, source_target_pairs={{0,2},{2,4},{4,6},{6,7},{7,5},{5,3},{3,1},{1,0},{8,10},{10,12},{12... | collective-permute-start | bytes 786440 | tf_op jit(solution)/shard_map/ppermute | solution.py:55
  93.2 9.4 %collective-permute-start.31 = (bf16[64,2048]{1,0:T(8,128)(2,1)S(1)}, bf16[64,2048]{1,0:T(8,128)(2,1)S(1)}, u32[]{:S(2)}, u32[]{:S(2)}) collective-permute-start(bf16[64,2048]{1,0:T(8,128)(2,1)S(1)} %add_convert_fusion.4), channel_id=1, source_target_pairs={{0,1},{2,0},{4,2},{6,4},{7,6},{5,7},{3,5},{1,3},{8,9},{10,8},{12,1... | collective-permute-start | bytes 786440 | tf_op jit(solution)/shard_map/ppermute | solution.py:55
  94.6 9.8 %collective-permute-start.30 = (bf16[64,2048]{1,0:T(8,128)(2,1)S(1)}, bf16[64,2048]{1,0:T(8,128)(2,1)S(1)}, u32[]{:S(2)}, u32[]{:S(2)}) collective-permute-start(bf16[64,2048]{1,0:T(8,128)(2,1)S(1)} %add_convert_fusion.5), channel_id=1, source_target_pairs={{0,2},{2,4},{4,6},{6,7},{7,5},{5,3},{3,1},{1,0},{8,10},{10,12},{12... | collective-permute-start | bytes 786440 | tf_op jit(solution)/shard_map/ppermute | solution.py:55
  98.8 11.1 %collective-permute-start.28 = (bf16[64,2048]{1,0:T(8,128)(2,1)S(1)}, bf16[64,2048]{1,0:T(8,128)(2,1)S(1)}, u32[]{:S(2)}, u32[]{:S(2)}) collective-permute-start(bf16[64,2048]{1,0:T(8,128)(2,1)S(1)} %add_convert_fusion.7), channel_id=1, source_target_pairs={{0,2},{2,4},{4,6},{6,7},{7,5},{5,3},{3,1},{1,0},{8,10},{10,12},{12... | collective-permute-start | bytes 786440 | tf_op jit(solution)/shard_map/ppermute | solution.py:55
  99.0 10.9 %collective-permute-start.29 = (bf16[64,2048]{1,0:T(8,128)(2,1)S(1)}, bf16[64,2048]{1,0:T(8,128)(2,1)S(1)}, u32[]{:S(2)}, u32[]{:S(2)}) collective-permute-start(bf16[64,2048]{1,0:T(8,128)(2,1)S(1)} %add_convert_fusion.6), channel_id=1, source_target_pairs={{0,1},{2,0},{4,2},{6,4},{7,6},{5,7},{3,5},{1,3},{8,9},{10,8},{12,1... | collective-permute-start | bytes 786440 | tf_op jit(solution)/shard_map/ppermute | solution.py:55
  104.4 8.0 %collective-permute-start.32 = (bf16[64,2048]{1,0:T(8,128)(2,1)S(1)}, bf16[64,2048]{1,0:T(8,128)(2,1)S(1)}, u32[]{:S(2)}, u32[]{:S(2)}) collective-permute-start(bf16[64,2048]{1,0:T(8,128)(2,1)S(1)} %add_convert_fusion.3), channel_id=1, source_target_pairs={{0,2},{2,4},{4,6},{6,7},{7,5},{5,3},{3,1},{1,0},{8,10},{10,12},{12... | collective-permute-start | bytes 786440 | tf_op jit(solution)/shard_map/ppermute | solution.py:55
  104.7 7.9 %collective-permute-start.33 = (bf16[64,2048]{1,0:T(8,128)(2,1)S(1)}, bf16[64,2048]{1,0:T(8,128)(2,1)S(1)}, u32[]{:S(2)}, u32[]{:S(2)}) collective-permute-start(bf16[64,2048]{1,0:T(8,128)(2,1)S(1)} %add_convert_fusion.2), channel_id=1, source_target_pairs={{0,1},{2,0},{4,2},{6,4},{7,6},{5,7},{3,5},{1,3},{8,9},{10,8},{12,1... | collective-permute-start | bytes 786440 | tf_op jit(solution)/shard_map/ppermute | solution.py:55

commit v8 on v7

--- a/solution.py
+++ b/solution.py
@@ -161,7 +161,7 @@
     def body(*refs):
         piece_refs = refs[: len(pieces)]
         weight_refs = refs[len(pieces) : len(pieces) + parts]
-        out_ref, left = refs[-2 - 2 * shared], refs[-1]
+        out_ref, left = refs[-2 - 4 * shared], refs[-1]
         for index, ref in enumerate(piece_refs):
             chunk, piece = divmod(index, span)
             left[chunk * rows : (chunk + 1) * rows, piece * depth : (piece + 1) * depth] = ref[...]
@@ -172,18 +172,20 @@
             out_ref[part] = term.astype(dtype)
             if shared:
                 side = lax.axis_index("tok") % 2
-                refs[-3][part] = out_ref[part, :, lanes(1 - side, width // 2)]
-                refs[-2][part] = out_ref[part, :, lanes(side, width // 2)]
+                refs[-5][part] = out_ref[part, :, lanes(1 - side, width // 2)]
+                refs[-4][part] = out_ref[part, :, lanes(side, width // 2)]
+                refs[-3 + part][0] = refs[-5][part]
 
     aliased = before is not None and not final
     args = [*pieces, *weights] + ([] if before is None else [before])
     return call(
         body,
         [WHOLE] * len(args),
-        [WHOLE] * (1 + 2 * shared),
+        [WHOLE] * (1 + 4 * shared),
         [
-            jax.ShapeDtypeStruct((parts, total, size), dtype)
-            for size in (width, width // 2, width // 2)[: 1 + 2 * shared]
+            jax.ShapeDtypeStruct((count, total, size), dtype)
+            for count, size in [(parts, width)] + [(parts, width // 2)] * 2 * shared
+            + [(1, width // 2)] * 2 * shared
         ],
         [pltpu.VMEM((total, span * depth), BF16)],
         vmem=12,
@@ -205,22 +207,22 @@
     return (values * scale).astype(BF16)
 
 
-def head_grads(kv, rate, fast_gate, fast_up, fast_down, before=None):
-    rows = kv.shape[1]
+def head_grads(keys, values, rate, fast_gate, fast_up, fast_down, before=None):
+    rows = keys.shape[1]
     size, hidden_size = fast_gate.shape[1:]
     count = rate.shape[0]
     heads = count // 2
-    whole = kv.shape[2] == count * size
-
-    def body(kv_ref, rate_ref, gate_ref, up_ref, down_ref, *rest):
+    whole = keys.shape[2] == count * size
+
+    def body(key_ref, value_ref, rate_ref, gate_ref, up_ref, down_ref, *rest):
         rates = rate_ref[...].T
         column = lax.broadcasted_iota(jnp.int32, (rows, count), 1)
         for index in range(heads):
             head = first_head(heads) + index
             mine = jnp.sum(jnp.where(column == head, rates, 0.0), axis=1, keepdims=True)
             lane = lanes(head if whole else index, size)
-            knorm = normed(kv_ref[0, :, lane])
-            target = (-mine * kv_ref[1, :, lane].astype(F32)).astype(BF16)
+            knorm = normed(key_ref[0, :, lane])
+            target = (-mine * value_ref[value_ref.shape[0] - 1, :, lane].astype(F32)).astype(BF16)
             gate_pre = mm(knorm, gate_ref[head].astype(BF16))
             up_pre = mm(knorm, up_ref[head].astype(BF16))
             back = mm(target, down_ref[head].astype(BF16), ((1,), (1,)))
@@ -239,7 +241,7 @@
                 else:
                     rest[-1][index, part] = term
 
-    args = [kv, rate, fast_gate, fast_up, fast_down] + ([] if before is None else [before])
+    args = [keys, values, rate, fast_gate, fast_up, fast_down] + ([] if before is None else [before])
     kinds = [F32] if before is None else [F32, BF16]
     return call(
         body,
@@ -304,22 +306,23 @@
     return [slice(index * rows // 2, (index + 1) * rows // 2) for index in range(2)]
 
 
-def earlier_blocks(ref, index, lane):
-    rows = ref.shape[1]
+def earlier_blocks(keys, values, index, lane):
+    rows = keys.shape[1]
+    last = values.shape[0] - 1
     row = lax.broadcasted_iota(jnp.int32, (rows // 2, rows // 2), 0)
     col = lax.broadcasted_iota(jnp.int32, (rows // 2, rows // 2), 1)
-    blocks = [(ref[0, halves(rows)[index], lane], ref[1, halves(rows)[index], lane], col > row)]
+    blocks = [(keys[0, halves(rows)[index], lane], values[last, halves(rows)[index], lane], col > row)]
     if index == 0:
-        blocks.append((ref[0, halves(rows)[1], lane], ref[1, halves(rows)[1], lane], None))
+        blocks.append((keys[0, halves(rows)[1], lane], values[last, halves(rows)[1], lane], None))
     return blocks
 
 
-def attend_own(query, kv, size):
+def attend_own(query, kv, size, after):
     rows = query.shape[1]
     heads = query.shape[2] // size
     row = (rows // 2, rows // 2)
 
-    def body(q_ref, kv_ref, out_ref, stats_ref):
+    def body(q_ref, kv_ref, _, out_ref, stats_ref):
         alone = lax.axis_index("tok") == 0
         causal = lax.broadcasted_iota(jnp.int32, row, 1) <= lax.broadcasted_iota(jnp.int32, row, 0)
         for index, where in enumerate(halves(rows)):
@@ -336,31 +339,31 @@
 
     return call(
         body,
-        [WHOLE] * 2,
+        [WHOLE] * 2 + [AFTER],
         [WHOLE] * 2,
         [
             jax.ShapeDtypeStruct((rows, heads * size), F32),
             jax.ShapeDtypeStruct((2, rows, heads * size), F32),
         ],
         cost=cost(3 * heads * size * rows * rows, 8 * rows * heads * size, heads * rows * rows),
-    )(query, kv)
+    )(query, kv, after)
 
 
 def attend_earlier(summed, stats, query, sources, other, size, after=()):
     rows = query.shape[1]
-    heads = sources[0].shape[2] // size
+    heads = sources[0][0].shape[2] // size
 
     def body(sum_ref, stats_ref, q_ref, *refs):
         out_ref = refs[-1]
         place = lax.axis_index("tok")
 
-        def add(ref):
+        def add(keys, values):
             for index, where in enumerate(halves(rows)):
                 for at in range(heads):
                     lane = lanes(first_head(heads, other) + at, size)
                     result, top, total = attend_blocks(
                         q_ref[0, where, lane],
-                        earlier_blocks(ref, index, slice(at * size, (at + 1) * size)),
+                        earlier_blocks(keys, values, index, slice(at * size, (at + 1) * size)),
                     )
                     before = stats_ref[0, where, lane]
                     both = jnp.maximum(before, top)
@@ -369,19 +372,19 @@
                     out_ref[where, lane] = (sum_ref[where, lane] * old + result * new) / total
 
         if len(sources) == 1:
-            pl.when(place > 0)(lambda: add(refs[0]))
+            pl.when(place > 0)(lambda: add(*refs[:2]))
         else:
-            pl.when((place > 0) & (place % 2 == 0))(lambda: add(refs[0]))
-            pl.when(place % 2 == 1)(lambda: add(refs[1]))
-
-    return call(
-        body,
-        [WHOLE] * (3 + len(sources)) + [AFTER] * len(after),
+            pl.when((place > 0) & (place % 2 == 0))(lambda: add(*refs[:2]))
+            pl.when(place % 2 == 1)(lambda: add(*refs[2:4]))
+
+    return call(
+        body,
+        [WHOLE] * (3 + 2 * len(sources)) + [AFTER] * len(after),
         WHOLE,
         jax.ShapeDtypeStruct(summed.shape, F32),
         cost=cost(3 * heads * size * rows * rows, 8 * rows * heads * size, heads * rows * rows),
         aliases={0: 0},
-    )(summed, stats, query, *sources, *after)
+    )(summed, stats, query, *[ref for pair in sources for ref in pair], *after)
 
 
 def fast_apply(query, gate, upper, down):
@@ -471,8 +474,9 @@
     ordered = ()
     for which in range(2 * steps - 1):
         step, half = steps - (which + 1) // 2, which % 2
-        if which == 2:
-            parts |= partial_out(signed[2:] + [0], *shared, tuple(coming.values())[:2])
+        if which % 2 == 0 and 2 <= which <= 2 * (steps - 2):
+            later = signed[which : which + 2] + [0] * (which == 2 * (steps - 2))
+            parts |= partial_out(later, *shared, tuple(coming.values())[:2])
         terms = []
         for way in (1, -1):
             side = half if way == 1 else 1 - half
@@ -538,13 +542,13 @@
             known = [chunk[: 2 * step - 1] for chunk in chunks]
             (sums,) = accumulate(known, done, 2 * step - 1, weights, sums)
             done = 2 * step - 1
-    kv, far, near = accumulate(chunks, done, 2 * steps, weights[:2], sums, shared=True)
+    kv, far, near, *apart = accumulate(chunks, done, 2 * steps, weights[:2], sums, shared=True)
     (query,) = accumulate(chunks, done, 2 * steps, weights[2:], sums, 2)
 
     behind = lax.ppermute(far, "tok", [(index, index + 1) for index in range(1, tok_count - 1, 2)])
-    beside = swap(far, 1)
-    (grads,) = head_grads(kv, rate, *nets)
-    grads, travel = head_grads(beside, rate_beside, *nets, grads)
+    beside = [swap(part, 1) for part in apart]
+    (grads,) = head_grads(kv, kv, rate, *nets)
+    grads, travel = head_grads(*beside, rate_beside, *nets, grads)
     received = []
     for bit in range(1, tok_count.bit_length() - 1):
         if received:
@@ -553,13 +557,13 @@
                 travel = travel + more.astype(F32)
             travel = travel.astype(BF16)
         received.append(swap(travel, 1 << bit))
-    attended, stats = attend_own(query, kv, head_size)
+    attended, stats = attend_own(query, kv, head_size, behind)
     near, _ = lax.optimization_barrier((near, attended))
     behind_far = lax.ppermute(near, "tok", [(index, index + 1) for index in range(tok_count - 1)])
-    attended = attend_earlier(attended, stats, query, (behind, beside), False, head_size)
+    attended = attend_earlier(attended, stats, query, ((behind, behind), beside), False, head_size)
     mine = renew(grads, received, head_step, *nets, (attended,))
     near = combine_near(query, attended, mine)
-    attended = attend_earlier(attended, stats, query, (behind_far,), True, head_size, (near,))
+    attended = attend_earlier(attended, stats, query, ((behind_far, behind_far),), True, head_size, (near,))
     return ring_reduce(query, attended, swap(mine, 1), near, w_out)
 
 

time: 114 us -> 114 us (level)
  waiting for transfers between devices: 53.2 us -> 50 us
  starting transfers between devices: 31.2 us -> 34.1 us
    ppermute x4 -> x5, waiting for transfers between devices: 4.61 us -> 0.01 us  [swap(): lax.ppermute(value, 'tok', [(index, index ^ bit) for index in range(count)])]
    ppermute x1, waiting for transfers between devices: 1.21 us -> 3.77 us  [shards(): lax.ppermute(far, 'tok', [(index, index + 1) for index in range(1, tok_co...]
    ppermute x1, starting transfers between devices: 1.92 us -> 4.39 us  [shards(): lax.ppermute(near, 'tok', [(index, index + 1) for index in range(tok_coun...]
    ppermute x1, starting transfers between devices: 3.07 us -> 4.92 us  [shards(): lax.ppermute(far, 'tok', [(index, index + 1) for index in range(1, tok_co...]
    ppermute x4 -> x5, starting transfers between devices: 4.43 us -> 3.07 us  [swap(): lax.ppermute(value, 'tok', [(index, index ^ bit) for index in range(count)])]
    pallas_call x3 -> x4, Pallas kernels: 4.55 us -> 5.17 us  [partial_out(): call(body, [WHOLE] * 5 + [AFTER] * len(after), [WHOLE] * (2 * count), [ja...]
  transfers between devices with their start and end apart: 34 -> 35, of which waited for: 23 -> 22; matrix products, arithmetic and copies ran while one was open for 1% -> 1% of each run, Pallas kernels for 21% -> 22%
where the time goes in v8:
time: 114 us
  waiting for transfers between devices  50 us (44%)
  starting transfers between devices  34.1 us (30%)
  Pallas kernels  28 us (25%)
  other arithmetic  1.59 us (1%)
    ppermute x28, waiting for transfers between devices, ring_send(): lax.ppermute(value, 'head', [(order[i], order[(i + step) % count]) for i...  43.3 us
    ppermute x28, starting transfers between devices, ring_send(): lax.ppermute(value, 'head', [(order[i], order[(i + step) % count]) for i...  21.7 us
    pallas_call x5, Pallas kernels, accumulate(): call(body, [WHOLE] * len(args), [WHOLE] * (1 + 4 * shared), [jax.ShapeDty...  7.65 us
    pallas_call x4, Pallas kernels, partial_out(): call(body, [WHOLE] * 5 + [AFTER] * len(after), [WHOLE] * (2 * count), [ja...  5.17 us
    ppermute x1, starting transfers between devices, shards(): lax.ppermute(far, 'tok', [(index, index + 1) for index in range(1, tok_co...  4.92 us
    pallas_call x1, Pallas kernels, load(): call(body, [IN_HBM] * count, [WHOLE] * count, [jax.ShapeDtypeStruct(array...  4.78 us
    ppermute x1, starting transfers between devices, shards(): lax.ppermute(near, 'tok', [(index, index + 1) for index in range(tok_coun...  4.39 us
    ppermute x1, waiting for transfers between devices, shards(): lax.ppermute(far, 'tok', [(index, index + 1) for index in range(1, tok_co...  3.77 us
  transfers between devices with their start and end apart: 35, of which 22 were waited for; matrix products, arithmetic and copies ran while one was open for 1% of the time, Pallas kernels for 22%

profile of v8, /device:TPU:1, one launch (start us, length us, event | category | flops | bytes accessed | tf_op | source)
XLA Modules:
  0.0 114.1 jit_solution(3839818181681841695)
XLA Ops:
  0.0 1.0 shard_map.100
  1.1 2.1 %collective-permute-start.4 = (bf16[256,512]{1,0:T(8,128)(2,1)S(1)}, bf16[256,512]{1,0:T(8,128)(2,1)S(1)}, u32[]{:S(2)}, u32[]{:S(2)}) collective-permute-start(bf16[256,512]{1,0:T(8,128)(2,1)S(1)} %get-tuple-element.61.refs_3_), channel_id=1, source_target_pairs={{0,1},{2,0},{4,2},{6,4},{7,6},{5,7},{3,5},{1,3},{8,9},{10,8},{12,1... | collective-permute-start | bytes 786440 | tf_op jit(solution)/shard_map/ppermute | solution.py:55
  3.3 1.4 %collective-permute-start.3 = (bf16[256,512]{1,0:T(8,128)(2,1)S(1)}, bf16[256,512]{1,0:T(8,128)(2,1)S(1)}, u32[]{:S(2)}, u32[]{:S(2)}) collective-permute-start(bf16[256,512]{1,0:T(8,128)(2,1)S(1)} %get-tuple-element.61.refs_3_), channel_id=1, source_target_pairs={{0,2},{2,4},{4,6},{6,7},{7,5},{5,3},{3,1},{1,0},{8,10},{10,12},{12... | collective-permute-start | bytes 786440 | tf_op jit(solution)/shard_map/ppermute | solution.py:55
  4.8 4.8 %shard_map.101 = (bf16[4096,512]{1,0:T(8,128)(2,1)S(1)}, bf16[4096,512]{1,0:T(8,128)(2,1)S(1)}, bf16[4096,512]{1,0:T(8,128)(2,1)S(1)}) custom-call(bf16[4096,512]{1,0:T(8,128)(2,1)} %refs_0_.1, bf16[4096,512]{1,0:T(8,128)(2,1)} %refs_1_.1, bf16[4096,512]{1,0:T(8,128)(2,1)} %refs_2_.1), custom_call_target="tpu_custom_call" | custom-call | bytes 25165824 | tf_op jit(solution)/shard_map/pallas_call | solution.py:108
  9.6 1.4 %collective-permute-start.8 = (bf16[256,512]{1,0:T(8,128)(2,1)S(1)}, bf16[256,512]{1,0:T(8,128)(2,1)S(1)}, u32[]{:S(2)}, u32[]{:S(2)}) collective-permute-start(bf16[256,512]{1,0:T(8,128)(2,1)S(1)} %collective-permute-done.4.refs_5_), channel_id=1, source_target_pairs={{0,1},{2,0},{4,2},{6,4},{7,6},{5,7},{3,5},{1,3},{8,9},{10,8},{12,1... | collective-permute-start | bytes 786440 | tf_op jit(solution)/shard_map/ppermute | solution.py:55
  11.1 2.4 %collective-permute-start.5 = (f32[4,512]{1,0:T(4,128)S(1)}, f32[4,512]{1,0:T(4,128)S(1)}, u32[]{:S(2)}, u32[]{:S(2)}) collective-permute-start(f32[4,512]{1,0:T(4,128)S(1)} %bitcast.1), channel_id=1, source_target_pairs={{0,8},{8,0},{16,24},{24,16},{1,9},{9,1},{17,25},{25,17},{2,10},{10... | collective-permute-start | bytes 24584 | tf_op jit(solution)/shard_map/ppermute | solution.py:517
  13.5 2.2 %collective-permute-done.3.refs_4_ = bf16[256,512]{1,0:T(8,128)(2,1)S(1)} collective-permute-done((bf16[256,512]{1,0:T(8,128)(2,1)S(1)}, bf16[256,512]{1,0:T(8,128)(2,1)S(1)}, u32[]{:S(2)}, u32[]{:S(2)}) %collective-permute-start.3) | collective-permute-done | bytes 262176 | tf_op jit(solution)/shard_map/ppermute | solution.py:55
  15.6 0.5 collective-permute-start.13
  16.1 1.0 collective-permute-start.11
  17.1 2.6 %shard_map.102.refs_7_ = f32[3,512,512]{2,1,0:T(8,128)S(1)} custom-call(bf16[256,512]{1,0:T(8,128)(2,1)S(1)} %get-tuple-element.58.refs_0_, bf16[256,512]{1,0:T(8,128)(2,1)S(1)} %collective-permute-done.refs_1_, bf16[256,512]{1,0:T(8,128)(2,1)S(1)} %collective-permute-done.2.refs_2_, bf16[256,512]{1,0:T(8,128)(2,1)S(1)} %get-tuple-element.61.refs_3_, ...), custom_call_target="tpu_custom_call" | custom-call | flops 2415919104 | bytes 12582912 | tf_op jit(solution)/shard_map/pallas_call | solution.py:181
  19.7 0.8 collective-permute-done.8.refs_3_
  20.5 0.7 collective-permute-done.1.refs_0_
  21.2 1.3 %collective-permute-start.9 = (bf16[256,512]{1,0:T(8,128)(2,1)S(1)}, bf16[256,512]{1,0:T(8,128)(2,1)S(1)}, u32[]{:S(2)}, u32[]{:S(2)}) collective-permute-start(bf16[256,512]{1,0:T(8,128)(2,1)S(1)} %collective-permute-done.8.refs_3_), channel_id=1, source_target_pairs={{0,1},{2,0},{4,2},{6,4},{7,6},{5,7},{3,5},{1,3},{8,9},{10,8},{12,1... | collective-permute-start | bytes 786440 | tf_op jit(solution)/shard_map/ppermute | solution.py:55
  22.7 4.2 %collective-permute-done.13.refs_2_ = bf16[256,512]{1,0:T(8,128)(2,1)S(1)} collective-permute-done((bf16[256,512]{1,0:T(8,128)(2,1)S(1)}, bf16[256,512]{1,0:T(8,128)(2,1)S(1)}, u32[]{:S(2)}, u32[]{:S(2)}) %collective-permute-start.13) | collective-permute-done | bytes 262176 | tf_op jit(solution)/shard_map/ppermute | solution.py:55
  26.9 0.5 collective-permute-start.14
  27.3 1.0 collective-permute-start.12
  28.3 3.3 %collective-permute-done.9.refs_3_ = bf16[256,512]{1,0:T(8,128)(2,1)S(1)} collective-permute-done((bf16[256,512]{1,0:T(8,128)(2,1)S(1)}, bf16[256,512]{1,0:T(8,128)(2,1)S(1)}, u32[]{:S(2)}, u32[]{:S(2)}) %collective-permute-start.9) | collective-permute-done | bytes 262176 | tf_op jit(solution)/shard_map/ppermute | solution.py:55
  31.6 1.1 collective-permute-start.10
  32.7 0.3 collective-permute-start.7
  33.1 1.8 %shard_map.103.refs_7_ = f32[3,512,512]{2,1,0:T(8,128)S(1)} custom-call(bf16[256,512]{1,0:T(8,128)(2,1)S(1)} %collective-permute-done.1.refs_0_, bf16[256,512]{1,0:T(8,128)(2,1)S(1)} %collective-permute-done.11.refs_1_, bf16[256,512]{1,0:T(8,128)(2,1)S(1)} %collective-permute-done.13.refs_2_, ...), custom_call_target="tpu_custom_call", output_to_operand_aliasing={{}: (7, {})} | custom-call | flops 1610612736 | bytes 10485760 | tf_op jit(solution)/shard_map/pallas_call | solution.py:181
  34.9 3.2 %collective-permute-done.14.refs_2_ = bf16[256,512]{1,0:T(8,128)(2,1)S(1)} collective-permute-done((bf16[256,512]{1,0:T(8,128)(2,1)S(1)}, bf16[256,512]{1,0:T(8,128)(2,1)S(1)}, u32[]{:S(2)}, u32[]{:S(2)}) %collective-permute-start.14) | collective-permute-done | bytes 262176 | tf_op jit(solution)/shard_map/ppermute | solution.py:55
  38.1 1.8 %shard_map.104.refs_3_.refs_4_ = f32[3,512,512]{2,1,0:T(8,128)S(1)} custom-call(bf16[256,512]{1,0:T(8,128)(2,1)S(1)} %collective-permute-done.6.refs_0_, bf16[256,512]{1,0:T(8,128)(2,1)S(1)} %collective-permute-done.12.refs_1_, bf16[256,512]{1,0:T(8,128)(2,1)S(1)} %collective-permute-done.14.refs_2_, ...), custom_call_target="tpu_custom_call", output_to_operand_aliasing={{}: (7, {})} | custom-call | flops 1610612736 | bytes 10485760 | tf_op jit(solution)/shard_map/pallas_call | solution.py:181
  40.0 2.8 %collective-permute-done.10.refs_1_ = bf16[256,512]{1,0:T(8,128)(2,1)S(1)} collective-permute-done((bf16[256,512]{1,0:T(8,128)(2,1)S(1)}, bf16[256,512]{1,0:T(8,128)(2,1)S(1)}, u32[]{:S(2)}, u32[]{:S(2)}) %collective-permute-start.10) | collective-permute-done | bytes 262176 | tf_op jit(solution)/shard_map/ppermute | solution.py:55
  42.8 0.9 collective-permute-done.7.refs_0_
  43.7 0.9 shard_map.106
  44.6 4.9 %collective-permute-start.15 = (bf16[2,512,256]{2,1,0:T(8,128)(2,1)S(1)}, bf16[2,512,256]{2,1,0:T(8,128)(2,1)S(1)}, u32[]{:S(2)}, u32[]{:S(2)}) collective-permute-start(bf16[2,512,256]{2,1,0:T(8,128)(2,1)S(1)} %get-tuple-element.72), channel_id=1, source_target_pairs={{8,16},{9,17},{10,18},{11,19},{12,20},{13,21},{14,22},{15,23}} | collective-permute-start | bytes 1572872 | tf_op jit(solution)/shard_map/ppermute | solution.py:548
  49.6 0.5 collective-permute-start.17
  50.2 1.4 %shard_map.109.rest_0_ = f32[2,3,128,256]{3,2,1,0:T(8,128)S(1)} custom-call(bf16[2,512,512]{2,1,0:T(8,128)(2,1)S(1)} %get-tuple-element.71.kv_ref.key_ref.value_ref, bf16[2,512,512]{2,1,0:T(8,128)(2,1)S(1)} %get-tuple-element.71.kv_ref.key_ref.value_ref, f32[4,512]{1,0:T(4,128)S(1)} %bitcast.2, f32[4,128,256]{2,1,0:T(8,128)S(1)} %copy-done.1, ...), custom_call_target="tpu_custom_call" | custom-call | flops 402653184 | bytes 1572864 | tf_op jit(solution)/shard_map/pallas_call | solution.py:246
  51.6 1.4 %shard_map.110 = (f32[2,3,128,256]{3,2,1,0:T(8,128)S(1)}, bf16[2,3,128,256]{3,2,1,0:T(8,128)(2,1)S(1)}) custom-call(bf16[1,512,256]{2,1,0:T(8,128)(2,1)S(1)} %collective-permute-done.16.refs_2_.key_ref, bf16[1,512,256]{2,1,0:T(8,128)(2,1)S(1)} %collective-permute-done.17.refs_3_.value_ref, f32[4,512]{1,0:T(4,128)S(1)} %collective-permute-done.5.rate_ref, ...), custom_call_target="tpu_custom_call" | custom-call | flops 402653184 | bytes 1572864 | tf_op jit(solution)/shard_map/pallas_call | solution.py:246
  53.1 0.4 shard_map.105.q_ref
  53.6 3.8 %collective-permute-done.15._.refs_0_.refs_1_ = bf16[2,512,256]{2,1,0:T(8,128)(2,1)S(1)} collective-permute-done((bf16[2,512,256]{2,1,0:T(8,128)(2,1)S(1)}, bf16[2,512,256]{2,1,0:T(8,128)(2,1)S(1)}, u32[]{:S(2)}, u32[]{:S(2)}) %collective-permute-start.15) | collective-permute-done | bytes 524320 | tf_op jit(solution)/shard_map/ppermute | solution.py:548
  57.4 2.1 %shard_map.107 = (f32[512,512]{1,0:T(8,128)S(1)}, f32[2,512,512]{2,1,0:T(8,128)S(1)}) custom-call(bf16[1,512,512]{2,1,0:T(8,128)(2,1)S(1)} %shard_map.105.q_ref, bf16[2,512,512]{2,1,0:T(8,128)(2,1)S(1)} %get-tuple-element.71.kv_ref.key_ref.value_ref, bf16[2,512,256]{2,1,0:T(8,128)(2,1)S(1)} %collective-permute-done.15._.refs_0_.refs_1_), custom_call_target="tpu_custom_call" | custom-call | flops 402653184 | bytes 2097152 | tf_op jit(solution)/shard_map/pallas_call | solution.py:340
  59.4 4.4 %collective-permute-start.18 = (bf16[2,512,256]{2,1,0:T(8,128)(2,1)S(1)}, bf16[2,512,256]{2,1,0:T(8,128)(2,1)S(1)}, u32[]{:S(2)}, u32[]{:S(2)}) collective-permute-start(bf16[2,512,256]{2,1,0:T(8,128)(2,1)S(1)} %get-tuple-element.78), channel_id=1, source_target_pairs={{0,8},{8,16},{16,24},{1,9},{9,17},{17,25},{2,10},{10,18},{18,26},{... | collective-permute-start | bytes 1572872 | tf_op jit(solution)/shard_map/ppermute | solution.py:562
  63.8 1.4 %shard_map.108.rest_1_.attended_ref.sum_ref = f32[512,512]{1,0:T(8,128)S(1)} custom-call(f32[512,512]{1,0:T(8,128)S(1)} %get-tuple-element.73.sum_ref, f32[2,512,512]{2,1,0:T(8,128)S(1)} %get-tuple-element.74.stats_ref, bf16[1,512,512]{2,1,0:T(8,128)(2,1)S(1)} %shard_map.105.q_ref, ...), custom_call_target="tpu_custom_call", output_to_operand_aliasing={{}: (0, {})} | custom-call | flops 201326592 | bytes 1048576 | tf_op jit(solution)/shard_map/pallas_call | solution.py:380
  65.3 0.8 shard_map.111.net_ref
  66.2 0.8 shard_map.112.refs_2_.near_ref
  67.0 2.9 %collective-permute-done.18.refs_0_.refs_1_ = bf16[2,512,256]{2,1,0:T(8,128)(2,1)S(1)} collective-permute-done((bf16[2,512,256]{2,1,0:T(8,128)(2,1)S(1)}, bf16[2,512,256]{2,1,0:T(8,128)(2,1)S(1)}, u32[]{:S(2)}, u32[]{:S(2)}) %collective-permute-start.18) | collective-permute-done | bytes 524320 | tf_op jit(solution)/shard_map/ppermute | solution.py:562
  69.9 1.2 %shard_map.113.attended_ref = f32[512,512]{1,0:T(8,128)S(1)} custom-call(f32[512,512]{1,0:T(8,128)S(1)} %shard_map.108.rest_1_.attended_ref.sum_ref, f32[2,512,512]{2,1,0:T(8,128)S(1)} %get-tuple-element.74.stats_ref, bf16[1,512,512]{2,1,0:T(8,128)(2,1)S(1)} %shard_map.105.q_ref, ...), custom_call_target="tpu_custom_call", output_to_operand_aliasing={{}: (0, {})} | custom-call | flops 201326592 | bytes 1048576 | tf_op jit(solution)/shard_map/pallas_call | solution.py:380
  71.2 1.2 %shard_map.115 = (bf16[64,2048]{1,0:T(8,128)(2,1)S(1)}, bf16[64,2048]{1,0:T(8,128)(2,1)S(1)}) custom-call(bf16[1,512,512]{2,1,0:T(8,128)(2,1)S(1)} %shard_map.105.q_ref, f32[512,512]{1,0:T(8,128)S(1)} %shard_map.113.attended_ref, bf16[2,3,128,256]{3,2,1,0:T(8,128)(2,1)S(1)} %collective-permute-done.20.net_ref, ...), custom_call_target="tpu_custom_call" | custom-call | flops 268435456 | bytes 4718592 | tf_op jit(solution)/shard_map/pallas_call | solution.py:456
  72.4 1.3 %collective-permute-start.22 = (bf16[64,2048]{1,0:T(8,128)(2,1)S(1)}, bf16[64,2048]{1,0:T(8,128)(2,1)S(1)}, u32[]{:S(2)}, u32[]{:S(2)}) collective-permute-start(bf16[64,2048]{1,0:T(8,128)(2,1)S(1)} %get-tuple-element.84), channel_id=1, source_target_pairs={{0,1},{2,0},{4,2},{6,4},{7,6},{5,7},{3,5},{1,3},{8,9},{10,8},{12,1... | collective-permute-start | bytes 786440 | tf_op jit(solution)/shard_map/ppermute | solution.py:55
  73.9 1.2 %shard_map.114 = (bf16[64,2048]{1,0:T(8,128)(2,1)S(1)}, bf16[64,2048]{1,0:T(8,128)(2,1)S(1)}, bf16[64,2048]{1,0:T(8,128)(2,1)S(1)}, bf16[64,2048]{1,0:T(8,128)(2,1)S(1)}) custom-call(bf16[1,512,512]{2,1,0:T(8,128)(2,1)S(1)} %shard_map.105.q_ref, f32[512,512]{1,0:T(8,128)S(1)} %shard_map.113.attended_ref, ...), custom_call_target="tpu_custom_call" | custom-call | flops 536870912 | bytes 5242880 | tf_op jit(solution)/shard_map/pallas_call | solution.py:456
  75.1 1.4 %collective-permute-start.26 = (bf16[64,2048]{1,0:T(8,128)(2,1)S(1)}, bf16[64,2048]{1,0:T(8,128)(2,1)S(1)}, u32[]{:S(2)}, u32[]{:S(2)}) collective-permute-start(bf16[64,2048]{1,0:T(8,128)(2,1)S(1)} %get-tuple-element.88), channel_id=1, source_target_pairs={{0,1},{2,0},{4,2},{6,4},{7,6},{5,7},{3,5},{1,3},{8,9},{10,8},{12,1... | collective-permute-start | bytes 786440 | tf_op jit(solution)/shard_map/ppermute | solution.py:55
  76.7 3.8 %collective-permute-done.22.refs_1_ = bf16[64,2048]{1,0:T(8,128)(2,1)S(1)} collective-permute-done((bf16[64,2048]{1,0:T(8,128)(2,1)S(1)}, bf16[64,2048]{1,0:T(8,128)(2,1)S(1)}, u32[]{:S(2)}, u32[]{:S(2)}) %collective-permute-start.22) | collective-permute-done | bytes 262176 | tf_op jit(solution)/shard_map/ppermute | solution.py:55
  80.5 1.5 %collective-permute-done.21.refs_0_ = bf16[64,2048]{1,0:T(8,128)(2,1)S(1)} collective-permute-done((bf16[64,2048]{1,0:T(8,128)(2,1)S(1)}, bf16[64,2048]{1,0:T(8,128)(2,1)S(1)}, u32[]{:S(2)}, u32[]{:S(2)}) %collective-permute-start.21) | collective-permute-done | bytes 262176 | tf_op jit(solution)/shard_map/ppermute | solution.py:55
  82.1 1.3 %collective-permute-start.24 = (bf16[64,2048]{1,0:T(8,128)(2,1)S(1)}, bf16[64,2048]{1,0:T(8,128)(2,1)S(1)}, u32[]{:S(2)}, u32[]{:S(2)}) collective-permute-start(bf16[64,2048]{1,0:T(8,128)(2,1)S(1)} %add_convert_fusion.10), channel_id=1, source_target_pairs={{0,1},{2,0},{4,2},{6,4},{7,6},{5,7},{3,5},{1,3},{8,9},{10,8},{12,1... | collective-permute-start | bytes 786440 | tf_op jit(solution)/shard_map/ppermute | solution.py:55
  83.6 1.2 %shard_map.117 = (bf16[64,2048]{1,0:T(8,128)(2,1)S(1)}, bf16[64,2048]{1,0:T(8,128)(2,1)S(1)}, bf16[64,2048]{1,0:T(8,128)(2,1)S(1)}, bf16[64,2048]{1,0:T(8,128)(2,1)S(1)}) custom-call(bf16[1,512,512]{2,1,0:T(8,128)(2,1)S(1)} %shard_map.105.q_ref, f32[512,512]{1,0:T(8,128)S(1)} %shard_map.113.attended_ref, ...), custom_call_target="tpu_custom_call" | custom-call | flops 536870912 | bytes 5242880 | tf_op jit(solution)/shard_map/pallas_call | solution.py:456
  84.9 1.2 %collective-permute-done.26 = bf16[64,2048]{1,0:T(8,128)(2,1)S(1)} collective-permute-done((bf16[64,2048]{1,0:T(8,128)(2,1)S(1)}, bf16[64,2048]{1,0:T(8,128)(2,1)S(1)}, u32[]{:S(2)}, u32[]{:S(2)}) %collective-permute-start.26) | collective-permute-done | bytes 262176 | tf_op jit(solution)/shard_map/ppermute | solution.py:55
  86.2 1.5 %collective-permute-done.25 = bf16[64,2048]{1,0:T(8,128)(2,1)S(1)} collective-permute-done((bf16[64,2048]{1,0:T(8,128)(2,1)S(1)}, bf16[64,2048]{1,0:T(8,128)(2,1)S(1)}, u32[]{:S(2)}, u32[]{:S(2)}) %collective-permute-start.25) | collective-permute-done | bytes 262176 | tf_op jit(solution)/shard_map/ppermute | solution.py:55
  87.7 1.3 %collective-permute-start.28 = (bf16[64,2048]{1,0:T(8,128)(2,1)S(1)}, bf16[64,2048]{1,0:T(8,128)(2,1)S(1)}, u32[]{:S(2)}, u32[]{:S(2)}) collective-permute-start(bf16[64,2048]{1,0:T(8,128)(2,1)S(1)} %add_convert_fusion.8), channel_id=1, source_target_pairs={{0,1},{2,0},{4,2},{6,4},{7,6},{5,7},{3,5},{1,3},{8,9},{10,8},{12,1... | collective-permute-start | bytes 786440 | tf_op jit(solution)/shard_map/ppermute | solution.py:55
  89.2 2.5 %collective-permute-done.24.refs_1_ = bf16[64,2048]{1,0:T(8,128)(2,1)S(1)} collective-permute-done((bf16[64,2048]{1,0:T(8,128)(2,1)S(1)}, bf16[64,2048]{1,0:T(8,128)(2,1)S(1)}, u32[]{:S(2)}, u32[]{:S(2)}) %collective-permute-start.24) | collective-permute-done | bytes 262176 | tf_op jit(solution)/shard_map/ppermute | solution.py:55
  91.8 1.5 %collective-permute-done.23.refs_0_ = bf16[64,2048]{1,0:T(8,128)(2,1)S(1)} collective-permute-done((bf16[64,2048]{1,0:T(8,128)(2,1)S(1)}, bf16[64,2048]{1,0:T(8,128)(2,1)S(1)}, u32[]{:S(2)}, u32[]{:S(2)}) %collective-permute-start.23) | collective-permute-done | bytes 262176 | tf_op jit(solution)/shard_map/ppermute | solution.py:55
  93.3 1.3 %collective-permute-start.32 = (bf16[64,2048]{1,0:T(8,128)(2,1)S(1)}, bf16[64,2048]{1,0:T(8,128)(2,1)S(1)}, u32[]{:S(2)}, u32[]{:S(2)}) collective-permute-start(bf16[64,2048]{1,0:T(8,128)(2,1)S(1)} %add_convert_fusion.4), channel_id=1, source_target_pairs={{0,1},{2,0},{4,2},{6,4},{7,6},{5,7},{3,5},{1,3},{8,9},{10,8},{12,1... | collective-permute-start | bytes 786440 | tf_op jit(solution)/shard_map/ppermute | solution.py:55
  94.9 1.5 %shard_map.116 = (bf16[64,2048]{1,0:T(8,128)(2,1)S(1)}, bf16[64,2048]{1,0:T(8,128)(2,1)S(1)}, bf16[64,2048]{1,0:T(8,128)(2,1)S(1)}, bf16[64,2048]{1,0:T(8,128)(2...) custom-call(bf16[1,512,512]{2,1,0:T(8,128)(2,1)S(1)} %shard_map.105.q_ref, ...), custom_call_target="tpu_custom_call" | custom-call | flops 805306368 | bytes 5767168 | tf_op jit(solution)/shard_map/pallas_call | solution.py:456
  96.4 1.0 collective-permute-done.28
  97.4 1.5 %collective-permute-done.27 = bf16[64,2048]{1,0:T(8,128)(2,1)S(1)} collective-permute-done((bf16[64,2048]{1,0:T(8,128)(2,1)S(1)}, bf16[64,2048]{1,0:T(8,128)(2,1)S(1)}, u32[]{:S(2)}, u32[]{:S(2)}) %collective-permute-start.27) | collective-permute-done | bytes 262176 | tf_op jit(solution)/shard_map/ppermute | solution.py:55
  99.0 0.2 collective-permute-start.29
  99.2 1.3 %collective-permute-start.30 = (bf16[64,2048]{1,0:T(8,128)(2,1)S(1)}, bf16[64,2048]{1,0:T(8,128)(2,1)S(1)}, u32[]{:S(2)}, u32[]{:S(2)}) collective-permute-start(bf16[64,2048]{1,0:T(8,128)(2,1)S(1)} %add_convert_fusion.6), channel_id=1, source_target_pairs={{0,1},{2,0},{4,2},{6,4},{7,6},{5,7},{3,5},{1,3},{8,9},{10,8},{12,1... | collective-permute-start | bytes 786440 | tf_op jit(solution)/shard_map/ppermute | solution.py:55
  100.5 2.3 %collective-permute-done.32 = bf16[64,2048]{1,0:T(8,128)(2,1)S(1)} collective-permute-done((bf16[64,2048]{1,0:T(8,128)(2,1)S(1)}, bf16[64,2048]{1,0:T(8,128)(2,1)S(1)}, u32[]{:S(2)}, u32[]{:S(2)}) %collective-permute-start.32) | collective-permute-done | bytes 262176 | tf_op jit(solution)/shard_map/ppermute | solution.py:55
  102.8 1.7 %collective-permute-done.31 = bf16[64,2048]{1,0:T(8,128)(2,1)S(1)} collective-permute-done((bf16[64,2048]{1,0:T(8,128)(2,1)S(1)}, bf16[64,2048]{1,0:T(8,128)(2,1)S(1)}, u32[]{:S(2)}, u32[]{:S(2)}) %collective-permute-start.31) | collective-permute-done | bytes 262176 | tf_op jit(solution)/shard_map/ppermute | solution.py:55
  104.6 0.2 collective-permute-start.33
  104.8 1.3 %collective-permute-start.34 = (bf16[64,2048]{1,0:T(8,128)(2,1)S(1)}, bf16[64,2048]{1,0:T(8,128)(2,1)S(1)}, u32[]{:S(2)}, u32[]{:S(2)}) collective-permute-start(bf16[64,2048]{1,0:T(8,128)(2,1)S(1)} %add_convert_fusion.2), channel_id=1, source_target_pairs={{0,1},{2,0},{4,2},{6,4},{7,6},{5,7},{3,5},{1,3},{8,9},{10,8},{12,1... | collective-permute-start | bytes 786440 | tf_op jit(solution)/shard_map/ppermute | solution.py:55
  106.1 4.0 %collective-permute-done.29.refs_2_ = bf16[64,2048]{1,0:T(8,128)(2,1)S(1)} collective-permute-done((bf16[64,2048]{1,0:T(8,128)(2,1)S(1)}, bf16[64,2048]{1,0:T(8,128)(2,1)S(1)}, u32[]{:S(2)}, u32[]{:S(2)}) %collective-permute-start.29) | collective-permute-done | bytes 262176 | tf_op jit(solution)/shard_map/ppermute | solution.py:55
  110.3 2.9 %collective-permute-done.33 = bf16[64,2048]{1,0:T(8,128)(2,1)S(1)} collective-permute-done((bf16[64,2048]{1,0:T(8,128)(2,1)S(1)}, bf16[64,2048]{1,0:T(8,128)(2,1)S(1)}, u32[]{:S(2)}, u32[]{:S(2)}) %collective-permute-start.33) | collective-permute-done | bytes 262176 | tf_op jit(solution)/shard_map/ppermute | solution.py:55
  113.3 0.8 pad_maximum_fusion
  (50 shorter events, 2.6 us)
Async XLA Ops:
  1.1 8.5 %collective-permute-start.4 = (bf16[256,512]{1,0:T(8,128)(2,1)S(1)}, bf16[256,512]{1,0:T(8,128)(2,1)S(1)}, u32[]{:S(2)}, u32[]{:S(2)}) collective-permute-start(bf16[256,512]{1,0:T(8,128)(2,1)S(1)} %get-tuple-element.61.refs_3_), channel_id=1, source_target_pairs={{0,1},{2,0},{4,2},{6,4},{7,6},{5,7},{3,5},{1,3},{8,9},{10,8},{12,1... | collective-permute-start | bytes 786440 | tf_op jit(solution)/shard_map/ppermute | solution.py:55
  3.1 8.0 %copy-start.4 = (f32[512,4]{0,1:T(4,128)S(1)}, f32[512,4]{0,1:T(4,128)}, u32[]{:S(2)}) copy-start(f32[512,4]{0,1:T(4,128)} %param.18) | copy-start | bytes 24580
  3.1 7.8 %collective-permute-start = (bf16[256,512]{1,0:T(8,128)(2,1)S(1)}, bf16[256,512]{1,0:T(8,128)(2,1)S(1)}, u32[]{:S(2)}, u32[]{:S(2)}) collective-permute-start(bf16[256,512]{1,0:T(8,128)(2,1)S(1)} %get-tuple-element.58.refs_0_), channel_id=1, source_target_pairs={{0,2},{2,4},{4,6},{6,7},{7,5},{5,3},{3,1},{1,0},{8,10},{10,12},{12... | collective-permute-start | bytes 786440 | tf_op jit(solution)/shard_map/ppermute | solution.py:55
  3.3 12.3 %collective-permute-start.3 = (bf16[256,512]{1,0:T(8,128)(2,1)S(1)}, bf16[256,512]{1,0:T(8,128)(2,1)S(1)}, u32[]{:S(2)}, u32[]{:S(2)}) collective-permute-start(bf16[256,512]{1,0:T(8,128)(2,1)S(1)} %get-tuple-element.61.refs_3_), channel_id=1, source_target_pairs={{0,2},{2,4},{4,6},{6,7},{7,5},{5,3},{3,1},{1,0},{8,10},{10,12},{12... | collective-permute-start | bytes 786440 | tf_op jit(solution)/shard_map/ppermute | solution.py:55
  4.7 11.4 %collective-permute-start.2 = (bf16[256,512]{1,0:T(8,128)(2,1)S(1)}, bf16[256,512]{1,0:T(8,128)(2,1)S(1)}, u32[]{:S(2)}, u32[]{:S(2)}) collective-permute-start(bf16[256,512]{1,0:T(8,128)(2,1)S(1)} %get-tuple-element.58.refs_0_), channel_id=1, source_target_pairs={{0,1},{2,0},{4,2},{6,4},{7,6},{5,7},{3,5},{1,3},{8,9},{10,8},{12,1... | collective-permute-start | bytes 786440 | tf_op jit(solution)/shard_map/ppermute | solution.py:55
  9.6 10.9 %collective-permute-start.8 = (bf16[256,512]{1,0:T(8,128)(2,1)S(1)}, bf16[256,512]{1,0:T(8,128)(2,1)S(1)}, u32[]{:S(2)}, u32[]{:S(2)}) collective-permute-start(bf16[256,512]{1,0:T(8,128)(2,1)S(1)} %collective-permute-done.4.refs_5_), channel_id=1, source_target_pairs={{0,1},{2,0},{4,2},{6,4},{7,6},{5,7},{3,5},{1,3},{8,9},{10,8},{12,1... | collective-permute-start | bytes 786440 | tf_op jit(solution)/shard_map/ppermute | solution.py:55
  10.9 10.3 %collective-permute-start.1 = (bf16[256,512]{1,0:T(8,128)(2,1)S(1)}, bf16[256,512]{1,0:T(8,128)(2,1)S(1)}, u32[]{:S(2)}, u32[]{:S(2)}) collective-permute-start(bf16[256,512]{1,0:T(8,128)(2,1)S(1)} %collective-permute-done.refs_1_), channel_id=1, source_target_pairs={{0,2},{2,4},{4,6},{6,7},{7,5},{5,3},{3,1},{1,0},{8,10},{10,12},{12... | collective-permute-start | bytes 786440 | tf_op jit(solution)/shard_map/ppermute | solution.py:55
  11.1 8.6 %collective-permute-start.5 = (f32[4,512]{1,0:T(4,128)S(1)}, f32[4,512]{1,0:T(4,128)S(1)}, u32[]{:S(2)}, u32[]{:S(2)}) collective-permute-start(f32[4,512]{1,0:T(4,128)S(1)} %bitcast.1), channel_id=1, source_target_pairs={{0,8},{8,0},{16,24},{24,16},{1,9},{9,1},{17,25},{25,17},{2,10},{10... | collective-permute-start | bytes 24584 | tf_op jit(solution)/shard_map/ppermute | solution.py:517
  15.6 11.2 %collective-permute-start.13 = (bf16[256,512]{1,0:T(8,128)(2,1)S(1)}, bf16[256,512]{1,0:T(8,128)(2,1)S(1)}, u32[]{:S(2)}, u32[]{:S(2)}) collective-permute-start(bf16[256,512]{1,0:T(8,128)(2,1)S(1)} %collective-permute-done.3.refs_4_), channel_id=1, source_target_pairs={{0,2},{2,4},{4,6},{6,7},{7,5},{5,3},{3,1},{1,0},{8,10},{10,12},{12... | collective-permute-start | bytes 786440 | tf_op jit(solution)/shard_map/ppermute | solution.py:55
  16.1 10.8 %collective-permute-start.11 = (bf16[256,512]{1,0:T(8,128)(2,1)S(1)}, bf16[256,512]{1,0:T(8,128)(2,1)S(1)}, u32[]{:S(2)}, u32[]{:S(2)}) collective-permute-start(bf16[256,512]{1,0:T(8,128)(2,1)S(1)} %collective-permute-done.2.refs_2_), channel_id=1, source_target_pairs={{0,1},{2,0},{4,2},{6,4},{7,6},{5,7},{3,5},{1,3},{8,9},{10,8},{12,1... | collective-permute-start | bytes 786440 | tf_op jit(solution)/shard_map/ppermute | solution.py:55
  21.2 10.3 %collective-permute-start.9 = (bf16[256,512]{1,0:T(8,128)(2,1)S(1)}, bf16[256,512]{1,0:T(8,128)(2,1)S(1)}, u32[]{:S(2)}, u32[]{:S(2)}) collective-permute-start(bf16[256,512]{1,0:T(8,128)(2,1)S(1)} %collective-permute-done.8.refs_3_), channel_id=1, source_target_pairs={{0,1},{2,0},{4,2},{6,4},{7,6},{5,7},{3,5},{1,3},{8,9},{10,8},{12,1... | collective-permute-start | bytes 786440 | tf_op jit(solution)/shard_map/ppermute | solution.py:55
  22.5 10.2 %collective-permute-start.6 = (bf16[256,512]{1,0:T(8,128)(2,1)S(1)}, bf16[256,512]{1,0:T(8,128)(2,1)S(1)}, u32[]{:S(2)}, u32[]{:S(2)}) collective-permute-start(bf16[256,512]{1,0:T(8,128)(2,1)S(1)} %collective-permute-done.1.refs_0_), channel_id=1, source_target_pairs={{0,2},{2,4},{4,6},{6,7},{7,5},{5,3},{3,1},{1,0},{8,10},{10,12},{12... | collective-permute-start | bytes 786440 | tf_op jit(solution)/shard_map/ppermute | solution.py:55
  26.9 11.2 %collective-permute-start.14 = (bf16[256,512]{1,0:T(8,128)(2,1)S(1)}, bf16[256,512]{1,0:T(8,128)(2,1)S(1)}, u32[]{:S(2)}, u32[]{:S(2)}) collective-permute-start(bf16[256,512]{1,0:T(8,128)(2,1)S(1)} %collective-permute-done.13.refs_2_), channel_id=1, source_target_pairs={{0,2},{2,4},{4,6},{6,7},{7,5},{5,3},{3,1},{1,0},{8,10},{10,12},{12... | collective-permute-start | bytes 786440 | tf_op jit(solution)/shard_map/ppermute | solution.py:55
  27.3 10.8 %collective-permute-start.12 = (bf16[256,512]{1,0:T(8,128)(2,1)S(1)}, bf16[256,512]{1,0:T(8,128)(2,1)S(1)}, u32[]{:S(2)}, u32[]{:S(2)}) collective-permute-start(bf16[256,512]{1,0:T(8,128)(2,1)S(1)} %collective-permute-done.11.refs_1_), channel_id=1, source_target_pairs={{0,1},{2,0},{4,2},{6,4},{7,6},{5,7},{3,5},{1,3},{8,9},{10,8},{12,1... | collective-permute-start | bytes 786440 | tf_op jit(solution)/shard_map/ppermute | solution.py:55
  31.6 11.2 %collective-permute-start.10 = (bf16[256,512]{1,0:T(8,128)(2,1)S(1)}, bf16[256,512]{1,0:T(8,128)(2,1)S(1)}, u32[]{:S(2)}, u32[]{:S(2)}) collective-permute-start(bf16[256,512]{1,0:T(8,128)(2,1)S(1)} %collective-permute-done.9.refs_3_), channel_id=1, source_target_pairs={{0,1},{2,0},{4,2},{6,4},{7,6},{5,7},{3,5},{1,3},{8,9},{10,8},{12,1... | collective-permute-start | bytes 786440 | tf_op jit(solution)/shard_map/ppermute | solution.py:55
  32.7 11.0 %collective-permute-start.7 = (bf16[256,512]{1,0:T(8,128)(2,1)S(1)}, bf16[256,512]{1,0:T(8,128)(2,1)S(1)}, u32[]{:S(2)}, u32[]{:S(2)}) collective-permute-start(bf16[256,512]{1,0:T(8,128)(2,1)S(1)} %collective-permute-done.6.refs_0_), channel_id=1, source_target_pairs={{0,2},{2,4},{4,6},{6,7},{7,5},{5,3},{3,1},{1,0},{8,10},{10,12},{12... | collective-permute-start | bytes 786440 | tf_op jit(solution)/shard_map/ppermute | solution.py:55
  39.9 10.2 %copy-start.1 = (f32[4,128,256]{2,1,0:T(8,128)S(1)}, f32[4,128,256]{2,1,0:T(8,128)}, u32[]{:S(2)}) copy-start(f32[4,128,256]{2,1,0:T(8,128)} %gate_ref.5) | copy-start | bytes 1572868
  40.0 10.2 %copy-start.2 = (f32[4,128,256]{2,1,0:T(8,128)S(1)}, f32[4,128,256]{2,1,0:T(8,128)}, u32[]{:S(2)}) copy-start(f32[4,128,256]{2,1,0:T(8,128)} %up_ref.5) | copy-start | bytes 1572868
  40.0 10.2 %copy-start.3 = (f32[4,256,128]{2,1,0:T(8,128)S(1)}, f32[4,256,128]{2,1,0:T(8,128)}, u32[]{:S(2)}) copy-start(f32[4,256,128]{2,1,0:T(8,128)} %down_ref.5) | copy-start | bytes 1572868
  44.6 12.7 %collective-permute-start.15 = (bf16[2,512,256]{2,1,0:T(8,128)(2,1)S(1)}, bf16[2,512,256]{2,1,0:T(8,128)(2,1)S(1)}, u32[]{:S(2)}, u32[]{:S(2)}) collective-permute-start(bf16[2,512,256]{2,1,0:T(8,128)(2,1)S(1)} %get-tuple-element.72), channel_id=1, source_target_pairs={{8,16},{9,17},{10,18},{11,19},{12,20},{13,21},{14,22},{15,23}} | collective-permute-start | bytes 1572872 | tf_op jit(solution)/shard_map/ppermute | solution.py:548
  49.6 2.0 %collective-permute-start.16 = (bf16[1,512,256]{2,1,0:T(8,128)(2,1)S(1)}, bf16[1,512,256]{2,1,0:T(8,128)(2,1)S(1)}, u32[]{:S(2)}, u32[]{:S(2)}) collective-permute-start(bf16[1,512,256]{2,1,0:T(8,128)(2,1)S(1)} %get-tuple-element.75), channel_id=1, source_target_pairs={{0,8},{8,0},{16,24},{24,16},{1,9},{9,1},{17,25},{25,17},{2,10},{10... | collective-permute-start | bytes 786440 | tf_op jit(solution)/shard_map/ppermute | solution.py:517
  49.6 2.0 %collective-permute-start.17 = (bf16[1,512,256]{2,1,0:T(8,128)(2,1)S(1)}, bf16[1,512,256]{2,1,0:T(8,128)(2,1)S(1)}, u32[]{:S(2)}, u32[]{:S(2)}) collective-permute-start(bf16[1,512,256]{2,1,0:T(8,128)(2,1)S(1)} %get-tuple-element.76), channel_id=1, source_target_pairs={{0,8},{8,0},{16,24},{24,16},{1,9},{9,1},{17,25},{25,17},{2,10},{10... | collective-permute-start | bytes 786440 | tf_op jit(solution)/shard_map/ppermute | solution.py:517
  53.0 12.2 %collective-permute-start.19 = (bf16[2,3,128,256]{3,2,1,0:T(8,128)(2,1)S(1)}, bf16[2,3,128,256]{3,2,1,0:T(8,128)(2,1)S(1)}, u32[]{:S(2)}, u32[]{:S(2)}) collective-permute-start(bf16[2,3,128,256]{3,2,1,0:T(8,128)(2,1)S(1)} %get-tuple-element.80), channel_id=1, source_target_pairs={{0,16},{8,24},{16,0},{24,8},{1,17},{9,25},{17,1},{25,9},{2,18},{10... | collective-permute-start | bytes 1179656 | tf_op jit(solution)/shard_map/ppermute | solution.py:517
  53.6 11.7 %copy-start.5 = (f32[4]{0:T(128)S(1)}, f32[4]{0:T(128)}, u32[]{:S(2)}) copy-start(f32[4]{0:T(128)} %step_ref.1) | copy-start | bytes 52
  59.4 10.5 %collective-permute-start.18 = (bf16[2,512,256]{2,1,0:T(8,128)(2,1)S(1)}, bf16[2,512,256]{2,1,0:T(8,128)(2,1)S(1)}, u32[]{:S(2)}, u32[]{:S(2)}) collective-permute-start(bf16[2,512,256]{2,1,0:T(8,128)(2,1)S(1)} %get-tuple-element.78), channel_id=1, source_target_pairs={{0,8},{8,16},{16,24},{1,9},{9,17},{17,25},{2,10},{10,18},{18,26},{... | collective-permute-start | bytes 1572872 | tf_op jit(solution)/shard_map/ppermute | solution.py:562
  66.1 5.0 %copy-start = (bf16[512,4096]{1,0:T(8,128)(2,1)S(1)}, bf16[512,4096]{1,0:T(8,128)(2,1)}, u32[]{:S(2)}) copy-start(bf16[512,4096]{1,0:T(8,128)(2,1)} %w_ref.7) | copy-start | bytes 12582916
  66.1 5.0 %collective-permute-start.20 = (bf16[2,3,128,256]{3,2,1,0:T(8,128)(2,1)S(1)}, bf16[2,3,128,256]{3,2,1,0:T(8,128)(2,1)S(1)}, u32[]{:S(2)}, u32[]{:S(2)}) collective-permute-start(bf16[2,3,128,256]{3,2,1,0:T(8,128)(2,1)S(1)} %shard_map.111.net_ref), channel_id=1, source_target_pairs={{0,8},{8,0},{16,24},{24,16},{1,9},{9,1},{17,25},{25,17},{2,10},{10... | collective-permute-start | bytes 1179656 | tf_op jit(solution)/shard_map/ppermute | solution.py:517
  72.4 8.1 %collective-permute-start.22 = (bf16[64,2048]{1,0:T(8,128)(2,1)S(1)}, bf16[64,2048]{1,0:T(8,128)(2,1)S(1)}, u32[]{:S(2)}, u32[]{:S(2)}) collective-permute-start(bf16[64,2048]{1,0:T(8,128)(2,1)S(1)} %get-tuple-element.84), channel_id=1, source_target_pairs={{0,1},{2,0},{4,2},{6,4},{7,6},{5,7},{3,5},{1,3},{8,9},{10,8},{12,1... | collective-permute-start | bytes 786440 | tf_op jit(solution)/shard_map/ppermute | solution.py:55
  73.7 8.3 %collective-permute-start.21 = (bf16[64,2048]{1,0:T(8,128)(2,1)S(1)}, bf16[64,2048]{1,0:T(8,128)(2,1)S(1)}, u32[]{:S(2)}, u32[]{:S(2)}) collective-permute-start(bf16[64,2048]{1,0:T(8,128)(2,1)S(1)} %get-tuple-element.82), channel_id=1, source_target_pairs={{0,2},{2,4},{4,6},{6,7},{7,5},{5,3},{3,1},{1,0},{8,10},{10,12},{12... | collective-permute-start | bytes 786440 | tf_op jit(solution)/shard_map/ppermute | solution.py:55
  75.1 11.0 %collective-permute-start.26 = (bf16[64,2048]{1,0:T(8,128)(2,1)S(1)}, bf16[64,2048]{1,0:T(8,128)(2,1)S(1)}, u32[]{:S(2)}, u32[]{:S(2)}) collective-permute-start(bf16[64,2048]{1,0:T(8,128)(2,1)S(1)} %get-tuple-element.88), channel_id=1, source_target_pairs={{0,1},{2,0},{4,2},{6,4},{7,6},{5,7},{3,5},{1,3},{8,9},{10,8},{12,1... | collective-permute-start | bytes 786440 | tf_op jit(solution)/shard_map/ppermute | solution.py:55
  76.5 11.1 %collective-permute-start.25 = (bf16[64,2048]{1,0:T(8,128)(2,1)S(1)}, bf16[64,2048]{1,0:T(8,128)(2,1)S(1)}, u32[]{:S(2)}, u32[]{:S(2)}) collective-permute-start(bf16[64,2048]{1,0:T(8,128)(2,1)S(1)} %get-tuple-element.87), channel_id=1, source_target_pairs={{0,2},{2,4},{4,6},{6,7},{7,5},{5,3},{3,1},{1,0},{8,10},{10,12},{12... | collective-permute-start | bytes 786440 | tf_op jit(solution)/shard_map/ppermute | solution.py:55
  82.1 9.6 %collective-permute-start.24 = (bf16[64,2048]{1,0:T(8,128)(2,1)S(1)}, bf16[64,2048]{1,0:T(8,128)(2,1)S(1)}, u32[]{:S(2)}, u32[]{:S(2)}) collective-permute-start(bf16[64,2048]{1,0:T(8,128)(2,1)S(1)} %add_convert_fusion.10), channel_id=1, source_target_pairs={{0,1},{2,0},{4,2},{6,4},{7,6},{5,7},{3,5},{1,3},{8,9},{10,8},{12,1... | collective-permute-start | bytes 786440 | tf_op jit(solution)/shard_map/ppermute | solution.py:55
  83.5 9.8 %collective-permute-start.23 = (bf16[64,2048]{1,0:T(8,128)(2,1)S(1)}, bf16[64,2048]{1,0:T(8,128)(2,1)S(1)}, u32[]{:S(2)}, u32[]{:S(2)}) collective-permute-start(bf16[64,2048]{1,0:T(8,128)(2,1)S(1)} %add_convert_fusion.11), channel_id=1, source_target_pairs={{0,2},{2,4},{4,6},{6,7},{7,5},{5,3},{3,1},{1,0},{8,10},{10,12},{12... | collective-permute-start | bytes 786440 | tf_op jit(solution)/shard_map/ppermute | solution.py:55
  87.7 9.6 %collective-permute-start.28 = (bf16[64,2048]{1,0:T(8,128)(2,1)S(1)}, bf16[64,2048]{1,0:T(8,128)(2,1)S(1)}, u32[]{:S(2)}, u32[]{:S(2)}) collective-permute-start(bf16[64,2048]{1,0:T(8,128)(2,1)S(1)} %add_convert_fusion.8), channel_id=1, source_target_pairs={{0,1},{2,0},{4,2},{6,4},{7,6},{5,7},{3,5},{1,3},{8,9},{10,8},{12,1... | collective-permute-start | bytes 786440 | tf_op jit(solution)/shard_map/ppermute | solution.py:55
  89.1 9.8 %collective-permute-start.27 = (bf16[64,2048]{1,0:T(8,128)(2,1)S(1)}, bf16[64,2048]{1,0:T(8,128)(2,1)S(1)}, u32[]{:S(2)}, u32[]{:S(2)}) collective-permute-start(bf16[64,2048]{1,0:T(8,128)(2,1)S(1)} %add_convert_fusion.9), channel_id=1, source_target_pairs={{0,2},{2,4},{4,6},{6,7},{7,5},{5,3},{3,1},{1,0},{8,10},{10,12},{12... | collective-permute-start | bytes 786440 | tf_op jit(solution)/shard_map/ppermute | solution.py:55
  93.3 9.4 %collective-permute-start.32 = (bf16[64,2048]{1,0:T(8,128)(2,1)S(1)}, bf16[64,2048]{1,0:T(8,128)(2,1)S(1)}, u32[]{:S(2)}, u32[]{:S(2)}) collective-permute-start(bf16[64,2048]{1,0:T(8,128)(2,1)S(1)} %add_convert_fusion.4), channel_id=1, source_target_pairs={{0,1},{2,0},{4,2},{6,4},{7,6},{5,7},{3,5},{1,3},{8,9},{10,8},{12,1... | collective-permute-start | bytes 786440 | tf_op jit(solution)/shard_map/ppermute | solution.py:55
  94.7 9.8 %collective-permute-start.31 = (bf16[64,2048]{1,0:T(8,128)(2,1)S(1)}, bf16[64,2048]{1,0:T(8,128)(2,1)S(1)}, u32[]{:S(2)}, u32[]{:S(2)}) collective-permute-start(bf16[64,2048]{1,0:T(8,128)(2,1)S(1)} %add_convert_fusion.5), channel_id=1, source_target_pairs={{0,2},{2,4},{4,6},{6,7},{7,5},{5,3},{3,1},{1,0},{8,10},{10,12},{12... | collective-permute-start | bytes 786440 | tf_op jit(solution)/shard_map/ppermute | solution.py:55
  99.0 11.2 %collective-permute-start.29 = (bf16[64,2048]{1,0:T(8,128)(2,1)S(1)}, bf16[64,2048]{1,0:T(8,128)(2,1)S(1)}, u32[]{:S(2)}, u32[]{:S(2)}) collective-permute-start(bf16[64,2048]{1,0:T(8,128)(2,1)S(1)} %add_convert_fusion.7), channel_id=1, source_target_pairs={{0,2},{2,4},{4,6},{6,7},{7,5},{5,3},{3,1},{1,0},{8,10},{10,12},{12... | collective-permute-start | bytes 786440 | tf_op jit(solution)/shard_map/ppermute | solution.py:55
  99.2 11.0 %collective-permute-start.30 = (bf16[64,2048]{1,0:T(8,128)(2,1)S(1)}, bf16[64,2048]{1,0:T(8,128)(2,1)S(1)}, u32[]{:S(2)}, u32[]{:S(2)}) collective-permute-start(bf16[64,2048]{1,0:T(8,128)(2,1)S(1)} %add_convert_fusion.6), channel_id=1, source_target_pairs={{0,1},{2,0},{4,2},{6,4},{7,6},{5,7},{3,5},{1,3},{8,9},{10,8},{12,1... | collective-permute-start | bytes 786440 | tf_op jit(solution)/shard_map/ppermute | solution.py:55
  104.6 8.6 %collective-permute-start.33 = (bf16[64,2048]{1,0:T(8,128)(2,1)S(1)}, bf16[64,2048]{1,0:T(8,128)(2,1)S(1)}, u32[]{:S(2)}, u32[]{:S(2)}) collective-permute-start(bf16[64,2048]{1,0:T(8,128)(2,1)S(1)} %add_convert_fusion.3), channel_id=1, source_target_pairs={{0,2},{2,4},{4,6},{6,7},{7,5},{5,3},{3,1},{1,0},{8,10},{10,12},{12... | collective-permute-start | bytes 786440 | tf_op jit(solution)/shard_map/ppermute | solution.py:55
  104.8 8.4 %collective-permute-start.34 = (bf16[64,2048]{1,0:T(8,128)(2,1)S(1)}, bf16[64,2048]{1,0:T(8,128)(2,1)S(1)}, u32[]{:S(2)}, u32[]{:S(2)}) collective-permute-start(bf16[64,2048]{1,0:T(8,128)(2,1)S(1)} %add_convert_fusion.2), channel_id=1, source_target_pairs={{0,1},{2,0},{4,2},{6,4},{7,6},{5,7},{3,5},{1,3},{8,9},{10,8},{12,1... | collective-permute-start | bytes 786440 | tf_op jit(solution)/shard_map/ppermute | solution.py:55

commit v9 on v7

--- a/solution.py
+++ b/solution.py
@@ -78,10 +78,12 @@
     return pltpu.with_memory_space_constraint(array, pltpu.HBM)
 
 
-def run_copies(copies):
-    for copy in copies:
+def run_copies(copies, most):
+    for index, copy in enumerate(copies):
+        if index >= most:
+            copies[index - most].wait()
         copy.start()
-    for copy in copies:
+    for copy in copies[-most:]:
         copy.wait()
 
 
@@ -102,7 +104,8 @@
                 )
                 for block in range(blocks)
                 for index in range(count)
-            ]
+            ],
+            4,
         )
 
     return call(
@@ -125,7 +128,8 @@
             [
                 pltpu.make_async_copy(in_ref.at[pl.ds(c * rows, rows)], out_refs[c], sems.at[c])
                 for c in range(CHUNKS)
-            ]
+            ],
+            CHUNKS,
         )
 
     return call(
@@ -471,8 +475,9 @@
     ordered = ()
     for which in range(2 * steps - 1):
         step, half = steps - (which + 1) // 2, which % 2
-        if which == 2:
-            parts |= partial_out(signed[2:] + [0], *shared, tuple(coming.values())[:2])
+        if which % 2 == 0 and 2 <= which <= 2 * (steps - 2):
+            later = signed[which : which + 2] + [0] * (which == 2 * (steps - 2))
+            parts |= partial_out(later, *shared, tuple(coming.values())[:2])
         terms = []
         for way in (1, -1):
             side = half if way == 1 else 1 - half

time: 114 us -> 114 us (level)
  waiting for transfers between devices: 53.2 us -> 49.5 us
  Pallas kernels: 27.1 us -> 30.5 us
    ppermute x28, waiting for transfers between devices: 43.5 us -> 39.8 us  [ring_send(): lax.ppermute(value, 'head', [(order[i], order[(i + step) % count]) for i...]
    pallas_call x1, Pallas kernels: 4.78 us -> 7.47 us  [load(): call(body, [IN_HBM] * count, [WHOLE] * count, [jax.ShapeDtypeStruct(array...]
    pallas_call x3 -> x4, Pallas kernels: 4.55 us -> 5.2 us  [partial_out(): call(body, [WHOLE] * 5 + [AFTER] * len(after), [WHOLE] * (2 * count), [ja...]
  transfers between devices with their start and end apart: 34 -> 34, of which waited for: 23 -> 21; matrix products, arithmetic and copies ran while one was open for 1% -> 1% of each run, Pallas kernels for 21% -> 24%
where the time goes in v9:
time: 114 us; the launch traced here: 113 us
  waiting for transfers between devices  49.5 us (43%)
  starting transfers between devices  31.5 us (28%)
  Pallas kernels  30.5 us (27%)
  other arithmetic  1.59 us (1%)
    ppermute x28, waiting for transfers between devices, ring_send(): lax.ppermute(value, 'head', [(order[i], order[(i + step) % count]) for i...  39.8 us
    ppermute x28, starting transfers between devices, ring_send(): lax.ppermute(value, 'head', [(order[i], order[(i + step) % count]) for i...  22 us
    pallas_call x5, Pallas kernels, accumulate(): call(body, [WHOLE] * len(args), [WHOLE] * (1 + 2 * shared), [jax.ShapeDty...  7.65 us
    pallas_call x1, Pallas kernels, load(): call(body, [IN_HBM] * count, [WHOLE] * count, [jax.ShapeDtypeStruct(array...  7.47 us
    pallas_call x4, Pallas kernels, partial_out(): call(body, [WHOLE] * 5 + [AFTER] * len(after), [WHOLE] * (2 * count), [ja...  5.2 us
    ppermute x4, waiting for transfers between devices, swap(): lax.ppermute(value, 'tok', [(index, index ^ bit) for index in range(count)])  4.61 us
    ppermute x4, starting transfers between devices, swap(): lax.ppermute(value, 'tok', [(index, index ^ bit) for index in range(count)])  4.51 us
    ppermute x1, waiting for transfers between devices, shards(): lax.ppermute(near, 'tok', [(index, index + 1) for index in range(tok_coun...  3.89 us
  transfers between devices with their start and end apart: 34, of which 21 were waited for; matrix products, arithmetic and copies ran while one was open for 1% of the time, Pallas kernels for 24%

profile of v9, /device:TPU:1, one launch (start us, length us, event | category | flops | bytes accessed | tf_op | source)
XLA Modules:
  0.0 113.4 jit_solution(12980523824154148846)
XLA Ops:
  0.0 1.0 shard_map.100
  1.1 2.1 %collective-permute-start.4 = (bf16[256,512]{1,0:T(8,128)(2,1)S(1)}, bf16[256,512]{1,0:T(8,128)(2,1)S(1)}, u32[]{:S(2)}, u32[]{:S(2)}) collective-permute-start(bf16[256,512]{1,0:T(8,128)(2,1)S(1)} %get-tuple-element.59.refs_3_), channel_id=1, source_target_pairs={{0,1},{2,0},{4,2},{6,4},{7,6},{5,7},{3,5},{1,3},{8,9},{10,8},{12,1... | collective-permute-start | bytes 786440 | tf_op jit(solution)/shard_map/ppermute | solution.py:55
  3.3 1.4 %collective-permute-start.3 = (bf16[256,512]{1,0:T(8,128)(2,1)S(1)}, bf16[256,512]{1,0:T(8,128)(2,1)S(1)}, u32[]{:S(2)}, u32[]{:S(2)}) collective-permute-start(bf16[256,512]{1,0:T(8,128)(2,1)S(1)} %get-tuple-element.59.refs_3_), channel_id=1, source_target_pairs={{0,2},{2,4},{4,6},{6,7},{7,5},{5,3},{3,1},{1,0},{8,10},{10,12},{12... | collective-permute-start | bytes 786440 | tf_op jit(solution)/shard_map/ppermute | solution.py:55
  4.8 7.5 %shard_map.101 = (bf16[4096,512]{1,0:T(8,128)(2,1)S(1)}, bf16[4096,512]{1,0:T(8,128)(2,1)S(1)}, bf16[4096,512]{1,0:T(8,128)(2,1)S(1)}) custom-call(bf16[4096,512]{1,0:T(8,128)(2,1)} %refs_0_.1, bf16[4096,512]{1,0:T(8,128)(2,1)} %refs_1_.1, bf16[4096,512]{1,0:T(8,128)(2,1)} %refs_2_.1), custom_call_target="tpu_custom_call" | custom-call | bytes 25165824 | tf_op jit(solution)/shard_map/pallas_call | solution.py:111
  12.3 1.4 %collective-permute-start.8 = (bf16[256,512]{1,0:T(8,128)(2,1)S(1)}, bf16[256,512]{1,0:T(8,128)(2,1)S(1)}, u32[]{:S(2)}, u32[]{:S(2)}) collective-permute-start(bf16[256,512]{1,0:T(8,128)(2,1)S(1)} %collective-permute-done.4.refs_5_), channel_id=1, source_target_pairs={{0,1},{2,0},{4,2},{6,4},{7,6},{5,7},{3,5},{1,3},{8,9},{10,8},{12,1... | collective-permute-start | bytes 786440 | tf_op jit(solution)/shard_map/ppermute | solution.py:55
  13.8 2.1 %collective-permute-start.5 = (f32[4,512]{1,0:T(4,128)S(1)}, f32[4,512]{1,0:T(4,128)S(1)}, u32[]{:S(2)}, u32[]{:S(2)}) collective-permute-start(f32[4,512]{1,0:T(4,128)S(1)} %bitcast.1), channel_id=1, source_target_pairs={{0,8},{8,0},{16,24},{24,16},{1,9},{9,1},{17,25},{25,17},{2,10},{10... | collective-permute-start | bytes 24584 | tf_op jit(solution)/shard_map/ppermute | solution.py:518
  15.9 1.7 %collective-permute-start.13 = (bf16[256,512]{1,0:T(8,128)(2,1)S(1)}, bf16[256,512]{1,0:T(8,128)(2,1)S(1)}, u32[]{:S(2)}, u32[]{:S(2)}) collective-permute-start(bf16[256,512]{1,0:T(8,128)(2,1)S(1)} %collective-permute-done.3.refs_4_), channel_id=1, source_target_pairs={{0,2},{2,4},{4,6},{6,7},{7,5},{5,3},{3,1},{1,0},{8,10},{10,12},{12... | collective-permute-start | bytes 786440 | tf_op jit(solution)/shard_map/ppermute | solution.py:55
  17.5 2.6 %shard_map.102.refs_7_ = f32[3,512,512]{2,1,0:T(8,128)S(1)} custom-call(bf16[256,512]{1,0:T(8,128)(2,1)S(1)} %get-tuple-element.56.refs_0_, bf16[256,512]{1,0:T(8,128)(2,1)S(1)} %collective-permute-done.refs_1_, bf16[256,512]{1,0:T(8,128)(2,1)S(1)} %collective-permute-done.2.refs_2_, bf16[256,512]{1,0:T(8,128)(2,1)S(1)} %get-tuple-element.59.refs_3_, ...), custom_call_target="tpu_custom_call" | custom-call | flops 2415919104 | bytes 12582912 | tf_op jit(solution)/shard_map/pallas_call | solution.py:184
  20.2 0.7 collective-permute-done.1.refs_0_
  20.9 1.3 %collective-permute-start.9 = (bf16[256,512]{1,0:T(8,128)(2,1)S(1)}, bf16[256,512]{1,0:T(8,128)(2,1)S(1)}, u32[]{:S(2)}, u32[]{:S(2)}) collective-permute-start(bf16[256,512]{1,0:T(8,128)(2,1)S(1)} %collective-permute-done.8.refs_3_), channel_id=1, source_target_pairs={{0,1},{2,0},{4,2},{6,4},{7,6},{5,7},{3,5},{1,3},{8,9},{10,8},{12,1... | collective-permute-start | bytes 786440 | tf_op jit(solution)/shard_map/ppermute | solution.py:55
  22.3 4.2 %collective-permute-done.13.refs_2_ = bf16[256,512]{1,0:T(8,128)(2,1)S(1)} collective-permute-done((bf16[256,512]{1,0:T(8,128)(2,1)S(1)}, bf16[256,512]{1,0:T(8,128)(2,1)S(1)}, u32[]{:S(2)}, u32[]{:S(2)}) %collective-permute-start.13) | collective-permute-done | bytes 262176 | tf_op jit(solution)/shard_map/ppermute | solution.py:55
  26.5 0.7 collective-permute-start.14
  27.2 0.7 collective-permute-start.12
  28.0 3.4 %collective-permute-done.9.refs_3_ = bf16[256,512]{1,0:T(8,128)(2,1)S(1)} collective-permute-done((bf16[256,512]{1,0:T(8,128)(2,1)S(1)}, bf16[256,512]{1,0:T(8,128)(2,1)S(1)}, u32[]{:S(2)}, u32[]{:S(2)}) %collective-permute-start.9) | collective-permute-done | bytes 262176 | tf_op jit(solution)/shard_map/ppermute | solution.py:55
  31.3 1.0 collective-permute-start.10
  32.4 0.5 collective-permute-start.7
  32.9 1.8 %shard_map.103.refs_7_ = f32[3,512,512]{2,1,0:T(8,128)S(1)} custom-call(bf16[256,512]{1,0:T(8,128)(2,1)S(1)} %collective-permute-done.1.refs_0_, bf16[256,512]{1,0:T(8,128)(2,1)S(1)} %collective-permute-done.11.refs_1_, bf16[256,512]{1,0:T(8,128)(2,1)S(1)} %collective-permute-done.13.refs_2_, ...), custom_call_target="tpu_custom_call", output_to_operand_aliasing={{}: (7, {})} | custom-call | flops 1610612736 | bytes 10485760 | tf_op jit(solution)/shard_map/pallas_call | solution.py:184
  34.7 3.0 %collective-permute-done.14.refs_2_ = bf16[256,512]{1,0:T(8,128)(2,1)S(1)} collective-permute-done((bf16[256,512]{1,0:T(8,128)(2,1)S(1)}, bf16[256,512]{1,0:T(8,128)(2,1)S(1)}, u32[]{:S(2)}, u32[]{:S(2)}) %collective-permute-start.14) | collective-permute-done | bytes 262176 | tf_op jit(solution)/shard_map/ppermute | solution.py:55
  37.7 1.8 %shard_map.104.refs_3_.refs_4_ = f32[3,512,512]{2,1,0:T(8,128)S(1)} custom-call(bf16[256,512]{1,0:T(8,128)(2,1)S(1)} %collective-permute-done.6.refs_0_, bf16[256,512]{1,0:T(8,128)(2,1)S(1)} %collective-permute-done.12.refs_1_, bf16[256,512]{1,0:T(8,128)(2,1)S(1)} %collective-permute-done.14.refs_2_, ...), custom_call_target="tpu_custom_call", output_to_operand_aliasing={{}: (7, {})} | custom-call | flops 1610612736 | bytes 10485760 | tf_op jit(solution)/shard_map/pallas_call | solution.py:184
  39.6 2.8 %collective-permute-done.10.refs_1_ = bf16[256,512]{1,0:T(8,128)(2,1)S(1)} collective-permute-done((bf16[256,512]{1,0:T(8,128)(2,1)S(1)}, bf16[256,512]{1,0:T(8,128)(2,1)S(1)}, u32[]{:S(2)}, u32[]{:S(2)}) %collective-permute-start.10) | collective-permute-done | bytes 262176 | tf_op jit(solution)/shard_map/ppermute | solution.py:55
  42.4 0.9 collective-permute-done.7.refs_0_
  43.3 0.9 shard_map.106
  44.3 2.3 %collective-permute-start.16 = (bf16[2,512,256]{2,1,0:T(8,128)(2,1)S(1)}, bf16[2,512,256]{2,1,0:T(8,128)(2,1)S(1)}, u32[]{:S(2)}, u32[]{:S(2)}) collective-permute-start(bf16[2,512,256]{2,1,0:T(8,128)(2,1)S(1)} %get-tuple-element.72), channel_id=1, source_target_pairs={{0,8},{8,0},{16,24},{24,16},{1,9},{9,1},{17,25},{25,17},{2,10},{10... | collective-permute-start | bytes 1572872 | tf_op jit(solution)/shard_map/ppermute | solution.py:518
  46.6 3.1 %collective-permute-start.15 = (bf16[2,512,256]{2,1,0:T(8,128)(2,1)S(1)}, bf16[2,512,256]{2,1,0:T(8,128)(2,1)S(1)}, u32[]{:S(2)}, u32[]{:S(2)}) collective-permute-start(bf16[2,512,256]{2,1,0:T(8,128)(2,1)S(1)} %get-tuple-element.72), channel_id=1, source_target_pairs={{8,16},{9,17},{10,18},{11,19},{12,20},{13,21},{14,22},{15,23}} | collective-permute-start | bytes 1572872 | tf_op jit(solution)/shard_map/ppermute | solution.py:549
  49.7 1.4 %shard_map.109.rest_0_ = f32[2,3,128,256]{3,2,1,0:T(8,128)S(1)} custom-call(bf16[2,512,512]{2,1,0:T(8,128)(2,1)S(1)} %get-tuple-element.69.kv_ref, f32[4,512]{1,0:T(4,128)S(1)} %bitcast.2, f32[4,128,256]{2,1,0:T(8,128)S(1)} %copy-done.1, f32[4,128,256]{2,1,0:T(8,128)S(1)} %copy-done.2, f32[4,256,128]{2,1,0:T(8,128)S(1)} %copy-done.3), custom_call_target="tpu_custom_call" | custom-call | flops 402653184 | bytes 1572864 | tf_op jit(solution)/shard_map/pallas_call | solution.py:248
  51.1 1.4 %shard_map.110 = (f32[2,3,128,256]{3,2,1,0:T(8,128)S(1)}, bf16[2,3,128,256]{3,2,1,0:T(8,128)(2,1)S(1)}) custom-call(bf16[2,512,256]{2,1,0:T(8,128)(2,1)S(1)} %collective-permute-done.16.refs_1_.kv_ref, f32[4,512]{1,0:T(4,128)S(1)} %collective-permute-done.5.rate_ref, f32[4,128,256]{2,1,0:T(8,128)S(1)} %copy-done.1, f32[4,128,256]{2,1,0:T(8,128)S(1)} %copy-done.2, ...), custom_call_target="tpu_custom_call" | custom-call | flops 402653184 | bytes 1572864 | tf_op jit(solution)/shard_map/pallas_call | solution.py:248
  52.6 0.4 shard_map.105.q_ref
  53.1 2.1 %shard_map.107 = (f32[512,512]{1,0:T(8,128)S(1)}, f32[2,512,512]{2,1,0:T(8,128)S(1)}) custom-call(bf16[1,512,512]{2,1,0:T(8,128)(2,1)S(1)} %shard_map.105.q_ref, bf16[2,512,512]{2,1,0:T(8,128)(2,1)S(1)} %get-tuple-element.69.kv_ref), custom_call_target="tpu_custom_call" | custom-call | flops 402653184 | bytes 2097152 | tf_op jit(solution)/shard_map/pallas_call | solution.py:341
  55.2 1.9 %collective-permute-start.17 = (bf16[2,512,256]{2,1,0:T(8,128)(2,1)S(1)}, bf16[2,512,256]{2,1,0:T(8,128)(2,1)S(1)}, u32[]{:S(2)}, u32[]{:S(2)}) collective-permute-start(bf16[2,512,256]{2,1,0:T(8,128)(2,1)S(1)} %get-tuple-element.74), channel_id=1, source_target_pairs={{0,8},{8,16},{16,24},{1,9},{9,17},{17,25},{2,10},{10,18},{18,26},{... | collective-permute-start | bytes 1572872 | tf_op jit(solution)/shard_map/ppermute | solution.py:563
  57.1 1.2 %collective-permute-done.15.refs_0_ = bf16[2,512,256]{2,1,0:T(8,128)(2,1)S(1)} collective-permute-done((bf16[2,512,256]{2,1,0:T(8,128)(2,1)S(1)}, bf16[2,512,256]{2,1,0:T(8,128)(2,1)S(1)}, u32[]{:S(2)}, u32[]{:S(2)}) %collective-permute-start.15) | collective-permute-done | bytes 524320 | tf_op jit(solution)/shard_map/ppermute | solution.py:549
  58.3 1.2 %shard_map.108.rest_1_.attended_ref.sum_ref = f32[512,512]{1,0:T(8,128)S(1)} custom-call(f32[512,512]{1,0:T(8,128)S(1)} %get-tuple-element.70.sum_ref, f32[2,512,512]{2,1,0:T(8,128)S(1)} %get-tuple-element.71.stats_ref, bf16[1,512,512]{2,1,0:T(8,128)(2,1)S(1)} %shard_map.105.q_ref, ...), custom_call_target="tpu_custom_call", output_to_operand_aliasing={{}: (0, {})} | custom-call | flops 201326592 | bytes 1048576 | tf_op jit(solution)/shard_map/pallas_call | solution.py:381
  59.6 4.6 %collective-permute-done.18.rest_0_ = bf16[2,3,128,256]{3,2,1,0:T(8,128)(2,1)S(1)} collective-permute-done((bf16[2,3,128,256]{3,2,1,0:T(8,128)(2,1)S(1)}, bf16[2,3,128,256]{3,2,1,0:T(8,128)(2,1)S(1)}, u32[]{:S(2)}, u32[]{:S(2)}) %collective-permute-start.18) | collective-permute-done | bytes 393248 | tf_op jit(solution)/shard_map/ppermute | solution.py:518
  64.2 0.8 shard_map.111.net_ref
  65.1 0.8 shard_map.112.refs_1_.near_ref
  65.9 3.9 %collective-permute-done.17.refs_0_ = bf16[2,512,256]{2,1,0:T(8,128)(2,1)S(1)} collective-permute-done((bf16[2,512,256]{2,1,0:T(8,128)(2,1)S(1)}, bf16[2,512,256]{2,1,0:T(8,128)(2,1)S(1)}, u32[]{:S(2)}, u32[]{:S(2)}) %collective-permute-start.17) | collective-permute-done | bytes 524320 | tf_op jit(solution)/shard_map/ppermute | solution.py:563
  69.8 1.2 %shard_map.113.attended_ref = f32[512,512]{1,0:T(8,128)S(1)} custom-call(f32[512,512]{1,0:T(8,128)S(1)} %shard_map.108.rest_1_.attended_ref.sum_ref, f32[2,512,512]{2,1,0:T(8,128)S(1)} %get-tuple-element.71.stats_ref, bf16[1,512,512]{2,1,0:T(8,128)(2,1)S(1)} %shard_map.105.q_ref, ...), custom_call_target="tpu_custom_call", output_to_operand_aliasing={{}: (0, {})} | custom-call | flops 201326592 | bytes 1048576 | tf_op jit(solution)/shard_map/pallas_call | solution.py:381
  71.0 1.2 %shard_map.115 = (bf16[64,2048]{1,0:T(8,128)(2,1)S(1)}, bf16[64,2048]{1,0:T(8,128)(2,1)S(1)}) custom-call(bf16[1,512,512]{2,1,0:T(8,128)(2,1)S(1)} %shard_map.105.q_ref, f32[512,512]{1,0:T(8,128)S(1)} %shard_map.113.attended_ref, bf16[2,3,128,256]{3,2,1,0:T(8,128)(2,1)S(1)} %collective-permute-done.19.net_ref, ...), custom_call_target="tpu_custom_call" | custom-call | flops 268435456 | bytes 4718592 | tf_op jit(solution)/shard_map/pallas_call | solution.py:457
  72.2 1.3 %collective-permute-start.21 = (bf16[64,2048]{1,0:T(8,128)(2,1)S(1)}, bf16[64,2048]{1,0:T(8,128)(2,1)S(1)}, u32[]{:S(2)}, u32[]{:S(2)}) collective-permute-start(bf16[64,2048]{1,0:T(8,128)(2,1)S(1)} %get-tuple-element.80), channel_id=1, source_target_pairs={{0,1},{2,0},{4,2},{6,4},{7,6},{5,7},{3,5},{1,3},{8,9},{10,8},{12,1... | collective-permute-start | bytes 786440 | tf_op jit(solution)/shard_map/ppermute | solution.py:55
  73.6 0.2 collective-permute-start.20
  73.7 1.2 %shard_map.114 = (bf16[64,2048]{1,0:T(8,128)(2,1)S(1)}, bf16[64,2048]{1,0:T(8,128)(2,1)S(1)}, bf16[64,2048]{1,0:T(8,128)(2,1)S(1)}, bf16[64,2048]{1,0:T(8,128)(2,1)S(1)}) custom-call(bf16[1,512,512]{2,1,0:T(8,128)(2,1)S(1)} %shard_map.105.q_ref, f32[512,512]{1,0:T(8,128)S(1)} %shard_map.113.attended_ref, ...), custom_call_target="tpu_custom_call" | custom-call | flops 536870912 | bytes 5242880 | tf_op jit(solution)/shard_map/pallas_call | solution.py:457
  75.0 1.3 %collective-permute-start.25 = (bf16[64,2048]{1,0:T(8,128)(2,1)S(1)}, bf16[64,2048]{1,0:T(8,128)(2,1)S(1)}, u32[]{:S(2)}, u32[]{:S(2)}) collective-permute-start(bf16[64,2048]{1,0:T(8,128)(2,1)S(1)} %get-tuple-element.84), channel_id=1, source_target_pairs={{0,1},{2,0},{4,2},{6,4},{7,6},{5,7},{3,5},{1,3},{8,9},{10,8},{12,1... | collective-permute-start | bytes 786440 | tf_op jit(solution)/shard_map/ppermute | solution.py:55
  76.3 0.2 collective-permute-start.24
  76.5 4.1 %collective-permute-done.21.refs_1_ = bf16[64,2048]{1,0:T(8,128)(2,1)S(1)} collective-permute-done((bf16[64,2048]{1,0:T(8,128)(2,1)S(1)}, bf16[64,2048]{1,0:T(8,128)(2,1)S(1)}, u32[]{:S(2)}, u32[]{:S(2)}) %collective-permute-start.21) | collective-permute-done | bytes 262176 | tf_op jit(solution)/shard_map/ppermute | solution.py:55
  80.7 1.2 %collective-permute-done.20.refs_0_ = bf16[64,2048]{1,0:T(8,128)(2,1)S(1)} collective-permute-done((bf16[64,2048]{1,0:T(8,128)(2,1)S(1)}, bf16[64,2048]{1,0:T(8,128)(2,1)S(1)}, u32[]{:S(2)}, u32[]{:S(2)}) %collective-permute-start.20) | collective-permute-done | bytes 262176 | tf_op jit(solution)/shard_map/ppermute | solution.py:55
  82.0 1.3 %collective-permute-start.23 = (bf16[64,2048]{1,0:T(8,128)(2,1)S(1)}, bf16[64,2048]{1,0:T(8,128)(2,1)S(1)}, u32[]{:S(2)}, u32[]{:S(2)}) collective-permute-start(bf16[64,2048]{1,0:T(8,128)(2,1)S(1)} %add_convert_fusion.10), channel_id=1, source_target_pairs={{0,1},{2,0},{4,2},{6,4},{7,6},{5,7},{3,5},{1,3},{8,9},{10,8},{12,1... | collective-permute-start | bytes 786440 | tf_op jit(solution)/shard_map/ppermute | solution.py:55
  83.5 1.2 %shard_map.117 = (bf16[64,2048]{1,0:T(8,128)(2,1)S(1)}, bf16[64,2048]{1,0:T(8,128)(2,1)S(1)}, bf16[64,2048]{1,0:T(8,128)(2,1)S(1)}, bf16[64,2048]{1,0:T(8,128)(2,1)S(1)}) custom-call(bf16[1,512,512]{2,1,0:T(8,128)(2,1)S(1)} %shard_map.105.q_ref, f32[512,512]{1,0:T(8,128)S(1)} %shard_map.113.attended_ref, ...), custom_call_target="tpu_custom_call" | custom-call | flops 536870912 | bytes 5242880 | tf_op jit(solution)/shard_map/pallas_call | solution.py:457
  84.7 1.5 %collective-permute-done.25 = bf16[64,2048]{1,0:T(8,128)(2,1)S(1)} collective-permute-done((bf16[64,2048]{1,0:T(8,128)(2,1)S(1)}, bf16[64,2048]{1,0:T(8,128)(2,1)S(1)}, u32[]{:S(2)}, u32[]{:S(2)}) %collective-permute-start.25) | collective-permute-done | bytes 262176 | tf_op jit(solution)/shard_map/ppermute | solution.py:55
  86.3 1.2 %collective-permute-done.24 = bf16[64,2048]{1,0:T(8,128)(2,1)S(1)} collective-permute-done((bf16[64,2048]{1,0:T(8,128)(2,1)S(1)}, bf16[64,2048]{1,0:T(8,128)(2,1)S(1)}, u32[]{:S(2)}, u32[]{:S(2)}) %collective-permute-start.24) | collective-permute-done | bytes 262176 | tf_op jit(solution)/shard_map/ppermute | solution.py:55
  87.6 1.3 %collective-permute-start.27 = (bf16[64,2048]{1,0:T(8,128)(2,1)S(1)}, bf16[64,2048]{1,0:T(8,128)(2,1)S(1)}, u32[]{:S(2)}, u32[]{:S(2)}) collective-permute-start(bf16[64,2048]{1,0:T(8,128)(2,1)S(1)} %add_convert_fusion.8), channel_id=1, source_target_pairs={{0,1},{2,0},{4,2},{6,4},{7,6},{5,7},{3,5},{1,3},{8,9},{10,8},{12,1... | collective-permute-start | bytes 786440 | tf_op jit(solution)/shard_map/ppermute | solution.py:55
  89.1 2.7 %collective-permute-done.23.refs_1_ = bf16[64,2048]{1,0:T(8,128)(2,1)S(1)} collective-permute-done((bf16[64,2048]{1,0:T(8,128)(2,1)S(1)}, bf16[64,2048]{1,0:T(8,128)(2,1)S(1)}, u32[]{:S(2)}, u32[]{:S(2)}) %collective-permute-start.23) | collective-permute-done | bytes 262176 | tf_op jit(solution)/shard_map/ppermute | solution.py:55
  91.9 1.2 %collective-permute-done.22.refs_0_ = bf16[64,2048]{1,0:T(8,128)(2,1)S(1)} collective-permute-done((bf16[64,2048]{1,0:T(8,128)(2,1)S(1)}, bf16[64,2048]{1,0:T(8,128)(2,1)S(1)}, u32[]{:S(2)}, u32[]{:S(2)}) %collective-permute-start.22) | collective-permute-done | bytes 262176 | tf_op jit(solution)/shard_map/ppermute | solution.py:55
  93.2 1.3 %collective-permute-start.31 = (bf16[64,2048]{1,0:T(8,128)(2,1)S(1)}, bf16[64,2048]{1,0:T(8,128)(2,1)S(1)}, u32[]{:S(2)}, u32[]{:S(2)}) collective-permute-start(bf16[64,2048]{1,0:T(8,128)(2,1)S(1)} %add_convert_fusion.4), channel_id=1, source_target_pairs={{0,1},{2,0},{4,2},{6,4},{7,6},{5,7},{3,5},{1,3},{8,9},{10,8},{12,1... | collective-permute-start | bytes 786440 | tf_op jit(solution)/shard_map/ppermute | solution.py:55
  94.7 1.5 %shard_map.116 = (bf16[64,2048]{1,0:T(8,128)(2,1)S(1)}, bf16[64,2048]{1,0:T(8,128)(2,1)S(1)}, bf16[64,2048]{1,0:T(8,128)(2,1)S(1)}, bf16[64,2048]{1,0:T(8,128)(2...) custom-call(bf16[1,512,512]{2,1,0:T(8,128)(2,1)S(1)} %shard_map.105.q_ref, ...), custom_call_target="tpu_custom_call" | custom-call | flops 805306368 | bytes 5767168 | tf_op jit(solution)/shard_map/pallas_call | solution.py:457
  96.2 0.9 collective-permute-done.27
  97.2 1.5 %collective-permute-done.26 = bf16[64,2048]{1,0:T(8,128)(2,1)S(1)} collective-permute-done((bf16[64,2048]{1,0:T(8,128)(2,1)S(1)}, bf16[64,2048]{1,0:T(8,128)(2,1)S(1)}, u32[]{:S(2)}, u32[]{:S(2)}) %collective-permute-start.26) | collective-permute-done | bytes 262176 | tf_op jit(solution)/shard_map/ppermute | solution.py:55
  98.8 0.2 collective-permute-start.28
  99.0 1.3 %collective-permute-start.29 = (bf16[64,2048]{1,0:T(8,128)(2,1)S(1)}, bf16[64,2048]{1,0:T(8,128)(2,1)S(1)}, u32[]{:S(2)}, u32[]{:S(2)}) collective-permute-start(bf16[64,2048]{1,0:T(8,128)(2,1)S(1)} %add_convert_fusion.6), channel_id=1, source_target_pairs={{0,1},{2,0},{4,2},{6,4},{7,6},{5,7},{3,5},{1,3},{8,9},{10,8},{12,1... | collective-permute-start | bytes 786440 | tf_op jit(solution)/shard_map/ppermute | solution.py:55
  100.3 2.3 %collective-permute-done.31 = bf16[64,2048]{1,0:T(8,128)(2,1)S(1)} collective-permute-done((bf16[64,2048]{1,0:T(8,128)(2,1)S(1)}, bf16[64,2048]{1,0:T(8,128)(2,1)S(1)}, u32[]{:S(2)}, u32[]{:S(2)}) %collective-permute-start.31) | collective-permute-done | bytes 262176 | tf_op jit(solution)/shard_map/ppermute | solution.py:55
  102.7 1.7 %collective-permute-done.30 = bf16[64,2048]{1,0:T(8,128)(2,1)S(1)} collective-permute-done((bf16[64,2048]{1,0:T(8,128)(2,1)S(1)}, bf16[64,2048]{1,0:T(8,128)(2,1)S(1)}, u32[]{:S(2)}, u32[]{:S(2)}) %collective-permute-start.30) | collective-permute-done | bytes 262176 | tf_op jit(solution)/shard_map/ppermute | solution.py:55
  104.4 0.2 collective-permute-start.32
  104.7 1.3 %collective-permute-start.33 = (bf16[64,2048]{1,0:T(8,128)(2,1)S(1)}, bf16[64,2048]{1,0:T(8,128)(2,1)S(1)}, u32[]{:S(2)}, u32[]{:S(2)}) collective-permute-start(bf16[64,2048]{1,0:T(8,128)(2,1)S(1)} %add_convert_fusion.2), channel_id=1, source_target_pairs={{0,1},{2,0},{4,2},{6,4},{7,6},{5,7},{3,5},{1,3},{8,9},{10,8},{12,1... | collective-permute-start | bytes 786440 | tf_op jit(solution)/shard_map/ppermute | solution.py:55
  106.0 4.0 %collective-permute-done.28.refs_2_ = bf16[64,2048]{1,0:T(8,128)(2,1)S(1)} collective-permute-done((bf16[64,2048]{1,0:T(8,128)(2,1)S(1)}, bf16[64,2048]{1,0:T(8,128)(2,1)S(1)}, u32[]{:S(2)}, u32[]{:S(2)}) %collective-permute-start.28) | collective-permute-done | bytes 262176 | tf_op jit(solution)/shard_map/ppermute | solution.py:55
  110.1 2.4 %collective-permute-done.32 = bf16[64,2048]{1,0:T(8,128)(2,1)S(1)} collective-permute-done((bf16[64,2048]{1,0:T(8,128)(2,1)S(1)}, bf16[64,2048]{1,0:T(8,128)(2,1)S(1)}, u32[]{:S(2)}, u32[]{:S(2)}) %collective-permute-start.32) | collective-permute-done | bytes 262176 | tf_op jit(solution)/shard_map/ppermute | solution.py:55
  112.6 0.8 pad_maximum_fusion
  (48 shorter events, 2.2 us)
Async XLA Ops:
  1.1 11.2 %collective-permute-start.4 = (bf16[256,512]{1,0:T(8,128)(2,1)S(1)}, bf16[256,512]{1,0:T(8,128)(2,1)S(1)}, u32[]{:S(2)}, u32[]{:S(2)}) collective-permute-start(bf16[256,512]{1,0:T(8,128)(2,1)S(1)} %get-tuple-element.59.refs_3_), channel_id=1, source_target_pairs={{0,1},{2,0},{4,2},{6,4},{7,6},{5,7},{3,5},{1,3},{8,9},{10,8},{12,1... | collective-permute-start | bytes 786440 | tf_op jit(solution)/shard_map/ppermute | solution.py:55
  3.1 10.6 %copy-start.4 = (f32[512,4]{0,1:T(4,128)S(1)}, f32[512,4]{0,1:T(4,128)}, u32[]{:S(2)}) copy-start(f32[512,4]{0,1:T(4,128)} %param.18) | copy-start | bytes 24580
  3.1 10.5 %collective-permute-start = (bf16[256,512]{1,0:T(8,128)(2,1)S(1)}, bf16[256,512]{1,0:T(8,128)(2,1)S(1)}, u32[]{:S(2)}, u32[]{:S(2)}) collective-permute-start(bf16[256,512]{1,0:T(8,128)(2,1)S(1)} %get-tuple-element.56.refs_0_), channel_id=1, source_target_pairs={{0,2},{2,4},{4,6},{6,7},{7,5},{5,3},{3,1},{1,0},{8,10},{10,12},{12... | collective-permute-start | bytes 786440 | tf_op jit(solution)/shard_map/ppermute | solution.py:55
  3.3 12.6 %collective-permute-start.3 = (bf16[256,512]{1,0:T(8,128)(2,1)S(1)}, bf16[256,512]{1,0:T(8,128)(2,1)S(1)}, u32[]{:S(2)}, u32[]{:S(2)}) collective-permute-start(bf16[256,512]{1,0:T(8,128)(2,1)S(1)} %get-tuple-element.59.refs_3_), channel_id=1, source_target_pairs={{0,2},{2,4},{4,6},{6,7},{7,5},{5,3},{3,1},{1,0},{8,10},{10,12},{12... | collective-permute-start | bytes 786440 | tf_op jit(solution)/shard_map/ppermute | solution.py:55
  4.7 12.8 %collective-permute-start.2 = (bf16[256,512]{1,0:T(8,128)(2,1)S(1)}, bf16[256,512]{1,0:T(8,128)(2,1)S(1)}, u32[]{:S(2)}, u32[]{:S(2)}) collective-permute-start(bf16[256,512]{1,0:T(8,128)(2,1)S(1)} %get-tuple-element.56.refs_0_), channel_id=1, source_target_pairs={{0,1},{2,0},{4,2},{6,4},{7,6},{5,7},{3,5},{1,3},{8,9},{10,8},{12,1... | collective-permute-start | bytes 786440 | tf_op jit(solution)/shard_map/ppermute | solution.py:55
  12.3 7.9 %collective-permute-start.8 = (bf16[256,512]{1,0:T(8,128)(2,1)S(1)}, bf16[256,512]{1,0:T(8,128)(2,1)S(1)}, u32[]{:S(2)}, u32[]{:S(2)}) collective-permute-start(bf16[256,512]{1,0:T(8,128)(2,1)S(1)} %collective-permute-done.4.refs_5_), channel_id=1, source_target_pairs={{0,1},{2,0},{4,2},{6,4},{7,6},{5,7},{3,5},{1,3},{8,9},{10,8},{12,1... | collective-permute-start | bytes 786440 | tf_op jit(solution)/shard_map/ppermute | solution.py:55
  13.6 7.2 %collective-permute-start.1 = (bf16[256,512]{1,0:T(8,128)(2,1)S(1)}, bf16[256,512]{1,0:T(8,128)(2,1)S(1)}, u32[]{:S(2)}, u32[]{:S(2)}) collective-permute-start(bf16[256,512]{1,0:T(8,128)(2,1)S(1)} %collective-permute-done.refs_1_), channel_id=1, source_target_pairs={{0,2},{2,4},{4,6},{6,7},{7,5},{5,3},{3,1},{1,0},{8,10},{10,12},{12... | collective-permute-start | bytes 786440 | tf_op jit(solution)/shard_map/ppermute | solution.py:55
  13.8 6.4 %collective-permute-start.5 = (f32[4,512]{1,0:T(4,128)S(1)}, f32[4,512]{1,0:T(4,128)S(1)}, u32[]{:S(2)}, u32[]{:S(2)}) collective-permute-start(f32[4,512]{1,0:T(4,128)S(1)} %bitcast.1), channel_id=1, source_target_pairs={{0,8},{8,0},{16,24},{24,16},{1,9},{9,1},{17,25},{25,17},{2,10},{10... | collective-permute-start | bytes 24584 | tf_op jit(solution)/shard_map/ppermute | solution.py:518
  15.9 10.6 %collective-permute-start.13 = (bf16[256,512]{1,0:T(8,128)(2,1)S(1)}, bf16[256,512]{1,0:T(8,128)(2,1)S(1)}, u32[]{:S(2)}, u32[]{:S(2)}) collective-permute-start(bf16[256,512]{1,0:T(8,128)(2,1)S(1)} %collective-permute-done.3.refs_4_), channel_id=1, source_target_pairs={{0,2},{2,4},{4,6},{6,7},{7,5},{5,3},{3,1},{1,0},{8,10},{10,12},{12... | collective-permute-start | bytes 786440 | tf_op jit(solution)/shard_map/ppermute | solution.py:55
  17.5 8.9 %collective-permute-start.11 = (bf16[256,512]{1,0:T(8,128)(2,1)S(1)}, bf16[256,512]{1,0:T(8,128)(2,1)S(1)}, u32[]{:S(2)}, u32[]{:S(2)}) collective-permute-start(bf16[256,512]{1,0:T(8,128)(2,1)S(1)} %collective-permute-done.2.refs_2_), channel_id=1, source_target_pairs={{0,1},{2,0},{4,2},{6,4},{7,6},{5,7},{3,5},{1,3},{8,9},{10,8},{12,1... | collective-permute-start | bytes 786440 | tf_op jit(solution)/shard_map/ppermute | solution.py:55
  20.9 10.5 %collective-permute-start.9 = (bf16[256,512]{1,0:T(8,128)(2,1)S(1)}, bf16[256,512]{1,0:T(8,128)(2,1)S(1)}, u32[]{:S(2)}, u32[]{:S(2)}) collective-permute-start(bf16[256,512]{1,0:T(8,128)(2,1)S(1)} %collective-permute-done.8.refs_3_), channel_id=1, source_target_pairs={{0,1},{2,0},{4,2},{6,4},{7,6},{5,7},{3,5},{1,3},{8,9},{10,8},{12,1... | collective-permute-start | bytes 786440 | tf_op jit(solution)/shard_map/ppermute | solution.py:55
  22.2 10.2 %collective-permute-start.6 = (bf16[256,512]{1,0:T(8,128)(2,1)S(1)}, bf16[256,512]{1,0:T(8,128)(2,1)S(1)}, u32[]{:S(2)}, u32[]{:S(2)}) collective-permute-start(bf16[256,512]{1,0:T(8,128)(2,1)S(1)} %collective-permute-done.1.refs_0_), channel_id=1, source_target_pairs={{0,2},{2,4},{4,6},{6,7},{7,5},{5,3},{3,1},{1,0},{8,10},{10,12},{12... | collective-permute-start | bytes 786440 | tf_op jit(solution)/shard_map/ppermute | solution.py:55
  26.5 11.2 %collective-permute-start.14 = (bf16[256,512]{1,0:T(8,128)(2,1)S(1)}, bf16[256,512]{1,0:T(8,128)(2,1)S(1)}, u32[]{:S(2)}, u32[]{:S(2)}) collective-permute-start(bf16[256,512]{1,0:T(8,128)(2,1)S(1)} %collective-permute-done.13.refs_2_), channel_id=1, source_target_pairs={{0,2},{2,4},{4,6},{6,7},{7,5},{5,3},{3,1},{1,0},{8,10},{10,12},{12... | collective-permute-start | bytes 786440 | tf_op jit(solution)/shard_map/ppermute | solution.py:55
  27.2 10.5 %collective-permute-start.12 = (bf16[256,512]{1,0:T(8,128)(2,1)S(1)}, bf16[256,512]{1,0:T(8,128)(2,1)S(1)}, u32[]{:S(2)}, u32[]{:S(2)}) collective-permute-start(bf16[256,512]{1,0:T(8,128)(2,1)S(1)} %collective-permute-done.11.refs_1_), channel_id=1, source_target_pairs={{0,1},{2,0},{4,2},{6,4},{7,6},{5,7},{3,5},{1,3},{8,9},{10,8},{12,1... | collective-permute-start | bytes 786440 | tf_op jit(solution)/shard_map/ppermute | solution.py:55
  31.3 11.1 %collective-permute-start.10 = (bf16[256,512]{1,0:T(8,128)(2,1)S(1)}, bf16[256,512]{1,0:T(8,128)(2,1)S(1)}, u32[]{:S(2)}, u32[]{:S(2)}) collective-permute-start(bf16[256,512]{1,0:T(8,128)(2,1)S(1)} %collective-permute-done.9.refs_3_), channel_id=1, source_target_pairs={{0,1},{2,0},{4,2},{6,4},{7,6},{5,7},{3,5},{1,3},{8,9},{10,8},{12,1... | collective-permute-start | bytes 786440 | tf_op jit(solution)/shard_map/ppermute | solution.py:55
  32.4 10.9 %collective-permute-start.7 = (bf16[256,512]{1,0:T(8,128)(2,1)S(1)}, bf16[256,512]{1,0:T(8,128)(2,1)S(1)}, u32[]{:S(2)}, u32[]{:S(2)}) collective-permute-start(bf16[256,512]{1,0:T(8,128)(2,1)S(1)} %collective-permute-done.6.refs_0_), channel_id=1, source_target_pairs={{0,2},{2,4},{4,6},{6,7},{7,5},{5,3},{3,1},{1,0},{8,10},{10,12},{12... | collective-permute-start | bytes 786440 | tf_op jit(solution)/shard_map/ppermute | solution.py:55
  39.6 10.1 %copy-start.1 = (f32[4,128,256]{2,1,0:T(8,128)S(1)}, f32[4,128,256]{2,1,0:T(8,128)}, u32[]{:S(2)}) copy-start(f32[4,128,256]{2,1,0:T(8,128)} %gate_ref.5) | copy-start | bytes 1572868
  39.6 10.1 %copy-start.2 = (f32[4,128,256]{2,1,0:T(8,128)S(1)}, f32[4,128,256]{2,1,0:T(8,128)}, u32[]{:S(2)}) copy-start(f32[4,128,256]{2,1,0:T(8,128)} %up_ref.5) | copy-start | bytes 1572868
  39.6 10.1 %copy-start.3 = (f32[4,256,128]{2,1,0:T(8,128)S(1)}, f32[4,256,128]{2,1,0:T(8,128)}, u32[]{:S(2)}) copy-start(f32[4,256,128]{2,1,0:T(8,128)} %down_ref.5) | copy-start | bytes 1572868
  44.3 6.9 %collective-permute-start.16 = (bf16[2,512,256]{2,1,0:T(8,128)(2,1)S(1)}, bf16[2,512,256]{2,1,0:T(8,128)(2,1)S(1)}, u32[]{:S(2)}, u32[]{:S(2)}) collective-permute-start(bf16[2,512,256]{2,1,0:T(8,128)(2,1)S(1)} %get-tuple-element.72), channel_id=1, source_target_pairs={{0,8},{8,0},{16,24},{24,16},{1,9},{9,1},{17,25},{25,17},{2,10},{10... | collective-permute-start | bytes 1572872 | tf_op jit(solution)/shard_map/ppermute | solution.py:518
  46.6 11.8 %collective-permute-start.15 = (bf16[2,512,256]{2,1,0:T(8,128)(2,1)S(1)}, bf16[2,512,256]{2,1,0:T(8,128)(2,1)S(1)}, u32[]{:S(2)}, u32[]{:S(2)}) collective-permute-start(bf16[2,512,256]{2,1,0:T(8,128)(2,1)S(1)} %get-tuple-element.72), channel_id=1, source_target_pairs={{8,16},{9,17},{10,18},{11,19},{12,20},{13,21},{14,22},{15,23}} | collective-permute-start | bytes 1572872 | tf_op jit(solution)/shard_map/ppermute | solution.py:549
  52.6 11.6 %collective-permute-start.18 = (bf16[2,3,128,256]{3,2,1,0:T(8,128)(2,1)S(1)}, bf16[2,3,128,256]{3,2,1,0:T(8,128)(2,1)S(1)}, u32[]{:S(2)}, u32[]{:S(2)}) collective-permute-start(bf16[2,3,128,256]{3,2,1,0:T(8,128)(2,1)S(1)} %get-tuple-element.76), channel_id=1, source_target_pairs={{0,16},{8,24},{16,0},{24,8},{1,17},{9,25},{17,1},{25,9},{2,18},{10... | collective-permute-start | bytes 1179656 | tf_op jit(solution)/shard_map/ppermute | solution.py:518
  53.1 11.1 %copy-start.5 = (f32[4]{0:T(128)S(1)}, f32[4]{0:T(128)}, u32[]{:S(2)}) copy-start(f32[4]{0:T(128)} %step_ref.1) | copy-start | bytes 52
  55.2 14.6 %collective-permute-start.17 = (bf16[2,512,256]{2,1,0:T(8,128)(2,1)S(1)}, bf16[2,512,256]{2,1,0:T(8,128)(2,1)S(1)}, u32[]{:S(2)}, u32[]{:S(2)}) collective-permute-start(bf16[2,512,256]{2,1,0:T(8,128)(2,1)S(1)} %get-tuple-element.74), channel_id=1, source_target_pairs={{0,8},{8,16},{16,24},{1,9},{9,17},{17,25},{2,10},{10,18},{18,26},{... | collective-permute-start | bytes 1572872 | tf_op jit(solution)/shard_map/ppermute | solution.py:563
  65.0 6.0 %copy-start = (bf16[512,4096]{1,0:T(8,128)(2,1)S(1)}, bf16[512,4096]{1,0:T(8,128)(2,1)}, u32[]{:S(2)}) copy-start(bf16[512,4096]{1,0:T(8,128)(2,1)} %w_ref.7) | copy-start | bytes 12582916
  65.0 6.0 %collective-permute-start.19 = (bf16[2,3,128,256]{3,2,1,0:T(8,128)(2,1)S(1)}, bf16[2,3,128,256]{3,2,1,0:T(8,128)(2,1)S(1)}, u32[]{:S(2)}, u32[]{:S(2)}) collective-permute-start(bf16[2,3,128,256]{3,2,1,0:T(8,128)(2,1)S(1)} %shard_map.111.net_ref), channel_id=1, source_target_pairs={{0,8},{8,0},{16,24},{24,16},{1,9},{9,1},{17,25},{25,17},{2,10},{10... | collective-permute-start | bytes 1179656 | tf_op jit(solution)/shard_map/ppermute | solution.py:518
  72.2 8.4 %collective-permute-start.21 = (bf16[64,2048]{1,0:T(8,128)(2,1)S(1)}, bf16[64,2048]{1,0:T(8,128)(2,1)S(1)}, u32[]{:S(2)}, u32[]{:S(2)}) collective-permute-start(bf16[64,2048]{1,0:T(8,128)(2,1)S(1)} %get-tuple-element.80), channel_id=1, source_target_pairs={{0,1},{2,0},{4,2},{6,4},{7,6},{5,7},{3,5},{1,3},{8,9},{10,8},{12,1... | collective-permute-start | bytes 786440 | tf_op jit(solution)/shard_map/ppermute | solution.py:55
  73.6 8.3 %collective-permute-start.20 = (bf16[64,2048]{1,0:T(8,128)(2,1)S(1)}, bf16[64,2048]{1,0:T(8,128)(2,1)S(1)}, u32[]{:S(2)}, u32[]{:S(2)}) collective-permute-start(bf16[64,2048]{1,0:T(8,128)(2,1)S(1)} %get-tuple-element.78), channel_id=1, source_target_pairs={{0,2},{2,4},{4,6},{6,7},{7,5},{5,3},{3,1},{1,0},{8,10},{10,12},{12... | collective-permute-start | bytes 786440 | tf_op jit(solution)/shard_map/ppermute | solution.py:55
  75.0 11.2 %collective-permute-start.25 = (bf16[64,2048]{1,0:T(8,128)(2,1)S(1)}, bf16[64,2048]{1,0:T(8,128)(2,1)S(1)}, u32[]{:S(2)}, u32[]{:S(2)}) collective-permute-start(bf16[64,2048]{1,0:T(8,128)(2,1)S(1)} %get-tuple-element.84), channel_id=1, source_target_pairs={{0,1},{2,0},{4,2},{6,4},{7,6},{5,7},{3,5},{1,3},{8,9},{10,8},{12,1... | collective-permute-start | bytes 786440 | tf_op jit(solution)/shard_map/ppermute | solution.py:55
  76.3 11.2 %collective-permute-start.24 = (bf16[64,2048]{1,0:T(8,128)(2,1)S(1)}, bf16[64,2048]{1,0:T(8,128)(2,1)S(1)}, u32[]{:S(2)}, u32[]{:S(2)}) collective-permute-start(bf16[64,2048]{1,0:T(8,128)(2,1)S(1)} %get-tuple-element.83), channel_id=1, source_target_pairs={{0,2},{2,4},{4,6},{6,7},{7,5},{5,3},{3,1},{1,0},{8,10},{10,12},{12... | collective-permute-start | bytes 786440 | tf_op jit(solution)/shard_map/ppermute | solution.py:55
  82.0 9.9 %collective-permute-start.23 = (bf16[64,2048]{1,0:T(8,128)(2,1)S(1)}, bf16[64,2048]{1,0:T(8,128)(2,1)S(1)}, u32[]{:S(2)}, u32[]{:S(2)}) collective-permute-start(bf16[64,2048]{1,0:T(8,128)(2,1)S(1)} %add_convert_fusion.10), channel_id=1, source_target_pairs={{0,1},{2,0},{4,2},{6,4},{7,6},{5,7},{3,5},{1,3},{8,9},{10,8},{12,1... | collective-permute-start | bytes 786440 | tf_op jit(solution)/shard_map/ppermute | solution.py:55
  83.3 9.8 %collective-permute-start.22 = (bf16[64,2048]{1,0:T(8,128)(2,1)S(1)}, bf16[64,2048]{1,0:T(8,128)(2,1)S(1)}, u32[]{:S(2)}, u32[]{:S(2)}) collective-permute-start(bf16[64,2048]{1,0:T(8,128)(2,1)S(1)} %add_convert_fusion.11), channel_id=1, source_target_pairs={{0,2},{2,4},{4,6},{6,7},{7,5},{5,3},{3,1},{1,0},{8,10},{10,12},{12... | collective-permute-start | bytes 786440 | tf_op jit(solution)/shard_map/ppermute | solution.py:55
  87.6 9.6 %collective-permute-start.27 = (bf16[64,2048]{1,0:T(8,128)(2,1)S(1)}, bf16[64,2048]{1,0:T(8,128)(2,1)S(1)}, u32[]{:S(2)}, u32[]{:S(2)}) collective-permute-start(bf16[64,2048]{1,0:T(8,128)(2,1)S(1)} %add_convert_fusion.8), channel_id=1, source_target_pairs={{0,1},{2,0},{4,2},{6,4},{7,6},{5,7},{3,5},{1,3},{8,9},{10,8},{12,1... | collective-permute-start | bytes 786440 | tf_op jit(solution)/shard_map/ppermute | solution.py:55
  88.9 9.8 %collective-permute-start.26 = (bf16[64,2048]{1,0:T(8,128)(2,1)S(1)}, bf16[64,2048]{1,0:T(8,128)(2,1)S(1)}, u32[]{:S(2)}, u32[]{:S(2)}) collective-permute-start(bf16[64,2048]{1,0:T(8,128)(2,1)S(1)} %add_convert_fusion.9), channel_id=1, source_target_pairs={{0,2},{2,4},{4,6},{6,7},{7,5},{5,3},{3,1},{1,0},{8,10},{10,12},{12... | collective-permute-start | bytes 786440 | tf_op jit(solution)/shard_map/ppermute | solution.py:55
  93.2 9.4 %collective-permute-start.31 = (bf16[64,2048]{1,0:T(8,128)(2,1)S(1)}, bf16[64,2048]{1,0:T(8,128)(2,1)S(1)}, u32[]{:S(2)}, u32[]{:S(2)}) collective-permute-start(bf16[64,2048]{1,0:T(8,128)(2,1)S(1)} %add_convert_fusion.4), channel_id=1, source_target_pairs={{0,1},{2,0},{4,2},{6,4},{7,6},{5,7},{3,5},{1,3},{8,9},{10,8},{12,1... | collective-permute-start | bytes 786440 | tf_op jit(solution)/shard_map/ppermute | solution.py:55
  94.6 9.8 %collective-permute-start.30 = (bf16[64,2048]{1,0:T(8,128)(2,1)S(1)}, bf16[64,2048]{1,0:T(8,128)(2,1)S(1)}, u32[]{:S(2)}, u32[]{:S(2)}) collective-permute-start(bf16[64,2048]{1,0:T(8,128)(2,1)S(1)} %add_convert_fusion.5), channel_id=1, source_target_pairs={{0,2},{2,4},{4,6},{6,7},{7,5},{5,3},{3,1},{1,0},{8,10},{10,12},{12... | collective-permute-start | bytes 786440 | tf_op jit(solution)/shard_map/ppermute | solution.py:55
  98.8 11.1 %collective-permute-start.28 = (bf16[64,2048]{1,0:T(8,128)(2,1)S(1)}, bf16[64,2048]{1,0:T(8,128)(2,1)S(1)}, u32[]{:S(2)}, u32[]{:S(2)}) collective-permute-start(bf16[64,2048]{1,0:T(8,128)(2,1)S(1)} %add_convert_fusion.7), channel_id=1, source_target_pairs={{0,2},{2,4},{4,6},{6,7},{7,5},{5,3},{3,1},{1,0},{8,10},{10,12},{12... | collective-permute-start | bytes 786440 | tf_op jit(solution)/shard_map/ppermute | solution.py:55
  99.0 10.9 %collective-permute-start.29 = (bf16[64,2048]{1,0:T(8,128)(2,1)S(1)}, bf16[64,2048]{1,0:T(8,128)(2,1)S(1)}, u32[]{:S(2)}, u32[]{:S(2)}) collective-permute-start(bf16[64,2048]{1,0:T(8,128)(2,1)S(1)} %add_convert_fusion.6), channel_id=1, source_target_pairs={{0,1},{2,0},{4,2},{6,4},{7,6},{5,7},{3,5},{1,3},{8,9},{10,8},{12,1... | collective-permute-start | bytes 786440 | tf_op jit(solution)/shard_map/ppermute | solution.py:55
  104.4 8.0 %collective-permute-start.32 = (bf16[64,2048]{1,0:T(8,128)(2,1)S(1)}, bf16[64,2048]{1,0:T(8,128)(2,1)S(1)}, u32[]{:S(2)}, u32[]{:S(2)}) collective-permute-start(bf16[64,2048]{1,0:T(8,128)(2,1)S(1)} %add_convert_fusion.3), channel_id=1, source_target_pairs={{0,2},{2,4},{4,6},{6,7},{7,5},{5,3},{3,1},{1,0},{8,10},{10,12},{12... | collective-permute-start | bytes 786440 | tf_op jit(solution)/shard_map/ppermute | solution.py:55
  104.7 7.9 %collective-permute-start.33 = (bf16[64,2048]{1,0:T(8,128)(2,1)S(1)}, bf16[64,2048]{1,0:T(8,128)(2,1)S(1)}, u32[]{:S(2)}, u32[]{:S(2)}) collective-permute-start(bf16[64,2048]{1,0:T(8,128)(2,1)S(1)} %add_convert_fusion.2), channel_id=1, source_target_pairs={{0,1},{2,0},{4,2},{6,4},{7,6},{5,7},{3,5},{1,3},{8,9},{10,8},{12,1... | collective-permute-start | bytes 786440 | tf_op jit(solution)/shard_map/ppermute | solution.py:55

commit v10 on v9

--- a/solution.py
+++ b/solution.py
@@ -105,7 +105,7 @@
                 for block in range(blocks)
                 for index in range(count)
             ],
-            4,
+            count * blocks,
         )
 
     return call(
@@ -334,7 +334,8 @@
                     for at, keys in enumerate(halves(rows)[: index + 1])
                 ]
                 result, top, total = attend_blocks(q_ref[0, where, lane], blocks)
-                out_ref[where, lane] = result / jnp.where(alone, total, 1.0)
+                share = jnp.where(alone, total, 1.0) if head < heads // 2 else 1.0
+                out_ref[where, lane] = result / share
                 stats_ref[0, where, lane] = jnp.broadcast_to(top, result.shape)
                 stats_ref[1, where, lane] = jnp.broadcast_to(total, result.shape)
 
@@ -350,42 +351,44 @@
     )(query, kv)
 
 
-def attend_earlier(summed, stats, query, sources, other, size, after=()):
+def merged(summed, before, sums, result, top, total):
+    both = jnp.maximum(before, top)
+    old, new = jnp.exp2(before - both), jnp.exp2(top - both)
+    return (summed * old + result * new) / (sums * old + total * new)
+
+
+def attend_earlier(summed, stats, query, sources, size):
     rows = query.shape[1]
     heads = sources[0].shape[2] // size
 
-    def body(sum_ref, stats_ref, q_ref, *refs):
-        out_ref = refs[-1]
+    def body(sum_ref, stats_ref, q_ref, behind_ref, beside_ref, out_ref):
         place = lax.axis_index("tok")
 
         def add(ref):
             for index, where in enumerate(halves(rows)):
                 for at in range(heads):
-                    lane = lanes(first_head(heads, other) + at, size)
-                    result, top, total = attend_blocks(
-                        q_ref[0, where, lane],
-                        earlier_blocks(ref, index, slice(at * size, (at + 1) * size)),
+                    lane = lanes(first_head(heads) + at, size)
+                    out_ref[where, lane] = merged(
+                        sum_ref[where, lane],
+                        stats_ref[0, where, lane],
+                        stats_ref[1, where, lane],
+                        *attend_blocks(
+                            q_ref[0, where, lane],
+                            earlier_blocks(ref, index, slice(at * size, (at + 1) * size)),
+                        ),
                     )
-                    before = stats_ref[0, where, lane]
-                    both = jnp.maximum(before, top)
-                    old, new = jnp.exp2(before - both), jnp.exp2(top - both)
-                    total = stats_ref[1, where, lane] * old + total * new
-                    out_ref[where, lane] = (sum_ref[where, lane] * old + result * new) / total
-
-        if len(sources) == 1:
-            pl.when(place > 0)(lambda: add(refs[0]))
-        else:
-            pl.when((place > 0) & (place % 2 == 0))(lambda: add(refs[0]))
-            pl.when(place % 2 == 1)(lambda: add(refs[1]))
-
-    return call(
-        body,
-        [WHOLE] * (3 + len(sources)) + [AFTER] * len(after),
+
+        pl.when((place > 0) & (place % 2 == 0))(lambda: add(behind_ref))
+        pl.when(place % 2 == 1)(lambda: add(beside_ref))
+
+    return call(
+        body,
+        [WHOLE] * 5,
         WHOLE,
         jax.ShapeDtypeStruct(summed.shape, F32),
         cost=cost(3 * heads * size * rows * rows, 8 * rows * heads * size, heads * rows * rows),
         aliases={0: 0},
-    )(summed, stats, query, *sources, *after)
+    )(summed, stats, query, *sources)
 
 
 def fast_apply(query, gate, upper, down):
@@ -419,7 +422,7 @@
     )(query, attended, nets)
 
 
-def partial_out(offsets, query, attended, nets, near, w_out, after=()):
+def partial_out(offsets, query, attended, stats, behind, nets, near, w_out, after=()):
     rows = near.shape[0] // lax.axis_size("head")
     heads, _, size, hidden_size = nets.shape
     depth = heads * size
@@ -427,20 +430,29 @@
     width = w_out.shape[1]
     block = width // 8
 
-    def body(q_ref, attended_ref, net_ref, near_ref, w_ref, *refs):
+    def body(q_ref, attended_ref, stats_ref, behind_ref, net_ref, near_ref, w_ref, *refs):
         out_refs, far_ref = refs[len(after) : -1], refs[-1]
         starts = [pl.multiple_of(ring_index(offset) * rows, rows) for offset in offsets]
 
         def take(ref, lane):
             return jnp.concatenate([ref[pl.ds(start, rows), lane] for start in starts], axis=0)
 
+        row = lax.broadcasted_iota(jnp.int32, (rows, behind.shape[1]), 0)
+        row = jnp.concatenate([row + start for start in starts], axis=0)
+        col = lax.broadcasted_iota(jnp.int32, row.shape, 1)
+        within = (col > row) & (lax.axis_index("tok") > 0)
         for index in range(heads):
             lane = lanes(first_head(heads, True) + index, size)
-            fast = fast_apply(
-                take(q_ref.at[0], lane), *(net_ref[index, part] for part in range(3))
+            where = slice(index * size, (index + 1) * size)
+            queries = take(q_ref.at[0], lane)
+            fast = fast_apply(queries, *(net_ref[index, part] for part in range(3)))
+            seen = merged(
+                take(attended_ref, lane),
+                take(stats_ref.at[0], lane),
+                take(stats_ref.at[1], lane),
+                *attend_blocks(queries, [(behind_ref[0, :, where], behind_ref[1, :, where], within)]),
             )
-            where = slice(index * size, (index + 1) * size)
-            far_ref[:, where] = (take(attended_ref, lane) + fast).astype(BF16)
+            far_ref[:, where] = (seen + fast).astype(BF16)
         left = take(near_ref, slice(None))
         near_rows = pl.ds(pl.multiple_of(first_head(heads) * size, depth), depth)
         far_rows = pl.ds(pl.multiple_of(first_head(heads, True) * size, depth), depth)
@@ -456,20 +468,19 @@
 
     outs = call(
         body,
-        [WHOLE] * 5 + [AFTER] * len(after),
+        [WHOLE] * 7 + [AFTER] * len(after),
         [WHOLE] * (2 * count),
         [jax.ShapeDtypeStruct((rows, width // 2), BF16)] * (2 * count),
         [pltpu.VMEM((count * rows, depth), BF16)],
         vmem=8,
         cost=cost(4 * count * rows * depth * width, 2 * width * (2 * depth + count * rows)),
-    )(query, attended, nets, near, w_out, *after)
+    )(query, attended, stats, behind, nets, near, w_out, *after)
     return {offset: tuple(outs[2 * at : 2 * at + 2]) for at, offset in enumerate(offsets)}
 
 
-def ring_reduce(query, attended, nets, near, w_out):
+def ring_reduce(*shared):
     steps = lax.axis_size("head") // 2
     signed = [sign * step for step in range(steps - 1, 0, -1) for sign in (1, -1)]
-    shared = (query, attended, nets, near, w_out)
     parts = partial_out([steps], *shared) | partial_out(signed[:2], *shared)
     coming = {}
     ordered = ()
@@ -559,13 +570,12 @@
             travel = travel.astype(BF16)
         received.append(swap(travel, 1 << bit))
     attended, stats = attend_own(query, kv, head_size)
+    attended = attend_earlier(attended, stats, query, (behind, beside), head_size)
     near, _ = lax.optimization_barrier((near, attended))
     behind_far = lax.ppermute(near, "tok", [(index, index + 1) for index in range(tok_count - 1)])
-    attended = attend_earlier(attended, stats, query, (behind, beside), False, head_size)
     mine = renew(grads, received, head_step, *nets, (attended,))
     near = combine_near(query, attended, mine)
-    attended = attend_earlier(attended, stats, query, (behind_far,), True, head_size, (near,))
-    return ring_reduce(query, attended, swap(mine, 1), near, w_out)
+    return ring_reduce(query, attended, stats, behind_far, swap(mine, 1), near, w_out)
 
 
 def solution(mesh):

time: 114 us -> 114 us (level)
  starting transfers between devices: 31.5 us -> 34 us
  Pallas kernels: 30.5 us -> 28.9 us
    ppermute x4, waiting for transfers between devices: 4.61 us -> 0.01 us  [swap(): lax.ppermute(value, 'tok', [(index, index ^ bit) for index in range(count)])]
    ppermute x1, starting transfers between devices: 1.92 us -> 4.82 us  [shards(): lax.ppermute(near, 'tok', [(index, index + 1) for index in range(tok_coun...]
    pallas_call x1, Pallas kernels: 7.47 us -> 4.78 us  [load(): call(body, [IN_HBM] * count, [WHOLE] * count, [jax.ShapeDtypeStruct(array...]
    ppermute x1, waiting for transfers between devices: 1.22 us -> 3.14 us  [shards(): lax.ppermute(far, 'tok', [(index, index + 1) for index in range(1, tok_co...]
    ppermute x28, waiting for transfers between devices: 39.8 us -> 41.4 us  [ring_send(): lax.ppermute(value, 'head', [(order[i], order[(i + step) % count]) for i...]
    pallas_call x6 -> x5, Pallas kernels: 7.63 us -> 8.74 us  [the longest x4 7.51 us: partial_out(): call(body, [WHOLE] * 7 + [AFTER] * len(after), [WHOLE] * (2 * count), [ja...]
  transfers between devices with their start and end apart: 34 -> 34, of which waited for: 21 -> 22; matrix products, arithmetic and copies ran while one was open for 1% -> 1% of each run, Pallas kernels for 24% -> 22%
where the time goes in v10:
time: 114 us
  waiting for transfers between devices  49 us (43%)
  starting transfers between devices  34 us (30%)
  Pallas kernels  28.9 us (25%)
  other arithmetic  1.58 us (1%)
    ppermute x28, waiting for transfers between devices, ring_send(): lax.ppermute(value, 'head', [(order[i], order[(i + step) % count]) for i...  41.4 us
    ppermute x28, starting transfers between devices, ring_send(): lax.ppermute(value, 'head', [(order[i], order[(i + step) % count]) for i...  21.7 us
    pallas_call x5, Pallas kernels, accumulate(): call(body, [WHOLE] * len(args), [WHOLE] * (1 + 2 * shared), [jax.ShapeDty...  7.64 us
    pallas_call x4, Pallas kernels, partial_out(): call(body, [WHOLE] * 7 + [AFTER] * len(after), [WHOLE] * (2 * count), [ja...  7.51 us
    ppermute x1, starting transfers between devices, shards(): lax.ppermute(near, 'tok', [(index, index + 1) for index in range(tok_coun...  4.82 us
    pallas_call x1, Pallas kernels, load(): call(body, [IN_HBM] * count, [WHOLE] * count, [jax.ShapeDtypeStruct(array...  4.78 us
    ppermute x4, starting transfers between devices, swap(): lax.ppermute(value, 'tok', [(index, index ^ bit) for index in range(count)])  4.43 us
    ppermute x1, waiting for transfers between devices, shards(): lax.ppermute(near, 'tok', [(index, index + 1) for index in range(tok_coun...  4.37 us
  transfers between devices with their start and end apart: 34, of which 22 were waited for; matrix products, arithmetic and copies ran while one was open for 1% of the time, Pallas kernels for 22%

profile of v10, /device:TPU:1, one launch (start us, length us, event | category | flops | bytes accessed | tf_op | source)
XLA Modules:
  0.0 113.8 jit_solution(16964915193704323959)
XLA Ops:
  0.0 1.0 shard_map.100
  1.1 2.1 %collective-permute-start.4 = (bf16[256,512]{1,0:T(8,128)(2,1)S(1)}, bf16[256,512]{1,0:T(8,128)(2,1)S(1)}, u32[]{:S(2)}, u32[]{:S(2)}) collective-permute-start(bf16[256,512]{1,0:T(8,128)(2,1)S(1)} %get-tuple-element.59.refs_3_), channel_id=1, source_target_pairs={{0,1},{2,0},{4,2},{6,4},{7,6},{5,7},{3,5},{1,3},{8,9},{10,8},{12,1... | collective-permute-start | bytes 786440 | tf_op jit(solution)/shard_map/ppermute | solution.py:55
  3.3 1.4 %collective-permute-start.3 = (bf16[256,512]{1,0:T(8,128)(2,1)S(1)}, bf16[256,512]{1,0:T(8,128)(2,1)S(1)}, u32[]{:S(2)}, u32[]{:S(2)}) collective-permute-start(bf16[256,512]{1,0:T(8,128)(2,1)S(1)} %get-tuple-element.59.refs_3_), channel_id=1, source_target_pairs={{0,2},{2,4},{4,6},{6,7},{7,5},{5,3},{3,1},{1,0},{8,10},{10,12},{12... | collective-permute-start | bytes 786440 | tf_op jit(solution)/shard_map/ppermute | solution.py:55
  4.8 4.8 %shard_map.101 = (bf16[4096,512]{1,0:T(8,128)(2,1)S(1)}, bf16[4096,512]{1,0:T(8,128)(2,1)S(1)}, bf16[4096,512]{1,0:T(8,128)(2,1)S(1)}) custom-call(bf16[4096,512]{1,0:T(8,128)(2,1)} %refs_0_.1, bf16[4096,512]{1,0:T(8,128)(2,1)} %refs_1_.1, bf16[4096,512]{1,0:T(8,128)(2,1)} %refs_2_.1), custom_call_target="tpu_custom_call" | custom-call | bytes 25165824 | tf_op jit(solution)/shard_map/pallas_call | solution.py:111
  9.6 1.4 %collective-permute-start.8 = (bf16[256,512]{1,0:T(8,128)(2,1)S(1)}, bf16[256,512]{1,0:T(8,128)(2,1)S(1)}, u32[]{:S(2)}, u32[]{:S(2)}) collective-permute-start(bf16[256,512]{1,0:T(8,128)(2,1)S(1)} %collective-permute-done.4.refs_5_), channel_id=1, source_target_pairs={{0,1},{2,0},{4,2},{6,4},{7,6},{5,7},{3,5},{1,3},{8,9},{10,8},{12,1... | collective-permute-start | bytes 786440 | tf_op jit(solution)/shard_map/ppermute | solution.py:55
  11.1 2.4 %collective-permute-start.5 = (f32[4,512]{1,0:T(4,128)S(1)}, f32[4,512]{1,0:T(4,128)S(1)}, u32[]{:S(2)}, u32[]{:S(2)}) collective-permute-start(f32[4,512]{1,0:T(4,128)S(1)} %bitcast.1), channel_id=1, source_target_pairs={{0,8},{8,0},{16,24},{24,16},{1,9},{9,1},{17,25},{25,17},{2,10},{10... | collective-permute-start | bytes 24584 | tf_op jit(solution)/shard_map/ppermute | solution.py:529
  13.5 2.2 %collective-permute-done.3.refs_4_ = bf16[256,512]{1,0:T(8,128)(2,1)S(1)} collective-permute-done((bf16[256,512]{1,0:T(8,128)(2,1)S(1)}, bf16[256,512]{1,0:T(8,128)(2,1)S(1)}, u32[]{:S(2)}, u32[]{:S(2)}) %collective-permute-start.3) | collective-permute-done | bytes 262176 | tf_op jit(solution)/shard_map/ppermute | solution.py:55
  15.6 0.5 collective-permute-start.13
  16.1 1.0 collective-permute-start.11
  17.1 2.6 %shard_map.102.refs_7_ = f32[3,512,512]{2,1,0:T(8,128)S(1)} custom-call(bf16[256,512]{1,0:T(8,128)(2,1)S(1)} %get-tuple-element.56.refs_0_, bf16[256,512]{1,0:T(8,128)(2,1)S(1)} %collective-permute-done.refs_1_, bf16[256,512]{1,0:T(8,128)(2,1)S(1)} %collective-permute-done.2.refs_2_, bf16[256,512]{1,0:T(8,128)(2,1)S(1)} %get-tuple-element.59.refs_3_, ...), custom_call_target="tpu_custom_call" | custom-call | flops 2415919104 | bytes 12582912 | tf_op jit(solution)/shard_map/pallas_call | solution.py:184
  19.7 0.8 collective-permute-done.8.refs_3_
  20.5 0.7 collective-permute-done.1.refs_0_
  21.2 1.3 %collective-permute-start.9 = (bf16[256,512]{1,0:T(8,128)(2,1)S(1)}, bf16[256,512]{1,0:T(8,128)(2,1)S(1)}, u32[]{:S(2)}, u32[]{:S(2)}) collective-permute-start(bf16[256,512]{1,0:T(8,128)(2,1)S(1)} %collective-permute-done.8.refs_3_), channel_id=1, source_target_pairs={{0,1},{2,0},{4,2},{6,4},{7,6},{5,7},{3,5},{1,3},{8,9},{10,8},{12,1... | collective-permute-start | bytes 786440 | tf_op jit(solution)/shard_map/ppermute | solution.py:55
  22.7 4.2 %collective-permute-done.13.refs_2_ = bf16[256,512]{1,0:T(8,128)(2,1)S(1)} collective-permute-done((bf16[256,512]{1,0:T(8,128)(2,1)S(1)}, bf16[256,512]{1,0:T(8,128)(2,1)S(1)}, u32[]{:S(2)}, u32[]{:S(2)}) %collective-permute-start.13) | collective-permute-done | bytes 262176 | tf_op jit(solution)/shard_map/ppermute | solution.py:55
  26.9 0.5 collective-permute-start.14
  27.3 1.0 collective-permute-start.12
  28.3 3.3 %collective-permute-done.9.refs_3_ = bf16[256,512]{1,0:T(8,128)(2,1)S(1)} collective-permute-done((bf16[256,512]{1,0:T(8,128)(2,1)S(1)}, bf16[256,512]{1,0:T(8,128)(2,1)S(1)}, u32[]{:S(2)}, u32[]{:S(2)}) %collective-permute-start.9) | collective-permute-done | bytes 262176 | tf_op jit(solution)/shard_map/ppermute | solution.py:55
  31.6 1.1 collective-permute-start.10
  32.7 0.3 collective-permute-start.7
  33.1 1.8 %shard_map.103.refs_7_ = f32[3,512,512]{2,1,0:T(8,128)S(1)} custom-call(bf16[256,512]{1,0:T(8,128)(2,1)S(1)} %collective-permute-done.1.refs_0_, bf16[256,512]{1,0:T(8,128)(2,1)S(1)} %collective-permute-done.11.refs_1_, bf16[256,512]{1,0:T(8,128)(2,1)S(1)} %collective-permute-done.13.refs_2_, ...), custom_call_target="tpu_custom_call", output_to_operand_aliasing={{}: (7, {})} | custom-call | flops 1610612736 | bytes 10485760 | tf_op jit(solution)/shard_map/pallas_call | solution.py:184
  34.9 3.2 %collective-permute-done.14.refs_2_ = bf16[256,512]{1,0:T(8,128)(2,1)S(1)} collective-permute-done((bf16[256,512]{1,0:T(8,128)(2,1)S(1)}, bf16[256,512]{1,0:T(8,128)(2,1)S(1)}, u32[]{:S(2)}, u32[]{:S(2)}) %collective-permute-start.14) | collective-permute-done | bytes 262176 | tf_op jit(solution)/shard_map/ppermute | solution.py:55
  38.1 1.8 %shard_map.104.refs_3_.refs_4_ = f32[3,512,512]{2,1,0:T(8,128)S(1)} custom-call(bf16[256,512]{1,0:T(8,128)(2,1)S(1)} %collective-permute-done.6.refs_0_, bf16[256,512]{1,0:T(8,128)(2,1)S(1)} %collective-permute-done.12.refs_1_, bf16[256,512]{1,0:T(8,128)(2,1)S(1)} %collective-permute-done.14.refs_2_, ...), custom_call_target="tpu_custom_call", output_to_operand_aliasing={{}: (7, {})} | custom-call | flops 1610612736 | bytes 10485760 | tf_op jit(solution)/shard_map/pallas_call | solution.py:184
  40.0 2.8 %collective-permute-done.10.refs_1_ = bf16[256,512]{1,0:T(8,128)(2,1)S(1)} collective-permute-done((bf16[256,512]{1,0:T(8,128)(2,1)S(1)}, bf16[256,512]{1,0:T(8,128)(2,1)S(1)}, u32[]{:S(2)}, u32[]{:S(2)}) %collective-permute-start.10) | collective-permute-done | bytes 262176 | tf_op jit(solution)/shard_map/ppermute | solution.py:55
  42.8 0.9 collective-permute-done.7.refs_0_
  43.7 0.9 shard_map.106
  44.6 1.9 %collective-permute-start.16 = (bf16[2,512,256]{2,1,0:T(8,128)(2,1)S(1)}, bf16[2,512,256]{2,1,0:T(8,128)(2,1)S(1)}, u32[]{:S(2)}, u32[]{:S(2)}) collective-permute-start(bf16[2,512,256]{2,1,0:T(8,128)(2,1)S(1)} %get-tuple-element.72), channel_id=1, source_target_pairs={{0,8},{8,0},{16,24},{24,16},{1,9},{9,1},{17,25},{25,17},{2,10},{10... | collective-permute-start | bytes 1572872 | tf_op jit(solution)/shard_map/ppermute | solution.py:529
  46.6 3.1 %collective-permute-start.15 = (bf16[2,512,256]{2,1,0:T(8,128)(2,1)S(1)}, bf16[2,512,256]{2,1,0:T(8,128)(2,1)S(1)}, u32[]{:S(2)}, u32[]{:S(2)}) collective-permute-start(bf16[2,512,256]{2,1,0:T(8,128)(2,1)S(1)} %get-tuple-element.72), channel_id=1, source_target_pairs={{8,16},{9,17},{10,18},{11,19},{12,20},{13,21},{14,22},{15,23}} | collective-permute-start | bytes 1572872 | tf_op jit(solution)/shard_map/ppermute | solution.py:560
  49.7 1.4 %shard_map.109.rest_0_ = f32[2,3,128,256]{3,2,1,0:T(8,128)S(1)} custom-call(bf16[2,512,512]{2,1,0:T(8,128)(2,1)S(1)} %get-tuple-element.69.kv_ref, f32[4,512]{1,0:T(4,128)S(1)} %bitcast.2, f32[4,128,256]{2,1,0:T(8,128)S(1)} %copy-done.1, f32[4,128,256]{2,1,0:T(8,128)S(1)} %copy-done.2, f32[4,256,128]{2,1,0:T(8,128)S(1)} %copy-done.3), custom_call_target="tpu_custom_call" | custom-call | flops 402653184 | bytes 1572864 | tf_op jit(solution)/shard_map/pallas_call | solution.py:248
  51.1 1.4 %shard_map.110 = (f32[2,3,128,256]{3,2,1,0:T(8,128)S(1)}, bf16[2,3,128,256]{3,2,1,0:T(8,128)(2,1)S(1)}) custom-call(bf16[2,512,256]{2,1,0:T(8,128)(2,1)S(1)} %collective-permute-done.16.beside_ref.kv_ref, f32[4,512]{1,0:T(4,128)S(1)} %collective-permute-done.5.rate_ref, f32[4,128,256]{2,1,0:T(8,128)S(1)} %copy-done.1, f32[4,128,256]{2,1,0:T(8,128)S(1)} %copy-done.2, ...), custom_call_target="tpu_custom_call" | custom-call | flops 402653184 | bytes 1572864 | tf_op jit(solution)/shard_map/pallas_call | solution.py:248
  52.6 0.4 shard_map.105.q_ref
  53.1 2.1 %shard_map.107 = (f32[512,512]{1,0:T(8,128)S(1)}, f32[2,512,512]{2,1,0:T(8,128)S(1)}) custom-call(bf16[1,512,512]{2,1,0:T(8,128)(2,1)S(1)} %shard_map.105.q_ref, bf16[2,512,512]{2,1,0:T(8,128)(2,1)S(1)} %get-tuple-element.69.kv_ref), custom_call_target="tpu_custom_call" | custom-call | flops 402653184 | bytes 2097152 | tf_op jit(solution)/shard_map/pallas_call | solution.py:342
  55.2 3.1 %collective-permute-done.15.behind_ref = bf16[2,512,256]{2,1,0:T(8,128)(2,1)S(1)} collective-permute-done((bf16[2,512,256]{2,1,0:T(8,128)(2,1)S(1)}, bf16[2,512,256]{2,1,0:T(8,128)(2,1)S(1)}, u32[]{:S(2)}, u32[]{:S(2)}) %collective-permute-start.15) | collective-permute-done | bytes 524320 | tf_op jit(solution)/shard_map/ppermute | solution.py:560
  58.3 1.2 %shard_map.108.rest_1_.attended_ref = f32[512,512]{1,0:T(8,128)S(1)} custom-call(f32[512,512]{1,0:T(8,128)S(1)} %get-tuple-element.70.sum_ref, f32[2,512,512]{2,1,0:T(8,128)S(1)} %get-tuple-element.71.stats_ref, bf16[1,512,512]{2,1,0:T(8,128)(2,1)S(1)} %shard_map.105.q_ref, ...), custom_call_target="tpu_custom_call", output_to_operand_aliasing={{}: (0, {})} | custom-call | flops 201326592 | bytes 1048576 | tf_op jit(solution)/shard_map/pallas_call | solution.py:384
  59.6 4.8 %collective-permute-start.17 = (bf16[2,512,256]{2,1,0:T(8,128)(2,1)S(1)}, bf16[2,512,256]{2,1,0:T(8,128)(2,1)S(1)}, u32[]{:S(2)}, u32[]{:S(2)}) collective-permute-start(bf16[2,512,256]{2,1,0:T(8,128)(2,1)S(1)} %get-tuple-element.74), channel_id=1, source_target_pairs={{0,8},{8,16},{16,24},{1,9},{9,17},{17,25},{2,10},{10,18},{18,26},{... | collective-permute-start | bytes 1572872 | tf_op jit(solution)/shard_map/ppermute | solution.py:575
  64.4 0.8 shard_map.111.net_ref
  65.3 0.8 shard_map.112.near_ref
  66.1 4.4 %collective-permute-done.17.behind_ref = bf16[2,512,256]{2,1,0:T(8,128)(2,1)S(1)} collective-permute-done((bf16[2,512,256]{2,1,0:T(8,128)(2,1)S(1)}, bf16[2,512,256]{2,1,0:T(8,128)(2,1)S(1)}, u32[]{:S(2)}, u32[]{:S(2)}) %collective-permute-start.17) | collective-permute-done | bytes 524320 | tf_op jit(solution)/shard_map/ppermute | solution.py:575
  70.5 1.9 %shard_map.114 = (bf16[64,2048]{1,0:T(8,128)(2,1)S(1)}, bf16[64,2048]{1,0:T(8,128)(2,1)S(1)}) custom-call(bf16[1,512,512]{2,1,0:T(8,128)(2,1)S(1)} %shard_map.105.q_ref, f32[512,512]{1,0:T(8,128)S(1)} %shard_map.108.rest_1_.attended_ref, f32[2,512,512]{2,1,0:T(8,128)S(1)} %get-tuple-element.71.stats_ref, ...), custom_call_target="tpu_custom_call" | custom-call | flops 268435456 | bytes 4718592 | tf_op jit(solution)/shard_map/pallas_call | solution.py:469
  72.4 1.3 %collective-permute-start.21 = (bf16[64,2048]{1,0:T(8,128)(2,1)S(1)}, bf16[64,2048]{1,0:T(8,128)(2,1)S(1)}, u32[]{:S(2)}, u32[]{:S(2)}) collective-permute-start(bf16[64,2048]{1,0:T(8,128)(2,1)S(1)} %get-tuple-element.80), channel_id=1, source_target_pairs={{0,1},{2,0},{4,2},{6,4},{7,6},{5,7},{3,5},{1,3},{8,9},{10,8},{12,1... | collective-permute-start | bytes 786440 | tf_op jit(solution)/shard_map/ppermute | solution.py:55
  73.7 0.2 collective-permute-start.20
  73.9 1.8 %shard_map.113 = (bf16[64,2048]{1,0:T(8,128)(2,1)S(1)}, bf16[64,2048]{1,0:T(8,128)(2,1)S(1)}, bf16[64,2048]{1,0:T(8,128)(2,1)S(1)}, bf16[64,2048]{1,0:T(8,128)(2,1)S(1)}) custom-call(bf16[1,512,512]{2,1,0:T(8,128)(2,1)S(1)} %shard_map.105.q_ref, f32[512,512]{1,0:T(8,128)S(1)} %shard_map.108.rest_1_.attended_ref, ...), custom_call_target="tpu_custom_call" | custom-call | flops 536870912 | bytes 5242880 | tf_op jit(solution)/shard_map/pallas_call | solution.py:469
  75.6 1.3 %collective-permute-start.25 = (bf16[64,2048]{1,0:T(8,128)(2,1)S(1)}, bf16[64,2048]{1,0:T(8,128)(2,1)S(1)}, u32[]{:S(2)}, u32[]{:S(2)}) collective-permute-start(bf16[64,2048]{1,0:T(8,128)(2,1)S(1)} %get-tuple-element.84), channel_id=1, source_target_pairs={{0,1},{2,0},{4,2},{6,4},{7,6},{5,7},{3,5},{1,3},{8,9},{10,8},{12,1... | collective-permute-start | bytes 786440 | tf_op jit(solution)/shard_map/ppermute | solution.py:55
  77.2 2.6 %collective-permute-done.21.refs_1_ = bf16[64,2048]{1,0:T(8,128)(2,1)S(1)} collective-permute-done((bf16[64,2048]{1,0:T(8,128)(2,1)S(1)}, bf16[64,2048]{1,0:T(8,128)(2,1)S(1)}, u32[]{:S(2)}, u32[]{:S(2)}) %collective-permute-start.21) | collective-permute-done | bytes 262176 | tf_op jit(solution)/shard_map/ppermute | solution.py:55
  79.8 1.4 %collective-permute-done.20.refs_0_ = bf16[64,2048]{1,0:T(8,128)(2,1)S(1)} collective-permute-done((bf16[64,2048]{1,0:T(8,128)(2,1)S(1)}, bf16[64,2048]{1,0:T(8,128)(2,1)S(1)}, u32[]{:S(2)}, u32[]{:S(2)}) %collective-permute-start.20) | collective-permute-done | bytes 262176 | tf_op jit(solution)/shard_map/ppermute | solution.py:55
  81.3 1.3 %collective-permute-start.23 = (bf16[64,2048]{1,0:T(8,128)(2,1)S(1)}, bf16[64,2048]{1,0:T(8,128)(2,1)S(1)}, u32[]{:S(2)}, u32[]{:S(2)}) collective-permute-start(bf16[64,2048]{1,0:T(8,128)(2,1)S(1)} %add_convert_fusion.10), channel_id=1, source_target_pairs={{0,1},{2,0},{4,2},{6,4},{7,6},{5,7},{3,5},{1,3},{8,9},{10,8},{12,1... | collective-permute-start | bytes 786440 | tf_op jit(solution)/shard_map/ppermute | solution.py:55
  82.8 1.8 %shard_map.116 = (bf16[64,2048]{1,0:T(8,128)(2,1)S(1)}, bf16[64,2048]{1,0:T(8,128)(2,1)S(1)}, bf16[64,2048]{1,0:T(8,128)(2,1)S(1)}, bf16[64,2048]{1,0:T(8,128)(2,1)S(1)}) custom-call(bf16[1,512,512]{2,1,0:T(8,128)(2,1)S(1)} %shard_map.105.q_ref, f32[512,512]{1,0:T(8,128)S(1)} %shard_map.108.rest_1_.attended_ref, ...), custom_call_target="tpu_custom_call" | custom-call | flops 536870912 | bytes 5242880 | tf_op jit(solution)/shard_map/pallas_call | solution.py:469
  84.5 0.8 collective-permute-done.25
  85.4 1.4 %collective-permute-done.24 = bf16[64,2048]{1,0:T(8,128)(2,1)S(1)} collective-permute-done((bf16[64,2048]{1,0:T(8,128)(2,1)S(1)}, bf16[64,2048]{1,0:T(8,128)(2,1)S(1)}, u32[]{:S(2)}, u32[]{:S(2)}) %collective-permute-start.24) | collective-permute-done | bytes 262176 | tf_op jit(solution)/shard_map/ppermute | solution.py:55
  86.9 1.3 %collective-permute-start.27 = (bf16[64,2048]{1,0:T(8,128)(2,1)S(1)}, bf16[64,2048]{1,0:T(8,128)(2,1)S(1)}, u32[]{:S(2)}, u32[]{:S(2)}) collective-permute-start(bf16[64,2048]{1,0:T(8,128)(2,1)S(1)} %add_convert_fusion.8), channel_id=1, source_target_pairs={{0,1},{2,0},{4,2},{6,4},{7,6},{5,7},{3,5},{1,3},{8,9},{10,8},{12,1... | collective-permute-start | bytes 786440 | tf_op jit(solution)/shard_map/ppermute | solution.py:55
  88.4 2.6 %collective-permute-done.23.refs_1_ = bf16[64,2048]{1,0:T(8,128)(2,1)S(1)} collective-permute-done((bf16[64,2048]{1,0:T(8,128)(2,1)S(1)}, bf16[64,2048]{1,0:T(8,128)(2,1)S(1)}, u32[]{:S(2)}, u32[]{:S(2)}) %collective-permute-start.23) | collective-permute-done | bytes 262176 | tf_op jit(solution)/shard_map/ppermute | solution.py:55
  91.1 1.4 %collective-permute-done.22.refs_0_ = bf16[64,2048]{1,0:T(8,128)(2,1)S(1)} collective-permute-done((bf16[64,2048]{1,0:T(8,128)(2,1)S(1)}, bf16[64,2048]{1,0:T(8,128)(2,1)S(1)}, u32[]{:S(2)}, u32[]{:S(2)}) %collective-permute-start.22) | collective-permute-done | bytes 262176 | tf_op jit(solution)/shard_map/ppermute | solution.py:55
  92.5 1.3 %collective-permute-start.31 = (bf16[64,2048]{1,0:T(8,128)(2,1)S(1)}, bf16[64,2048]{1,0:T(8,128)(2,1)S(1)}, u32[]{:S(2)}, u32[]{:S(2)}) collective-permute-start(bf16[64,2048]{1,0:T(8,128)(2,1)S(1)} %add_convert_fusion.4), channel_id=1, source_target_pairs={{0,1},{2,0},{4,2},{6,4},{7,6},{5,7},{3,5},{1,3},{8,9},{10,8},{12,1... | collective-permute-start | bytes 786440 | tf_op jit(solution)/shard_map/ppermute | solution.py:55
  94.0 2.1 %shard_map.115 = (bf16[64,2048]{1,0:T(8,128)(2,1)S(1)}, bf16[64,2048]{1,0:T(8,128)(2,1)S(1)}, bf16[64,2048]{1,0:T(8,128)(2,1)S(1)}, bf16[64,2048]{1,0:T(8,128)(2...) custom-call(bf16[1,512,512]{2,1,0:T(8,128)(2,1)S(1)} %shard_map.105.q_ref, ...), custom_call_target="tpu_custom_call" | custom-call | flops 805306368 | bytes 5767168 | tf_op jit(solution)/shard_map/pallas_call | solution.py:469
  96.2 0.4 collective-permute-done.27
  96.7 1.4 %collective-permute-done.26 = bf16[64,2048]{1,0:T(8,128)(2,1)S(1)} collective-permute-done((bf16[64,2048]{1,0:T(8,128)(2,1)S(1)}, bf16[64,2048]{1,0:T(8,128)(2,1)S(1)}, u32[]{:S(2)}, u32[]{:S(2)}) %collective-permute-start.26) | collective-permute-done | bytes 262176 | tf_op jit(solution)/shard_map/ppermute | solution.py:55
  98.1 0.2 collective-permute-start.28
  98.3 1.3 %collective-permute-start.29 = (bf16[64,2048]{1,0:T(8,128)(2,1)S(1)}, bf16[64,2048]{1,0:T(8,128)(2,1)S(1)}, u32[]{:S(2)}, u32[]{:S(2)}) collective-permute-start(bf16[64,2048]{1,0:T(8,128)(2,1)S(1)} %add_convert_fusion.6), channel_id=1, source_target_pairs={{0,1},{2,0},{4,2},{6,4},{7,6},{5,7},{3,5},{1,3},{8,9},{10,8},{12,1... | collective-permute-start | bytes 786440 | tf_op jit(solution)/shard_map/ppermute | solution.py:55
  99.6 2.4 %collective-permute-done.31 = bf16[64,2048]{1,0:T(8,128)(2,1)S(1)} collective-permute-done((bf16[64,2048]{1,0:T(8,128)(2,1)S(1)}, bf16[64,2048]{1,0:T(8,128)(2,1)S(1)}, u32[]{:S(2)}, u32[]{:S(2)}) %collective-permute-start.31) | collective-permute-done | bytes 262176 | tf_op jit(solution)/shard_map/ppermute | solution.py:55
  102.1 1.6 %collective-permute-done.30 = bf16[64,2048]{1,0:T(8,128)(2,1)S(1)} collective-permute-done((bf16[64,2048]{1,0:T(8,128)(2,1)S(1)}, bf16[64,2048]{1,0:T(8,128)(2,1)S(1)}, u32[]{:S(2)}, u32[]{:S(2)}) %collective-permute-start.30) | collective-permute-done | bytes 262176 | tf_op jit(solution)/shard_map/ppermute | solution.py:55
  103.7 0.2 collective-permute-start.32
  104.0 1.3 %collective-permute-start.33 = (bf16[64,2048]{1,0:T(8,128)(2,1)S(1)}, bf16[64,2048]{1,0:T(8,128)(2,1)S(1)}, u32[]{:S(2)}, u32[]{:S(2)}) collective-permute-start(bf16[64,2048]{1,0:T(8,128)(2,1)S(1)} %add_convert_fusion.2), channel_id=1, source_target_pairs={{0,1},{2,0},{4,2},{6,4},{7,6},{5,7},{3,5},{1,3},{8,9},{10,8},{12,1... | collective-permute-start | bytes 786440 | tf_op jit(solution)/shard_map/ppermute | solution.py:55
  105.3 4.0 %collective-permute-done.28.refs_2_ = bf16[64,2048]{1,0:T(8,128)(2,1)S(1)} collective-permute-done((bf16[64,2048]{1,0:T(8,128)(2,1)S(1)}, bf16[64,2048]{1,0:T(8,128)(2,1)S(1)}, u32[]{:S(2)}, u32[]{:S(2)}) %collective-permute-start.28) | collective-permute-done | bytes 262176 | tf_op jit(solution)/shard_map/ppermute | solution.py:55
  109.4 3.5 %collective-permute-done.32 = bf16[64,2048]{1,0:T(8,128)(2,1)S(1)} collective-permute-done((bf16[64,2048]{1,0:T(8,128)(2,1)S(1)}, bf16[64,2048]{1,0:T(8,128)(2,1)S(1)}, u32[]{:S(2)}, u32[]{:S(2)}) %collective-permute-start.32) | collective-permute-done | bytes 262176 | tf_op jit(solution)/shard_map/ppermute | solution.py:55
  113.0 0.8 pad_maximum_fusion
  (47 shorter events, 2.3 us)
Async XLA Ops:
  1.1 8.5 %collective-permute-start.4 = (bf16[256,512]{1,0:T(8,128)(2,1)S(1)}, bf16[256,512]{1,0:T(8,128)(2,1)S(1)}, u32[]{:S(2)}, u32[]{:S(2)}) collective-permute-start(bf16[256,512]{1,0:T(8,128)(2,1)S(1)} %get-tuple-element.59.refs_3_), channel_id=1, source_target_pairs={{0,1},{2,0},{4,2},{6,4},{7,6},{5,7},{3,5},{1,3},{8,9},{10,8},{12,1... | collective-permute-start | bytes 786440 | tf_op jit(solution)/shard_map/ppermute | solution.py:55
  3.1 8.0 %copy-start.4 = (f32[512,4]{0,1:T(4,128)S(1)}, f32[512,4]{0,1:T(4,128)}, u32[]{:S(2)}) copy-start(f32[512,4]{0,1:T(4,128)} %param.18) | copy-start | bytes 24580
  3.1 7.8 %collective-permute-start = (bf16[256,512]{1,0:T(8,128)(2,1)S(1)}, bf16[256,512]{1,0:T(8,128)(2,1)S(1)}, u32[]{:S(2)}, u32[]{:S(2)}) collective-permute-start(bf16[256,512]{1,0:T(8,128)(2,1)S(1)} %get-tuple-element.56.refs_0_), channel_id=1, source_target_pairs={{0,2},{2,4},{4,6},{6,7},{7,5},{5,3},{3,1},{1,0},{8,10},{10,12},{12... | collective-permute-start | bytes 786440 | tf_op jit(solution)/shard_map/ppermute | solution.py:55
  3.3 12.3 %collective-permute-start.3 = (bf16[256,512]{1,0:T(8,128)(2,1)S(1)}, bf16[256,512]{1,0:T(8,128)(2,1)S(1)}, u32[]{:S(2)}, u32[]{:S(2)}) collective-permute-start(bf16[256,512]{1,0:T(8,128)(2,1)S(1)} %get-tuple-element.59.refs_3_), channel_id=1, source_target_pairs={{0,2},{2,4},{4,6},{6,7},{7,5},{5,3},{3,1},{1,0},{8,10},{10,12},{12... | collective-permute-start | bytes 786440 | tf_op jit(solution)/shard_map/ppermute | solution.py:55
  4.7 11.4 %collective-permute-start.2 = (bf16[256,512]{1,0:T(8,128)(2,1)S(1)}, bf16[256,512]{1,0:T(8,128)(2,1)S(1)}, u32[]{:S(2)}, u32[]{:S(2)}) collective-permute-start(bf16[256,512]{1,0:T(8,128)(2,1)S(1)} %get-tuple-element.56.refs_0_), channel_id=1, source_target_pairs={{0,1},{2,0},{4,2},{6,4},{7,6},{5,7},{3,5},{1,3},{8,9},{10,8},{12,1... | collective-permute-start | bytes 786440 | tf_op jit(solution)/shard_map/ppermute | solution.py:55
  9.6 10.9 %collective-permute-start.8 = (bf16[256,512]{1,0:T(8,128)(2,1)S(1)}, bf16[256,512]{1,0:T(8,128)(2,1)S(1)}, u32[]{:S(2)}, u32[]{:S(2)}) collective-permute-start(bf16[256,512]{1,0:T(8,128)(2,1)S(1)} %collective-permute-done.4.refs_5_), channel_id=1, source_target_pairs={{0,1},{2,0},{4,2},{6,4},{7,6},{5,7},{3,5},{1,3},{8,9},{10,8},{12,1... | collective-permute-start | bytes 786440 | tf_op jit(solution)/shard_map/ppermute | solution.py:55
  10.9 10.3 %collective-permute-start.1 = (bf16[256,512]{1,0:T(8,128)(2,1)S(1)}, bf16[256,512]{1,0:T(8,128)(2,1)S(1)}, u32[]{:S(2)}, u32[]{:S(2)}) collective-permute-start(bf16[256,512]{1,0:T(8,128)(2,1)S(1)} %collective-permute-done.refs_1_), channel_id=1, source_target_pairs={{0,2},{2,4},{4,6},{6,7},{7,5},{5,3},{3,1},{1,0},{8,10},{10,12},{12... | collective-permute-start | bytes 786440 | tf_op jit(solution)/shard_map/ppermute | solution.py:55
  11.1 8.6 %collective-permute-start.5 = (f32[4,512]{1,0:T(4,128)S(1)}, f32[4,512]{1,0:T(4,128)S(1)}, u32[]{:S(2)}, u32[]{:S(2)}) collective-permute-start(f32[4,512]{1,0:T(4,128)S(1)} %bitcast.1), channel_id=1, source_target_pairs={{0,8},{8,0},{16,24},{24,16},{1,9},{9,1},{17,25},{25,17},{2,10},{10... | collective-permute-start | bytes 24584 | tf_op jit(solution)/shard_map/ppermute | solution.py:529
  15.6 11.2 %collective-permute-start.13 = (bf16[256,512]{1,0:T(8,128)(2,1)S(1)}, bf16[256,512]{1,0:T(8,128)(2,1)S(1)}, u32[]{:S(2)}, u32[]{:S(2)}) collective-permute-start(bf16[256,512]{1,0:T(8,128)(2,1)S(1)} %collective-permute-done.3.refs_4_), channel_id=1, source_target_pairs={{0,2},{2,4},{4,6},{6,7},{7,5},{5,3},{3,1},{1,0},{8,10},{10,12},{12... | collective-permute-start | bytes 786440 | tf_op jit(solution)/shard_map/ppermute | solution.py:55
  16.1 10.8 %collective-permute-start.11 = (bf16[256,512]{1,0:T(8,128)(2,1)S(1)}, bf16[256,512]{1,0:T(8,128)(2,1)S(1)}, u32[]{:S(2)}, u32[]{:S(2)}) collective-permute-start(bf16[256,512]{1,0:T(8,128)(2,1)S(1)} %collective-permute-done.2.refs_2_), channel_id=1, source_target_pairs={{0,1},{2,0},{4,2},{6,4},{7,6},{5,7},{3,5},{1,3},{8,9},{10,8},{12,1... | collective-permute-start | bytes 786440 | tf_op jit(solution)/shard_map/ppermute | solution.py:55
  21.2 10.3 %collective-permute-start.9 = (bf16[256,512]{1,0:T(8,128)(2,1)S(1)}, bf16[256,512]{1,0:T(8,128)(2,1)S(1)}, u32[]{:S(2)}, u32[]{:S(2)}) collective-permute-start(bf16[256,512]{1,0:T(8,128)(2,1)S(1)} %collective-permute-done.8.refs_3_), channel_id=1, source_target_pairs={{0,1},{2,0},{4,2},{6,4},{7,6},{5,7},{3,5},{1,3},{8,9},{10,8},{12,1... | collective-permute-start | bytes 786440 | tf_op jit(solution)/shard_map/ppermute | solution.py:55
  22.5 10.2 %collective-permute-start.6 = (bf16[256,512]{1,0:T(8,128)(2,1)S(1)}, bf16[256,512]{1,0:T(8,128)(2,1)S(1)}, u32[]{:S(2)}, u32[]{:S(2)}) collective-permute-start(bf16[256,512]{1,0:T(8,128)(2,1)S(1)} %collective-permute-done.1.refs_0_), channel_id=1, source_target_pairs={{0,2},{2,4},{4,6},{6,7},{7,5},{5,3},{3,1},{1,0},{8,10},{10,12},{12... | collective-permute-start | bytes 786440 | tf_op jit(solution)/shard_map/ppermute | solution.py:55
  26.9 11.2 %collective-permute-start.14 = (bf16[256,512]{1,0:T(8,128)(2,1)S(1)}, bf16[256,512]{1,0:T(8,128)(2,1)S(1)}, u32[]{:S(2)}, u32[]{:S(2)}) collective-permute-start(bf16[256,512]{1,0:T(8,128)(2,1)S(1)} %collective-permute-done.13.refs_2_), channel_id=1, source_target_pairs={{0,2},{2,4},{4,6},{6,7},{7,5},{5,3},{3,1},{1,0},{8,10},{10,12},{12... | collective-permute-start | bytes 786440 | tf_op jit(solution)/shard_map/ppermute | solution.py:55
  27.3 10.8 %collective-permute-start.12 = (bf16[256,512]{1,0:T(8,128)(2,1)S(1)}, bf16[256,512]{1,0:T(8,128)(2,1)S(1)}, u32[]{:S(2)}, u32[]{:S(2)}) collective-permute-start(bf16[256,512]{1,0:T(8,128)(2,1)S(1)} %collective-permute-done.11.refs_1_), channel_id=1, source_target_pairs={{0,1},{2,0},{4,2},{6,4},{7,6},{5,7},{3,5},{1,3},{8,9},{10,8},{12,1... | collective-permute-start | bytes 786440 | tf_op jit(solution)/shard_map/ppermute | solution.py:55
  31.6 11.2 %collective-permute-start.10 = (bf16[256,512]{1,0:T(8,128)(2,1)S(1)}, bf16[256,512]{1,0:T(8,128)(2,1)S(1)}, u32[]{:S(2)}, u32[]{:S(2)}) collective-permute-start(bf16[256,512]{1,0:T(8,128)(2,1)S(1)} %collective-permute-done.9.refs_3_), channel_id=1, source_target_pairs={{0,1},{2,0},{4,2},{6,4},{7,6},{5,7},{3,5},{1,3},{8,9},{10,8},{12,1... | collective-permute-start | bytes 786440 | tf_op jit(solution)/shard_map/ppermute | solution.py:55
  32.7 11.0 %collective-permute-start.7 = (bf16[256,512]{1,0:T(8,128)(2,1)S(1)}, bf16[256,512]{1,0:T(8,128)(2,1)S(1)}, u32[]{:S(2)}, u32[]{:S(2)}) collective-permute-start(bf16[256,512]{1,0:T(8,128)(2,1)S(1)} %collective-permute-done.6.refs_0_), channel_id=1, source_target_pairs={{0,2},{2,4},{4,6},{6,7},{7,5},{5,3},{3,1},{1,0},{8,10},{10,12},{12... | collective-permute-start | bytes 786440 | tf_op jit(solution)/shard_map/ppermute | solution.py:55
  39.9 9.7 %copy-start.1 = (f32[4,128,256]{2,1,0:T(8,128)S(1)}, f32[4,128,256]{2,1,0:T(8,128)}, u32[]{:S(2)}) copy-start(f32[4,128,256]{2,1,0:T(8,128)} %gate_ref.5) | copy-start | bytes 1572868
  40.0 9.7 %copy-start.2 = (f32[4,128,256]{2,1,0:T(8,128)S(1)}, f32[4,128,256]{2,1,0:T(8,128)}, u32[]{:S(2)}) copy-start(f32[4,128,256]{2,1,0:T(8,128)} %up_ref.5) | copy-start | bytes 1572868
  40.0 9.7 %copy-start.3 = (f32[4,256,128]{2,1,0:T(8,128)S(1)}, f32[4,256,128]{2,1,0:T(8,128)}, u32[]{:S(2)}) copy-start(f32[4,256,128]{2,1,0:T(8,128)} %down_ref.5) | copy-start | bytes 1572868
  44.6 6.5 %collective-permute-start.16 = (bf16[2,512,256]{2,1,0:T(8,128)(2,1)S(1)}, bf16[2,512,256]{2,1,0:T(8,128)(2,1)S(1)}, u32[]{:S(2)}, u32[]{:S(2)}) collective-permute-start(bf16[2,512,256]{2,1,0:T(8,128)(2,1)S(1)} %get-tuple-element.72), channel_id=1, source_target_pairs={{0,8},{8,0},{16,24},{24,16},{1,9},{9,1},{17,25},{25,17},{2,10},{10... | collective-permute-start | bytes 1572872 | tf_op jit(solution)/shard_map/ppermute | solution.py:529
  46.6 11.8 %collective-permute-start.15 = (bf16[2,512,256]{2,1,0:T(8,128)(2,1)S(1)}, bf16[2,512,256]{2,1,0:T(8,128)(2,1)S(1)}, u32[]{:S(2)}, u32[]{:S(2)}) collective-permute-start(bf16[2,512,256]{2,1,0:T(8,128)(2,1)S(1)} %get-tuple-element.72), channel_id=1, source_target_pairs={{8,16},{9,17},{10,18},{11,19},{12,20},{13,21},{14,22},{15,23}} | collective-permute-start | bytes 1572872 | tf_op jit(solution)/shard_map/ppermute | solution.py:560
  52.6 11.8 %collective-permute-start.18 = (bf16[2,3,128,256]{3,2,1,0:T(8,128)(2,1)S(1)}, bf16[2,3,128,256]{3,2,1,0:T(8,128)(2,1)S(1)}, u32[]{:S(2)}, u32[]{:S(2)}) collective-permute-start(bf16[2,3,128,256]{3,2,1,0:T(8,128)(2,1)S(1)} %get-tuple-element.76), channel_id=1, source_target_pairs={{0,16},{8,24},{16,0},{24,8},{1,17},{9,25},{17,1},{25,9},{2,18},{10... | collective-permute-start | bytes 1179656 | tf_op jit(solution)/shard_map/ppermute | solution.py:529
  53.1 11.3 %copy-start.5 = (f32[4]{0:T(128)S(1)}, f32[4]{0:T(128)}, u32[]{:S(2)}) copy-start(f32[4]{0:T(128)} %step_ref.1) | copy-start | bytes 52
  59.6 10.9 %copy-start = (bf16[512,4096]{1,0:T(8,128)(2,1)S(1)}, bf16[512,4096]{1,0:T(8,128)(2,1)}, u32[]{:S(2)}) copy-start(bf16[512,4096]{1,0:T(8,128)(2,1)} %w_ref.7) | copy-start | bytes 12582916
  59.6 10.9 %collective-permute-start.17 = (bf16[2,512,256]{2,1,0:T(8,128)(2,1)S(1)}, bf16[2,512,256]{2,1,0:T(8,128)(2,1)S(1)}, u32[]{:S(2)}, u32[]{:S(2)}) collective-permute-start(bf16[2,512,256]{2,1,0:T(8,128)(2,1)S(1)} %get-tuple-element.74), channel_id=1, source_target_pairs={{0,8},{8,16},{16,24},{1,9},{9,17},{17,25},{2,10},{10,18},{18,26},{... | collective-permute-start | bytes 1572872 | tf_op jit(solution)/shard_map/ppermute | solution.py:575
  65.3 5.2 %collective-permute-start.19 = (bf16[2,3,128,256]{3,2,1,0:T(8,128)(2,1)S(1)}, bf16[2,3,128,256]{3,2,1,0:T(8,128)(2,1)S(1)}, u32[]{:S(2)}, u32[]{:S(2)}) collective-permute-start(bf16[2,3,128,256]{3,2,1,0:T(8,128)(2,1)S(1)} %shard_map.111.net_ref), channel_id=1, source_target_pairs={{0,8},{8,0},{16,24},{24,16},{1,9},{9,1},{17,25},{25,17},{2,10},{10... | collective-permute-start | bytes 1179656 | tf_op jit(solution)/shard_map/ppermute | solution.py:529
  72.4 7.4 %collective-permute-start.21 = (bf16[64,2048]{1,0:T(8,128)(2,1)S(1)}, bf16[64,2048]{1,0:T(8,128)(2,1)S(1)}, u32[]{:S(2)}, u32[]{:S(2)}) collective-permute-start(bf16[64,2048]{1,0:T(8,128)(2,1)S(1)} %get-tuple-element.80), channel_id=1, source_target_pairs={{0,1},{2,0},{4,2},{6,4},{7,6},{5,7},{3,5},{1,3},{8,9},{10,8},{12,1... | collective-permute-start | bytes 786440 | tf_op jit(solution)/shard_map/ppermute | solution.py:55
  73.7 7.5 %collective-permute-start.20 = (bf16[64,2048]{1,0:T(8,128)(2,1)S(1)}, bf16[64,2048]{1,0:T(8,128)(2,1)S(1)}, u32[]{:S(2)}, u32[]{:S(2)}) collective-permute-start(bf16[64,2048]{1,0:T(8,128)(2,1)S(1)} %get-tuple-element.78), channel_id=1, source_target_pairs={{0,2},{2,4},{4,6},{6,7},{7,5},{5,3},{3,1},{1,0},{8,10},{10,12},{12... | collective-permute-start | bytes 786440 | tf_op jit(solution)/shard_map/ppermute | solution.py:55
  75.6 9.7 %collective-permute-start.25 = (bf16[64,2048]{1,0:T(8,128)(2,1)S(1)}, bf16[64,2048]{1,0:T(8,128)(2,1)S(1)}, u32[]{:S(2)}, u32[]{:S(2)}) collective-permute-start(bf16[64,2048]{1,0:T(8,128)(2,1)S(1)} %get-tuple-element.84), channel_id=1, source_target_pairs={{0,1},{2,0},{4,2},{6,4},{7,6},{5,7},{3,5},{1,3},{8,9},{10,8},{12,1... | collective-permute-start | bytes 786440 | tf_op jit(solution)/shard_map/ppermute | solution.py:55
  77.0 9.8 %collective-permute-start.24 = (bf16[64,2048]{1,0:T(8,128)(2,1)S(1)}, bf16[64,2048]{1,0:T(8,128)(2,1)S(1)}, u32[]{:S(2)}, u32[]{:S(2)}) collective-permute-start(bf16[64,2048]{1,0:T(8,128)(2,1)S(1)} %get-tuple-element.83), channel_id=1, source_target_pairs={{0,2},{2,4},{4,6},{6,7},{7,5},{5,3},{3,1},{1,0},{8,10},{10,12},{12... | collective-permute-start | bytes 786440 | tf_op jit(solution)/shard_map/ppermute | solution.py:55
  81.3 9.7 %collective-permute-start.23 = (bf16[64,2048]{1,0:T(8,128)(2,1)S(1)}, bf16[64,2048]{1,0:T(8,128)(2,1)S(1)}, u32[]{:S(2)}, u32[]{:S(2)}) collective-permute-start(bf16[64,2048]{1,0:T(8,128)(2,1)S(1)} %add_convert_fusion.10), channel_id=1, source_target_pairs={{0,1},{2,0},{4,2},{6,4},{7,6},{5,7},{3,5},{1,3},{8,9},{10,8},{12,1... | collective-permute-start | bytes 786440 | tf_op jit(solution)/shard_map/ppermute | solution.py:55
  82.6 9.8 %collective-permute-start.22 = (bf16[64,2048]{1,0:T(8,128)(2,1)S(1)}, bf16[64,2048]{1,0:T(8,128)(2,1)S(1)}, u32[]{:S(2)}, u32[]{:S(2)}) collective-permute-start(bf16[64,2048]{1,0:T(8,128)(2,1)S(1)} %add_convert_fusion.11), channel_id=1, source_target_pairs={{0,2},{2,4},{4,6},{6,7},{7,5},{5,3},{3,1},{1,0},{8,10},{10,12},{12... | collective-permute-start | bytes 786440 | tf_op jit(solution)/shard_map/ppermute | solution.py:55
  86.9 9.7 %collective-permute-start.27 = (bf16[64,2048]{1,0:T(8,128)(2,1)S(1)}, bf16[64,2048]{1,0:T(8,128)(2,1)S(1)}, u32[]{:S(2)}, u32[]{:S(2)}) collective-permute-start(bf16[64,2048]{1,0:T(8,128)(2,1)S(1)} %add_convert_fusion.8), channel_id=1, source_target_pairs={{0,1},{2,0},{4,2},{6,4},{7,6},{5,7},{3,5},{1,3},{8,9},{10,8},{12,1... | collective-permute-start | bytes 786440 | tf_op jit(solution)/shard_map/ppermute | solution.py:55
  88.2 9.8 %collective-permute-start.26 = (bf16[64,2048]{1,0:T(8,128)(2,1)S(1)}, bf16[64,2048]{1,0:T(8,128)(2,1)S(1)}, u32[]{:S(2)}, u32[]{:S(2)}) collective-permute-start(bf16[64,2048]{1,0:T(8,128)(2,1)S(1)} %add_convert_fusion.9), channel_id=1, source_target_pairs={{0,2},{2,4},{4,6},{6,7},{7,5},{5,3},{3,1},{1,0},{8,10},{10,12},{12... | collective-permute-start | bytes 786440 | tf_op jit(solution)/shard_map/ppermute | solution.py:55
  92.5 9.5 %collective-permute-start.31 = (bf16[64,2048]{1,0:T(8,128)(2,1)S(1)}, bf16[64,2048]{1,0:T(8,128)(2,1)S(1)}, u32[]{:S(2)}, u32[]{:S(2)}) collective-permute-start(bf16[64,2048]{1,0:T(8,128)(2,1)S(1)} %add_convert_fusion.4), channel_id=1, source_target_pairs={{0,1},{2,0},{4,2},{6,4},{7,6},{5,7},{3,5},{1,3},{8,9},{10,8},{12,1... | collective-permute-start | bytes 786440 | tf_op jit(solution)/shard_map/ppermute | solution.py:55
  93.9 9.8 %collective-permute-start.30 = (bf16[64,2048]{1,0:T(8,128)(2,1)S(1)}, bf16[64,2048]{1,0:T(8,128)(2,1)S(1)}, u32[]{:S(2)}, u32[]{:S(2)}) collective-permute-start(bf16[64,2048]{1,0:T(8,128)(2,1)S(1)} %add_convert_fusion.5), channel_id=1, source_target_pairs={{0,2},{2,4},{4,6},{6,7},{7,5},{5,3},{3,1},{1,0},{8,10},{10,12},{12... | collective-permute-start | bytes 786440 | tf_op jit(solution)/shard_map/ppermute | solution.py:55
  98.1 11.2 %collective-permute-start.28 = (bf16[64,2048]{1,0:T(8,128)(2,1)S(1)}, bf16[64,2048]{1,0:T(8,128)(2,1)S(1)}, u32[]{:S(2)}, u32[]{:S(2)}) collective-permute-start(bf16[64,2048]{1,0:T(8,128)(2,1)S(1)} %add_convert_fusion.7), channel_id=1, source_target_pairs={{0,2},{2,4},{4,6},{6,7},{7,5},{5,3},{3,1},{1,0},{8,10},{10,12},{12... | collective-permute-start | bytes 786440 | tf_op jit(solution)/shard_map/ppermute | solution.py:55
  98.3 11.0 %collective-permute-start.29 = (bf16[64,2048]{1,0:T(8,128)(2,1)S(1)}, bf16[64,2048]{1,0:T(8,128)(2,1)S(1)}, u32[]{:S(2)}, u32[]{:S(2)}) collective-permute-start(bf16[64,2048]{1,0:T(8,128)(2,1)S(1)} %add_convert_fusion.6), channel_id=1, source_target_pairs={{0,1},{2,0},{4,2},{6,4},{7,6},{5,7},{3,5},{1,3},{8,9},{10,8},{12,1... | collective-permute-start | bytes 786440 | tf_op jit(solution)/shard_map/ppermute | solution.py:55
  103.7 9.1 %collective-permute-start.32 = (bf16[64,2048]{1,0:T(8,128)(2,1)S(1)}, bf16[64,2048]{1,0:T(8,128)(2,1)S(1)}, u32[]{:S(2)}, u32[]{:S(2)}) collective-permute-start(bf16[64,2048]{1,0:T(8,128)(2,1)S(1)} %add_convert_fusion.3), channel_id=1, source_target_pairs={{0,2},{2,4},{4,6},{6,7},{7,5},{5,3},{3,1},{1,0},{8,10},{10,12},{12... | collective-permute-start | bytes 786440 | tf_op jit(solution)/shard_map/ppermute | solution.py:55
  104.0 9.0 %collective-permute-start.33 = (bf16[64,2048]{1,0:T(8,128)(2,1)S(1)}, bf16[64,2048]{1,0:T(8,128)(2,1)S(1)}, u32[]{:S(2)}, u32[]{:S(2)}) collective-permute-start(bf16[64,2048]{1,0:T(8,128)(2,1)S(1)} %add_convert_fusion.2), channel_id=1, source_target_pairs={{0,1},{2,0},{4,2},{6,4},{7,6},{5,7},{3,5},{1,3},{8,9},{10,8},{12,1... | collective-permute-start | bytes 786440 | tf_op jit(solution)/shard_map/ppermute | solution.py:55

commit v11 on v10

--- a/solution.py
+++ b/solution.py
@@ -153,7 +153,7 @@
     return moved
 
 
-def accumulate(chunks, first, last, weights, before=None, lead=0, shared=False):
+def accumulate(chunks, first, last, weights, before=None, lead=0):
     rows, depth = chunks[0][0].shape
     width = weights[0].shape[1]
     parts, span = len(weights), last - first
@@ -165,30 +165,23 @@
     def body(*refs):
         piece_refs = refs[: len(pieces)]
         weight_refs = refs[len(pieces) : len(pieces) + parts]
-        out_ref, left = refs[-2 - 2 * shared], refs[-1]
+        out_ref, left = refs[-2:]
         for index, ref in enumerate(piece_refs):
             chunk, piece = divmod(index, span)
             left[chunk * rows : (chunk + 1) * rows, piece * depth : (piece + 1) * depth] = ref[...]
         for part in range(parts):
             term = mm(left[...], weight_refs[part][first * depth : last * depth])
             if before is not None:
-                term = term + refs[len(args) - 1][lead + part]
+                term = term + refs[-3][lead + part]
             out_ref[part] = term.astype(dtype)
-            if shared:
-                side = lax.axis_index("tok") % 2
-                refs[-3][part] = out_ref[part, :, lanes(1 - side, width // 2)]
-                refs[-2][part] = out_ref[part, :, lanes(side, width // 2)]
 
     aliased = before is not None and not final
     args = [*pieces, *weights] + ([] if before is None else [before])
     return call(
         body,
         [WHOLE] * len(args),
-        [WHOLE] * (1 + 2 * shared),
-        [
-            jax.ShapeDtypeStruct((parts, total, size), dtype)
-            for size in (width, width // 2, width // 2)[: 1 + 2 * shared]
-        ],
+        WHOLE,
+        jax.ShapeDtypeStruct((parts, total, width), dtype),
         [pltpu.VMEM((total, span * depth), BF16)],
         vmem=12,
         cost=cost(
@@ -196,6 +189,37 @@
             2 * span * depth * (total + width * parts) + 8 * total * width * parts,
         ),
         aliases={len(args) - 1: 0} if aliased else None,
+    )(*args)
+
+
+def finish(chunk, piece, weights, sums, filled):
+    rows, depth = piece.shape
+    width = weights[0].shape[1]
+    parts = len(weights)
+    where = slice(chunk * rows, (chunk + 1) * rows)
+
+    def body(piece_ref, *refs):
+        weight_refs, sum_ref = refs[:parts], refs[parts]
+        out_ref, far_ref, near_ref = refs[-3:]
+        side = lax.axis_index("tok") % 2
+        for part in range(parts):
+            term = mm(piece_ref[...], weight_refs[part][-depth:]) + sum_ref[part, where]
+            out_ref[part, where] = term.astype(BF16)
+            far_ref[part, where] = out_ref[part, where, lanes(1 - side, width // 2)]
+            near_ref[part, where] = out_ref[part, where, lanes(side, width // 2)]
+
+    total = sums.shape[1]
+    args = [piece, *weights, sums, *filled]
+    return call(
+        body,
+        [WHOLE] * len(args),
+        [WHOLE] * 3,
+        [
+            jax.ShapeDtypeStruct((parts, total, size), BF16)
+            for size in (width, width // 2, width // 2)
+        ],
+        cost=cost(2 * rows * depth * width * parts, 2 * width * parts * (depth + 4 * rows)),
+        aliases={len(args) - 3 + index: index for index in range(3)} if filled else None,
     )(*args)
 
 
@@ -552,10 +576,13 @@
             chunks[c] += held[c].values()
         if step > 1:
             known = [chunk[: 2 * step - 1] for chunk in chunks]
-            (sums,) = accumulate(known, done, 2 * step - 1, weights, sums)
+            sums = accumulate(known, done, 2 * step - 1, weights, sums)
             done = 2 * step - 1
-    kv, far, near = accumulate(chunks, done, 2 * steps, weights[:2], sums, shared=True)
-    (query,) = accumulate(chunks, done, 2 * steps, weights[2:], sums, 2)
+    filled = ()
+    for c in reversed(range(CHUNKS)):
+        filled = finish(c, chunks[c][-1], weights[:2], sums, filled)
+    kv, far, near = filled
+    query = accumulate(chunks, done, 2 * steps, weights[2:], sums, 2)
 
     behind = lax.ppermute(far, "tok", [(index, index + 1) for index in range(1, tok_count - 1, 2)])
     beside = swap(far, 1)
@@ -570,9 +597,9 @@
             travel = travel.astype(BF16)
         received.append(swap(travel, 1 << bit))
     attended, stats = attend_own(query, kv, head_size)
-    attended = attend_earlier(attended, stats, query, (behind, beside), head_size)
     near, _ = lax.optimization_barrier((near, attended))
     behind_far = lax.ppermute(near, "tok", [(index, index + 1) for index in range(tok_count - 1)])
+    attended = attend_earlier(attended, stats, query, (behind, beside), head_size)
     mine = renew(grads, received, head_step, *nets, (attended,))
     near = combine_near(query, attended, mine)
     return ring_reduce(query, attended, stats, behind_far, swap(mine, 1), near, w_out)

time: 114 us -> 113 us (level)
  starting transfers between devices: 34 us -> 31.2 us
  waiting for transfers between devices: 49 us -> 51.1 us
    ppermute x4, waiting for transfers between devices: 0.01 us -> 4.6 us  [swap(): lax.ppermute(value, 'tok', [(index, index ^ bit) for index in range(count)])]
    ppermute x1, starting transfers between devices: 4.82 us -> 1.92 us  [shards(): lax.ppermute(near, 'tok', [(index, index + 1) for index in range(tok_coun...]
    ppermute x1, waiting for transfers between devices: 3.14 us -> 1.21 us  [shards(): lax.ppermute(far, 'tok', [(index, index + 1) for index in range(1, tok_co...]
    pallas_call x5 -> x6, Pallas kernels: 7.64 us -> 7.76 us  [the longest x4 6.72 us: accumulate(): call(body, [WHOLE] * len(args), WHOLE, jax.ShapeDtypeStruct((parts, total...]
  transfers between devices with their start and end apart: 34 -> 34, of which waited for: 22 -> 23; matrix products, arithmetic and copies ran while one was open for 1% -> 1% of each run, Pallas kernels for 22% -> 23%
where the time goes in v11:
time: 113 us
  waiting for transfers between devices  51.1 us (45%)
  starting transfers between devices  31.2 us (28%)
  Pallas kernels  29 us (26%)
  other arithmetic  1.58 us (1%)
    ppermute x28, waiting for transfers between devices, ring_send(): lax.ppermute(value, 'head', [(order[i], order[(i + step) % count]) for i...  41.4 us
    ppermute x28, starting transfers between devices, ring_send(): lax.ppermute(value, 'head', [(order[i], order[(i + step) % count]) for i...  21.7 us
    pallas_call x4, Pallas kernels, partial_out(): call(body, [WHOLE] * 7 + [AFTER] * len(after), [WHOLE] * (2 * count), [ja...  7.53 us
    pallas_call x4, Pallas kernels, accumulate(): call(body, [WHOLE] * len(args), WHOLE, jax.ShapeDtypeStruct((parts, total...  6.72 us
    pallas_call x1, Pallas kernels, load(): call(body, [IN_HBM] * count, [WHOLE] * count, [jax.ShapeDtypeStruct(array...  4.78 us
    ppermute x4, waiting for transfers between devices, swap(): lax.ppermute(value, 'tok', [(index, index ^ bit) for index in range(count)])  4.6 us
    ppermute x4, starting transfers between devices, swap(): lax.ppermute(value, 'tok', [(index, index ^ bit) for index in range(count)])  4.43 us
    ppermute x1, waiting for transfers between devices, shards(): lax.ppermute(near, 'tok', [(index, index + 1) for index in range(tok_coun...  3.9 us
  transfers between devices with their start and end apart: 34, of which 23 were waited for; matrix products, arithmetic and copies ran while one was open for 1% of the time, Pallas kernels for 23%

profile of v11, /device:TPU:1, one launch (start us, length us, event | category | flops | bytes accessed | tf_op | source)
XLA Modules:
  0.0 113.2 jit_solution(13428614761373320424)
XLA Ops:
  0.0 1.0 shard_map.100
  1.1 2.1 %collective-permute-start.4 = (bf16[256,512]{1,0:T(8,128)(2,1)S(1)}, bf16[256,512]{1,0:T(8,128)(2,1)S(1)}, u32[]{:S(2)}, u32[]{:S(2)}) collective-permute-start(bf16[256,512]{1,0:T(8,128)(2,1)S(1)} %get-tuple-element.62.refs_3_), channel_id=1, source_target_pairs={{0,1},{2,0},{4,2},{6,4},{7,6},{5,7},{3,5},{1,3},{8,9},{10,8},{12,1... | collective-permute-start | bytes 786440 | tf_op jit(solution)/shard_map/ppermute | solution.py:55
  3.3 1.4 %collective-permute-start.3 = (bf16[256,512]{1,0:T(8,128)(2,1)S(1)}, bf16[256,512]{1,0:T(8,128)(2,1)S(1)}, u32[]{:S(2)}, u32[]{:S(2)}) collective-permute-start(bf16[256,512]{1,0:T(8,128)(2,1)S(1)} %get-tuple-element.62.refs_3_), channel_id=1, source_target_pairs={{0,2},{2,4},{4,6},{6,7},{7,5},{5,3},{3,1},{1,0},{8,10},{10,12},{12... | collective-permute-start | bytes 786440 | tf_op jit(solution)/shard_map/ppermute | solution.py:55
  4.8 4.8 %shard_map.101 = (bf16[4096,512]{1,0:T(8,128)(2,1)S(1)}, bf16[4096,512]{1,0:T(8,128)(2,1)S(1)}, bf16[4096,512]{1,0:T(8,128)(2,1)S(1)}) custom-call(bf16[4096,512]{1,0:T(8,128)(2,1)} %refs_0_.1, bf16[4096,512]{1,0:T(8,128)(2,1)} %refs_1_.1, bf16[4096,512]{1,0:T(8,128)(2,1)} %refs_2_.1), custom_call_target="tpu_custom_call" | custom-call | bytes 25165824 | tf_op jit(solution)/shard_map/pallas_call | solution.py:111
  9.6 1.4 %collective-permute-start.8 = (bf16[256,512]{1,0:T(8,128)(2,1)S(1)}, bf16[256,512]{1,0:T(8,128)(2,1)S(1)}, u32[]{:S(2)}, u32[]{:S(2)}) collective-permute-start(bf16[256,512]{1,0:T(8,128)(2,1)S(1)} %collective-permute-done.4.refs_5_), channel_id=1, source_target_pairs={{0,1},{2,0},{4,2},{6,4},{7,6},{5,7},{3,5},{1,3},{8,9},{10,8},{12,1... | collective-permute-start | bytes 786440 | tf_op jit(solution)/shard_map/ppermute | solution.py:55
  11.1 2.4 %collective-permute-start.5 = (f32[4,512]{1,0:T(4,128)S(1)}, f32[4,512]{1,0:T(4,128)S(1)}, u32[]{:S(2)}, u32[]{:S(2)}) collective-permute-start(f32[4,512]{1,0:T(4,128)S(1)} %bitcast.1), channel_id=1, source_target_pairs={{0,8},{8,0},{16,24},{24,16},{1,9},{9,1},{17,25},{25,17},{2,10},{10... | collective-permute-start | bytes 24584 | tf_op jit(solution)/shard_map/ppermute | solution.py:553
  13.5 2.2 %collective-permute-done.3.refs_4_ = bf16[256,512]{1,0:T(8,128)(2,1)S(1)} collective-permute-done((bf16[256,512]{1,0:T(8,128)(2,1)S(1)}, bf16[256,512]{1,0:T(8,128)(2,1)S(1)}, u32[]{:S(2)}, u32[]{:S(2)}) %collective-permute-start.3) | collective-permute-done | bytes 262176 | tf_op jit(solution)/shard_map/ppermute | solution.py:55
  15.6 0.5 collective-permute-start.13
  16.1 1.0 collective-permute-start.11
  17.1 2.6 %shard_map.102.refs_7_ = f32[3,512,512]{2,1,0:T(8,128)S(1)} custom-call(bf16[256,512]{1,0:T(8,128)(2,1)S(1)} %get-tuple-element.59.refs_0_, bf16[256,512]{1,0:T(8,128)(2,1)S(1)} %collective-permute-done.refs_1_, bf16[256,512]{1,0:T(8,128)(2,1)S(1)} %collective-permute-done.2.refs_2_, bf16[256,512]{1,0:T(8,128)(2,1)S(1)} %get-tuple-element.62.refs_3_, ...), custom_call_target="tpu_custom_call" | custom-call | flops 2415919104 | bytes 12582912 | tf_op jit(solution)/shard_map/pallas_call | solution.py:180
  19.7 0.8 collective-permute-done.8.refs_3_
  20.5 0.7 collective-permute-done.1.refs_0_
  21.2 1.3 %collective-permute-start.9 = (bf16[256,512]{1,0:T(8,128)(2,1)S(1)}, bf16[256,512]{1,0:T(8,128)(2,1)S(1)}, u32[]{:S(2)}, u32[]{:S(2)}) collective-permute-start(bf16[256,512]{1,0:T(8,128)(2,1)S(1)} %collective-permute-done.8.refs_3_), channel_id=1, source_target_pairs={{0,1},{2,0},{4,2},{6,4},{7,6},{5,7},{3,5},{1,3},{8,9},{10,8},{12,1... | collective-permute-start | bytes 786440 | tf_op jit(solution)/shard_map/ppermute | solution.py:55
  22.7 4.2 %collective-permute-done.13.refs_2_ = bf16[256,512]{1,0:T(8,128)(2,1)S(1)} collective-permute-done((bf16[256,512]{1,0:T(8,128)(2,1)S(1)}, bf16[256,512]{1,0:T(8,128)(2,1)S(1)}, u32[]{:S(2)}, u32[]{:S(2)}) %collective-permute-start.13) | collective-permute-done | bytes 262176 | tf_op jit(solution)/shard_map/ppermute | solution.py:55
  26.9 0.5 collective-permute-start.14
  27.3 1.0 collective-permute-start.12
  28.3 3.3 %collective-permute-done.9.refs_3_ = bf16[256,512]{1,0:T(8,128)(2,1)S(1)} collective-permute-done((bf16[256,512]{1,0:T(8,128)(2,1)S(1)}, bf16[256,512]{1,0:T(8,128)(2,1)S(1)}, u32[]{:S(2)}, u32[]{:S(2)}) %collective-permute-start.9) | collective-permute-done | bytes 262176 | tf_op jit(solution)/shard_map/ppermute | solution.py:55
  31.6 1.1 collective-permute-start.10
  32.7 0.3 collective-permute-start.7
  33.1 1.8 %shard_map.103.refs_7_ = f32[3,512,512]{2,1,0:T(8,128)S(1)} custom-call(bf16[256,512]{1,0:T(8,128)(2,1)S(1)} %collective-permute-done.1.refs_0_, bf16[256,512]{1,0:T(8,128)(2,1)S(1)} %collective-permute-done.11.refs_1_, bf16[256,512]{1,0:T(8,128)(2,1)S(1)} %collective-permute-done.13.refs_2_, ...), custom_call_target="tpu_custom_call", output_to_operand_aliasing={{}: (7, {})} | custom-call | flops 1610612736 | bytes 10485760 | tf_op jit(solution)/shard_map/pallas_call | solution.py:180
  34.9 3.2 %collective-permute-done.14.refs_2_ = bf16[256,512]{1,0:T(8,128)(2,1)S(1)} collective-permute-done((bf16[256,512]{1,0:T(8,128)(2,1)S(1)}, bf16[256,512]{1,0:T(8,128)(2,1)S(1)}, u32[]{:S(2)}, u32[]{:S(2)}) %collective-permute-start.14) | collective-permute-done | bytes 262176 | tf_op jit(solution)/shard_map/ppermute | solution.py:55
  38.1 1.8 %shard_map.104.refs_3_.refs_2_ = f32[3,512,512]{2,1,0:T(8,128)S(1)} custom-call(bf16[256,512]{1,0:T(8,128)(2,1)S(1)} %collective-permute-done.6.refs_0_, bf16[256,512]{1,0:T(8,128)(2,1)S(1)} %collective-permute-done.12.refs_1_, bf16[256,512]{1,0:T(8,128)(2,1)S(1)} %collective-permute-done.14.refs_2_, ...), custom_call_target="tpu_custom_call", output_to_operand_aliasing={{}: (7, {})} | custom-call | flops 1610612736 | bytes 10485760 | tf_op jit(solution)/shard_map/pallas_call | solution.py:180
  39.9 2.9 %collective-permute-done.10.refs_1_.piece_ref = bf16[256,512]{1,0:T(8,128)(2,1)S(1)} collective-permute-done((bf16[256,512]{1,0:T(8,128)(2,1)S(1)}, bf16[256,512]{1,0:T(8,128)(2,1)S(1)}, u32[]{:S(2)}, u32[]{:S(2)}) %collective-permute-start.10) | collective-permute-done | bytes 262176 | tf_op jit(solution)/shard_map/ppermute | solution.py:55
  42.8 0.5 shard_map.106
  43.3 0.4 collective-permute-done.7.refs_0_.piece_ref
  43.7 0.5 shard_map.107
  44.2 1.9 %collective-permute-start.16 = (bf16[2,512,256]{2,1,0:T(8,128)(2,1)S(1)}, bf16[2,512,256]{2,1,0:T(8,128)(2,1)S(1)}, u32[]{:S(2)}, u32[]{:S(2)}) collective-permute-start(bf16[2,512,256]{2,1,0:T(8,128)(2,1)S(1)} %get-tuple-element.78), channel_id=1, source_target_pairs={{0,8},{8,0},{16,24},{24,16},{1,9},{9,1},{17,25},{25,17},{2,10},{10... | collective-permute-start | bytes 1572872 | tf_op jit(solution)/shard_map/ppermute | solution.py:553
  46.2 3.1 %collective-permute-start.15 = (bf16[2,512,256]{2,1,0:T(8,128)(2,1)S(1)}, bf16[2,512,256]{2,1,0:T(8,128)(2,1)S(1)}, u32[]{:S(2)}, u32[]{:S(2)}) collective-permute-start(bf16[2,512,256]{2,1,0:T(8,128)(2,1)S(1)} %get-tuple-element.78), channel_id=1, source_target_pairs={{8,16},{9,17},{10,18},{11,19},{12,20},{13,21},{14,22},{15,23}} | collective-permute-start | bytes 1572872 | tf_op jit(solution)/shard_map/ppermute | solution.py:587
  49.3 1.4 %shard_map.110.rest_0_ = f32[2,3,128,256]{3,2,1,0:T(8,128)S(1)} custom-call(bf16[2,512,512]{2,1,0:T(8,128)(2,1)S(1)} %get-tuple-element.75.kv_ref, f32[4,512]{1,0:T(4,128)S(1)} %bitcast.2, f32[4,128,256]{2,1,0:T(8,128)S(1)} %copy-done.1, f32[4,128,256]{2,1,0:T(8,128)S(1)} %copy-done.2, f32[4,256,128]{2,1,0:T(8,128)S(1)} %copy-done.3), custom_call_target="tpu_custom_call" | custom-call | flops 402653184 | bytes 1572864 | tf_op jit(solution)/shard_map/pallas_call | solution.py:272
  50.7 1.4 %shard_map.111 = (f32[2,3,128,256]{3,2,1,0:T(8,128)S(1)}, bf16[2,3,128,256]{3,2,1,0:T(8,128)(2,1)S(1)}) custom-call(bf16[2,512,256]{2,1,0:T(8,128)(2,1)S(1)} %collective-permute-done.16.beside_ref.kv_ref, f32[4,512]{1,0:T(4,128)S(1)} %collective-permute-done.5.rate_ref, f32[4,128,256]{2,1,0:T(8,128)S(1)} %copy-done.1, f32[4,128,256]{2,1,0:T(8,128)S(1)} %copy-done.2, ...), custom_call_target="tpu_custom_call" | custom-call | flops 402653184 | bytes 1572864 | tf_op jit(solution)/shard_map/pallas_call | solution.py:272
  52.2 0.4 shard_map.105.q_ref
  52.7 2.1 %shard_map.108 = (f32[512,512]{1,0:T(8,128)S(1)}, f32[2,512,512]{2,1,0:T(8,128)S(1)}) custom-call(bf16[1,512,512]{2,1,0:T(8,128)(2,1)S(1)} %shard_map.105.q_ref, bf16[2,512,512]{2,1,0:T(8,128)(2,1)S(1)} %get-tuple-element.75.kv_ref), custom_call_target="tpu_custom_call" | custom-call | flops 402653184 | bytes 2097152 | tf_op jit(solution)/shard_map/pallas_call | solution.py:366
  54.8 1.9 %collective-permute-start.17 = (bf16[2,512,256]{2,1,0:T(8,128)(2,1)S(1)}, bf16[2,512,256]{2,1,0:T(8,128)(2,1)S(1)}, u32[]{:S(2)}, u32[]{:S(2)}) collective-permute-start(bf16[2,512,256]{2,1,0:T(8,128)(2,1)S(1)} %get-tuple-element.80), channel_id=1, source_target_pairs={{0,8},{8,16},{16,24},{1,9},{9,17},{17,25},{2,10},{10,18},{18,26},{... | collective-permute-start | bytes 1572872 | tf_op jit(solution)/shard_map/ppermute | solution.py:601
  56.7 1.2 %collective-permute-done.15.behind_ref = bf16[2,512,256]{2,1,0:T(8,128)(2,1)S(1)} collective-permute-done((bf16[2,512,256]{2,1,0:T(8,128)(2,1)S(1)}, bf16[2,512,256]{2,1,0:T(8,128)(2,1)S(1)}, u32[]{:S(2)}, u32[]{:S(2)}) %collective-permute-start.15) | collective-permute-done | bytes 524320 | tf_op jit(solution)/shard_map/ppermute | solution.py:587
  57.9 1.2 %shard_map.109.rest_1_.attended_ref = f32[512,512]{1,0:T(8,128)S(1)} custom-call(f32[512,512]{1,0:T(8,128)S(1)} %get-tuple-element.76.sum_ref, f32[2,512,512]{2,1,0:T(8,128)S(1)} %get-tuple-element.77.stats_ref, bf16[1,512,512]{2,1,0:T(8,128)(2,1)S(1)} %shard_map.105.q_ref, ...), custom_call_target="tpu_custom_call", output_to_operand_aliasing={{}: (0, {})} | custom-call | flops 201326592 | bytes 1048576 | tf_op jit(solution)/shard_map/pallas_call | solution.py:408
  59.2 4.6 %collective-permute-done.18.rest_0_ = bf16[2,3,128,256]{3,2,1,0:T(8,128)(2,1)S(1)} collective-permute-done((bf16[2,3,128,256]{3,2,1,0:T(8,128)(2,1)S(1)}, bf16[2,3,128,256]{3,2,1,0:T(8,128)(2,1)S(1)}, u32[]{:S(2)}, u32[]{:S(2)}) %collective-permute-start.18) | collective-permute-done | bytes 393248 | tf_op jit(solution)/shard_map/ppermute | solution.py:553
  63.8 0.8 shard_map.112.net_ref
  64.7 0.8 shard_map.113.near_ref
  65.5 3.9 %collective-permute-done.17.behind_ref = bf16[2,512,256]{2,1,0:T(8,128)(2,1)S(1)} collective-permute-done((bf16[2,512,256]{2,1,0:T(8,128)(2,1)S(1)}, bf16[2,512,256]{2,1,0:T(8,128)(2,1)S(1)}, u32[]{:S(2)}, u32[]{:S(2)}) %collective-permute-start.17) | collective-permute-done | bytes 524320 | tf_op jit(solution)/shard_map/ppermute | solution.py:601
  69.4 1.9 %shard_map.115 = (bf16[64,2048]{1,0:T(8,128)(2,1)S(1)}, bf16[64,2048]{1,0:T(8,128)(2,1)S(1)}) custom-call(bf16[1,512,512]{2,1,0:T(8,128)(2,1)S(1)} %shard_map.105.q_ref, f32[512,512]{1,0:T(8,128)S(1)} %shard_map.109.rest_1_.attended_ref, f32[2,512,512]{2,1,0:T(8,128)S(1)} %get-tuple-element.77.stats_ref, ...), custom_call_target="tpu_custom_call" | custom-call | flops 268435456 | bytes 4718592 | tf_op jit(solution)/shard_map/pallas_call | solution.py:493
  71.2 1.3 %collective-permute-start.21 = (bf16[64,2048]{1,0:T(8,128)(2,1)S(1)}, bf16[64,2048]{1,0:T(8,128)(2,1)S(1)}, u32[]{:S(2)}, u32[]{:S(2)}) collective-permute-start(bf16[64,2048]{1,0:T(8,128)(2,1)S(1)} %get-tuple-element.86), channel_id=1, source_target_pairs={{0,1},{2,0},{4,2},{6,4},{7,6},{5,7},{3,5},{1,3},{8,9},{10,8},{12,1... | collective-permute-start | bytes 786440 | tf_op jit(solution)/shard_map/ppermute | solution.py:55
  72.8 1.8 %shard_map.114 = (bf16[64,2048]{1,0:T(8,128)(2,1)S(1)}, bf16[64,2048]{1,0:T(8,128)(2,1)S(1)}, bf16[64,2048]{1,0:T(8,128)(2,1)S(1)}, bf16[64,2048]{1,0:T(8,128)(2,1)S(1)}) custom-call(bf16[1,512,512]{2,1,0:T(8,128)(2,1)S(1)} %shard_map.105.q_ref, f32[512,512]{1,0:T(8,128)S(1)} %shard_map.109.rest_1_.attended_ref, ...), custom_call_target="tpu_custom_call" | custom-call | flops 536870912 | bytes 5242880 | tf_op jit(solution)/shard_map/pallas_call | solution.py:493
  74.5 1.3 %collective-permute-start.25 = (bf16[64,2048]{1,0:T(8,128)(2,1)S(1)}, bf16[64,2048]{1,0:T(8,128)(2,1)S(1)}, u32[]{:S(2)}, u32[]{:S(2)}) collective-permute-start(bf16[64,2048]{1,0:T(8,128)(2,1)S(1)} %get-tuple-element.90), channel_id=1, source_target_pairs={{0,1},{2,0},{4,2},{6,4},{7,6},{5,7},{3,5},{1,3},{8,9},{10,8},{12,1... | collective-permute-start | bytes 786440 | tf_op jit(solution)/shard_map/ppermute | solution.py:55
  76.0 2.9 %collective-permute-done.21.refs_1_ = bf16[64,2048]{1,0:T(8,128)(2,1)S(1)} collective-permute-done((bf16[64,2048]{1,0:T(8,128)(2,1)S(1)}, bf16[64,2048]{1,0:T(8,128)(2,1)S(1)}, u32[]{:S(2)}, u32[]{:S(2)}) %collective-permute-start.21) | collective-permute-done | bytes 262176 | tf_op jit(solution)/shard_map/ppermute | solution.py:55
  79.0 1.5 %collective-permute-done.20.refs_0_ = bf16[64,2048]{1,0:T(8,128)(2,1)S(1)} collective-permute-done((bf16[64,2048]{1,0:T(8,128)(2,1)S(1)}, bf16[64,2048]{1,0:T(8,128)(2,1)S(1)}, u32[]{:S(2)}, u32[]{:S(2)}) %collective-permute-start.20) | collective-permute-done | bytes 262176 | tf_op jit(solution)/shard_map/ppermute | solution.py:55
  80.6 1.3 %collective-permute-start.23 = (bf16[64,2048]{1,0:T(8,128)(2,1)S(1)}, bf16[64,2048]{1,0:T(8,128)(2,1)S(1)}, u32[]{:S(2)}, u32[]{:S(2)}) collective-permute-start(bf16[64,2048]{1,0:T(8,128)(2,1)S(1)} %add_convert_fusion.10), channel_id=1, source_target_pairs={{0,1},{2,0},{4,2},{6,4},{7,6},{5,7},{3,5},{1,3},{8,9},{10,8},{12,1... | collective-permute-start | bytes 786440 | tf_op jit(solution)/shard_map/ppermute | solution.py:55
  82.1 1.8 %shard_map.117 = (bf16[64,2048]{1,0:T(8,128)(2,1)S(1)}, bf16[64,2048]{1,0:T(8,128)(2,1)S(1)}, bf16[64,2048]{1,0:T(8,128)(2,1)S(1)}, bf16[64,2048]{1,0:T(8,128)(2,1)S(1)}) custom-call(bf16[1,512,512]{2,1,0:T(8,128)(2,1)S(1)} %shard_map.105.q_ref, f32[512,512]{1,0:T(8,128)S(1)} %shard_map.109.rest_1_.attended_ref, ...), custom_call_target="tpu_custom_call" | custom-call | flops 536870912 | bytes 5242880 | tf_op jit(solution)/shard_map/pallas_call | solution.py:493
  83.9 0.7 collective-permute-done.25
  84.6 1.5 %collective-permute-done.24 = bf16[64,2048]{1,0:T(8,128)(2,1)S(1)} collective-permute-done((bf16[64,2048]{1,0:T(8,128)(2,1)S(1)}, bf16[64,2048]{1,0:T(8,128)(2,1)S(1)}, u32[]{:S(2)}, u32[]{:S(2)}) %collective-permute-start.24) | collective-permute-done | bytes 262176 | tf_op jit(solution)/shard_map/ppermute | solution.py:55
  86.2 1.3 %collective-permute-start.27 = (bf16[64,2048]{1,0:T(8,128)(2,1)S(1)}, bf16[64,2048]{1,0:T(8,128)(2,1)S(1)}, u32[]{:S(2)}, u32[]{:S(2)}) collective-permute-start(bf16[64,2048]{1,0:T(8,128)(2,1)S(1)} %add_convert_fusion.8), channel_id=1, source_target_pairs={{0,1},{2,0},{4,2},{6,4},{7,6},{5,7},{3,5},{1,3},{8,9},{10,8},{12,1... | collective-permute-start | bytes 786440 | tf_op jit(solution)/shard_map/ppermute | solution.py:55
  87.7 2.5 %collective-permute-done.23.refs_1_ = bf16[64,2048]{1,0:T(8,128)(2,1)S(1)} collective-permute-done((bf16[64,2048]{1,0:T(8,128)(2,1)S(1)}, bf16[64,2048]{1,0:T(8,128)(2,1)S(1)}, u32[]{:S(2)}, u32[]{:S(2)}) %collective-permute-start.23) | collective-permute-done | bytes 262176 | tf_op jit(solution)/shard_map/ppermute | solution.py:55
  90.3 1.5 %collective-permute-done.22.refs_0_ = bf16[64,2048]{1,0:T(8,128)(2,1)S(1)} collective-permute-done((bf16[64,2048]{1,0:T(8,128)(2,1)S(1)}, bf16[64,2048]{1,0:T(8,128)(2,1)S(1)}, u32[]{:S(2)}, u32[]{:S(2)}) %collective-permute-start.22) | collective-permute-done | bytes 262176 | tf_op jit(solution)/shard_map/ppermute | solution.py:55
  91.8 1.3 %collective-permute-start.31 = (bf16[64,2048]{1,0:T(8,128)(2,1)S(1)}, bf16[64,2048]{1,0:T(8,128)(2,1)S(1)}, u32[]{:S(2)}, u32[]{:S(2)}) collective-permute-start(bf16[64,2048]{1,0:T(8,128)(2,1)S(1)} %add_convert_fusion.4), channel_id=1, source_target_pairs={{0,1},{2,0},{4,2},{6,4},{7,6},{5,7},{3,5},{1,3},{8,9},{10,8},{12,1... | collective-permute-start | bytes 786440 | tf_op jit(solution)/shard_map/ppermute | solution.py:55
  93.3 2.1 %shard_map.116 = (bf16[64,2048]{1,0:T(8,128)(2,1)S(1)}, bf16[64,2048]{1,0:T(8,128)(2,1)S(1)}, bf16[64,2048]{1,0:T(8,128)(2,1)S(1)}, bf16[64,2048]{1,0:T(8,128)(2...) custom-call(bf16[1,512,512]{2,1,0:T(8,128)(2,1)S(1)} %shard_map.105.q_ref, ...), custom_call_target="tpu_custom_call" | custom-call | flops 805306368 | bytes 5767168 | tf_op jit(solution)/shard_map/pallas_call | solution.py:493
  95.5 0.3 collective-permute-done.27
  95.9 1.5 %collective-permute-done.26 = bf16[64,2048]{1,0:T(8,128)(2,1)S(1)} collective-permute-done((bf16[64,2048]{1,0:T(8,128)(2,1)S(1)}, bf16[64,2048]{1,0:T(8,128)(2,1)S(1)}, u32[]{:S(2)}, u32[]{:S(2)}) %collective-permute-start.26) | collective-permute-done | bytes 262176 | tf_op jit(solution)/shard_map/ppermute | solution.py:55
  97.7 1.3 %collective-permute-start.29 = (bf16[64,2048]{1,0:T(8,128)(2,1)S(1)}, bf16[64,2048]{1,0:T(8,128)(2,1)S(1)}, u32[]{:S(2)}, u32[]{:S(2)}) collective-permute-start(bf16[64,2048]{1,0:T(8,128)(2,1)S(1)} %add_convert_fusion.6), channel_id=1, source_target_pairs={{0,1},{2,0},{4,2},{6,4},{7,6},{5,7},{3,5},{1,3},{8,9},{10,8},{12,1... | collective-permute-start | bytes 786440 | tf_op jit(solution)/shard_map/ppermute | solution.py:55
  99.0 2.3 %collective-permute-done.31 = bf16[64,2048]{1,0:T(8,128)(2,1)S(1)} collective-permute-done((bf16[64,2048]{1,0:T(8,128)(2,1)S(1)}, bf16[64,2048]{1,0:T(8,128)(2,1)S(1)}, u32[]{:S(2)}, u32[]{:S(2)}) %collective-permute-start.31) | collective-permute-done | bytes 262176 | tf_op jit(solution)/shard_map/ppermute | solution.py:55
  101.3 1.7 %collective-permute-done.30 = bf16[64,2048]{1,0:T(8,128)(2,1)S(1)} collective-permute-done((bf16[64,2048]{1,0:T(8,128)(2,1)S(1)}, bf16[64,2048]{1,0:T(8,128)(2,1)S(1)}, u32[]{:S(2)}, u32[]{:S(2)}) %collective-permute-start.30) | collective-permute-done | bytes 262176 | tf_op jit(solution)/shard_map/ppermute | solution.py:55
  103.1 0.2 collective-permute-start.32
  103.3 1.3 %collective-permute-start.33 = (bf16[64,2048]{1,0:T(8,128)(2,1)S(1)}, bf16[64,2048]{1,0:T(8,128)(2,1)S(1)}, u32[]{:S(2)}, u32[]{:S(2)}) collective-permute-start(bf16[64,2048]{1,0:T(8,128)(2,1)S(1)} %add_convert_fusion.2), channel_id=1, source_target_pairs={{0,1},{2,0},{4,2},{6,4},{7,6},{5,7},{3,5},{1,3},{8,9},{10,8},{12,1... | collective-permute-start | bytes 786440 | tf_op jit(solution)/shard_map/ppermute | solution.py:55
  104.6 4.0 %collective-permute-done.28.refs_2_ = bf16[64,2048]{1,0:T(8,128)(2,1)S(1)} collective-permute-done((bf16[64,2048]{1,0:T(8,128)(2,1)S(1)}, bf16[64,2048]{1,0:T(8,128)(2,1)S(1)}, u32[]{:S(2)}, u32[]{:S(2)}) %collective-permute-start.28) | collective-permute-done | bytes 262176 | tf_op jit(solution)/shard_map/ppermute | solution.py:55
  108.7 3.5 %collective-permute-done.32 = bf16[64,2048]{1,0:T(8,128)(2,1)S(1)} collective-permute-done((bf16[64,2048]{1,0:T(8,128)(2,1)S(1)}, bf16[64,2048]{1,0:T(8,128)(2,1)S(1)}, u32[]{:S(2)}, u32[]{:S(2)}) %collective-permute-start.32) | collective-permute-done | bytes 262176 | tf_op jit(solution)/shard_map/ppermute | solution.py:55
  112.3 0.8 pad_maximum_fusion
  (48 shorter events, 2.7 us)
Async XLA Ops:
  1.1 8.5 %collective-permute-start.4 = (bf16[256,512]{1,0:T(8,128)(2,1)S(1)}, bf16[256,512]{1,0:T(8,128)(2,1)S(1)}, u32[]{:S(2)}, u32[]{:S(2)}) collective-permute-start(bf16[256,512]{1,0:T(8,128)(2,1)S(1)} %get-tuple-element.62.refs_3_), channel_id=1, source_target_pairs={{0,1},{2,0},{4,2},{6,4},{7,6},{5,7},{3,5},{1,3},{8,9},{10,8},{12,1... | collective-permute-start | bytes 786440 | tf_op jit(solution)/shard_map/ppermute | solution.py:55
  3.1 8.0 %copy-start.4 = (f32[512,4]{0,1:T(4,128)S(1)}, f32[512,4]{0,1:T(4,128)}, u32[]{:S(2)}) copy-start(f32[512,4]{0,1:T(4,128)} %param.18) | copy-start | bytes 24580
  3.1 7.8 %collective-permute-start = (bf16[256,512]{1,0:T(8,128)(2,1)S(1)}, bf16[256,512]{1,0:T(8,128)(2,1)S(1)}, u32[]{:S(2)}, u32[]{:S(2)}) collective-permute-start(bf16[256,512]{1,0:T(8,128)(2,1)S(1)} %get-tuple-element.59.refs_0_), channel_id=1, source_target_pairs={{0,2},{2,4},{4,6},{6,7},{7,5},{5,3},{3,1},{1,0},{8,10},{10,12},{12... | collective-permute-start | bytes 786440 | tf_op jit(solution)/shard_map/ppermute | solution.py:55
  3.3 12.3 %collective-permute-start.3 = (bf16[256,512]{1,0:T(8,128)(2,1)S(1)}, bf16[256,512]{1,0:T(8,128)(2,1)S(1)}, u32[]{:S(2)}, u32[]{:S(2)}) collective-permute-start(bf16[256,512]{1,0:T(8,128)(2,1)S(1)} %get-tuple-element.62.refs_3_), channel_id=1, source_target_pairs={{0,2},{2,4},{4,6},{6,7},{7,5},{5,3},{3,1},{1,0},{8,10},{10,12},{12... | collective-permute-start | bytes 786440 | tf_op jit(solution)/shard_map/ppermute | solution.py:55
  4.7 11.4 %collective-permute-start.2 = (bf16[256,512]{1,0:T(8,128)(2,1)S(1)}, bf16[256,512]{1,0:T(8,128)(2,1)S(1)}, u32[]{:S(2)}, u32[]{:S(2)}) collective-permute-start(bf16[256,512]{1,0:T(8,128)(2,1)S(1)} %get-tuple-element.59.refs_0_), channel_id=1, source_target_pairs={{0,1},{2,0},{4,2},{6,4},{7,6},{5,7},{3,5},{1,3},{8,9},{10,8},{12,1... | collective-permute-start | bytes 786440 | tf_op jit(solution)/shard_map/ppermute | solution.py:55
  9.6 10.9 %collective-permute-start.8 = (bf16[256,512]{1,0:T(8,128)(2,1)S(1)}, bf16[256,512]{1,0:T(8,128)(2,1)S(1)}, u32[]{:S(2)}, u32[]{:S(2)}) collective-permute-start(bf16[256,512]{1,0:T(8,128)(2,1)S(1)} %collective-permute-done.4.refs_5_), channel_id=1, source_target_pairs={{0,1},{2,0},{4,2},{6,4},{7,6},{5,7},{3,5},{1,3},{8,9},{10,8},{12,1... | collective-permute-start | bytes 786440 | tf_op jit(solution)/shard_map/ppermute | solution.py:55
  10.9 10.3 %collective-permute-start.1 = (bf16[256,512]{1,0:T(8,128)(2,1)S(1)}, bf16[256,512]{1,0:T(8,128)(2,1)S(1)}, u32[]{:S(2)}, u32[]{:S(2)}) collective-permute-start(bf16[256,512]{1,0:T(8,128)(2,1)S(1)} %collective-permute-done.refs_1_), channel_id=1, source_target_pairs={{0,2},{2,4},{4,6},{6,7},{7,5},{5,3},{3,1},{1,0},{8,10},{10,12},{12... | collective-permute-start | bytes 786440 | tf_op jit(solution)/shard_map/ppermute | solution.py:55
  11.1 8.6 %collective-permute-start.5 = (f32[4,512]{1,0:T(4,128)S(1)}, f32[4,512]{1,0:T(4,128)S(1)}, u32[]{:S(2)}, u32[]{:S(2)}) collective-permute-start(f32[4,512]{1,0:T(4,128)S(1)} %bitcast.1), channel_id=1, source_target_pairs={{0,8},{8,0},{16,24},{24,16},{1,9},{9,1},{17,25},{25,17},{2,10},{10... | collective-permute-start | bytes 24584 | tf_op jit(solution)/shard_map/ppermute | solution.py:553
  15.6 11.2 %collective-permute-start.13 = (bf16[256,512]{1,0:T(8,128)(2,1)S(1)}, bf16[256,512]{1,0:T(8,128)(2,1)S(1)}, u32[]{:S(2)}, u32[]{:S(2)}) collective-permute-start(bf16[256,512]{1,0:T(8,128)(2,1)S(1)} %collective-permute-done.3.refs_4_), channel_id=1, source_target_pairs={{0,2},{2,4},{4,6},{6,7},{7,5},{5,3},{3,1},{1,0},{8,10},{10,12},{12... | collective-permute-start | bytes 786440 | tf_op jit(solution)/shard_map/ppermute | solution.py:55
  16.1 10.8 %collective-permute-start.11 = (bf16[256,512]{1,0:T(8,128)(2,1)S(1)}, bf16[256,512]{1,0:T(8,128)(2,1)S(1)}, u32[]{:S(2)}, u32[]{:S(2)}) collective-permute-start(bf16[256,512]{1,0:T(8,128)(2,1)S(1)} %collective-permute-done.2.refs_2_), channel_id=1, source_target_pairs={{0,1},{2,0},{4,2},{6,4},{7,6},{5,7},{3,5},{1,3},{8,9},{10,8},{12,1... | collective-permute-start | bytes 786440 | tf_op jit(solution)/shard_map/ppermute | solution.py:55
  21.2 10.3 %collective-permute-start.9 = (bf16[256,512]{1,0:T(8,128)(2,1)S(1)}, bf16[256,512]{1,0:T(8,128)(2,1)S(1)}, u32[]{:S(2)}, u32[]{:S(2)}) collective-permute-start(bf16[256,512]{1,0:T(8,128)(2,1)S(1)} %collective-permute-done.8.refs_3_), channel_id=1, source_target_pairs={{0,1},{2,0},{4,2},{6,4},{7,6},{5,7},{3,5},{1,3},{8,9},{10,8},{12,1... | collective-permute-start | bytes 786440 | tf_op jit(solution)/shard_map/ppermute | solution.py:55
  22.5 10.2 %collective-permute-start.6 = (bf16[256,512]{1,0:T(8,128)(2,1)S(1)}, bf16[256,512]{1,0:T(8,128)(2,1)S(1)}, u32[]{:S(2)}, u32[]{:S(2)}) collective-permute-start(bf16[256,512]{1,0:T(8,128)(2,1)S(1)} %collective-permute-done.1.refs_0_), channel_id=1, source_target_pairs={{0,2},{2,4},{4,6},{6,7},{7,5},{5,3},{3,1},{1,0},{8,10},{10,12},{12... | collective-permute-start | bytes 786440 | tf_op jit(solution)/shard_map/ppermute | solution.py:55
  26.9 11.2 %collective-permute-start.14 = (bf16[256,512]{1,0:T(8,128)(2,1)S(1)}, bf16[256,512]{1,0:T(8,128)(2,1)S(1)}, u32[]{:S(2)}, u32[]{:S(2)}) collective-permute-start(bf16[256,512]{1,0:T(8,128)(2,1)S(1)} %collective-permute-done.13.refs_2_), channel_id=1, source_target_pairs={{0,2},{2,4},{4,6},{6,7},{7,5},{5,3},{3,1},{1,0},{8,10},{10,12},{12... | collective-permute-start | bytes 786440 | tf_op jit(solution)/shard_map/ppermute | solution.py:55
  27.3 10.8 %collective-permute-start.12 = (bf16[256,512]{1,0:T(8,128)(2,1)S(1)}, bf16[256,512]{1,0:T(8,128)(2,1)S(1)}, u32[]{:S(2)}, u32[]{:S(2)}) collective-permute-start(bf16[256,512]{1,0:T(8,128)(2,1)S(1)} %collective-permute-done.11.refs_1_), channel_id=1, source_target_pairs={{0,1},{2,0},{4,2},{6,4},{7,6},{5,7},{3,5},{1,3},{8,9},{10,8},{12,1... | collective-permute-start | bytes 786440 | tf_op jit(solution)/shard_map/ppermute | solution.py:55
  31.6 11.2 %collective-permute-start.10 = (bf16[256,512]{1,0:T(8,128)(2,1)S(1)}, bf16[256,512]{1,0:T(8,128)(2,1)S(1)}, u32[]{:S(2)}, u32[]{:S(2)}) collective-permute-start(bf16[256,512]{1,0:T(8,128)(2,1)S(1)} %collective-permute-done.9.refs_3_), channel_id=1, source_target_pairs={{0,1},{2,0},{4,2},{6,4},{7,6},{5,7},{3,5},{1,3},{8,9},{10,8},{12,1... | collective-permute-start | bytes 786440 | tf_op jit(solution)/shard_map/ppermute | solution.py:55
  32.7 11.0 %collective-permute-start.7 = (bf16[256,512]{1,0:T(8,128)(2,1)S(1)}, bf16[256,512]{1,0:T(8,128)(2,1)S(1)}, u32[]{:S(2)}, u32[]{:S(2)}) collective-permute-start(bf16[256,512]{1,0:T(8,128)(2,1)S(1)} %collective-permute-done.6.refs_0_), channel_id=1, source_target_pairs={{0,2},{2,4},{4,6},{6,7},{7,5},{5,3},{3,1},{1,0},{8,10},{10,12},{12... | collective-permute-start | bytes 786440 | tf_op jit(solution)/shard_map/ppermute | solution.py:55
  43.7 5.5 %copy-start.1 = (f32[4,128,256]{2,1,0:T(8,128)S(1)}, f32[4,128,256]{2,1,0:T(8,128)}, u32[]{:S(2)}) copy-start(f32[4,128,256]{2,1,0:T(8,128)} %gate_ref.5) | copy-start | bytes 1572868
  43.7 5.6 %copy-start.2 = (f32[4,128,256]{2,1,0:T(8,128)S(1)}, f32[4,128,256]{2,1,0:T(8,128)}, u32[]{:S(2)}) copy-start(f32[4,128,256]{2,1,0:T(8,128)} %up_ref.5) | copy-start | bytes 1572868
  43.7 5.6 %copy-start.3 = (f32[4,256,128]{2,1,0:T(8,128)S(1)}, f32[4,256,128]{2,1,0:T(8,128)}, u32[]{:S(2)}) copy-start(f32[4,256,128]{2,1,0:T(8,128)} %down_ref.5) | copy-start | bytes 1572868
  44.2 6.5 %collective-permute-start.16 = (bf16[2,512,256]{2,1,0:T(8,128)(2,1)S(1)}, bf16[2,512,256]{2,1,0:T(8,128)(2,1)S(1)}, u32[]{:S(2)}, u32[]{:S(2)}) collective-permute-start(bf16[2,512,256]{2,1,0:T(8,128)(2,1)S(1)} %get-tuple-element.78), channel_id=1, source_target_pairs={{0,8},{8,0},{16,24},{24,16},{1,9},{9,1},{17,25},{25,17},{2,10},{10... | collective-permute-start | bytes 1572872 | tf_op jit(solution)/shard_map/ppermute | solution.py:553
  46.2 11.8 %collective-permute-start.15 = (bf16[2,512,256]{2,1,0:T(8,128)(2,1)S(1)}, bf16[2,512,256]{2,1,0:T(8,128)(2,1)S(1)}, u32[]{:S(2)}, u32[]{:S(2)}) collective-permute-start(bf16[2,512,256]{2,1,0:T(8,128)(2,1)S(1)} %get-tuple-element.78), channel_id=1, source_target_pairs={{8,16},{9,17},{10,18},{11,19},{12,20},{13,21},{14,22},{15,23}} | collective-permute-start | bytes 1572872 | tf_op jit(solution)/shard_map/ppermute | solution.py:587
  52.2 11.6 %collective-permute-start.18 = (bf16[2,3,128,256]{3,2,1,0:T(8,128)(2,1)S(1)}, bf16[2,3,128,256]{3,2,1,0:T(8,128)(2,1)S(1)}, u32[]{:S(2)}, u32[]{:S(2)}) collective-permute-start(bf16[2,3,128,256]{3,2,1,0:T(8,128)(2,1)S(1)} %get-tuple-element.82), channel_id=1, source_target_pairs={{0,16},{8,24},{16,0},{24,8},{1,17},{9,25},{17,1},{25,9},{2,18},{10... | collective-permute-start | bytes 1179656 | tf_op jit(solution)/shard_map/ppermute | solution.py:553
  52.7 11.1 %copy-start.5 = (f32[4]{0:T(128)S(1)}, f32[4]{0:T(128)}, u32[]{:S(2)}) copy-start(f32[4]{0:T(128)} %step_ref.1) | copy-start | bytes 52
  54.8 14.6 %collective-permute-start.17 = (bf16[2,512,256]{2,1,0:T(8,128)(2,1)S(1)}, bf16[2,512,256]{2,1,0:T(8,128)(2,1)S(1)}, u32[]{:S(2)}, u32[]{:S(2)}) collective-permute-start(bf16[2,512,256]{2,1,0:T(8,128)(2,1)S(1)} %get-tuple-element.80), channel_id=1, source_target_pairs={{0,8},{8,16},{16,24},{1,9},{9,17},{17,25},{2,10},{10,18},{18,26},{... | collective-permute-start | bytes 1572872 | tf_op jit(solution)/shard_map/ppermute | solution.py:601
  59.2 10.2 %copy-start = (bf16[512,4096]{1,0:T(8,128)(2,1)S(1)}, bf16[512,4096]{1,0:T(8,128)(2,1)}, u32[]{:S(2)}) copy-start(bf16[512,4096]{1,0:T(8,128)(2,1)} %w_ref.7) | copy-start | bytes 12582916
  64.6 4.8 %collective-permute-start.19 = (bf16[2,3,128,256]{3,2,1,0:T(8,128)(2,1)S(1)}, bf16[2,3,128,256]{3,2,1,0:T(8,128)(2,1)S(1)}, u32[]{:S(2)}, u32[]{:S(2)}) collective-permute-start(bf16[2,3,128,256]{3,2,1,0:T(8,128)(2,1)S(1)} %shard_map.112.net_ref), channel_id=1, source_target_pairs={{0,8},{8,0},{16,24},{24,16},{1,9},{9,1},{17,25},{25,17},{2,10},{10... | collective-permute-start | bytes 1179656 | tf_op jit(solution)/shard_map/ppermute | solution.py:553
  71.2 7.7 %collective-permute-start.21 = (bf16[64,2048]{1,0:T(8,128)(2,1)S(1)}, bf16[64,2048]{1,0:T(8,128)(2,1)S(1)}, u32[]{:S(2)}, u32[]{:S(2)}) collective-permute-start(bf16[64,2048]{1,0:T(8,128)(2,1)S(1)} %get-tuple-element.86), channel_id=1, source_target_pairs={{0,1},{2,0},{4,2},{6,4},{7,6},{5,7},{3,5},{1,3},{8,9},{10,8},{12,1... | collective-permute-start | bytes 786440 | tf_op jit(solution)/shard_map/ppermute | solution.py:55
  72.6 7.9 %collective-permute-start.20 = (bf16[64,2048]{1,0:T(8,128)(2,1)S(1)}, bf16[64,2048]{1,0:T(8,128)(2,1)S(1)}, u32[]{:S(2)}, u32[]{:S(2)}) collective-permute-start(bf16[64,2048]{1,0:T(8,128)(2,1)S(1)} %get-tuple-element.84), channel_id=1, source_target_pairs={{0,2},{2,4},{4,6},{6,7},{7,5},{5,3},{3,1},{1,0},{8,10},{10,12},{12... | collective-permute-start | bytes 786440 | tf_op jit(solution)/shard_map/ppermute | solution.py:55
  74.5 10.0 %collective-permute-start.25 = (bf16[64,2048]{1,0:T(8,128)(2,1)S(1)}, bf16[64,2048]{1,0:T(8,128)(2,1)S(1)}, u32[]{:S(2)}, u32[]{:S(2)}) collective-permute-start(bf16[64,2048]{1,0:T(8,128)(2,1)S(1)} %get-tuple-element.90), channel_id=1, source_target_pairs={{0,1},{2,0},{4,2},{6,4},{7,6},{5,7},{3,5},{1,3},{8,9},{10,8},{12,1... | collective-permute-start | bytes 786440 | tf_op jit(solution)/shard_map/ppermute | solution.py:55
  75.9 10.3 %collective-permute-start.24 = (bf16[64,2048]{1,0:T(8,128)(2,1)S(1)}, bf16[64,2048]{1,0:T(8,128)(2,1)S(1)}, u32[]{:S(2)}, u32[]{:S(2)}) collective-permute-start(bf16[64,2048]{1,0:T(8,128)(2,1)S(1)} %get-tuple-element.89), channel_id=1, source_target_pairs={{0,2},{2,4},{4,6},{6,7},{7,5},{5,3},{3,1},{1,0},{8,10},{10,12},{12... | collective-permute-start | bytes 786440 | tf_op jit(solution)/shard_map/ppermute | solution.py:55
  80.6 9.6 %collective-permute-start.23 = (bf16[64,2048]{1,0:T(8,128)(2,1)S(1)}, bf16[64,2048]{1,0:T(8,128)(2,1)S(1)}, u32[]{:S(2)}, u32[]{:S(2)}) collective-permute-start(bf16[64,2048]{1,0:T(8,128)(2,1)S(1)} %add_convert_fusion.10), channel_id=1, source_target_pairs={{0,1},{2,0},{4,2},{6,4},{7,6},{5,7},{3,5},{1,3},{8,9},{10,8},{12,1... | collective-permute-start | bytes 786440 | tf_op jit(solution)/shard_map/ppermute | solution.py:55
  81.9 9.8 %collective-permute-start.22 = (bf16[64,2048]{1,0:T(8,128)(2,1)S(1)}, bf16[64,2048]{1,0:T(8,128)(2,1)S(1)}, u32[]{:S(2)}, u32[]{:S(2)}) collective-permute-start(bf16[64,2048]{1,0:T(8,128)(2,1)S(1)} %add_convert_fusion.11), channel_id=1, source_target_pairs={{0,2},{2,4},{4,6},{6,7},{7,5},{5,3},{3,1},{1,0},{8,10},{10,12},{12... | collective-permute-start | bytes 786440 | tf_op jit(solution)/shard_map/ppermute | solution.py:55
  86.2 9.6 %collective-permute-start.27 = (bf16[64,2048]{1,0:T(8,128)(2,1)S(1)}, bf16[64,2048]{1,0:T(8,128)(2,1)S(1)}, u32[]{:S(2)}, u32[]{:S(2)}) collective-permute-start(bf16[64,2048]{1,0:T(8,128)(2,1)S(1)} %add_convert_fusion.8), channel_id=1, source_target_pairs={{0,1},{2,0},{4,2},{6,4},{7,6},{5,7},{3,5},{1,3},{8,9},{10,8},{12,1... | collective-permute-start | bytes 786440 | tf_op jit(solution)/shard_map/ppermute | solution.py:55
  87.5 9.8 %collective-permute-start.26 = (bf16[64,2048]{1,0:T(8,128)(2,1)S(1)}, bf16[64,2048]{1,0:T(8,128)(2,1)S(1)}, u32[]{:S(2)}, u32[]{:S(2)}) collective-permute-start(bf16[64,2048]{1,0:T(8,128)(2,1)S(1)} %add_convert_fusion.9), channel_id=1, source_target_pairs={{0,2},{2,4},{4,6},{6,7},{7,5},{5,3},{3,1},{1,0},{8,10},{10,12},{12... | collective-permute-start | bytes 786440 | tf_op jit(solution)/shard_map/ppermute | solution.py:55
  91.8 9.4 %collective-permute-start.31 = (bf16[64,2048]{1,0:T(8,128)(2,1)S(1)}, bf16[64,2048]{1,0:T(8,128)(2,1)S(1)}, u32[]{:S(2)}, u32[]{:S(2)}) collective-permute-start(bf16[64,2048]{1,0:T(8,128)(2,1)S(1)} %add_convert_fusion.4), channel_id=1, source_target_pairs={{0,1},{2,0},{4,2},{6,4},{7,6},{5,7},{3,5},{1,3},{8,9},{10,8},{12,1... | collective-permute-start | bytes 786440 | tf_op jit(solution)/shard_map/ppermute | solution.py:55
  93.2 9.8 %collective-permute-start.30 = (bf16[64,2048]{1,0:T(8,128)(2,1)S(1)}, bf16[64,2048]{1,0:T(8,128)(2,1)S(1)}, u32[]{:S(2)}, u32[]{:S(2)}) collective-permute-start(bf16[64,2048]{1,0:T(8,128)(2,1)S(1)} %add_convert_fusion.5), channel_id=1, source_target_pairs={{0,2},{2,4},{4,6},{6,7},{7,5},{5,3},{3,1},{1,0},{8,10},{10,12},{12... | collective-permute-start | bytes 786440 | tf_op jit(solution)/shard_map/ppermute | solution.py:55
  97.4 11.2 %collective-permute-start.28 = (bf16[64,2048]{1,0:T(8,128)(2,1)S(1)}, bf16[64,2048]{1,0:T(8,128)(2,1)S(1)}, u32[]{:S(2)}, u32[]{:S(2)}) collective-permute-start(bf16[64,2048]{1,0:T(8,128)(2,1)S(1)} %add_convert_fusion.7), channel_id=1, source_target_pairs={{0,2},{2,4},{4,6},{6,7},{7,5},{5,3},{3,1},{1,0},{8,10},{10,12},{12... | collective-permute-start | bytes 786440 | tf_op jit(solution)/shard_map/ppermute | solution.py:55
  97.7 10.9 %collective-permute-start.29 = (bf16[64,2048]{1,0:T(8,128)(2,1)S(1)}, bf16[64,2048]{1,0:T(8,128)(2,1)S(1)}, u32[]{:S(2)}, u32[]{:S(2)}) collective-permute-start(bf16[64,2048]{1,0:T(8,128)(2,1)S(1)} %add_convert_fusion.6), channel_id=1, source_target_pairs={{0,1},{2,0},{4,2},{6,4},{7,6},{5,7},{3,5},{1,3},{8,9},{10,8},{12,1... | collective-permute-start | bytes 786440 | tf_op jit(solution)/shard_map/ppermute | solution.py:55
  103.1 9.2 %collective-permute-start.32 = (bf16[64,2048]{1,0:T(8,128)(2,1)S(1)}, bf16[64,2048]{1,0:T(8,128)(2,1)S(1)}, u32[]{:S(2)}, u32[]{:S(2)}) collective-permute-start(bf16[64,2048]{1,0:T(8,128)(2,1)S(1)} %add_convert_fusion.3), channel_id=1, source_target_pairs={{0,2},{2,4},{4,6},{6,7},{7,5},{5,3},{3,1},{1,0},{8,10},{10,12},{12... | collective-permute-start | bytes 786440 | tf_op jit(solution)/shard_map/ppermute | solution.py:55
  103.3 9.0 %collective-permute-start.33 = (bf16[64,2048]{1,0:T(8,128)(2,1)S(1)}, bf16[64,2048]{1,0:T(8,128)(2,1)S(1)}, u32[]{:S(2)}, u32[]{:S(2)}) collective-permute-start(bf16[64,2048]{1,0:T(8,128)(2,1)S(1)} %add_convert_fusion.2), channel_id=1, source_target_pairs={{0,1},{2,0},{4,2},{6,4},{7,6},{5,7},{3,5},{1,3},{8,9},{10,8},{12,1... | collective-permute-start | bytes 786440 | tf_op jit(solution)/shard_map/ppermute | solution.py:55

commit v12 on v9

--- a/solution.py
+++ b/solution.py
@@ -105,7 +105,7 @@
                 for block in range(blocks)
                 for index in range(count)
             ],
-            4,
+            count * blocks,
         )
 
     return call(
@@ -153,7 +153,7 @@
     return moved
 
 
-def accumulate(chunks, first, last, weights, before=None, lead=0, shared=False):
+def accumulate(chunks, first, last, weights, before=None, lead=0):
     rows, depth = chunks[0][0].shape
     width = weights[0].shape[1]
     parts, span = len(weights), last - first
@@ -165,30 +165,23 @@
     def body(*refs):
         piece_refs = refs[: len(pieces)]
         weight_refs = refs[len(pieces) : len(pieces) + parts]
-        out_ref, left = refs[-2 - 2 * shared], refs[-1]
+        out_ref, left = refs[-2:]
         for index, ref in enumerate(piece_refs):
             chunk, piece = divmod(index, span)
             left[chunk * rows : (chunk + 1) * rows, piece * depth : (piece + 1) * depth] = ref[...]
         for part in range(parts):
             term = mm(left[...], weight_refs[part][first * depth : last * depth])
             if before is not None:
-                term = term + refs[len(args) - 1][lead + part]
+                term = term + refs[-3][lead + part]
             out_ref[part] = term.astype(dtype)
-            if shared:
-                side = lax.axis_index("tok") % 2
-                refs[-3][part] = out_ref[part, :, lanes(1 - side, width // 2)]
-                refs[-2][part] = out_ref[part, :, lanes(side, width // 2)]
 
     aliased = before is not None and not final
     args = [*pieces, *weights] + ([] if before is None else [before])
     return call(
         body,
         [WHOLE] * len(args),
-        [WHOLE] * (1 + 2 * shared),
-        [
-            jax.ShapeDtypeStruct((parts, total, size), dtype)
-            for size in (width, width // 2, width // 2)[: 1 + 2 * shared]
-        ],
+        WHOLE,
+        jax.ShapeDtypeStruct((parts, total, width), dtype),
         [pltpu.VMEM((total, span * depth), BF16)],
         vmem=12,
         cost=cost(
@@ -196,6 +189,37 @@
             2 * span * depth * (total + width * parts) + 8 * total * width * parts,
         ),
         aliases={len(args) - 1: 0} if aliased else None,
+    )(*args)
+
+
+def finish(chunk, piece, weights, sums, filled):
+    rows, depth = piece.shape
+    width = weights[0].shape[1]
+    parts = len(weights)
+    where = slice(chunk * rows, (chunk + 1) * rows)
+
+    def body(piece_ref, *refs):
+        weight_refs, sum_ref = refs[:parts], refs[parts]
+        out_ref, far_ref, near_ref = refs[-3:]
+        side = lax.axis_index("tok") % 2
+        for part in range(parts):
+            term = mm(piece_ref[...], weight_refs[part][-depth:]) + sum_ref[part, where]
+            out_ref[part, where] = term.astype(BF16)
+            far_ref[part, where] = out_ref[part, where, lanes(1 - side, width // 2)]
+            near_ref[part, where] = out_ref[part, where, lanes(side, width // 2)]
+
+    total = sums.shape[1]
+    args = [piece, *weights, sums, *filled]
+    return call(
+        body,
+        [WHOLE] * len(args),
+        [WHOLE] * 3,
+        [
+            jax.ShapeDtypeStruct((parts, total, size), BF16)
+            for size in (width, width // 2, width // 2)
+        ],
+        cost=cost(2 * rows * depth * width * parts, 2 * width * parts * (depth + 4 * rows)),
+        aliases={len(args) - 3 + index: index for index in range(3)} if filled else None,
     )(*args)
 
 
@@ -541,10 +565,13 @@
             chunks[c] += held[c].values()
         if step > 1:
             known = [chunk[: 2 * step - 1] for chunk in chunks]
-            (sums,) = accumulate(known, done, 2 * step - 1, weights, sums)
+            sums = accumulate(known, done, 2 * step - 1, weights, sums)
             done = 2 * step - 1
-    kv, far, near = accumulate(chunks, done, 2 * steps, weights[:2], sums, shared=True)
-    (query,) = accumulate(chunks, done, 2 * steps, weights[2:], sums, 2)
+    filled = ()
+    for c in reversed(range(CHUNKS)):
+        filled = finish(c, chunks[c][-1], weights[:2], sums, filled)
+    kv, far, near = filled
+    query = accumulate(chunks, done, 2 * steps, weights[2:], sums, 2)
 
     behind = lax.ppermute(far, "tok", [(index, index + 1) for index in range(1, tok_count - 1, 2)])
     beside = swap(far, 1)

time: 114 us -> 113 us (level)
  Pallas kernels: 30.5 us -> 27.9 us
  waiting for transfers between devices: 49.5 us -> 52.1 us
    pallas_call x1, Pallas kernels: 7.47 us -> 4.78 us  [load(): call(body, [IN_HBM] * count, [WHOLE] * count, [jax.ShapeDtypeStruct(array...]
    ppermute x28, waiting for transfers between devices: 39.8 us -> 42.4 us  [ring_send(): lax.ppermute(value, 'head', [(order[i], order[(i + step) % count]) for i...]
    pallas_call x5 -> x6, Pallas kernels: 7.65 us -> 7.76 us  [the longest x4 6.72 us: accumulate(): call(body, [WHOLE] * len(args), WHOLE, jax.ShapeDtypeStruct((parts, total...]
  transfers between devices with their start and end apart: 34 -> 34, of which waited for: 21 -> 23; matrix products, arithmetic and copies ran while one was open for 1% -> 1% of each run, Pallas kernels for 24% -> 22%
where the time goes in v12:
time: 113 us
  waiting for transfers between devices  52.1 us (46%)
  starting transfers between devices  31.2 us (28%)
  Pallas kernels  27.9 us (25%)
  other arithmetic  1.59 us (1%)
    ppermute x28, waiting for transfers between devices, ring_send(): lax.ppermute(value, 'head', [(order[i], order[(i + step) % count]) for i...  42.4 us
    ppermute x28, starting transfers between devices, ring_send(): lax.ppermute(value, 'head', [(order[i], order[(i + step) % count]) for i...  21.7 us
    pallas_call x4, Pallas kernels, accumulate(): call(body, [WHOLE] * len(args), WHOLE, jax.ShapeDtypeStruct((parts, total...  6.72 us
    pallas_call x4, Pallas kernels, partial_out(): call(body, [WHOLE] * 5 + [AFTER] * len(after), [WHOLE] * (2 * count), [ja...  5.18 us
    pallas_call x1, Pallas kernels, load(): call(body, [IN_HBM] * count, [WHOLE] * count, [jax.ShapeDtypeStruct(array...  4.78 us
    ppermute x4, waiting for transfers between devices, swap(): lax.ppermute(value, 'tok', [(index, index ^ bit) for index in range(count)])  4.61 us
    ppermute x4, starting transfers between devices, swap(): lax.ppermute(value, 'tok', [(index, index ^ bit) for index in range(count)])  4.43 us
    ppermute x1, waiting for transfers between devices, shards(): lax.ppermute(near, 'tok', [(index, index + 1) for index in range(tok_coun...  3.89 us
  transfers between devices with their start and end apart: 34, of which 23 were waited for; matrix products, arithmetic and copies ran while one was open for 1% of the time, Pallas kernels for 22%

profile of v12, /device:TPU:1, one launch (start us, length us, event | category | flops | bytes accessed | tf_op | source)
XLA Modules:
  0.0 113.1 jit_solution(9243112505095082327)
XLA Ops:
  0.0 1.0 shard_map.100
  1.1 2.1 %collective-permute-start.4 = (bf16[256,512]{1,0:T(8,128)(2,1)S(1)}, bf16[256,512]{1,0:T(8,128)(2,1)S(1)}, u32[]{:S(2)}, u32[]{:S(2)}) collective-permute-start(bf16[256,512]{1,0:T(8,128)(2,1)S(1)} %get-tuple-element.62.refs_3_), channel_id=1, source_target_pairs={{0,1},{2,0},{4,2},{6,4},{7,6},{5,7},{3,5},{1,3},{8,9},{10,8},{12,1... | collective-permute-start | bytes 786440 | tf_op jit(solution)/shard_map/ppermute | solution.py:55
  3.3 1.4 %collective-permute-start.3 = (bf16[256,512]{1,0:T(8,128)(2,1)S(1)}, bf16[256,512]{1,0:T(8,128)(2,1)S(1)}, u32[]{:S(2)}, u32[]{:S(2)}) collective-permute-start(bf16[256,512]{1,0:T(8,128)(2,1)S(1)} %get-tuple-element.62.refs_3_), channel_id=1, source_target_pairs={{0,2},{2,4},{4,6},{6,7},{7,5},{5,3},{3,1},{1,0},{8,10},{10,12},{12... | collective-permute-start | bytes 786440 | tf_op jit(solution)/shard_map/ppermute | solution.py:55
  4.8 4.8 %shard_map.101 = (bf16[4096,512]{1,0:T(8,128)(2,1)S(1)}, bf16[4096,512]{1,0:T(8,128)(2,1)S(1)}, bf16[4096,512]{1,0:T(8,128)(2,1)S(1)}) custom-call(bf16[4096,512]{1,0:T(8,128)(2,1)} %refs_0_.1, bf16[4096,512]{1,0:T(8,128)(2,1)} %refs_1_.1, bf16[4096,512]{1,0:T(8,128)(2,1)} %refs_2_.1), custom_call_target="tpu_custom_call" | custom-call | bytes 25165824 | tf_op jit(solution)/shard_map/pallas_call | solution.py:111
  9.6 1.4 %collective-permute-start.8 = (bf16[256,512]{1,0:T(8,128)(2,1)S(1)}, bf16[256,512]{1,0:T(8,128)(2,1)S(1)}, u32[]{:S(2)}, u32[]{:S(2)}) collective-permute-start(bf16[256,512]{1,0:T(8,128)(2,1)S(1)} %collective-permute-done.4.refs_5_), channel_id=1, source_target_pairs={{0,1},{2,0},{4,2},{6,4},{7,6},{5,7},{3,5},{1,3},{8,9},{10,8},{12,1... | collective-permute-start | bytes 786440 | tf_op jit(solution)/shard_map/ppermute | solution.py:55
  11.1 2.4 %collective-permute-start.5 = (f32[4,512]{1,0:T(4,128)S(1)}, f32[4,512]{1,0:T(4,128)S(1)}, u32[]{:S(2)}, u32[]{:S(2)}) collective-permute-start(f32[4,512]{1,0:T(4,128)S(1)} %bitcast.1), channel_id=1, source_target_pairs={{0,8},{8,0},{16,24},{24,16},{1,9},{9,1},{17,25},{25,17},{2,10},{10... | collective-permute-start | bytes 24584 | tf_op jit(solution)/shard_map/ppermute | solution.py:542
  13.5 2.2 %collective-permute-done.3.refs_4_ = bf16[256,512]{1,0:T(8,128)(2,1)S(1)} collective-permute-done((bf16[256,512]{1,0:T(8,128)(2,1)S(1)}, bf16[256,512]{1,0:T(8,128)(2,1)S(1)}, u32[]{:S(2)}, u32[]{:S(2)}) %collective-permute-start.3) | collective-permute-done | bytes 262176 | tf_op jit(solution)/shard_map/ppermute | solution.py:55
  15.6 0.5 collective-permute-start.13
  16.1 1.0 collective-permute-start.11
  17.1 2.6 %shard_map.102.refs_7_ = f32[3,512,512]{2,1,0:T(8,128)S(1)} custom-call(bf16[256,512]{1,0:T(8,128)(2,1)S(1)} %get-tuple-element.59.refs_0_, bf16[256,512]{1,0:T(8,128)(2,1)S(1)} %collective-permute-done.refs_1_, bf16[256,512]{1,0:T(8,128)(2,1)S(1)} %collective-permute-done.2.refs_2_, bf16[256,512]{1,0:T(8,128)(2,1)S(1)} %get-tuple-element.62.refs_3_, ...), custom_call_target="tpu_custom_call" | custom-call | flops 2415919104 | bytes 12582912 | tf_op jit(solution)/shard_map/pallas_call | solution.py:180
  19.7 0.8 collective-permute-done.8.refs_3_
  20.5 0.7 collective-permute-done.1.refs_0_
  21.2 1.3 %collective-permute-start.9 = (bf16[256,512]{1,0:T(8,128)(2,1)S(1)}, bf16[256,512]{1,0:T(8,128)(2,1)S(1)}, u32[]{:S(2)}, u32[]{:S(2)}) collective-permute-start(bf16[256,512]{1,0:T(8,128)(2,1)S(1)} %collective-permute-done.8.refs_3_), channel_id=1, source_target_pairs={{0,1},{2,0},{4,2},{6,4},{7,6},{5,7},{3,5},{1,3},{8,9},{10,8},{12,1... | collective-permute-start | bytes 786440 | tf_op jit(solution)/shard_map/ppermute | solution.py:55
  22.7 4.2 %collective-permute-done.13.refs_2_ = bf16[256,512]{1,0:T(8,128)(2,1)S(1)} collective-permute-done((bf16[256,512]{1,0:T(8,128)(2,1)S(1)}, bf16[256,512]{1,0:T(8,128)(2,1)S(1)}, u32[]{:S(2)}, u32[]{:S(2)}) %collective-permute-start.13) | collective-permute-done | bytes 262176 | tf_op jit(solution)/shard_map/ppermute | solution.py:55
  26.9 0.5 collective-permute-start.14
  27.3 1.0 collective-permute-start.12
  28.3 3.3 %collective-permute-done.9.refs_3_ = bf16[256,512]{1,0:T(8,128)(2,1)S(1)} collective-permute-done((bf16[256,512]{1,0:T(8,128)(2,1)S(1)}, bf16[256,512]{1,0:T(8,128)(2,1)S(1)}, u32[]{:S(2)}, u32[]{:S(2)}) %collective-permute-start.9) | collective-permute-done | bytes 262176 | tf_op jit(solution)/shard_map/ppermute | solution.py:55
  31.6 1.1 collective-permute-start.10
  32.7 0.3 collective-permute-start.7
  33.1 1.8 %shard_map.103.refs_7_ = f32[3,512,512]{2,1,0:T(8,128)S(1)} custom-call(bf16[256,512]{1,0:T(8,128)(2,1)S(1)} %collective-permute-done.1.refs_0_, bf16[256,512]{1,0:T(8,128)(2,1)S(1)} %collective-permute-done.11.refs_1_, bf16[256,512]{1,0:T(8,128)(2,1)S(1)} %collective-permute-done.13.refs_2_, ...), custom_call_target="tpu_custom_call", output_to_operand_aliasing={{}: (7, {})} | custom-call | flops 1610612736 | bytes 10485760 | tf_op jit(solution)/shard_map/pallas_call | solution.py:180
  34.9 3.2 %collective-permute-done.14.refs_2_ = bf16[256,512]{1,0:T(8,128)(2,1)S(1)} collective-permute-done((bf16[256,512]{1,0:T(8,128)(2,1)S(1)}, bf16[256,512]{1,0:T(8,128)(2,1)S(1)}, u32[]{:S(2)}, u32[]{:S(2)}) %collective-permute-start.14) | collective-permute-done | bytes 262176 | tf_op jit(solution)/shard_map/ppermute | solution.py:55
  38.1 1.8 %shard_map.104.refs_3_.refs_2_ = f32[3,512,512]{2,1,0:T(8,128)S(1)} custom-call(bf16[256,512]{1,0:T(8,128)(2,1)S(1)} %collective-permute-done.6.refs_0_, bf16[256,512]{1,0:T(8,128)(2,1)S(1)} %collective-permute-done.12.refs_1_, bf16[256,512]{1,0:T(8,128)(2,1)S(1)} %collective-permute-done.14.refs_2_, ...), custom_call_target="tpu_custom_call", output_to_operand_aliasing={{}: (7, {})} | custom-call | flops 1610612736 | bytes 10485760 | tf_op jit(solution)/shard_map/pallas_call | solution.py:180
  39.9 2.9 %collective-permute-done.10.refs_1_.piece_ref = bf16[256,512]{1,0:T(8,128)(2,1)S(1)} collective-permute-done((bf16[256,512]{1,0:T(8,128)(2,1)S(1)}, bf16[256,512]{1,0:T(8,128)(2,1)S(1)}, u32[]{:S(2)}, u32[]{:S(2)}) %collective-permute-start.10) | collective-permute-done | bytes 262176 | tf_op jit(solution)/shard_map/ppermute | solution.py:55
  42.8 0.5 shard_map.106
  43.3 0.4 collective-permute-done.7.refs_0_.piece_ref
  43.7 0.5 shard_map.107
  44.2 1.9 %collective-permute-start.16 = (bf16[2,512,256]{2,1,0:T(8,128)(2,1)S(1)}, bf16[2,512,256]{2,1,0:T(8,128)(2,1)S(1)}, u32[]{:S(2)}, u32[]{:S(2)}) collective-permute-start(bf16[2,512,256]{2,1,0:T(8,128)(2,1)S(1)} %get-tuple-element.78), channel_id=1, source_target_pairs={{0,8},{8,0},{16,24},{24,16},{1,9},{9,1},{17,25},{25,17},{2,10},{10... | collective-permute-start | bytes 1572872 | tf_op jit(solution)/shard_map/ppermute | solution.py:542
  46.2 3.1 %collective-permute-start.15 = (bf16[2,512,256]{2,1,0:T(8,128)(2,1)S(1)}, bf16[2,512,256]{2,1,0:T(8,128)(2,1)S(1)}, u32[]{:S(2)}, u32[]{:S(2)}) collective-permute-start(bf16[2,512,256]{2,1,0:T(8,128)(2,1)S(1)} %get-tuple-element.78), channel_id=1, source_target_pairs={{8,16},{9,17},{10,18},{11,19},{12,20},{13,21},{14,22},{15,23}} | collective-permute-start | bytes 1572872 | tf_op jit(solution)/shard_map/ppermute | solution.py:576
  49.3 1.4 %shard_map.110.rest_0_ = f32[2,3,128,256]{3,2,1,0:T(8,128)S(1)} custom-call(bf16[2,512,512]{2,1,0:T(8,128)(2,1)S(1)} %get-tuple-element.75.kv_ref, f32[4,512]{1,0:T(4,128)S(1)} %bitcast.2, f32[4,128,256]{2,1,0:T(8,128)S(1)} %copy-done.1, f32[4,128,256]{2,1,0:T(8,128)S(1)} %copy-done.2, f32[4,256,128]{2,1,0:T(8,128)S(1)} %copy-done.3), custom_call_target="tpu_custom_call" | custom-call | flops 402653184 | bytes 1572864 | tf_op jit(solution)/shard_map/pallas_call | solution.py:272
  50.7 1.4 %shard_map.111 = (f32[2,3,128,256]{3,2,1,0:T(8,128)S(1)}, bf16[2,3,128,256]{3,2,1,0:T(8,128)(2,1)S(1)}) custom-call(bf16[2,512,256]{2,1,0:T(8,128)(2,1)S(1)} %collective-permute-done.16.refs_1_.kv_ref, f32[4,512]{1,0:T(4,128)S(1)} %collective-permute-done.5.rate_ref, f32[4,128,256]{2,1,0:T(8,128)S(1)} %copy-done.1, f32[4,128,256]{2,1,0:T(8,128)S(1)} %copy-done.2, ...), custom_call_target="tpu_custom_call" | custom-call | flops 402653184 | bytes 1572864 | tf_op jit(solution)/shard_map/pallas_call | solution.py:272
  52.2 0.4 shard_map.105.q_ref
  52.7 2.1 %shard_map.108 = (f32[512,512]{1,0:T(8,128)S(1)}, f32[2,512,512]{2,1,0:T(8,128)S(1)}) custom-call(bf16[1,512,512]{2,1,0:T(8,128)(2,1)S(1)} %shard_map.105.q_ref, bf16[2,512,512]{2,1,0:T(8,128)(2,1)S(1)} %get-tuple-element.75.kv_ref), custom_call_target="tpu_custom_call" | custom-call | flops 402653184 | bytes 2097152 | tf_op jit(solution)/shard_map/pallas_call | solution.py:365
  54.8 1.9 %collective-permute-start.17 = (bf16[2,512,256]{2,1,0:T(8,128)(2,1)S(1)}, bf16[2,512,256]{2,1,0:T(8,128)(2,1)S(1)}, u32[]{:S(2)}, u32[]{:S(2)}) collective-permute-start(bf16[2,512,256]{2,1,0:T(8,128)(2,1)S(1)} %get-tuple-element.80), channel_id=1, source_target_pairs={{0,8},{8,16},{16,24},{1,9},{9,17},{17,25},{2,10},{10,18},{18,26},{... | collective-permute-start | bytes 1572872 | tf_op jit(solution)/shard_map/ppermute | solution.py:590
  56.7 1.2 %collective-permute-done.15.refs_0_ = bf16[2,512,256]{2,1,0:T(8,128)(2,1)S(1)} collective-permute-done((bf16[2,512,256]{2,1,0:T(8,128)(2,1)S(1)}, bf16[2,512,256]{2,1,0:T(8,128)(2,1)S(1)}, u32[]{:S(2)}, u32[]{:S(2)}) %collective-permute-start.15) | collective-permute-done | bytes 524320 | tf_op jit(solution)/shard_map/ppermute | solution.py:576
  57.9 1.2 %shard_map.109.rest_1_.attended_ref.sum_ref = f32[512,512]{1,0:T(8,128)S(1)} custom-call(f32[512,512]{1,0:T(8,128)S(1)} %get-tuple-element.76.sum_ref, f32[2,512,512]{2,1,0:T(8,128)S(1)} %get-tuple-element.77.stats_ref, bf16[1,512,512]{2,1,0:T(8,128)(2,1)S(1)} %shard_map.105.q_ref, ...), custom_call_target="tpu_custom_call", output_to_operand_aliasing={{}: (0, {})} | custom-call | flops 201326592 | bytes 1048576 | tf_op jit(solution)/shard_map/pallas_call | solution.py:405
  59.2 4.6 %collective-permute-done.18.rest_0_ = bf16[2,3,128,256]{3,2,1,0:T(8,128)(2,1)S(1)} collective-permute-done((bf16[2,3,128,256]{3,2,1,0:T(8,128)(2,1)S(1)}, bf16[2,3,128,256]{3,2,1,0:T(8,128)(2,1)S(1)}, u32[]{:S(2)}, u32[]{:S(2)}) %collective-permute-start.18) | collective-permute-done | bytes 393248 | tf_op jit(solution)/shard_map/ppermute | solution.py:542
  63.8 0.8 shard_map.112.net_ref
  64.7 0.8 shard_map.113.refs_1_.near_ref
  65.5 3.9 %collective-permute-done.17.refs_0_ = bf16[2,512,256]{2,1,0:T(8,128)(2,1)S(1)} collective-permute-done((bf16[2,512,256]{2,1,0:T(8,128)(2,1)S(1)}, bf16[2,512,256]{2,1,0:T(8,128)(2,1)S(1)}, u32[]{:S(2)}, u32[]{:S(2)}) %collective-permute-start.17) | collective-permute-done | bytes 524320 | tf_op jit(solution)/shard_map/ppermute | solution.py:590
  69.4 1.2 %shard_map.114.attended_ref = f32[512,512]{1,0:T(8,128)S(1)} custom-call(f32[512,512]{1,0:T(8,128)S(1)} %shard_map.109.rest_1_.attended_ref.sum_ref, f32[2,512,512]{2,1,0:T(8,128)S(1)} %get-tuple-element.77.stats_ref, bf16[1,512,512]{2,1,0:T(8,128)(2,1)S(1)} %shard_map.105.q_ref, ...), custom_call_target="tpu_custom_call", output_to_operand_aliasing={{}: (0, {})} | custom-call | flops 201326592 | bytes 1048576 | tf_op jit(solution)/shard_map/pallas_call | solution.py:405
  70.6 1.2 %shard_map.116 = (bf16[64,2048]{1,0:T(8,128)(2,1)S(1)}, bf16[64,2048]{1,0:T(8,128)(2,1)S(1)}) custom-call(bf16[1,512,512]{2,1,0:T(8,128)(2,1)S(1)} %shard_map.105.q_ref, f32[512,512]{1,0:T(8,128)S(1)} %shard_map.114.attended_ref, bf16[2,3,128,256]{3,2,1,0:T(8,128)(2,1)S(1)} %collective-permute-done.19.net_ref, ...), custom_call_target="tpu_custom_call" | custom-call | flops 268435456 | bytes 4718592 | tf_op jit(solution)/shard_map/pallas_call | solution.py:481
  71.8 1.3 %collective-permute-start.21 = (bf16[64,2048]{1,0:T(8,128)(2,1)S(1)}, bf16[64,2048]{1,0:T(8,128)(2,1)S(1)}, u32[]{:S(2)}, u32[]{:S(2)}) collective-permute-start(bf16[64,2048]{1,0:T(8,128)(2,1)S(1)} %get-tuple-element.86), channel_id=1, source_target_pairs={{0,1},{2,0},{4,2},{6,4},{7,6},{5,7},{3,5},{1,3},{8,9},{10,8},{12,1... | collective-permute-start | bytes 786440 | tf_op jit(solution)/shard_map/ppermute | solution.py:55
  73.4 1.2 %shard_map.115 = (bf16[64,2048]{1,0:T(8,128)(2,1)S(1)}, bf16[64,2048]{1,0:T(8,128)(2,1)S(1)}, bf16[64,2048]{1,0:T(8,128)(2,1)S(1)}, bf16[64,2048]{1,0:T(8,128)(2,1)S(1)}) custom-call(bf16[1,512,512]{2,1,0:T(8,128)(2,1)S(1)} %shard_map.105.q_ref, f32[512,512]{1,0:T(8,128)S(1)} %shard_map.114.attended_ref, ...), custom_call_target="tpu_custom_call" | custom-call | flops 536870912 | bytes 5242880 | tf_op jit(solution)/shard_map/pallas_call | solution.py:481
  74.6 1.4 %collective-permute-start.25 = (bf16[64,2048]{1,0:T(8,128)(2,1)S(1)}, bf16[64,2048]{1,0:T(8,128)(2,1)S(1)}, u32[]{:S(2)}, u32[]{:S(2)}) collective-permute-start(bf16[64,2048]{1,0:T(8,128)(2,1)S(1)} %get-tuple-element.90), channel_id=1, source_target_pairs={{0,1},{2,0},{4,2},{6,4},{7,6},{5,7},{3,5},{1,3},{8,9},{10,8},{12,1... | collective-permute-start | bytes 786440 | tf_op jit(solution)/shard_map/ppermute | solution.py:55
  76.1 4.1 %collective-permute-done.21.refs_1_ = bf16[64,2048]{1,0:T(8,128)(2,1)S(1)} collective-permute-done((bf16[64,2048]{1,0:T(8,128)(2,1)S(1)}, bf16[64,2048]{1,0:T(8,128)(2,1)S(1)}, u32[]{:S(2)}, u32[]{:S(2)}) %collective-permute-start.21) | collective-permute-done | bytes 262176 | tf_op jit(solution)/shard_map/ppermute | solution.py:55
  80.3 1.2 %collective-permute-done.20.refs_0_ = bf16[64,2048]{1,0:T(8,128)(2,1)S(1)} collective-permute-done((bf16[64,2048]{1,0:T(8,128)(2,1)S(1)}, bf16[64,2048]{1,0:T(8,128)(2,1)S(1)}, u32[]{:S(2)}, u32[]{:S(2)}) %collective-permute-start.20) | collective-permute-done | bytes 262176 | tf_op jit(solution)/shard_map/ppermute | solution.py:55
  81.6 1.3 %collective-permute-start.23 = (bf16[64,2048]{1,0:T(8,128)(2,1)S(1)}, bf16[64,2048]{1,0:T(8,128)(2,1)S(1)}, u32[]{:S(2)}, u32[]{:S(2)}) collective-permute-start(bf16[64,2048]{1,0:T(8,128)(2,1)S(1)} %add_convert_fusion.10), channel_id=1, source_target_pairs={{0,1},{2,0},{4,2},{6,4},{7,6},{5,7},{3,5},{1,3},{8,9},{10,8},{12,1... | collective-permute-start | bytes 786440 | tf_op jit(solution)/shard_map/ppermute | solution.py:55
  83.1 1.2 %shard_map.118 = (bf16[64,2048]{1,0:T(8,128)(2,1)S(1)}, bf16[64,2048]{1,0:T(8,128)(2,1)S(1)}, bf16[64,2048]{1,0:T(8,128)(2,1)S(1)}, bf16[64,2048]{1,0:T(8,128)(2,1)S(1)}) custom-call(bf16[1,512,512]{2,1,0:T(8,128)(2,1)S(1)} %shard_map.105.q_ref, f32[512,512]{1,0:T(8,128)S(1)} %shard_map.114.attended_ref, ...), custom_call_target="tpu_custom_call" | custom-call | flops 536870912 | bytes 5242880 | tf_op jit(solution)/shard_map/pallas_call | solution.py:481
  84.3 1.5 %collective-permute-done.25 = bf16[64,2048]{1,0:T(8,128)(2,1)S(1)} collective-permute-done((bf16[64,2048]{1,0:T(8,128)(2,1)S(1)}, bf16[64,2048]{1,0:T(8,128)(2,1)S(1)}, u32[]{:S(2)}, u32[]{:S(2)}) %collective-permute-start.25) | collective-permute-done | bytes 262176 | tf_op jit(solution)/shard_map/ppermute | solution.py:55
  85.9 1.2 %collective-permute-done.24 = bf16[64,2048]{1,0:T(8,128)(2,1)S(1)} collective-permute-done((bf16[64,2048]{1,0:T(8,128)(2,1)S(1)}, bf16[64,2048]{1,0:T(8,128)(2,1)S(1)}, u32[]{:S(2)}, u32[]{:S(2)}) %collective-permute-start.24) | collective-permute-done | bytes 262176 | tf_op jit(solution)/shard_map/ppermute | solution.py:55
  87.2 1.3 %collective-permute-start.27 = (bf16[64,2048]{1,0:T(8,128)(2,1)S(1)}, bf16[64,2048]{1,0:T(8,128)(2,1)S(1)}, u32[]{:S(2)}, u32[]{:S(2)}) collective-permute-start(bf16[64,2048]{1,0:T(8,128)(2,1)S(1)} %add_convert_fusion.8), channel_id=1, source_target_pairs={{0,1},{2,0},{4,2},{6,4},{7,6},{5,7},{3,5},{1,3},{8,9},{10,8},{12,1... | collective-permute-start | bytes 786440 | tf_op jit(solution)/shard_map/ppermute | solution.py:55
  88.7 2.7 %collective-permute-done.23.refs_1_ = bf16[64,2048]{1,0:T(8,128)(2,1)S(1)} collective-permute-done((bf16[64,2048]{1,0:T(8,128)(2,1)S(1)}, bf16[64,2048]{1,0:T(8,128)(2,1)S(1)}, u32[]{:S(2)}, u32[]{:S(2)}) %collective-permute-start.23) | collective-permute-done | bytes 262176 | tf_op jit(solution)/shard_map/ppermute | solution.py:55
  91.5 1.2 %collective-permute-done.22.refs_0_ = bf16[64,2048]{1,0:T(8,128)(2,1)S(1)} collective-permute-done((bf16[64,2048]{1,0:T(8,128)(2,1)S(1)}, bf16[64,2048]{1,0:T(8,128)(2,1)S(1)}, u32[]{:S(2)}, u32[]{:S(2)}) %collective-permute-start.22) | collective-permute-done | bytes 262176 | tf_op jit(solution)/shard_map/ppermute | solution.py:55
  92.8 1.3 %collective-permute-start.31 = (bf16[64,2048]{1,0:T(8,128)(2,1)S(1)}, bf16[64,2048]{1,0:T(8,128)(2,1)S(1)}, u32[]{:S(2)}, u32[]{:S(2)}) collective-permute-start(bf16[64,2048]{1,0:T(8,128)(2,1)S(1)} %add_convert_fusion.4), channel_id=1, source_target_pairs={{0,1},{2,0},{4,2},{6,4},{7,6},{5,7},{3,5},{1,3},{8,9},{10,8},{12,1... | collective-permute-start | bytes 786440 | tf_op jit(solution)/shard_map/ppermute | solution.py:55
  94.3 1.5 %shard_map.117 = (bf16[64,2048]{1,0:T(8,128)(2,1)S(1)}, bf16[64,2048]{1,0:T(8,128)(2,1)S(1)}, bf16[64,2048]{1,0:T(8,128)(2,1)S(1)}, bf16[64,2048]{1,0:T(8,128)(2...) custom-call(bf16[1,512,512]{2,1,0:T(8,128)(2,1)S(1)} %shard_map.105.q_ref, ...), custom_call_target="tpu_custom_call" | custom-call | flops 805306368 | bytes 5767168 | tf_op jit(solution)/shard_map/pallas_call | solution.py:481
  95.9 0.9 collective-permute-done.27
  96.8 1.5 %collective-permute-done.26 = bf16[64,2048]{1,0:T(8,128)(2,1)S(1)} collective-permute-done((bf16[64,2048]{1,0:T(8,128)(2,1)S(1)}, bf16[64,2048]{1,0:T(8,128)(2,1)S(1)}, u32[]{:S(2)}, u32[]{:S(2)}) %collective-permute-start.26) | collective-permute-done | bytes 262176 | tf_op jit(solution)/shard_map/ppermute | solution.py:55
  98.7 1.3 %collective-permute-start.29 = (bf16[64,2048]{1,0:T(8,128)(2,1)S(1)}, bf16[64,2048]{1,0:T(8,128)(2,1)S(1)}, u32[]{:S(2)}, u32[]{:S(2)}) collective-permute-start(bf16[64,2048]{1,0:T(8,128)(2,1)S(1)} %add_convert_fusion.6), channel_id=1, source_target_pairs={{0,1},{2,0},{4,2},{6,4},{7,6},{5,7},{3,5},{1,3},{8,9},{10,8},{12,1... | collective-permute-start | bytes 786440 | tf_op jit(solution)/shard_map/ppermute | solution.py:55
  100.0 2.3 %collective-permute-done.31 = bf16[64,2048]{1,0:T(8,128)(2,1)S(1)} collective-permute-done((bf16[64,2048]{1,0:T(8,128)(2,1)S(1)}, bf16[64,2048]{1,0:T(8,128)(2,1)S(1)}, u32[]{:S(2)}, u32[]{:S(2)}) %collective-permute-start.31) | collective-permute-done | bytes 262176 | tf_op jit(solution)/shard_map/ppermute | solution.py:55
  102.3 1.7 %collective-permute-done.30 = bf16[64,2048]{1,0:T(8,128)(2,1)S(1)} collective-permute-done((bf16[64,2048]{1,0:T(8,128)(2,1)S(1)}, bf16[64,2048]{1,0:T(8,128)(2,1)S(1)}, u32[]{:S(2)}, u32[]{:S(2)}) %collective-permute-start.30) | collective-permute-done | bytes 262176 | tf_op jit(solution)/shard_map/ppermute | solution.py:55
  104.3 1.3 %collective-permute-start.33 = (bf16[64,2048]{1,0:T(8,128)(2,1)S(1)}, bf16[64,2048]{1,0:T(8,128)(2,1)S(1)}, u32[]{:S(2)}, u32[]{:S(2)}) collective-permute-start(bf16[64,2048]{1,0:T(8,128)(2,1)S(1)} %add_convert_fusion.2), channel_id=1, source_target_pairs={{0,1},{2,0},{4,2},{6,4},{7,6},{5,7},{3,5},{1,3},{8,9},{10,8},{12,1... | collective-permute-start | bytes 786440 | tf_op jit(solution)/shard_map/ppermute | solution.py:55
  105.6 4.0 %collective-permute-done.28.refs_2_ = bf16[64,2048]{1,0:T(8,128)(2,1)S(1)} collective-permute-done((bf16[64,2048]{1,0:T(8,128)(2,1)S(1)}, bf16[64,2048]{1,0:T(8,128)(2,1)S(1)}, u32[]{:S(2)}, u32[]{:S(2)}) %collective-permute-start.28) | collective-permute-done | bytes 262176 | tf_op jit(solution)/shard_map/ppermute | solution.py:55
  109.7 2.4 %collective-permute-done.32 = bf16[64,2048]{1,0:T(8,128)(2,1)S(1)} collective-permute-done((bf16[64,2048]{1,0:T(8,128)(2,1)S(1)}, bf16[64,2048]{1,0:T(8,128)(2,1)S(1)}, u32[]{:S(2)}, u32[]{:S(2)}) %collective-permute-start.32) | collective-permute-done | bytes 262176 | tf_op jit(solution)/shard_map/ppermute | solution.py:55
  112.2 0.8 pad_maximum_fusion
  (49 shorter events, 3.0 us)
Async XLA Ops:
  1.1 8.5 %collective-permute-start.4 = (bf16[256,512]{1,0:T(8,128)(2,1)S(1)}, bf16[256,512]{1,0:T(8,128)(2,1)S(1)}, u32[]{:S(2)}, u32[]{:S(2)}) collective-permute-start(bf16[256,512]{1,0:T(8,128)(2,1)S(1)} %get-tuple-element.62.refs_3_), channel_id=1, source_target_pairs={{0,1},{2,0},{4,2},{6,4},{7,6},{5,7},{3,5},{1,3},{8,9},{10,8},{12,1... | collective-permute-start | bytes 786440 | tf_op jit(solution)/shard_map/ppermute | solution.py:55
  3.1 8.0 %copy-start.4 = (f32[512,4]{0,1:T(4,128)S(1)}, f32[512,4]{0,1:T(4,128)}, u32[]{:S(2)}) copy-start(f32[512,4]{0,1:T(4,128)} %param.18) | copy-start | bytes 24580
  3.1 7.8 %collective-permute-start = (bf16[256,512]{1,0:T(8,128)(2,1)S(1)}, bf16[256,512]{1,0:T(8,128)(2,1)S(1)}, u32[]{:S(2)}, u32[]{:S(2)}) collective-permute-start(bf16[256,512]{1,0:T(8,128)(2,1)S(1)} %get-tuple-element.59.refs_0_), channel_id=1, source_target_pairs={{0,2},{2,4},{4,6},{6,7},{7,5},{5,3},{3,1},{1,0},{8,10},{10,12},{12... | collective-permute-start | bytes 786440 | tf_op jit(solution)/shard_map/ppermute | solution.py:55
  3.3 12.3 %collective-permute-start.3 = (bf16[256,512]{1,0:T(8,128)(2,1)S(1)}, bf16[256,512]{1,0:T(8,128)(2,1)S(1)}, u32[]{:S(2)}, u32[]{:S(2)}) collective-permute-start(bf16[256,512]{1,0:T(8,128)(2,1)S(1)} %get-tuple-element.62.refs_3_), channel_id=1, source_target_pairs={{0,2},{2,4},{4,6},{6,7},{7,5},{5,3},{3,1},{1,0},{8,10},{10,12},{12... | collective-permute-start | bytes 786440 | tf_op jit(solution)/shard_map/ppermute | solution.py:55
  4.7 11.4 %collective-permute-start.2 = (bf16[256,512]{1,0:T(8,128)(2,1)S(1)}, bf16[256,512]{1,0:T(8,128)(2,1)S(1)}, u32[]{:S(2)}, u32[]{:S(2)}) collective-permute-start(bf16[256,512]{1,0:T(8,128)(2,1)S(1)} %get-tuple-element.59.refs_0_), channel_id=1, source_target_pairs={{0,1},{2,0},{4,2},{6,4},{7,6},{5,7},{3,5},{1,3},{8,9},{10,8},{12,1... | collective-permute-start | bytes 786440 | tf_op jit(solution)/shard_map/ppermute | solution.py:55
  9.6 10.9 %collective-permute-start.8 = (bf16[256,512]{1,0:T(8,128)(2,1)S(1)}, bf16[256,512]{1,0:T(8,128)(2,1)S(1)}, u32[]{:S(2)}, u32[]{:S(2)}) collective-permute-start(bf16[256,512]{1,0:T(8,128)(2,1)S(1)} %collective-permute-done.4.refs_5_), channel_id=1, source_target_pairs={{0,1},{2,0},{4,2},{6,4},{7,6},{5,7},{3,5},{1,3},{8,9},{10,8},{12,1... | collective-permute-start | bytes 786440 | tf_op jit(solution)/shard_map/ppermute | solution.py:55
  10.9 10.3 %collective-permute-start.1 = (bf16[256,512]{1,0:T(8,128)(2,1)S(1)}, bf16[256,512]{1,0:T(8,128)(2,1)S(1)}, u32[]{:S(2)}, u32[]{:S(2)}) collective-permute-start(bf16[256,512]{1,0:T(8,128)(2,1)S(1)} %collective-permute-done.refs_1_), channel_id=1, source_target_pairs={{0,2},{2,4},{4,6},{6,7},{7,5},{5,3},{3,1},{1,0},{8,10},{10,12},{12... | collective-permute-start | bytes 786440 | tf_op jit(solution)/shard_map/ppermute | solution.py:55
  11.1 8.6 %collective-permute-start.5 = (f32[4,512]{1,0:T(4,128)S(1)}, f32[4,512]{1,0:T(4,128)S(1)}, u32[]{:S(2)}, u32[]{:S(2)}) collective-permute-start(f32[4,512]{1,0:T(4,128)S(1)} %bitcast.1), channel_id=1, source_target_pairs={{0,8},{8,0},{16,24},{24,16},{1,9},{9,1},{17,25},{25,17},{2,10},{10... | collective-permute-start | bytes 24584 | tf_op jit(solution)/shard_map/ppermute | solution.py:542
  15.6 11.2 %collective-permute-start.13 = (bf16[256,512]{1,0:T(8,128)(2,1)S(1)}, bf16[256,512]{1,0:T(8,128)(2,1)S(1)}, u32[]{:S(2)}, u32[]{:S(2)}) collective-permute-start(bf16[256,512]{1,0:T(8,128)(2,1)S(1)} %collective-permute-done.3.refs_4_), channel_id=1, source_target_pairs={{0,2},{2,4},{4,6},{6,7},{7,5},{5,3},{3,1},{1,0},{8,10},{10,12},{12... | collective-permute-start | bytes 786440 | tf_op jit(solution)/shard_map/ppermute | solution.py:55
  16.1 10.8 %collective-permute-start.11 = (bf16[256,512]{1,0:T(8,128)(2,1)S(1)}, bf16[256,512]{1,0:T(8,128)(2,1)S(1)}, u32[]{:S(2)}, u32[]{:S(2)}) collective-permute-start(bf16[256,512]{1,0:T(8,128)(2,1)S(1)} %collective-permute-done.2.refs_2_), channel_id=1, source_target_pairs={{0,1},{2,0},{4,2},{6,4},{7,6},{5,7},{3,5},{1,3},{8,9},{10,8},{12,1... | collective-permute-start | bytes 786440 | tf_op jit(solution)/shard_map/ppermute | solution.py:55
  21.2 10.3 %collective-permute-start.9 = (bf16[256,512]{1,0:T(8,128)(2,1)S(1)}, bf16[256,512]{1,0:T(8,128)(2,1)S(1)}, u32[]{:S(2)}, u32[]{:S(2)}) collective-permute-start(bf16[256,512]{1,0:T(8,128)(2,1)S(1)} %collective-permute-done.8.refs_3_), channel_id=1, source_target_pairs={{0,1},{2,0},{4,2},{6,4},{7,6},{5,7},{3,5},{1,3},{8,9},{10,8},{12,1... | collective-permute-start | bytes 786440 | tf_op jit(solution)/shard_map/ppermute | solution.py:55
  22.5 10.2 %collective-permute-start.6 = (bf16[256,512]{1,0:T(8,128)(2,1)S(1)}, bf16[256,512]{1,0:T(8,128)(2,1)S(1)}, u32[]{:S(2)}, u32[]{:S(2)}) collective-permute-start(bf16[256,512]{1,0:T(8,128)(2,1)S(1)} %collective-permute-done.1.refs_0_), channel_id=1, source_target_pairs={{0,2},{2,4},{4,6},{6,7},{7,5},{5,3},{3,1},{1,0},{8,10},{10,12},{12... | collective-permute-start | bytes 786440 | tf_op jit(solution)/shard_map/ppermute | solution.py:55
  26.9 11.2 %collective-permute-start.14 = (bf16[256,512]{1,0:T(8,128)(2,1)S(1)}, bf16[256,512]{1,0:T(8,128)(2,1)S(1)}, u32[]{:S(2)}, u32[]{:S(2)}) collective-permute-start(bf16[256,512]{1,0:T(8,128)(2,1)S(1)} %collective-permute-done.13.refs_2_), channel_id=1, source_target_pairs={{0,2},{2,4},{4,6},{6,7},{7,5},{5,3},{3,1},{1,0},{8,10},{10,12},{12... | collective-permute-start | bytes 786440 | tf_op jit(solution)/shard_map/ppermute | solution.py:55
  27.3 10.8 %collective-permute-start.12 = (bf16[256,512]{1,0:T(8,128)(2,1)S(1)}, bf16[256,512]{1,0:T(8,128)(2,1)S(1)}, u32[]{:S(2)}, u32[]{:S(2)}) collective-permute-start(bf16[256,512]{1,0:T(8,128)(2,1)S(1)} %collective-permute-done.11.refs_1_), channel_id=1, source_target_pairs={{0,1},{2,0},{4,2},{6,4},{7,6},{5,7},{3,5},{1,3},{8,9},{10,8},{12,1... | collective-permute-start | bytes 786440 | tf_op jit(solution)/shard_map/ppermute | solution.py:55
  31.6 11.2 %collective-permute-start.10 = (bf16[256,512]{1,0:T(8,128)(2,1)S(1)}, bf16[256,512]{1,0:T(8,128)(2,1)S(1)}, u32[]{:S(2)}, u32[]{:S(2)}) collective-permute-start(bf16[256,512]{1,0:T(8,128)(2,1)S(1)} %collective-permute-done.9.refs_3_), channel_id=1, source_target_pairs={{0,1},{2,0},{4,2},{6,4},{7,6},{5,7},{3,5},{1,3},{8,9},{10,8},{12,1... | collective-permute-start | bytes 786440 | tf_op jit(solution)/shard_map/ppermute | solution.py:55
  32.7 11.0 %collective-permute-start.7 = (bf16[256,512]{1,0:T(8,128)(2,1)S(1)}, bf16[256,512]{1,0:T(8,128)(2,1)S(1)}, u32[]{:S(2)}, u32[]{:S(2)}) collective-permute-start(bf16[256,512]{1,0:T(8,128)(2,1)S(1)} %collective-permute-done.6.refs_0_), channel_id=1, source_target_pairs={{0,2},{2,4},{4,6},{6,7},{7,5},{5,3},{3,1},{1,0},{8,10},{10,12},{12... | collective-permute-start | bytes 786440 | tf_op jit(solution)/shard_map/ppermute | solution.py:55
  43.7 5.5 %copy-start.1 = (f32[4,128,256]{2,1,0:T(8,128)S(1)}, f32[4,128,256]{2,1,0:T(8,128)}, u32[]{:S(2)}) copy-start(f32[4,128,256]{2,1,0:T(8,128)} %gate_ref.5) | copy-start | bytes 1572868
  43.7 5.6 %copy-start.2 = (f32[4,128,256]{2,1,0:T(8,128)S(1)}, f32[4,128,256]{2,1,0:T(8,128)}, u32[]{:S(2)}) copy-start(f32[4,128,256]{2,1,0:T(8,128)} %up_ref.5) | copy-start | bytes 1572868
  43.7 5.6 %copy-start.3 = (f32[4,256,128]{2,1,0:T(8,128)S(1)}, f32[4,256,128]{2,1,0:T(8,128)}, u32[]{:S(2)}) copy-start(f32[4,256,128]{2,1,0:T(8,128)} %down_ref.5) | copy-start | bytes 1572868
  44.2 6.5 %collective-permute-start.16 = (bf16[2,512,256]{2,1,0:T(8,128)(2,1)S(1)}, bf16[2,512,256]{2,1,0:T(8,128)(2,1)S(1)}, u32[]{:S(2)}, u32[]{:S(2)}) collective-permute-start(bf16[2,512,256]{2,1,0:T(8,128)(2,1)S(1)} %get-tuple-element.78), channel_id=1, source_target_pairs={{0,8},{8,0},{16,24},{24,16},{1,9},{9,1},{17,25},{25,17},{2,10},{10... | collective-permute-start | bytes 1572872 | tf_op jit(solution)/shard_map/ppermute | solution.py:542
  46.2 11.8 %collective-permute-start.15 = (bf16[2,512,256]{2,1,0:T(8,128)(2,1)S(1)}, bf16[2,512,256]{2,1,0:T(8,128)(2,1)S(1)}, u32[]{:S(2)}, u32[]{:S(2)}) collective-permute-start(bf16[2,512,256]{2,1,0:T(8,128)(2,1)S(1)} %get-tuple-element.78), channel_id=1, source_target_pairs={{8,16},{9,17},{10,18},{11,19},{12,20},{13,21},{14,22},{15,23}} | collective-permute-start | bytes 1572872 | tf_op jit(solution)/shard_map/ppermute | solution.py:576
  52.2 11.6 %collective-permute-start.18 = (bf16[2,3,128,256]{3,2,1,0:T(8,128)(2,1)S(1)}, bf16[2,3,128,256]{3,2,1,0:T(8,128)(2,1)S(1)}, u32[]{:S(2)}, u32[]{:S(2)}) collective-permute-start(bf16[2,3,128,256]{3,2,1,0:T(8,128)(2,1)S(1)} %get-tuple-element.82), channel_id=1, source_target_pairs={{0,16},{8,24},{16,0},{24,8},{1,17},{9,25},{17,1},{25,9},{2,18},{10... | collective-permute-start | bytes 1179656 | tf_op jit(solution)/shard_map/ppermute | solution.py:542
  52.7 11.1 %copy-start.5 = (f32[4]{0:T(128)S(1)}, f32[4]{0:T(128)}, u32[]{:S(2)}) copy-start(f32[4]{0:T(128)} %step_ref.1) | copy-start | bytes 52
  54.8 14.6 %collective-permute-start.17 = (bf16[2,512,256]{2,1,0:T(8,128)(2,1)S(1)}, bf16[2,512,256]{2,1,0:T(8,128)(2,1)S(1)}, u32[]{:S(2)}, u32[]{:S(2)}) collective-permute-start(bf16[2,512,256]{2,1,0:T(8,128)(2,1)S(1)} %get-tuple-element.80), channel_id=1, source_target_pairs={{0,8},{8,16},{16,24},{1,9},{9,17},{17,25},{2,10},{10,18},{18,26},{... | collective-permute-start | bytes 1572872 | tf_op jit(solution)/shard_map/ppermute | solution.py:590
  64.6 6.0 %copy-start = (bf16[512,4096]{1,0:T(8,128)(2,1)S(1)}, bf16[512,4096]{1,0:T(8,128)(2,1)}, u32[]{:S(2)}) copy-start(bf16[512,4096]{1,0:T(8,128)(2,1)} %w_ref.7) | copy-start | bytes 12582916
  64.6 6.0 %collective-permute-start.19 = (bf16[2,3,128,256]{3,2,1,0:T(8,128)(2,1)S(1)}, bf16[2,3,128,256]{3,2,1,0:T(8,128)(2,1)S(1)}, u32[]{:S(2)}, u32[]{:S(2)}) collective-permute-start(bf16[2,3,128,256]{3,2,1,0:T(8,128)(2,1)S(1)} %shard_map.112.net_ref), channel_id=1, source_target_pairs={{0,8},{8,0},{16,24},{24,16},{1,9},{9,1},{17,25},{25,17},{2,10},{10... | collective-permute-start | bytes 1179656 | tf_op jit(solution)/shard_map/ppermute | solution.py:542
  71.8 8.4 %collective-permute-start.21 = (bf16[64,2048]{1,0:T(8,128)(2,1)S(1)}, bf16[64,2048]{1,0:T(8,128)(2,1)S(1)}, u32[]{:S(2)}, u32[]{:S(2)}) collective-permute-start(bf16[64,2048]{1,0:T(8,128)(2,1)S(1)} %get-tuple-element.86), channel_id=1, source_target_pairs={{0,1},{2,0},{4,2},{6,4},{7,6},{5,7},{3,5},{1,3},{8,9},{10,8},{12,1... | collective-permute-start | bytes 786440 | tf_op jit(solution)/shard_map/ppermute | solution.py:55
  73.2 8.3 %collective-permute-start.20 = (bf16[64,2048]{1,0:T(8,128)(2,1)S(1)}, bf16[64,2048]{1,0:T(8,128)(2,1)S(1)}, u32[]{:S(2)}, u32[]{:S(2)}) collective-permute-start(bf16[64,2048]{1,0:T(8,128)(2,1)S(1)} %get-tuple-element.84), channel_id=1, source_target_pairs={{0,2},{2,4},{4,6},{6,7},{7,5},{5,3},{3,1},{1,0},{8,10},{10,12},{12... | collective-permute-start | bytes 786440 | tf_op jit(solution)/shard_map/ppermute | solution.py:55
  74.6 11.2 %collective-permute-start.25 = (bf16[64,2048]{1,0:T(8,128)(2,1)S(1)}, bf16[64,2048]{1,0:T(8,128)(2,1)S(1)}, u32[]{:S(2)}, u32[]{:S(2)}) collective-permute-start(bf16[64,2048]{1,0:T(8,128)(2,1)S(1)} %get-tuple-element.90), channel_id=1, source_target_pairs={{0,1},{2,0},{4,2},{6,4},{7,6},{5,7},{3,5},{1,3},{8,9},{10,8},{12,1... | collective-permute-start | bytes 786440 | tf_op jit(solution)/shard_map/ppermute | solution.py:55
  75.9 11.2 %collective-permute-start.24 = (bf16[64,2048]{1,0:T(8,128)(2,1)S(1)}, bf16[64,2048]{1,0:T(8,128)(2,1)S(1)}, u32[]{:S(2)}, u32[]{:S(2)}) collective-permute-start(bf16[64,2048]{1,0:T(8,128)(2,1)S(1)} %get-tuple-element.89), channel_id=1, source_target_pairs={{0,2},{2,4},{4,6},{6,7},{7,5},{5,3},{3,1},{1,0},{8,10},{10,12},{12... | collective-permute-start | bytes 786440 | tf_op jit(solution)/shard_map/ppermute | solution.py:55
  81.6 9.9 %collective-permute-start.23 = (bf16[64,2048]{1,0:T(8,128)(2,1)S(1)}, bf16[64,2048]{1,0:T(8,128)(2,1)S(1)}, u32[]{:S(2)}, u32[]{:S(2)}) collective-permute-start(bf16[64,2048]{1,0:T(8,128)(2,1)S(1)} %add_convert_fusion.10), channel_id=1, source_target_pairs={{0,1},{2,0},{4,2},{6,4},{7,6},{5,7},{3,5},{1,3},{8,9},{10,8},{12,1... | collective-permute-start | bytes 786440 | tf_op jit(solution)/shard_map/ppermute | solution.py:55
  82.9 9.8 %collective-permute-start.22 = (bf16[64,2048]{1,0:T(8,128)(2,1)S(1)}, bf16[64,2048]{1,0:T(8,128)(2,1)S(1)}, u32[]{:S(2)}, u32[]{:S(2)}) collective-permute-start(bf16[64,2048]{1,0:T(8,128)(2,1)S(1)} %add_convert_fusion.11), channel_id=1, source_target_pairs={{0,2},{2,4},{4,6},{6,7},{7,5},{5,3},{3,1},{1,0},{8,10},{10,12},{12... | collective-permute-start | bytes 786440 | tf_op jit(solution)/shard_map/ppermute | solution.py:55
  87.2 9.6 %collective-permute-start.27 = (bf16[64,2048]{1,0:T(8,128)(2,1)S(1)}, bf16[64,2048]{1,0:T(8,128)(2,1)S(1)}, u32[]{:S(2)}, u32[]{:S(2)}) collective-permute-start(bf16[64,2048]{1,0:T(8,128)(2,1)S(1)} %add_convert_fusion.8), channel_id=1, source_target_pairs={{0,1},{2,0},{4,2},{6,4},{7,6},{5,7},{3,5},{1,3},{8,9},{10,8},{12,1... | collective-permute-start | bytes 786440 | tf_op jit(solution)/shard_map/ppermute | solution.py:55
  88.5 9.8 %collective-permute-start.26 = (bf16[64,2048]{1,0:T(8,128)(2,1)S(1)}, bf16[64,2048]{1,0:T(8,128)(2,1)S(1)}, u32[]{:S(2)}, u32[]{:S(2)}) collective-permute-start(bf16[64,2048]{1,0:T(8,128)(2,1)S(1)} %add_convert_fusion.9), channel_id=1, source_target_pairs={{0,2},{2,4},{4,6},{6,7},{7,5},{5,3},{3,1},{1,0},{8,10},{10,12},{12... | collective-permute-start | bytes 786440 | tf_op jit(solution)/shard_map/ppermute | solution.py:55
  92.8 9.4 %collective-permute-start.31 = (bf16[64,2048]{1,0:T(8,128)(2,1)S(1)}, bf16[64,2048]{1,0:T(8,128)(2,1)S(1)}, u32[]{:S(2)}, u32[]{:S(2)}) collective-permute-start(bf16[64,2048]{1,0:T(8,128)(2,1)S(1)} %add_convert_fusion.4), channel_id=1, source_target_pairs={{0,1},{2,0},{4,2},{6,4},{7,6},{5,7},{3,5},{1,3},{8,9},{10,8},{12,1... | collective-permute-start | bytes 786440 | tf_op jit(solution)/shard_map/ppermute | solution.py:55
  94.2 9.8 %collective-permute-start.30 = (bf16[64,2048]{1,0:T(8,128)(2,1)S(1)}, bf16[64,2048]{1,0:T(8,128)(2,1)S(1)}, u32[]{:S(2)}, u32[]{:S(2)}) collective-permute-start(bf16[64,2048]{1,0:T(8,128)(2,1)S(1)} %add_convert_fusion.5), channel_id=1, source_target_pairs={{0,2},{2,4},{4,6},{6,7},{7,5},{5,3},{3,1},{1,0},{8,10},{10,12},{12... | collective-permute-start | bytes 786440 | tf_op jit(solution)/shard_map/ppermute | solution.py:55
  98.4 11.1 %collective-permute-start.28 = (bf16[64,2048]{1,0:T(8,128)(2,1)S(1)}, bf16[64,2048]{1,0:T(8,128)(2,1)S(1)}, u32[]{:S(2)}, u32[]{:S(2)}) collective-permute-start(bf16[64,2048]{1,0:T(8,128)(2,1)S(1)} %add_convert_fusion.7), channel_id=1, source_target_pairs={{0,2},{2,4},{4,6},{6,7},{7,5},{5,3},{3,1},{1,0},{8,10},{10,12},{12... | collective-permute-start | bytes 786440 | tf_op jit(solution)/shard_map/ppermute | solution.py:55
  98.7 10.9 %collective-permute-start.29 = (bf16[64,2048]{1,0:T(8,128)(2,1)S(1)}, bf16[64,2048]{1,0:T(8,128)(2,1)S(1)}, u32[]{:S(2)}, u32[]{:S(2)}) collective-permute-start(bf16[64,2048]{1,0:T(8,128)(2,1)S(1)} %add_convert_fusion.6), channel_id=1, source_target_pairs={{0,1},{2,0},{4,2},{6,4},{7,6},{5,7},{3,5},{1,3},{8,9},{10,8},{12,1... | collective-permute-start | bytes 786440 | tf_op jit(solution)/shard_map/ppermute | solution.py:55
  104.0 8.0 %collective-permute-start.32 = (bf16[64,2048]{1,0:T(8,128)(2,1)S(1)}, bf16[64,2048]{1,0:T(8,128)(2,1)S(1)}, u32[]{:S(2)}, u32[]{:S(2)}) collective-permute-start(bf16[64,2048]{1,0:T(8,128)(2,1)S(1)} %add_convert_fusion.3), channel_id=1, source_target_pairs={{0,2},{2,4},{4,6},{6,7},{7,5},{5,3},{3,1},{1,0},{8,10},{10,12},{12... | collective-permute-start | bytes 786440 | tf_op jit(solution)/shard_map/ppermute | solution.py:55
  104.3 7.9 %collective-permute-start.33 = (bf16[64,2048]{1,0:T(8,128)(2,1)S(1)}, bf16[64,2048]{1,0:T(8,128)(2,1)S(1)}, u32[]{:S(2)}, u32[]{:S(2)}) collective-permute-start(bf16[64,2048]{1,0:T(8,128)(2,1)S(1)} %add_convert_fusion.2), channel_id=1, source_target_pairs={{0,1},{2,0},{4,2},{6,4},{7,6},{5,7},{3,5},{1,3},{8,9},{10,8},{12,1... | collective-permute-start | bytes 786440 | tf_op jit(solution)/shard_map/ppermute | solution.py:55

commit v13 on v12

--- a/solution.py
+++ b/solution.py
@@ -376,7 +376,7 @@
 
 def attend_earlier(summed, stats, query, sources, other, size, after=()):
     rows = query.shape[1]
-    heads = sources[0].shape[2] // size
+    heads = next(iter(sources.values())).shape[2] // size
 
     def body(sum_ref, stats_ref, q_ref, *refs):
         out_ref = refs[-1]
@@ -396,11 +396,8 @@
                     total = stats_ref[1, where, lane] * old + total * new
                     out_ref[where, lane] = (sum_ref[where, lane] * old + result * new) / total
 
-        if len(sources) == 1:
-            pl.when(place > 0)(lambda: add(refs[0]))
-        else:
-            pl.when((place > 0) & (place % 2 == 0))(lambda: add(refs[0]))
-            pl.when(place % 2 == 1)(lambda: add(refs[1]))
+        for core, ref in zip(sources, refs):
+            pl.when((place > 0) & (place % 2 == core))(functools.partial(add, ref))
 
     return call(
         body,
@@ -409,7 +406,7 @@
         jax.ShapeDtypeStruct(summed.shape, F32),
         cost=cost(3 * heads * size * rows * rows, 8 * rows * heads * size, heads * rows * rows),
         aliases={0: 0},
-    )(summed, stats, query, *sources, *after)
+    )(summed, stats, query, *sources.values(), *after)
 
 
 def fast_apply(query, gate, upper, down):
@@ -586,12 +583,16 @@
             travel = travel.astype(BF16)
         received.append(swap(travel, 1 << bit))
     attended, stats = attend_own(query, kv, head_size)
-    near, _ = lax.optimization_barrier((near, attended))
-    behind_far = lax.ppermute(near, "tok", [(index, index + 1) for index in range(tok_count - 1)])
-    attended = attend_earlier(attended, stats, query, (behind, beside), False, head_size)
+    early, _ = lax.optimization_barrier((near, grads))
+    late, _ = lax.optimization_barrier((near, attended))
+    beside_far = lax.ppermute(early, "tok", [(index, index + 1) for index in range(0, tok_count, 2)])
+    behind_far = lax.ppermute(late, "tok", [(index, index + 1) for index in range(1, tok_count - 1, 2)])
+    nearer = {0: behind, 1: beside}
+    attended = attend_earlier(attended, stats, query, nearer, False, head_size)
+    attended = attend_earlier(attended, stats, query, {1: beside_far}, True, head_size)
     mine = renew(grads, received, head_step, *nets, (attended,))
     near = combine_near(query, attended, mine)
-    attended = attend_earlier(attended, stats, query, (behind_far,), True, head_size, (near,))
+    attended = attend_earlier(attended, stats, query, {0: behind_far}, True, head_size, (near,))
     return ring_reduce(query, attended, swap(mine, 1), near, w_out)
 
 

time: 113 us -> 114 us (level)
  starting transfers between devices: 31.2 us -> 36.7 us
  waiting for transfers between devices: 52.1 us -> 47.4 us
    ppermute x4, waiting for transfers between devices: 4.61 us -> 0.16 us  [swap(): lax.ppermute(value, 'tok', [(index, index ^ bit) for index in range(count)])]
    ppermute x1 -> x2, starting transfers between devices: 1.92 us -> 6 us  [the longest x1 4.71 us: shards(): lax.ppermute(late, 'tok', [(index, index + 1) for index in range(1, tok_c...]
    ppermute x28, waiting for transfers between devices: 42.4 us -> 44.7 us  [ring_send(): lax.ppermute(value, 'head', [(order[i], order[(i + step) % count]) for i...]
    ppermute x4, starting transfers between devices: 4.43 us -> 5.85 us  [swap(): lax.ppermute(value, 'tok', [(index, index ^ bit) for index in range(count)])]
    ppermute x1 -> x2, waiting for transfers between devices: 3.89 us -> 2.6 us  [the longest x1 2.6 us: shards(): lax.ppermute(late, 'tok', [(index, index + 1) for index in range(1, tok_c...]
    ppermute x1, waiting for transfers between devices: 1.21 us -> 0.01 us  [shards(): lax.ppermute(far, 'tok', [(index, index + 1) for index in range(1, tok_co...]
    pallas_call x2 -> x3, Pallas kernels: 2.43 us -> 2.65 us  [attend_earlier(): call(body, [WHOLE] * (3 + len(sources)) + [AFTER] * len(after), WHOLE, ja...]
  transfers between devices with their start and end apart: 34 -> 35, of which waited for: 23 -> 22; matrix products, arithmetic and copies ran while one was open for 1% -> 1% of each run, Pallas kernels for 22% -> 22%
where the time goes in v13:
time: 114 us
  waiting for transfers between devices  47.4 us (42%)
  starting transfers between devices  36.7 us (32%)
  Pallas kernels  28.1 us (25%)
  other arithmetic  1.58 us (1%)
    ppermute x28, waiting for transfers between devices, ring_send(): lax.ppermute(value, 'head', [(order[i], order[(i + step) % count]) for i...  44.7 us
    ppermute x28, starting transfers between devices, ring_send(): lax.ppermute(value, 'head', [(order[i], order[(i + step) % count]) for i...  21.7 us
    pallas_call x4, Pallas kernels, accumulate(): call(body, [WHOLE] * len(args), WHOLE, jax.ShapeDtypeStruct((parts, total...  6.72 us
    ppermute x4, starting transfers between devices, swap(): lax.ppermute(value, 'tok', [(index, index ^ bit) for index in range(count)])  5.85 us
    pallas_call x4, Pallas kernels, partial_out(): call(body, [WHOLE] * 5 + [AFTER] * len(after), [WHOLE] * (2 * count), [ja...  5.17 us
    pallas_call x1, Pallas kernels, load(): call(body, [IN_HBM] * count, [WHOLE] * count, [jax.ShapeDtypeStruct(array...  4.78 us
    ppermute x1, starting transfers between devices, shards(): lax.ppermute(late, 'tok', [(index, index + 1) for index in range(1, tok_c...  4.71 us
    ppermute x1, starting transfers between devices, shards(): lax.ppermute(far, 'tok', [(index, index + 1) for index in range(1, tok_co...  3.07 us
  transfers between devices with their start and end apart: 35, of which 22 were waited for; matrix products, arithmetic and copies ran while one was open for 1% of the time, Pallas kernels for 22%

profile of v13, /device:TPU:1, one launch (start us, length us, event | category | flops | bytes accessed | tf_op | source)
XLA Modules:
  0.0 114.1 jit_solution(6270562391837667796)
XLA Ops:
  0.0 1.0 shard_map.100
  1.1 2.1 %collective-permute-start.4 = (bf16[256,512]{1,0:T(8,128)(2,1)S(1)}, bf16[256,512]{1,0:T(8,128)(2,1)S(1)}, u32[]{:S(2)}, u32[]{:S(2)}) collective-permute-start(bf16[256,512]{1,0:T(8,128)(2,1)S(1)} %get-tuple-element.63.refs_3_), channel_id=1, source_target_pairs={{0,1},{2,0},{4,2},{6,4},{7,6},{5,7},{3,5},{1,3},{8,9},{10,8},{12,1... | collective-permute-start | bytes 786440 | tf_op jit(solution)/shard_map/ppermute | solution.py:55
  3.3 1.4 %collective-permute-start.3 = (bf16[256,512]{1,0:T(8,128)(2,1)S(1)}, bf16[256,512]{1,0:T(8,128)(2,1)S(1)}, u32[]{:S(2)}, u32[]{:S(2)}) collective-permute-start(bf16[256,512]{1,0:T(8,128)(2,1)S(1)} %get-tuple-element.63.refs_3_), channel_id=1, source_target_pairs={{0,2},{2,4},{4,6},{6,7},{7,5},{5,3},{3,1},{1,0},{8,10},{10,12},{12... | collective-permute-start | bytes 786440 | tf_op jit(solution)/shard_map/ppermute | solution.py:55
  4.8 4.8 %shard_map.101 = (bf16[4096,512]{1,0:T(8,128)(2,1)S(1)}, bf16[4096,512]{1,0:T(8,128)(2,1)S(1)}, bf16[4096,512]{1,0:T(8,128)(2,1)S(1)}) custom-call(bf16[4096,512]{1,0:T(8,128)(2,1)} %refs_0_.1, bf16[4096,512]{1,0:T(8,128)(2,1)} %refs_1_.1, bf16[4096,512]{1,0:T(8,128)(2,1)} %refs_2_.1), custom_call_target="tpu_custom_call" | custom-call | bytes 25165824 | tf_op jit(solution)/shard_map/pallas_call | solution.py:111
  9.6 1.4 %collective-permute-start.8 = (bf16[256,512]{1,0:T(8,128)(2,1)S(1)}, bf16[256,512]{1,0:T(8,128)(2,1)S(1)}, u32[]{:S(2)}, u32[]{:S(2)}) collective-permute-start(bf16[256,512]{1,0:T(8,128)(2,1)S(1)} %collective-permute-done.4.refs_5_), channel_id=1, source_target_pairs={{0,1},{2,0},{4,2},{6,4},{7,6},{5,7},{3,5},{1,3},{8,9},{10,8},{12,1... | collective-permute-start | bytes 786440 | tf_op jit(solution)/shard_map/ppermute | solution.py:55
  11.1 2.4 %collective-permute-start.5 = (f32[4,512]{1,0:T(4,128)S(1)}, f32[4,512]{1,0:T(4,128)S(1)}, u32[]{:S(2)}, u32[]{:S(2)}) collective-permute-start(f32[4,512]{1,0:T(4,128)S(1)} %bitcast.1), channel_id=1, source_target_pairs={{0,8},{8,0},{16,24},{24,16},{1,9},{9,1},{17,25},{25,17},{2,10},{10... | collective-permute-start | bytes 24584 | tf_op jit(solution)/shard_map/ppermute | solution.py:539
  13.5 2.2 %collective-permute-done.3.refs_4_ = bf16[256,512]{1,0:T(8,128)(2,1)S(1)} collective-permute-done((bf16[256,512]{1,0:T(8,128)(2,1)S(1)}, bf16[256,512]{1,0:T(8,128)(2,1)S(1)}, u32[]{:S(2)}, u32[]{:S(2)}) %collective-permute-start.3) | collective-permute-done | bytes 262176 | tf_op jit(solution)/shard_map/ppermute | solution.py:55
  15.6 0.5 collective-permute-start.13
  16.1 1.0 collective-permute-start.11
  17.1 2.6 %shard_map.102.refs_7_ = f32[3,512,512]{2,1,0:T(8,128)S(1)} custom-call(bf16[256,512]{1,0:T(8,128)(2,1)S(1)} %get-tuple-element.60.refs_0_, bf16[256,512]{1,0:T(8,128)(2,1)S(1)} %collective-permute-done.refs_1_, bf16[256,512]{1,0:T(8,128)(2,1)S(1)} %collective-permute-done.2.refs_2_, bf16[256,512]{1,0:T(8,128)(2,1)S(1)} %get-tuple-element.63.refs_3_, ...), custom_call_target="tpu_custom_call" | custom-call | flops 2415919104 | bytes 12582912 | tf_op jit(solution)/shard_map/pallas_call | solution.py:180
  19.7 0.8 collective-permute-done.8.refs_3_
  20.5 0.7 collective-permute-done.1.refs_0_
  21.2 1.3 %collective-permute-start.9 = (bf16[256,512]{1,0:T(8,128)(2,1)S(1)}, bf16[256,512]{1,0:T(8,128)(2,1)S(1)}, u32[]{:S(2)}, u32[]{:S(2)}) collective-permute-start(bf16[256,512]{1,0:T(8,128)(2,1)S(1)} %collective-permute-done.8.refs_3_), channel_id=1, source_target_pairs={{0,1},{2,0},{4,2},{6,4},{7,6},{5,7},{3,5},{1,3},{8,9},{10,8},{12,1... | collective-permute-start | bytes 786440 | tf_op jit(solution)/shard_map/ppermute | solution.py:55
  22.7 4.2 %collective-permute-done.13.refs_2_ = bf16[256,512]{1,0:T(8,128)(2,1)S(1)} collective-permute-done((bf16[256,512]{1,0:T(8,128)(2,1)S(1)}, bf16[256,512]{1,0:T(8,128)(2,1)S(1)}, u32[]{:S(2)}, u32[]{:S(2)}) %collective-permute-start.13) | collective-permute-done | bytes 262176 | tf_op jit(solution)/shard_map/ppermute | solution.py:55
  26.9 0.5 collective-permute-start.14
  27.3 1.0 collective-permute-start.12
  28.3 3.3 %collective-permute-done.9.refs_3_ = bf16[256,512]{1,0:T(8,128)(2,1)S(1)} collective-permute-done((bf16[256,512]{1,0:T(8,128)(2,1)S(1)}, bf16[256,512]{1,0:T(8,128)(2,1)S(1)}, u32[]{:S(2)}, u32[]{:S(2)}) %collective-permute-start.9) | collective-permute-done | bytes 262176 | tf_op jit(solution)/shard_map/ppermute | solution.py:55
  31.6 1.1 collective-permute-start.10
  32.7 0.3 collective-permute-start.7
  33.1 1.8 %shard_map.103.refs_7_ = f32[3,512,512]{2,1,0:T(8,128)S(1)} custom-call(bf16[256,512]{1,0:T(8,128)(2,1)S(1)} %collective-permute-done.1.refs_0_, bf16[256,512]{1,0:T(8,128)(2,1)S(1)} %collective-permute-done.11.refs_1_, bf16[256,512]{1,0:T(8,128)(2,1)S(1)} %collective-permute-done.13.refs_2_, ...), custom_call_target="tpu_custom_call", output_to_operand_aliasing={{}: (7, {})} | custom-call | flops 1610612736 | bytes 10485760 | tf_op jit(solution)/shard_map/pallas_call | solution.py:180
  34.9 3.2 %collective-permute-done.14.refs_2_ = bf16[256,512]{1,0:T(8,128)(2,1)S(1)} collective-permute-done((bf16[256,512]{1,0:T(8,128)(2,1)S(1)}, bf16[256,512]{1,0:T(8,128)(2,1)S(1)}, u32[]{:S(2)}, u32[]{:S(2)}) %collective-permute-start.14) | collective-permute-done | bytes 262176 | tf_op jit(solution)/shard_map/ppermute | solution.py:55
  38.1 1.8 %shard_map.104.refs_3_.refs_2_ = f32[3,512,512]{2,1,0:T(8,128)S(1)} custom-call(bf16[256,512]{1,0:T(8,128)(2,1)S(1)} %collective-permute-done.6.refs_0_, bf16[256,512]{1,0:T(8,128)(2,1)S(1)} %collective-permute-done.12.refs_1_, bf16[256,512]{1,0:T(8,128)(2,1)S(1)} %collective-permute-done.14.refs_2_, ...), custom_call_target="tpu_custom_call", output_to_operand_aliasing={{}: (7, {})} | custom-call | flops 1610612736 | bytes 10485760 | tf_op jit(solution)/shard_map/pallas_call | solution.py:180
  39.9 2.9 %collective-permute-done.10.refs_1_.piece_ref = bf16[256,512]{1,0:T(8,128)(2,1)S(1)} collective-permute-done((bf16[256,512]{1,0:T(8,128)(2,1)S(1)}, bf16[256,512]{1,0:T(8,128)(2,1)S(1)}, u32[]{:S(2)}, u32[]{:S(2)}) %collective-permute-start.10) | collective-permute-done | bytes 262176 | tf_op jit(solution)/shard_map/ppermute | solution.py:55
  42.8 0.5 shard_map.106
  43.3 0.4 collective-permute-done.7.refs_0_.piece_ref
  43.7 0.5 shard_map.107
  44.2 1.9 %collective-permute-start.16 = (bf16[2,512,256]{2,1,0:T(8,128)(2,1)S(1)}, bf16[2,512,256]{2,1,0:T(8,128)(2,1)S(1)}, u32[]{:S(2)}, u32[]{:S(2)}) collective-permute-start(bf16[2,512,256]{2,1,0:T(8,128)(2,1)S(1)} %get-tuple-element.79), channel_id=1, source_target_pairs={{0,8},{8,0},{16,24},{24,16},{1,9},{9,1},{17,25},{25,17},{2,10},{10... | collective-permute-start | bytes 1572872 | tf_op jit(solution)/shard_map/ppermute | solution.py:539
  46.2 3.1 %collective-permute-start.15 = (bf16[2,512,256]{2,1,0:T(8,128)(2,1)S(1)}, bf16[2,512,256]{2,1,0:T(8,128)(2,1)S(1)}, u32[]{:S(2)}, u32[]{:S(2)}) collective-permute-start(bf16[2,512,256]{2,1,0:T(8,128)(2,1)S(1)} %get-tuple-element.79), channel_id=1, source_target_pairs={{8,16},{9,17},{10,18},{11,19},{12,20},{13,21},{14,22},{15,23}} | collective-permute-start | bytes 1572872 | tf_op jit(solution)/shard_map/ppermute | solution.py:573
  49.3 1.4 %shard_map.110.rest_0_ = f32[2,3,128,256]{3,2,1,0:T(8,128)S(1)} custom-call(bf16[2,512,512]{2,1,0:T(8,128)(2,1)S(1)} %get-tuple-element.76.kv_ref, f32[4,512]{1,0:T(4,128)S(1)} %bitcast.2, f32[4,128,256]{2,1,0:T(8,128)S(1)} %copy-done.1, f32[4,128,256]{2,1,0:T(8,128)S(1)} %copy-done.2, f32[4,256,128]{2,1,0:T(8,128)S(1)} %copy-done.3), custom_call_target="tpu_custom_call" | custom-call | flops 402653184 | bytes 1572864 | tf_op jit(solution)/shard_map/pallas_call | solution.py:272
  50.7 1.4 %shard_map.111 = (f32[2,3,128,256]{3,2,1,0:T(8,128)S(1)}, bf16[2,3,128,256]{3,2,1,0:T(8,128)(2,1)S(1)}) custom-call(bf16[2,512,256]{2,1,0:T(8,128)(2,1)S(1)} %collective-permute-done.16.refs_1_.kv_ref, f32[4,512]{1,0:T(4,128)S(1)} %collective-permute-done.5.rate_ref, f32[4,128,256]{2,1,0:T(8,128)S(1)} %copy-done.1, f32[4,128,256]{2,1,0:T(8,128)S(1)} %copy-done.2, ...), custom_call_target="tpu_custom_call" | custom-call | flops 402653184 | bytes 1572864 | tf_op jit(solution)/shard_map/pallas_call | solution.py:272
  52.2 1.3 %collective-permute-start.17 = (bf16[2,512,256]{2,1,0:T(8,128)(2,1)S(1)}, bf16[2,512,256]{2,1,0:T(8,128)(2,1)S(1)}, u32[]{:S(2)}, u32[]{:S(2)}) collective-permute-start(bf16[2,512,256]{2,1,0:T(8,128)(2,1)S(1)} %get-tuple-element.83), channel_id=1, source_target_pairs={{0,8},{16,24},{1,9},{17,25},{2,10},{18,26},{3,11},{19,27},{4,12},{... | collective-permute-start | bytes 1572872 | tf_op jit(solution)/shard_map/ppermute | solution.py:588
  53.5 0.4 shard_map.105.q_ref
  54.0 2.1 %shard_map.108 = (f32[512,512]{1,0:T(8,128)S(1)}, f32[2,512,512]{2,1,0:T(8,128)S(1)}) custom-call(bf16[1,512,512]{2,1,0:T(8,128)(2,1)S(1)} %shard_map.105.q_ref, bf16[2,512,512]{2,1,0:T(8,128)(2,1)S(1)} %get-tuple-element.76.kv_ref), custom_call_target="tpu_custom_call" | custom-call | flops 402653184 | bytes 2097152 | tf_op jit(solution)/shard_map/pallas_call | solution.py:365
  56.1 4.7 %collective-permute-start.18 = (bf16[2,512,256]{2,1,0:T(8,128)(2,1)S(1)}, bf16[2,512,256]{2,1,0:T(8,128)(2,1)S(1)}, u32[]{:S(2)}, u32[]{:S(2)}) collective-permute-start(bf16[2,512,256]{2,1,0:T(8,128)(2,1)S(1)} %get-tuple-element.83), channel_id=1, source_target_pairs={{8,16},{9,17},{10,18},{11,19},{12,20},{13,21},{14,22},{15,23}} | collective-permute-start | bytes 1572872 | tf_op jit(solution)/shard_map/ppermute | solution.py:589
  60.8 1.4 %shard_map.109.sum_ref = f32[512,512]{1,0:T(8,128)S(1)} custom-call(f32[512,512]{1,0:T(8,128)S(1)} %get-tuple-element.77.sum_ref, f32[2,512,512]{2,1,0:T(8,128)S(1)} %get-tuple-element.78.stats_ref, bf16[1,512,512]{2,1,0:T(8,128)(2,1)S(1)} %shard_map.105.q_ref, ...), custom_call_target="tpu_custom_call", output_to_operand_aliasing={{}: (0, {})} | custom-call | flops 201326592 | bytes 1048576 | tf_op jit(solution)/shard_map/pallas_call | solution.py:402
  62.3 1.2 %shard_map.112.rest_1_.attended_ref.sum_ref = f32[512,512]{1,0:T(8,128)S(1)} custom-call(f32[512,512]{1,0:T(8,128)S(1)} %shard_map.109.sum_ref, f32[2,512,512]{2,1,0:T(8,128)S(1)} %get-tuple-element.78.stats_ref, bf16[1,512,512]{2,1,0:T(8,128)(2,1)S(1)} %shard_map.105.q_ref, ...), custom_call_target="tpu_custom_call", output_to_operand_aliasing={{}: (0, {})} | custom-call | flops 201326592 | bytes 1048576 | tf_op jit(solution)/shard_map/pallas_call | solution.py:402
  63.6 0.8 shard_map.113.net_ref
  64.5 1.5 %collective-permute-start.20 = (bf16[2,3,128,256]{3,2,1,0:T(8,128)(2,1)S(1)}, bf16[2,3,128,256]{3,2,1,0:T(8,128)(2,1)S(1)}, u32[]{:S(2)}, u32[]{:S(2)}) collective-permute-start(bf16[2,3,128,256]{3,2,1,0:T(8,128)(2,1)S(1)} %shard_map.113.net_ref), channel_id=1, source_target_pairs={{0,8},{8,0},{16,24},{24,16},{1,9},{9,1},{17,25},{25,17},{2,10},{10... | collective-permute-start | bytes 1179656 | tf_op jit(solution)/shard_map/ppermute | solution.py:539
  66.0 0.8 shard_map.114.refs_1_.near_ref
  66.8 2.6 %collective-permute-done.18.refs_0_ = bf16[2,512,256]{2,1,0:T(8,128)(2,1)S(1)} collective-permute-done((bf16[2,512,256]{2,1,0:T(8,128)(2,1)S(1)}, bf16[2,512,256]{2,1,0:T(8,128)(2,1)S(1)}, u32[]{:S(2)}, u32[]{:S(2)}) %collective-permute-start.18) | collective-permute-done | bytes 524320 | tf_op jit(solution)/shard_map/ppermute | solution.py:589
  69.4 1.2 %shard_map.117 = (bf16[64,2048]{1,0:T(8,128)(2,1)S(1)}, bf16[64,2048]{1,0:T(8,128)(2,1)S(1)}) custom-call(bf16[1,512,512]{2,1,0:T(8,128)(2,1)S(1)} %shard_map.105.q_ref, f32[512,512]{1,0:T(8,128)S(1)} %shard_map.115.attended_ref, bf16[2,3,128,256]{3,2,1,0:T(8,128)(2,1)S(1)} %collective-permute-done.20.net_ref, ...), custom_call_target="tpu_custom_call" | custom-call | flops 268435456 | bytes 4718592 | tf_op jit(solution)/shard_map/pallas_call | solution.py:478
  70.6 1.3 %collective-permute-start.22 = (bf16[64,2048]{1,0:T(8,128)(2,1)S(1)}, bf16[64,2048]{1,0:T(8,128)(2,1)S(1)}, u32[]{:S(2)}, u32[]{:S(2)}) collective-permute-start(bf16[64,2048]{1,0:T(8,128)(2,1)S(1)} %get-tuple-element.88), channel_id=1, source_target_pairs={{0,1},{2,0},{4,2},{6,4},{7,6},{5,7},{3,5},{1,3},{8,9},{10,8},{12,1... | collective-permute-start | bytes 786440 | tf_op jit(solution)/shard_map/ppermute | solution.py:55
  72.1 1.2 %shard_map.116 = (bf16[64,2048]{1,0:T(8,128)(2,1)S(1)}, bf16[64,2048]{1,0:T(8,128)(2,1)S(1)}, bf16[64,2048]{1,0:T(8,128)(2,1)S(1)}, bf16[64,2048]{1,0:T(8,128)(2,1)S(1)}) custom-call(bf16[1,512,512]{2,1,0:T(8,128)(2,1)S(1)} %shard_map.105.q_ref, f32[512,512]{1,0:T(8,128)S(1)} %shard_map.115.attended_ref, ...), custom_call_target="tpu_custom_call" | custom-call | flops 536870912 | bytes 5242880 | tf_op jit(solution)/shard_map/pallas_call | solution.py:478
  73.4 1.3 %collective-permute-start.26 = (bf16[64,2048]{1,0:T(8,128)(2,1)S(1)}, bf16[64,2048]{1,0:T(8,128)(2,1)S(1)}, u32[]{:S(2)}, u32[]{:S(2)}) collective-permute-start(bf16[64,2048]{1,0:T(8,128)(2,1)S(1)} %get-tuple-element.92), channel_id=1, source_target_pairs={{0,1},{2,0},{4,2},{6,4},{7,6},{5,7},{3,5},{1,3},{8,9},{10,8},{12,1... | collective-permute-start | bytes 786440 | tf_op jit(solution)/shard_map/ppermute | solution.py:55
  74.9 4.1 %collective-permute-done.22.refs_1_ = bf16[64,2048]{1,0:T(8,128)(2,1)S(1)} collective-permute-done((bf16[64,2048]{1,0:T(8,128)(2,1)S(1)}, bf16[64,2048]{1,0:T(8,128)(2,1)S(1)}, u32[]{:S(2)}, u32[]{:S(2)}) %collective-permute-start.22) | collective-permute-done | bytes 262176 | tf_op jit(solution)/shard_map/ppermute | solution.py:55
  79.0 1.2 %collective-permute-done.21.refs_0_ = bf16[64,2048]{1,0:T(8,128)(2,1)S(1)} collective-permute-done((bf16[64,2048]{1,0:T(8,128)(2,1)S(1)}, bf16[64,2048]{1,0:T(8,128)(2,1)S(1)}, u32[]{:S(2)}, u32[]{:S(2)}) %collective-permute-start.21) | collective-permute-done | bytes 262176 | tf_op jit(solution)/shard_map/ppermute | solution.py:55
  80.3 1.3 %collective-permute-start.24 = (bf16[64,2048]{1,0:T(8,128)(2,1)S(1)}, bf16[64,2048]{1,0:T(8,128)(2,1)S(1)}, u32[]{:S(2)}, u32[]{:S(2)}) collective-permute-start(bf16[64,2048]{1,0:T(8,128)(2,1)S(1)} %add_convert_fusion.10), channel_id=1, source_target_pairs={{0,1},{2,0},{4,2},{6,4},{7,6},{5,7},{3,5},{1,3},{8,9},{10,8},{12,1... | collective-permute-start | bytes 786440 | tf_op jit(solution)/shard_map/ppermute | solution.py:55
  81.8 1.2 %shard_map.119 = (bf16[64,2048]{1,0:T(8,128)(2,1)S(1)}, bf16[64,2048]{1,0:T(8,128)(2,1)S(1)}, bf16[64,2048]{1,0:T(8,128)(2,1)S(1)}, bf16[64,2048]{1,0:T(8,128)(2,1)S(1)}) custom-call(bf16[1,512,512]{2,1,0:T(8,128)(2,1)S(1)} %shard_map.105.q_ref, f32[512,512]{1,0:T(8,128)S(1)} %shard_map.115.attended_ref, ...), custom_call_target="tpu_custom_call" | custom-call | flops 536870912 | bytes 5242880 | tf_op jit(solution)/shard_map/pallas_call | solution.py:478
  83.0 1.5 %collective-permute-done.26 = bf16[64,2048]{1,0:T(8,128)(2,1)S(1)} collective-permute-done((bf16[64,2048]{1,0:T(8,128)(2,1)S(1)}, bf16[64,2048]{1,0:T(8,128)(2,1)S(1)}, u32[]{:S(2)}, u32[]{:S(2)}) %collective-permute-start.26) | collective-permute-done | bytes 262176 | tf_op jit(solution)/shard_map/ppermute | solution.py:55
  84.6 1.2 %collective-permute-done.25 = bf16[64,2048]{1,0:T(8,128)(2,1)S(1)} collective-permute-done((bf16[64,2048]{1,0:T(8,128)(2,1)S(1)}, bf16[64,2048]{1,0:T(8,128)(2,1)S(1)}, u32[]{:S(2)}, u32[]{:S(2)}) %collective-permute-start.25) | collective-permute-done | bytes 262176 | tf_op jit(solution)/shard_map/ppermute | solution.py:55
  85.9 1.3 %collective-permute-start.28 = (bf16[64,2048]{1,0:T(8,128)(2,1)S(1)}, bf16[64,2048]{1,0:T(8,128)(2,1)S(1)}, u32[]{:S(2)}, u32[]{:S(2)}) collective-permute-start(bf16[64,2048]{1,0:T(8,128)(2,1)S(1)} %add_convert_fusion.8), channel_id=1, source_target_pairs={{0,1},{2,0},{4,2},{6,4},{7,6},{5,7},{3,5},{1,3},{8,9},{10,8},{12,1... | collective-permute-start | bytes 786440 | tf_op jit(solution)/shard_map/ppermute | solution.py:55
  87.4 2.8 %collective-permute-done.24.refs_1_ = bf16[64,2048]{1,0:T(8,128)(2,1)S(1)} collective-permute-done((bf16[64,2048]{1,0:T(8,128)(2,1)S(1)}, bf16[64,2048]{1,0:T(8,128)(2,1)S(1)}, u32[]{:S(2)}, u32[]{:S(2)}) %collective-permute-start.24) | collective-permute-done | bytes 262176 | tf_op jit(solution)/shard_map/ppermute | solution.py:55
  90.3 1.2 %collective-permute-done.23.refs_0_ = bf16[64,2048]{1,0:T(8,128)(2,1)S(1)} collective-permute-done((bf16[64,2048]{1,0:T(8,128)(2,1)S(1)}, bf16[64,2048]{1,0:T(8,128)(2,1)S(1)}, u32[]{:S(2)}, u32[]{:S(2)}) %collective-permute-start.23) | collective-permute-done | bytes 262176 | tf_op jit(solution)/shard_map/ppermute | solution.py:55
  91.5 1.3 %collective-permute-start.32 = (bf16[64,2048]{1,0:T(8,128)(2,1)S(1)}, bf16[64,2048]{1,0:T(8,128)(2,1)S(1)}, u32[]{:S(2)}, u32[]{:S(2)}) collective-permute-start(bf16[64,2048]{1,0:T(8,128)(2,1)S(1)} %add_convert_fusion.4), channel_id=1, source_target_pairs={{0,1},{2,0},{4,2},{6,4},{7,6},{5,7},{3,5},{1,3},{8,9},{10,8},{12,1... | collective-permute-start | bytes 786440 | tf_op jit(solution)/shard_map/ppermute | solution.py:55
  93.0 1.5 %shard_map.118 = (bf16[64,2048]{1,0:T(8,128)(2,1)S(1)}, bf16[64,2048]{1,0:T(8,128)(2,1)S(1)}, bf16[64,2048]{1,0:T(8,128)(2,1)S(1)}, bf16[64,2048]{1,0:T(8,128)(2...) custom-call(bf16[1,512,512]{2,1,0:T(8,128)(2,1)S(1)} %shard_map.105.q_ref, ...), custom_call_target="tpu_custom_call" | custom-call | flops 805306368 | bytes 5767168 | tf_op jit(solution)/shard_map/pallas_call | solution.py:478
  94.6 1.3 %collective-permute-done.28 = bf16[64,2048]{1,0:T(8,128)(2,1)S(1)} collective-permute-done((bf16[64,2048]{1,0:T(8,128)(2,1)S(1)}, bf16[64,2048]{1,0:T(8,128)(2,1)S(1)}, u32[]{:S(2)}, u32[]{:S(2)}) %collective-permute-start.28) | collective-permute-done | bytes 262176 | tf_op jit(solution)/shard_map/ppermute | solution.py:55
  95.9 1.2 %collective-permute-done.27 = bf16[64,2048]{1,0:T(8,128)(2,1)S(1)} collective-permute-done((bf16[64,2048]{1,0:T(8,128)(2,1)S(1)}, bf16[64,2048]{1,0:T(8,128)(2,1)S(1)}, u32[]{:S(2)}, u32[]{:S(2)}) %collective-permute-start.27) | collective-permute-done | bytes 262176 | tf_op jit(solution)/shard_map/ppermute | solution.py:55
  97.4 1.3 %collective-permute-start.30 = (bf16[64,2048]{1,0:T(8,128)(2,1)S(1)}, bf16[64,2048]{1,0:T(8,128)(2,1)S(1)}, u32[]{:S(2)}, u32[]{:S(2)}) collective-permute-start(bf16[64,2048]{1,0:T(8,128)(2,1)S(1)} %add_convert_fusion.6), channel_id=1, source_target_pairs={{0,1},{2,0},{4,2},{6,4},{7,6},{5,7},{3,5},{1,3},{8,9},{10,8},{12,1... | collective-permute-start | bytes 786440 | tf_op jit(solution)/shard_map/ppermute | solution.py:55
  98.7 2.3 %collective-permute-done.32 = bf16[64,2048]{1,0:T(8,128)(2,1)S(1)} collective-permute-done((bf16[64,2048]{1,0:T(8,128)(2,1)S(1)}, bf16[64,2048]{1,0:T(8,128)(2,1)S(1)}, u32[]{:S(2)}, u32[]{:S(2)}) %collective-permute-start.32) | collective-permute-done | bytes 262176 | tf_op jit(solution)/shard_map/ppermute | solution.py:55
  101.0 1.7 %collective-permute-done.31 = bf16[64,2048]{1,0:T(8,128)(2,1)S(1)} collective-permute-done((bf16[64,2048]{1,0:T(8,128)(2,1)S(1)}, bf16[64,2048]{1,0:T(8,128)(2,1)S(1)}, u32[]{:S(2)}, u32[]{:S(2)}) %collective-permute-start.31) | collective-permute-done | bytes 262176 | tf_op jit(solution)/shard_map/ppermute | solution.py:55
  103.0 1.3 %collective-permute-start.34 = (bf16[64,2048]{1,0:T(8,128)(2,1)S(1)}, bf16[64,2048]{1,0:T(8,128)(2,1)S(1)}, u32[]{:S(2)}, u32[]{:S(2)}) collective-permute-start(bf16[64,2048]{1,0:T(8,128)(2,1)S(1)} %add_convert_fusion.2), channel_id=1, source_target_pairs={{0,1},{2,0},{4,2},{6,4},{7,6},{5,7},{3,5},{1,3},{8,9},{10,8},{12,1... | collective-permute-start | bytes 786440 | tf_op jit(solution)/shard_map/ppermute | solution.py:55
  104.3 4.0 %collective-permute-done.29.refs_2_ = bf16[64,2048]{1,0:T(8,128)(2,1)S(1)} collective-permute-done((bf16[64,2048]{1,0:T(8,128)(2,1)S(1)}, bf16[64,2048]{1,0:T(8,128)(2,1)S(1)}, u32[]{:S(2)}, u32[]{:S(2)}) %collective-permute-start.29) | collective-permute-done | bytes 262176 | tf_op jit(solution)/shard_map/ppermute | solution.py:55
  108.4 4.7 %collective-permute-done.33 = bf16[64,2048]{1,0:T(8,128)(2,1)S(1)} collective-permute-done((bf16[64,2048]{1,0:T(8,128)(2,1)S(1)}, bf16[64,2048]{1,0:T(8,128)(2,1)S(1)}, u32[]{:S(2)}, u32[]{:S(2)}) %collective-permute-start.33) | collective-permute-done | bytes 262176 | tf_op jit(solution)/shard_map/ppermute | solution.py:55
  113.3 0.8 pad_maximum_fusion
  (52 shorter events, 3.0 us)
Async XLA Ops:
  1.1 8.5 %collective-permute-start.4 = (bf16[256,512]{1,0:T(8,128)(2,1)S(1)}, bf16[256,512]{1,0:T(8,128)(2,1)S(1)}, u32[]{:S(2)}, u32[]{:S(2)}) collective-permute-start(bf16[256,512]{1,0:T(8,128)(2,1)S(1)} %get-tuple-element.63.refs_3_), channel_id=1, source_target_pairs={{0,1},{2,0},{4,2},{6,4},{7,6},{5,7},{3,5},{1,3},{8,9},{10,8},{12,1... | collective-permute-start | bytes 786440 | tf_op jit(solution)/shard_map/ppermute | solution.py:55
  3.1 8.0 %copy-start.4 = (f32[512,4]{0,1:T(4,128)S(1)}, f32[512,4]{0,1:T(4,128)}, u32[]{:S(2)}) copy-start(f32[512,4]{0,1:T(4,128)} %param.18) | copy-start | bytes 24580
  3.1 7.8 %collective-permute-start = (bf16[256,512]{1,0:T(8,128)(2,1)S(1)}, bf16[256,512]{1,0:T(8,128)(2,1)S(1)}, u32[]{:S(2)}, u32[]{:S(2)}) collective-permute-start(bf16[256,512]{1,0:T(8,128)(2,1)S(1)} %get-tuple-element.60.refs_0_), channel_id=1, source_target_pairs={{0,2},{2,4},{4,6},{6,7},{7,5},{5,3},{3,1},{1,0},{8,10},{10,12},{12... | collective-permute-start | bytes 786440 | tf_op jit(solution)/shard_map/ppermute | solution.py:55
  3.3 12.3 %collective-permute-start.3 = (bf16[256,512]{1,0:T(8,128)(2,1)S(1)}, bf16[256,512]{1,0:T(8,128)(2,1)S(1)}, u32[]{:S(2)}, u32[]{:S(2)}) collective-permute-start(bf16[256,512]{1,0:T(8,128)(2,1)S(1)} %get-tuple-element.63.refs_3_), channel_id=1, source_target_pairs={{0,2},{2,4},{4,6},{6,7},{7,5},{5,3},{3,1},{1,0},{8,10},{10,12},{12... | collective-permute-start | bytes 786440 | tf_op jit(solution)/shard_map/ppermute | solution.py:55
  4.7 11.4 %collective-permute-start.2 = (bf16[256,512]{1,0:T(8,128)(2,1)S(1)}, bf16[256,512]{1,0:T(8,128)(2,1)S(1)}, u32[]{:S(2)}, u32[]{:S(2)}) collective-permute-start(bf16[256,512]{1,0:T(8,128)(2,1)S(1)} %get-tuple-element.60.refs_0_), channel_id=1, source_target_pairs={{0,1},{2,0},{4,2},{6,4},{7,6},{5,7},{3,5},{1,3},{8,9},{10,8},{12,1... | collective-permute-start | bytes 786440 | tf_op jit(solution)/shard_map/ppermute | solution.py:55
  9.6 10.9 %collective-permute-start.8 = (bf16[256,512]{1,0:T(8,128)(2,1)S(1)}, bf16[256,512]{1,0:T(8,128)(2,1)S(1)}, u32[]{:S(2)}, u32[]{:S(2)}) collective-permute-start(bf16[256,512]{1,0:T(8,128)(2,1)S(1)} %collective-permute-done.4.refs_5_), channel_id=1, source_target_pairs={{0,1},{2,0},{4,2},{6,4},{7,6},{5,7},{3,5},{1,3},{8,9},{10,8},{12,1... | collective-permute-start | bytes 786440 | tf_op jit(solution)/shard_map/ppermute | solution.py:55
  10.9 10.3 %collective-permute-start.1 = (bf16[256,512]{1,0:T(8,128)(2,1)S(1)}, bf16[256,512]{1,0:T(8,128)(2,1)S(1)}, u32[]{:S(2)}, u32[]{:S(2)}) collective-permute-start(bf16[256,512]{1,0:T(8,128)(2,1)S(1)} %collective-permute-done.refs_1_), channel_id=1, source_target_pairs={{0,2},{2,4},{4,6},{6,7},{7,5},{5,3},{3,1},{1,0},{8,10},{10,12},{12... | collective-permute-start | bytes 786440 | tf_op jit(solution)/shard_map/ppermute | solution.py:55
  11.1 8.6 %collective-permute-start.5 = (f32[4,512]{1,0:T(4,128)S(1)}, f32[4,512]{1,0:T(4,128)S(1)}, u32[]{:S(2)}, u32[]{:S(2)}) collective-permute-start(f32[4,512]{1,0:T(4,128)S(1)} %bitcast.1), channel_id=1, source_target_pairs={{0,8},{8,0},{16,24},{24,16},{1,9},{9,1},{17,25},{25,17},{2,10},{10... | collective-permute-start | bytes 24584 | tf_op jit(solution)/shard_map/ppermute | solution.py:539
  15.6 11.2 %collective-permute-start.13 = (bf16[256,512]{1,0:T(8,128)(2,1)S(1)}, bf16[256,512]{1,0:T(8,128)(2,1)S(1)}, u32[]{:S(2)}, u32[]{:S(2)}) collective-permute-start(bf16[256,512]{1,0:T(8,128)(2,1)S(1)} %collective-permute-done.3.refs_4_), channel_id=1, source_target_pairs={{0,2},{2,4},{4,6},{6,7},{7,5},{5,3},{3,1},{1,0},{8,10},{10,12},{12... | collective-permute-start | bytes 786440 | tf_op jit(solution)/shard_map/ppermute | solution.py:55
  16.1 10.8 %collective-permute-start.11 = (bf16[256,512]{1,0:T(8,128)(2,1)S(1)}, bf16[256,512]{1,0:T(8,128)(2,1)S(1)}, u32[]{:S(2)}, u32[]{:S(2)}) collective-permute-start(bf16[256,512]{1,0:T(8,128)(2,1)S(1)} %collective-permute-done.2.refs_2_), channel_id=1, source_target_pairs={{0,1},{2,0},{4,2},{6,4},{7,6},{5,7},{3,5},{1,3},{8,9},{10,8},{12,1... | collective-permute-start | bytes 786440 | tf_op jit(solution)/shard_map/ppermute | solution.py:55
  21.2 10.3 %collective-permute-start.9 = (bf16[256,512]{1,0:T(8,128)(2,1)S(1)}, bf16[256,512]{1,0:T(8,128)(2,1)S(1)}, u32[]{:S(2)}, u32[]{:S(2)}) collective-permute-start(bf16[256,512]{1,0:T(8,128)(2,1)S(1)} %collective-permute-done.8.refs_3_), channel_id=1, source_target_pairs={{0,1},{2,0},{4,2},{6,4},{7,6},{5,7},{3,5},{1,3},{8,9},{10,8},{12,1... | collective-permute-start | bytes 786440 | tf_op jit(solution)/shard_map/ppermute | solution.py:55
  22.5 10.2 %collective-permute-start.6 = (bf16[256,512]{1,0:T(8,128)(2,1)S(1)}, bf16[256,512]{1,0:T(8,128)(2,1)S(1)}, u32[]{:S(2)}, u32[]{:S(2)}) collective-permute-start(bf16[256,512]{1,0:T(8,128)(2,1)S(1)} %collective-permute-done.1.refs_0_), channel_id=1, source_target_pairs={{0,2},{2,4},{4,6},{6,7},{7,5},{5,3},{3,1},{1,0},{8,10},{10,12},{12... | collective-permute-start | bytes 786440 | tf_op jit(solution)/shard_map/ppermute | solution.py:55
  26.9 11.2 %collective-permute-start.14 = (bf16[256,512]{1,0:T(8,128)(2,1)S(1)}, bf16[256,512]{1,0:T(8,128)(2,1)S(1)}, u32[]{:S(2)}, u32[]{:S(2)}) collective-permute-start(bf16[256,512]{1,0:T(8,128)(2,1)S(1)} %collective-permute-done.13.refs_2_), channel_id=1, source_target_pairs={{0,2},{2,4},{4,6},{6,7},{7,5},{5,3},{3,1},{1,0},{8,10},{10,12},{12... | collective-permute-start | bytes 786440 | tf_op jit(solution)/shard_map/ppermute | solution.py:55
  27.3 10.8 %collective-permute-start.12 = (bf16[256,512]{1,0:T(8,128)(2,1)S(1)}, bf16[256,512]{1,0:T(8,128)(2,1)S(1)}, u32[]{:S(2)}, u32[]{:S(2)}) collective-permute-start(bf16[256,512]{1,0:T(8,128)(2,1)S(1)} %collective-permute-done.11.refs_1_), channel_id=1, source_target_pairs={{0,1},{2,0},{4,2},{6,4},{7,6},{5,7},{3,5},{1,3},{8,9},{10,8},{12,1... | collective-permute-start | bytes 786440 | tf_op jit(solution)/shard_map/ppermute | solution.py:55
  31.6 11.2 %collective-permute-start.10 = (bf16[256,512]{1,0:T(8,128)(2,1)S(1)}, bf16[256,512]{1,0:T(8,128)(2,1)S(1)}, u32[]{:S(2)}, u32[]{:S(2)}) collective-permute-start(bf16[256,512]{1,0:T(8,128)(2,1)S(1)} %collective-permute-done.9.refs_3_), channel_id=1, source_target_pairs={{0,1},{2,0},{4,2},{6,4},{7,6},{5,7},{3,5},{1,3},{8,9},{10,8},{12,1... | collective-permute-start | bytes 786440 | tf_op jit(solution)/shard_map/ppermute | solution.py:55
  32.7 11.0 %collective-permute-start.7 = (bf16[256,512]{1,0:T(8,128)(2,1)S(1)}, bf16[256,512]{1,0:T(8,128)(2,1)S(1)}, u32[]{:S(2)}, u32[]{:S(2)}) collective-permute-start(bf16[256,512]{1,0:T(8,128)(2,1)S(1)} %collective-permute-done.6.refs_0_), channel_id=1, source_target_pairs={{0,2},{2,4},{4,6},{6,7},{7,5},{5,3},{3,1},{1,0},{8,10},{10,12},{12... | collective-permute-start | bytes 786440 | tf_op jit(solution)/shard_map/ppermute | solution.py:55
  43.7 5.5 %copy-start.1 = (f32[4,128,256]{2,1,0:T(8,128)S(1)}, f32[4,128,256]{2,1,0:T(8,128)}, u32[]{:S(2)}) copy-start(f32[4,128,256]{2,1,0:T(8,128)} %gate_ref.5) | copy-start | bytes 1572868
  43.7 5.6 %copy-start.2 = (f32[4,128,256]{2,1,0:T(8,128)S(1)}, f32[4,128,256]{2,1,0:T(8,128)}, u32[]{:S(2)}) copy-start(f32[4,128,256]{2,1,0:T(8,128)} %up_ref.5) | copy-start | bytes 1572868
  43.7 5.6 %copy-start.3 = (f32[4,256,128]{2,1,0:T(8,128)S(1)}, f32[4,256,128]{2,1,0:T(8,128)}, u32[]{:S(2)}) copy-start(f32[4,256,128]{2,1,0:T(8,128)} %down_ref.5) | copy-start | bytes 1572868
  44.2 6.5 %collective-permute-start.16 = (bf16[2,512,256]{2,1,0:T(8,128)(2,1)S(1)}, bf16[2,512,256]{2,1,0:T(8,128)(2,1)S(1)}, u32[]{:S(2)}, u32[]{:S(2)}) collective-permute-start(bf16[2,512,256]{2,1,0:T(8,128)(2,1)S(1)} %get-tuple-element.79), channel_id=1, source_target_pairs={{0,8},{8,0},{16,24},{24,16},{1,9},{9,1},{17,25},{25,17},{2,10},{10... | collective-permute-start | bytes 1572872 | tf_op jit(solution)/shard_map/ppermute | solution.py:539
  46.2 14.6 %collective-permute-start.15 = (bf16[2,512,256]{2,1,0:T(8,128)(2,1)S(1)}, bf16[2,512,256]{2,1,0:T(8,128)(2,1)S(1)}, u32[]{:S(2)}, u32[]{:S(2)}) collective-permute-start(bf16[2,512,256]{2,1,0:T(8,128)(2,1)S(1)} %get-tuple-element.79), channel_id=1, source_target_pairs={{8,16},{9,17},{10,18},{11,19},{12,20},{13,21},{14,22},{15,23}} | collective-permute-start | bytes 1572872 | tf_op jit(solution)/shard_map/ppermute | solution.py:573
  52.2 10.1 %collective-permute-start.17 = (bf16[2,512,256]{2,1,0:T(8,128)(2,1)S(1)}, bf16[2,512,256]{2,1,0:T(8,128)(2,1)S(1)}, u32[]{:S(2)}, u32[]{:S(2)}) collective-permute-start(bf16[2,512,256]{2,1,0:T(8,128)(2,1)S(1)} %get-tuple-element.83), channel_id=1, source_target_pairs={{0,8},{16,24},{1,9},{17,25},{2,10},{18,26},{3,11},{19,27},{4,12},{... | collective-permute-start | bytes 1572872 | tf_op jit(solution)/shard_map/ppermute | solution.py:588
  53.5 10.2 %collective-permute-start.19 = (bf16[2,3,128,256]{3,2,1,0:T(8,128)(2,1)S(1)}, bf16[2,3,128,256]{3,2,1,0:T(8,128)(2,1)S(1)}, u32[]{:S(2)}, u32[]{:S(2)}) collective-permute-start(bf16[2,3,128,256]{3,2,1,0:T(8,128)(2,1)S(1)} %get-tuple-element.84), channel_id=1, source_target_pairs={{0,16},{8,24},{16,0},{24,8},{1,17},{9,25},{17,1},{25,9},{2,18},{10... | collective-permute-start | bytes 1179656 | tf_op jit(solution)/shard_map/ppermute | solution.py:539
  56.1 13.3 %collective-permute-start.18 = (bf16[2,512,256]{2,1,0:T(8,128)(2,1)S(1)}, bf16[2,512,256]{2,1,0:T(8,128)(2,1)S(1)}, u32[]{:S(2)}, u32[]{:S(2)}) collective-permute-start(bf16[2,512,256]{2,1,0:T(8,128)(2,1)S(1)} %get-tuple-element.83), channel_id=1, source_target_pairs={{8,16},{9,17},{10,18},{11,19},{12,20},{13,21},{14,22},{15,23}} | collective-permute-start | bytes 1572872 | tf_op jit(solution)/shard_map/ppermute | solution.py:589
  60.8 2.8 %copy-start.5 = (f32[4]{0:T(128)S(1)}, f32[4]{0:T(128)}, u32[]{:S(2)}) copy-start(f32[4]{0:T(128)} %step_ref.1) | copy-start | bytes 52
  64.5 4.9 %copy-start = (bf16[512,4096]{1,0:T(8,128)(2,1)S(1)}, bf16[512,4096]{1,0:T(8,128)(2,1)}, u32[]{:S(2)}) copy-start(bf16[512,4096]{1,0:T(8,128)(2,1)} %w_ref.7) | copy-start | bytes 12582916
  64.5 4.9 %collective-permute-start.20 = (bf16[2,3,128,256]{3,2,1,0:T(8,128)(2,1)S(1)}, bf16[2,3,128,256]{3,2,1,0:T(8,128)(2,1)S(1)}, u32[]{:S(2)}, u32[]{:S(2)}) collective-permute-start(bf16[2,3,128,256]{3,2,1,0:T(8,128)(2,1)S(1)} %shard_map.113.net_ref), channel_id=1, source_target_pairs={{0,8},{8,0},{16,24},{24,16},{1,9},{9,1},{17,25},{25,17},{2,10},{10... | collective-permute-start | bytes 1179656 | tf_op jit(solution)/shard_map/ppermute | solution.py:539
  70.6 8.3 %collective-permute-start.22 = (bf16[64,2048]{1,0:T(8,128)(2,1)S(1)}, bf16[64,2048]{1,0:T(8,128)(2,1)S(1)}, u32[]{:S(2)}, u32[]{:S(2)}) collective-permute-start(bf16[64,2048]{1,0:T(8,128)(2,1)S(1)} %get-tuple-element.88), channel_id=1, source_target_pairs={{0,1},{2,0},{4,2},{6,4},{7,6},{5,7},{3,5},{1,3},{8,9},{10,8},{12,1... | collective-permute-start | bytes 786440 | tf_op jit(solution)/shard_map/ppermute | solution.py:55
  72.0 8.3 %collective-permute-start.21 = (bf16[64,2048]{1,0:T(8,128)(2,1)S(1)}, bf16[64,2048]{1,0:T(8,128)(2,1)S(1)}, u32[]{:S(2)}, u32[]{:S(2)}) collective-permute-start(bf16[64,2048]{1,0:T(8,128)(2,1)S(1)} %get-tuple-element.86), channel_id=1, source_target_pairs={{0,2},{2,4},{4,6},{6,7},{7,5},{5,3},{3,1},{1,0},{8,10},{10,12},{12... | collective-permute-start | bytes 786440 | tf_op jit(solution)/shard_map/ppermute | solution.py:55
  73.4 11.2 %collective-permute-start.26 = (bf16[64,2048]{1,0:T(8,128)(2,1)S(1)}, bf16[64,2048]{1,0:T(8,128)(2,1)S(1)}, u32[]{:S(2)}, u32[]{:S(2)}) collective-permute-start(bf16[64,2048]{1,0:T(8,128)(2,1)S(1)} %get-tuple-element.92), channel_id=1, source_target_pairs={{0,1},{2,0},{4,2},{6,4},{7,6},{5,7},{3,5},{1,3},{8,9},{10,8},{12,1... | collective-permute-start | bytes 786440 | tf_op jit(solution)/shard_map/ppermute | solution.py:55
  74.7 11.1 %collective-permute-start.25 = (bf16[64,2048]{1,0:T(8,128)(2,1)S(1)}, bf16[64,2048]{1,0:T(8,128)(2,1)S(1)}, u32[]{:S(2)}, u32[]{:S(2)}) collective-permute-start(bf16[64,2048]{1,0:T(8,128)(2,1)S(1)} %get-tuple-element.91), channel_id=1, source_target_pairs={{0,2},{2,4},{4,6},{6,7},{7,5},{5,3},{3,1},{1,0},{8,10},{10,12},{12... | collective-permute-start | bytes 786440 | tf_op jit(solution)/shard_map/ppermute | solution.py:55
  80.3 9.9 %collective-permute-start.24 = (bf16[64,2048]{1,0:T(8,128)(2,1)S(1)}, bf16[64,2048]{1,0:T(8,128)(2,1)S(1)}, u32[]{:S(2)}, u32[]{:S(2)}) collective-permute-start(bf16[64,2048]{1,0:T(8,128)(2,1)S(1)} %add_convert_fusion.10), channel_id=1, source_target_pairs={{0,1},{2,0},{4,2},{6,4},{7,6},{5,7},{3,5},{1,3},{8,9},{10,8},{12,1... | collective-permute-start | bytes 786440 | tf_op jit(solution)/shard_map/ppermute | solution.py:55
  81.6 9.8 %collective-permute-start.23 = (bf16[64,2048]{1,0:T(8,128)(2,1)S(1)}, bf16[64,2048]{1,0:T(8,128)(2,1)S(1)}, u32[]{:S(2)}, u32[]{:S(2)}) collective-permute-start(bf16[64,2048]{1,0:T(8,128)(2,1)S(1)} %add_convert_fusion.11), channel_id=1, source_target_pairs={{0,2},{2,4},{4,6},{6,7},{7,5},{5,3},{3,1},{1,0},{8,10},{10,12},{12... | collective-permute-start | bytes 786440 | tf_op jit(solution)/shard_map/ppermute | solution.py:55
  85.9 9.9 %collective-permute-start.28 = (bf16[64,2048]{1,0:T(8,128)(2,1)S(1)}, bf16[64,2048]{1,0:T(8,128)(2,1)S(1)}, u32[]{:S(2)}, u32[]{:S(2)}) collective-permute-start(bf16[64,2048]{1,0:T(8,128)(2,1)S(1)} %add_convert_fusion.8), channel_id=1, source_target_pairs={{0,1},{2,0},{4,2},{6,4},{7,6},{5,7},{3,5},{1,3},{8,9},{10,8},{12,1... | collective-permute-start | bytes 786440 | tf_op jit(solution)/shard_map/ppermute | solution.py:55
  87.3 9.8 %collective-permute-start.27 = (bf16[64,2048]{1,0:T(8,128)(2,1)S(1)}, bf16[64,2048]{1,0:T(8,128)(2,1)S(1)}, u32[]{:S(2)}, u32[]{:S(2)}) collective-permute-start(bf16[64,2048]{1,0:T(8,128)(2,1)S(1)} %add_convert_fusion.9), channel_id=1, source_target_pairs={{0,2},{2,4},{4,6},{6,7},{7,5},{5,3},{3,1},{1,0},{8,10},{10,12},{12... | collective-permute-start | bytes 786440 | tf_op jit(solution)/shard_map/ppermute | solution.py:55
  91.5 9.4 %collective-permute-start.32 = (bf16[64,2048]{1,0:T(8,128)(2,1)S(1)}, bf16[64,2048]{1,0:T(8,128)(2,1)S(1)}, u32[]{:S(2)}, u32[]{:S(2)}) collective-permute-start(bf16[64,2048]{1,0:T(8,128)(2,1)S(1)} %add_convert_fusion.4), channel_id=1, source_target_pairs={{0,1},{2,0},{4,2},{6,4},{7,6},{5,7},{3,5},{1,3},{8,9},{10,8},{12,1... | collective-permute-start | bytes 786440 | tf_op jit(solution)/shard_map/ppermute | solution.py:55
  92.9 9.8 %collective-permute-start.31 = (bf16[64,2048]{1,0:T(8,128)(2,1)S(1)}, bf16[64,2048]{1,0:T(8,128)(2,1)S(1)}, u32[]{:S(2)}, u32[]{:S(2)}) collective-permute-start(bf16[64,2048]{1,0:T(8,128)(2,1)S(1)} %add_convert_fusion.5), channel_id=1, source_target_pairs={{0,2},{2,4},{4,6},{6,7},{7,5},{5,3},{3,1},{1,0},{8,10},{10,12},{12... | collective-permute-start | bytes 786440 | tf_op jit(solution)/shard_map/ppermute | solution.py:55
  97.1 11.2 %collective-permute-start.29 = (bf16[64,2048]{1,0:T(8,128)(2,1)S(1)}, bf16[64,2048]{1,0:T(8,128)(2,1)S(1)}, u32[]{:S(2)}, u32[]{:S(2)}) collective-permute-start(bf16[64,2048]{1,0:T(8,128)(2,1)S(1)} %add_convert_fusion.7), channel_id=1, source_target_pairs={{0,2},{2,4},{4,6},{6,7},{7,5},{5,3},{3,1},{1,0},{8,10},{10,12},{12... | collective-permute-start | bytes 786440 | tf_op jit(solution)/shard_map/ppermute | solution.py:55
  97.4 10.9 %collective-permute-start.30 = (bf16[64,2048]{1,0:T(8,128)(2,1)S(1)}, bf16[64,2048]{1,0:T(8,128)(2,1)S(1)}, u32[]{:S(2)}, u32[]{:S(2)}) collective-permute-start(bf16[64,2048]{1,0:T(8,128)(2,1)S(1)} %add_convert_fusion.6), channel_id=1, source_target_pairs={{0,1},{2,0},{4,2},{6,4},{7,6},{5,7},{3,5},{1,3},{8,9},{10,8},{12,1... | collective-permute-start | bytes 786440 | tf_op jit(solution)/shard_map/ppermute | solution.py:55
  102.8 10.4 %collective-permute-start.33 = (bf16[64,2048]{1,0:T(8,128)(2,1)S(1)}, bf16[64,2048]{1,0:T(8,128)(2,1)S(1)}, u32[]{:S(2)}, u32[]{:S(2)}) collective-permute-start(bf16[64,2048]{1,0:T(8,128)(2,1)S(1)} %add_convert_fusion.3), channel_id=1, source_target_pairs={{0,2},{2,4},{4,6},{6,7},{7,5},{5,3},{3,1},{1,0},{8,10},{10,12},{12... | collective-permute-start | bytes 786440 | tf_op jit(solution)/shard_map/ppermute | solution.py:55
  103.0 10.2 %collective-permute-start.34 = (bf16[64,2048]{1,0:T(8,128)(2,1)S(1)}, bf16[64,2048]{1,0:T(8,128)(2,1)S(1)}, u32[]{:S(2)}, u32[]{:S(2)}) collective-permute-start(bf16[64,2048]{1,0:T(8,128)(2,1)S(1)} %add_convert_fusion.2), channel_id=1, source_target_pairs={{0,1},{2,0},{4,2},{6,4},{7,6},{5,7},{3,5},{1,3},{8,9},{10,8},{12,1... | collective-permute-start | bytes 786440 | tf_op jit(solution)/shard_map/ppermute | solution.py:55

commit v14 on v12

--- a/solution.py
+++ b/solution.py
@@ -509,8 +509,10 @@
             if (way, side) in coming:
                 term = (term.astype(F32) + coming[way, side].astype(F32)).astype(BF16)
             terms.append(term)
-        ordered = lax.optimization_barrier((*terms, *ordered))[:2]
-        for way, term in zip((1, -1), ordered):
+        terms[0] = lax.optimization_barrier((terms[0], *ordered))[0]
+        terms[1] = lax.optimization_barrier((terms[1], terms[0]))[0]
+        ordered = terms[1:]
+        for way, term in zip((1, -1), terms):
             coming[way, half if way == 1 else 1 - half] = ring_send(term, way)
     sides = {1: 1 - half, -1: half}
     totals = add_pair(

time: 113 us -> 112 us (level)
  transfers between devices with their start and end apart: 34 -> 34, of which waited for: 23 -> 19; matrix products, arithmetic and copies ran while one was open for 1% -> 1% of each run, Pallas kernels for 22% -> 22%
where the time goes in v14:
time: 112 us
  waiting for transfers between devices  51.1 us (46%)
  starting transfers between devices  31.4 us (28%)
  Pallas kernels  27.9 us (25%)
  other arithmetic  1.56 us (1%)
    ppermute x28, waiting for transfers between devices, ring_send(): lax.ppermute(value, 'head', [(order[i], order[(i + step) % count]) for i...  41.4 us
    ppermute x28, starting transfers between devices, ring_send(): lax.ppermute(value, 'head', [(order[i], order[(i + step) % count]) for i...  22 us
    pallas_call x4, Pallas kernels, accumulate(): call(body, [WHOLE] * len(args), WHOLE, jax.ShapeDtypeStruct((parts, total...  6.72 us
    pallas_call x4, Pallas kernels, partial_out(): call(body, [WHOLE] * 5 + [AFTER] * len(after), [WHOLE] * (2 * count), [ja...  5.18 us
    pallas_call x1, Pallas kernels, load(): call(body, [IN_HBM] * count, [WHOLE] * count, [jax.ShapeDtypeStruct(array...  4.78 us
    ppermute x4, waiting for transfers between devices, swap(): lax.ppermute(value, 'tok', [(index, index ^ bit) for index in range(count)])  4.61 us
    ppermute x4, starting transfers between devices, swap(): lax.ppermute(value, 'tok', [(index, index ^ bit) for index in range(count)])  4.43 us
    ppermute x1, waiting for transfers between devices, shards(): lax.ppermute(near, 'tok', [(index, index + 1) for index in range(tok_coun...  3.89 us
  transfers between devices with their start and end apart: 34, of which 19 were waited for; matrix products, arithmetic and copies ran while one was open for 1% of the time, Pallas kernels for 22%

profile of v14, /device:TPU:1, one launch (start us, length us, event | category | flops | bytes accessed | tf_op | source)
XLA Modules:
  0.0 112.3 jit_solution(16434674358470928240)
XLA Ops:
  0.0 1.0 shard_map.100
  1.1 2.1 %collective-permute-start.4 = (bf16[256,512]{1,0:T(8,128)(2,1)S(1)}, bf16[256,512]{1,0:T(8,128)(2,1)S(1)}, u32[]{:S(2)}, u32[]{:S(2)}) collective-permute-start(bf16[256,512]{1,0:T(8,128)(2,1)S(1)} %get-tuple-element.63.refs_3_), channel_id=1, source_target_pairs={{0,1},{2,0},{4,2},{6,4},{7,6},{5,7},{3,5},{1,3},{8,9},{10,8},{12,1... | collective-permute-start | bytes 786440 | tf_op jit(solution)/shard_map/ppermute | solution.py:55
  3.3 1.4 %collective-permute-start.3 = (bf16[256,512]{1,0:T(8,128)(2,1)S(1)}, bf16[256,512]{1,0:T(8,128)(2,1)S(1)}, u32[]{:S(2)}, u32[]{:S(2)}) collective-permute-start(bf16[256,512]{1,0:T(8,128)(2,1)S(1)} %get-tuple-element.63.refs_3_), channel_id=1, source_target_pairs={{0,2},{2,4},{4,6},{6,7},{7,5},{5,3},{3,1},{1,0},{8,10},{10,12},{12... | collective-permute-start | bytes 786440 | tf_op jit(solution)/shard_map/ppermute | solution.py:55
  4.8 4.8 %shard_map.101 = (bf16[4096,512]{1,0:T(8,128)(2,1)S(1)}, bf16[4096,512]{1,0:T(8,128)(2,1)S(1)}, bf16[4096,512]{1,0:T(8,128)(2,1)S(1)}) custom-call(bf16[4096,512]{1,0:T(8,128)(2,1)} %refs_0_.1, bf16[4096,512]{1,0:T(8,128)(2,1)} %refs_1_.1, bf16[4096,512]{1,0:T(8,128)(2,1)} %refs_2_.1), custom_call_target="tpu_custom_call" | custom-call | bytes 25165824 | tf_op jit(solution)/shard_map/pallas_call | solution.py:111
  9.6 1.4 %collective-permute-start.8 = (bf16[256,512]{1,0:T(8,128)(2,1)S(1)}, bf16[256,512]{1,0:T(8,128)(2,1)S(1)}, u32[]{:S(2)}, u32[]{:S(2)}) collective-permute-start(bf16[256,512]{1,0:T(8,128)(2,1)S(1)} %collective-permute-done.4.refs_5_), channel_id=1, source_target_pairs={{0,1},{2,0},{4,2},{6,4},{7,6},{5,7},{3,5},{1,3},{8,9},{10,8},{12,1... | collective-permute-start | bytes 786440 | tf_op jit(solution)/shard_map/ppermute | solution.py:55
  11.1 2.4 %collective-permute-start.5 = (f32[4,512]{1,0:T(4,128)S(1)}, f32[4,512]{1,0:T(4,128)S(1)}, u32[]{:S(2)}, u32[]{:S(2)}) collective-permute-start(f32[4,512]{1,0:T(4,128)S(1)} %bitcast.1), channel_id=1, source_target_pairs={{0,8},{8,0},{16,24},{24,16},{1,9},{9,1},{17,25},{25,17},{2,10},{10... | collective-permute-start | bytes 24584 | tf_op jit(solution)/shard_map/ppermute | solution.py:544
  13.5 2.2 %collective-permute-done.3.refs_4_ = bf16[256,512]{1,0:T(8,128)(2,1)S(1)} collective-permute-done((bf16[256,512]{1,0:T(8,128)(2,1)S(1)}, bf16[256,512]{1,0:T(8,128)(2,1)S(1)}, u32[]{:S(2)}, u32[]{:S(2)}) %collective-permute-start.3) | collective-permute-done | bytes 262176 | tf_op jit(solution)/shard_map/ppermute | solution.py:55
  15.6 0.5 collective-permute-start.13
  16.1 1.0 collective-permute-start.11
  17.1 2.6 %shard_map.102.refs_7_ = f32[3,512,512]{2,1,0:T(8,128)S(1)} custom-call(bf16[256,512]{1,0:T(8,128)(2,1)S(1)} %get-tuple-element.60.refs_0_, bf16[256,512]{1,0:T(8,128)(2,1)S(1)} %collective-permute-done.refs_1_, bf16[256,512]{1,0:T(8,128)(2,1)S(1)} %collective-permute-done.2.refs_2_, bf16[256,512]{1,0:T(8,128)(2,1)S(1)} %get-tuple-element.63.refs_3_, ...), custom_call_target="tpu_custom_call" | custom-call | flops 2415919104 | bytes 12582912 | tf_op jit(solution)/shard_map/pallas_call | solution.py:180
  19.7 0.8 collective-permute-done.8.refs_3_
  20.5 0.7 collective-permute-done.1.refs_0_
  21.2 1.3 %collective-permute-start.9 = (bf16[256,512]{1,0:T(8,128)(2,1)S(1)}, bf16[256,512]{1,0:T(8,128)(2,1)S(1)}, u32[]{:S(2)}, u32[]{:S(2)}) collective-permute-start(bf16[256,512]{1,0:T(8,128)(2,1)S(1)} %collective-permute-done.8.refs_3_), channel_id=1, source_target_pairs={{0,1},{2,0},{4,2},{6,4},{7,6},{5,7},{3,5},{1,3},{8,9},{10,8},{12,1... | collective-permute-start | bytes 786440 | tf_op jit(solution)/shard_map/ppermute | solution.py:55
  22.7 4.2 %collective-permute-done.13.refs_2_ = bf16[256,512]{1,0:T(8,128)(2,1)S(1)} collective-permute-done((bf16[256,512]{1,0:T(8,128)(2,1)S(1)}, bf16[256,512]{1,0:T(8,128)(2,1)S(1)}, u32[]{:S(2)}, u32[]{:S(2)}) %collective-permute-start.13) | collective-permute-done | bytes 262176 | tf_op jit(solution)/shard_map/ppermute | solution.py:55
  26.9 0.5 collective-permute-start.14
  27.3 1.0 collective-permute-start.12
  28.3 3.3 %collective-permute-done.9.refs_3_ = bf16[256,512]{1,0:T(8,128)(2,1)S(1)} collective-permute-done((bf16[256,512]{1,0:T(8,128)(2,1)S(1)}, bf16[256,512]{1,0:T(8,128)(2,1)S(1)}, u32[]{:S(2)}, u32[]{:S(2)}) %collective-permute-start.9) | collective-permute-done | bytes 262176 | tf_op jit(solution)/shard_map/ppermute | solution.py:55
  31.6 1.1 collective-permute-start.10
  33.1 1.8 %shard_map.103.refs_7_ = f32[3,512,512]{2,1,0:T(8,128)S(1)} custom-call(bf16[256,512]{1,0:T(8,128)(2,1)S(1)} %collective-permute-done.1.refs_0_, bf16[256,512]{1,0:T(8,128)(2,1)S(1)} %collective-permute-done.11.refs_1_, bf16[256,512]{1,0:T(8,128)(2,1)S(1)} %collective-permute-done.13.refs_2_, ...), custom_call_target="tpu_custom_call", output_to_operand_aliasing={{}: (7, {})} | custom-call | flops 1610612736 | bytes 10485760 | tf_op jit(solution)/shard_map/pallas_call | solution.py:180
  34.9 3.2 %collective-permute-done.14.refs_2_ = bf16[256,512]{1,0:T(8,128)(2,1)S(1)} collective-permute-done((bf16[256,512]{1,0:T(8,128)(2,1)S(1)}, bf16[256,512]{1,0:T(8,128)(2,1)S(1)}, u32[]{:S(2)}, u32[]{:S(2)}) %collective-permute-start.14) | collective-permute-done | bytes 262176 | tf_op jit(solution)/shard_map/ppermute | solution.py:55
  38.1 1.8 %shard_map.104.refs_3_.refs_2_ = f32[3,512,512]{2,1,0:T(8,128)S(1)} custom-call(bf16[256,512]{1,0:T(8,128)(2,1)S(1)} %collective-permute-done.6.refs_0_, bf16[256,512]{1,0:T(8,128)(2,1)S(1)} %collective-permute-done.12.refs_1_, bf16[256,512]{1,0:T(8,128)(2,1)S(1)} %collective-permute-done.14.refs_2_, ...), custom_call_target="tpu_custom_call", output_to_operand_aliasing={{}: (7, {})} | custom-call | flops 1610612736 | bytes 10485760 | tf_op jit(solution)/shard_map/pallas_call | solution.py:180
  39.9 2.9 %collective-permute-done.10.refs_1_.piece_ref = bf16[256,512]{1,0:T(8,128)(2,1)S(1)} collective-permute-done((bf16[256,512]{1,0:T(8,128)(2,1)S(1)}, bf16[256,512]{1,0:T(8,128)(2,1)S(1)}, u32[]{:S(2)}, u32[]{:S(2)}) %collective-permute-start.10) | collective-permute-done | bytes 262176 | tf_op jit(solution)/shard_map/ppermute | solution.py:55
  42.8 0.5 shard_map.106
  43.7 0.5 shard_map.107
  44.2 1.9 %collective-permute-start.16 = (bf16[2,512,256]{2,1,0:T(8,128)(2,1)S(1)}, bf16[2,512,256]{2,1,0:T(8,128)(2,1)S(1)}, u32[]{:S(2)}, u32[]{:S(2)}) collective-permute-start(bf16[2,512,256]{2,1,0:T(8,128)(2,1)S(1)} %get-tuple-element.79), channel_id=1, source_target_pairs={{0,8},{8,0},{16,24},{24,16},{1,9},{9,1},{17,25},{25,17},{2,10},{10... | collective-permute-start | bytes 1572872 | tf_op jit(solution)/shard_map/ppermute | solution.py:544
  46.2 3.1 %collective-permute-start.15 = (bf16[2,512,256]{2,1,0:T(8,128)(2,1)S(1)}, bf16[2,512,256]{2,1,0:T(8,128)(2,1)S(1)}, u32[]{:S(2)}, u32[]{:S(2)}) collective-permute-start(bf16[2,512,256]{2,1,0:T(8,128)(2,1)S(1)} %get-tuple-element.79), channel_id=1, source_target_pairs={{8,16},{9,17},{10,18},{11,19},{12,20},{13,21},{14,22},{15,23}} | collective-permute-start | bytes 1572872 | tf_op jit(solution)/shard_map/ppermute | solution.py:578
  49.3 1.4 %shard_map.110.rest_0_ = f32[2,3,128,256]{3,2,1,0:T(8,128)S(1)} custom-call(bf16[2,512,512]{2,1,0:T(8,128)(2,1)S(1)} %get-tuple-element.76.kv_ref, f32[4,512]{1,0:T(4,128)S(1)} %bitcast.2, f32[4,128,256]{2,1,0:T(8,128)S(1)} %copy-done.1, f32[4,128,256]{2,1,0:T(8,128)S(1)} %copy-done.2, f32[4,256,128]{2,1,0:T(8,128)S(1)} %copy-done.3), custom_call_target="tpu_custom_call" | custom-call | flops 402653184 | bytes 1572864 | tf_op jit(solution)/shard_map/pallas_call | solution.py:272
  50.7 1.4 %shard_map.111 = (f32[2,3,128,256]{3,2,1,0:T(8,128)S(1)}, bf16[2,3,128,256]{3,2,1,0:T(8,128)(2,1)S(1)}) custom-call(bf16[2,512,256]{2,1,0:T(8,128)(2,1)S(1)} %collective-permute-done.16.refs_1_.kv_ref, f32[4,512]{1,0:T(4,128)S(1)} %collective-permute-done.5.rate_ref, f32[4,128,256]{2,1,0:T(8,128)S(1)} %copy-done.1, f32[4,128,256]{2,1,0:T(8,128)S(1)} %copy-done.2, ...), custom_call_target="tpu_custom_call" | custom-call | flops 402653184 | bytes 1572864 | tf_op jit(solution)/shard_map/pallas_call | solution.py:272
  52.7 2.1 %shard_map.108 = (f32[512,512]{1,0:T(8,128)S(1)}, f32[2,512,512]{2,1,0:T(8,128)S(1)}) custom-call(bf16[1,512,512]{2,1,0:T(8,128)(2,1)S(1)} %shard_map.105.q_ref, bf16[2,512,512]{2,1,0:T(8,128)(2,1)S(1)} %get-tuple-element.76.kv_ref), custom_call_target="tpu_custom_call" | custom-call | flops 402653184 | bytes 2097152 | tf_op jit(solution)/shard_map/pallas_call | solution.py:365
  54.8 1.9 %collective-permute-start.17 = (bf16[2,512,256]{2,1,0:T(8,128)(2,1)S(1)}, bf16[2,512,256]{2,1,0:T(8,128)(2,1)S(1)}, u32[]{:S(2)}, u32[]{:S(2)}) collective-permute-start(bf16[2,512,256]{2,1,0:T(8,128)(2,1)S(1)} %get-tuple-element.81), channel_id=1, source_target_pairs={{0,8},{8,16},{16,24},{1,9},{9,17},{17,25},{2,10},{10,18},{18,26},{... | collective-permute-start | bytes 1572872 | tf_op jit(solution)/shard_map/ppermute | solution.py:592
  56.7 1.2 %collective-permute-done.15.refs_0_ = bf16[2,512,256]{2,1,0:T(8,128)(2,1)S(1)} collective-permute-done((bf16[2,512,256]{2,1,0:T(8,128)(2,1)S(1)}, bf16[2,512,256]{2,1,0:T(8,128)(2,1)S(1)}, u32[]{:S(2)}, u32[]{:S(2)}) %collective-permute-start.15) | collective-permute-done | bytes 524320 | tf_op jit(solution)/shard_map/ppermute | solution.py:578
  57.9 1.2 %shard_map.109.rest_1_.attended_ref.sum_ref = f32[512,512]{1,0:T(8,128)S(1)} custom-call(f32[512,512]{1,0:T(8,128)S(1)} %get-tuple-element.77.sum_ref, f32[2,512,512]{2,1,0:T(8,128)S(1)} %get-tuple-element.78.stats_ref, bf16[1,512,512]{2,1,0:T(8,128)(2,1)S(1)} %shard_map.105.q_ref, ...), custom_call_target="tpu_custom_call", output_to_operand_aliasing={{}: (0, {})} | custom-call | flops 201326592 | bytes 1048576 | tf_op jit(solution)/shard_map/pallas_call | solution.py:405
  59.2 4.6 %collective-permute-done.18.rest_0_ = bf16[2,3,128,256]{3,2,1,0:T(8,128)(2,1)S(1)} collective-permute-done((bf16[2,3,128,256]{3,2,1,0:T(8,128)(2,1)S(1)}, bf16[2,3,128,256]{3,2,1,0:T(8,128)(2,1)S(1)}, u32[]{:S(2)}, u32[]{:S(2)}) %collective-permute-start.18) | collective-permute-done | bytes 393248 | tf_op jit(solution)/shard_map/ppermute | solution.py:544
  63.8 0.8 shard_map.112.net_ref
  64.7 0.8 shard_map.113.refs_1_.near_ref
  65.5 3.9 %collective-permute-done.17.refs_0_ = bf16[2,512,256]{2,1,0:T(8,128)(2,1)S(1)} collective-permute-done((bf16[2,512,256]{2,1,0:T(8,128)(2,1)S(1)}, bf16[2,512,256]{2,1,0:T(8,128)(2,1)S(1)}, u32[]{:S(2)}, u32[]{:S(2)}) %collective-permute-start.17) | collective-permute-done | bytes 524320 | tf_op jit(solution)/shard_map/ppermute | solution.py:592
  69.4 1.2 %shard_map.114.attended_ref = f32[512,512]{1,0:T(8,128)S(1)} custom-call(f32[512,512]{1,0:T(8,128)S(1)} %shard_map.109.rest_1_.attended_ref.sum_ref, f32[2,512,512]{2,1,0:T(8,128)S(1)} %get-tuple-element.78.stats_ref, bf16[1,512,512]{2,1,0:T(8,128)(2,1)S(1)} %shard_map.105.q_ref, ...), custom_call_target="tpu_custom_call", output_to_operand_aliasing={{}: (0, {})} | custom-call | flops 201326592 | bytes 1048576 | tf_op jit(solution)/shard_map/pallas_call | solution.py:405
  70.6 1.2 %shard_map.116 = (bf16[64,2048]{1,0:T(8,128)(2,1)S(1)}, bf16[64,2048]{1,0:T(8,128)(2,1)S(1)}) custom-call(bf16[1,512,512]{2,1,0:T(8,128)(2,1)S(1)} %shard_map.105.q_ref, f32[512,512]{1,0:T(8,128)S(1)} %shard_map.114.attended_ref, bf16[2,3,128,256]{3,2,1,0:T(8,128)(2,1)S(1)} %collective-permute-done.19.net_ref, ...), custom_call_target="tpu_custom_call" | custom-call | flops 268435456 | bytes 4718592 | tf_op jit(solution)/shard_map/pallas_call | solution.py:481
  71.8 0.7 collective-permute-start.20
  72.5 0.8 collective-permute-start.22
  73.4 1.2 %shard_map.115 = (bf16[64,2048]{1,0:T(8,128)(2,1)S(1)}, bf16[64,2048]{1,0:T(8,128)(2,1)S(1)}, bf16[64,2048]{1,0:T(8,128)(2,1)S(1)}, bf16[64,2048]{1,0:T(8,128)(2,1)S(1)}) custom-call(bf16[1,512,512]{2,1,0:T(8,128)(2,1)S(1)} %shard_map.105.q_ref, f32[512,512]{1,0:T(8,128)S(1)} %shard_map.114.attended_ref, ...), custom_call_target="tpu_custom_call" | custom-call | flops 536870912 | bytes 5242880 | tf_op jit(solution)/shard_map/pallas_call | solution.py:481
  74.6 0.7 collective-permute-start.24
  75.3 0.8 collective-permute-start.26
  76.1 4.1 %collective-permute-done.20.refs_0_ = bf16[64,2048]{1,0:T(8,128)(2,1)S(1)} collective-permute-done((bf16[64,2048]{1,0:T(8,128)(2,1)S(1)}, bf16[64,2048]{1,0:T(8,128)(2,1)S(1)}, u32[]{:S(2)}, u32[]{:S(2)}) %collective-permute-start.20) | collective-permute-done | bytes 262176 | tf_op jit(solution)/shard_map/ppermute | solution.py:55
  80.3 0.7 collective-permute-start.21
  81.1 0.9 collective-permute-start.23
  81.9 1.2 %shard_map.118 = (bf16[64,2048]{1,0:T(8,128)(2,1)S(1)}, bf16[64,2048]{1,0:T(8,128)(2,1)S(1)}, bf16[64,2048]{1,0:T(8,128)(2,1)S(1)}, bf16[64,2048]{1,0:T(8,128)(2,1)S(1)}) custom-call(bf16[1,512,512]{2,1,0:T(8,128)(2,1)S(1)} %shard_map.105.q_ref, f32[512,512]{1,0:T(8,128)S(1)} %shard_map.114.attended_ref, ...), custom_call_target="tpu_custom_call" | custom-call | flops 536870912 | bytes 5242880 | tf_op jit(solution)/shard_map/pallas_call | solution.py:481
  83.2 2.7 %collective-permute-done.24 = bf16[64,2048]{1,0:T(8,128)(2,1)S(1)} collective-permute-done((bf16[64,2048]{1,0:T(8,128)(2,1)S(1)}, bf16[64,2048]{1,0:T(8,128)(2,1)S(1)}, u32[]{:S(2)}, u32[]{:S(2)}) %collective-permute-start.24) | collective-permute-done | bytes 262176 | tf_op jit(solution)/shard_map/ppermute | solution.py:55
  85.9 0.7 collective-permute-start.25
  86.7 0.9 collective-permute-start.28
  87.5 3.9 %collective-permute-done.21.refs_0_ = bf16[64,2048]{1,0:T(8,128)(2,1)S(1)} collective-permute-done((bf16[64,2048]{1,0:T(8,128)(2,1)S(1)}, bf16[64,2048]{1,0:T(8,128)(2,1)S(1)}, u32[]{:S(2)}, u32[]{:S(2)}) %collective-permute-start.21) | collective-permute-done | bytes 262176 | tf_op jit(solution)/shard_map/ppermute | solution.py:55
  91.5 0.7 collective-permute-start.30
  92.3 0.9 collective-permute-start.32
  93.2 1.5 %shard_map.117 = (bf16[64,2048]{1,0:T(8,128)(2,1)S(1)}, bf16[64,2048]{1,0:T(8,128)(2,1)S(1)}, bf16[64,2048]{1,0:T(8,128)(2,1)S(1)}, bf16[64,2048]{1,0:T(8,128)(2...) custom-call(bf16[1,512,512]{2,1,0:T(8,128)(2,1)S(1)} %shard_map.105.q_ref, ...), custom_call_target="tpu_custom_call" | custom-call | flops 805306368 | bytes 5767168 | tf_op jit(solution)/shard_map/pallas_call | solution.py:481
  94.7 2.4 %collective-permute-done.25 = bf16[64,2048]{1,0:T(8,128)(2,1)S(1)} collective-permute-done((bf16[64,2048]{1,0:T(8,128)(2,1)S(1)}, bf16[64,2048]{1,0:T(8,128)(2,1)S(1)}, u32[]{:S(2)}, u32[]{:S(2)}) %collective-permute-start.25) | collective-permute-done | bytes 262176 | tf_op jit(solution)/shard_map/ppermute | solution.py:55
  97.1 0.7 collective-permute-start.27
  97.9 0.9 collective-permute-start.29
  98.8 3.9 %collective-permute-done.30 = bf16[64,2048]{1,0:T(8,128)(2,1)S(1)} collective-permute-done((bf16[64,2048]{1,0:T(8,128)(2,1)S(1)}, bf16[64,2048]{1,0:T(8,128)(2,1)S(1)}, u32[]{:S(2)}, u32[]{:S(2)}) %collective-permute-start.30) | collective-permute-done | bytes 262176 | tf_op jit(solution)/shard_map/ppermute | solution.py:55
  102.8 0.7 collective-permute-start.31
  103.5 0.9 collective-permute-start.33
  104.4 4.5 %collective-permute-done.29.refs_3_ = bf16[64,2048]{1,0:T(8,128)(2,1)S(1)} collective-permute-done((bf16[64,2048]{1,0:T(8,128)(2,1)S(1)}, bf16[64,2048]{1,0:T(8,128)(2,1)S(1)}, u32[]{:S(2)}, u32[]{:S(2)}) %collective-permute-start.29) | collective-permute-done | bytes 262176 | tf_op jit(solution)/shard_map/ppermute | solution.py:55
  109.0 1.5 %collective-permute-done.31 = bf16[64,2048]{1,0:T(8,128)(2,1)S(1)} collective-permute-done((bf16[64,2048]{1,0:T(8,128)(2,1)S(1)}, bf16[64,2048]{1,0:T(8,128)(2,1)S(1)}, u32[]{:S(2)}, u32[]{:S(2)}) %collective-permute-start.31) | collective-permute-done | bytes 262176 | tf_op jit(solution)/shard_map/ppermute | solution.py:55
  110.6 0.9 collective-permute-done.33
  111.5 0.8 pad_maximum_fusion
  (49 shorter events, 2.8 us)
Async XLA Ops:
  1.1 8.5 %collective-permute-start.4 = (bf16[256,512]{1,0:T(8,128)(2,1)S(1)}, bf16[256,512]{1,0:T(8,128)(2,1)S(1)}, u32[]{:S(2)}, u32[]{:S(2)}) collective-permute-start(bf16[256,512]{1,0:T(8,128)(2,1)S(1)} %get-tuple-element.63.refs_3_), channel_id=1, source_target_pairs={{0,1},{2,0},{4,2},{6,4},{7,6},{5,7},{3,5},{1,3},{8,9},{10,8},{12,1... | collective-permute-start | bytes 786440 | tf_op jit(solution)/shard_map/ppermute | solution.py:55
  3.1 8.0 %copy-start.4 = (f32[512,4]{0,1:T(4,128)S(1)}, f32[512,4]{0,1:T(4,128)}, u32[]{:S(2)}) copy-start(f32[512,4]{0,1:T(4,128)} %param.18) | copy-start | bytes 24580
  3.1 7.8 %collective-permute-start = (bf16[256,512]{1,0:T(8,128)(2,1)S(1)}, bf16[256,512]{1,0:T(8,128)(2,1)S(1)}, u32[]{:S(2)}, u32[]{:S(2)}) collective-permute-start(bf16[256,512]{1,0:T(8,128)(2,1)S(1)} %get-tuple-element.60.refs_0_), channel_id=1, source_target_pairs={{0,2},{2,4},{4,6},{6,7},{7,5},{5,3},{3,1},{1,0},{8,10},{10,12},{12... | collective-permute-start | bytes 786440 | tf_op jit(solution)/shard_map/ppermute | solution.py:55
  3.3 12.3 %collective-permute-start.3 = (bf16[256,512]{1,0:T(8,128)(2,1)S(1)}, bf16[256,512]{1,0:T(8,128)(2,1)S(1)}, u32[]{:S(2)}, u32[]{:S(2)}) collective-permute-start(bf16[256,512]{1,0:T(8,128)(2,1)S(1)} %get-tuple-element.63.refs_3_), channel_id=1, source_target_pairs={{0,2},{2,4},{4,6},{6,7},{7,5},{5,3},{3,1},{1,0},{8,10},{10,12},{12... | collective-permute-start | bytes 786440 | tf_op jit(solution)/shard_map/ppermute | solution.py:55
  4.7 11.4 %collective-permute-start.2 = (bf16[256,512]{1,0:T(8,128)(2,1)S(1)}, bf16[256,512]{1,0:T(8,128)(2,1)S(1)}, u32[]{:S(2)}, u32[]{:S(2)}) collective-permute-start(bf16[256,512]{1,0:T(8,128)(2,1)S(1)} %get-tuple-element.60.refs_0_), channel_id=1, source_target_pairs={{0,1},{2,0},{4,2},{6,4},{7,6},{5,7},{3,5},{1,3},{8,9},{10,8},{12,1... | collective-permute-start | bytes 786440 | tf_op jit(solution)/shard_map/ppermute | solution.py:55
  9.6 10.9 %collective-permute-start.8 = (bf16[256,512]{1,0:T(8,128)(2,1)S(1)}, bf16[256,512]{1,0:T(8,128)(2,1)S(1)}, u32[]{:S(2)}, u32[]{:S(2)}) collective-permute-start(bf16[256,512]{1,0:T(8,128)(2,1)S(1)} %collective-permute-done.4.refs_5_), channel_id=1, source_target_pairs={{0,1},{2,0},{4,2},{6,4},{7,6},{5,7},{3,5},{1,3},{8,9},{10,8},{12,1... | collective-permute-start | bytes 786440 | tf_op jit(solution)/shard_map/ppermute | solution.py:55
  10.9 10.3 %collective-permute-start.1 = (bf16[256,512]{1,0:T(8,128)(2,1)S(1)}, bf16[256,512]{1,0:T(8,128)(2,1)S(1)}, u32[]{:S(2)}, u32[]{:S(2)}) collective-permute-start(bf16[256,512]{1,0:T(8,128)(2,1)S(1)} %collective-permute-done.refs_1_), channel_id=1, source_target_pairs={{0,2},{2,4},{4,6},{6,7},{7,5},{5,3},{3,1},{1,0},{8,10},{10,12},{12... | collective-permute-start | bytes 786440 | tf_op jit(solution)/shard_map/ppermute | solution.py:55
  11.1 8.6 %collective-permute-start.5 = (f32[4,512]{1,0:T(4,128)S(1)}, f32[4,512]{1,0:T(4,128)S(1)}, u32[]{:S(2)}, u32[]{:S(2)}) collective-permute-start(f32[4,512]{1,0:T(4,128)S(1)} %bitcast.1), channel_id=1, source_target_pairs={{0,8},{8,0},{16,24},{24,16},{1,9},{9,1},{17,25},{25,17},{2,10},{10... | collective-permute-start | bytes 24584 | tf_op jit(solution)/shard_map/ppermute | solution.py:544
  15.6 11.2 %collective-permute-start.13 = (bf16[256,512]{1,0:T(8,128)(2,1)S(1)}, bf16[256,512]{1,0:T(8,128)(2,1)S(1)}, u32[]{:S(2)}, u32[]{:S(2)}) collective-permute-start(bf16[256,512]{1,0:T(8,128)(2,1)S(1)} %collective-permute-done.3.refs_4_), channel_id=1, source_target_pairs={{0,2},{2,4},{4,6},{6,7},{7,5},{5,3},{3,1},{1,0},{8,10},{10,12},{12... | collective-permute-start | bytes 786440 | tf_op jit(solution)/shard_map/ppermute | solution.py:55
  16.1 10.8 %collective-permute-start.11 = (bf16[256,512]{1,0:T(8,128)(2,1)S(1)}, bf16[256,512]{1,0:T(8,128)(2,1)S(1)}, u32[]{:S(2)}, u32[]{:S(2)}) collective-permute-start(bf16[256,512]{1,0:T(8,128)(2,1)S(1)} %collective-permute-done.2.refs_2_), channel_id=1, source_target_pairs={{0,1},{2,0},{4,2},{6,4},{7,6},{5,7},{3,5},{1,3},{8,9},{10,8},{12,1... | collective-permute-start | bytes 786440 | tf_op jit(solution)/shard_map/ppermute | solution.py:55
  21.2 10.3 %collective-permute-start.9 = (bf16[256,512]{1,0:T(8,128)(2,1)S(1)}, bf16[256,512]{1,0:T(8,128)(2,1)S(1)}, u32[]{:S(2)}, u32[]{:S(2)}) collective-permute-start(bf16[256,512]{1,0:T(8,128)(2,1)S(1)} %collective-permute-done.8.refs_3_), channel_id=1, source_target_pairs={{0,1},{2,0},{4,2},{6,4},{7,6},{5,7},{3,5},{1,3},{8,9},{10,8},{12,1... | collective-permute-start | bytes 786440 | tf_op jit(solution)/shard_map/ppermute | solution.py:55
  22.5 10.2 %collective-permute-start.6 = (bf16[256,512]{1,0:T(8,128)(2,1)S(1)}, bf16[256,512]{1,0:T(8,128)(2,1)S(1)}, u32[]{:S(2)}, u32[]{:S(2)}) collective-permute-start(bf16[256,512]{1,0:T(8,128)(2,1)S(1)} %collective-permute-done.1.refs_0_), channel_id=1, source_target_pairs={{0,2},{2,4},{4,6},{6,7},{7,5},{5,3},{3,1},{1,0},{8,10},{10,12},{12... | collective-permute-start | bytes 786440 | tf_op jit(solution)/shard_map/ppermute | solution.py:55
  26.9 11.2 %collective-permute-start.14 = (bf16[256,512]{1,0:T(8,128)(2,1)S(1)}, bf16[256,512]{1,0:T(8,128)(2,1)S(1)}, u32[]{:S(2)}, u32[]{:S(2)}) collective-permute-start(bf16[256,512]{1,0:T(8,128)(2,1)S(1)} %collective-permute-done.13.refs_2_), channel_id=1, source_target_pairs={{0,2},{2,4},{4,6},{6,7},{7,5},{5,3},{3,1},{1,0},{8,10},{10,12},{12... | collective-permute-start | bytes 786440 | tf_op jit(solution)/shard_map/ppermute | solution.py:55
  27.3 10.8 %collective-permute-start.12 = (bf16[256,512]{1,0:T(8,128)(2,1)S(1)}, bf16[256,512]{1,0:T(8,128)(2,1)S(1)}, u32[]{:S(2)}, u32[]{:S(2)}) collective-permute-start(bf16[256,512]{1,0:T(8,128)(2,1)S(1)} %collective-permute-done.11.refs_1_), channel_id=1, source_target_pairs={{0,1},{2,0},{4,2},{6,4},{7,6},{5,7},{3,5},{1,3},{8,9},{10,8},{12,1... | collective-permute-start | bytes 786440 | tf_op jit(solution)/shard_map/ppermute | solution.py:55
  31.6 11.2 %collective-permute-start.10 = (bf16[256,512]{1,0:T(8,128)(2,1)S(1)}, bf16[256,512]{1,0:T(8,128)(2,1)S(1)}, u32[]{:S(2)}, u32[]{:S(2)}) collective-permute-start(bf16[256,512]{1,0:T(8,128)(2,1)S(1)} %collective-permute-done.9.refs_3_), channel_id=1, source_target_pairs={{0,1},{2,0},{4,2},{6,4},{7,6},{5,7},{3,5},{1,3},{8,9},{10,8},{12,1... | collective-permute-start | bytes 786440 | tf_op jit(solution)/shard_map/ppermute | solution.py:55
  32.7 11.0 %collective-permute-start.7 = (bf16[256,512]{1,0:T(8,128)(2,1)S(1)}, bf16[256,512]{1,0:T(8,128)(2,1)S(1)}, u32[]{:S(2)}, u32[]{:S(2)}) collective-permute-start(bf16[256,512]{1,0:T(8,128)(2,1)S(1)} %collective-permute-done.6.refs_0_), channel_id=1, source_target_pairs={{0,2},{2,4},{4,6},{6,7},{7,5},{5,3},{3,1},{1,0},{8,10},{10,12},{12... | collective-permute-start | bytes 786440 | tf_op jit(solution)/shard_map/ppermute | solution.py:55
  43.7 5.5 %copy-start.1 = (f32[4,128,256]{2,1,0:T(8,128)S(1)}, f32[4,128,256]{2,1,0:T(8,128)}, u32[]{:S(2)}) copy-start(f32[4,128,256]{2,1,0:T(8,128)} %gate_ref.5) | copy-start | bytes 1572868
  43.7 5.6 %copy-start.2 = (f32[4,128,256]{2,1,0:T(8,128)S(1)}, f32[4,128,256]{2,1,0:T(8,128)}, u32[]{:S(2)}) copy-start(f32[4,128,256]{2,1,0:T(8,128)} %up_ref.5) | copy-start | bytes 1572868
  43.7 5.6 %copy-start.3 = (f32[4,256,128]{2,1,0:T(8,128)S(1)}, f32[4,256,128]{2,1,0:T(8,128)}, u32[]{:S(2)}) copy-start(f32[4,256,128]{2,1,0:T(8,128)} %down_ref.5) | copy-start | bytes 1572868
  44.2 6.5 %collective-permute-start.16 = (bf16[2,512,256]{2,1,0:T(8,128)(2,1)S(1)}, bf16[2,512,256]{2,1,0:T(8,128)(2,1)S(1)}, u32[]{:S(2)}, u32[]{:S(2)}) collective-permute-start(bf16[2,512,256]{2,1,0:T(8,128)(2,1)S(1)} %get-tuple-element.79), channel_id=1, source_target_pairs={{0,8},{8,0},{16,24},{24,16},{1,9},{9,1},{17,25},{25,17},{2,10},{10... | collective-permute-start | bytes 1572872 | tf_op jit(solution)/shard_map/ppermute | solution.py:544
  46.2 11.8 %collective-permute-start.15 = (bf16[2,512,256]{2,1,0:T(8,128)(2,1)S(1)}, bf16[2,512,256]{2,1,0:T(8,128)(2,1)S(1)}, u32[]{:S(2)}, u32[]{:S(2)}) collective-permute-start(bf16[2,512,256]{2,1,0:T(8,128)(2,1)S(1)} %get-tuple-element.79), channel_id=1, source_target_pairs={{8,16},{9,17},{10,18},{11,19},{12,20},{13,21},{14,22},{15,23}} | collective-permute-start | bytes 1572872 | tf_op jit(solution)/shard_map/ppermute | solution.py:578
  52.2 11.6 %collective-permute-start.18 = (bf16[2,3,128,256]{3,2,1,0:T(8,128)(2,1)S(1)}, bf16[2,3,128,256]{3,2,1,0:T(8,128)(2,1)S(1)}, u32[]{:S(2)}, u32[]{:S(2)}) collective-permute-start(bf16[2,3,128,256]{3,2,1,0:T(8,128)(2,1)S(1)} %get-tuple-element.83), channel_id=1, source_target_pairs={{0,16},{8,24},{16,0},{24,8},{1,17},{9,25},{17,1},{25,9},{2,18},{10... | collective-permute-start | bytes 1179656 | tf_op jit(solution)/shard_map/ppermute | solution.py:544
  52.7 11.1 %copy-start.5 = (f32[4]{0:T(128)S(1)}, f32[4]{0:T(128)}, u32[]{:S(2)}) copy-start(f32[4]{0:T(128)} %step_ref.1) | copy-start | bytes 52
  54.8 14.6 %collective-permute-start.17 = (bf16[2,512,256]{2,1,0:T(8,128)(2,1)S(1)}, bf16[2,512,256]{2,1,0:T(8,128)(2,1)S(1)}, u32[]{:S(2)}, u32[]{:S(2)}) collective-permute-start(bf16[2,512,256]{2,1,0:T(8,128)(2,1)S(1)} %get-tuple-element.81), channel_id=1, source_target_pairs={{0,8},{8,16},{16,24},{1,9},{9,17},{17,25},{2,10},{10,18},{18,26},{... | collective-permute-start | bytes 1572872 | tf_op jit(solution)/shard_map/ppermute | solution.py:592
  64.6 6.0 %copy-start = (bf16[512,4096]{1,0:T(8,128)(2,1)S(1)}, bf16[512,4096]{1,0:T(8,128)(2,1)}, u32[]{:S(2)}) copy-start(bf16[512,4096]{1,0:T(8,128)(2,1)} %w_ref.7) | copy-start | bytes 12582916
  64.6 6.0 %collective-permute-start.19 = (bf16[2,3,128,256]{3,2,1,0:T(8,128)(2,1)S(1)}, bf16[2,3,128,256]{3,2,1,0:T(8,128)(2,1)S(1)}, u32[]{:S(2)}, u32[]{:S(2)}) collective-permute-start(bf16[2,3,128,256]{3,2,1,0:T(8,128)(2,1)S(1)} %shard_map.112.net_ref), channel_id=1, source_target_pairs={{0,8},{8,0},{16,24},{24,16},{1,9},{9,1},{17,25},{25,17},{2,10},{10... | collective-permute-start | bytes 1179656 | tf_op jit(solution)/shard_map/ppermute | solution.py:544
  71.8 8.4 %collective-permute-start.20 = (bf16[64,2048]{1,0:T(8,128)(2,1)S(1)}, bf16[64,2048]{1,0:T(8,128)(2,1)S(1)}, u32[]{:S(2)}, u32[]{:S(2)}) collective-permute-start(bf16[64,2048]{1,0:T(8,128)(2,1)S(1)} %get-tuple-element.85), channel_id=1, source_target_pairs={{0,2},{2,4},{4,6},{6,7},{7,5},{5,3},{3,1},{1,0},{8,10},{10,12},{12... | collective-permute-start | bytes 786440 | tf_op jit(solution)/shard_map/ppermute | solution.py:55
  72.5 8.4 %collective-permute-start.22 = (bf16[64,2048]{1,0:T(8,128)(2,1)S(1)}, bf16[64,2048]{1,0:T(8,128)(2,1)S(1)}, u32[]{:S(2)}, u32[]{:S(2)}) collective-permute-start(bf16[64,2048]{1,0:T(8,128)(2,1)S(1)} %get-tuple-element.89), channel_id=1, source_target_pairs={{0,1},{2,0},{4,2},{6,4},{7,6},{5,7},{3,5},{1,3},{8,9},{10,8},{12,1... | collective-permute-start | bytes 786440 | tf_op jit(solution)/shard_map/ppermute | solution.py:55
  74.6 11.2 %collective-permute-start.24 = (bf16[64,2048]{1,0:T(8,128)(2,1)S(1)}, bf16[64,2048]{1,0:T(8,128)(2,1)S(1)}, u32[]{:S(2)}, u32[]{:S(2)}) collective-permute-start(bf16[64,2048]{1,0:T(8,128)(2,1)S(1)} %get-tuple-element.90), channel_id=1, source_target_pairs={{0,2},{2,4},{4,6},{6,7},{7,5},{5,3},{3,1},{1,0},{8,10},{10,12},{12... | collective-permute-start | bytes 786440 | tf_op jit(solution)/shard_map/ppermute | solution.py:55
  75.3 11.3 %collective-permute-start.26 = (bf16[64,2048]{1,0:T(8,128)(2,1)S(1)}, bf16[64,2048]{1,0:T(8,128)(2,1)S(1)}, u32[]{:S(2)}, u32[]{:S(2)}) collective-permute-start(bf16[64,2048]{1,0:T(8,128)(2,1)S(1)} %get-tuple-element.91), channel_id=1, source_target_pairs={{0,1},{2,0},{4,2},{6,4},{7,6},{5,7},{3,5},{1,3},{8,9},{10,8},{12,1... | collective-permute-start | bytes 786440 | tf_op jit(solution)/shard_map/ppermute | solution.py:55
  80.3 11.2 %collective-permute-start.21 = (bf16[64,2048]{1,0:T(8,128)(2,1)S(1)}, bf16[64,2048]{1,0:T(8,128)(2,1)S(1)}, u32[]{:S(2)}, u32[]{:S(2)}) collective-permute-start(bf16[64,2048]{1,0:T(8,128)(2,1)S(1)} %add_convert_fusion.11), channel_id=1, source_target_pairs={{0,2},{2,4},{4,6},{6,7},{7,5},{5,3},{3,1},{1,0},{8,10},{10,12},{12... | collective-permute-start | bytes 786440 | tf_op jit(solution)/shard_map/ppermute | solution.py:55
  81.1 11.2 %collective-permute-start.23 = (bf16[64,2048]{1,0:T(8,128)(2,1)S(1)}, bf16[64,2048]{1,0:T(8,128)(2,1)S(1)}, u32[]{:S(2)}, u32[]{:S(2)}) collective-permute-start(bf16[64,2048]{1,0:T(8,128)(2,1)S(1)} %add_convert_fusion.10), channel_id=1, source_target_pairs={{0,1},{2,0},{4,2},{6,4},{7,6},{5,7},{3,5},{1,3},{8,9},{10,8},{12,1... | collective-permute-start | bytes 786440 | tf_op jit(solution)/shard_map/ppermute | solution.py:55
  85.9 11.2 %collective-permute-start.25 = (bf16[64,2048]{1,0:T(8,128)(2,1)S(1)}, bf16[64,2048]{1,0:T(8,128)(2,1)S(1)}, u32[]{:S(2)}, u32[]{:S(2)}) collective-permute-start(bf16[64,2048]{1,0:T(8,128)(2,1)S(1)} %add_convert_fusion.9), channel_id=1, source_target_pairs={{0,2},{2,4},{4,6},{6,7},{7,5},{5,3},{3,1},{1,0},{8,10},{10,12},{12... | collective-permute-start | bytes 786440 | tf_op jit(solution)/shard_map/ppermute | solution.py:55
  86.7 11.2 %collective-permute-start.28 = (bf16[64,2048]{1,0:T(8,128)(2,1)S(1)}, bf16[64,2048]{1,0:T(8,128)(2,1)S(1)}, u32[]{:S(2)}, u32[]{:S(2)}) collective-permute-start(bf16[64,2048]{1,0:T(8,128)(2,1)S(1)} %add_convert_fusion.5), channel_id=1, source_target_pairs={{0,1},{2,0},{4,2},{6,4},{7,6},{5,7},{3,5},{1,3},{8,9},{10,8},{12,1... | collective-permute-start | bytes 786440 | tf_op jit(solution)/shard_map/ppermute | solution.py:55
  91.5 11.2 %collective-permute-start.30 = (bf16[64,2048]{1,0:T(8,128)(2,1)S(1)}, bf16[64,2048]{1,0:T(8,128)(2,1)S(1)}, u32[]{:S(2)}, u32[]{:S(2)}) collective-permute-start(bf16[64,2048]{1,0:T(8,128)(2,1)S(1)} %add_convert_fusion.6), channel_id=1, source_target_pairs={{0,2},{2,4},{4,6},{6,7},{7,5},{5,3},{3,1},{1,0},{8,10},{10,12},{12... | collective-permute-start | bytes 786440 | tf_op jit(solution)/shard_map/ppermute | solution.py:55
  92.3 11.2 %collective-permute-start.32 = (bf16[64,2048]{1,0:T(8,128)(2,1)S(1)}, bf16[64,2048]{1,0:T(8,128)(2,1)S(1)}, u32[]{:S(2)}, u32[]{:S(2)}) collective-permute-start(bf16[64,2048]{1,0:T(8,128)(2,1)S(1)} %add_convert_fusion.7), channel_id=1, source_target_pairs={{0,1},{2,0},{4,2},{6,4},{7,6},{5,7},{3,5},{1,3},{8,9},{10,8},{12,1... | collective-permute-start | bytes 786440 | tf_op jit(solution)/shard_map/ppermute | solution.py:55
  97.1 11.8 %collective-permute-start.27 = (bf16[64,2048]{1,0:T(8,128)(2,1)S(1)}, bf16[64,2048]{1,0:T(8,128)(2,1)S(1)}, u32[]{:S(2)}, u32[]{:S(2)}) collective-permute-start(bf16[64,2048]{1,0:T(8,128)(2,1)S(1)} %add_convert_fusion.8), channel_id=1, source_target_pairs={{0,2},{2,4},{4,6},{6,7},{7,5},{5,3},{3,1},{1,0},{8,10},{10,12},{12... | collective-permute-start | bytes 786440 | tf_op jit(solution)/shard_map/ppermute | solution.py:55
  97.9 11.0 %collective-permute-start.29 = (bf16[64,2048]{1,0:T(8,128)(2,1)S(1)}, bf16[64,2048]{1,0:T(8,128)(2,1)S(1)}, u32[]{:S(2)}, u32[]{:S(2)}) collective-permute-start(bf16[64,2048]{1,0:T(8,128)(2,1)S(1)} %add_convert_fusion.4), channel_id=1, source_target_pairs={{0,1},{2,0},{4,2},{6,4},{7,6},{5,7},{3,5},{1,3},{8,9},{10,8},{12,1... | collective-permute-start | bytes 786440 | tf_op jit(solution)/shard_map/ppermute | solution.py:55
  102.8 7.8 %collective-permute-start.31 = (bf16[64,2048]{1,0:T(8,128)(2,1)S(1)}, bf16[64,2048]{1,0:T(8,128)(2,1)S(1)}, u32[]{:S(2)}, u32[]{:S(2)}) collective-permute-start(bf16[64,2048]{1,0:T(8,128)(2,1)S(1)} %add_convert_fusion.3), channel_id=1, source_target_pairs={{0,2},{2,4},{4,6},{6,7},{7,5},{5,3},{3,1},{1,0},{8,10},{10,12},{12... | collective-permute-start | bytes 786440 | tf_op jit(solution)/shard_map/ppermute | solution.py:55
  103.5 7.9 %collective-permute-start.33 = (bf16[64,2048]{1,0:T(8,128)(2,1)S(1)}, bf16[64,2048]{1,0:T(8,128)(2,1)S(1)}, u32[]{:S(2)}, u32[]{:S(2)}) collective-permute-start(bf16[64,2048]{1,0:T(8,128)(2,1)S(1)} %add_convert_fusion.1), channel_id=1, source_target_pairs={{0,1},{2,0},{4,2},{6,4},{7,6},{5,7},{3,5},{1,3},{8,9},{10,8},{12,1... | collective-permute-start | bytes 786440 | tf_op jit(solution)/shard_map/ppermute | solution.py:55

commit v15 on v14

--- a/solution.py
+++ b/solution.py
@@ -560,13 +560,16 @@
     held = [{1: piece, -1: piece} for piece in own]
     sums, done = None, 0
     for step in range(1, steps + 1):
-        after = {2: weights[0], 3: (sums, rate_beside)}.get(step)
         for c in range(CHUNKS):
             last = (1,) if c % 2 == 0 else (-1,)
+            after = {(2, 0): weights[0], (2, 1): weights[0], (3, 1): (sums, rate_beside)}.get((step, c))
             held[c] = gather_step(held[c], (1, -1) if step < steps else last, after)
             chunks[c] += held[c].values()
         if step > 1:
             known = [chunk[: 2 * step - 1] for chunk in chunks]
+            if step < steps:
+                ahead = (known[0][done], *chunks[0][2 * step - 1 :])
+                known[0][done] = lax.optimization_barrier(ahead)[0]
             sums = accumulate(known, done, 2 * step - 1, weights, sums)
             done = 2 * step - 1
     filled = ()

time: 112 us -> 115 us (1.027)
  starting transfers between devices: 31.4 us -> 34 us
    ppermute x4, starting transfers between devices: 4.43 us -> 6.01 us  [swap(): lax.ppermute(value, 'tok', [(index, index ^ bit) for index in range(count)])]
  transfers between devices with their start and end apart: 34 -> 34, of which waited for: 19 -> 17; matrix products, arithmetic and copies ran while one was open for 1% -> 1% of each run, Pallas kernels for 22% -> 22%
where the time goes in v15:
time: 115 us
  waiting for transfers between devices  51 us (44%)
  starting transfers between devices  34 us (30%)
  Pallas kernels  27.9 us (24%)
  other arithmetic  1.56 us (1%)
    ppermute x28, waiting for transfers between devices, ring_send(): lax.ppermute(value, 'head', [(order[i], order[(i + step) % count]) for i...  41.3 us
    ppermute x28, starting transfers between devices, ring_send(): lax.ppermute(value, 'head', [(order[i], order[(i + step) % count]) for i...  23 us
    pallas_call x4, Pallas kernels, accumulate(): call(body, [WHOLE] * len(args), WHOLE, jax.ShapeDtypeStruct((parts, total...  6.72 us
    ppermute x4, starting transfers between devices, swap(): lax.ppermute(value, 'tok', [(index, index ^ bit) for index in range(count)])  6.01 us
    pallas_call x4, Pallas kernels, partial_out(): call(body, [WHOLE] * 5 + [AFTER] * len(after), [WHOLE] * (2 * count), [ja...  5.18 us
    pallas_call x1, Pallas kernels, load(): call(body, [IN_HBM] * count, [WHOLE] * count, [jax.ShapeDtypeStruct(array...  4.78 us
    ppermute x4, waiting for transfers between devices, swap(): lax.ppermute(value, 'tok', [(index, index ^ bit) for index in range(count)])  4.6 us
    ppermute x1, waiting for transfers between devices, shards(): lax.ppermute(near, 'tok', [(index, index + 1) for index in range(tok_coun...  3.89 us
  transfers between devices with their start and end apart: 34, of which 17 were waited for; matrix products, arithmetic and copies ran while one was open for 1% of the time, Pallas kernels for 22%

profile of v15, /device:TPU:1, one launch (start us, length us, event | category | flops | bytes accessed | tf_op | source)
XLA Modules:
  0.0 114.9 jit_solution(1448860255876430384)
XLA Ops:
  0.0 1.0 shard_map.100
  1.1 2.2 %collective-permute-start = (bf16[256,512]{1,0:T(8,128)(2,1)S(1)}, bf16[256,512]{1,0:T(8,128)(2,1)S(1)}, u32[]{:S(2)}, u32[]{:S(2)}) collective-permute-start(bf16[256,512]{1,0:T(8,128)(2,1)S(1)} %get-tuple-element.66.refs_0_), channel_id=1, source_target_pairs={{0,2},{2,4},{4,6},{6,7},{7,5},{5,3},{3,1},{1,0},{8,10},{10,12},{12... | collective-permute-start | bytes 786440 | tf_op jit(solution)/shard_map/ppermute | solution.py:55
  3.2 1.4 %collective-permute-start.4 = (bf16[256,512]{1,0:T(8,128)(2,1)S(1)}, bf16[256,512]{1,0:T(8,128)(2,1)S(1)}, u32[]{:S(2)}, u32[]{:S(2)}) collective-permute-start(bf16[256,512]{1,0:T(8,128)(2,1)S(1)} %get-tuple-element.63.refs_3_), channel_id=1, source_target_pairs={{0,1},{2,0},{4,2},{6,4},{7,6},{5,7},{3,5},{1,3},{8,9},{10,8},{12,1... | collective-permute-start | bytes 786440 | tf_op jit(solution)/shard_map/ppermute | solution.py:55
  4.7 4.8 %shard_map.101 = (bf16[4096,512]{1,0:T(8,128)(2,1)S(1)}, bf16[4096,512]{1,0:T(8,128)(2,1)S(1)}, bf16[4096,512]{1,0:T(8,128)(2,1)S(1)}) custom-call(bf16[4096,512]{1,0:T(8,128)(2,1)} %refs_0_.1, bf16[4096,512]{1,0:T(8,128)(2,1)} %refs_1_.1, bf16[4096,512]{1,0:T(8,128)(2,1)} %refs_2_.1), custom_call_target="tpu_custom_call" | custom-call | bytes 25165824 | tf_op jit(solution)/shard_map/pallas_call | solution.py:111
  9.5 1.5 %collective-permute-start.1 = (bf16[256,512]{1,0:T(8,128)(2,1)S(1)}, bf16[256,512]{1,0:T(8,128)(2,1)S(1)}, u32[]{:S(2)}, u32[]{:S(2)}) collective-permute-start(bf16[256,512]{1,0:T(8,128)(2,1)S(1)} %collective-permute-done.refs_1_), channel_id=1, source_target_pairs={{0,2},{2,4},{4,6},{6,7},{7,5},{5,3},{3,1},{1,0},{8,10},{10,12},{12... | collective-permute-start | bytes 786440 | tf_op jit(solution)/shard_map/ppermute | solution.py:55
  11.1 4.7 %collective-permute-done.4.refs_5_ = bf16[256,512]{1,0:T(8,128)(2,1)S(1)} collective-permute-done((bf16[256,512]{1,0:T(8,128)(2,1)S(1)}, bf16[256,512]{1,0:T(8,128)(2,1)S(1)}, u32[]{:S(2)}, u32[]{:S(2)}) %collective-permute-start.4) | collective-permute-done | bytes 262176 | tf_op jit(solution)/shard_map/ppermute | solution.py:55
  15.7 0.3 collective-permute-start.5
  16.0 3.0 %collective-permute-start.9 = (f32[4,512]{1,0:T(4,128)S(1)}, f32[4,512]{1,0:T(4,128)S(1)}, u32[]{:S(2)}, u32[]{:S(2)}) collective-permute-start(f32[4,512]{1,0:T(4,128)S(1)} %bitcast.1), channel_id=1, source_target_pairs={{0,8},{8,0},{16,24},{24,16},{1,9},{9,1},{17,25},{25,17},{2,10},{10... | collective-permute-start | bytes 24584 | tf_op jit(solution)/shard_map/ppermute | solution.py:544
  19.0 1.7 %collective-permute-start.13 = (bf16[256,512]{1,0:T(8,128)(2,1)S(1)}, bf16[256,512]{1,0:T(8,128)(2,1)S(1)}, u32[]{:S(2)}, u32[]{:S(2)}) collective-permute-start(bf16[256,512]{1,0:T(8,128)(2,1)S(1)} %collective-permute-done.8.refs_4_), channel_id=1, source_target_pairs={{0,2},{2,4},{4,6},{6,7},{7,5},{5,3},{3,1},{1,0},{8,10},{10,12},{12... | collective-permute-start | bytes 786440 | tf_op jit(solution)/shard_map/ppermute | solution.py:55
  20.8 0.5 collective-permute-done.7.refs_1_
  21.3 1.3 %collective-permute-start.2 = (bf16[256,512]{1,0:T(8,128)(2,1)S(1)}, bf16[256,512]{1,0:T(8,128)(2,1)S(1)}, u32[]{:S(2)}, u32[]{:S(2)}) collective-permute-start(bf16[256,512]{1,0:T(8,128)(2,1)S(1)} %collective-permute-done.1.refs_0_), channel_id=1, source_target_pairs={{0,2},{2,4},{4,6},{6,7},{7,5},{5,3},{3,1},{1,0},{8,10},{10,12},{12... | collective-permute-start | bytes 786440 | tf_op jit(solution)/shard_map/ppermute | solution.py:55
  22.8 2.6 %shard_map.102.refs_7_ = f32[3,512,512]{2,1,0:T(8,128)S(1)} custom-call(bf16[256,512]{1,0:T(8,128)(2,1)S(1)} %get-tuple-element.66.refs_0_, bf16[256,512]{1,0:T(8,128)(2,1)S(1)} %collective-permute-done.refs_1_, bf16[256,512]{1,0:T(8,128)(2,1)S(1)} %collective-permute-done.6.refs_2_, bf16[256,512]{1,0:T(8,128)(2,1)S(1)} %get-tuple-element.63.refs_3_, ...), custom_call_target="tpu_custom_call" | custom-call | flops 2415919104 | bytes 12582912 | tf_op jit(solution)/shard_map/pallas_call | solution.py:180
  25.4 1.5 %collective-permute-done.5.refs_3_ = bf16[256,512]{1,0:T(8,128)(2,1)S(1)} collective-permute-done((bf16[256,512]{1,0:T(8,128)(2,1)S(1)}, bf16[256,512]{1,0:T(8,128)(2,1)S(1)}, u32[]{:S(2)}, u32[]{:S(2)}) %collective-permute-start.5) | collective-permute-done | bytes 262176 | tf_op jit(solution)/shard_map/ppermute | solution.py:55
  26.9 0.3 collective-permute-start.10
  27.3 1.4 %collective-permute-start.14 = (bf16[256,512]{1,0:T(8,128)(2,1)S(1)}, bf16[256,512]{1,0:T(8,128)(2,1)S(1)}, u32[]{:S(2)}, u32[]{:S(2)}) collective-permute-start(bf16[256,512]{1,0:T(8,128)(2,1)S(1)} %collective-permute-done.13.refs_2_), channel_id=1, source_target_pairs={{0,2},{2,4},{4,6},{6,7},{7,5},{5,3},{3,1},{1,0},{8,10},{10,12},{12... | collective-permute-start | bytes 786440 | tf_op jit(solution)/shard_map/ppermute | solution.py:55
  28.7 4.2 %collective-permute-done.2.refs_0_ = bf16[256,512]{1,0:T(8,128)(2,1)S(1)} collective-permute-done((bf16[256,512]{1,0:T(8,128)(2,1)S(1)}, bf16[256,512]{1,0:T(8,128)(2,1)S(1)}, u32[]{:S(2)}, u32[]{:S(2)}) %collective-permute-start.2) | collective-permute-done | bytes 262176 | tf_op jit(solution)/shard_map/ppermute | solution.py:55
  32.9 1.4 %collective-permute-start.3 = (bf16[256,512]{1,0:T(8,128)(2,1)S(1)}, bf16[256,512]{1,0:T(8,128)(2,1)S(1)}, u32[]{:S(2)}, u32[]{:S(2)}) collective-permute-start(bf16[256,512]{1,0:T(8,128)(2,1)S(1)} %collective-permute-done.2.refs_0_), channel_id=1, source_target_pairs={{0,2},{2,4},{4,6},{6,7},{7,5},{5,3},{3,1},{1,0},{8,10},{10,12},{12... | collective-permute-start | bytes 786440 | tf_op jit(solution)/shard_map/ppermute | solution.py:55
  34.3 3.9 %collective-permute-done.10.refs_3_ = bf16[256,512]{1,0:T(8,128)(2,1)S(1)} collective-permute-done((bf16[256,512]{1,0:T(8,128)(2,1)S(1)}, bf16[256,512]{1,0:T(8,128)(2,1)S(1)}, u32[]{:S(2)}, u32[]{:S(2)}) %collective-permute-start.10) | collective-permute-done | bytes 262176 | tf_op jit(solution)/shard_map/ppermute | solution.py:55
  38.2 0.2 collective-permute-start.11
  38.4 1.8 %shard_map.103.refs_7_ = f32[3,512,512]{2,1,0:T(8,128)S(1)} custom-call(bf16[256,512]{1,0:T(8,128)(2,1)S(1)} %collective-permute-done.1.refs_0_, bf16[256,512]{1,0:T(8,128)(2,1)S(1)} %collective-permute-done.7.refs_1_, bf16[256,512]{1,0:T(8,128)(2,1)S(1)} %collective-permute-done.13.refs_2_, ...), custom_call_target="tpu_custom_call", output_to_operand_aliasing={{}: (7, {})} | custom-call | flops 1610612736 | bytes 10485760 | tf_op jit(solution)/shard_map/pallas_call | solution.py:180
  40.3 1.8 %shard_map.104.refs_3_.refs_2_ = f32[3,512,512]{2,1,0:T(8,128)S(1)} custom-call(bf16[256,512]{1,0:T(8,128)(2,1)S(1)} %collective-permute-done.2.refs_0_, bf16[256,512]{1,0:T(8,128)(2,1)S(1)} %collective-permute-done.12.refs_1_, bf16[256,512]{1,0:T(8,128)(2,1)S(1)} %collective-permute-done.14.refs_2_, ...), custom_call_target="tpu_custom_call", output_to_operand_aliasing={{}: (7, {})} | custom-call | flops 1610612736 | bytes 10485760 | tf_op jit(solution)/shard_map/pallas_call | solution.py:180
  42.1 2.0 %collective-permute-done.11.refs_1_.piece_ref = bf16[256,512]{1,0:T(8,128)(2,1)S(1)} collective-permute-done((bf16[256,512]{1,0:T(8,128)(2,1)S(1)}, bf16[256,512]{1,0:T(8,128)(2,1)S(1)}, u32[]{:S(2)}, u32[]{:S(2)}) %collective-permute-start.11) | collective-permute-done | bytes 262176 | tf_op jit(solution)/shard_map/ppermute | solution.py:55
  44.1 0.5 shard_map.106
  44.7 0.5 shard_map.107
  45.2 2.9 %collective-permute-start.16 = (bf16[2,512,256]{2,1,0:T(8,128)(2,1)S(1)}, bf16[2,512,256]{2,1,0:T(8,128)(2,1)S(1)}, u32[]{:S(2)}, u32[]{:S(2)}) collective-permute-start(bf16[2,512,256]{2,1,0:T(8,128)(2,1)S(1)} %get-tuple-element.79), channel_id=1, source_target_pairs={{0,8},{8,0},{16,24},{24,16},{1,9},{9,1},{17,25},{25,17},{2,10},{10... | collective-permute-start | bytes 1572872 | tf_op jit(solution)/shard_map/ppermute | solution.py:544
  48.1 3.1 %collective-permute-start.15 = (bf16[2,512,256]{2,1,0:T(8,128)(2,1)S(1)}, bf16[2,512,256]{2,1,0:T(8,128)(2,1)S(1)}, u32[]{:S(2)}, u32[]{:S(2)}) collective-permute-start(bf16[2,512,256]{2,1,0:T(8,128)(2,1)S(1)} %get-tuple-element.79), channel_id=1, source_target_pairs={{8,16},{9,17},{10,18},{11,19},{12,20},{13,21},{14,22},{15,23}} | collective-permute-start | bytes 1572872 | tf_op jit(solution)/shard_map/ppermute | solution.py:581
  51.2 1.4 %shard_map.110.rest_0_ = f32[2,3,128,256]{3,2,1,0:T(8,128)S(1)} custom-call(bf16[2,512,512]{2,1,0:T(8,128)(2,1)S(1)} %get-tuple-element.76.kv_ref, f32[4,512]{1,0:T(4,128)S(1)} %bitcast.2, f32[4,128,256]{2,1,0:T(8,128)S(1)} %copy-done.1, f32[4,128,256]{2,1,0:T(8,128)S(1)} %copy-done.2, f32[4,256,128]{2,1,0:T(8,128)S(1)} %copy-done.3), custom_call_target="tpu_custom_call" | custom-call | flops 402653184 | bytes 1572864 | tf_op jit(solution)/shard_map/pallas_call | solution.py:272
  52.6 1.4 %shard_map.111 = (f32[2,3,128,256]{3,2,1,0:T(8,128)S(1)}, bf16[2,3,128,256]{3,2,1,0:T(8,128)(2,1)S(1)}) custom-call(bf16[2,512,256]{2,1,0:T(8,128)(2,1)S(1)} %collective-permute-done.16.refs_1_.kv_ref, f32[4,512]{1,0:T(4,128)S(1)} %collective-permute-done.9.rate_ref, f32[4,128,256]{2,1,0:T(8,128)S(1)} %copy-done.1, f32[4,128,256]{2,1,0:T(8,128)S(1)} %copy-done.2, ...), custom_call_target="tpu_custom_call" | custom-call | flops 402653184 | bytes 1572864 | tf_op jit(solution)/shard_map/pallas_call | solution.py:272
  54.1 0.4 shard_map.105.q_ref
  54.6 2.1 %shard_map.108 = (f32[512,512]{1,0:T(8,128)S(1)}, f32[2,512,512]{2,1,0:T(8,128)S(1)}) custom-call(bf16[1,512,512]{2,1,0:T(8,128)(2,1)S(1)} %shard_map.105.q_ref, bf16[2,512,512]{2,1,0:T(8,128)(2,1)S(1)} %get-tuple-element.76.kv_ref), custom_call_target="tpu_custom_call" | custom-call | flops 402653184 | bytes 2097152 | tf_op jit(solution)/shard_map/pallas_call | solution.py:365
  56.7 1.9 %collective-permute-start.17 = (bf16[2,512,256]{2,1,0:T(8,128)(2,1)S(1)}, bf16[2,512,256]{2,1,0:T(8,128)(2,1)S(1)}, u32[]{:S(2)}, u32[]{:S(2)}) collective-permute-start(bf16[2,512,256]{2,1,0:T(8,128)(2,1)S(1)} %get-tuple-element.81), channel_id=1, source_target_pairs={{0,8},{8,16},{16,24},{1,9},{9,17},{17,25},{2,10},{10,18},{18,26},{... | collective-permute-start | bytes 1572872 | tf_op jit(solution)/shard_map/ppermute | solution.py:595
  58.6 1.2 %collective-permute-done.15.refs_0_ = bf16[2,512,256]{2,1,0:T(8,128)(2,1)S(1)} collective-permute-done((bf16[2,512,256]{2,1,0:T(8,128)(2,1)S(1)}, bf16[2,512,256]{2,1,0:T(8,128)(2,1)S(1)}, u32[]{:S(2)}, u32[]{:S(2)}) %collective-permute-start.15) | collective-permute-done | bytes 524320 | tf_op jit(solution)/shard_map/ppermute | solution.py:581
  59.8 1.2 %shard_map.109.rest_1_.attended_ref.sum_ref = f32[512,512]{1,0:T(8,128)S(1)} custom-call(f32[512,512]{1,0:T(8,128)S(1)} %get-tuple-element.77.sum_ref, f32[2,512,512]{2,1,0:T(8,128)S(1)} %get-tuple-element.78.stats_ref, bf16[1,512,512]{2,1,0:T(8,128)(2,1)S(1)} %shard_map.105.q_ref, ...), custom_call_target="tpu_custom_call", output_to_operand_aliasing={{}: (0, {})} | custom-call | flops 201326592 | bytes 1048576 | tf_op jit(solution)/shard_map/pallas_call | solution.py:405
  61.1 4.6 %collective-permute-done.18.rest_0_ = bf16[2,3,128,256]{3,2,1,0:T(8,128)(2,1)S(1)} collective-permute-done((bf16[2,3,128,256]{3,2,1,0:T(8,128)(2,1)S(1)}, bf16[2,3,128,256]{3,2,1,0:T(8,128)(2,1)S(1)}, u32[]{:S(2)}, u32[]{:S(2)}) %collective-permute-start.18) | collective-permute-done | bytes 393248 | tf_op jit(solution)/shard_map/ppermute | solution.py:544
  65.7 0.8 shard_map.112.net_ref
  66.6 0.8 shard_map.113.refs_1_.near_ref
  67.4 3.9 %collective-permute-done.17.refs_0_ = bf16[2,512,256]{2,1,0:T(8,128)(2,1)S(1)} collective-permute-done((bf16[2,512,256]{2,1,0:T(8,128)(2,1)S(1)}, bf16[2,512,256]{2,1,0:T(8,128)(2,1)S(1)}, u32[]{:S(2)}, u32[]{:S(2)}) %collective-permute-start.17) | collective-permute-done | bytes 524320 | tf_op jit(solution)/shard_map/ppermute | solution.py:595
  71.3 1.2 %shard_map.114.attended_ref = f32[512,512]{1,0:T(8,128)S(1)} custom-call(f32[512,512]{1,0:T(8,128)S(1)} %shard_map.109.rest_1_.attended_ref.sum_ref, f32[2,512,512]{2,1,0:T(8,128)S(1)} %get-tuple-element.78.stats_ref, bf16[1,512,512]{2,1,0:T(8,128)(2,1)S(1)} %shard_map.105.q_ref, ...), custom_call_target="tpu_custom_call", output_to_operand_aliasing={{}: (0, {})} | custom-call | flops 201326592 | bytes 1048576 | tf_op jit(solution)/shard_map/pallas_call | solution.py:405
  72.5 1.2 %shard_map.116 = (bf16[64,2048]{1,0:T(8,128)(2,1)S(1)}, bf16[64,2048]{1,0:T(8,128)(2,1)S(1)}) custom-call(bf16[1,512,512]{2,1,0:T(8,128)(2,1)S(1)} %shard_map.105.q_ref, f32[512,512]{1,0:T(8,128)S(1)} %shard_map.114.attended_ref, bf16[2,3,128,256]{3,2,1,0:T(8,128)(2,1)S(1)} %collective-permute-done.19.net_ref, ...), custom_call_target="tpu_custom_call" | custom-call | flops 268435456 | bytes 4718592 | tf_op jit(solution)/shard_map/pallas_call | solution.py:481
  73.7 1.3 %collective-permute-start.20 = (bf16[64,2048]{1,0:T(8,128)(2,1)S(1)}, bf16[64,2048]{1,0:T(8,128)(2,1)S(1)}, u32[]{:S(2)}, u32[]{:S(2)}) collective-permute-start(bf16[64,2048]{1,0:T(8,128)(2,1)S(1)} %get-tuple-element.85), channel_id=1, source_target_pairs={{0,2},{2,4},{4,6},{6,7},{7,5},{5,3},{3,1},{1,0},{8,10},{10,12},{12... | collective-permute-start | bytes 786440 | tf_op jit(solution)/shard_map/ppermute | solution.py:55
  75.1 0.2 collective-permute-start.22
  75.3 1.2 %shard_map.115 = (bf16[64,2048]{1,0:T(8,128)(2,1)S(1)}, bf16[64,2048]{1,0:T(8,128)(2,1)S(1)}, bf16[64,2048]{1,0:T(8,128)(2,1)S(1)}, bf16[64,2048]{1,0:T(8,128)(2,1)S(1)}) custom-call(bf16[1,512,512]{2,1,0:T(8,128)(2,1)S(1)} %shard_map.105.q_ref, f32[512,512]{1,0:T(8,128)S(1)} %shard_map.114.attended_ref, ...), custom_call_target="tpu_custom_call" | custom-call | flops 536870912 | bytes 5242880 | tf_op jit(solution)/shard_map/pallas_call | solution.py:481
  76.5 1.4 %collective-permute-start.24 = (bf16[64,2048]{1,0:T(8,128)(2,1)S(1)}, bf16[64,2048]{1,0:T(8,128)(2,1)S(1)}, u32[]{:S(2)}, u32[]{:S(2)}) collective-permute-start(bf16[64,2048]{1,0:T(8,128)(2,1)S(1)} %get-tuple-element.90), channel_id=1, source_target_pairs={{0,2},{2,4},{4,6},{6,7},{7,5},{5,3},{3,1},{1,0},{8,10},{10,12},{12... | collective-permute-start | bytes 786440 | tf_op jit(solution)/shard_map/ppermute | solution.py:55
  78.0 4.1 %collective-permute-done.20.refs_0_ = bf16[64,2048]{1,0:T(8,128)(2,1)S(1)} collective-permute-done((bf16[64,2048]{1,0:T(8,128)(2,1)S(1)}, bf16[64,2048]{1,0:T(8,128)(2,1)S(1)}, u32[]{:S(2)}, u32[]{:S(2)}) %collective-permute-start.20) | collective-permute-done | bytes 262176 | tf_op jit(solution)/shard_map/ppermute | solution.py:55
  82.2 1.3 %collective-permute-start.21 = (bf16[64,2048]{1,0:T(8,128)(2,1)S(1)}, bf16[64,2048]{1,0:T(8,128)(2,1)S(1)}, u32[]{:S(2)}, u32[]{:S(2)}) collective-permute-start(bf16[64,2048]{1,0:T(8,128)(2,1)S(1)} %add_convert_fusion.11), channel_id=1, source_target_pairs={{0,2},{2,4},{4,6},{6,7},{7,5},{5,3},{3,1},{1,0},{8,10},{10,12},{12... | collective-permute-start | bytes 786440 | tf_op jit(solution)/shard_map/ppermute | solution.py:55
  83.6 0.2 collective-permute-start.23
  83.8 1.2 %shard_map.118 = (bf16[64,2048]{1,0:T(8,128)(2,1)S(1)}, bf16[64,2048]{1,0:T(8,128)(2,1)S(1)}, bf16[64,2048]{1,0:T(8,128)(2,1)S(1)}, bf16[64,2048]{1,0:T(8,128)(2,1)S(1)}) custom-call(bf16[1,512,512]{2,1,0:T(8,128)(2,1)S(1)} %shard_map.105.q_ref, f32[512,512]{1,0:T(8,128)S(1)} %shard_map.114.attended_ref, ...), custom_call_target="tpu_custom_call" | custom-call | flops 536870912 | bytes 5242880 | tf_op jit(solution)/shard_map/pallas_call | solution.py:481
  85.0 2.7 %collective-permute-done.24 = bf16[64,2048]{1,0:T(8,128)(2,1)S(1)} collective-permute-done((bf16[64,2048]{1,0:T(8,128)(2,1)S(1)}, bf16[64,2048]{1,0:T(8,128)(2,1)S(1)}, u32[]{:S(2)}, u32[]{:S(2)}) %collective-permute-start.24) | collective-permute-done | bytes 262176 | tf_op jit(solution)/shard_map/ppermute | solution.py:55
  87.8 1.3 %collective-permute-start.25 = (bf16[64,2048]{1,0:T(8,128)(2,1)S(1)}, bf16[64,2048]{1,0:T(8,128)(2,1)S(1)}, u32[]{:S(2)}, u32[]{:S(2)}) collective-permute-start(bf16[64,2048]{1,0:T(8,128)(2,1)S(1)} %add_convert_fusion.9), channel_id=1, source_target_pairs={{0,2},{2,4},{4,6},{6,7},{7,5},{5,3},{3,1},{1,0},{8,10},{10,12},{12... | collective-permute-start | bytes 786440 | tf_op jit(solution)/shard_map/ppermute | solution.py:55
  89.2 0.2 collective-permute-start.28
  89.4 3.9 %collective-permute-done.21.refs_0_ = bf16[64,2048]{1,0:T(8,128)(2,1)S(1)} collective-permute-done((bf16[64,2048]{1,0:T(8,128)(2,1)S(1)}, bf16[64,2048]{1,0:T(8,128)(2,1)S(1)}, u32[]{:S(2)}, u32[]{:S(2)}) %collective-permute-start.21) | collective-permute-done | bytes 262176 | tf_op jit(solution)/shard_map/ppermute | solution.py:55
  93.4 1.3 %collective-permute-start.30 = (bf16[64,2048]{1,0:T(8,128)(2,1)S(1)}, bf16[64,2048]{1,0:T(8,128)(2,1)S(1)}, u32[]{:S(2)}, u32[]{:S(2)}) collective-permute-start(bf16[64,2048]{1,0:T(8,128)(2,1)S(1)} %add_convert_fusion.6), channel_id=1, source_target_pairs={{0,2},{2,4},{4,6},{6,7},{7,5},{5,3},{3,1},{1,0},{8,10},{10,12},{12... | collective-permute-start | bytes 786440 | tf_op jit(solution)/shard_map/ppermute | solution.py:55
  94.8 0.2 collective-permute-start.32
  95.1 1.5 %shard_map.117 = (bf16[64,2048]{1,0:T(8,128)(2,1)S(1)}, bf16[64,2048]{1,0:T(8,128)(2,1)S(1)}, bf16[64,2048]{1,0:T(8,128)(2,1)S(1)}, bf16[64,2048]{1,0:T(8,128)(2...) custom-call(bf16[1,512,512]{2,1,0:T(8,128)(2,1)S(1)} %shard_map.105.q_ref, ...), custom_call_target="tpu_custom_call" | custom-call | flops 805306368 | bytes 5767168 | tf_op jit(solution)/shard_map/pallas_call | solution.py:481
  96.6 2.4 %collective-permute-done.25 = bf16[64,2048]{1,0:T(8,128)(2,1)S(1)} collective-permute-done((bf16[64,2048]{1,0:T(8,128)(2,1)S(1)}, bf16[64,2048]{1,0:T(8,128)(2,1)S(1)}, u32[]{:S(2)}, u32[]{:S(2)}) %collective-permute-start.25) | collective-permute-done | bytes 262176 | tf_op jit(solution)/shard_map/ppermute | solution.py:55
  99.0 1.3 %collective-permute-start.27 = (bf16[64,2048]{1,0:T(8,128)(2,1)S(1)}, bf16[64,2048]{1,0:T(8,128)(2,1)S(1)}, u32[]{:S(2)}, u32[]{:S(2)}) collective-permute-start(bf16[64,2048]{1,0:T(8,128)(2,1)S(1)} %add_convert_fusion.8), channel_id=1, source_target_pairs={{0,2},{2,4},{4,6},{6,7},{7,5},{5,3},{3,1},{1,0},{8,10},{10,12},{12... | collective-permute-start | bytes 786440 | tf_op jit(solution)/shard_map/ppermute | solution.py:55
  100.4 0.2 collective-permute-start.29
  100.7 3.9 %collective-permute-done.30 = bf16[64,2048]{1,0:T(8,128)(2,1)S(1)} collective-permute-done((bf16[64,2048]{1,0:T(8,128)(2,1)S(1)}, bf16[64,2048]{1,0:T(8,128)(2,1)S(1)}, u32[]{:S(2)}, u32[]{:S(2)}) %collective-permute-start.30) | collective-permute-done | bytes 262176 | tf_op jit(solution)/shard_map/ppermute | solution.py:55
  104.6 1.3 %collective-permute-start.31 = (bf16[64,2048]{1,0:T(8,128)(2,1)S(1)}, bf16[64,2048]{1,0:T(8,128)(2,1)S(1)}, u32[]{:S(2)}, u32[]{:S(2)}) collective-permute-start(bf16[64,2048]{1,0:T(8,128)(2,1)S(1)} %add_convert_fusion.3), channel_id=1, source_target_pairs={{0,2},{2,4},{4,6},{6,7},{7,5},{5,3},{3,1},{1,0},{8,10},{10,12},{12... | collective-permute-start | bytes 786440 | tf_op jit(solution)/shard_map/ppermute | solution.py:55
  106.1 0.2 collective-permute-start.33
  106.3 5.1 %collective-permute-done.29.refs_3_ = bf16[64,2048]{1,0:T(8,128)(2,1)S(1)} collective-permute-done((bf16[64,2048]{1,0:T(8,128)(2,1)S(1)}, bf16[64,2048]{1,0:T(8,128)(2,1)S(1)}, u32[]{:S(2)}, u32[]{:S(2)}) %collective-permute-start.29) | collective-permute-done | bytes 262176 | tf_op jit(solution)/shard_map/ppermute | solution.py:55
  111.5 0.9 collective-permute-done.31
  112.4 1.5 %collective-permute-done.33 = bf16[64,2048]{1,0:T(8,128)(2,1)S(1)} collective-permute-done((bf16[64,2048]{1,0:T(8,128)(2,1)S(1)}, bf16[64,2048]{1,0:T(8,128)(2,1)S(1)}, u32[]{:S(2)}, u32[]{:S(2)}) %collective-permute-start.33) | collective-permute-done | bytes 262176 | tf_op jit(solution)/shard_map/ppermute | solution.py:55
  114.0 0.8 pad_maximum_fusion
  (49 shorter events, 1.5 us)
Async XLA Ops:
  1.1 8.5 %collective-permute-start = (bf16[256,512]{1,0:T(8,128)(2,1)S(1)}, bf16[256,512]{1,0:T(8,128)(2,1)S(1)}, u32[]{:S(2)}, u32[]{:S(2)}) collective-permute-start(bf16[256,512]{1,0:T(8,128)(2,1)S(1)} %get-tuple-element.66.refs_0_), channel_id=1, source_target_pairs={{0,2},{2,4},{4,6},{6,7},{7,5},{5,3},{3,1},{1,0},{8,10},{10,12},{12... | collective-permute-start | bytes 786440 | tf_op jit(solution)/shard_map/ppermute | solution.py:55
  3.2 7.8 %collective-permute-start.6 = (bf16[256,512]{1,0:T(8,128)(2,1)S(1)}, bf16[256,512]{1,0:T(8,128)(2,1)S(1)}, u32[]{:S(2)}, u32[]{:S(2)}) collective-permute-start(bf16[256,512]{1,0:T(8,128)(2,1)S(1)} %get-tuple-element.66.refs_0_), channel_id=1, source_target_pairs={{0,1},{2,0},{4,2},{6,4},{7,6},{5,7},{3,5},{1,3},{8,9},{10,8},{12,1... | collective-permute-start | bytes 786440 | tf_op jit(solution)/shard_map/ppermute | solution.py:55
  3.2 12.8 %copy-start.4 = (f32[512,4]{0,1:T(4,128)S(1)}, f32[512,4]{0,1:T(4,128)}, u32[]{:S(2)}) copy-start(f32[512,4]{0,1:T(4,128)} %param.18) | copy-start | bytes 24580
  3.2 12.5 %collective-permute-start.4 = (bf16[256,512]{1,0:T(8,128)(2,1)S(1)}, bf16[256,512]{1,0:T(8,128)(2,1)S(1)}, u32[]{:S(2)}, u32[]{:S(2)}) collective-permute-start(bf16[256,512]{1,0:T(8,128)(2,1)S(1)} %get-tuple-element.63.refs_3_), channel_id=1, source_target_pairs={{0,1},{2,0},{4,2},{6,4},{7,6},{5,7},{3,5},{1,3},{8,9},{10,8},{12,1... | collective-permute-start | bytes 786440 | tf_op jit(solution)/shard_map/ppermute | solution.py:55
  4.6 14.4 %collective-permute-start.8 = (bf16[256,512]{1,0:T(8,128)(2,1)S(1)}, bf16[256,512]{1,0:T(8,128)(2,1)S(1)}, u32[]{:S(2)}, u32[]{:S(2)}) collective-permute-start(bf16[256,512]{1,0:T(8,128)(2,1)S(1)} %get-tuple-element.63.refs_3_), channel_id=1, source_target_pairs={{0,2},{2,4},{4,6},{6,7},{7,5},{5,3},{3,1},{1,0},{8,10},{10,12},{12... | collective-permute-start | bytes 786440 | tf_op jit(solution)/shard_map/ppermute | solution.py:55
  9.5 11.3 %collective-permute-start.1 = (bf16[256,512]{1,0:T(8,128)(2,1)S(1)}, bf16[256,512]{1,0:T(8,128)(2,1)S(1)}, u32[]{:S(2)}, u32[]{:S(2)}) collective-permute-start(bf16[256,512]{1,0:T(8,128)(2,1)S(1)} %collective-permute-done.refs_1_), channel_id=1, source_target_pairs={{0,2},{2,4},{4,6},{6,7},{7,5},{5,3},{3,1},{1,0},{8,10},{10,12},{12... | collective-permute-start | bytes 786440 | tf_op jit(solution)/shard_map/ppermute | solution.py:55
  11.0 10.3 %collective-permute-start.7 = (bf16[256,512]{1,0:T(8,128)(2,1)S(1)}, bf16[256,512]{1,0:T(8,128)(2,1)S(1)}, u32[]{:S(2)}, u32[]{:S(2)}) collective-permute-start(bf16[256,512]{1,0:T(8,128)(2,1)S(1)} %collective-permute-done.6.refs_2_), channel_id=1, source_target_pairs={{0,1},{2,0},{4,2},{6,4},{7,6},{5,7},{3,5},{1,3},{8,9},{10,8},{12,1... | collective-permute-start | bytes 786440 | tf_op jit(solution)/shard_map/ppermute | solution.py:55
  15.7 11.2 %collective-permute-start.5 = (bf16[256,512]{1,0:T(8,128)(2,1)S(1)}, bf16[256,512]{1,0:T(8,128)(2,1)S(1)}, u32[]{:S(2)}, u32[]{:S(2)}) collective-permute-start(bf16[256,512]{1,0:T(8,128)(2,1)S(1)} %collective-permute-done.4.refs_5_), channel_id=1, source_target_pairs={{0,1},{2,0},{4,2},{6,4},{7,6},{5,7},{3,5},{1,3},{8,9},{10,8},{12,1... | collective-permute-start | bytes 786440 | tf_op jit(solution)/shard_map/ppermute | solution.py:55
  16.0 9.4 %collective-permute-start.9 = (f32[4,512]{1,0:T(4,128)S(1)}, f32[4,512]{1,0:T(4,128)S(1)}, u32[]{:S(2)}, u32[]{:S(2)}) collective-permute-start(f32[4,512]{1,0:T(4,128)S(1)} %bitcast.1), channel_id=1, source_target_pairs={{0,8},{8,0},{16,24},{24,16},{1,9},{9,1},{17,25},{25,17},{2,10},{10... | collective-permute-start | bytes 24584 | tf_op jit(solution)/shard_map/ppermute | solution.py:544
  19.0 8.2 %collective-permute-start.13 = (bf16[256,512]{1,0:T(8,128)(2,1)S(1)}, bf16[256,512]{1,0:T(8,128)(2,1)S(1)}, u32[]{:S(2)}, u32[]{:S(2)}) collective-permute-start(bf16[256,512]{1,0:T(8,128)(2,1)S(1)} %collective-permute-done.8.refs_4_), channel_id=1, source_target_pairs={{0,2},{2,4},{4,6},{6,7},{7,5},{5,3},{3,1},{1,0},{8,10},{10,12},{12... | collective-permute-start | bytes 786440 | tf_op jit(solution)/shard_map/ppermute | solution.py:55
  21.3 11.5 %collective-permute-start.2 = (bf16[256,512]{1,0:T(8,128)(2,1)S(1)}, bf16[256,512]{1,0:T(8,128)(2,1)S(1)}, u32[]{:S(2)}, u32[]{:S(2)}) collective-permute-start(bf16[256,512]{1,0:T(8,128)(2,1)S(1)} %collective-permute-done.1.refs_0_), channel_id=1, source_target_pairs={{0,2},{2,4},{4,6},{6,7},{7,5},{5,3},{3,1},{1,0},{8,10},{10,12},{12... | collective-permute-start | bytes 786440 | tf_op jit(solution)/shard_map/ppermute | solution.py:55
  22.6 10.2 %collective-permute-start.12 = (bf16[256,512]{1,0:T(8,128)(2,1)S(1)}, bf16[256,512]{1,0:T(8,128)(2,1)S(1)}, u32[]{:S(2)}, u32[]{:S(2)}) collective-permute-start(bf16[256,512]{1,0:T(8,128)(2,1)S(1)} %collective-permute-done.7.refs_1_), channel_id=1, source_target_pairs={{0,1},{2,0},{4,2},{6,4},{7,6},{5,7},{3,5},{1,3},{8,9},{10,8},{12,1... | collective-permute-start | bytes 786440 | tf_op jit(solution)/shard_map/ppermute | solution.py:55
  26.9 11.2 %collective-permute-start.10 = (bf16[256,512]{1,0:T(8,128)(2,1)S(1)}, bf16[256,512]{1,0:T(8,128)(2,1)S(1)}, u32[]{:S(2)}, u32[]{:S(2)}) collective-permute-start(bf16[256,512]{1,0:T(8,128)(2,1)S(1)} %collective-permute-done.5.refs_3_), channel_id=1, source_target_pairs={{0,1},{2,0},{4,2},{6,4},{7,6},{5,7},{3,5},{1,3},{8,9},{10,8},{12,1... | collective-permute-start | bytes 786440 | tf_op jit(solution)/shard_map/ppermute | solution.py:55
  27.3 13.0 %collective-permute-start.14 = (bf16[256,512]{1,0:T(8,128)(2,1)S(1)}, bf16[256,512]{1,0:T(8,128)(2,1)S(1)}, u32[]{:S(2)}, u32[]{:S(2)}) collective-permute-start(bf16[256,512]{1,0:T(8,128)(2,1)S(1)} %collective-permute-done.13.refs_2_), channel_id=1, source_target_pairs={{0,2},{2,4},{4,6},{6,7},{7,5},{5,3},{3,1},{1,0},{8,10},{10,12},{12... | collective-permute-start | bytes 786440 | tf_op jit(solution)/shard_map/ppermute | solution.py:55
  32.9 11.8 %collective-permute-start.3 = (bf16[256,512]{1,0:T(8,128)(2,1)S(1)}, bf16[256,512]{1,0:T(8,128)(2,1)S(1)}, u32[]{:S(2)}, u32[]{:S(2)}) collective-permute-start(bf16[256,512]{1,0:T(8,128)(2,1)S(1)} %collective-permute-done.2.refs_0_), channel_id=1, source_target_pairs={{0,2},{2,4},{4,6},{6,7},{7,5},{5,3},{3,1},{1,0},{8,10},{10,12},{12... | collective-permute-start | bytes 786440 | tf_op jit(solution)/shard_map/ppermute | solution.py:55
  38.2 5.9 %collective-permute-start.11 = (bf16[256,512]{1,0:T(8,128)(2,1)S(1)}, bf16[256,512]{1,0:T(8,128)(2,1)S(1)}, u32[]{:S(2)}, u32[]{:S(2)}) collective-permute-start(bf16[256,512]{1,0:T(8,128)(2,1)S(1)} %collective-permute-done.10.refs_3_), channel_id=1, source_target_pairs={{0,1},{2,0},{4,2},{6,4},{7,6},{5,7},{3,5},{1,3},{8,9},{10,8},{12,1... | collective-permute-start | bytes 786440 | tf_op jit(solution)/shard_map/ppermute | solution.py:55
  44.6 6.5 %copy-start.1 = (f32[4,128,256]{2,1,0:T(8,128)S(1)}, f32[4,128,256]{2,1,0:T(8,128)}, u32[]{:S(2)}) copy-start(f32[4,128,256]{2,1,0:T(8,128)} %gate_ref.5) | copy-start | bytes 1572868
  44.7 6.5 %copy-start.2 = (f32[4,128,256]{2,1,0:T(8,128)S(1)}, f32[4,128,256]{2,1,0:T(8,128)}, u32[]{:S(2)}) copy-start(f32[4,128,256]{2,1,0:T(8,128)} %up_ref.5) | copy-start | bytes 1572868
  44.7 6.5 %copy-start.3 = (f32[4,256,128]{2,1,0:T(8,128)S(1)}, f32[4,256,128]{2,1,0:T(8,128)}, u32[]{:S(2)}) copy-start(f32[4,256,128]{2,1,0:T(8,128)} %down_ref.5) | copy-start | bytes 1572868
  45.2 7.4 %collective-permute-start.16 = (bf16[2,512,256]{2,1,0:T(8,128)(2,1)S(1)}, bf16[2,512,256]{2,1,0:T(8,128)(2,1)S(1)}, u32[]{:S(2)}, u32[]{:S(2)}) collective-permute-start(bf16[2,512,256]{2,1,0:T(8,128)(2,1)S(1)} %get-tuple-element.79), channel_id=1, source_target_pairs={{0,8},{8,0},{16,24},{24,16},{1,9},{9,1},{17,25},{25,17},{2,10},{10... | collective-permute-start | bytes 1572872 | tf_op jit(solution)/shard_map/ppermute | solution.py:544
  48.1 11.8 %collective-permute-start.15 = (bf16[2,512,256]{2,1,0:T(8,128)(2,1)S(1)}, bf16[2,512,256]{2,1,0:T(8,128)(2,1)S(1)}, u32[]{:S(2)}, u32[]{:S(2)}) collective-permute-start(bf16[2,512,256]{2,1,0:T(8,128)(2,1)S(1)} %get-tuple-element.79), channel_id=1, source_target_pairs={{8,16},{9,17},{10,18},{11,19},{12,20},{13,21},{14,22},{15,23}} | collective-permute-start | bytes 1572872 | tf_op jit(solution)/shard_map/ppermute | solution.py:581
  54.1 11.6 %collective-permute-start.18 = (bf16[2,3,128,256]{3,2,1,0:T(8,128)(2,1)S(1)}, bf16[2,3,128,256]{3,2,1,0:T(8,128)(2,1)S(1)}, u32[]{:S(2)}, u32[]{:S(2)}) collective-permute-start(bf16[2,3,128,256]{3,2,1,0:T(8,128)(2,1)S(1)} %get-tuple-element.83), channel_id=1, source_target_pairs={{0,16},{8,24},{16,0},{24,8},{1,17},{9,25},{17,1},{25,9},{2,18},{10... | collective-permute-start | bytes 1179656 | tf_op jit(solution)/shard_map/ppermute | solution.py:544
  54.6 11.1 %copy-start.5 = (f32[4]{0:T(128)S(1)}, f32[4]{0:T(128)}, u32[]{:S(2)}) copy-start(f32[4]{0:T(128)} %step_ref.1) | copy-start | bytes 52
  56.7 14.6 %collective-permute-start.17 = (bf16[2,512,256]{2,1,0:T(8,128)(2,1)S(1)}, bf16[2,512,256]{2,1,0:T(8,128)(2,1)S(1)}, u32[]{:S(2)}, u32[]{:S(2)}) collective-permute-start(bf16[2,512,256]{2,1,0:T(8,128)(2,1)S(1)} %get-tuple-element.81), channel_id=1, source_target_pairs={{0,8},{8,16},{16,24},{1,9},{9,17},{17,25},{2,10},{10,18},{18,26},{... | collective-permute-start | bytes 1572872 | tf_op jit(solution)/shard_map/ppermute | solution.py:595
  66.5 6.0 %copy-start = (bf16[512,4096]{1,0:T(8,128)(2,1)S(1)}, bf16[512,4096]{1,0:T(8,128)(2,1)}, u32[]{:S(2)}) copy-start(bf16[512,4096]{1,0:T(8,128)(2,1)} %w_ref.7) | copy-start | bytes 12582916
  66.5 6.0 %collective-permute-start.19 = (bf16[2,3,128,256]{3,2,1,0:T(8,128)(2,1)S(1)}, bf16[2,3,128,256]{3,2,1,0:T(8,128)(2,1)S(1)}, u32[]{:S(2)}, u32[]{:S(2)}) collective-permute-start(bf16[2,3,128,256]{3,2,1,0:T(8,128)(2,1)S(1)} %shard_map.112.net_ref), channel_id=1, source_target_pairs={{0,8},{8,0},{16,24},{24,16},{1,9},{9,1},{17,25},{25,17},{2,10},{10... | collective-permute-start | bytes 1179656 | tf_op jit(solution)/shard_map/ppermute | solution.py:544
  73.7 8.4 %collective-permute-start.20 = (bf16[64,2048]{1,0:T(8,128)(2,1)S(1)}, bf16[64,2048]{1,0:T(8,128)(2,1)S(1)}, u32[]{:S(2)}, u32[]{:S(2)}) collective-permute-start(bf16[64,2048]{1,0:T(8,128)(2,1)S(1)} %get-tuple-element.85), channel_id=1, source_target_pairs={{0,2},{2,4},{4,6},{6,7},{7,5},{5,3},{3,1},{1,0},{8,10},{10,12},{12... | collective-permute-start | bytes 786440 | tf_op jit(solution)/shard_map/ppermute | solution.py:55
  75.1 8.4 %collective-permute-start.22 = (bf16[64,2048]{1,0:T(8,128)(2,1)S(1)}, bf16[64,2048]{1,0:T(8,128)(2,1)S(1)}, u32[]{:S(2)}, u32[]{:S(2)}) collective-permute-start(bf16[64,2048]{1,0:T(8,128)(2,1)S(1)} %get-tuple-element.89), channel_id=1, source_target_pairs={{0,1},{2,0},{4,2},{6,4},{7,6},{5,7},{3,5},{1,3},{8,9},{10,8},{12,1... | collective-permute-start | bytes 786440 | tf_op jit(solution)/shard_map/ppermute | solution.py:55
  76.5 11.2 %collective-permute-start.24 = (bf16[64,2048]{1,0:T(8,128)(2,1)S(1)}, bf16[64,2048]{1,0:T(8,128)(2,1)S(1)}, u32[]{:S(2)}, u32[]{:S(2)}) collective-permute-start(bf16[64,2048]{1,0:T(8,128)(2,1)S(1)} %get-tuple-element.90), channel_id=1, source_target_pairs={{0,2},{2,4},{4,6},{6,7},{7,5},{5,3},{3,1},{1,0},{8,10},{10,12},{12... | collective-permute-start | bytes 786440 | tf_op jit(solution)/shard_map/ppermute | solution.py:55
  77.8 11.3 %collective-permute-start.26 = (bf16[64,2048]{1,0:T(8,128)(2,1)S(1)}, bf16[64,2048]{1,0:T(8,128)(2,1)S(1)}, u32[]{:S(2)}, u32[]{:S(2)}) collective-permute-start(bf16[64,2048]{1,0:T(8,128)(2,1)S(1)} %get-tuple-element.91), channel_id=1, source_target_pairs={{0,1},{2,0},{4,2},{6,4},{7,6},{5,7},{3,5},{1,3},{8,9},{10,8},{12,1... | collective-permute-start | bytes 786440 | tf_op jit(solution)/shard_map/ppermute | solution.py:55
  82.2 11.2 %collective-permute-start.21 = (bf16[64,2048]{1,0:T(8,128)(2,1)S(1)}, bf16[64,2048]{1,0:T(8,128)(2,1)S(1)}, u32[]{:S(2)}, u32[]{:S(2)}) collective-permute-start(bf16[64,2048]{1,0:T(8,128)(2,1)S(1)} %add_convert_fusion.11), channel_id=1, source_target_pairs={{0,2},{2,4},{4,6},{6,7},{7,5},{5,3},{3,1},{1,0},{8,10},{10,12},{12... | collective-permute-start | bytes 786440 | tf_op jit(solution)/shard_map/ppermute | solution.py:55
  83.6 11.2 %collective-permute-start.23 = (bf16[64,2048]{1,0:T(8,128)(2,1)S(1)}, bf16[64,2048]{1,0:T(8,128)(2,1)S(1)}, u32[]{:S(2)}, u32[]{:S(2)}) collective-permute-start(bf16[64,2048]{1,0:T(8,128)(2,1)S(1)} %add_convert_fusion.10), channel_id=1, source_target_pairs={{0,1},{2,0},{4,2},{6,4},{7,6},{5,7},{3,5},{1,3},{8,9},{10,8},{12,1... | collective-permute-start | bytes 786440 | tf_op jit(solution)/shard_map/ppermute | solution.py:55
  87.8 11.2 %collective-permute-start.25 = (bf16[64,2048]{1,0:T(8,128)(2,1)S(1)}, bf16[64,2048]{1,0:T(8,128)(2,1)S(1)}, u32[]{:S(2)}, u32[]{:S(2)}) collective-permute-start(bf16[64,2048]{1,0:T(8,128)(2,1)S(1)} %add_convert_fusion.9), channel_id=1, source_target_pairs={{0,2},{2,4},{4,6},{6,7},{7,5},{5,3},{3,1},{1,0},{8,10},{10,12},{12... | collective-permute-start | bytes 786440 | tf_op jit(solution)/shard_map/ppermute | solution.py:55
  89.2 11.2 %collective-permute-start.28 = (bf16[64,2048]{1,0:T(8,128)(2,1)S(1)}, bf16[64,2048]{1,0:T(8,128)(2,1)S(1)}, u32[]{:S(2)}, u32[]{:S(2)}) collective-permute-start(bf16[64,2048]{1,0:T(8,128)(2,1)S(1)} %add_convert_fusion.5), channel_id=1, source_target_pairs={{0,1},{2,0},{4,2},{6,4},{7,6},{5,7},{3,5},{1,3},{8,9},{10,8},{12,1... | collective-permute-start | bytes 786440 | tf_op jit(solution)/shard_map/ppermute | solution.py:55
  93.4 11.2 %collective-permute-start.30 = (bf16[64,2048]{1,0:T(8,128)(2,1)S(1)}, bf16[64,2048]{1,0:T(8,128)(2,1)S(1)}, u32[]{:S(2)}, u32[]{:S(2)}) collective-permute-start(bf16[64,2048]{1,0:T(8,128)(2,1)S(1)} %add_convert_fusion.6), channel_id=1, source_target_pairs={{0,2},{2,4},{4,6},{6,7},{7,5},{5,3},{3,1},{1,0},{8,10},{10,12},{12... | collective-permute-start | bytes 786440 | tf_op jit(solution)/shard_map/ppermute | solution.py:55
  94.8 11.2 %collective-permute-start.32 = (bf16[64,2048]{1,0:T(8,128)(2,1)S(1)}, bf16[64,2048]{1,0:T(8,128)(2,1)S(1)}, u32[]{:S(2)}, u32[]{:S(2)}) collective-permute-start(bf16[64,2048]{1,0:T(8,128)(2,1)S(1)} %add_convert_fusion.7), channel_id=1, source_target_pairs={{0,1},{2,0},{4,2},{6,4},{7,6},{5,7},{3,5},{1,3},{8,9},{10,8},{12,1... | collective-permute-start | bytes 786440 | tf_op jit(solution)/shard_map/ppermute | solution.py:55
  99.0 12.4 %collective-permute-start.27 = (bf16[64,2048]{1,0:T(8,128)(2,1)S(1)}, bf16[64,2048]{1,0:T(8,128)(2,1)S(1)}, u32[]{:S(2)}, u32[]{:S(2)}) collective-permute-start(bf16[64,2048]{1,0:T(8,128)(2,1)S(1)} %add_convert_fusion.8), channel_id=1, source_target_pairs={{0,2},{2,4},{4,6},{6,7},{7,5},{5,3},{3,1},{1,0},{8,10},{10,12},{12... | collective-permute-start | bytes 786440 | tf_op jit(solution)/shard_map/ppermute | solution.py:55
  100.4 11.0 %collective-permute-start.29 = (bf16[64,2048]{1,0:T(8,128)(2,1)S(1)}, bf16[64,2048]{1,0:T(8,128)(2,1)S(1)}, u32[]{:S(2)}, u32[]{:S(2)}) collective-permute-start(bf16[64,2048]{1,0:T(8,128)(2,1)S(1)} %add_convert_fusion.4), channel_id=1, source_target_pairs={{0,1},{2,0},{4,2},{6,4},{7,6},{5,7},{3,5},{1,3},{8,9},{10,8},{12,1... | collective-permute-start | bytes 786440 | tf_op jit(solution)/shard_map/ppermute | solution.py:55
  104.6 7.7 %collective-permute-start.31 = (bf16[64,2048]{1,0:T(8,128)(2,1)S(1)}, bf16[64,2048]{1,0:T(8,128)(2,1)S(1)}, u32[]{:S(2)}, u32[]{:S(2)}) collective-permute-start(bf16[64,2048]{1,0:T(8,128)(2,1)S(1)} %add_convert_fusion.3), channel_id=1, source_target_pairs={{0,2},{2,4},{4,6},{6,7},{7,5},{5,3},{3,1},{1,0},{8,10},{10,12},{12... | collective-permute-start | bytes 786440 | tf_op jit(solution)/shard_map/ppermute | solution.py:55
  106.1 7.9 %collective-permute-start.33 = (bf16[64,2048]{1,0:T(8,128)(2,1)S(1)}, bf16[64,2048]{1,0:T(8,128)(2,1)S(1)}, u32[]{:S(2)}, u32[]{:S(2)}) collective-permute-start(bf16[64,2048]{1,0:T(8,128)(2,1)S(1)} %add_convert_fusion.1), channel_id=1, source_target_pairs={{0,1},{2,0},{4,2},{6,4},{7,6},{5,7},{3,5},{1,3},{8,9},{10,8},{12,1... | collective-permute-start | bytes 786440 | tf_op jit(solution)/shard_map/ppermute | solution.py:55
